TPU v7x, 32 devices: a whole 2x2x4 slice. The times are simulated.
32 devices in a mesh: groups: 2 (over y), blk: 4 (over z), chan: 2 (over x), sub: 2 (over core).
Axes of the slice: x: 2, y: 2, z: 4, core: 2. Of those that a mesh axis runs over, the one named last changes fastest.
Arguments:
- pair: bfloat16 [64, 64, 64, 128], P(('groups', 'blk'), 'chan', 'sub'), parts along dimension 0, may hold values from -6 to 6
- block_list: int32 [64, 2], P('groups'), parts along dimension 0, may hold values from 0 to 63
- term_owner: int32 [64, 2], P('groups'), parts along dimension 0, may hold values from 0 to 3, all different within a row; in each aligned block of 8 rows (0 to 7, 8 to 15, ...) at most 4 rows name the same one
- term_slots: int32 [64, 2, 2], P('groups'), parts along dimension 0, may hold values from 0 to 7
- chain_ids: int32 [8192], P('groups'), parts along dimension 0, may hold values from -1 to 1, as said below
- w_in: bfloat16 [2, 128, 640], replicated, may hold values from -0.5 to 0.5
- w_out: bfloat16 [2, 128, 128], replicated, may hold values from -0.5 to 0.5
Outputs:
- updated_pair: bfloat16 [64, 64, 64, 128], P(('groups', 'blk'), 'chan', 'sub'), parts along dimension 0
There are 2 independent parts, one for each index of `groups`. A program takes and returns all parts, laid end to end along the dimension named above; an argument that names none is the same for every part. Nothing has to cross between parts.
Inputs may be any that keep to these rules, and one draw needn't show every extreme that they name: term_owner[s, t] is the blk index of the device that holds both operands of term t of kept block s; the 2 values of a block differ; within the rows of one device (aligned runs of 8 kept blocks) no value stands more than 4 times, and some value stands exactly 4 times. term_slots[s, t, r] is the slot, among the 8 blocks that device holds, of the left (r = 0) or right (r = 1) operand. `block_list`: block coordinates in units of 64 residues. `chain_ids`: padding (-1) fills the last eighth to quarter of the residues; before it, chain 0 is followed by chain 1.
All inputs are finite; a program needn't handle non-finite values.
Results may differ from a plain program's by a relative error of at most 0.009.
Values may be sent and summed in bfloat16 or wider, within the bound.
No kernel may reach another device: no remote copies, remote signals or barrier semaphores. Data moves between devices by JAX's collectives and lax.ppermute only.
A program may use at most 128 MiB of HBM per device.

v0:
```python
import jax
import jax.numpy as jnp
from jax import lax
from jax.sharding import PartitionSpec as P

norm_epsilon = 1e-05


def layer_norm(values, channel_axis):
    values = values.astype(jnp.float32)
    average = jnp.mean(values, axis=channel_axis, keepdims=True)
    centred = values - average
    variance = jnp.mean(centred * centred, axis=channel_axis, keepdims=True)
    return centred * lax.rsqrt(variance + norm_epsilon)


def project(current, weights, pair_mask, hidden):
    normed = layer_norm(current, 3).astype(jnp.bfloat16)
    projected = jnp.einsum(
        "sijc,ch->sijh", normed, weights[:, : 4 * hidden], preferred_element_type=jnp.float32
    )
    gate_logit = jnp.einsum(
        "sijc,cd->sijd", normed, weights[:, 4 * hidden :], preferred_element_type=jnp.float32
    )
    scaled = pair_mask[:, :, :, None]
    left_part = (
        scaled * jax.nn.sigmoid(projected[..., hidden : 2 * hidden]) * projected[..., :hidden]
    )
    right_part = (
        scaled
        * jax.nn.sigmoid(projected[..., 3 * hidden :])
        * projected[..., 2 * hidden : 3 * hidden]
    )
    paired = jnp.stack([left_part, right_part], axis=1).astype(jnp.bfloat16)
    return (jnp.transpose(paired, (0, 1, 4, 2, 3)), gate_logit)


def finish(current, mixture, gate_logit, weights):
    normed = layer_norm(mixture, 1).astype(jnp.bfloat16)
    update = jnp.einsum("shij,hc->sijc", normed, weights, preferred_element_type=jnp.float32)
    return (current.astype(jnp.float32) + jax.nn.sigmoid(gate_logit) * update).astype(jnp.bfloat16)


def reorder_rows(weights, n_chan, n_sub):
    hidden = weights.shape[0]
    grouped = weights.reshape(n_chan, n_sub, hidden // (n_chan * n_sub), weights.shape[1])
    return jnp.transpose(grouped, (1, 0, 2, 3)).reshape(hidden, weights.shape[1])


def routing(term_owner, term_slots, position, n_blk, capacity):
    row_width = term_owner.shape[0] // n_blk * term_owner.shape[1]
    owners = term_owner.reshape(n_blk, row_width)
    left_slot = term_slots[:, :, 0].reshape(n_blk, row_width)
    right_slot = term_slots[:, :, 1].reshape(n_blk, row_width)
    positions = jnp.arange(row_width, dtype=jnp.int32)
    before = positions[:, None] < positions[None, :]
    same_owner = owners[:, :, None] == owners[:, None, :]
    earlier_count = jnp.sum(jnp.logical_and(same_owner, before[None]), axis=1)
    held_here = owners == position
    choose = jnp.logical_and(
        held_here[:, None, :],
        earlier_count[:, None, :] == jnp.arange(capacity, dtype=jnp.int32)[None, :, None],
    )
    send_left = jnp.sum(jnp.where(choose, left_slot[:, None, :], 0), axis=2)
    send_right = jnp.sum(jnp.where(choose, right_slot[:, None, :], 0), axis=2)
    filled = jnp.any(choose, axis=2)
    own_owners = lax.dynamic_index_in_dim(owners, position, 0, keepdims=False)
    own_counts = lax.dynamic_index_in_dim(earlier_count, position, 0, keepdims=False)
    arrival = own_owners * capacity + own_counts
    return (send_left.reshape(-1), send_right.reshape(-1), filled.reshape(-1), arrival)


def term_product(left_part, right_part):
    products = jnp.einsum(
        "...hki,...hkj->...hij", left_part, right_part, preferred_element_type=jnp.float32
    )
    return products.astype(jnp.bfloat16)


def add_terms(rounded, slots_dev):
    shaped = rounded.reshape((slots_dev, -1) + rounded.shape[-3:])
    return jnp.sum(shaped, axis=1, dtype=jnp.float32)


def fetch_terms(spread, plan, term_count):
    send_left, send_right, filled, arrival = plan
    slots_dev = spread.shape[0]
    chosen = jnp.stack([spread[send_left, 0], spread[send_right, 1]], axis=1)
    chosen = jnp.where(filled[:, None, None, None, None], chosen, jnp.zeros((), jnp.bfloat16))
    arrived = lax.all_to_all(chosen, "blk", split_axis=0, concat_axis=0, tiled=True)
    picked = arrived[arrival].reshape((slots_dev, term_count) + arrived.shape[1:])
    summed = add_terms(term_product(picked[:, 0, 0], picked[:, 0, 1]), slots_dev)
    rounded = term_product(picked[:, 1, 0], picked[:, 1, 1])
    summed = summed + add_terms(rounded, slots_dev)
    return summed


def per_device(pair, block_list, term_owner, term_slots, chain_ids, w_in, w_out):
    n_blk = lax.axis_size("blk")
    n_chan = lax.axis_size("chan")
    n_sub = lax.axis_size("sub")
    position = lax.axis_index("blk")
    row_group = lax.axis_index("chan")
    col_group = lax.axis_index("sub")
    slots_dev, rows_dev, cols_dev, channels = pair.shape
    block_size = rows_dev * n_chan
    hidden = w_out.shape[1]
    term_count = term_owner.shape[1]
    capacity = max(2, -(-slots_dev * term_count // n_blk))
    coords = lax.dynamic_slice_in_dim(block_list, position * slots_dev, slots_dev, 0)
    row_index = (
        coords[:, 0:1] * block_size
        + row_group * rows_dev
        + jnp.arange(rows_dev, dtype=jnp.int32)[None, :]
    )
    col_index = (
        coords[:, 1:2] * block_size
        + col_group * cols_dev
        + jnp.arange(cols_dev, dtype=jnp.int32)[None, :]
    )
    row_alive = (jnp.take(chain_ids, row_index) >= 0).astype(jnp.float32)
    col_alive = (jnp.take(chain_ids, col_index) >= 0).astype(jnp.float32)
    pair_mask = row_alive[:, :, None] * col_alive[:, None, :]
    plan = routing(term_owner, term_slots, position, n_blk, capacity)
    paired, gate_logit = project(pair, w_in[0], pair_mask, hidden)
    spread = lax.all_to_all(paired, "chan", split_axis=2, concat_axis=3, tiled=True)
    spread = jnp.swapaxes(spread, 3, 4)
    summed = fetch_terms(spread, plan, term_count)
    mixture = lax.psum_scatter(summed, "sub", scatter_dimension=3, tiled=True).astype(jnp.bfloat16)
    mixture = lax.all_to_all(mixture, "chan", split_axis=2, concat_axis=1, tiled=True)
    out_weights = w_out[0]
    current = finish(pair, mixture, gate_logit, out_weights)
    paired, gate_logit = project(current, w_in[1], pair_mask, hidden)
    spread = lax.all_to_all(
        lax.all_to_all(paired, "chan", split_axis=2, concat_axis=3, tiled=True),
        "sub",
        split_axis=2,
        concat_axis=4,
        tiled=True,
    )
    summed = fetch_terms(spread, plan, term_count)
    mixture = lax.all_to_all(
        lax.all_to_all(
            summed.astype(jnp.bfloat16), "chan", split_axis=2, concat_axis=1, tiled=True
        ),
        "sub",
        split_axis=3,
        concat_axis=1,
        tiled=True,
    )
    return finish(current, mixture, gate_logit, reorder_rows(w_out[1], n_chan, n_sub))


def solution(mesh):
    in_specs = (
        P(("groups", "blk"), "chan", "sub", None),
        P("groups", None),
        P("groups", None),
        P("groups", None, None),
        P("groups"),
        P(),
        P(),
    )
    out_specs = P(("groups", "blk"), "chan", "sub", None)
    return jax.shard_map(
        per_device, mesh=mesh, in_specs=in_specs, out_specs=out_specs, check_vma=False
    )
```

profile of v0, /device:TPU:11, one launch (start us, length us, event | category | flops | bytes accessed | tf_op | source)
XLA Modules:
  0.0 1253.8 jit_solution(7442598335516041275)
XLA Ops:
  23.0 23.1 %copy.156 = bf16[8,2,128,32,32]{4,3,0,1,2:T(8,128)(2,1)} copy(bf16[8,2,128,32,32]{2,4,3,0,1:T(8,128)(2,1)} %maximum_bitcast_fusion) | data formatting | bytes 8388608 | tf_op jit(solution)/shard_map/transpose | solution.py:35
  46.1 25.3 %reshape.289 = bf16[2,2,524288]{2,1,0:T(2,128)(2,1)} reshape(bf16[128,2,8,32,32]{4,3,2,1,0:T(8,128)(2,1)} %bitcast.193) | data formatting | bytes 8388608
  78.6 44.4 %all-to-all-done = bf16[2,2,524288]{2,1,0:T(2,128)(2,1)} async-done(((bf16[2,2,524288]{2,1,0:T(2,128)(2,1)}), bf16[2,2,524288]{2,1,0:T(2,128)(2,1)}, u32[]{:S(2)}, u32[]{:S(2)}) %all-to-all-start) | async-done | bytes 4194336 | tf_op jit(solution)/shard_map/all_to_all | solution.py:126
  123.0 18.8 %reshape.290 = bf16[128,2,8,32,32]{4,3,2,1,0:T(8,128)(2,1)} reshape(bf16[2,2,524288]{2,1,0:T(2,128)(2,1)} %all-to-all-done) | data formatting | bytes 8388608
  141.8 28.6 %copy.195 = bf16[8,2,2,64,32,32]{3,2,5,4,1,0:T(2,128)(2,1)} copy(bf16[8,2,2,64,32,32]{5,4,0,1,3,2:T(8,128)(2,1)} %bitcast.194) | data formatting | bytes 8388608 | tf_op jit(solution)/shard_map/all_to_all | solution.py:126
  179.1 16.4 %copy.159 = bf16[8,2,64,64,32]{3,4,2,1,0:T(8,128)(2,1)} copy(bf16[8,2,64,64,32]{2,4,3,1,0:T(8,128)(2,1)} %bitcast.215) | data formatting | bytes 8388608 | tf_op jit(solution)/shard_map/all_to_all | solution.py:126
  211.9 9.5 maximum_select_fusion
  229.7 16.6 %reshape.291 = bf16[4,2,524288]{2,1,0:T(2,128)(2,1)} reshape(bf16[16,2,64,32,64]{4,3,2,1,0:T(8,128)(2,1)} %copy.162) | data formatting | bytes 16777216
  252.0 179.0 %all-to-all-done.1 = bf16[4,2,524288]{2,1,0:T(2,128)(2,1)} async-done(((bf16[4,2,524288]{2,1,0:T(2,128)(2,1)}), bf16[4,2,524288]{2,1,0:T(2,128)(2,1)}, u32[]{:S(2)}, u32[]{:S(2)}) %all-to-all-start.1) | async-done | bytes 8388640 | tf_op jit(solution)/shard_map/all_to_all | solution.py:90
  431.0 16.1 %reshape.292 = bf16[16,2,64,32,64]{4,3,2,1,0:T(8,128)(2,1)} reshape(bf16[4,2,524288]{2,1,0:T(2,128)(2,1)} %all-to-all-done.1) | data formatting | bytes 16777216
  447.1 13.0 %gather_fusion.2 = bf16[16,2,64,32,64]{4,3,2,1,0:T(8,128)(2,1)} fusion(bf16[16,2,64,32,64]{4,3,2,1,0:T(8,128)(2,1)} %reshape.292, s32[1024]{0:T(1024)S(1)} %pad_clamp_fusion), kind=kCustom, calls=%fused_computation.4 | custom fusion | bytes 16777280 | tf_op jit(solution)/shard_map/gather | solution.py:91
  469.3 14.3 %convert_add_fusion = f32[8,64,64,64]{2,3,1,0:T(8,128)} fusion(bf16[8,64,64,64]{2,3,1,0:T(8,128)(2,1)} %fusion.34, bf16[8,2,2,64,32,64]{5,4,3,2,1,0:T(8,128)(2,1)} %bitcast.204), kind=kOutput, calls=%fused_computation.10 | convolution fusion | flops 142606336 | bytes 25165824 | tf_op jit(solution)/shard_map/...hki,...hkj->...hij/dot_general | solution.py:74
  483.6 30.3 %reduce-scatter.2.cloned.1.call-done = f32[8,64,64,32]{2,3,1,0:T(8,128)} async-done(((f32[8,64,64,64]{2,3,1,0:T(8,128)}), f32[8,64,64,32]{2,3,1,0:T(8,128)}) %reduce-scatter.2.cloned.1.call-update) | async-done | bytes 4194320 | tf_op jit(solution)/shard_map/reduce_scatter | solution.py:129
  544.8 19.3 %all-to-all-done.2 = bf16[2,2,262144]{2,1,0:T(2,128)(2,1)} async-done(((bf16[2,2,262144]{2,1,0:T(2,128)(2,1)}), bf16[2,2,262144]{2,1,0:T(2,128)(2,1)}, u32[]{:S(2)}, u32[]{:S(2)}) %all-to-all-start.2) | async-done | bytes 2097184 | tf_op jit(solution)/shard_map/all_to_all | solution.py:130
  580.8 10.7 copy.169
  613.6 23.1 %copy.170 = bf16[8,2,128,32,32]{4,3,0,1,2:T(8,128)(2,1)} copy(bf16[8,2,128,32,32]{2,4,3,0,1:T(8,128)(2,1)} %maximum_bitcast_fusion.1) | data formatting | bytes 8388608 | tf_op jit(solution)/shard_map/transpose | solution.py:35
  636.6 25.1 %reshape.295 = bf16[2,2,524288]{2,1,0:T(2,128)(2,1)} reshape(bf16[128,2,8,32,32]{4,3,2,1,0:T(8,128)(2,1)} %bitcast.195) | data formatting | bytes 8388608
  661.7 53.9 %all_to_all.100 = bf16[2,2,524288]{2,1,0:T(2,128)(2,1)} all-to-all(bf16[2,2,524288]{2,1,0:T(2,128)(2,1)} %reshape.295), channel_id=1, replica_groups=mesh['groups'=2,'blk'=4,'chan'=2,'sub'=2] {'chan'}, dimensions={0} | all-to-all | bytes 8388608 | tf_op jit(solution)/shard_map/all_to_all | solution.py:135
  715.6 18.5 %reshape.296 = bf16[128,2,8,32,32]{4,3,2,1,0:T(8,128)(2,1)} reshape(bf16[2,2,524288]{2,1,0:T(2,128)(2,1)} %all_to_all.100) | data formatting | bytes 8388608
  734.1 28.6 %copy.196 = bf16[8,2,2,64,32,32]{3,2,5,4,1,0:T(2,128)(2,1)} copy(bf16[8,2,2,64,32,32]{5,4,0,1,3,2:T(8,128)(2,1)} %bitcast.196) | data formatting | bytes 8388608 | tf_op jit(solution)/shard_map/all_to_all | solution.py:135
  771.3 16.4 %copy.173 = bf16[8,2,64,64,32]{3,4,1,0,2:T(8,128)(2,1)} copy(bf16[8,2,64,64,32]{2,4,3,1,0:T(8,128)(2,1)} %bitcast.216) | data formatting | bytes 8388608 | tf_op jit(solution)/shard_map/all_to_all | solution.py:135
  787.7 10.0 reshape.297
  797.7 13.6 %all_to_all.101 = bf16[2,2,524288]{2,1,0:T(2,128)(2,1)} all-to-all(bf16[2,2,524288]{2,1,0:T(2,128)(2,1)} %reshape.297), channel_id=1, replica_groups=mesh['groups'=2,'blk'=4,'chan'=2,'sub'=2] {'sub'}, dimensions={0} | all-to-all | bytes 8388608 | tf_op jit(solution)/shard_map/all_to_all | solution.py:134
  811.3 9.7 reshape.298
  846.7 16.0 %copy_bitcast_fusion = bf16[16,2,32,64,64]{4,3,2,1,0:T(8,128)(2,1)} fusion(bf16[16,1,32,64,64]{3,4,2,0,1:T(8,128)(2,1)} %bitcast.212, bf16[16,1,32,64,64]{3,4,2,0,1:T(8,128)(2,1)} %bitcast.211, pred[16]{0:T(512)(128)(4,1)S(1)} %copy-done.17), kind=kLoop, calls=%fused_computation.144 | loop fusion | flops 8388608 | bytes 16777232
  862.7 16.6 %reshape.299 = bf16[4,2,524288]{2,1,0:T(2,128)(2,1)} reshape(bf16[16,2,32,64,64]{4,3,2,1,0:T(8,128)(2,1)} %copy_bitcast_fusion) | data formatting | bytes 16777216
  879.3 188.5 %all_to_all.102 = bf16[4,2,524288]{2,1,0:T(2,128)(2,1)} all-to-all(bf16[4,2,524288]{2,1,0:T(2,128)(2,1)} %reshape.299), channel_id=1, replica_groups=mesh['groups'=2,'blk'=4,'chan'=2,'sub'=2] {'blk'}, dimensions={0} | all-to-all | bytes 16777216 | tf_op jit(solution)/shard_map/all_to_all | solution.py:90
  1067.8 16.0 %reshape.300 = bf16[16,2,32,64,64]{4,3,2,1,0:T(8,128)(2,1)} reshape(bf16[4,2,524288]{2,1,0:T(2,128)(2,1)} %all_to_all.102) | data formatting | bytes 16777216
  1083.8 21.3 %copy.177 = bf16[16,2,32,64,64]{4,3,2,1,0:T(8,128)(2,1)} copy(bf16[16,2,32,64,64]{3,4,2,1,0:T(8,128)(2,1)} %bitcast.199) | data formatting | bytes 16777216 | tf_op jit(solution)/shard_map/all_to_all | solution.py:90
  1105.1 13.1 %gather_fusion.5 = bf16[16,2,32,64,64]{4,3,2,1,0:T(8,128)(2,1)} fusion(bf16[16,2,32,64,64]{4,3,2,1,0:T(8,128)(2,1)} %copy.177, s32[1024]{0:T(1024)} %copy-done.15), kind=kCustom, calls=%fused_computation.7 | custom fusion | bytes 16777280 | tf_op jit(solution)/shard_map/gather | solution.py:91
  1150.0 17.7 %all-to-all-done.6 = bf16[2,2,262144]{2,1,0:T(2,128)(2,1)} async-done(((bf16[2,2,262144]{2,1,0:T(2,128)(2,1)}), bf16[2,2,262144]{2,1,0:T(2,128)(2,1)}, u32[]{:S(2)}, u32[]{:S(2)}) %all-to-all-start.6) | async-done | bytes 2097184 | tf_op jit(solution)/shard_map/all_to_all | solution.py:143
  1195.0 10.7 all_to_all.103
  (136 shorter events, 275.3 us)
Async XLA Ops:
  6.5 0.9 copy-start
  7.5 3.9 copy-start.2
  9.5 5.5 copy-start.13
  15.7 2.4 copy-start.6
  71.3 6.0 copy-start.19
  71.3 6.1 copy-start.18
  71.3 51.7 %all-to-all-start = ((bf16[2,2,524288]{2,1,0:T(2,128)(2,1)}), bf16[2,2,524288]{2,1,0:T(2,128)(2,1)}, u32[]{:S(2)}, u32[]{:S(2)}) async-start(bf16[2,2,524288]{2,1,0:T(2,128)(2,1)} %reshape.289), calls=%async_computation | async-start | bytes 8388608 | tf_op jit(solution)/shard_map/all_to_all | solution.py:126
  78.6 133.3 %copy-start.16 = (pred[16]{0:T(512)(128)(4,1)}, pred[16]{0:T(512)(128)(4,1)S(1)}, u32[]{:S(2)}) copy-start(pred[16]{0:T(512)(128)(4,1)S(1)} %broadcast_in_dim.80) | copy-start | bytes 52
  78.6 116.8 %copy-start.11 = (s32[16]{0:T(128)}, s32[16]{0:T(128)S(1)}, u32[]{:S(2)}) copy-start(s32[16]{0:T(128)S(1)} %get-tuple-element.20) | copy-start | bytes 196
  78.6 125.1 %copy-start.9 = (s32[16]{0:T(128)}, s32[16]{0:T(128)S(1)}, u32[]{:S(2)}) copy-start(s32[16]{0:T(128)S(1)} %get-tuple-element.21) | copy-start | bytes 196
  246.3 184.7 %all-to-all-start.1 = ((bf16[4,2,524288]{2,1,0:T(2,128)(2,1)}), bf16[4,2,524288]{2,1,0:T(2,128)(2,1)}, u32[]{:S(2)}, u32[]{:S(2)}) async-start(bf16[4,2,524288]{2,1,0:T(2,128)(2,1)} %reshape.291), calls=%async_computation.1 | async-start | bytes 16777216 | tf_op jit(solution)/shard_map/all_to_all | solution.py:90
  251.9 262.0 %reduce-scatter.2.cloned.1.call-start = ((), (), s32[]{:S(2)}) async-start(), calls=%async_computation.9 | async-start | bytes 25165824 | tf_op jit(solution)/shard_map/reduce_scatter | solution.py:129
  252.0 195.1 %copy-start.15 = (s32[1024]{0:T(1024)}, s32[1024]{0:T(1024)S(1)}, u32[]{:S(2)}) copy-start(s32[1024]{0:T(1024)S(1)} %pad_clamp_fusion) | copy-start | bytes 12292
  535.3 28.8 %all-to-all-start.2 = ((bf16[2,2,262144]{2,1,0:T(2,128)(2,1)}), bf16[2,2,262144]{2,1,0:T(2,128)(2,1)}, u32[]{:S(2)}, u32[]{:S(2)}) async-start(bf16[2,2,262144]{2,1,0:T(2,128)(2,1)} %reshape.293), calls=%async_computation.3 | async-start | bytes 4194304 | tf_op jit(solution)/shard_map/all_to_all | solution.py:130
  591.5 7.8 copy-start.14
  599.3 7.0 copy-start.8
  603.7 5.0 copy-start.4
  606.3 2.4 copy-start.7
  821.1 9.2 copy-start.12
  830.3 8.2 copy-start.10
  838.5 8.2 copy-start.17
  1133.1 12.3 slice-start
  1133.1 12.3 copy-start.5
  1139.1 28.5 %all-to-all-start.6 = ((bf16[2,2,262144]{2,1,0:T(2,128)(2,1)}), bf16[2,2,262144]{2,1,0:T(2,128)(2,1)}, u32[]{:S(2)}, u32[]{:S(2)}) async-start(bf16[2,2,262144]{2,1,0:T(2,128)(2,1)} %reshape.301), calls=%async_computation.7 | async-start | bytes 4194304 | tf_op jit(solution)/shard_map/all_to_all | solution.py:143
  1216.3 3.8 copy-start.3
  1241.0 5.5 copy-start.1
Sparse Core Ops, SparseCore 0:
  483.7 30.1 reduce-scatter.1
where the time goes:
time: 1270 us; the launch traced here: 1250 us
  local copies, waits for them, and re-layouts  537 us (42%)
  waiting for transfers between devices  291 us (23%)
  blocking collectives  267 us (21%)
  other arithmetic  64.5 us (5%)
  matrix products  57.1 us (4%)
  starting transfers between devices  23.1 us (2%)
  between operations  14.3 us (1%)
    unnamed x57, local copies, waits for them, and re-layouts  208 us
    all_to_all x1, blocking collectives, fetch_terms(): lax.all_to_all(chosen, 'blk', split_axis=0, concat_axis=0, tiled=True)  189 us
    all_to_all x1, waiting for transfers between devices, fetch_terms(): lax.all_to_all(chosen, 'blk', split_axis=0, concat_axis=0, tiled=True)  179 us
    all_to_all x6, local copies, waits for them, and re-layouts, per_device(): lax.all_to_all(paired, 'chan', split_axis=2, concat_axis=3, tiled=True)  107 us
    all_to_all x1, blocking collectives, per_device(): lax.all_to_all(paired, 'chan', split_axis=2, concat_axis=3, tiled=True)  53.9 us
    transpose x2, local copies, waits for them, and re-layouts, project(): return (jnp.transpose(paired, (0, 1, 4, 2, 3)), gate_logit)  46.2 us
    all_to_all x1, waiting for transfers between devices, per_device(): lax.all_to_all(paired, 'chan', split_axis=2, concat_axis=3, tiled=True)  44.4 us
    convert_element_type x4, local copies, waits for them, and re-layouts, finish(): normed = layer_norm(mixture, 1).astype(jnp.bfloat16)  35.1 us
  transfers between devices with their start and end apart: 5, of which 5 were waited for; matrix products, arithmetic and copies ran while one was open for 1% of the time, Pallas kernels for 0%

commit v1 on v0

v1 whole, which is shorter than its diff:
```python
import functools

import jax
import jax.numpy as jnp
from jax import lax
from jax.experimental import pallas as pl
from jax.experimental.pallas import tpu as pltpu
from jax.sharding import PartitionSpec as P

norm_epsilon = 1e-05
vmem_limit = 56 * 1024 * 1024


def sigmoid(values):
    return 0.5 + 0.5 * jnp.tanh(0.5 * values)


def layer_norm(values):
    average = jnp.mean(values, axis=-1, keepdims=True)
    centred = values - average
    variance = jnp.mean(centred * centred, axis=-1, keepdims=True)
    return centred * lax.rsqrt(variance + norm_epsilon)


def dot(a, b):
    return jnp.dot(a, b, preferred_element_type=jnp.float32)


def gated_pair(projected, mask, hidden):
    left = mask * sigmoid(projected[:, hidden : 2 * hidden]) * projected[:, :hidden]
    right = mask * sigmoid(projected[:, 3 * hidden : 4 * hidden]) * projected[:, 2 * hidden : 3 * hidden]
    return left.astype(jnp.bfloat16), right.astype(jnp.bfloat16)


def first_kernel(hidden, row_parts, ids, blocks, pair_ref, row_ref, col_ref, w_ref, gate_ref, left_ref, *rest):
    right_refs, (norm_ref, turned_ref) = rest[:row_parts], rest[row_parts:]
    _, rows, cols, channels = pair_ref.shape
    normed = layer_norm(pair_ref[0].reshape(rows * cols, channels).astype(jnp.float32))
    norm_ref[...] = normed
    gate = sigmoid(dot(normed.astype(jnp.bfloat16), w_ref[:, 4 * hidden :]))
    gate_ref[0] = gate.reshape(rows, cols, channels)
    for col in range(cols):
        turned_ref[col] = norm_ref[pl.ds(col, rows, stride=cols), :].astype(jnp.bfloat16)
    step = max(1, 128 // rows)
    part = rows // row_parts
    for start in range(0, cols, step):
        taken = turned_ref[start : start + step].reshape(step * rows, channels)
        projected = dot(taken, w_ref[:, : 4 * hidden])
        mask = col_ref[0, start : start + step, :][:, None, :] * row_ref[0][None, :, :]
        left, right = gated_pair(projected, mask.reshape(step * rows, -1), hidden)
        left_ref[0, start : start + step] = left.reshape(step, rows, hidden)
        right = right.reshape(step, rows, hidden)
        for p, right_ref in enumerate(right_refs):
            right_ref[0, start : start + step] = right[:, p * part : (p + 1) * part]


def first_operands(ids, blocks, pair, row_alive, col_alive, weights, hidden, row_parts):
    slots, rows, cols, channels = pair.shape
    n_rows = lax.axis_size("chan")
    n_cols = lax.axis_size("sub")
    part = rows // row_parts
    operand = jax.ShapeDtypeStruct((slots, cols, rows, hidden), jnp.bfloat16)
    right = jax.ShapeDtypeStruct((slots, cols, part, hidden), jnp.bfloat16)
    return pl.pallas_call(
        functools.partial(first_kernel, hidden, row_parts),
        grid_spec=pltpu.PrefetchScalarGridSpec(
            num_scalar_prefetch=2,
            grid=(slots,),
            in_specs=[
                pl.BlockSpec((1, rows, cols, channels), lambda s, ids, blocks: (s, 0, 0, 0)),
                pl.BlockSpec(
                    (1, rows, channels),
                    lambda s, ids, blocks: (blocks[2 * (ids[0] * slots + s)] * n_rows + ids[1], 0, 0),
                ),
                pl.BlockSpec(
                    (1, cols, channels),
                    lambda s, ids, blocks: (blocks[2 * (ids[0] * slots + s) + 1] * n_cols + ids[2], 0, 0),
                ),
                pl.BlockSpec(weights.shape, lambda s, ids, blocks: (0, 0)),
            ],
            out_specs=[
                pl.BlockSpec((1, rows, cols, channels), lambda s, ids, blocks: (s, 0, 0, 0)),
                pl.BlockSpec((1, cols, rows, hidden), lambda s, ids, blocks: (s, 0, 0, 0)),
            ]
            + [pl.BlockSpec((1, cols, part, hidden), lambda s, ids, blocks: (s, 0, 0, 0))] * row_parts,
            scratch_shapes=[
                pltpu.VMEM((rows * cols, channels), jnp.float32),
                pltpu.VMEM((cols, rows, channels), jnp.bfloat16),
            ],
        ),
        out_shape=[jax.ShapeDtypeStruct(pair.shape, jnp.float32), operand] + [right] * row_parts,
        compiler_params=pltpu.CompilerParams(vmem_limit_bytes=vmem_limit),
        name="first_operands",
    )(ids, blocks, pair, row_alive, col_alive, weights)


def product_kernel(shift, n_blk, width, capacity, pieces, n_refs, ids, owners, slots, *rest):
    refs = rest[:n_refs]
    out_ref, left_held, right_held, left_wide, right_wide, chosen, sems = rest[n_refs:]
    step = pl.program_id(0)
    turn = lax.rem(step, 2)
    depth, n_i, hidden = left_wide.shape
    n_j = right_wide.shape[1]

    @pl.when(step == 0)
    def _():
        target = lax.rem(ids[0] + shift, n_blk)
        for e in range(2 * capacity):
            chosen[e] = 0

        def scan(e, count):
            at = target * width + e
            here = jnp.logical_and(owners[at] == ids[0], count < capacity)

            @pl.when(here)
            def _():
                chosen[2 * count] = slots[2 * at]
                chosen[2 * count + 1] = slots[2 * at + 1]

            return count + here.astype(jnp.int32)

        lax.fori_loop(0, width, scan, jnp.int32(0))

    def copy(n, term, buffer, source):
        side, _, _, k0, depth_of, i0, size = pieces[n]
        held = (left_held, right_held)[side]
        return pltpu.make_async_copy(
            refs[source].at[chosen[2 * term + side]],
            held.at[buffer, pl.ds(k0, depth_of), pl.ds(i0, size), :],
            sems.at[buffer, n],
        )

    def start(term, buffer):
        for n, (_, on, off, *_) in enumerate(pieces):
            if on == off:
                copy(n, term, buffer, on).start()
            else:

                @pl.when(ids[3] == 1)
                def _(n=n, on=on):
                    copy(n, term, buffer, on).start()

                @pl.when(ids[3] == 0)
                def _(n=n, off=off):
                    copy(n, term, buffer, off).start()

    @pl.when(step == 0)
    def _():
        start(0, 0)

    @pl.when(step + 1 < capacity)
    def _():
        start(step + 1, 1 - turn)

    for n, piece in enumerate(pieces):
        copy(n, step, turn, piece[1]).wait()

    span = 8

    def widen(n, carry):
        at = pl.ds(n * span, span)
        left_wide[at] = left_held[turn, at].astype(jnp.float32)
        right_wide[at] = right_held[turn, at].astype(jnp.float32)
        return carry

    lax.fori_loop(0, depth // span, widen, 0)

    group = min(16, n_i)
    unroll = 4
    for i0 in range(0, n_i, group):

        def body(n, sums):
            for u in range(unroll):
                k = n * unroll + u
                right = right_wide[k]
                sums = tuple(
                    total + jnp.broadcast_to(left_wide[k, pl.ds(i0 + i, 1), :], (n_j, hidden)) * right
                    for i, total in enumerate(sums)
                )
            return sums

        zero = jnp.zeros((n_j, hidden), jnp.float32)
        sums = lax.fori_loop(0, depth // unroll, body, (zero,) * group)
        for i, total in enumerate(sums):
            out_ref[0, i0 + i] = total.astype(jnp.bfloat16)


def term_products(shift, ids, owners, slots, lefts, rights, capacity, width):
    n_blk = lax.axis_size("blk")
    refs, pieces = [], []

    def index_of(array):
        for n, known in enumerate(refs):
            if known is array:
                return n
        refs.append(array)
        return len(refs) - 1

    for side, operands in ((0, lefts), (1, rights)):
        for on, off, k0, i0 in operands:
            pieces.append((side, index_of(on), index_of(off), k0, on.shape[1], i0, on.shape[2]))
    hidden = lefts[0][0].shape[3]
    n_i = max(p[5] + p[6] for p in pieces if p[0] == 0)
    n_j = max(p[5] + p[6] for p in pieces if p[0] == 1)
    depth = max(p[3] + p[4] for p in pieces)
    return pl.pallas_call(
        functools.partial(product_kernel, shift, n_blk, width, capacity, tuple(pieces), len(refs)),
        grid_spec=pltpu.PrefetchScalarGridSpec(
            num_scalar_prefetch=3,
            grid=(capacity,),
            in_specs=[pl.BlockSpec(memory_space=pl.ANY)] * len(refs),
            out_specs=pl.BlockSpec((1, n_i, n_j, hidden), lambda t, *_: (t, 0, 0, 0)),
            scratch_shapes=[
                pltpu.VMEM((2, depth, n_i, hidden), jnp.bfloat16),
                pltpu.VMEM((2, depth, n_j, hidden), jnp.bfloat16),
                pltpu.VMEM((depth, n_i, hidden), jnp.float32),
                pltpu.VMEM((depth, n_j, hidden), jnp.float32),
                pltpu.SMEM((2 * capacity,), jnp.int32),
                pltpu.SemaphoreType.DMA((2, len(pieces))),
            ],
        ),
        out_shape=jax.ShapeDtypeStruct((capacity, n_i, n_j, hidden), jnp.bfloat16),
        compiler_params=pltpu.CompilerParams(vmem_limit_bytes=vmem_limit),
        cost_estimate=pl.CostEstimate(
            flops=2 * capacity * n_i * n_j * depth * hidden * 100,
            bytes_accessed=capacity * (depth * (n_i + n_j) + n_i * n_j) * hidden * 2,
            transcendentals=0,
        ),
        name="term_products",
    )(ids, owners, slots, *refs)


def home_kernel(last, hidden, n_blk, width, capacity, terms, ids, blocks, owners, *rest):
    parts, rest = rest[:n_blk], rest[n_blk:]
    if last:
        cur_ref, gate_ref, w_out_ref = rest[:3]
        rest = rest[3:]
        if len(rest) == 6:
            rest = rest[1:]
        out_ref, held, place, seen, sems = rest
    else:
        cur_ref, gate_ref, w_out_ref, row_ref, col_ref, w_ref = rest[:6]
        out_ref, next_gate_ref, left_ref, right_ref, held, place, seen, sems = rest[6:]
    step = pl.program_id(0)

    @pl.when(step == 0)
    def _():
        for shift in range(n_blk):
            pltpu.make_async_copy(
                parts[shift], held.at[pl.ds(shift * capacity, capacity)], sems.at[shift]
            ).start()
            seen[shift] = 0

        def scan(e, carry):
            owner = owners[ids[0] * width + e]
            shift = lax.rem(ids[0] - owner + n_blk, n_blk)
            count = seen[owner]
            seen[owner] = count + 1
            place[e] = shift * capacity + count
            return carry

        lax.fori_loop(0, width, scan, jnp.int32(0))
        for shift in range(n_blk):
            pltpu.make_async_copy(
                parts[shift], held.at[pl.ds(shift * capacity, capacity)], sems.at[shift]
            ).wait()

    _, rows, cols, channels = cur_ref.shape
    group = max(1, 128 // cols)
    for start in range(0, rows, group):
        at = pl.ds(start, group)
        total = held[place[step * terms], at].astype(jnp.float32)
        for t in range(1, terms):
            total = total + held[place[step * terms + t], at].astype(jnp.float32)
        mixture = total.astype(jnp.bfloat16).astype(jnp.float32).reshape(group * cols, hidden)
        update = dot(layer_norm(mixture).astype(jnp.bfloat16), w_out_ref[...])
        current = cur_ref[0, at].astype(jnp.float32).reshape(group * cols, channels)
        gate = gate_ref[0, at].reshape(group * cols, channels)
        result = (current + gate * update).astype(jnp.bfloat16)
        out_ref[0, at] = result.reshape(group, cols, channels)
        if not last:
            normed = layer_norm(result.astype(jnp.float32)).astype(jnp.bfloat16)
            projected = dot(normed, w_ref[...])
            next_gate_ref[0, at] = sigmoid(projected[:, 4 * hidden :]).reshape(group, cols, channels)
            mask = row_ref[0, start : start + group, :][:, None, :] * col_ref[0][None, :, :]
            left, right = gated_pair(projected, mask.reshape(group * cols, channels), hidden)
            left_ref[0, at] = left.reshape(group, cols, hidden)
            right_ref[0, at] = right.reshape(group, cols, hidden)


def home(parts, ids, blocks, owners, current, gate, w_out, capacity, terms, at, of, masks=None, w_in=None, into=None):
    n_blk = len(parts)
    slots, rows, _, channels = current.shape
    hidden = w_out.shape[0]
    cols = parts[0].shape[2]
    last = masks is None
    width = slots * terms
    n_rows, n_cols = lax.axis_size("chan"), lax.axis_size("sub")
    chunk = (1, rows, cols, channels)

    def chunk_spec(array):
        whole = array.shape[2] != cols
        return pl.BlockSpec(chunk, lambda s, *_: (s, 0, at if whole else 0, 0))

    in_specs = [pl.BlockSpec(memory_space=pl.ANY)] * n_blk + [
        chunk_spec(current),
        chunk_spec(gate),
        pl.BlockSpec(w_out.shape, lambda s, *_: (0, 0)),
    ]
    operands = [*parts, current, gate, w_out]
    aliases = {}
    if last:
        if into is not None:
            aliases = {3 + len(operands): 0}
            operands.append(into)
            in_specs.append(pl.BlockSpec(memory_space=pl.ANY))
        out_shape = [jax.ShapeDtypeStruct((slots, rows, cols * of, channels), jnp.bfloat16)]
        out_specs = [pl.BlockSpec(chunk, lambda s, *_: (s, 0, at, 0))]
    else:
        row_alive, col_alive = masks
        operands += [row_alive, col_alive, w_in]
        in_specs += [
            pl.BlockSpec(
                (1, rows, channels),
                lambda s, ids, blocks, owners: (blocks[2 * (ids[0] * slots + s)] * n_rows + ids[1], 0, 0),
            ),
            pl.BlockSpec(
                (1, cols, channels),
                lambda s, ids, blocks, owners: (blocks[2 * (ids[0] * slots + s) + 1] * n_cols + ids[2], at, 0),
            ),
            pl.BlockSpec(w_in.shape, lambda s, *_: (0, 0)),
        ]
        small = (slots, rows, cols, channels)
        out_shape = [
            jax.ShapeDtypeStruct(small, jnp.bfloat16),
            jax.ShapeDtypeStruct(small, jnp.float32),
            jax.ShapeDtypeStruct(small, jnp.bfloat16),
            jax.ShapeDtypeStruct(small, jnp.bfloat16),
        ]
        out_specs = [pl.BlockSpec(chunk, lambda s, *_: (s, 0, 0, 0))] * 4
    return pl.pallas_call(
        functools.partial(home_kernel, last, hidden, n_blk, width, capacity, terms),
        grid_spec=pltpu.PrefetchScalarGridSpec(
            num_scalar_prefetch=3,
            grid=(slots,),
            in_specs=in_specs,
            out_specs=out_specs,
            scratch_shapes=[
                pltpu.VMEM((n_blk * capacity, rows, cols, hidden), jnp.bfloat16),
                pltpu.SMEM((width,), jnp.int32),
                pltpu.SMEM((n_blk,), jnp.int32),
                pltpu.SemaphoreType.DMA((n_blk,)),
            ],
        ),
        out_shape=out_shape,
        input_output_aliases=aliases,
        compiler_params=pltpu.CompilerParams(vmem_limit_bytes=vmem_limit),
        cost_estimate=pl.CostEstimate(
            flops=2 * slots * rows * cols * channels * 6 * channels * 10,
            bytes_accessed=slots * rows * cols * channels * 16,
            transcendentals=0,
        ),
        name="home",
    )(ids, blocks, owners, *operands)


def exchange_outgoing(left, rights, n_chan, n_sub):
    if n_chan == 2 and n_sub == 2:
        both = ("chan", "sub")
        other_left = lax.ppermute(left, "sub", [(0, 1), (1, 0)])
        lefts = [(other_left, left, 0, 0), (left, other_left, left.shape[1], 0)]
        chunks = []
        for right in rights:
            one = lax.ppermute(right, both, [(0, 2), (3, 1), (1, 0), (2, 3)])
            two = lax.ppermute(right, both, [(1, 2), (2, 1)])
            chunks.append([(one, one, 0, 0), (right, two, right.shape[1], 0)])
        return lefts, chunks
    left = lax.all_gather(left, "sub", axis=1, tiled=True)
    right = jnp.concatenate(rights, axis=2)
    right = lax.all_gather(right, "chan", axis=2, tiled=True)
    right = lax.all_to_all(right, "sub", split_axis=2, concat_axis=1, tiled=True)
    cols = right.shape[2] // 2
    chunks = [right[:, :, :cols], right[:, :, cols:]]
    return [(left, left, 0, 0)], [[(r, r, 0, 0)] for r in chunks]


def exchange_incoming(lefts, rights, n_chan, n_sub):
    if n_chan == 2 and n_sub == 2:
        both = ("chan", "sub")
        left_pieces, chunks = [], []
        at = 0
        for left, right in zip(lefts, rights):
            depth = left.shape[1]
            one = lax.ppermute(left, both, [(1, 3), (2, 0), (0, 1), (3, 2)])
            two = lax.ppermute(one, both, [(0, 1), (3, 2)])
            left_pieces += [(left, one, 0, at), (one, two, depth, at)]
            other = lax.ppermute(right, "chan", [(0, 1), (1, 0)])
            chunks.append([(right, right, 0, 0), (other, other, depth, 0)])
            at += left.shape[2]
        return left_pieces, chunks
    left = lax.all_gather(jnp.concatenate(lefts, axis=2), "chan", axis=1, tiled=True)
    left = lax.all_gather(left, "sub", axis=2, tiled=True)
    size = left.shape[2] // n_chan
    left = lax.dynamic_slice_in_dim(left, lax.axis_index("chan") * size, size, 2)
    gathered = [lax.all_gather(right, "chan", axis=1, tiled=True) for right in rights]
    return [(left, left, 0, 0)], [[(r, r, 0, 0)] for r in gathered]


def per_device(pair, block_list, term_owner, term_slots, chain_ids, w_in, w_out):
    n_blk = lax.axis_size("blk")
    n_chan = lax.axis_size("chan")
    n_sub = lax.axis_size("sub")
    position = lax.axis_index("blk")
    row_group = lax.axis_index("chan")
    col_group = lax.axis_index("sub")
    slots, rows, cols, channels = pair.shape
    hidden = w_out.shape[1]
    terms = term_owner.shape[1]
    width = slots * terms
    capacity = max(2, -(-width // n_blk))
    fast = n_chan == 2 and n_sub == 2
    on_diagonal = (row_group == col_group).astype(jnp.int32)
    ids = jnp.stack([position, row_group, col_group, on_diagonal]).astype(jnp.int32)
    blocks = block_list.reshape(-1)
    owners = term_owner.reshape(-1)
    slot_of = term_slots.reshape(-1)
    alive = (chain_ids >= 0).astype(jnp.float32)

    def spread(size):
        return jnp.broadcast_to(alive.reshape(-1, size, 1), (alive.shape[0] // size, size, channels))

    row_alive, col_alive = spread(rows), spread(cols)
    shifts = [n_blk // 2] + [s for s in range(1, n_blk) if s != n_blk // 2] + [0]

    def all_products(lefts, right):
        parts = [None] * n_blk
        for shift in shifts:
            made = term_products(shift, ids, owners, slot_of, lefts, right, capacity, width)
            if shift:
                pairs = [(p, (p + shift) % n_blk) for p in range(n_blk)]
                made = lax.ppermute(made, "blk", pairs)
            parts[shift] = made
        return parts

    gate, left, *rights = first_operands(
        ids, blocks, pair, row_alive, col_alive, w_in[0], hidden, 2 if fast else 1
    )
    lefts, chunks = exchange_outgoing(left, rights, n_chan, n_sub)
    count = len(chunks)
    made = [all_products(lefts, right) for right in chunks]
    homes = [
        home(parts, ids, blocks, owners, pair, gate, w_out[0], capacity, terms, at, count, (row_alive, col_alive), w_in[1])
        for at, parts in enumerate(made)
    ]
    lefts, chunks = exchange_incoming([h[2] for h in homes], [h[3] for h in homes], n_chan, n_sub)
    made = [all_products(lefts, right) for right in chunks]
    out = None
    for at, parts in enumerate(made):
        (out,) = home(
            parts, ids, blocks, owners, homes[at][0], homes[at][1], w_out[1], capacity, terms, at, count, into=out
        )
    return out


def solution(mesh):
    in_specs = (
        P(("groups", "blk"), "chan", "sub", None),
        P("groups", None),
        P("groups", None),
        P("groups", None, None),
        P("groups"),
        P(),
        P(),
    )
    out_specs = P(("groups", "blk"), "chan", "sub", None)
    return jax.shard_map(
        per_device, mesh=mesh, in_specs=in_specs, out_specs=out_specs, check_vma=False
    )
```

time: 1270 us -> 358 us (0.28)
  local copies, waits for them, and re-layouts: 537 us -> 16.9 us
  blocking collectives: 267 us -> 0 us
  Pallas kernels: 0 us -> 216 us
  waiting for transfers between devices: 291 us -> 87.2 us
  other arithmetic: 64.5 us -> 1.34 us
  matrix products: 57.1 us -> 0 us
  between operations: 14.3 us -> 0.41 us
    all_to_all x4 -> x0, blocking collectives: 267 us -> none  [the longest x1 189 us: fetch_terms(): lax.all_to_all(chosen, 'blk', split_axis=0, concat_axis=0, tiled=True)]
    all_to_all x4 -> x0, waiting for transfers between devices: 260 us -> none  [the longest x1 179 us: fetch_terms(): lax.all_to_all(chosen, 'blk', split_axis=0, concat_axis=0, tiled=True)]
    pallas_call x0 -> x21, Pallas kernels: none -> 216 us  [the longest x16 148 us: term_products(): pl.pallas_call(functools.partial(product_kernel, shift, n_blk, width, cap...]
    unnamed x57 -> x55, local copies, waits for them, and re-layouts: 208 us -> 10.5 us
    all_to_all x12 -> x0, local copies, waits for them, and re-layouts: 162 us -> none  [the longest x6 107 us: per_device(): lax.all_to_all(paired, 'chan', split_axis=2, concat_axis=3, tiled=True)]
    ppermute x0 -> x23, waiting for transfers between devices: none -> 87.2 us  [the longest x12 35.5 us: all_products(): made = lax.ppermute(made, 'blk', pairs)]
    gather x10 -> x0, local copies, waits for them, and re-layouts: 62.6 us -> none  [the longest x4 32.9 us: fetch_terms(): chosen = jnp.stack([spread[send_left, 0], spread[send_right, 1]], axis=1)]
    dot_general x10 -> x0, matrix products: 57.1 us -> none  [the longest x4 33.7 us: term_product(): jnp.einsum('...hki,...hkj->...hij', left_part, right_part, preferred_elem...]
  transfers between devices with their start and end apart: 5 -> 23, of which waited for: 5 -> 5; matrix products, arithmetic and copies ran while one was open for 1% -> 1% of each run, Pallas kernels for 0% -> 55%
where the time goes in v1:
time: 358 us; the launch traced here: 354 us
  Pallas kernels  216 us (60%)
  waiting for transfers between devices  87.2 us (24%)
  starting transfers between devices  32.5 us (9%)
  local copies, waits for them, and re-layouts  16.9 us (5%)
    pallas_call x16, Pallas kernels, term_products(): pl.pallas_call(functools.partial(product_kernel, shift, n_blk, width, cap...  148 us
    pallas_call x4, Pallas kernels, home(): pl.pallas_call(functools.partial(home_kernel, last, hidden, n_blk, width,...  56.2 us
    ppermute x12, waiting for transfers between devices, all_products(): made = lax.ppermute(made, 'blk', pairs)  35.5 us
    ppermute x2, waiting for transfers between devices, exchange_incoming(): one = lax.ppermute(left, both, [(1, 3), (2, 0), (0, 1), (3, 2)])  18.5 us
    ppermute x2, waiting for transfers between devices, exchange_outgoing(): one = lax.ppermute(right, both, [(0, 2), (3, 1), (1, 0), (2, 3)])  18.5 us
    ppermute x12, starting transfers between devices, all_products(): made = lax.ppermute(made, 'blk', pairs)  15.4 us
    ppermute x2, waiting for transfers between devices, exchange_incoming(): other = lax.ppermute(right, 'chan', [(0, 1), (1, 0)])  14.6 us
    pallas_call x1, Pallas kernels, first_operands(): pl.pallas_call(functools.partial(first_kernel, hidden, row_parts), grid_s...  11.5 us
  transfers between devices with their start and end apart: 23, of which 5 were waited for; matrix products, arithmetic and copies ran while one was open for 1% of the time, Pallas kernels for 55%

profile of v1, /device:TPU:11, one launch (start us, length us, event | category | flops | bytes accessed | tf_op | source)
XLA Modules:
  0.0 354.4 jit_solution(14503719609701511457)
XLA Ops:
  6.5 11.5 %first_operands.1 = (f32[8,32,32,128]{3,2,1,0:T(8,128)}, bf16[8,32,32,128]{3,2,1,0:T(8,128)(2,1)}, bf16[8,32,16,128]{3,2,1,0:T(8,128)(2,1)}, bf16[8,32,16,128]{3,2,1,0:T(8,128)(2,1)}) custom-call(s32[4]{0:T(128)} %pad_add_fusion.ids, s32[64]{0:T(128)} %reshape.12.blocks, bf16[8,32,32,128]{3,2,1,0:T(8,128)(2,1)} %rest_4_.3, ...), custom_call_target="tpu_custom_call" | custom-call | tf_op jit(solution)/shard_map/first_operands/pallas_call | solution.py:64
  19.4 2.6 collective-permute-start.1
  26.7 18.5 %collective-permute-done.1.rest_2_ = bf16[8,32,16,128]{3,2,1,0:T(8,128)(2,1)} collective-permute-done((bf16[8,32,16,128]{3,2,1,0:T(8,128)(2,1)}, bf16[8,32,16,128]{3,2,1,0:T(8,128)(2,1)}, u32[]{:S(2)}, u32[]{:S(2)}) %collective-permute-start.1) | collective-permute-done | bytes 1048608 | tf_op jit(solution)/shard_map/ppermute | solution.py:374
  46.6 9.1 %term_products.17 = bf16[4,32,16,128]{3,2,1,0:T(8,128)(2,1)} custom-call(s32[4]{0:T(128)} %pad_add_fusion.ids, s32[64]{0:T(128)} %reshape.13.owners, s32[128]{0:T(128)} %reshape.14.slots, bf16[8,32,32,128]{3,2,1,0:T(8,128)(2,1)} %copy-done.3, bf16[8,32,32,128]{3,2,1,0:T(8,128)(2,1)} %get-tuple-element.17.rest_1_, ...), custom_call_target="tpu_custom_call" | custom-call | flops 3355443200 | bytes 3670016 | tf_op jit(solution)/shard_map/term_products/pallas_call | solution.py:206
  57.0 9.1 %term_products.18 = bf16[4,32,16,128]{3,2,1,0:T(8,128)(2,1)} custom-call(s32[4]{0:T(128)} %pad_add_fusion.ids, s32[64]{0:T(128)} %reshape.13.owners, s32[128]{0:T(128)} %reshape.14.slots, bf16[8,32,32,128]{3,2,1,0:T(8,128)(2,1)} %copy-done.3, bf16[8,32,32,128]{3,2,1,0:T(8,128)(2,1)} %get-tuple-element.17.rest_1_, ...), custom_call_target="tpu_custom_call" | custom-call | flops 3355443200 | bytes 3670016 | tf_op jit(solution)/shard_map/term_products/pallas_call | solution.py:206
  67.3 9.1 %term_products.21 = bf16[4,32,16,128]{3,2,1,0:T(8,128)(2,1)} custom-call(s32[4]{0:T(128)} %pad_add_fusion.ids, s32[64]{0:T(128)} %reshape.13.owners, s32[128]{0:T(128)} %reshape.14.slots, bf16[8,32,32,128]{3,2,1,0:T(8,128)(2,1)} %copy-done.3, bf16[8,32,32,128]{3,2,1,0:T(8,128)(2,1)} %get-tuple-element.17.rest_1_, ...), custom_call_target="tpu_custom_call" | custom-call | flops 3355443200 | bytes 3670016 | tf_op jit(solution)/shard_map/term_products/pallas_call | solution.py:206
  77.6 9.1 %term_products.22 = bf16[4,32,16,128]{3,2,1,0:T(8,128)(2,1)} custom-call(s32[4]{0:T(128)} %pad_add_fusion.ids, s32[64]{0:T(128)} %reshape.13.owners, s32[128]{0:T(128)} %reshape.14.slots, bf16[8,32,32,128]{3,2,1,0:T(8,128)(2,1)} %copy-done.3, bf16[8,32,32,128]{3,2,1,0:T(8,128)(2,1)} %get-tuple-element.17.rest_1_, ...), custom_call_target="tpu_custom_call" | custom-call | flops 3355443200 | bytes 3670016 | tf_op jit(solution)/shard_map/term_products/pallas_call | solution.py:206
  86.7 2.4 collective-permute-start.11
  89.1 9.1 %term_products.23 = bf16[4,32,16,128]{3,2,1,0:T(8,128)(2,1)} custom-call(s32[4]{0:T(128)} %pad_add_fusion.ids, s32[64]{0:T(128)} %reshape.13.owners, s32[128]{0:T(128)} %reshape.14.slots, bf16[8,32,32,128]{3,2,1,0:T(8,128)(2,1)} %copy-done.3, bf16[8,32,32,128]{3,2,1,0:T(8,128)(2,1)} %get-tuple-element.17.rest_1_, ...), custom_call_target="tpu_custom_call" | custom-call | flops 3355443200 | bytes 3670016 | tf_op jit(solution)/shard_map/term_products/pallas_call | solution.py:206
  98.4 9.1 %term_products.20.rest_0_ = bf16[4,32,16,128]{3,2,1,0:T(8,128)(2,1)} custom-call(s32[4]{0:T(128)} %pad_add_fusion.ids, s32[64]{0:T(128)} %reshape.13.owners, s32[128]{0:T(128)} %reshape.14.slots, bf16[8,32,32,128]{3,2,1,0:T(8,128)(2,1)} %copy-done.3, bf16[8,32,32,128]{3,2,1,0:T(8,128)(2,1)} %get-tuple-element.17.rest_1_, ...), custom_call_target="tpu_custom_call" | custom-call | flops 3355443200 | bytes 3670016 | tf_op jit(solution)/shard_map/term_products/pallas_call | solution.py:206
  107.5 9.1 %term_products.19 = bf16[4,32,16,128]{3,2,1,0:T(8,128)(2,1)} custom-call(s32[4]{0:T(128)} %pad_add_fusion.ids, s32[64]{0:T(128)} %reshape.13.owners, s32[128]{0:T(128)} %reshape.14.slots, bf16[8,32,32,128]{3,2,1,0:T(8,128)(2,1)} %copy-done.3, bf16[8,32,32,128]{3,2,1,0:T(8,128)(2,1)} %get-tuple-element.17.rest_1_, ...), custom_call_target="tpu_custom_call" | custom-call | flops 3355443200 | bytes 3670016 | tf_op jit(solution)/shard_map/term_products/pallas_call | solution.py:206
  116.6 9.2 %term_products.16.rest_0_ = bf16[4,32,16,128]{3,2,1,0:T(8,128)(2,1)} custom-call(s32[4]{0:T(128)} %pad_add_fusion.ids, s32[64]{0:T(128)} %reshape.13.owners, s32[128]{0:T(128)} %reshape.14.slots, bf16[8,32,32,128]{3,2,1,0:T(8,128)(2,1)} %copy-done.3, bf16[8,32,32,128]{3,2,1,0:T(8,128)(2,1)} %get-tuple-element.17.rest_1_, ...), custom_call_target="tpu_custom_call" | custom-call | flops 3355443200 | bytes 3670016 | tf_op jit(solution)/shard_map/term_products/pallas_call | solution.py:206
  127.0 19.8 %collective-permute-done.11.rest_2_ = bf16[4,32,16,128]{3,2,1,0:T(8,128)(2,1)S(1)} collective-permute-done((bf16[4,32,16,128]{3,2,1,0:T(8,128)(2,1)}, bf16[4,32,16,128]{3,2,1,0:T(8,128)(2,1)S(1)}, u32[]{:S(2)}, u32[]{:S(2)}) %collective-permute-start.11) | collective-permute-done | bytes 524320 | tf_op jit(solution)/shard_map/ppermute | solution.py:441
  147.9 18.8 %home.5 = (bf16[8,32,16,128]{3,2,1,0:T(8,128)(2,1)}, f32[8,32,16,128]{3,2,1,0:T(8,128)}, bf16[8,32,16,128]{3,2,1,0:T(8,128)(2,1)}, bf16[8,32,16,128]{3,2,1,0:T(8,128)(2,1)}) custom-call(s32[4]{0:T(128)} %pad_add_fusion.ids, s32[64]{0:T(128)} %reshape.12.blocks, s32[64]{0:T(128)} %reshape.13.owners, bf16[4,32,16,128]{3,2,1,0:T(8,128)(2,1)} %term_products.20.rest_0_, ...), custom_call_target="tpu_custom_call" | custom-call | flops 8053063680 | bytes 8388608 | tf_op jit(solution)/shard_map/home/pallas_call | solution.py:341
  169.9 18.8 %home.4 = (bf16[8,32,16,128]{3,2,1,0:T(8,128)(2,1)}, f32[8,32,16,128]{3,2,1,0:T(8,128)}, bf16[8,32,16,128]{3,2,1,0:T(8,128)(2,1)}, bf16[8,32,16,128]{3,2,1,0:T(8,128)(2,1)}) custom-call(s32[4]{0:T(128)} %pad_add_fusion.ids, s32[64]{0:T(128)} %reshape.12.blocks, s32[64]{0:T(128)} %reshape.13.owners, bf16[4,32,16,128]{3,2,1,0:T(8,128)(2,1)} %term_products.16.rest_0_, ...), custom_call_target="tpu_custom_call" | custom-call | flops 8053063680 | bytes 8388608 | tf_op jit(solution)/shard_map/home/pallas_call | solution.py:341
  188.7 2.2 collective-permute-start.6
  193.0 18.5 %collective-permute-done.6.rest_1_ = bf16[8,32,16,128]{3,2,1,0:T(8,128)(2,1)S(1)} collective-permute-done((bf16[8,32,16,128]{3,2,1,0:T(8,128)(2,1)}, bf16[8,32,16,128]{3,2,1,0:T(8,128)(2,1)S(1)}, u32[]{:S(2)}, u32[]{:S(2)}) %collective-permute-start.6) | collective-permute-done | bytes 1048608 | tf_op jit(solution)/shard_map/ppermute | solution.py:394
  211.5 4.8 %collective-permute-start.7 = (bf16[8,32,16,128]{3,2,1,0:T(8,128)(2,1)S(1)}, bf16[8,32,16,128]{3,2,1,0:T(8,128)(2,1)S(1)}, u32[]{:S(2)}, u32[]{:S(2)}) collective-permute-start(bf16[8,32,16,128]{3,2,1,0:T(8,128)(2,1)S(1)} %collective-permute-done.6.rest_1_), channel_id=1, source_target_pairs={{0,1},{3,2},{4,5},{7,6},{8,9},{11,10},{12,13},{15,14},{16,17},{19,... | collective-permute-start | bytes 3145736 | tf_op jit(solution)/shard_map/ppermute | solution.py:395
  216.4 14.6 %collective-permute-done.15.rest_7_ = bf16[8,32,16,128]{3,2,1,0:T(8,128)(2,1)S(1)} collective-permute-done((bf16[8,32,16,128]{3,2,1,0:T(8,128)(2,1)S(1)}, bf16[8,32,16,128]{3,2,1,0:T(8,128)(2,1)S(1)}, u32[]{:S(2)}, u32[]{:S(2)}) %collective-permute-start.15) | collective-permute-done | bytes 1048608 | tf_op jit(solution)/shard_map/ppermute | solution.py:397
  233.4 9.4 %term_products.25 = bf16[4,32,16,128]{3,2,1,0:T(8,128)(2,1)} custom-call(s32[4]{0:T(128)} %pad_add_fusion.ids, s32[64]{0:T(128)} %reshape.13.owners, s32[128]{0:T(128)} %reshape.14.slots, bf16[8,32,16,128]{3,2,1,0:T(8,128)(2,1)} %get-tuple-element.20.rest_0_, bf16[8,32,16,128]{3,2,1,0:T(8,128)(2,1)} %copy-done.7, bf16[8,32,16,128]{3,2,1,0:T(8,128)(2,1)} %copy-done.10, ...), custom_call_target="tpu_custom_call" | custom-call | flops 3355443200 | bytes 3670016 | tf_op jit(solution)/shard_map/term_products/pallas_call | solution.py:206
  242.9 9.4 %term_products.26 = bf16[4,32,16,128]{3,2,1,0:T(8,128)(2,1)} custom-call(s32[4]{0:T(128)} %pad_add_fusion.ids, s32[64]{0:T(128)} %reshape.13.owners, s32[128]{0:T(128)} %reshape.14.slots, bf16[8,32,16,128]{3,2,1,0:T(8,128)(2,1)} %get-tuple-element.20.rest_0_, bf16[8,32,16,128]{3,2,1,0:T(8,128)(2,1)} %copy-done.7, bf16[8,32,16,128]{3,2,1,0:T(8,128)(2,1)} %copy-done.10, ...), custom_call_target="tpu_custom_call" | custom-call | flops 3355443200 | bytes 3670016 | tf_op jit(solution)/shard_map/term_products/pallas_call | solution.py:206
  252.3 3.1 collective-permute-start.17
  256.3 9.4 %term_products.29 = bf16[4,32,16,128]{3,2,1,0:T(8,128)(2,1)} custom-call(s32[4]{0:T(128)} %pad_add_fusion.ids, s32[64]{0:T(128)} %reshape.13.owners, s32[128]{0:T(128)} %reshape.14.slots, bf16[8,32,16,128]{3,2,1,0:T(8,128)(2,1)} %get-tuple-element.20.rest_0_, bf16[8,32,16,128]{3,2,1,0:T(8,128)(2,1)} %copy-done.7, bf16[8,32,16,128]{3,2,1,0:T(8,128)(2,1)} %copy-done.10, ...), custom_call_target="tpu_custom_call" | custom-call | flops 3355443200 | bytes 3670016 | tf_op jit(solution)/shard_map/term_products/pallas_call | solution.py:206
  266.1 9.4 %term_products.30 = bf16[4,32,16,128]{3,2,1,0:T(8,128)(2,1)} custom-call(s32[4]{0:T(128)} %pad_add_fusion.ids, s32[64]{0:T(128)} %reshape.13.owners, s32[128]{0:T(128)} %reshape.14.slots, bf16[8,32,16,128]{3,2,1,0:T(8,128)(2,1)} %get-tuple-element.20.rest_0_, bf16[8,32,16,128]{3,2,1,0:T(8,128)(2,1)} %copy-done.7, bf16[8,32,16,128]{3,2,1,0:T(8,128)(2,1)} %copy-done.10, ...), custom_call_target="tpu_custom_call" | custom-call | flops 3355443200 | bytes 3670016 | tf_op jit(solution)/shard_map/term_products/pallas_call | solution.py:206
  275.5 3.3 collective-permute-start.21
  278.8 9.4 %term_products.31 = bf16[4,32,16,128]{3,2,1,0:T(8,128)(2,1)} custom-call(s32[4]{0:T(128)} %pad_add_fusion.ids, s32[64]{0:T(128)} %reshape.13.owners, s32[128]{0:T(128)} %reshape.14.slots, bf16[8,32,16,128]{3,2,1,0:T(8,128)(2,1)} %get-tuple-element.20.rest_0_, bf16[8,32,16,128]{3,2,1,0:T(8,128)(2,1)} %copy-done.7, bf16[8,32,16,128]{3,2,1,0:T(8,128)(2,1)} %copy-done.10, ...), custom_call_target="tpu_custom_call" | custom-call | flops 3355443200 | bytes 3670016 | tf_op jit(solution)/shard_map/term_products/pallas_call | solution.py:206
  288.3 9.4 %term_products.28.rest_0_ = bf16[4,32,16,128]{3,2,1,0:T(8,128)(2,1)} custom-call(s32[4]{0:T(128)} %pad_add_fusion.ids, s32[64]{0:T(128)} %reshape.13.owners, s32[128]{0:T(128)} %reshape.14.slots, bf16[8,32,16,128]{3,2,1,0:T(8,128)(2,1)} %get-tuple-element.20.rest_0_, bf16[8,32,16,128]{3,2,1,0:T(8,128)(2,1)} %copy-done.7, ...), custom_call_target="tpu_custom_call" | custom-call | flops 3355443200 | bytes 3670016 | tf_op jit(solution)/shard_map/term_products/pallas_call | solution.py:206
  297.7 9.4 %term_products.27 = bf16[4,32,16,128]{3,2,1,0:T(8,128)(2,1)} custom-call(s32[4]{0:T(128)} %pad_add_fusion.ids, s32[64]{0:T(128)} %reshape.13.owners, s32[128]{0:T(128)} %reshape.14.slots, bf16[8,32,16,128]{3,2,1,0:T(8,128)(2,1)} %get-tuple-element.20.rest_0_, bf16[8,32,16,128]{3,2,1,0:T(8,128)(2,1)} %copy-done.7, bf16[8,32,16,128]{3,2,1,0:T(8,128)(2,1)} %copy-done.10, ...), custom_call_target="tpu_custom_call" | custom-call | flops 3355443200 | bytes 3670016 | tf_op jit(solution)/shard_map/term_products/pallas_call | solution.py:206
  307.1 9.5 %term_products.24.rest_0_ = bf16[4,32,16,128]{3,2,1,0:T(8,128)(2,1)} custom-call(s32[4]{0:T(128)} %pad_add_fusion.ids, s32[64]{0:T(128)} %reshape.13.owners, s32[128]{0:T(128)} %reshape.14.slots, bf16[8,32,16,128]{3,2,1,0:T(8,128)(2,1)} %get-tuple-element.20.rest_0_, bf16[8,32,16,128]{3,2,1,0:T(8,128)(2,1)} %copy-done.7, ...), custom_call_target="tpu_custom_call" | custom-call | flops 3355443200 | bytes 3670016 | tf_op jit(solution)/shard_map/term_products/pallas_call | solution.py:206
  317.9 15.7 %collective-permute-done.21.rest_2_ = bf16[4,32,16,128]{3,2,1,0:T(8,128)(2,1)S(1)} collective-permute-done((bf16[4,32,16,128]{3,2,1,0:T(8,128)(2,1)}, bf16[4,32,16,128]{3,2,1,0:T(8,128)(2,1)S(1)}, u32[]{:S(2)}, u32[]{:S(2)}) %collective-permute-start.21) | collective-permute-done | bytes 524320 | tf_op jit(solution)/shard_map/ppermute | solution.py:441
  334.6 9.3 %home.6.rest_7_ = bf16[8,32,32,128]{3,2,1,0:T(8,128)(2,1)} custom-call(s32[4]{0:T(128)} %pad_add_fusion.ids, s32[64]{0:T(128)} %reshape.12.blocks, s32[64]{0:T(128)} %reshape.13.owners, bf16[4,32,16,128]{3,2,1,0:T(8,128)(2,1)} %term_products.28.rest_0_, bf16[4,32,16,128]{3,2,1,0:T(8,128)(2,1)} %copy-done.18, bf16[4,32,16,128]{3,2,1,0:T(8,128)(2,1)} %copy-done.21, ...), custom_call_target="tpu_custom_call" | custom-call | flops 8053063680 | bytes 8388608 | tf_op jit(solution)/shard_map/home/pallas_call | solution.py:341
  345.1 9.3 %home.7 = bf16[8,32,32,128]{3,2,1,0:T(8,128)(2,1)} custom-call(s32[4]{0:T(128)} %pad_add_fusion.ids, s32[64]{0:T(128)} %reshape.12.blocks, s32[64]{0:T(128)} %reshape.13.owners, bf16[4,32,16,128]{3,2,1,0:T(8,128)(2,1)} %term_products.24.rest_0_, bf16[4,32,16,128]{3,2,1,0:T(8,128)(2,1)} %copy-done.14, ...), custom_call_target="tpu_custom_call", output_to_operand_aliasing={{}: (10, {})} | custom-call | flops 8053063680 | bytes 8388608 | tf_op jit(solution)/shard_map/home/pallas_call | solution.py:341
  (99 shorter events, 32.4 us)
Async XLA Ops:
  6.5 18.0 %copy-start.2 = (s32[32,2]{0,1:T(2,128)S(1)}, s32[32,2]{0,1:T(2,128)}, u32[]{:S(2)}) copy-start(s32[32,2]{0,1:T(2,128)} %param.9) | copy-start | bytes 772
  6.5 18.8 %copy-start.1 = (s32[32,2,2]{0,2,1:T(2,128)S(1)}, s32[32,2,2]{0,2,1:T(2,128)}, u32[]{:S(2)}) copy-start(s32[32,2,2]{0,2,1:T(2,128)} %param.10) | copy-start | bytes 1540
  6.5 19.6 %copy-start = (bf16[2,128,128]{2,1,0:T(8,128)(2,1)S(1)}, bf16[2,128,128]{2,1,0:T(8,128)(2,1)}, u32[]{:S(2)}) copy-start(bf16[2,128,128]{2,1,0:T(8,128)(2,1)} %param.13) | copy-start | bytes 196612
  18.0 27.2 %collective-permute-start = (bf16[8,32,32,128]{3,2,1,0:T(8,128)(2,1)}, bf16[8,32,32,128]{3,2,1,0:T(8,128)(2,1)S(1)}, u32[]{:S(2)}, u32[]{:S(2)}) collective-permute-start(bf16[8,32,32,128]{3,2,1,0:T(8,128)(2,1)} %get-tuple-element.17.rest_1_), channel_id=1, source_target_pairs={{0,1},{1,0},{2,3},{3,2},{4,5},{5,4},{6,7},{7,6},{8,9},{9,8},{10,11... | collective-permute-start | bytes 6291464 | tf_op jit(solution)/shard_map/ppermute | solution.py:370
  18.6 8.0 %collective-permute-start.2 = (bf16[8,32,16,128]{3,2,1,0:T(8,128)(2,1)}, bf16[8,32,16,128]{3,2,1,0:T(8,128)(2,1)S(1)}, u32[]{:S(2)}, u32[]{:S(2)}) collective-permute-start(bf16[8,32,16,128]{3,2,1,0:T(8,128)(2,1)} %get-tuple-element.18.rest_3_), channel_id=1, source_target_pairs={{1,2},{2,1},{5,6},{6,5},{9,10},{10,9},{13,14},{14,13},{17,18},{18,... | collective-permute-start | bytes 3145736 | tf_op jit(solution)/shard_map/ppermute | solution.py:375
  19.4 25.8 %collective-permute-start.1 = (bf16[8,32,16,128]{3,2,1,0:T(8,128)(2,1)}, bf16[8,32,16,128]{3,2,1,0:T(8,128)(2,1)}, u32[]{:S(2)}, u32[]{:S(2)}) collective-permute-start(bf16[8,32,16,128]{3,2,1,0:T(8,128)(2,1)} %get-tuple-element.18.rest_3_), channel_id=1, source_target_pairs={{0,2},{3,1},{1,0},{2,3},{4,6},{7,5},{5,4},{6,7},{8,10},{11,9},{9,8... | collective-permute-start | bytes 3145736 | tf_op jit(solution)/shard_map/ppermute | solution.py:374
  21.9 45.3 %collective-permute-start.9 = (bf16[8,32,16,128]{3,2,1,0:T(8,128)(2,1)}, bf16[8,32,16,128]{3,2,1,0:T(8,128)(2,1)}, u32[]{:S(2)}, u32[]{:S(2)}) collective-permute-start(bf16[8,32,16,128]{3,2,1,0:T(8,128)(2,1)} %get-tuple-element.21.rest_3_), channel_id=1, source_target_pairs={{1,2},{2,1},{5,6},{6,5},{9,10},{10,9},{13,14},{14,13},{17,18},{18,... | collective-permute-start | bytes 3145736 | tf_op jit(solution)/shard_map/ppermute | solution.py:375
  23.6 43.7 %collective-permute-start.8 = (bf16[8,32,16,128]{3,2,1,0:T(8,128)(2,1)}, bf16[8,32,16,128]{3,2,1,0:T(8,128)(2,1)}, u32[]{:S(2)}, u32[]{:S(2)}) collective-permute-start(bf16[8,32,16,128]{3,2,1,0:T(8,128)(2,1)} %get-tuple-element.21.rest_3_), channel_id=1, source_target_pairs={{0,2},{3,1},{1,0},{2,3},{4,6},{7,5},{5,4},{6,7},{8,10},{11,9},{9,8... | collective-permute-start | bytes 3145736 | tf_op jit(solution)/shard_map/ppermute | solution.py:374
  26.7 18.5 %copy-start.6 = (bf16[8,32,16,128]{3,2,1,0:T(8,128)(2,1)}, bf16[8,32,16,128]{3,2,1,0:T(8,128)(2,1)S(1)}, u32[]{:S(2)}) copy-start(bf16[8,32,16,128]{3,2,1,0:T(8,128)(2,1)S(1)} %collective-permute-done.2.rest_4_) | copy-start | bytes 3145732
  55.7 112.4 %collective-permute-start.3 = (bf16[4,32,16,128]{3,2,1,0:T(8,128)(2,1)}, bf16[4,32,16,128]{3,2,1,0:T(8,128)(2,1)S(1)}, u32[]{:S(2)}, u32[]{:S(2)}) collective-permute-start(bf16[4,32,16,128]{3,2,1,0:T(8,128)(2,1)} %term_products.17), channel_id=1, source_target_pairs={{0,4},{4,8},{8,12},{12,0},{1,5},{5,9},{9,13},{13,1},{2,6},{6,10},{... | collective-permute-start | bytes 1572872 | tf_op jit(solution)/shard_map/ppermute | solution.py:441
  66.2 101.9 %collective-permute-start.4 = (bf16[4,32,16,128]{3,2,1,0:T(8,128)(2,1)}, bf16[4,32,16,128]{3,2,1,0:T(8,128)(2,1)S(1)}, u32[]{:S(2)}, u32[]{:S(2)}) collective-permute-start(bf16[4,32,16,128]{3,2,1,0:T(8,128)(2,1)} %term_products.18), channel_id=1, source_target_pairs={{0,8},{4,12},{8,0},{12,4},{1,9},{5,13},{9,1},{13,5},{2,10},{6,14},... | collective-permute-start | bytes 1572872 | tf_op jit(solution)/shard_map/ppermute | solution.py:441
  76.4 49.5 %collective-permute-start.10 = (bf16[4,32,16,128]{3,2,1,0:T(8,128)(2,1)}, bf16[4,32,16,128]{3,2,1,0:T(8,128)(2,1)S(1)}, u32[]{:S(2)}, u32[]{:S(2)}) collective-permute-start(bf16[4,32,16,128]{3,2,1,0:T(8,128)(2,1)} %term_products.21), channel_id=1, source_target_pairs={{0,4},{4,8},{8,12},{12,0},{1,5},{5,9},{9,13},{13,1},{2,6},{6,10},{... | collective-permute-start | bytes 1572872 | tf_op jit(solution)/shard_map/ppermute | solution.py:441
  86.7 60.2 %collective-permute-start.11 = (bf16[4,32,16,128]{3,2,1,0:T(8,128)(2,1)}, bf16[4,32,16,128]{3,2,1,0:T(8,128)(2,1)S(1)}, u32[]{:S(2)}, u32[]{:S(2)}) collective-permute-start(bf16[4,32,16,128]{3,2,1,0:T(8,128)(2,1)} %term_products.22), channel_id=1, source_target_pairs={{0,8},{4,12},{8,0},{12,4},{1,9},{5,13},{9,1},{13,5},{2,10},{6,14},... | collective-permute-start | bytes 1572872 | tf_op jit(solution)/shard_map/ppermute | solution.py:441
  98.2 48.6 %collective-permute-start.12 = (bf16[4,32,16,128]{3,2,1,0:T(8,128)(2,1)}, bf16[4,32,16,128]{3,2,1,0:T(8,128)(2,1)S(1)}, u32[]{:S(2)}, u32[]{:S(2)}) collective-permute-start(bf16[4,32,16,128]{3,2,1,0:T(8,128)(2,1)} %term_products.23), channel_id=1, source_target_pairs={{0,12},{4,0},{8,4},{12,8},{1,13},{5,1},{9,5},{13,9},{2,14},{6,2},{... | collective-permute-start | bytes 1572872 | tf_op jit(solution)/shard_map/ppermute | solution.py:441
  125.9 21.0 %copy-start.19 = (bf16[4,32,16,128]{3,2,1,0:T(8,128)(2,1)}, bf16[4,32,16,128]{3,2,1,0:T(8,128)(2,1)S(1)}, u32[]{:S(2)}) copy-start(bf16[4,32,16,128]{3,2,1,0:T(8,128)(2,1)S(1)} %collective-permute-done.10.rest_1_) | copy-start | bytes 1572868
  125.9 42.2 %collective-permute-start.5 = (bf16[4,32,16,128]{3,2,1,0:T(8,128)(2,1)S(1)}, bf16[4,32,16,128]{3,2,1,0:T(8,128)(2,1)S(1)}, u32[]{:S(2)}, u32[]{:S(2)}) collective-permute-start(bf16[4,32,16,128]{3,2,1,0:T(8,128)(2,1)S(1)} %copy-done.17), channel_id=1, source_target_pairs={{0,12},{4,0},{8,4},{12,8},{1,13},{5,1},{9,5},{13,9},{2,14},{6,2},{... | collective-permute-start | bytes 1572872 | tf_op jit(solution)/shard_map/ppermute | solution.py:441
  166.7 24.2 %copy-start.4 = (bf16[8,32,16,128]{3,2,1,0:T(8,128)(2,1)S(1)}, bf16[8,32,16,128]{3,2,1,0:T(8,128)(2,1)}, u32[]{:S(2)}) copy-start(bf16[8,32,16,128]{3,2,1,0:T(8,128)(2,1)} %get-tuple-element.23.rest_6_) | copy-start | bytes 3145732
  166.7 24.2 %collective-permute-start.13 = (bf16[8,32,16,128]{3,2,1,0:T(8,128)(2,1)}, bf16[8,32,16,128]{3,2,1,0:T(8,128)(2,1)S(1)}, u32[]{:S(2)}, u32[]{:S(2)}) collective-permute-start(bf16[8,32,16,128]{3,2,1,0:T(8,128)(2,1)} %get-tuple-element.22.rest_3_), channel_id=1, source_target_pairs={{1,3},{2,0},{0,1},{3,2},{5,7},{6,4},{4,5},{7,6},{9,11},{10,8},{8,9... | collective-permute-start | bytes 3145736 | tf_op jit(solution)/shard_map/ppermute | solution.py:394
  188.7 22.8 %collective-permute-start.6 = (bf16[8,32,16,128]{3,2,1,0:T(8,128)(2,1)}, bf16[8,32,16,128]{3,2,1,0:T(8,128)(2,1)S(1)}, u32[]{:S(2)}, u32[]{:S(2)}) collective-permute-start(bf16[8,32,16,128]{3,2,1,0:T(8,128)(2,1)} %get-tuple-element.20.rest_0_), channel_id=1, source_target_pairs={{1,3},{2,0},{0,1},{3,2},{5,7},{6,4},{4,5},{7,6},{9,11},{10,8},{8,9... | collective-permute-start | bytes 3145736 | tf_op jit(solution)/shard_map/ppermute | solution.py:394
  190.9 40.2 %collective-permute-start.15 = (bf16[8,32,16,128]{3,2,1,0:T(8,128)(2,1)S(1)}, bf16[8,32,16,128]{3,2,1,0:T(8,128)(2,1)S(1)}, u32[]{:S(2)}, u32[]{:S(2)}) collective-permute-start(bf16[8,32,16,128]{3,2,1,0:T(8,128)(2,1)S(1)} %copy-done.4), channel_id=1, source_target_pairs={{0,2},{2,0},{1,3},{3,1},{4,6},{6,4},{5,7},{7,5},{8,10},{10,8},{9,1... | collective-permute-start | bytes 3145736 | tf_op jit(solution)/shard_map/ppermute | solution.py:397
  190.9 40.2 %copy-start.5 = (bf16[8,32,16,128]{3,2,1,0:T(8,128)(2,1)}, bf16[8,32,16,128]{3,2,1,0:T(8,128)(2,1)S(1)}, u32[]{:S(2)}) copy-start(bf16[8,32,16,128]{3,2,1,0:T(8,128)(2,1)S(1)} %collective-permute-done.13.rest_4_) | copy-start | bytes 3145732
  190.9 40.2 %collective-permute-start.14 = (bf16[8,32,16,128]{3,2,1,0:T(8,128)(2,1)S(1)}, bf16[8,32,16,128]{3,2,1,0:T(8,128)(2,1)S(1)}, u32[]{:S(2)}, u32[]{:S(2)}) collective-permute-start(bf16[8,32,16,128]{3,2,1,0:T(8,128)(2,1)S(1)} %collective-permute-done.13.rest_4_), channel_id=1, source_target_pairs={{0,1},{3,2},{4,5},{7,6},{8,9},{11,10},{12,13},{15,14},{16,17},{19,... | collective-permute-start | bytes 3145736 | tf_op jit(solution)/shard_map/ppermute | solution.py:395
  211.5 19.6 %copy-start.7 = (bf16[8,32,16,128]{3,2,1,0:T(8,128)(2,1)}, bf16[8,32,16,128]{3,2,1,0:T(8,128)(2,1)S(1)}, u32[]{:S(2)}) copy-start(bf16[8,32,16,128]{3,2,1,0:T(8,128)(2,1)S(1)} %collective-permute-done.6.rest_1_) | copy-start | bytes 3145732
  211.5 19.6 %collective-permute-start.7 = (bf16[8,32,16,128]{3,2,1,0:T(8,128)(2,1)S(1)}, bf16[8,32,16,128]{3,2,1,0:T(8,128)(2,1)S(1)}, u32[]{:S(2)}, u32[]{:S(2)}) collective-permute-start(bf16[8,32,16,128]{3,2,1,0:T(8,128)(2,1)S(1)} %collective-permute-done.6.rest_1_), channel_id=1, source_target_pairs={{0,1},{3,2},{4,5},{7,6},{8,9},{11,10},{12,13},{15,14},{16,17},{19,... | collective-permute-start | bytes 3145736 | tf_op jit(solution)/shard_map/ppermute | solution.py:395
  216.3 39.0 %collective-permute-start.19 = (bf16[8,32,16,128]{3,2,1,0:T(8,128)(2,1)}, bf16[8,32,16,128]{3,2,1,0:T(8,128)(2,1)S(1)}, u32[]{:S(2)}, u32[]{:S(2)}) collective-permute-start(bf16[8,32,16,128]{3,2,1,0:T(8,128)(2,1)} %get-tuple-element.26.rest_6_), channel_id=1, source_target_pairs={{0,2},{2,0},{1,3},{3,1},{4,6},{6,4},{5,7},{7,5},{8,10},{10,8},{9,1... | collective-permute-start | bytes 3145736 | tf_op jit(solution)/shard_map/ppermute | solution.py:397
  242.8 101.1 %collective-permute-start.16 = (bf16[4,32,16,128]{3,2,1,0:T(8,128)(2,1)}, bf16[4,32,16,128]{3,2,1,0:T(8,128)(2,1)S(1)}, u32[]{:S(2)}, u32[]{:S(2)}) collective-permute-start(bf16[4,32,16,128]{3,2,1,0:T(8,128)(2,1)} %term_products.25), channel_id=1, source_target_pairs={{0,4},{4,8},{8,12},{12,0},{1,5},{5,9},{9,13},{13,1},{2,6},{6,10},{... | collective-permute-start | bytes 1572872 | tf_op jit(solution)/shard_map/ppermute | solution.py:441
  252.3 91.6 %collective-permute-start.17 = (bf16[4,32,16,128]{3,2,1,0:T(8,128)(2,1)}, bf16[4,32,16,128]{3,2,1,0:T(8,128)(2,1)S(1)}, u32[]{:S(2)}, u32[]{:S(2)}) collective-permute-start(bf16[4,32,16,128]{3,2,1,0:T(8,128)(2,1)} %term_products.26), channel_id=1, source_target_pairs={{0,8},{4,12},{8,0},{12,4},{1,9},{5,13},{9,1},{13,5},{2,10},{6,14},... | collective-permute-start | bytes 1572872 | tf_op jit(solution)/shard_map/ppermute | solution.py:441
  265.7 50.9 %collective-permute-start.20 = (bf16[4,32,16,128]{3,2,1,0:T(8,128)(2,1)}, bf16[4,32,16,128]{3,2,1,0:T(8,128)(2,1)S(1)}, u32[]{:S(2)}, u32[]{:S(2)}) collective-permute-start(bf16[4,32,16,128]{3,2,1,0:T(8,128)(2,1)} %term_products.29), channel_id=1, source_target_pairs={{0,4},{4,8},{8,12},{12,0},{1,5},{5,9},{9,13},{13,1},{2,6},{6,10},{... | collective-permute-start | bytes 1572872 | tf_op jit(solution)/shard_map/ppermute | solution.py:441
  275.5 58.1 %collective-permute-start.21 = (bf16[4,32,16,128]{3,2,1,0:T(8,128)(2,1)}, bf16[4,32,16,128]{3,2,1,0:T(8,128)(2,1)S(1)}, u32[]{:S(2)}, u32[]{:S(2)}) collective-permute-start(bf16[4,32,16,128]{3,2,1,0:T(8,128)(2,1)} %term_products.30), channel_id=1, source_target_pairs={{0,8},{4,12},{8,0},{12,4},{1,9},{5,13},{9,1},{13,5},{2,10},{6,14},... | collective-permute-start | bytes 1572872 | tf_op jit(solution)/shard_map/ppermute | solution.py:441
  288.2 45.4 %collective-permute-start.22 = (bf16[4,32,16,128]{3,2,1,0:T(8,128)(2,1)}, bf16[4,32,16,128]{3,2,1,0:T(8,128)(2,1)S(1)}, u32[]{:S(2)}, u32[]{:S(2)}) collective-permute-start(bf16[4,32,16,128]{3,2,1,0:T(8,128)(2,1)} %term_products.31), channel_id=1, source_target_pairs={{0,12},{4,0},{8,4},{12,8},{1,13},{5,1},{9,5},{13,9},{2,14},{6,2},{... | collective-permute-start | bytes 1572872 | tf_op jit(solution)/shard_map/ppermute | solution.py:441
  316.7 16.9 %copy-start.18 = (bf16[4,32,16,128]{3,2,1,0:T(8,128)(2,1)}, bf16[4,32,16,128]{3,2,1,0:T(8,128)(2,1)S(1)}, u32[]{:S(2)}) copy-start(bf16[4,32,16,128]{3,2,1,0:T(8,128)(2,1)S(1)} %collective-permute-done.20.rest_1_) | copy-start | bytes 1572868
  316.7 27.3 %collective-permute-start.18 = (bf16[4,32,16,128]{3,2,1,0:T(8,128)(2,1)S(1)}, bf16[4,32,16,128]{3,2,1,0:T(8,128)(2,1)S(1)}, u32[]{:S(2)}, u32[]{:S(2)}) collective-permute-start(bf16[4,32,16,128]{3,2,1,0:T(8,128)(2,1)S(1)} %copy-done.20), channel_id=1, source_target_pairs={{0,12},{4,0},{8,4},{12,8},{1,13},{5,1},{9,5},{13,9},{2,14},{6,2},{... | collective-permute-start | bytes 1572872 | tf_op jit(solution)/shard_map/ppermute | solution.py:441
  (17 other events, 33.6 us)

commit v2 on v1

v2 whole, which is shorter than its diff:
```python
import functools

import jax
import jax.numpy as jnp
from jax import lax
from jax.experimental import pallas as pl
from jax.experimental.pallas import tpu as pltpu
from jax.sharding import PartitionSpec as P

norm_epsilon = 1e-05
vmem_limit = 56 * 1024 * 1024


def sigmoid(values):
    return 0.5 + 0.5 * jnp.tanh(0.5 * values)


def layer_norm(values):
    size = values.shape[1]
    ones = jnp.ones((2 * size, size), jnp.bfloat16)
    centred = values.astype(jnp.float32) - dot(values, ones[:size]) * (1.0 / size)
    squares = centred * centred
    high = squares.astype(jnp.bfloat16)
    low = (squares - high.astype(jnp.float32)).astype(jnp.bfloat16)
    variance = dot(jnp.concatenate([high, low], axis=1), ones) * (1.0 / size)
    return centred * lax.rsqrt(variance + norm_epsilon)


def alive_rows(chain_ref, start, size):
    lanes = chain_ref.shape[1]
    line = chain_ref[pl.ds(start // lanes, 1), :] >= 0
    spot = lax.broadcasted_iota(jnp.int32, (size, lanes), 0) + lax.rem(start, lanes)
    pick = jnp.logical_and(lax.broadcasted_iota(jnp.int32, (size, lanes), 1) == spot, line)
    return dot(pick.astype(jnp.float32).astype(jnp.bfloat16), jnp.ones((lanes, lanes), jnp.bfloat16))


def dot(a, b):
    return jnp.dot(a, b, preferred_element_type=jnp.float32)


def gated_pair(projected, mask, hidden):
    left = mask * sigmoid(projected[:, hidden : 2 * hidden]) * projected[:, :hidden]
    right = mask * sigmoid(projected[:, 3 * hidden : 4 * hidden]) * projected[:, 2 * hidden : 3 * hidden]
    return left.astype(jnp.bfloat16), right.astype(jnp.bfloat16)


def first_kernel(hidden, row_parts, n_chan, n_sub, ids, blocks, pair_ref, chain_ref, w_ref, gate_ref, left_ref, *rest):
    right_refs, (norm_ref, turned_ref) = rest[:row_parts], rest[row_parts:]
    slots = pl.num_programs(0)
    _, rows, cols, channels = pair_ref.shape
    block = ids[0] * slots + pl.program_id(0)
    row_alive = alive_rows(chain_ref, (blocks[0, block] * n_chan + ids[1]) * rows, rows)
    col_alive = alive_rows(chain_ref, (blocks[1, block] * n_sub + ids[2]) * cols, cols)
    group = max(1, 256 // cols)
    for start in range(0, rows, group):
        at = pl.ds(start, group)
        normed = layer_norm(pair_ref[0, at].reshape(group * cols, channels))
        norm_ref[pl.ds(start * cols, group * cols), :] = normed
        gate = sigmoid(dot(normed.astype(jnp.bfloat16), w_ref[0, :, 4 * hidden :]))
        gate_ref[0, at] = gate.reshape(group, cols, channels)
    for col in range(cols):
        turned_ref[col] = norm_ref[pl.ds(col, rows, stride=cols), :].astype(jnp.bfloat16)
    step = max(1, 128 // rows)
    part = rows // row_parts
    for start in range(0, cols, step):
        taken = turned_ref[start : start + step].reshape(step * rows, channels)
        projected = dot(taken, w_ref[0, :, : 4 * hidden])
        mask = col_alive[start : start + step][:, None, :] * row_alive[None, :, :]
        left, right = gated_pair(projected, mask.reshape(step * rows, -1), hidden)
        left_ref[0, start : start + step] = left.reshape(step, rows, hidden)
        right = right.reshape(step, rows, hidden)
        for p, right_ref in enumerate(right_refs):
            right_ref[0, start : start + step] = right[:, p * part : (p + 1) * part]


def first_operands(ids, blocks, pair, chains, w_in, hidden, row_parts):
    slots, rows, cols, channels = pair.shape
    part = rows // row_parts
    operand = jax.ShapeDtypeStruct((slots, cols, rows, hidden), jnp.bfloat16)
    right = jax.ShapeDtypeStruct((slots, cols, part, hidden), jnp.bfloat16)
    return pl.pallas_call(
        functools.partial(first_kernel, hidden, row_parts, lax.axis_size("chan"), lax.axis_size("sub")),
        grid_spec=pltpu.PrefetchScalarGridSpec(
            num_scalar_prefetch=2,
            grid=(slots,),
            in_specs=[
                pl.BlockSpec((1, rows, cols, channels), lambda s, *_: (s, 0, 0, 0)),
                pl.BlockSpec(chains.shape, lambda s, *_: (0, 0)),
                pl.BlockSpec((1,) + w_in.shape[1:], lambda s, *_: (0, 0, 0)),
            ],
            out_specs=[
                pl.BlockSpec((1, rows, cols, channels), lambda s, *_: (s, 0, 0, 0)),
                pl.BlockSpec((1, cols, rows, hidden), lambda s, *_: (s, 0, 0, 0)),
            ]
            + [pl.BlockSpec((1, cols, part, hidden), lambda s, *_: (s, 0, 0, 0))] * row_parts,
            scratch_shapes=[
                pltpu.VMEM((rows * cols, channels), jnp.float32),
                pltpu.VMEM((cols, rows, channels), jnp.bfloat16),
            ],
        ),
        out_shape=[jax.ShapeDtypeStruct(pair.shape, jnp.float32), operand] + [right] * row_parts,
        compiler_params=pltpu.CompilerParams(vmem_limit_bytes=vmem_limit),
        name="first_operands",
    )(ids, blocks, pair, chains, w_in)


def product_kernel(shift, n_blk, slots_dev, terms, capacity, pieces, n_refs, ids, owners, slots, *rest):
    refs = rest[:n_refs]
    out_ref, left_held, right_held, right_wide, chosen, sems = rest[n_refs:]
    step = pl.program_id(0)
    turn = lax.rem(step, 2)
    _, depth, n_i, hidden = left_held.shape
    n_j = right_wide.shape[1]

    @pl.when(step == 0)
    def _():
        target = lax.rem(ids[0] + shift, n_blk)
        for e in range(2 * capacity):
            chosen[e] = 0

        def scan(e, count):
            block, term = target * slots_dev + e // terms, lax.rem(e, terms)
            here = jnp.logical_and(owners[term, block] == ids[0], count < capacity)

            @pl.when(here)
            def _():
                chosen[2 * count] = slots[term, 0, block]
                chosen[2 * count + 1] = slots[term, 1, block]

            return count + here.astype(jnp.int32)

        lax.fori_loop(0, slots_dev * terms, scan, jnp.int32(0))

    def copy(n, term, buffer, source):
        side, _, _, k0, depth_of, i0, size = pieces[n]
        held = (left_held, right_held)[side]
        return pltpu.make_async_copy(
            refs[source].at[chosen[2 * term + side]],
            held.at[buffer, pl.ds(k0, depth_of), pl.ds(i0, size), :],
            sems.at[buffer, n],
        )

    def start(term, buffer):
        for n, (_, on, off, *_) in enumerate(pieces):
            if on == off:
                copy(n, term, buffer, on).start()
            else:

                @pl.when(ids[3] == 1)
                def _(n=n, on=on):
                    copy(n, term, buffer, on).start()

                @pl.when(ids[3] == 0)
                def _(n=n, off=off):
                    copy(n, term, buffer, off).start()

    @pl.when(step == 0)
    def _():
        start(0, 0)

    @pl.when(step + 1 < capacity)
    def _():
        start(step + 1, 1 - turn)

    for n, piece in enumerate(pieces):
        copy(n, step, turn, piece[1]).wait()

    span = 8

    def widen(n, carry):
        at = pl.ds(n * span, span)
        right_wide[at] = right_held[turn, at].astype(jnp.float32)
        return carry

    lax.fori_loop(0, depth // span, widen, 0)

    group = min(8, n_j)
    unroll = 4
    for j0 in range(0, n_j, group):

        def body(n, sums):
            for u in range(unroll):
                k = n * unroll + u
                left = left_held[turn, k].astype(jnp.float32).reshape(n_i // 8, 8, hidden)
                sums = tuple(
                    total + left * right_wide[k, pl.ds(j0 + j, 8, stride=0), :][None]
                    for j, total in enumerate(sums)
                )
            return sums

        zero = jnp.zeros((n_i // 8, 8, hidden), jnp.float32)
        sums = lax.fori_loop(0, depth // unroll, body, (zero,) * group)
        for j, total in enumerate(sums):
            out_ref[0, j0 + j] = total.reshape(n_i, hidden).astype(jnp.bfloat16)


def term_products(shift, ids, owners, slots, lefts, rights, capacity, slots_dev, terms):
    n_blk = lax.axis_size("blk")
    refs, pieces = [], []

    def index_of(array):
        for n, known in enumerate(refs):
            if known is array:
                return n
        refs.append(array)
        return len(refs) - 1

    for side, operands in ((0, lefts), (1, rights)):
        for on, off, k0, i0 in operands:
            pieces.append((side, index_of(on), index_of(off), k0, on.shape[1], i0, on.shape[2]))
    hidden = lefts[0][0].shape[3]
    n_i = max(p[5] + p[6] for p in pieces if p[0] == 0)
    n_j = max(p[5] + p[6] for p in pieces if p[0] == 1)
    depth = max(p[3] + p[4] for p in pieces)
    return pl.pallas_call(
        functools.partial(
            product_kernel, shift, n_blk, slots_dev, terms, capacity, tuple(pieces), len(refs)
        ),
        grid_spec=pltpu.PrefetchScalarGridSpec(
            num_scalar_prefetch=3,
            grid=(capacity,),
            in_specs=[pl.BlockSpec(memory_space=pl.ANY)] * len(refs),
            out_specs=pl.BlockSpec((1, n_j, n_i, hidden), lambda t, *_: (t, 0, 0, 0)),
            scratch_shapes=[
                pltpu.VMEM((2, depth, n_i, hidden), jnp.bfloat16),
                pltpu.VMEM((2, depth, n_j, hidden), jnp.bfloat16),
                pltpu.VMEM((depth, n_j, hidden), jnp.float32),
                pltpu.SMEM((2 * capacity,), jnp.int32),
                pltpu.SemaphoreType.DMA((2, len(pieces))),
            ],
        ),
        out_shape=jax.ShapeDtypeStruct((capacity, n_j, n_i, hidden), jnp.bfloat16),
        compiler_params=pltpu.CompilerParams(vmem_limit_bytes=vmem_limit),
        cost_estimate=pl.CostEstimate(
            flops=2 * capacity * n_i * n_j * depth * hidden * 100,
            bytes_accessed=capacity * (depth * (n_i + n_j) + n_i * n_j) * hidden * 2,
            transcendentals=0,
        ),
        name="term_products",
    )(ids, owners, slots, *refs)


def home_kernel(last, hidden, n_blk, n_chan, n_sub, at, of, slots_dev, terms, capacity, ids, blocks, owners, *rest):
    parts, rest = rest[:n_blk], rest[n_blk:]
    scratch, rest = rest[-5:], rest[:-5]
    held, turned, place, seen, sems = scratch
    cur_ref, gate_ref, w_out_ref = rest[:3]
    if last:
        out_ref = rest[-1]
    else:
        chain_ref, w_ref, out_ref, next_gate_ref, left_ref, right_ref = rest[3:]
    step = pl.program_id(0)
    _, rows, cols, channels = cur_ref.shape

    def arrival(shift):
        return pltpu.make_async_copy(parts[shift], held.at[pl.ds(shift * capacity, capacity)], sems.at[shift])

    @pl.when(step == 0)
    def _():
        for shift in range(n_blk):
            arrival(shift).start()
            seen[shift] = 0

        def scan(e, carry):
            owner = owners[lax.rem(e, terms), ids[0] * slots_dev + e // terms]
            shift = lax.rem(ids[0] - owner + n_blk, n_blk)
            count = seen[owner]
            seen[owner] = count + 1
            place[e] = shift * capacity + count
            return carry

        lax.fori_loop(0, slots_dev * terms, scan, jnp.int32(0))
        for shift in range(n_blk):
            arrival(shift).wait()

    if not last:
        block = ids[0] * slots_dev + step
        row_alive = alive_rows(chain_ref, (blocks[0, block] * n_chan + ids[1]) * rows, rows)
        col_alive = alive_rows(chain_ref, ((blocks[1, block] * n_sub + ids[2]) * of + at) * cols, cols)
    span = max(1, 128 // rows)
    for start in range(0, cols, span):
        taken = pl.ds(start, span)
        total = held[place[step * terms], taken].astype(jnp.float32)
        for t in range(1, terms):
            total = total + held[place[step * terms + t], taken].astype(jnp.float32)
        rounded = total.astype(jnp.bfloat16).astype(jnp.float32)
        turned[pl.ds(start * rows, span * rows), :] = rounded.reshape(span * rows, hidden)
    group = min(rows, max(1, 256 // cols))
    for start in range(0, rows, group):
        taken = pl.ds(start, group)
        mixture = jnp.concatenate(
            [turned[pl.ds(row, cols, stride=rows), :].astype(jnp.bfloat16) for row in range(start, start + group)]
        )
        update = dot(layer_norm(mixture).astype(jnp.bfloat16), w_out_ref[0])
        current = cur_ref[0, taken].astype(jnp.float32).reshape(group * cols, channels)
        gate = gate_ref[0, taken].reshape(group * cols, channels)
        result = (current + gate * update).astype(jnp.bfloat16)
        out_ref[0, taken] = result.reshape(group, cols, channels)
        if not last:
            normed = layer_norm(result).astype(jnp.bfloat16)
            projected = dot(normed, w_ref[0])
            next_gate_ref[0, taken] = sigmoid(projected[:, 4 * hidden :]).reshape(group, cols, channels)
            mask = row_alive[start : start + group][:, None, :] * col_alive[None, :, :]
            left, right = gated_pair(projected, mask.reshape(group * cols, channels), hidden)
            left_ref[0, taken] = left.reshape(group, cols, hidden)
            right_ref[0, taken] = right.reshape(group, cols, hidden)


def home(layer, parts, ids, blocks, owners, current, gate, w_out, capacity, terms, at, of, chains, w_in, last, into=None):
    n_blk = len(parts)
    slots, rows, _, channels = current.shape
    hidden = w_out.shape[1]
    cols = parts[0].shape[1]
    chunk = (1, rows, cols, channels)

    def chunk_spec(array):
        whole = array.shape[2] != cols
        return pl.BlockSpec(chunk, lambda s, *_: (s, 0, at if whole else 0, 0))

    def layer_spec(array, index):
        return pl.BlockSpec((1,) + array.shape[1:], lambda s, *_: (index, 0, 0))

    in_specs = [pl.BlockSpec(memory_space=pl.ANY)] * n_blk + [
        chunk_spec(current),
        chunk_spec(gate),
        layer_spec(w_out, layer),
    ]
    operands = [*parts, current, gate, w_out]
    aliases = {}
    if last:
        if into is not None:
            aliases = {3 + len(operands): 0}
            operands.append(into)
            in_specs.append(pl.BlockSpec(memory_space=pl.ANY))
        out_shape = [jax.ShapeDtypeStruct((slots, rows, cols * of, channels), jnp.bfloat16)]
        out_specs = [pl.BlockSpec(chunk, lambda s, *_: (s, 0, at, 0))]
    else:
        operands += [chains, w_in]
        in_specs += [pl.BlockSpec(chains.shape, lambda s, *_: (0, 0)), layer_spec(w_in, layer + 1)]
        small = (slots, rows, cols, channels)
        out_shape = [jax.ShapeDtypeStruct(small, t) for t in (jnp.bfloat16, jnp.float32, jnp.bfloat16, jnp.bfloat16)]
        out_specs = [pl.BlockSpec(chunk, lambda s, *_: (s, 0, 0, 0))] * 4
    return pl.pallas_call(
        functools.partial(
            home_kernel, last, hidden, n_blk, lax.axis_size("chan"), lax.axis_size("sub"), at, of, slots, terms, capacity
        ),
        grid_spec=pltpu.PrefetchScalarGridSpec(
            num_scalar_prefetch=3,
            grid=(slots,),
            in_specs=in_specs,
            out_specs=out_specs,
            scratch_shapes=[
                pltpu.VMEM((n_blk * capacity, cols, rows, hidden), jnp.bfloat16),
                pltpu.VMEM((rows * cols, hidden), jnp.float32),
                pltpu.SMEM((slots * terms,), jnp.int32),
                pltpu.SMEM((n_blk,), jnp.int32),
                pltpu.SemaphoreType.DMA((n_blk,)),
            ],
        ),
        out_shape=out_shape,
        input_output_aliases=aliases,
        compiler_params=pltpu.CompilerParams(vmem_limit_bytes=vmem_limit),
        cost_estimate=pl.CostEstimate(
            flops=2 * slots * rows * cols * channels * 6 * channels * 10,
            bytes_accessed=slots * rows * cols * channels * 16,
            transcendentals=0,
        ),
        name="home",
    )(ids, blocks, owners, *operands)


def exchange_outgoing(left, rights, n_chan, n_sub):
    if n_chan == 2 and n_sub == 2:
        both = ("chan", "sub")
        other_left = lax.ppermute(left, "sub", [(0, 1), (1, 0)])
        lefts = [(other_left, left, 0, 0), (left, other_left, left.shape[1], 0)]
        chunks = []
        for right in rights:
            if chunks:
                (one, *_), (_, two, *_) = chunks[-1]
                right, *_ = lax.optimization_barrier((right, one, two))
            one = lax.ppermute(right, both, [(0, 2), (3, 1), (1, 0), (2, 3)])
            two = lax.ppermute(right, both, [(1, 2), (2, 1)])
            chunks.append([(one, one, 0, 0), (right, two, right.shape[1], 0)])
        return lefts, chunks
    left = lax.all_gather(left, "sub", axis=1, tiled=True)
    right = jnp.concatenate(rights, axis=2)
    right = lax.all_gather(right, "chan", axis=2, tiled=True)
    right = lax.all_to_all(right, "sub", split_axis=2, concat_axis=1, tiled=True)
    cols = right.shape[2] // 2
    chunks = [right[:, :, :cols], right[:, :, cols:]]
    return [(left, left, 0, 0)], [[(r, r, 0, 0)] for r in chunks]


def exchange_incoming(lefts, rights, n_chan, n_sub):
    if n_chan == 2 and n_sub == 2:
        both = ("chan", "sub")
        left_pieces, chunks = [], []
        at = 0
        for left, right in zip(lefts, rights):
            depth = left.shape[1]
            one = lax.ppermute(left, both, [(1, 3), (2, 0), (0, 1), (3, 2)])
            two = lax.ppermute(one, both, [(0, 1), (3, 2)])
            left_pieces += [(left, one, 0, at), (one, two, depth, at)]
            other = lax.ppermute(right, "chan", [(0, 1), (1, 0)])
            chunks.append([(right, right, 0, 0), (other, other, depth, 0)])
            at += left.shape[2]
        return left_pieces, chunks
    left = lax.all_gather(jnp.concatenate(lefts, axis=2), "chan", axis=1, tiled=True)
    left = lax.all_gather(left, "sub", axis=2, tiled=True)
    size = left.shape[2] // n_chan
    left = lax.dynamic_slice_in_dim(left, lax.axis_index("chan") * size, size, 2)
    gathered = [lax.all_gather(right, "chan", axis=1, tiled=True) for right in rights]
    return [(left, left, 0, 0)], [[(r, r, 0, 0)] for r in gathered]


def per_device(pair, block_list, term_owner, term_slots, chain_ids, w_in, w_out):
    n_blk = lax.axis_size("blk")
    n_chan = lax.axis_size("chan")
    n_sub = lax.axis_size("sub")
    position = lax.axis_index("blk")
    row_group = lax.axis_index("chan")
    col_group = lax.axis_index("sub")
    slots, rows, cols, channels = pair.shape
    hidden = w_out.shape[1]
    terms = term_owner.shape[1]
    capacity = max(2, -(-slots * terms // n_blk))
    fast = n_chan == 2 and n_sub == 2
    on_diagonal = (row_group == col_group).astype(jnp.int32)
    ids = jnp.stack([position, row_group, col_group, on_diagonal]).astype(jnp.int32)
    blocks = block_list.T
    owners = term_owner.T
    slot_of = jnp.transpose(term_slots, (1, 2, 0))
    chains = chain_ids.reshape(-1, 128)
    shifts = [n_blk // 2] + [s for s in range(1, n_blk) if s != n_blk // 2] + [0]

    def all_products(lefts, right):
        parts = [None] * n_blk
        for shift in shifts:
            made = term_products(shift, ids, owners, slot_of, lefts, right, capacity, slots, terms)
            if shift:
                pairs = [(p, (p + shift) % n_blk) for p in range(n_blk)]
                made = lax.ppermute(made, "blk", pairs)
            parts[shift] = made
        return parts

    def at_home(layer, parts, current, gate, at, of, into=None):
        last = layer == w_in.shape[0] - 1
        return home(
            layer, parts, ids, blocks, owners, current, gate, w_out, capacity, terms, at, of, chains, w_in, last, into
        )

    gate, left, *rights = first_operands(ids, blocks, pair, chains, w_in, hidden, 2 if fast else 1)
    lefts, chunks = exchange_outgoing(left, rights, n_chan, n_sub)
    count = len(chunks)
    made = [all_products(lefts, right) for right in chunks]
    homes = [at_home(0, parts, pair, gate, at, count) for at, parts in enumerate(made)]
    lefts, chunks = exchange_incoming([h[2] for h in homes], [h[3] for h in homes], n_chan, n_sub)
    made = [all_products(lefts, right) for right in chunks]
    out = None
    for at, parts in enumerate(made):
        (out,) = at_home(1, parts, homes[at][0], homes[at][1], at, count, into=out)
    return out


def solution(mesh):
    in_specs = (
        P(("groups", "blk"), "chan", "sub", None),
        P("groups", None),
        P("groups", None),
        P("groups", None, None),
        P("groups"),
        P(),
        P(),
    )
    out_specs = P(("groups", "blk"), "chan", "sub", None)
    return jax.shard_map(
        per_device, mesh=mesh, in_specs=in_specs, out_specs=out_specs, check_vma=False
    )
```

time: 358 us -> 367 us (1.025)
  Pallas kernels: 216 us -> 228 us
  local copies, waits for them, and re-layouts: 16.9 us -> 11.2 us
  waiting for transfers between devices: 87.2 us -> 92.8 us
    pallas_call x21, Pallas kernels: 216 us -> 228 us  [the longest x16 151 us: term_products(): pl.pallas_call(functools.partial(product_kernel, shift, n_blk, slots_dev,...]
    ppermute x2, waiting for transfers between devices: 18.5 us -> 23.1 us  [exchange_outgoing(): one = lax.ppermute(right, both, [(0, 2), (3, 1), (1, 0), (2, 3)])]
    unnamed x55 -> x52, local copies, waits for them, and re-layouts: 10.5 us -> 11.2 us
  transfers between devices with their start and end apart: 23 -> 23, of which waited for: 5 -> 6; matrix products, arithmetic and copies ran while one was open for 1% -> 0% of each run, Pallas kernels for 55% -> 55%
where the time goes in v2:
time: 367 us; the launch traced here: 364 us
  Pallas kernels  228 us (62%)
  waiting for transfers between devices  92.8 us (25%)
  starting transfers between devices  30.6 us (8%)
  local copies, waits for them, and re-layouts  11.2 us (3%)
    pallas_call x16, Pallas kernels, term_products(): pl.pallas_call(functools.partial(product_kernel, shift, n_blk, slots_dev,...  151 us
    pallas_call x4, Pallas kernels, home(): pl.pallas_call(functools.partial(home_kernel, last, hidden, n_blk, lax.ax...  58.7 us
    ppermute x12, waiting for transfers between devices, all_products(): made = lax.ppermute(made, 'blk', pairs)  32.3 us
    ppermute x2, waiting for transfers between devices, exchange_outgoing(): one = lax.ppermute(right, both, [(0, 2), (3, 1), (1, 0), (2, 3)])  23.1 us
    ppermute x2, waiting for transfers between devices, exchange_incoming(): one = lax.ppermute(left, both, [(1, 3), (2, 0), (0, 1), (3, 2)])  20.2 us
    pallas_call x1, Pallas kernels, first_operands(): pl.pallas_call(functools.partial(first_kernel, hidden, row_parts, lax.axi...  18.4 us
    ppermute x2, waiting for transfers between devices, exchange_incoming(): other = lax.ppermute(right, 'chan', [(0, 1), (1, 0)])  17.2 us
    ppermute x12, starting transfers between devices, all_products(): made = lax.ppermute(made, 'blk', pairs)  15.5 us
  transfers between devices with their start and end apart: 23, of which 6 were waited for; matrix products, arithmetic and copies ran while one was open for 0% of the time, Pallas kernels for 55%

profile of v2, /device:TPU:11, one launch (start us, length us, event | category | flops | bytes accessed | tf_op | source)
XLA Modules:
  0.0 364.0 jit_solution(9342674810644353501)
XLA Ops:
  0.6 18.4 %first_operands.1 = (f32[8,32,32,128]{3,2,1,0:T(8,128)}, bf16[8,32,32,128]{3,2,1,0:T(8,128)(2,1)}, bf16[8,32,16,128]{3,2,1,0:T(8,128)(2,1)}, bf16[8,32,16,128]{3,2,1,0:T(8,128)(2,1)}) custom-call(s32[4]{0:T(128)} %pad_add_fusion.ids, s32[2,32]{1,0:T(2,128)} %bitcast.11, bf16[8,32,32,128]{3,2,1,0:T(8,128)(2,1)} %rest_4_.3, s32[32,128]{1,0:T(8,128)} %bitcast.8, ...), custom_call_target="tpu_custom_call" | custom-call | tf_op jit(solution)/shard_map/first_operands/pallas_call | solution.py:81
  20.4 2.6 collective-permute-start.1
  22.9 22.7 %collective-permute-done.1.rest_2_ = bf16[8,32,16,128]{3,2,1,0:T(8,128)(2,1)S(1)} collective-permute-done((bf16[8,32,16,128]{3,2,1,0:T(8,128)(2,1)}, bf16[8,32,16,128]{3,2,1,0:T(8,128)(2,1)S(1)}, u32[]{:S(2)}, u32[]{:S(2)}) %collective-permute-start.1) | collective-permute-done | bytes 1048608 | tf_op jit(solution)/shard_map/ppermute | solution.py:382
  46.4 4.1 %collective-permute-start.8 = (bf16[8,32,16,128]{3,2,1,0:T(8,128)(2,1)}, bf16[8,32,16,128]{3,2,1,0:T(8,128)(2,1)S(1)}, u32[]{:S(2)}, u32[]{:S(2)}) collective-permute-start(bf16[8,32,16,128]{3,2,1,0:T(8,128)(2,1)} %get-tuple-element.23.rest_3_), channel_id=1, source_target_pairs={{0,2},{3,1},{1,0},{2,3},{4,6},{7,5},{5,4},{6,7},{8,10},{11,9},{9,8... | collective-permute-start | bytes 3145736 | tf_op jit(solution)/shard_map/ppermute | solution.py:382
  51.9 9.2 %term_products.17 = bf16[4,16,32,128]{3,2,1,0:T(8,128)(2,1)} custom-call(s32[4]{0:T(128)} %pad_add_fusion.ids, s32[2,32]{1,0:T(2,128)} %bitcast.32, s32[2,2,32]{2,1,0:T(2,128)} %bitcast.16, bf16[8,32,32,128]{3,2,1,0:T(8,128)(2,1)} %copy-done, bf16[8,32,32,128]{3,2,1,0:T(8,128)(2,1)} %get-tuple-element.18.rest_1_, bf16[8,32,16,128]{3,2,1,0:T(8,128)(2,1)} %copy-done.7, ...), custom_call_target="tpu_custom_call" | custom-call | flops 3355443200 | bytes 3670016 | tf_op jit(solution)/shard_map/term_products/pallas_call | solution.py:215
  62.5 9.2 %term_products.18 = bf16[4,16,32,128]{3,2,1,0:T(8,128)(2,1)} custom-call(s32[4]{0:T(128)} %pad_add_fusion.ids, s32[2,32]{1,0:T(2,128)} %bitcast.33, s32[2,2,32]{2,1,0:T(2,128)} %bitcast.17, bf16[8,32,32,128]{3,2,1,0:T(8,128)(2,1)} %copy-done, bf16[8,32,32,128]{3,2,1,0:T(8,128)(2,1)} %get-tuple-element.18.rest_1_, bf16[8,32,16,128]{3,2,1,0:T(8,128)(2,1)} %copy-done.7, ...), custom_call_target="tpu_custom_call" | custom-call | flops 3355443200 | bytes 3670016 | tf_op jit(solution)/shard_map/term_products/pallas_call | solution.py:215
  74.8 9.2 %term_products.21 = bf16[4,16,32,128]{3,2,1,0:T(8,128)(2,1)} custom-call(s32[4]{0:T(128)} %pad_add_fusion.ids, s32[2,32]{1,0:T(2,128)} %bitcast.34, s32[2,2,32]{2,1,0:T(2,128)} %bitcast.18, bf16[8,32,32,128]{3,2,1,0:T(8,128)(2,1)} %copy-done, bf16[8,32,32,128]{3,2,1,0:T(8,128)(2,1)} %get-tuple-element.18.rest_1_, bf16[8,32,16,128]{3,2,1,0:T(8,128)(2,1)} %copy-done.11, ...), custom_call_target="tpu_custom_call" | custom-call | flops 3355443200 | bytes 3670016 | tf_op jit(solution)/shard_map/term_products/pallas_call | solution.py:215
  84.7 9.2 %term_products.22 = bf16[4,16,32,128]{3,2,1,0:T(8,128)(2,1)} custom-call(s32[4]{0:T(128)} %pad_add_fusion.ids, s32[2,32]{1,0:T(2,128)} %bitcast.35, s32[2,2,32]{2,1,0:T(2,128)} %bitcast.19, bf16[8,32,32,128]{3,2,1,0:T(8,128)(2,1)} %copy-done, bf16[8,32,32,128]{3,2,1,0:T(8,128)(2,1)} %get-tuple-element.18.rest_1_, bf16[8,32,16,128]{3,2,1,0:T(8,128)(2,1)} %copy-done.11, ...), custom_call_target="tpu_custom_call" | custom-call | flops 3355443200 | bytes 3670016 | tf_op jit(solution)/shard_map/term_products/pallas_call | solution.py:215
  94.0 3.0 collective-permute-start.11
  96.9 9.2 %term_products.23 = bf16[4,16,32,128]{3,2,1,0:T(8,128)(2,1)} custom-call(s32[4]{0:T(128)} %pad_add_fusion.ids, s32[2,32]{1,0:T(2,128)} %bitcast.36, s32[2,2,32]{2,1,0:T(2,128)} %bitcast.20, bf16[8,32,32,128]{3,2,1,0:T(8,128)(2,1)} %copy-done, bf16[8,32,32,128]{3,2,1,0:T(8,128)(2,1)} %get-tuple-element.18.rest_1_, bf16[8,32,16,128]{3,2,1,0:T(8,128)(2,1)} %copy-done.11, ...), custom_call_target="tpu_custom_call" | custom-call | flops 3355443200 | bytes 3670016 | tf_op jit(solution)/shard_map/term_products/pallas_call | solution.py:215
  106.2 9.2 %term_products.20.rest_0_ = bf16[4,16,32,128]{3,2,1,0:T(8,128)(2,1)} custom-call(s32[4]{0:T(128)} %pad_add_fusion.ids, s32[2,32]{1,0:T(2,128)} %bitcast.37, s32[2,2,32]{2,1,0:T(2,128)} %bitcast.21, bf16[8,32,32,128]{3,2,1,0:T(8,128)(2,1)} %copy-done, bf16[8,32,32,128]{3,2,1,0:T(8,128)(2,1)} %get-tuple-element.18.rest_1_, ...), custom_call_target="tpu_custom_call" | custom-call | flops 3355443200 | bytes 3670016 | tf_op jit(solution)/shard_map/term_products/pallas_call | solution.py:215
  115.5 9.2 %term_products.19 = bf16[4,16,32,128]{3,2,1,0:T(8,128)(2,1)} custom-call(s32[4]{0:T(128)} %pad_add_fusion.ids, s32[2,32]{1,0:T(2,128)} %bitcast.38, s32[2,2,32]{2,1,0:T(2,128)} %bitcast.22, bf16[8,32,32,128]{3,2,1,0:T(8,128)(2,1)} %copy-done, bf16[8,32,32,128]{3,2,1,0:T(8,128)(2,1)} %get-tuple-element.18.rest_1_, bf16[8,32,16,128]{3,2,1,0:T(8,128)(2,1)} %copy-done.7, ...), custom_call_target="tpu_custom_call" | custom-call | flops 3355443200 | bytes 3670016 | tf_op jit(solution)/shard_map/term_products/pallas_call | solution.py:215
  124.7 9.4 %term_products.16.rest_0_ = bf16[4,16,32,128]{3,2,1,0:T(8,128)(2,1)} custom-call(s32[4]{0:T(128)} %pad_add_fusion.ids, s32[2,32]{1,0:T(2,128)} %bitcast.39, s32[2,2,32]{2,1,0:T(2,128)} %bitcast.23, bf16[8,32,32,128]{3,2,1,0:T(8,128)(2,1)} %copy-done, bf16[8,32,32,128]{3,2,1,0:T(8,128)(2,1)} %get-tuple-element.18.rest_1_, bf16[8,32,16,128]{3,2,1,0:T(8,128)(2,1)} %copy-done.7, ...), custom_call_target="tpu_custom_call" | custom-call | flops 3355443200 | bytes 3670016 | tf_op jit(solution)/shard_map/term_products/pallas_call | solution.py:215
  135.4 17.6 %collective-permute-done.11.rest_2_ = bf16[4,16,32,128]{3,2,1,0:T(8,128)(2,1)S(1)} collective-permute-done((bf16[4,16,32,128]{3,2,1,0:T(8,128)(2,1)}, bf16[4,16,32,128]{3,2,1,0:T(8,128)(2,1)S(1)}, u32[]{:S(2)}, u32[]{:S(2)}) %collective-permute-start.11) | collective-permute-done | bytes 524320 | tf_op jit(solution)/shard_map/ppermute | solution.py:443
  153.9 18.0 %home.5 = (bf16[8,32,16,128]{3,2,1,0:T(8,128)(2,1)}, f32[8,32,16,128]{3,2,1,0:T(8,128)}, bf16[8,32,16,128]{3,2,1,0:T(8,128)(2,1)}, bf16[8,32,16,128]{3,2,1,0:T(8,128)(2,1)}) custom-call(s32[4]{0:T(128)} %pad_add_fusion.ids, s32[2,32]{1,0:T(2,128)} %bitcast.12, s32[2,32]{1,0:T(2,128)} %bitcast.40, bf16[4,16,32,128]{3,2,1,0:T(8,128)(2,1)} %term_products.20.rest_0_, ...), custom_call_target="tpu_custom_call" | custom-call | flops 8053063680 | bytes 8388608 | tf_op jit(solution)/shard_map/home/pallas_call | solution.py:343
  173.9 18.0 %home.4 = (bf16[8,32,16,128]{3,2,1,0:T(8,128)(2,1)}, f32[8,32,16,128]{3,2,1,0:T(8,128)}, bf16[8,32,16,128]{3,2,1,0:T(8,128)(2,1)}, bf16[8,32,16,128]{3,2,1,0:T(8,128)(2,1)}) custom-call(s32[4]{0:T(128)} %pad_add_fusion.ids, s32[2,32]{1,0:T(2,128)} %bitcast.13, s32[2,32]{1,0:T(2,128)} %bitcast.41, bf16[4,16,32,128]{3,2,1,0:T(8,128)(2,1)} %term_products.16.rest_0_, ...), custom_call_target="tpu_custom_call" | custom-call | flops 8053063680 | bytes 8388608 | tf_op jit(solution)/shard_map/home/pallas_call | solution.py:343
  193.4 2.6 collective-permute-start.14
  196.0 20.2 %collective-permute-done.6.rest_1_ = bf16[8,32,16,128]{3,2,1,0:T(8,128)(2,1)S(1)} collective-permute-done((bf16[8,32,16,128]{3,2,1,0:T(8,128)(2,1)}, bf16[8,32,16,128]{3,2,1,0:T(8,128)(2,1)S(1)}, u32[]{:S(2)}, u32[]{:S(2)}) %collective-permute-start.6) | collective-permute-done | bytes 1048608 | tf_op jit(solution)/shard_map/ppermute | solution.py:402
  218.3 17.2 %collective-permute-done.15.rest_7_ = bf16[8,32,16,128]{3,2,1,0:T(8,128)(2,1)S(1)} collective-permute-done((bf16[8,32,16,128]{3,2,1,0:T(8,128)(2,1)S(1)}, bf16[8,32,16,128]{3,2,1,0:T(8,128)(2,1)S(1)}, u32[]{:S(2)}, u32[]{:S(2)}) %collective-permute-start.15) | collective-permute-done | bytes 1048608 | tf_op jit(solution)/shard_map/ppermute | solution.py:405
  237.9 9.6 %term_products.25 = bf16[4,16,32,128]{3,2,1,0:T(8,128)(2,1)} custom-call(s32[4]{0:T(128)} %pad_add_fusion.ids, s32[2,32]{1,0:T(2,128)} %bitcast.42, s32[2,2,32]{2,1,0:T(2,128)} %bitcast.24, bf16[8,32,16,128]{3,2,1,0:T(8,128)(2,1)} %get-tuple-element.21.rest_0_, bf16[8,32,16,128]{3,2,1,0:T(8,128)(2,1)} %copy-done.3, bf16[8,32,16,128]{3,2,1,0:T(8,128)(2,1)} %copy-done.8, ...), custom_call_target="tpu_custom_call" | custom-call | flops 3355443200 | bytes 3670016 | tf_op jit(solution)/shard_map/term_products/pallas_call | solution.py:215
  247.6 9.6 %term_products.26 = bf16[4,16,32,128]{3,2,1,0:T(8,128)(2,1)} custom-call(s32[4]{0:T(128)} %pad_add_fusion.ids, s32[2,32]{1,0:T(2,128)} %bitcast.43, s32[2,2,32]{2,1,0:T(2,128)} %bitcast.25, bf16[8,32,16,128]{3,2,1,0:T(8,128)(2,1)} %get-tuple-element.21.rest_0_, bf16[8,32,16,128]{3,2,1,0:T(8,128)(2,1)} %copy-done.3, bf16[8,32,16,128]{3,2,1,0:T(8,128)(2,1)} %copy-done.8, ...), custom_call_target="tpu_custom_call" | custom-call | flops 3355443200 | bytes 3670016 | tf_op jit(solution)/shard_map/term_products/pallas_call | solution.py:215
  257.2 3.1 collective-permute-start.17
  261.3 9.6 %term_products.29 = bf16[4,16,32,128]{3,2,1,0:T(8,128)(2,1)} custom-call(s32[4]{0:T(128)} %pad_add_fusion.ids, s32[2,32]{1,0:T(2,128)} %bitcast.44, s32[2,2,32]{2,1,0:T(2,128)} %bitcast.26, bf16[8,32,16,128]{3,2,1,0:T(8,128)(2,1)} %get-tuple-element.21.rest_0_, bf16[8,32,16,128]{3,2,1,0:T(8,128)(2,1)} %copy-done.3, bf16[8,32,16,128]{3,2,1,0:T(8,128)(2,1)} %copy-done.8, ...), custom_call_target="tpu_custom_call" | custom-call | flops 3355443200 | bytes 3670016 | tf_op jit(solution)/shard_map/term_products/pallas_call | solution.py:215
  271.3 9.6 %term_products.30 = bf16[4,16,32,128]{3,2,1,0:T(8,128)(2,1)} custom-call(s32[4]{0:T(128)} %pad_add_fusion.ids, s32[2,32]{1,0:T(2,128)} %bitcast.45, s32[2,2,32]{2,1,0:T(2,128)} %bitcast.27, bf16[8,32,16,128]{3,2,1,0:T(8,128)(2,1)} %get-tuple-element.21.rest_0_, bf16[8,32,16,128]{3,2,1,0:T(8,128)(2,1)} %copy-done.3, bf16[8,32,16,128]{3,2,1,0:T(8,128)(2,1)} %copy-done.8, ...), custom_call_target="tpu_custom_call" | custom-call | flops 3355443200 | bytes 3670016 | tf_op jit(solution)/shard_map/term_products/pallas_call | solution.py:215
  280.9 3.3 collective-permute-start.21
  284.3 9.6 %term_products.31 = bf16[4,16,32,128]{3,2,1,0:T(8,128)(2,1)} custom-call(s32[4]{0:T(128)} %pad_add_fusion.ids, s32[2,32]{1,0:T(2,128)} %bitcast.46, s32[2,2,32]{2,1,0:T(2,128)} %bitcast.28, bf16[8,32,16,128]{3,2,1,0:T(8,128)(2,1)} %get-tuple-element.21.rest_0_, bf16[8,32,16,128]{3,2,1,0:T(8,128)(2,1)} %copy-done.3, bf16[8,32,16,128]{3,2,1,0:T(8,128)(2,1)} %copy-done.8, ...), custom_call_target="tpu_custom_call" | custom-call | flops 3355443200 | bytes 3670016 | tf_op jit(solution)/shard_map/term_products/pallas_call | solution.py:215
  294.0 9.6 %term_products.28.rest_0_ = bf16[4,16,32,128]{3,2,1,0:T(8,128)(2,1)} custom-call(s32[4]{0:T(128)} %pad_add_fusion.ids, s32[2,32]{1,0:T(2,128)} %bitcast.47, s32[2,2,32]{2,1,0:T(2,128)} %bitcast.29, bf16[8,32,16,128]{3,2,1,0:T(8,128)(2,1)} %get-tuple-element.21.rest_0_, bf16[8,32,16,128]{3,2,1,0:T(8,128)(2,1)} %copy-done.3, ...), custom_call_target="tpu_custom_call" | custom-call | flops 3355443200 | bytes 3670016 | tf_op jit(solution)/shard_map/term_products/pallas_call | solution.py:215
  303.6 9.7 %term_products.27 = bf16[4,16,32,128]{3,2,1,0:T(8,128)(2,1)} custom-call(s32[4]{0:T(128)} %pad_add_fusion.ids, s32[2,32]{1,0:T(2,128)} %bitcast.48, s32[2,2,32]{2,1,0:T(2,128)} %bitcast.30, bf16[8,32,16,128]{3,2,1,0:T(8,128)(2,1)} %get-tuple-element.21.rest_0_, bf16[8,32,16,128]{3,2,1,0:T(8,128)(2,1)} %copy-done.3, bf16[8,32,16,128]{3,2,1,0:T(8,128)(2,1)} %copy-done.8, ...), custom_call_target="tpu_custom_call" | custom-call | flops 3355443200 | bytes 3670016 | tf_op jit(solution)/shard_map/term_products/pallas_call | solution.py:215
  313.3 9.8 %term_products.24.rest_0_ = bf16[4,16,32,128]{3,2,1,0:T(8,128)(2,1)} custom-call(s32[4]{0:T(128)} %pad_add_fusion.ids, s32[2,32]{1,0:T(2,128)} %bitcast.49, s32[2,2,32]{2,1,0:T(2,128)} %bitcast.31, bf16[8,32,16,128]{3,2,1,0:T(8,128)(2,1)} %get-tuple-element.21.rest_0_, bf16[8,32,16,128]{3,2,1,0:T(8,128)(2,1)} %copy-done.3, ...), custom_call_target="tpu_custom_call" | custom-call | flops 3355443200 | bytes 3670016 | tf_op jit(solution)/shard_map/term_products/pallas_call | solution.py:215
  324.4 14.7 %collective-permute-done.21.rest_2_ = bf16[4,16,32,128]{3,2,1,0:T(8,128)(2,1)S(1)} collective-permute-done((bf16[4,16,32,128]{3,2,1,0:T(8,128)(2,1)}, bf16[4,16,32,128]{3,2,1,0:T(8,128)(2,1)S(1)}, u32[]{:S(2)}, u32[]{:S(2)}) %collective-permute-start.21) | collective-permute-done | bytes 524320 | tf_op jit(solution)/shard_map/ppermute | solution.py:443
  340.1 11.3 %home.6.rest_7_ = bf16[8,32,32,128]{3,2,1,0:T(8,128)(2,1)} custom-call(s32[4]{0:T(128)} %pad_add_fusion.ids, s32[2,32]{1,0:T(2,128)} %bitcast.14, s32[2,32]{1,0:T(2,128)} %bitcast.50, bf16[4,16,32,128]{3,2,1,0:T(8,128)(2,1)} %term_products.28.rest_0_, bf16[4,16,32,128]{3,2,1,0:T(8,128)(2,1)} %copy-done.19, bf16[4,16,32,128]{3,2,1,0:T(8,128)(2,1)} %copy-done.22, ...), custom_call_target="tpu_custom_call" | custom-call | flops 8053063680 | bytes 8388608 | tf_op jit(solution)/shard_map/home/pallas_call | solution.py:343
  352.7 11.3 %home.7 = bf16[8,32,32,128]{3,2,1,0:T(8,128)(2,1)} custom-call(s32[4]{0:T(128)} %pad_add_fusion.ids, s32[2,32]{1,0:T(2,128)} %bitcast.15, s32[2,32]{1,0:T(2,128)} %bitcast.51, bf16[4,16,32,128]{3,2,1,0:T(8,128)(2,1)} %term_products.24.rest_0_, bf16[4,16,32,128]{3,2,1,0:T(8,128)(2,1)} %copy-done.14, ...), custom_call_target="tpu_custom_call", output_to_operand_aliasing={{}: (10, {})} | custom-call | flops 8053063680 | bytes 8388608 | tf_op jit(solution)/shard_map/home/pallas_call | solution.py:343
  (88 shorter events, 24.2 us)
Async XLA Ops:
  19.0 31.5 %collective-permute-start = (bf16[8,32,32,128]{3,2,1,0:T(8,128)(2,1)}, bf16[8,32,32,128]{3,2,1,0:T(8,128)(2,1)S(1)}, u32[]{:S(2)}, u32[]{:S(2)}) collective-permute-start(bf16[8,32,32,128]{3,2,1,0:T(8,128)(2,1)} %get-tuple-element.18.rest_1_), channel_id=1, source_target_pairs={{0,1},{1,0},{2,3},{3,2},{4,5},{5,4},{6,7},{7,6},{8,9},{9,8},{10,11... | collective-permute-start | bytes 6291464 | tf_op jit(solution)/shard_map/ppermute | solution.py:375
  19.6 3.3 collective-permute-start.2
  20.4 25.3 %collective-permute-start.1 = (bf16[8,32,16,128]{3,2,1,0:T(8,128)(2,1)}, bf16[8,32,16,128]{3,2,1,0:T(8,128)(2,1)S(1)}, u32[]{:S(2)}, u32[]{:S(2)}) collective-permute-start(bf16[8,32,16,128]{3,2,1,0:T(8,128)(2,1)} %get-tuple-element.19.rest_3_), channel_id=1, source_target_pairs={{0,2},{3,1},{1,0},{2,3},{4,6},{7,5},{5,4},{6,7},{8,10},{11,9},{9,8... | collective-permute-start | bytes 3145736 | tf_op jit(solution)/shard_map/ppermute | solution.py:382
  22.9 27.6 %copy-start.5 = (bf16[8,32,16,128]{3,2,1,0:T(8,128)(2,1)}, bf16[8,32,16,128]{3,2,1,0:T(8,128)(2,1)S(1)}, u32[]{:S(2)}) copy-start(bf16[8,32,16,128]{3,2,1,0:T(8,128)(2,1)S(1)} %collective-permute-done.2.rest_4_) | copy-start | bytes 3145732
  45.7 4.8 %copy-start.7 = (bf16[8,32,16,128]{3,2,1,0:T(8,128)(2,1)}, bf16[8,32,16,128]{3,2,1,0:T(8,128)(2,1)S(1)}, u32[]{:S(2)}) copy-start(bf16[8,32,16,128]{3,2,1,0:T(8,128)(2,1)S(1)} %collective-permute-done.1.rest_2_) | copy-start | bytes 3145732
  45.7 27.1 %collective-permute-start.9 = (bf16[8,32,16,128]{3,2,1,0:T(8,128)(2,1)}, bf16[8,32,16,128]{3,2,1,0:T(8,128)(2,1)S(1)}, u32[]{:S(2)}, u32[]{:S(2)}) collective-permute-start(bf16[8,32,16,128]{3,2,1,0:T(8,128)(2,1)} %get-tuple-element.23.rest_3_), channel_id=1, source_target_pairs={{1,2},{2,1},{5,6},{6,5},{9,10},{10,9},{13,14},{14,13},{17,18},{18,... | collective-permute-start | bytes 3145736 | tf_op jit(solution)/shard_map/ppermute | solution.py:383
  46.4 26.8 %collective-permute-start.8 = (bf16[8,32,16,128]{3,2,1,0:T(8,128)(2,1)}, bf16[8,32,16,128]{3,2,1,0:T(8,128)(2,1)S(1)}, u32[]{:S(2)}, u32[]{:S(2)}) collective-permute-start(bf16[8,32,16,128]{3,2,1,0:T(8,128)(2,1)} %get-tuple-element.23.rest_3_), channel_id=1, source_target_pairs={{0,2},{3,1},{1,0},{2,3},{4,6},{7,5},{5,4},{6,7},{8,10},{11,9},{9,8... | collective-permute-start | bytes 3145736 | tf_op jit(solution)/shard_map/ppermute | solution.py:382
  61.1 111.0 %collective-permute-start.3 = (bf16[4,16,32,128]{3,2,1,0:T(8,128)(2,1)}, bf16[4,16,32,128]{3,2,1,0:T(8,128)(2,1)S(1)}, u32[]{:S(2)}, u32[]{:S(2)}) collective-permute-start(bf16[4,16,32,128]{3,2,1,0:T(8,128)(2,1)} %term_products.17), channel_id=1, source_target_pairs={{0,4},{4,8},{8,12},{12,0},{1,5},{5,9},{9,13},{13,1},{2,6},{6,10},{... | collective-permute-start | bytes 1572872 | tf_op jit(solution)/shard_map/ppermute | solution.py:443
  71.7 100.4 %collective-permute-start.4 = (bf16[4,16,32,128]{3,2,1,0:T(8,128)(2,1)}, bf16[4,16,32,128]{3,2,1,0:T(8,128)(2,1)S(1)}, u32[]{:S(2)}, u32[]{:S(2)}) collective-permute-start(bf16[4,16,32,128]{3,2,1,0:T(8,128)(2,1)} %term_products.18), channel_id=1, source_target_pairs={{0,8},{4,12},{8,0},{12,4},{1,9},{5,13},{9,1},{13,5},{2,10},{6,14},... | collective-permute-start | bytes 1572872 | tf_op jit(solution)/shard_map/ppermute | solution.py:443
  84.0 50.1 %collective-permute-start.10 = (bf16[4,16,32,128]{3,2,1,0:T(8,128)(2,1)}, bf16[4,16,32,128]{3,2,1,0:T(8,128)(2,1)S(1)}, u32[]{:S(2)}, u32[]{:S(2)}) collective-permute-start(bf16[4,16,32,128]{3,2,1,0:T(8,128)(2,1)} %term_products.21), channel_id=1, source_target_pairs={{0,4},{4,8},{8,12},{12,0},{1,5},{5,9},{9,13},{13,1},{2,6},{6,10},{... | collective-permute-start | bytes 1572872 | tf_op jit(solution)/shard_map/ppermute | solution.py:443
  94.0 59.0 %collective-permute-start.11 = (bf16[4,16,32,128]{3,2,1,0:T(8,128)(2,1)}, bf16[4,16,32,128]{3,2,1,0:T(8,128)(2,1)S(1)}, u32[]{:S(2)}, u32[]{:S(2)}) collective-permute-start(bf16[4,16,32,128]{3,2,1,0:T(8,128)(2,1)} %term_products.22), channel_id=1, source_target_pairs={{0,8},{4,12},{8,0},{12,4},{1,9},{5,13},{9,1},{13,5},{2,10},{6,14},... | collective-permute-start | bytes 1572872 | tf_op jit(solution)/shard_map/ppermute | solution.py:443
  106.2 46.8 %collective-permute-start.12 = (bf16[4,16,32,128]{3,2,1,0:T(8,128)(2,1)}, bf16[4,16,32,128]{3,2,1,0:T(8,128)(2,1)S(1)}, u32[]{:S(2)}, u32[]{:S(2)}) collective-permute-start(bf16[4,16,32,128]{3,2,1,0:T(8,128)(2,1)} %term_products.23), channel_id=1, source_target_pairs={{0,12},{4,0},{8,4},{12,8},{1,13},{5,1},{9,5},{13,9},{2,14},{6,2},{... | collective-permute-start | bytes 1572872 | tf_op jit(solution)/shard_map/ppermute | solution.py:443
  124.7 9.4 %copy-start.16 = (bf16[4,16,32,128]{3,2,1,0:T(8,128)(2,1)S(1)}, bf16[4,16,32,128]{3,2,1,0:T(8,128)(2,1)}, u32[]{:S(2)}) copy-start(bf16[4,16,32,128]{3,2,1,0:T(8,128)(2,1)} %term_products.19) | copy-start | bytes 1572868
  134.1 18.8 %copy-start.17 = (bf16[4,16,32,128]{3,2,1,0:T(8,128)(2,1)}, bf16[4,16,32,128]{3,2,1,0:T(8,128)(2,1)S(1)}, u32[]{:S(2)}) copy-start(bf16[4,16,32,128]{3,2,1,0:T(8,128)(2,1)S(1)} %collective-permute-done.10.rest_1_) | copy-start | bytes 1572868
  134.2 38.0 %collective-permute-start.5 = (bf16[4,16,32,128]{3,2,1,0:T(8,128)(2,1)S(1)}, bf16[4,16,32,128]{3,2,1,0:T(8,128)(2,1)S(1)}, u32[]{:S(2)}, u32[]{:S(2)}) collective-permute-start(bf16[4,16,32,128]{3,2,1,0:T(8,128)(2,1)S(1)} %copy-done.16), channel_id=1, source_target_pairs={{0,12},{4,0},{8,4},{12,8},{1,13},{5,1},{9,5},{13,9},{2,14},{6,2},{... | collective-permute-start | bytes 1572872 | tf_op jit(solution)/shard_map/ppermute | solution.py:443
  171.9 20.8 %copy-start.1 = (bf16[8,32,16,128]{3,2,1,0:T(8,128)(2,1)S(1)}, bf16[8,32,16,128]{3,2,1,0:T(8,128)(2,1)}, u32[]{:S(2)}) copy-start(bf16[8,32,16,128]{3,2,1,0:T(8,128)(2,1)} %get-tuple-element.25.rest_6_) | copy-start | bytes 3145732
  171.9 21.4 %collective-permute-start.13 = (bf16[8,32,16,128]{3,2,1,0:T(8,128)(2,1)}, bf16[8,32,16,128]{3,2,1,0:T(8,128)(2,1)S(1)}, u32[]{:S(2)}, u32[]{:S(2)}) collective-permute-start(bf16[8,32,16,128]{3,2,1,0:T(8,128)(2,1)} %get-tuple-element.24.rest_3_), channel_id=1, source_target_pairs={{1,3},{2,0},{0,1},{3,2},{5,7},{6,4},{4,5},{7,6},{9,11},{10,8},{8,9... | collective-permute-start | bytes 3145736 | tf_op jit(solution)/shard_map/ppermute | solution.py:402
  191.9 24.3 %collective-permute-start.6 = (bf16[8,32,16,128]{3,2,1,0:T(8,128)(2,1)}, bf16[8,32,16,128]{3,2,1,0:T(8,128)(2,1)S(1)}, u32[]{:S(2)}, u32[]{:S(2)}) collective-permute-start(bf16[8,32,16,128]{3,2,1,0:T(8,128)(2,1)} %get-tuple-element.21.rest_0_), channel_id=1, source_target_pairs={{1,3},{2,0},{0,1},{3,2},{5,7},{6,4},{4,5},{7,6},{9,11},{10,8},{8,9... | collective-permute-start | bytes 3145736 | tf_op jit(solution)/shard_map/ppermute | solution.py:402
  192.7 42.9 %collective-permute-start.15 = (bf16[8,32,16,128]{3,2,1,0:T(8,128)(2,1)S(1)}, bf16[8,32,16,128]{3,2,1,0:T(8,128)(2,1)S(1)}, u32[]{:S(2)}, u32[]{:S(2)}) collective-permute-start(bf16[8,32,16,128]{3,2,1,0:T(8,128)(2,1)S(1)} %copy-done.1), channel_id=1, source_target_pairs={{0,2},{2,0},{1,3},{3,1},{4,6},{6,4},{5,7},{7,5},{8,10},{10,8},{9,1... | collective-permute-start | bytes 3145736 | tf_op jit(solution)/shard_map/ppermute | solution.py:405
  193.4 42.2 %copy-start.2 = (bf16[8,32,16,128]{3,2,1,0:T(8,128)(2,1)}, bf16[8,32,16,128]{3,2,1,0:T(8,128)(2,1)S(1)}, u32[]{:S(2)}) copy-start(bf16[8,32,16,128]{3,2,1,0:T(8,128)(2,1)S(1)} %collective-permute-done.13.rest_4_) | copy-start | bytes 3145732
  193.4 42.2 %collective-permute-start.14 = (bf16[8,32,16,128]{3,2,1,0:T(8,128)(2,1)S(1)}, bf16[8,32,16,128]{3,2,1,0:T(8,128)(2,1)S(1)}, u32[]{:S(2)}, u32[]{:S(2)}) collective-permute-start(bf16[8,32,16,128]{3,2,1,0:T(8,128)(2,1)S(1)} %collective-permute-done.13.rest_4_), channel_id=1, source_target_pairs={{0,1},{3,2},{4,5},{7,6},{8,9},{11,10},{12,13},{15,14},{16,17},{19,... | collective-permute-start | bytes 3145736 | tf_op jit(solution)/shard_map/ppermute | solution.py:403
  216.2 19.4 %copy-start.3 = (bf16[8,32,16,128]{3,2,1,0:T(8,128)(2,1)}, bf16[8,32,16,128]{3,2,1,0:T(8,128)(2,1)S(1)}, u32[]{:S(2)}) copy-start(bf16[8,32,16,128]{3,2,1,0:T(8,128)(2,1)S(1)} %collective-permute-done.6.rest_1_) | copy-start | bytes 3145732
  216.2 19.4 %collective-permute-start.7 = (bf16[8,32,16,128]{3,2,1,0:T(8,128)(2,1)S(1)}, bf16[8,32,16,128]{3,2,1,0:T(8,128)(2,1)S(1)}, u32[]{:S(2)}, u32[]{:S(2)}) collective-permute-start(bf16[8,32,16,128]{3,2,1,0:T(8,128)(2,1)S(1)} %collective-permute-done.6.rest_1_), channel_id=1, source_target_pairs={{0,1},{3,2},{4,5},{7,6},{8,9},{11,10},{12,13},{15,14},{16,17},{19,... | collective-permute-start | bytes 3145736 | tf_op jit(solution)/shard_map/ppermute | solution.py:403
  218.3 42.0 %collective-permute-start.19 = (bf16[8,32,16,128]{3,2,1,0:T(8,128)(2,1)}, bf16[8,32,16,128]{3,2,1,0:T(8,128)(2,1)S(1)}, u32[]{:S(2)}, u32[]{:S(2)}) collective-permute-start(bf16[8,32,16,128]{3,2,1,0:T(8,128)(2,1)} %get-tuple-element.28.rest_6_), channel_id=1, source_target_pairs={{0,2},{2,0},{1,3},{3,1},{4,6},{6,4},{5,7},{7,5},{8,10},{10,8},{9,1... | collective-permute-start | bytes 3145736 | tf_op jit(solution)/shard_map/ppermute | solution.py:405
  247.5 103.9 %collective-permute-start.16 = (bf16[4,16,32,128]{3,2,1,0:T(8,128)(2,1)}, bf16[4,16,32,128]{3,2,1,0:T(8,128)(2,1)S(1)}, u32[]{:S(2)}, u32[]{:S(2)}) collective-permute-start(bf16[4,16,32,128]{3,2,1,0:T(8,128)(2,1)} %term_products.25), channel_id=1, source_target_pairs={{0,4},{4,8},{8,12},{12,0},{1,5},{5,9},{9,13},{13,1},{2,6},{6,10},{... | collective-permute-start | bytes 1572872 | tf_op jit(solution)/shard_map/ppermute | solution.py:443
  257.2 94.2 %collective-permute-start.17 = (bf16[4,16,32,128]{3,2,1,0:T(8,128)(2,1)}, bf16[4,16,32,128]{3,2,1,0:T(8,128)(2,1)S(1)}, u32[]{:S(2)}, u32[]{:S(2)}) collective-permute-start(bf16[4,16,32,128]{3,2,1,0:T(8,128)(2,1)} %term_products.26), channel_id=1, source_target_pairs={{0,8},{4,12},{8,0},{12,4},{1,9},{5,13},{9,1},{13,5},{2,10},{6,14},... | collective-permute-start | bytes 1572872 | tf_op jit(solution)/shard_map/ppermute | solution.py:443
  271.0 52.1 %collective-permute-start.20 = (bf16[4,16,32,128]{3,2,1,0:T(8,128)(2,1)}, bf16[4,16,32,128]{3,2,1,0:T(8,128)(2,1)S(1)}, u32[]{:S(2)}, u32[]{:S(2)}) collective-permute-start(bf16[4,16,32,128]{3,2,1,0:T(8,128)(2,1)} %term_products.29), channel_id=1, source_target_pairs={{0,4},{4,8},{8,12},{12,0},{1,5},{5,9},{9,13},{13,1},{2,6},{6,10},{... | collective-permute-start | bytes 1572872 | tf_op jit(solution)/shard_map/ppermute | solution.py:443
  280.9 58.1 %collective-permute-start.21 = (bf16[4,16,32,128]{3,2,1,0:T(8,128)(2,1)}, bf16[4,16,32,128]{3,2,1,0:T(8,128)(2,1)S(1)}, u32[]{:S(2)}, u32[]{:S(2)}) collective-permute-start(bf16[4,16,32,128]{3,2,1,0:T(8,128)(2,1)} %term_products.30), channel_id=1, source_target_pairs={{0,8},{4,12},{8,0},{12,4},{1,9},{5,13},{9,1},{13,5},{2,10},{6,14},... | collective-permute-start | bytes 1572872 | tf_op jit(solution)/shard_map/ppermute | solution.py:443
  293.9 45.2 %collective-permute-start.22 = (bf16[4,16,32,128]{3,2,1,0:T(8,128)(2,1)}, bf16[4,16,32,128]{3,2,1,0:T(8,128)(2,1)S(1)}, u32[]{:S(2)}, u32[]{:S(2)}) collective-permute-start(bf16[4,16,32,128]{3,2,1,0:T(8,128)(2,1)} %term_products.31), channel_id=1, source_target_pairs={{0,12},{4,0},{8,4},{12,8},{1,13},{5,1},{9,5},{13,9},{2,14},{6,2},{... | collective-permute-start | bytes 1572872 | tf_op jit(solution)/shard_map/ppermute | solution.py:443
  313.3 9.8 %copy-start.20 = (bf16[4,16,32,128]{3,2,1,0:T(8,128)(2,1)S(1)}, bf16[4,16,32,128]{3,2,1,0:T(8,128)(2,1)}, u32[]{:S(2)}) copy-start(bf16[4,16,32,128]{3,2,1,0:T(8,128)(2,1)} %term_products.27) | copy-start | bytes 1572868
  323.1 16.0 %copy-start.19 = (bf16[4,16,32,128]{3,2,1,0:T(8,128)(2,1)}, bf16[4,16,32,128]{3,2,1,0:T(8,128)(2,1)S(1)}, u32[]{:S(2)}) copy-start(bf16[4,16,32,128]{3,2,1,0:T(8,128)(2,1)S(1)} %collective-permute-done.20.rest_1_) | copy-start | bytes 1572868
  323.1 28.4 %collective-permute-start.18 = (bf16[4,16,32,128]{3,2,1,0:T(8,128)(2,1)S(1)}, bf16[4,16,32,128]{3,2,1,0:T(8,128)(2,1)S(1)}, u32[]{:S(2)}, u32[]{:S(2)}) collective-permute-start(bf16[4,16,32,128]{3,2,1,0:T(8,128)(2,1)S(1)} %copy-done.20), channel_id=1, source_target_pairs={{0,12},{4,0},{8,4},{12,8},{1,13},{5,1},{9,5},{13,9},{2,14},{6,2},{... | collective-permute-start | bytes 1572872 | tf_op jit(solution)/shard_map/ppermute | solution.py:443
  (17 other events, 16.7 us)

commit v3 on v2

--- a/solution.py
+++ b/solution.py
@@ -16,13 +16,9 @@
 
 
 def layer_norm(values):
-    size = values.shape[1]
-    ones = jnp.ones((2 * size, size), jnp.bfloat16)
-    centred = values.astype(jnp.float32) - dot(values, ones[:size]) * (1.0 / size)
-    squares = centred * centred
-    high = squares.astype(jnp.bfloat16)
-    low = (squares - high.astype(jnp.float32)).astype(jnp.bfloat16)
-    variance = dot(jnp.concatenate([high, low], axis=1), ones) * (1.0 / size)
+    values = values.astype(jnp.float32)
+    centred = values - jnp.mean(values, axis=-1, keepdims=True)
+    variance = jnp.mean(centred * centred, axis=-1, keepdims=True)
     return centred * lax.rsqrt(variance + norm_epsilon)
 
 
@@ -414,6 +410,435 @@
     return [(left, left, 0, 0)], [[(r, r, 0, 0)] for r in gathered]
 
 
+def lane_group(shape, size):
+    return lax.broadcasted_iota(jnp.int32, shape, 1) // size
+
+
+def spread_weights(w_ref, wide_ref, hidden, size):
+    parts = hidden // size
+    for kind in range(4):
+        weights = w_ref[0, :, kind * hidden : (kind + 1) * hidden].astype(jnp.float32)
+        group = lane_group(weights.shape, size)
+        for part in range(parts):
+            kept = jnp.where(group == part, weights, 0.0)
+            for a in range(parts):
+                moved = pltpu.roll(kept, ((a - part) % parts) * size, 1) if a != part else kept
+                at = (kind * parts + part) * hidden
+                wide_ref[a * hidden : (a + 1) * hidden, at : at + hidden] = moved.astype(jnp.bfloat16)
+
+
+def make_operands(taken, wide_ref, row_alive, k_alive, out_refs, laid, turned):
+    rows, size, hidden = taken.shape
+    parts, bands = hidden // size, size
+    groups = rows // parts
+    stacked = jnp.concatenate(
+        [jnp.concatenate([taken[g * parts + a] for a in range(parts)], axis=1) for g in range(groups)], axis=0
+    )
+    mask = (row_alive[:, None, :] * k_alive[None, :, :]).reshape(groups * size, hidden)
+    for part in range(parts):
+        made = []
+        for kind in range(4):
+            at = (kind * parts + part) * hidden
+            made.append(dot(stacked, wide_ref[:, at : at + hidden]))
+        for side in range(2):
+            value = mask * sigmoid(made[2 * side + 1]) * made[2 * side]
+            laid[side, :, part * size : (part + 1) * size, :] = value.reshape(groups, size, hidden)
+    for side in range(2):
+        for g in range(groups):
+            block = laid[side, g].T
+            for a in range(parts):
+                turned[side, pl.ds(g * parts + a, bands, stride=rows), :] = block[a * bands : (a + 1) * bands]
+        start = 0
+        for ref in out_refs[side]:
+            count = ref.shape[1]
+            value = turned[side, start * rows : (start + count) * rows].astype(jnp.bfloat16)
+            ref[0] = value.reshape(count, rows, hidden)
+            start += count
+
+
+def alive_groups(chain_ref, start, rows, parts):
+    lanes = chain_ref.shape[1]
+    groups = rows // parts
+    line = chain_ref[pl.ds(start // lanes, 1), :] >= 0
+    row = lax.broadcasted_iota(jnp.int32, (groups, lanes), 1) - lax.rem(start, lanes)
+    group = lax.broadcasted_iota(jnp.int32, (groups, lanes), 0)
+    pick = jnp.logical_and(jnp.logical_and(row >= group * parts, row < (group + 1) * parts), line)
+    fold = lax.rem(lax.broadcasted_iota(jnp.int32, (lanes, lanes), 0), parts) == lane_group(
+        (lanes, lanes), lanes // parts
+    )
+    return dot(pick.astype(jnp.float32).astype(jnp.bfloat16), fold.astype(jnp.float32).astype(jnp.bfloat16))
+
+
+def open_kernel(hidden, chunks, n_chan, n_sub, ids, blocks, pair_ref, chain_ref, w_ref, gate_ref, *rest):
+    left_refs, right_refs = rest[:chunks], rest[chunks : 2 * chunks]
+    wide, laid, turned = rest[2 * chunks :]
+    slots = pl.num_programs(0)
+    step = pl.program_id(0)
+    _, rows, cols, channels = pair_ref.shape
+    block = ids[0] * slots + step
+
+    @pl.when(step == 0)
+    def _():
+        spread_weights(w_ref, wide, hidden, cols)
+
+    normed = layer_norm(pair_ref[0].reshape(rows * cols, channels)).astype(jnp.bfloat16)
+    gate = sigmoid(dot(normed, w_ref[0, :, 4 * hidden :]))
+    gate_ref[0] = gate.reshape(rows, cols, channels)
+    row_alive = alive_groups(chain_ref, (blocks[0, block] * n_chan + ids[1]) * rows, rows, hidden // cols)
+    k_alive = alive_rows(chain_ref, (blocks[1, block] * n_sub + ids[2]) * cols, cols)
+    taken = normed.reshape(rows, cols, channels)
+    make_operands(taken, wide, row_alive, k_alive, (left_refs, right_refs), laid, turned)
+
+
+def operand_scratch(rows, size, hidden):
+    parts = hidden // size
+    return [
+        pltpu.VMEM((parts * hidden, 4 * parts * hidden), jnp.bfloat16),
+        pltpu.VMEM((2, rows // parts, parts * size, hidden), jnp.float32),
+        pltpu.VMEM((2, size * rows, hidden), jnp.float32),
+    ]
+
+
+def open_operands(ids, blocks, pair, chains, w_in, hidden, bands):
+    slots, rows, cols, channels = pair.shape
+    operands = [jax.ShapeDtypeStruct((slots, count, rows, hidden), jnp.bfloat16) for count in bands] * 2
+    out = pl.pallas_call(
+        functools.partial(open_kernel, hidden, len(bands), lax.axis_size("chan"), lax.axis_size("sub")),
+        grid_spec=pltpu.PrefetchScalarGridSpec(
+            num_scalar_prefetch=2,
+            grid=(slots,),
+            in_specs=[
+                pl.BlockSpec((1, rows, cols, channels), lambda s, *_: (s, 0, 0, 0)),
+                pl.BlockSpec(chains.shape, lambda s, *_: (0, 0)),
+                pl.BlockSpec((1,) + w_in.shape[1:], lambda s, *_: (0, 0, 0)),
+            ],
+            out_specs=[pl.BlockSpec((1, rows, cols, channels), lambda s, *_: (s, 0, 0, 0))]
+            + [pl.BlockSpec((1,) + o.shape[1:], lambda s, *_: (s, 0, 0, 0)) for o in operands],
+            scratch_shapes=operand_scratch(rows, cols, hidden),
+        ),
+        out_shape=[jax.ShapeDtypeStruct(pair.shape, jnp.float32)] + operands,
+        compiler_params=pltpu.CompilerParams(vmem_limit_bytes=vmem_limit),
+        name="open_operands",
+    )(ids, blocks, pair, chains, w_in)
+    return out[0], out[1 : 1 + len(bands)], out[1 + len(bands) :]
+
+
+def banded_kernel(shift, n_blk, slots_dev, terms, capacity, pieces, n_refs, size, ids, owners, slots, *rest):
+    refs = rest[:n_refs]
+    out_ref, left_held, right_held, chosen, sems = rest[n_refs:]
+    step = pl.program_id(0)
+    turn = lax.rem(step, 2)
+    _, halves, bands, rows, hidden = left_held.shape
+    cols = right_held.shape[3]
+    parts = hidden // size
+
+    @pl.when(step == 0)
+    def _():
+        target = lax.rem(ids[0] + shift, n_blk)
+        for e in range(2 * capacity):
+            chosen[e] = 0
+
+        def scan(e, count):
+            block, term = target * slots_dev + e // terms, lax.rem(e, terms)
+            here = jnp.logical_and(owners[term, block] == ids[0], count < capacity)
+
+            @pl.when(here)
+            def _():
+                chosen[2 * count] = slots[term, 0, block]
+                chosen[2 * count + 1] = slots[term, 1, block]
+
+            return count + here.astype(jnp.int32)
+
+        lax.fori_loop(0, slots_dev * terms, scan, jnp.int32(0))
+
+    def copy(n, term, buffer, source):
+        side, half, *_ = pieces[n]
+        held = (left_held, right_held)[side]
+        return pltpu.make_async_copy(
+            refs[source].at[chosen[2 * term + side]], held.at[buffer, half], sems.at[buffer, n]
+        )
+
+    def start(term, buffer):
+        for n, (_, _, on, off) in enumerate(pieces):
+            if on == off:
+                copy(n, term, buffer, on).start()
+            else:
+
+                @pl.when(ids[3] == 1)
+                def _(n=n, on=on):
+                    copy(n, term, buffer, on).start()
+
+                @pl.when(ids[3] == 0)
+                def _(n=n, off=off):
+                    copy(n, term, buffer, off).start()
+
+    @pl.when(step == 0)
+    def _():
+        start(0, 0)
+
+    @pl.when(step + 1 < capacity)
+    def _():
+        start(step + 1, 1 - turn)
+
+    for n, piece in enumerate(pieces):
+        copy(n, step, turn, piece[2]).wait()
+
+    group = lax.rem(lane_group((cols, halves * hidden), size), parts)
+    for band in range(bands):
+        left = jnp.concatenate([left_held[turn, h, band] for h in range(halves)], axis=1)
+        right = jnp.concatenate([right_held[turn, h, band] for h in range(halves)], axis=1)
+        apart = jnp.concatenate(
+            [jnp.where(group == part, right, jnp.zeros_like(right)) for part in range(parts)], axis=0
+        )
+        made = lax.dot_general(left, apart, (((1,), (1,)), ((), ())), preferred_element_type=jnp.float32)
+        out_ref[0, band] = made.astype(jnp.bfloat16)
+
+
+def banded_products(shift, ids, owners, slots, lefts, rights, capacity, slots_dev, terms, size):
+    n_blk = lax.axis_size("blk")
+    refs, pieces = [], []
+
+    def index_of(array):
+        for n, known in enumerate(refs):
+            if known is array:
+                return n
+        refs.append(array)
+        return len(refs) - 1
+
+    for side, operands in ((0, lefts), (1, rights)):
+        for half, (on, off) in enumerate(operands):
+            pieces.append((side, half, index_of(on), index_of(off)))
+    _, bands, rows, hidden = lefts[0][0].shape
+    cols = rights[0][0].shape[2]
+    return pl.pallas_call(
+        functools.partial(
+            banded_kernel, shift, n_blk, slots_dev, terms, capacity, tuple(pieces), len(refs), size
+        ),
+        grid_spec=pltpu.PrefetchScalarGridSpec(
+            num_scalar_prefetch=3,
+            grid=(capacity,),
+            in_specs=[pl.BlockSpec(memory_space=pl.ANY)] * len(refs),
+            out_specs=pl.BlockSpec((1, bands, rows, hidden), lambda t, *_: (t, 0, 0, 0)),
+            scratch_shapes=[
+                pltpu.VMEM((2, len(lefts), bands, rows, hidden), jnp.bfloat16),
+                pltpu.VMEM((2, len(rights), bands, cols, hidden), jnp.bfloat16),
+                pltpu.SMEM((2 * capacity,), jnp.int32),
+                pltpu.SemaphoreType.DMA((2, len(pieces))),
+            ],
+        ),
+        out_shape=jax.ShapeDtypeStruct((capacity, bands, rows, hidden), jnp.bfloat16),
+        compiler_params=pltpu.CompilerParams(vmem_limit_bytes=vmem_limit),
+        cost_estimate=pl.CostEstimate(
+            flops=2 * capacity * bands * rows * hidden * hidden * len(lefts) * 50,
+            bytes_accessed=capacity * bands * rows * hidden * 2 * 5,
+            transcendentals=0,
+        ),
+        name="banded_products",
+    )(ids, owners, slots, *refs)
+
+
+def close_kernel(last, n_parts, n_blk, n_chan, n_sub, slots_dev, terms, capacity, ids, blocks, owners, *rest):
+    chunks = n_parts // n_blk
+    arrived, rest = rest[:n_parts], rest[n_parts:]
+    cur_ref, gate_ref, w_out_ref = rest[:3]
+    if last:
+        out_ref, held, summed, wide_out, place, seen, sems = rest[3:]
+    else:
+        chain_ref, w_ref, out_ref, next_gate_ref = rest[3:7]
+        left_refs, right_refs = rest[7 : 7 + chunks], rest[7 + chunks : 7 + 2 * chunks]
+        held, summed, wide_out, place, seen, sems, norm_ref, wide, laid, turned = rest[7 + 2 * chunks :]
+    step = pl.program_id(0)
+    _, rows, cols, channels = cur_ref.shape
+    _, bands, _, hidden = held.shape
+    parts, size = hidden // bands, bands
+
+    def arrival(n):
+        at = sum(arrived[m * n_blk].shape[1] for m in range(n // n_blk))
+        count = arrived[n].shape[1]
+        target = held.at[pl.ds(n % n_blk * capacity, capacity), pl.ds(at, count)]
+        return pltpu.make_async_copy(arrived[n], target, sems.at[n])
+
+    @pl.when(step == 0)
+    def _():
+        for n in range(n_parts):
+            arrival(n).start()
+        for shift in range(n_blk):
+            seen[shift] = 0
+
+        def scan(e, carry):
+            owner = owners[lax.rem(e, terms), ids[0] * slots_dev + e // terms]
+            shift = lax.rem(ids[0] - owner + n_blk, n_blk)
+            count = seen[owner]
+            seen[owner] = count + 1
+            place[e] = shift * capacity + count
+            return carry
+
+        lax.fori_loop(0, slots_dev * terms, scan, jnp.int32(0))
+        wide_out[...] = jnp.zeros_like(wide_out)
+        for part in range(parts):
+            for a in range(parts):
+                at = (part * parts + a) * bands
+                wide_out[at : at + bands, a * channels : (a + 1) * channels] = w_out_ref[
+                    0, part * bands : (part + 1) * bands, :
+                ]
+        if not last:
+            spread_weights(w_ref, wide, hidden, rows)
+        for n in range(n_parts):
+            arrival(n).wait()
+
+    span = 4
+    for band in range(0, bands, span):
+        taken = pl.ds(band, span)
+        total = held[place[step * terms], taken].astype(jnp.float32)
+        for t in range(1, terms):
+            total = total + held[place[step * terms + t], taken].astype(jnp.float32)
+        rounded = total.astype(jnp.bfloat16).astype(jnp.float32)
+        summed[pl.ds(band * rows, span * rows), :] = rounded.reshape(span * rows, hidden)
+    groups = rows // parts
+    pieces = []
+    for g in range(groups):
+        block = jnp.concatenate([summed[pl.ds(g * parts + a, bands, stride=rows), :] for a in range(parts)]).T
+        pieces.append(jnp.concatenate([block[p * cols : (p + 1) * cols] for p in range(parts)], axis=1))
+    mixture = jnp.concatenate(pieces)
+    together = (lane_group((hidden, hidden), size) == lax.broadcasted_iota(jnp.int32, (hidden, hidden), 0) // size)
+    together = together.astype(jnp.float32).astype(jnp.bfloat16)
+    average = dot(mixture.astype(jnp.bfloat16), jnp.concatenate([together] * parts)) * (1.0 / hidden)
+    centred = [mixture[:, p * hidden : (p + 1) * hidden] - average for p in range(parts)]
+    squares = sum(c * c for c in centred)
+    high = squares.astype(jnp.bfloat16)
+    low = (squares - high.astype(jnp.float32)).astype(jnp.bfloat16)
+    variance = dot(jnp.concatenate([high, low], axis=1), jnp.concatenate([together] * 2)) * (1.0 / hidden)
+    scale = lax.rsqrt(variance + norm_epsilon)
+    normed = jnp.concatenate([(c * scale).astype(jnp.bfloat16) for c in centred], axis=1)
+    update = dot(normed, wide_out[...])
+    for g in range(groups):
+        taken = pl.ds(g * parts, parts)
+        change = jnp.concatenate(
+            [update[g * cols : (g + 1) * cols, a * channels : (a + 1) * channels] for a in range(parts)]
+        )
+        gate = gate_ref[0, taken].reshape(parts * cols, channels)
+        current = cur_ref[0, taken].astype(jnp.float32).reshape(parts * cols, channels)
+        result = (current + gate * change).astype(jnp.bfloat16)
+        out_ref[0, taken] = result.reshape(parts, cols, channels)
+        if not last:
+            norm = layer_norm(result)
+            norm_ref[pl.ds(g * parts * cols, parts * cols), :] = norm
+            next_gate = sigmoid(dot(norm.astype(jnp.bfloat16), w_ref[0, :, 4 * hidden :]))
+            next_gate_ref[0, taken] = next_gate.reshape(parts, cols, channels)
+    if not last:
+        block = ids[0] * slots_dev + step
+        k_alive = alive_rows(chain_ref, (blocks[0, block] * n_chan + ids[1]) * rows, rows)
+        col_alive = alive_groups(chain_ref, (blocks[1, block] * n_sub + ids[2]) * cols, cols, parts)
+        taken = jnp.stack([norm_ref[pl.ds(col, rows, stride=cols), :].astype(jnp.bfloat16) for col in range(cols)])
+        make_operands(taken, wide, col_alive, k_alive, (left_refs, right_refs), laid, turned)
+
+
+def close_layer(layer, arrived, ids, blocks, owners, current, gate, w_out, capacity, terms, chains, w_in, last, bands):
+    n_blk = len(arrived[0])
+    flat = [part for chunk in arrived for part in chunk]
+    slots, rows, cols, channels = current.shape
+    hidden = w_out.shape[1]
+    whole = pl.BlockSpec((1, rows, cols, channels), lambda s, *_: (s, 0, 0, 0))
+
+    def layer_spec(array, index):
+        return pl.BlockSpec((1,) + array.shape[1:], lambda s, *_: (index, 0, 0))
+
+    in_specs = [pl.BlockSpec(memory_space=pl.ANY)] * len(flat) + [whole, whole, layer_spec(w_out, layer)]
+    operands = [*flat, current, gate, w_out]
+    out_shape = [jax.ShapeDtypeStruct(current.shape, jnp.bfloat16)]
+    out_specs = [whole]
+    scratch = [
+        pltpu.VMEM((n_blk * capacity, sum(bands), rows, hidden), jnp.bfloat16),
+        pltpu.VMEM((sum(bands) * rows, hidden), jnp.float32),
+        pltpu.VMEM((hidden // cols * hidden, hidden // cols * channels), jnp.bfloat16),
+        pltpu.SMEM((slots * terms,), jnp.int32),
+        pltpu.SMEM((n_blk,), jnp.int32),
+        pltpu.SemaphoreType.DMA((len(flat),)),
+    ]
+    if not last:
+        operands += [chains, w_in]
+        in_specs += [pl.BlockSpec(chains.shape, lambda s, *_: (0, 0)), layer_spec(w_in, layer + 1)]
+        made = [jax.ShapeDtypeStruct((slots, count, cols, hidden), jnp.bfloat16) for count in bands] * 2
+        out_shape += [jax.ShapeDtypeStruct(current.shape, jnp.float32)] + made
+        out_specs += [whole] + [pl.BlockSpec((1,) + o.shape[1:], lambda s, *_: (s, 0, 0, 0)) for o in made]
+        scratch += [pltpu.VMEM((rows * cols, channels), jnp.float32)] + operand_scratch(cols, rows, hidden)
+    out = pl.pallas_call(
+        functools.partial(
+            close_kernel, last, len(flat), n_blk, lax.axis_size("chan"), lax.axis_size("sub"), slots, terms, capacity
+        ),
+        grid_spec=pltpu.PrefetchScalarGridSpec(
+            num_scalar_prefetch=3, grid=(slots,), in_specs=in_specs, out_specs=out_specs, scratch_shapes=scratch
+        ),
+        out_shape=out_shape,
+        compiler_params=pltpu.CompilerParams(vmem_limit_bytes=vmem_limit),
+        name="close_layer",
+    )(ids, blocks, owners, *operands)
+    if last:
+        return out[0]
+    return out[0], out[1], out[2 : 2 + len(bands)], out[2 + len(bands) :]
+
+
+def after(value, *others):
+    return lax.optimization_barrier((value, *others))[0]
+
+
+def exchange_bands_outgoing(lefts, rights):
+    both = ("chan", "sub")
+    made = []
+    for left, right in zip(lefts, rights):
+        if made:
+            (_, other_left), *_ = made[-1][0]
+            _, (_, two) = made[-1][1]
+            right = after(right, two)
+        other_left = lax.ppermute(left, "sub", [(0, 1), (1, 0)])
+        one = lax.ppermute(right, both, [(0, 2), (3, 1), (1, 0), (2, 3)])
+        two = lax.ppermute(right, both, [(1, 2), (2, 1)])
+        made.append(([(other_left, left), (left, other_left)], [(one, one), (right, two)]))
+    return made
+
+
+def exchange_bands_incoming(lefts, rights):
+    both = ("chan", "sub")
+    made = []
+    for left, right in zip(lefts, rights):
+        if made:
+            right, left = lax.optimization_barrier((right, left, made[-1][1][1][0]))[:2]
+        one = lax.ppermute(left, both, [(1, 3), (2, 0), (0, 1), (3, 2)])
+        two = lax.ppermute(one, both, [(0, 1), (3, 2)])
+        other = lax.ppermute(right, "chan", [(0, 1), (1, 0)])
+        made.append(([(left, one), (one, two)], [(right, right), (other, other)]))
+    return made
+
+
+def banded(pair, ids, blocks, owners, slot_of, chains, w_in, w_out, capacity, terms, n_blk):
+    slots, rows, cols, channels = pair.shape
+    hidden = w_out.shape[1]
+    shifts = [n_blk // 2] + [s for s in range(1, n_blk) if s != n_blk // 2] + [0]
+    layers = w_in.shape[0]
+    current = pair
+    for layer in range(layers):
+        bands = [cols // 2, cols // 2]
+        if layer == 0:
+            gate, lefts, rights = open_operands(ids, blocks, pair, chains, w_in, hidden, bands)
+        exchange = exchange_bands_incoming if layer % 2 else exchange_bands_outgoing
+        arrived = []
+        for left, right in exchange(lefts, rights):
+            parts = [None] * n_blk
+            for shift in shifts:
+                made = banded_products(shift, ids, owners, slot_of, left, right, capacity, slots, terms, cols)
+                if shift:
+                    made = lax.ppermute(made, "blk", [(p, (p + shift) % n_blk) for p in range(n_blk)])
+                parts[shift] = made
+            arrived.append(parts)
+        last = layer == layers - 1
+        out = close_layer(
+            layer, arrived, ids, blocks, owners, current, gate, w_out, capacity, terms, chains, w_in, last, bands
+        )
+        if last:
+            return out
+        current, gate, lefts, rights = out
+
+
 def per_device(pair, block_list, term_owner, term_slots, chain_ids, w_in, w_out):
     n_blk = lax.axis_size("blk")
     n_chan = lax.axis_size("chan")
@@ -432,6 +857,8 @@
     owners = term_owner.T
     slot_of = jnp.transpose(term_slots, (1, 2, 0))
     chains = chain_ids.reshape(-1, 128)
+    if fast and rows == cols and channels == hidden == 128 and hidden % cols == 0:
+        return banded(pair, ids, blocks, owners, slot_of, chains, w_in, w_out, capacity, terms, n_blk)
     shifts = [n_blk // 2] + [s for s in range(1, n_blk) if s != n_blk // 2] + [0]
 
     def all_products(lefts, right):

time: 367 us -> 340 us (0.926)
  Pallas kernels: 228 us -> 157 us
  starting transfers between devices: 30.6 us -> 56 us
  waiting for transfers between devices: 92.8 us -> 116 us
    pallas_call x21 -> x19, Pallas kernels: 228 us -> 157 us  [the longest x16 89 us: banded_products(): pl.pallas_call(functools.partial(banded_kernel, shift, n_blk, slots_dev,...]
    ppermute x23 -> x24, starting transfers between devices: 30.6 us -> 56 us  [the longest x2 27.3 us: exchange_bands_outgoing(): one = lax.ppermute(right, both, [(0, 2), (3, 1), (1, 0), (2, 3)])]
    ppermute x23 -> x24, waiting for transfers between devices: 92.8 us -> 116 us  [the longest x12 77.5 us: banded(): lax.ppermute(made, 'blk', [(p, (p + shift) % n_blk) for p in range(n_blk)])]
    unnamed x52 -> x50, local copies, waits for them, and re-layouts: 11.2 us -> 7.8 us
  transfers between devices with their start and end apart: 23 -> 24, of which waited for: 6 -> 12; matrix products, arithmetic and copies ran while one was open for 0% -> 0% of each run, Pallas kernels for 55% -> 26%
where the time goes in v3:
time: 340 us; the launch traced here: 338 us
  Pallas kernels  157 us (46%)
  waiting for transfers between devices  116 us (34%)
  starting transfers between devices  56 us (16%)
  local copies, waits for them, and re-layouts  7.8 us (2%)
    pallas_call x16, Pallas kernels, banded_products(): pl.pallas_call(functools.partial(banded_kernel, shift, n_blk, slots_dev,...  89 us
    ppermute x12, waiting for transfers between devices, banded(): lax.ppermute(made, 'blk', [(p, (p + shift) % n_blk) for p in range(n_blk)])  77.5 us
    pallas_call x2, Pallas kernels, close_layer(): pl.pallas_call(functools.partial(close_kernel, last, len(flat), n_blk, la...  46.6 us
    ppermute x2, waiting for transfers between devices, exchange_bands_incoming(): one = lax.ppermute(left, both, [(1, 3), (2, 0), (0, 1), (3, 2)])  29.1 us
    ppermute x2, starting transfers between devices, exchange_bands_outgoing(): one = lax.ppermute(right, both, [(0, 2), (3, 1), (1, 0), (2, 3)])  27.3 us
    pallas_call x1, Pallas kernels, open_operands(): pl.pallas_call(functools.partial(open_kernel, hidden, len(bands), lax.axi...  21.5 us
    ppermute x12, starting transfers between devices, banded(): lax.ppermute(made, 'blk', [(p, (p + shift) % n_blk) for p in range(n_blk)])  13.7 us
    ppermute x2, waiting for transfers between devices, exchange_bands_incoming(): other = lax.ppermute(right, 'chan', [(0, 1), (1, 0)])  9.21 us
  transfers between devices with their start and end apart: 24, of which 12 were waited for; matrix products, arithmetic and copies ran while one was open for 0% of the time, Pallas kernels for 26%

profile of v3, /device:TPU:11, one launch (start us, length us, event | category | flops | bytes accessed | tf_op | source)
XLA Modules:
  0.0 338.0 jit_solution(13945626390977771062)
XLA Ops:
  0.7 21.5 %open_operands.1 = (f32[8,32,32,128]{3,2,1,0:T(8,128)}, bf16[8,16,32,128]{3,2,1,0:T(8,128)(2,1)}, bf16[8,16,32,128]{3,2,1,0:T(8,128)(2,1)}, bf16[8,16,32,128]{3,2,1,0:T(8,128)(2,1)}, bf16[8,16,32,128]{3,2,1,0:T(8,128)(2,1)}) custom-call(s32[4]{0:T(128)} %pad_add_fusion.ids, s32[2,32]{1,0:T(2,128)} %bitcast.10, bf16[8,32,32,128]{3,2,1,0:T(8,128)(2,1)} %rest_8_.1, ...), custom_call_target="tpu_custom_call" | custom-call | tf_op jit(solution)/shard_map/open_operands/pallas_call | solution.py:505
  26.9 26.0 %collective-permute-start.7 = (bf16[8,16,32,128]{3,2,1,0:T(8,128)(2,1)}, bf16[8,16,32,128]{3,2,1,0:T(8,128)(2,1)S(1)}, u32[]{:S(2)}, u32[]{:S(2)}) collective-permute-start(bf16[8,16,32,128]{3,2,1,0:T(8,128)(2,1)} %get-tuple-element.23.rest_3_), channel_id=1, source_target_pairs={{0,2},{3,1},{1,0},{2,3},{4,6},{7,5},{5,4},{6,7},{8,10},{11,9},{9,8... | collective-permute-start | bytes 3145736 | tf_op jit(solution)/shard_map/ppermute | solution.py:794
  54.2 5.6 %banded_products.17 = bf16[4,16,32,128]{3,2,1,0:T(8,128)(2,1)} custom-call(s32[4]{0:T(128)} %pad_add_fusion.ids, s32[2,32]{1,0:T(2,128)} %bitcast.13, s32[2,2,32]{2,1,0:T(2,128)} %bitcast.31, bf16[8,16,32,128]{3,2,1,0:T(8,128)(2,1)} %copy-done.22, bf16[8,16,32,128]{3,2,1,0:T(8,128)(2,1)} %get-tuple-element.19.rest_1_, bf16[8,16,32,128]{3,2,1,0:T(8,128)(2,1)} %copy-done.23, ...), custom_call_target="tpu_custom_call" | custom-call | flops 6710886400 | bytes 2621440 | tf_op jit(solution)/shard_map/banded_products/pallas_call | solution.py:613
  61.2 5.5 %banded_products.18 = bf16[4,16,32,128]{3,2,1,0:T(8,128)(2,1)} custom-call(s32[4]{0:T(128)} %pad_add_fusion.ids, s32[2,32]{1,0:T(2,128)} %bitcast.14, s32[2,2,32]{2,1,0:T(2,128)} %bitcast.32, bf16[8,16,32,128]{3,2,1,0:T(8,128)(2,1)} %copy-done.22, bf16[8,16,32,128]{3,2,1,0:T(8,128)(2,1)} %get-tuple-element.19.rest_1_, bf16[8,16,32,128]{3,2,1,0:T(8,128)(2,1)} %copy-done.23, ...), custom_call_target="tpu_custom_call" | custom-call | flops 6710886400 | bytes 2621440 | tf_op jit(solution)/shard_map/banded_products/pallas_call | solution.py:613
  67.8 5.6 %banded_products.19 = bf16[4,16,32,128]{3,2,1,0:T(8,128)(2,1)} custom-call(s32[4]{0:T(128)} %pad_add_fusion.ids, s32[2,32]{1,0:T(2,128)} %bitcast.15, s32[2,2,32]{2,1,0:T(2,128)} %bitcast.33, bf16[8,16,32,128]{3,2,1,0:T(8,128)(2,1)} %copy-done.22, bf16[8,16,32,128]{3,2,1,0:T(8,128)(2,1)} %get-tuple-element.19.rest_1_, bf16[8,16,32,128]{3,2,1,0:T(8,128)(2,1)} %copy-done.23, ...), custom_call_target="tpu_custom_call" | custom-call | flops 6710886400 | bytes 2621440 | tf_op jit(solution)/shard_map/banded_products/pallas_call | solution.py:613
  73.4 5.7 %banded_products.16.rest_0_ = bf16[4,16,32,128]{3,2,1,0:T(8,128)(2,1)} custom-call(s32[4]{0:T(128)} %pad_add_fusion.ids, s32[2,32]{1,0:T(2,128)} %bitcast.16, s32[2,2,32]{2,1,0:T(2,128)} %bitcast.34, bf16[8,16,32,128]{3,2,1,0:T(8,128)(2,1)} %copy-done.22, bf16[8,16,32,128]{3,2,1,0:T(8,128)(2,1)} %get-tuple-element.19.rest_1_, ...), custom_call_target="tpu_custom_call" | custom-call | flops 6710886400 | bytes 2621440 | tf_op jit(solution)/shard_map/banded_products/pallas_call | solution.py:613
  82.6 5.6 %banded_products.21 = bf16[4,16,32,128]{3,2,1,0:T(8,128)(2,1)} custom-call(s32[4]{0:T(128)} %pad_add_fusion.ids, s32[2,32]{1,0:T(2,128)} %bitcast.17, s32[2,2,32]{2,1,0:T(2,128)} %bitcast.35, bf16[8,16,32,128]{3,2,1,0:T(8,128)(2,1)} %copy-done.12, bf16[8,16,32,128]{3,2,1,0:T(8,128)(2,1)} %get-tuple-element.21.rest_1_, bf16[8,16,32,128]{3,2,1,0:T(8,128)(2,1)} %copy-done.15, ...), custom_call_target="tpu_custom_call" | custom-call | flops 6710886400 | bytes 2621440 | tf_op jit(solution)/shard_map/banded_products/pallas_call | solution.py:613
  88.2 5.5 %banded_products.22 = bf16[4,16,32,128]{3,2,1,0:T(8,128)(2,1)} custom-call(s32[4]{0:T(128)} %pad_add_fusion.ids, s32[2,32]{1,0:T(2,128)} %bitcast.18, s32[2,2,32]{2,1,0:T(2,128)} %bitcast.36, bf16[8,16,32,128]{3,2,1,0:T(8,128)(2,1)} %copy-done.12, bf16[8,16,32,128]{3,2,1,0:T(8,128)(2,1)} %get-tuple-element.21.rest_1_, bf16[8,16,32,128]{3,2,1,0:T(8,128)(2,1)} %copy-done.15, ...), custom_call_target="tpu_custom_call" | custom-call | flops 6710886400 | bytes 2621440 | tf_op jit(solution)/shard_map/banded_products/pallas_call | solution.py:613
  97.0 5.5 %banded_products.23 = bf16[4,16,32,128]{3,2,1,0:T(8,128)(2,1)} custom-call(s32[4]{0:T(128)} %pad_add_fusion.ids, s32[2,32]{1,0:T(2,128)} %bitcast.19, s32[2,2,32]{2,1,0:T(2,128)} %bitcast.37, bf16[8,16,32,128]{3,2,1,0:T(8,128)(2,1)} %copy-done.12, bf16[8,16,32,128]{3,2,1,0:T(8,128)(2,1)} %get-tuple-element.21.rest_1_, bf16[8,16,32,128]{3,2,1,0:T(8,128)(2,1)} %copy-done.15, ...), custom_call_target="tpu_custom_call" | custom-call | flops 6710886400 | bytes 2621440 | tf_op jit(solution)/shard_map/banded_products/pallas_call | solution.py:613
  102.6 5.5 %banded_products.20.rest_4_ = bf16[4,16,32,128]{3,2,1,0:T(8,128)(2,1)} custom-call(s32[4]{0:T(128)} %pad_add_fusion.ids, s32[2,32]{1,0:T(2,128)} %bitcast.20, s32[2,2,32]{2,1,0:T(2,128)} %bitcast.38, bf16[8,16,32,128]{3,2,1,0:T(8,128)(2,1)} %copy-done.12, bf16[8,16,32,128]{3,2,1,0:T(8,128)(2,1)} %get-tuple-element.21.rest_1_, ...), custom_call_target="tpu_custom_call" | custom-call | flops 6710886400 | bytes 2621440 | tf_op jit(solution)/shard_map/banded_products/pallas_call | solution.py:613
  108.2 21.1 %collective-permute-done.4.rest_2_ = bf16[4,16,32,128]{3,2,1,0:T(8,128)(2,1)S(1)} collective-permute-done((bf16[4,16,32,128]{3,2,1,0:T(8,128)(2,1)}, bf16[4,16,32,128]{3,2,1,0:T(8,128)(2,1)S(1)}, u32[]{:S(2)}, u32[]{:S(2)}) %collective-permute-start.4) | collective-permute-done | bytes 524320 | tf_op jit(solution)/shard_map/ppermute | solution.py:830
  130.1 10.5 %collective-permute-done.9.rest_5_ = bf16[4,16,32,128]{3,2,1,0:T(8,128)(2,1)S(1)} collective-permute-done((bf16[4,16,32,128]{3,2,1,0:T(8,128)(2,1)}, bf16[4,16,32,128]{3,2,1,0:T(8,128)(2,1)S(1)}, u32[]{:S(2)}, u32[]{:S(2)}) %collective-permute-start.9) | collective-permute-done | bytes 524320 | tf_op jit(solution)/shard_map/ppermute | solution.py:830
  140.6 10.4 %collective-permute-done.10.rest_6_ = bf16[4,16,32,128]{3,2,1,0:T(8,128)(2,1)S(1)} collective-permute-done((bf16[4,16,32,128]{3,2,1,0:T(8,128)(2,1)}, bf16[4,16,32,128]{3,2,1,0:T(8,128)(2,1)S(1)}, u32[]{:S(2)}, u32[]{:S(2)}) %collective-permute-start.10) | collective-permute-done | bytes 524320 | tf_op jit(solution)/shard_map/ppermute | solution.py:830
  153.4 33.1 %close_layer.2 = (bf16[8,32,32,128]{3,2,1,0:T(8,128)(2,1)}, f32[8,32,32,128]{3,2,1,0:T(8,128)}, bf16[8,16,32,128]{3,2,1,0:T(8,128)(2,1)}, bf16[8,16,32,128]{3,2,...) custom-call(s32[4]{0:T(128)} %pad_add_fusion.ids, s32[2,32]{1,0:T(2,128)} %bitcast.11, ...), custom_call_target="tpu_custom_call" | custom-call | tf_op jit(solution)/shard_map/close_layer/pallas_call | solution.py:765
  188.0 21.7 %collective-permute-done.12.rest_1_ = bf16[8,16,32,128]{3,2,1,0:T(8,128)(2,1)S(1)} collective-permute-done((bf16[8,16,32,128]{3,2,1,0:T(8,128)(2,1)}, bf16[8,16,32,128]{3,2,1,0:T(8,128)(2,1)S(1)}, u32[]{:S(2)}, u32[]{:S(2)}) %collective-permute-start.12) | collective-permute-done | bytes 1048608 | tf_op jit(solution)/shard_map/ppermute | solution.py:806
  209.7 3.9 %collective-permute-start.13 = (bf16[8,16,32,128]{3,2,1,0:T(8,128)(2,1)S(1)}, bf16[8,16,32,128]{3,2,1,0:T(8,128)(2,1)S(1)}, u32[]{:S(2)}, u32[]{:S(2)}) collective-permute-start(bf16[8,16,32,128]{3,2,1,0:T(8,128)(2,1)S(1)} %collective-permute-done.12.rest_1_), channel_id=1, source_target_pairs={{0,1},{3,2},{4,5},{7,6},{8,9},{11,10},{12,13},{15,14},{16,17},{19,... | collective-permute-start | bytes 3145736 | tf_op jit(solution)/shard_map/ppermute | solution.py:807
  213.6 9.2 %collective-permute-done.14.rest_4_ = bf16[8,16,32,128]{3,2,1,0:T(8,128)(2,1)S(1)} collective-permute-done((bf16[8,16,32,128]{3,2,1,0:T(8,128)(2,1)}, bf16[8,16,32,128]{3,2,1,0:T(8,128)(2,1)S(1)}, u32[]{:S(2)}, u32[]{:S(2)}) %collective-permute-start.14) | collective-permute-done | bytes 1048608 | tf_op jit(solution)/shard_map/ppermute | solution.py:808
  225.3 5.5 %banded_products.25 = bf16[4,16,32,128]{3,2,1,0:T(8,128)(2,1)} custom-call(s32[4]{0:T(128)} %pad_add_fusion.ids, s32[2,32]{1,0:T(2,128)} %bitcast.22, s32[2,2,32]{2,1,0:T(2,128)} %bitcast.39, bf16[8,16,32,128]{3,2,1,0:T(8,128)(2,1)} %get-tuple-element.25.rest_0_, bf16[8,16,32,128]{3,2,1,0:T(8,128)(2,1)} %copy-done.17, bf16[8,16,32,128]{3,2,1,0:T(8,128)(2,1)} %copy-done.20, ...), custom_call_target="tpu_custom_call" | custom-call | flops 6710886400 | bytes 2621440 | tf_op jit(solution)/shard_map/banded_products/pallas_call | solution.py:613
  230.9 5.6 %banded_products.26 = bf16[4,16,32,128]{3,2,1,0:T(8,128)(2,1)} custom-call(s32[4]{0:T(128)} %pad_add_fusion.ids, s32[2,32]{1,0:T(2,128)} %bitcast.23, s32[2,2,32]{2,1,0:T(2,128)} %bitcast.40, bf16[8,16,32,128]{3,2,1,0:T(8,128)(2,1)} %get-tuple-element.25.rest_0_, bf16[8,16,32,128]{3,2,1,0:T(8,128)(2,1)} %copy-done.17, bf16[8,16,32,128]{3,2,1,0:T(8,128)(2,1)} %copy-done.20, ...), custom_call_target="tpu_custom_call" | custom-call | flops 6710886400 | bytes 2621440 | tf_op jit(solution)/shard_map/banded_products/pallas_call | solution.py:613
  237.9 7.4 %collective-permute-done.18.rest_1_ = bf16[8,16,32,128]{3,2,1,0:T(8,128)(2,1)S(1)} collective-permute-done((bf16[8,16,32,128]{3,2,1,0:T(8,128)(2,1)}, bf16[8,16,32,128]{3,2,1,0:T(8,128)(2,1)S(1)}, u32[]{:S(2)}, u32[]{:S(2)}) %collective-permute-start.18) | collective-permute-done | bytes 1048608 | tf_op jit(solution)/shard_map/ppermute | solution.py:806
  245.3 4.7 %collective-permute-start.19 = (bf16[8,16,32,128]{3,2,1,0:T(8,128)(2,1)S(1)}, bf16[8,16,32,128]{3,2,1,0:T(8,128)(2,1)S(1)}, u32[]{:S(2)}, u32[]{:S(2)}) collective-permute-start(bf16[8,16,32,128]{3,2,1,0:T(8,128)(2,1)S(1)} %collective-permute-done.18.rest_1_), channel_id=1, source_target_pairs={{0,1},{3,2},{4,5},{7,6},{8,9},{11,10},{12,13},{15,14},{16,17},{19,... | collective-permute-start | bytes 3145736 | tf_op jit(solution)/shard_map/ppermute | solution.py:807
  249.9 5.6 %banded_products.27 = bf16[4,16,32,128]{3,2,1,0:T(8,128)(2,1)} custom-call(s32[4]{0:T(128)} %pad_add_fusion.ids, s32[2,32]{1,0:T(2,128)} %bitcast.24, s32[2,2,32]{2,1,0:T(2,128)} %bitcast.41, bf16[8,16,32,128]{3,2,1,0:T(8,128)(2,1)} %get-tuple-element.25.rest_0_, bf16[8,16,32,128]{3,2,1,0:T(8,128)(2,1)} %copy-done.17, bf16[8,16,32,128]{3,2,1,0:T(8,128)(2,1)} %copy-done.20, ...), custom_call_target="tpu_custom_call" | custom-call | flops 6710886400 | bytes 2621440 | tf_op jit(solution)/shard_map/banded_products/pallas_call | solution.py:613
  255.8 5.6 %banded_products.24.rest_0_ = bf16[4,16,32,128]{3,2,1,0:T(8,128)(2,1)} custom-call(s32[4]{0:T(128)} %pad_add_fusion.ids, s32[2,32]{1,0:T(2,128)} %bitcast.25, s32[2,2,32]{2,1,0:T(2,128)} %bitcast.42, bf16[8,16,32,128]{3,2,1,0:T(8,128)(2,1)} %get-tuple-element.25.rest_0_, bf16[8,16,32,128]{3,2,1,0:T(8,128)(2,1)} %copy-done.17, ...), custom_call_target="tpu_custom_call" | custom-call | flops 6710886400 | bytes 2621440 | tf_op jit(solution)/shard_map/banded_products/pallas_call | solution.py:613
  263.3 5.6 %banded_products.29 = bf16[4,16,32,128]{3,2,1,0:T(8,128)(2,1)} custom-call(s32[4]{0:T(128)} %pad_add_fusion.ids, s32[2,32]{1,0:T(2,128)} %bitcast.26, s32[2,2,32]{2,1,0:T(2,128)} %bitcast.43, bf16[8,16,32,128]{3,2,1,0:T(8,128)(2,1)} %get-tuple-element.29.rest_0_, bf16[8,16,32,128]{3,2,1,0:T(8,128)(2,1)} %copy-done.14, bf16[8,16,32,128]{3,2,1,0:T(8,128)(2,1)} %copy-done.21, ...), custom_call_target="tpu_custom_call" | custom-call | flops 6710886400 | bytes 2621440 | tf_op jit(solution)/shard_map/banded_products/pallas_call | solution.py:613
  270.4 5.6 %banded_products.30 = bf16[4,16,32,128]{3,2,1,0:T(8,128)(2,1)} custom-call(s32[4]{0:T(128)} %pad_add_fusion.ids, s32[2,32]{1,0:T(2,128)} %bitcast.27, s32[2,2,32]{2,1,0:T(2,128)} %bitcast.44, bf16[8,16,32,128]{3,2,1,0:T(8,128)(2,1)} %get-tuple-element.29.rest_0_, bf16[8,16,32,128]{3,2,1,0:T(8,128)(2,1)} %copy-done.14, bf16[8,16,32,128]{3,2,1,0:T(8,128)(2,1)} %copy-done.21, ...), custom_call_target="tpu_custom_call" | custom-call | flops 6710886400 | bytes 2621440 | tf_op jit(solution)/shard_map/banded_products/pallas_call | solution.py:613
  276.0 3.2 collective-permute-start.22
  279.2 5.6 %banded_products.31 = bf16[4,16,32,128]{3,2,1,0:T(8,128)(2,1)} custom-call(s32[4]{0:T(128)} %pad_add_fusion.ids, s32[2,32]{1,0:T(2,128)} %bitcast.28, s32[2,2,32]{2,1,0:T(2,128)} %bitcast.45, bf16[8,16,32,128]{3,2,1,0:T(8,128)(2,1)} %get-tuple-element.29.rest_0_, bf16[8,16,32,128]{3,2,1,0:T(8,128)(2,1)} %copy-done.14, bf16[8,16,32,128]{3,2,1,0:T(8,128)(2,1)} %copy-done.21, ...), custom_call_target="tpu_custom_call" | custom-call | flops 6710886400 | bytes 2621440 | tf_op jit(solution)/shard_map/banded_products/pallas_call | solution.py:613
  284.8 5.6 %banded_products.28.rest_4_ = bf16[4,16,32,128]{3,2,1,0:T(8,128)(2,1)} custom-call(s32[4]{0:T(128)} %pad_add_fusion.ids, s32[2,32]{1,0:T(2,128)} %bitcast.29, s32[2,2,32]{2,1,0:T(2,128)} %bitcast.46, bf16[8,16,32,128]{3,2,1,0:T(8,128)(2,1)} %get-tuple-element.29.rest_0_, bf16[8,16,32,128]{3,2,1,0:T(8,128)(2,1)} %copy-done.14, ...), custom_call_target="tpu_custom_call" | custom-call | flops 6710886400 | bytes 2621440 | tf_op jit(solution)/shard_map/banded_products/pallas_call | solution.py:613
  290.4 10.6 %collective-permute-done.17.rest_3_ = bf16[4,16,32,128]{3,2,1,0:T(8,128)(2,1)S(1)} collective-permute-done((bf16[4,16,32,128]{3,2,1,0:T(8,128)(2,1)}, bf16[4,16,32,128]{3,2,1,0:T(8,128)(2,1)S(1)}, u32[]{:S(2)}, u32[]{:S(2)}) %collective-permute-start.17) | collective-permute-done | bytes 524320 | tf_op jit(solution)/shard_map/ppermute | solution.py:830
  301.1 8.2 %collective-permute-done.21.rest_5_ = bf16[4,16,32,128]{3,2,1,0:T(8,128)(2,1)S(1)} collective-permute-done((bf16[4,16,32,128]{3,2,1,0:T(8,128)(2,1)}, bf16[4,16,32,128]{3,2,1,0:T(8,128)(2,1)S(1)}, u32[]{:S(2)}, u32[]{:S(2)}) %collective-permute-start.21) | collective-permute-done | bytes 524320 | tf_op jit(solution)/shard_map/ppermute | solution.py:830
  309.2 11.2 %collective-permute-done.22.rest_6_ = bf16[4,16,32,128]{3,2,1,0:T(8,128)(2,1)S(1)} collective-permute-done((bf16[4,16,32,128]{3,2,1,0:T(8,128)(2,1)}, bf16[4,16,32,128]{3,2,1,0:T(8,128)(2,1)S(1)}, u32[]{:S(2)}, u32[]{:S(2)}) %collective-permute-start.22) | collective-permute-done | bytes 524320 | tf_op jit(solution)/shard_map/ppermute | solution.py:830
  324.3 13.5 %close_layer.3 = bf16[8,32,32,128]{3,2,1,0:T(8,128)(2,1)} custom-call(s32[4]{0:T(128)} %pad_add_fusion.ids, s32[2,32]{1,0:T(2,128)} %bitcast.12, s32[2,32]{1,0:T(2,128)} %bitcast.30, bf16[4,16,32,128]{3,2,1,0:T(8,128)(2,1)} %banded_products.24.rest_0_, bf16[4,16,32,128]{3,2,1,0:T(8,128)(2,1)} %copy-done.6, bf16[4,16,32,128]{3,2,1,0:T(8,128)(2,1)} %copy-done.7, ...), custom_call_target="tpu_custom_call" | custom-call | tf_op jit(solution)/shard_map/close_layer/pallas_call | solution.py:765
  (86 shorter events, 32.2 us)
Async XLA Ops:
  22.1 4.0 %collective-permute-start.2 = (bf16[8,16,32,128]{3,2,1,0:T(8,128)(2,1)}, bf16[8,16,32,128]{3,2,1,0:T(8,128)(2,1)S(1)}, u32[]{:S(2)}, u32[]{:S(2)}) collective-permute-start(bf16[8,16,32,128]{3,2,1,0:T(8,128)(2,1)} %get-tuple-element.20.rest_3_), channel_id=1, source_target_pairs={{1,2},{2,1},{5,6},{6,5},{9,10},{10,9},{13,14},{14,13},{17,18},{18,... | collective-permute-start | bytes 3145736 | tf_op jit(solution)/shard_map/ppermute | solution.py:795
  22.9 30.0 %collective-permute-start = (bf16[8,16,32,128]{3,2,1,0:T(8,128)(2,1)}, bf16[8,16,32,128]{3,2,1,0:T(8,128)(2,1)S(1)}, u32[]{:S(2)}, u32[]{:S(2)}) collective-permute-start(bf16[8,16,32,128]{3,2,1,0:T(8,128)(2,1)} %get-tuple-element.19.rest_1_), channel_id=1, source_target_pairs={{0,1},{1,0},{2,3},{3,2},{4,5},{5,4},{6,7},{7,6},{8,9},{9,8},{10,11... | collective-permute-start | bytes 3145736 | tf_op jit(solution)/shard_map/ppermute | solution.py:793
  24.8 28.1 %collective-permute-start.1 = (bf16[8,16,32,128]{3,2,1,0:T(8,128)(2,1)}, bf16[8,16,32,128]{3,2,1,0:T(8,128)(2,1)S(1)}, u32[]{:S(2)}, u32[]{:S(2)}) collective-permute-start(bf16[8,16,32,128]{3,2,1,0:T(8,128)(2,1)} %get-tuple-element.20.rest_3_), channel_id=1, source_target_pairs={{0,2},{3,1},{1,0},{2,3},{4,6},{7,5},{5,4},{6,7},{8,10},{11,9},{9,8... | collective-permute-start | bytes 3145736 | tf_op jit(solution)/shard_map/ppermute | solution.py:794
  26.2 52.9 %collective-permute-start.6 = (bf16[8,16,32,128]{3,2,1,0:T(8,128)(2,1)}, bf16[8,16,32,128]{3,2,1,0:T(8,128)(2,1)S(1)}, u32[]{:S(2)}, u32[]{:S(2)}) collective-permute-start(bf16[8,16,32,128]{3,2,1,0:T(8,128)(2,1)} %get-tuple-element.21.rest_1_), channel_id=1, source_target_pairs={{0,1},{1,0},{2,3},{3,2},{4,5},{5,4},{6,7},{7,6},{8,9},{9,8},{10,11... | collective-permute-start | bytes 3145736 | tf_op jit(solution)/shard_map/ppermute | solution.py:793
  26.2 26.7 %copy-start.19 = (bf16[8,16,32,128]{3,2,1,0:T(8,128)(2,1)}, bf16[8,16,32,128]{3,2,1,0:T(8,128)(2,1)S(1)}, u32[]{:S(2)}) copy-start(bf16[8,16,32,128]{3,2,1,0:T(8,128)(2,1)S(1)} %collective-permute-done.2.rest_4_) | copy-start | bytes 3145732
  26.2 54.5 %collective-permute-start.8 = (bf16[8,16,32,128]{3,2,1,0:T(8,128)(2,1)}, bf16[8,16,32,128]{3,2,1,0:T(8,128)(2,1)S(1)}, u32[]{:S(2)}, u32[]{:S(2)}) collective-permute-start(bf16[8,16,32,128]{3,2,1,0:T(8,128)(2,1)} %get-tuple-element.23.rest_3_), channel_id=1, source_target_pairs={{1,2},{2,1},{5,6},{6,5},{9,10},{10,9},{13,14},{14,13},{17,18},{18,... | collective-permute-start | bytes 3145736 | tf_op jit(solution)/shard_map/ppermute | solution.py:795
  26.9 53.7 %collective-permute-start.7 = (bf16[8,16,32,128]{3,2,1,0:T(8,128)(2,1)}, bf16[8,16,32,128]{3,2,1,0:T(8,128)(2,1)S(1)}, u32[]{:S(2)}, u32[]{:S(2)}) collective-permute-start(bf16[8,16,32,128]{3,2,1,0:T(8,128)(2,1)} %get-tuple-element.23.rest_3_), channel_id=1, source_target_pairs={{0,2},{3,1},{1,0},{2,3},{4,6},{7,5},{5,4},{6,7},{8,10},{11,9},{9,8... | collective-permute-start | bytes 3145736 | tf_op jit(solution)/shard_map/ppermute | solution.py:794
  59.8 42.7 %collective-permute-start.3 = (bf16[4,16,32,128]{3,2,1,0:T(8,128)(2,1)}, bf16[4,16,32,128]{3,2,1,0:T(8,128)(2,1)S(1)}, u32[]{:S(2)}, u32[]{:S(2)}) collective-permute-start(bf16[4,16,32,128]{3,2,1,0:T(8,128)(2,1)} %banded_products.17), channel_id=1, source_target_pairs={{0,4},{4,8},{8,12},{12,0},{1,5},{5,9},{9,13},{13,1},{2,6},{6,10},{... | collective-permute-start | bytes 1572872 | tf_op jit(solution)/shard_map/ppermute | solution.py:830
  66.7 62.6 %collective-permute-start.4 = (bf16[4,16,32,128]{3,2,1,0:T(8,128)(2,1)}, bf16[4,16,32,128]{3,2,1,0:T(8,128)(2,1)S(1)}, u32[]{:S(2)}, u32[]{:S(2)}) collective-permute-start(bf16[4,16,32,128]{3,2,1,0:T(8,128)(2,1)} %banded_products.18), channel_id=1, source_target_pairs={{0,8},{4,12},{8,0},{12,4},{1,9},{5,13},{9,1},{13,5},{2,10},{6,14},... | collective-permute-start | bytes 1572872 | tf_op jit(solution)/shard_map/ppermute | solution.py:830
  79.1 51.0 %collective-permute-start.5 = (bf16[4,16,32,128]{3,2,1,0:T(8,128)(2,1)S(1)}, bf16[4,16,32,128]{3,2,1,0:T(8,128)(2,1)S(1)}, u32[]{:S(2)}, u32[]{:S(2)}) collective-permute-start(bf16[4,16,32,128]{3,2,1,0:T(8,128)(2,1)S(1)} %copy-done.24), channel_id=1, source_target_pairs={{0,12},{4,0},{8,4},{12,8},{1,13},{5,1},{9,5},{13,9},{2,14},{6,2},{... | collective-permute-start | bytes 1572872 | tf_op jit(solution)/shard_map/ppermute | solution.py:830
  88.2 52.5 %collective-permute-start.9 = (bf16[4,16,32,128]{3,2,1,0:T(8,128)(2,1)}, bf16[4,16,32,128]{3,2,1,0:T(8,128)(2,1)S(1)}, u32[]{:S(2)}, u32[]{:S(2)}) collective-permute-start(bf16[4,16,32,128]{3,2,1,0:T(8,128)(2,1)} %banded_products.21), channel_id=1, source_target_pairs={{0,4},{4,8},{8,12},{12,0},{1,5},{5,9},{9,13},{13,1},{2,6},{6,10},{... | collective-permute-start | bytes 1572872 | tf_op jit(solution)/shard_map/ppermute | solution.py:830
  93.8 57.3 %collective-permute-start.10 = (bf16[4,16,32,128]{3,2,1,0:T(8,128)(2,1)}, bf16[4,16,32,128]{3,2,1,0:T(8,128)(2,1)S(1)}, u32[]{:S(2)}, u32[]{:S(2)}) collective-permute-start(bf16[4,16,32,128]{3,2,1,0:T(8,128)(2,1)} %banded_products.22), channel_id=1, source_target_pairs={{0,8},{4,12},{8,0},{12,4},{1,9},{5,13},{9,1},{13,5},{2,10},{6,14},... | collective-permute-start | bytes 1572872 | tf_op jit(solution)/shard_map/ppermute | solution.py:830
  102.5 50.0 %collective-permute-start.11 = (bf16[4,16,32,128]{3,2,1,0:T(8,128)(2,1)}, bf16[4,16,32,128]{3,2,1,0:T(8,128)(2,1)S(1)}, u32[]{:S(2)}, u32[]{:S(2)}) collective-permute-start(bf16[4,16,32,128]{3,2,1,0:T(8,128)(2,1)} %banded_products.23), channel_id=1, source_target_pairs={{0,12},{4,0},{8,4},{12,8},{1,13},{5,1},{9,5},{13,9},{2,14},{6,2},{... | collective-permute-start | bytes 1572872 | tf_op jit(solution)/shard_map/ppermute | solution.py:830
  129.3 23.3 %copy-start.1 = (bf16[4,16,32,128]{3,2,1,0:T(8,128)(2,1)}, bf16[4,16,32,128]{3,2,1,0:T(8,128)(2,1)S(1)}, u32[]{:S(2)}) copy-start(bf16[4,16,32,128]{3,2,1,0:T(8,128)(2,1)S(1)} %collective-permute-done.4.rest_2_) | copy-start | bytes 1572868
  130.1 22.5 %copy-start.2 = (bf16[4,16,32,128]{3,2,1,0:T(8,128)(2,1)}, bf16[4,16,32,128]{3,2,1,0:T(8,128)(2,1)S(1)}, u32[]{:S(2)}) copy-start(bf16[4,16,32,128]{3,2,1,0:T(8,128)(2,1)S(1)} %collective-permute-done.5.rest_3_) | copy-start | bytes 1572868
  140.6 12.0 %copy-start.3 = (bf16[4,16,32,128]{3,2,1,0:T(8,128)(2,1)}, bf16[4,16,32,128]{3,2,1,0:T(8,128)(2,1)S(1)}, u32[]{:S(2)}) copy-start(bf16[4,16,32,128]{3,2,1,0:T(8,128)(2,1)S(1)} %collective-permute-done.9.rest_5_) | copy-start | bytes 1572868
  186.5 23.2 %collective-permute-start.12 = (bf16[8,16,32,128]{3,2,1,0:T(8,128)(2,1)}, bf16[8,16,32,128]{3,2,1,0:T(8,128)(2,1)S(1)}, u32[]{:S(2)}, u32[]{:S(2)}) collective-permute-start(bf16[8,16,32,128]{3,2,1,0:T(8,128)(2,1)} %get-tuple-element.25.rest_0_), channel_id=1, source_target_pairs={{1,3},{2,0},{0,1},{3,2},{5,7},{6,4},{4,5},{7,6},{9,11},{10,8},{8,9... | collective-permute-start | bytes 3145736 | tf_op jit(solution)/shard_map/ppermute | solution.py:806
  186.9 35.9 %collective-permute-start.14 = (bf16[8,16,32,128]{3,2,1,0:T(8,128)(2,1)}, bf16[8,16,32,128]{3,2,1,0:T(8,128)(2,1)S(1)}, u32[]{:S(2)}, u32[]{:S(2)}) collective-permute-start(bf16[8,16,32,128]{3,2,1,0:T(8,128)(2,1)} %get-tuple-element.26.rest_3_), channel_id=1, source_target_pairs={{0,2},{2,0},{1,3},{3,1},{4,6},{6,4},{5,7},{7,5},{8,10},{10,8},{9,1... | collective-permute-start | bytes 3145736 | tf_op jit(solution)/shard_map/ppermute | solution.py:808
  209.7 14.6 %copy-start.17 = (bf16[8,16,32,128]{3,2,1,0:T(8,128)(2,1)}, bf16[8,16,32,128]{3,2,1,0:T(8,128)(2,1)S(1)}, u32[]{:S(2)}) copy-start(bf16[8,16,32,128]{3,2,1,0:T(8,128)(2,1)S(1)} %collective-permute-done.12.rest_1_) | copy-start | bytes 3145732
  209.7 14.6 %collective-permute-start.13 = (bf16[8,16,32,128]{3,2,1,0:T(8,128)(2,1)S(1)}, bf16[8,16,32,128]{3,2,1,0:T(8,128)(2,1)S(1)}, u32[]{:S(2)}, u32[]{:S(2)}) collective-permute-start(bf16[8,16,32,128]{3,2,1,0:T(8,128)(2,1)S(1)} %collective-permute-done.12.rest_1_), channel_id=1, source_target_pairs={{0,1},{3,2},{4,5},{7,6},{8,9},{11,10},{12,13},{15,14},{16,17},{19,... | collective-permute-start | bytes 3145736 | tf_op jit(solution)/shard_map/ppermute | solution.py:807
  222.8 22.4 %collective-permute-start.18 = (bf16[8,16,32,128]{3,2,1,0:T(8,128)(2,1)}, bf16[8,16,32,128]{3,2,1,0:T(8,128)(2,1)S(1)}, u32[]{:S(2)}, u32[]{:S(2)}) collective-permute-start(bf16[8,16,32,128]{3,2,1,0:T(8,128)(2,1)} %get-tuple-element.29.rest_0_), channel_id=1, source_target_pairs={{1,3},{2,0},{0,1},{3,2},{5,7},{6,4},{4,5},{7,6},{9,11},{10,8},{8,9... | collective-permute-start | bytes 3145736 | tf_op jit(solution)/shard_map/ppermute | solution.py:806
  222.9 38.5 %collective-permute-start.20 = (bf16[8,16,32,128]{3,2,1,0:T(8,128)(2,1)}, bf16[8,16,32,128]{3,2,1,0:T(8,128)(2,1)S(1)}, u32[]{:S(2)}, u32[]{:S(2)}) collective-permute-start(bf16[8,16,32,128]{3,2,1,0:T(8,128)(2,1)} %get-tuple-element.30.rest_3_), channel_id=1, source_target_pairs={{0,2},{2,0},{1,3},{3,1},{4,6},{6,4},{5,7},{7,5},{8,10},{10,8},{9,1... | collective-permute-start | bytes 3145736 | tf_op jit(solution)/shard_map/ppermute | solution.py:808
  230.8 53.9 %collective-permute-start.15 = (bf16[4,16,32,128]{3,2,1,0:T(8,128)(2,1)}, bf16[4,16,32,128]{3,2,1,0:T(8,128)(2,1)S(1)}, u32[]{:S(2)}, u32[]{:S(2)}) collective-permute-start(bf16[4,16,32,128]{3,2,1,0:T(8,128)(2,1)} %banded_products.25), channel_id=1, source_target_pairs={{0,4},{4,8},{8,12},{12,0},{1,5},{5,9},{9,13},{13,1},{2,6},{6,10},{... | collective-permute-start | bytes 1572872 | tf_op jit(solution)/shard_map/ppermute | solution.py:830
  236.5 53.9 %collective-permute-start.16 = (bf16[4,16,32,128]{3,2,1,0:T(8,128)(2,1)}, bf16[4,16,32,128]{3,2,1,0:T(8,128)(2,1)S(1)}, u32[]{:S(2)}, u32[]{:S(2)}) collective-permute-start(bf16[4,16,32,128]{3,2,1,0:T(8,128)(2,1)} %banded_products.26), channel_id=1, source_target_pairs={{0,8},{4,12},{8,0},{12,4},{1,9},{5,13},{9,1},{13,5},{2,10},{6,14},... | collective-permute-start | bytes 1572872 | tf_op jit(solution)/shard_map/ppermute | solution.py:830
  245.3 16.1 %collective-permute-start.19 = (bf16[8,16,32,128]{3,2,1,0:T(8,128)(2,1)S(1)}, bf16[8,16,32,128]{3,2,1,0:T(8,128)(2,1)S(1)}, u32[]{:S(2)}, u32[]{:S(2)}) collective-permute-start(bf16[8,16,32,128]{3,2,1,0:T(8,128)(2,1)S(1)} %collective-permute-done.18.rest_1_), channel_id=1, source_target_pairs={{0,1},{3,2},{4,5},{7,6},{8,9},{11,10},{12,13},{15,14},{16,17},{19,... | collective-permute-start | bytes 3145736 | tf_op jit(solution)/shard_map/ppermute | solution.py:807
  255.5 45.5 %collective-permute-start.17 = (bf16[4,16,32,128]{3,2,1,0:T(8,128)(2,1)}, bf16[4,16,32,128]{3,2,1,0:T(8,128)(2,1)S(1)}, u32[]{:S(2)}, u32[]{:S(2)}) collective-permute-start(bf16[4,16,32,128]{3,2,1,0:T(8,128)(2,1)} %banded_products.27), channel_id=1, source_target_pairs={{0,12},{4,0},{8,4},{12,8},{1,13},{5,1},{9,5},{13,9},{2,14},{6,2},{... | collective-permute-start | bytes 1572872 | tf_op jit(solution)/shard_map/ppermute | solution.py:830
  268.9 40.3 %collective-permute-start.21 = (bf16[4,16,32,128]{3,2,1,0:T(8,128)(2,1)}, bf16[4,16,32,128]{3,2,1,0:T(8,128)(2,1)S(1)}, u32[]{:S(2)}, u32[]{:S(2)}) collective-permute-start(bf16[4,16,32,128]{3,2,1,0:T(8,128)(2,1)} %banded_products.29), channel_id=1, source_target_pairs={{0,4},{4,8},{8,12},{12,0},{1,5},{5,9},{9,13},{13,1},{2,6},{6,10},{... | collective-permute-start | bytes 1572872 | tf_op jit(solution)/shard_map/ppermute | solution.py:830
  276.0 44.5 %collective-permute-start.22 = (bf16[4,16,32,128]{3,2,1,0:T(8,128)(2,1)}, bf16[4,16,32,128]{3,2,1,0:T(8,128)(2,1)S(1)}, u32[]{:S(2)}, u32[]{:S(2)}) collective-permute-start(bf16[4,16,32,128]{3,2,1,0:T(8,128)(2,1)} %banded_products.30), channel_id=1, source_target_pairs={{0,8},{4,12},{8,0},{12,4},{1,9},{5,13},{9,1},{13,5},{2,10},{6,14},... | collective-permute-start | bytes 1572872 | tf_op jit(solution)/shard_map/ppermute | solution.py:830
  284.7 38.8 %collective-permute-start.23 = (bf16[4,16,32,128]{3,2,1,0:T(8,128)(2,1)}, bf16[4,16,32,128]{3,2,1,0:T(8,128)(2,1)S(1)}, u32[]{:S(2)}, u32[]{:S(2)}) collective-permute-start(bf16[4,16,32,128]{3,2,1,0:T(8,128)(2,1)} %banded_products.31), channel_id=1, source_target_pairs={{0,12},{4,0},{8,4},{12,8},{1,13},{5,1},{9,5},{13,9},{2,14},{6,2},{... | collective-permute-start | bytes 1572872 | tf_op jit(solution)/shard_map/ppermute | solution.py:830
  290.4 33.1 %copy-start.7 = (bf16[4,16,32,128]{3,2,1,0:T(8,128)(2,1)}, bf16[4,16,32,128]{3,2,1,0:T(8,128)(2,1)S(1)}, u32[]{:S(2)}) copy-start(bf16[4,16,32,128]{3,2,1,0:T(8,128)(2,1)S(1)} %collective-permute-done.16.rest_2_) | copy-start | bytes 1572868
  301.1 22.5 %copy-start.8 = (bf16[4,16,32,128]{3,2,1,0:T(8,128)(2,1)}, bf16[4,16,32,128]{3,2,1,0:T(8,128)(2,1)S(1)}, u32[]{:S(2)}) copy-start(bf16[4,16,32,128]{3,2,1,0:T(8,128)(2,1)S(1)} %collective-permute-done.17.rest_3_) | copy-start | bytes 1572868
  309.2 14.3 %copy-start.9 = (bf16[4,16,32,128]{3,2,1,0:T(8,128)(2,1)}, bf16[4,16,32,128]{3,2,1,0:T(8,128)(2,1)S(1)}, u32[]{:S(2)}) copy-start(bf16[4,16,32,128]{3,2,1,0:T(8,128)(2,1)S(1)} %collective-permute-done.21.rest_5_) | copy-start | bytes 1572868
  (17 other events, 43.8 us)

commit v4 on v3

--- a/solution.py
+++ b/solution.py
@@ -416,44 +416,65 @@
 
 def spread_weights(w_ref, wide_ref, hidden, size):
     parts = hidden // size
-    for kind in range(4):
-        weights = w_ref[0, :, kind * hidden : (kind + 1) * hidden].astype(jnp.float32)
-        group = lane_group(weights.shape, size)
-        for part in range(parts):
-            kept = jnp.where(group == part, weights, 0.0)
-            for a in range(parts):
-                moved = pltpu.roll(kept, ((a - part) % parts) * size, 1) if a != part else kept
-                at = (kind * parts + part) * hidden
-                wide_ref[a * hidden : (a + 1) * hidden, at : at + hidden] = moved.astype(jnp.bfloat16)
-
-
-def make_operands(taken, wide_ref, row_alive, k_alive, out_refs, laid, turned):
+    for side in range(2):
+        for kind in range(2):
+            start = (2 * side + kind) * hidden
+            weights = w_ref[0, :, start : start + hidden].astype(jnp.float32)
+            group = lane_group(weights.shape, size)
+            for part in range(parts):
+                kept = jnp.where(group == part, weights, 0.0)
+                at = ((side * parts + part) * 2 + kind) * hidden
+                for a in range(parts):
+                    moved = pltpu.roll(kept, ((a - part) % parts) * size, 1) if a != part else kept
+                    wide_ref[a * hidden : (a + 1) * hidden, at : at + hidden] = moved.astype(jnp.bfloat16)
+
+
+def swap_matrix(half):
+    shape = (half * half, half * half)
+    to, of = lax.broadcasted_iota(jnp.int32, shape, 0), lax.broadcasted_iota(jnp.int32, shape, 1)
+    same = jnp.logical_and(to // half == lax.rem(of, half), lax.rem(to, half) == of // half)
+    return same.astype(jnp.float32).astype(jnp.bfloat16)
+
+
+def swapped(values, swap_ref):
+    half, _, lanes = values.shape
+    moved = dot(swap_ref[...], values.reshape(half * half, lanes))
+    return moved.astype(jnp.bfloat16).reshape(half, half, lanes)
+
+
+def turn(taken, turned, swap_ref):
+    half = 16
+    for x in range(0, taken.shape[0], half):
+        for y in range(0, taken.shape[1], half):
+            turned[y : y + half, x : x + half] = swapped(taken[x : x + half, y : y + half], swap_ref)
+
+
+def make_operand(side, taken, row_alive, inner_alive, wide_ref, out_refs, laid, swap_ref):
     rows, size, hidden = taken.shape
-    parts, bands = hidden // size, size
+    parts, bands, half = hidden // size, size, 16
     groups = rows // parts
     stacked = jnp.concatenate(
         [jnp.concatenate([taken[g * parts + a] for a in range(parts)], axis=1) for g in range(groups)], axis=0
     )
-    mask = (row_alive[:, None, :] * k_alive[None, :, :]).reshape(groups * size, hidden)
+    mask = (row_alive[:, None, :] * inner_alive[None, :, :]).reshape(groups * size, hidden)
     for part in range(parts):
-        made = []
-        for kind in range(4):
-            at = (kind * parts + part) * hidden
-            made.append(dot(stacked, wide_ref[:, at : at + hidden]))
-        for side in range(2):
-            value = mask * sigmoid(made[2 * side + 1]) * made[2 * side]
-            laid[side, :, part * size : (part + 1) * size, :] = value.reshape(groups, size, hidden)
-    for side in range(2):
-        for g in range(groups):
-            block = laid[side, g].T
-            for a in range(parts):
-                turned[side, pl.ds(g * parts + a, bands, stride=rows), :] = block[a * bands : (a + 1) * bands]
-        start = 0
-        for ref in out_refs[side]:
-            count = ref.shape[1]
-            value = turned[side, start * rows : (start + count) * rows].astype(jnp.bfloat16)
-            ref[0] = value.reshape(count, rows, hidden)
-            start += count
+        at = (side * parts + part) * 2 * hidden
+        made = dot(stacked, wide_ref[:, at : at + 2 * hidden])
+        value = mask * sigmoid(made[:, hidden:]) * made[:, :hidden]
+        laid[side, :, part * size : (part + 1) * size, :] = value.astype(jnp.bfloat16).reshape(groups, size, hidden)
+    blocks = [laid[side, g].T for g in range(groups)]
+    starts = [sum(ref.shape[1] for ref in out_refs[:n]) for n in range(len(out_refs))]
+    for first in range(0, bands, half):
+        for row in range(0, rows, half):
+            tiles = []
+            for r in range(row, row + half):
+                at = r % parts * bands + first
+                tiles.append(blocks[r // parts][at : at + half])
+            moved = swapped(jnp.stack(tiles), swap_ref)
+            for start, ref in zip(starts, out_refs):
+                low, high = max(start, first), min(start + ref.shape[1], first + half)
+                if low < high:
+                    ref[0, low - start : high - start, row : row + half] = moved[low - first : high - first]
 
 
 def alive_groups(chain_ref, start, rows, parts):
@@ -469,9 +490,22 @@
     return dot(pick.astype(jnp.float32).astype(jnp.bfloat16), fold.astype(jnp.float32).astype(jnp.bfloat16))
 
 
+def open_layer(layer, natural, chain_ref, row_start, col_start, w_ref, left_refs, right_refs, wide, laid, turned, swap):
+    rows, cols, hidden = natural.shape
+    parts = hidden // rows
+    turn(natural, turned, swap)
+    row_mask = alive_groups(chain_ref, row_start, rows, parts), alive_rows(chain_ref, col_start, cols)
+    col_mask = alive_groups(chain_ref, col_start, cols, parts), alive_rows(chain_ref, row_start, rows)
+    for side, refs in ((0, left_refs), (1, right_refs)):
+        if side == layer % 2:
+            make_operand(side, natural, *row_mask, wide, refs, laid, swap)
+        else:
+            make_operand(side, turned[...], *col_mask, wide, refs, laid, swap)
+
+
 def open_kernel(hidden, chunks, n_chan, n_sub, ids, blocks, pair_ref, chain_ref, w_ref, gate_ref, *rest):
     left_refs, right_refs = rest[:chunks], rest[chunks : 2 * chunks]
-    wide, laid, turned = rest[2 * chunks :]
+    wide, laid, turned, swap = rest[2 * chunks :]
     slots = pl.num_programs(0)
     step = pl.program_id(0)
     _, rows, cols, channels = pair_ref.shape
@@ -480,22 +514,23 @@
     @pl.when(step == 0)
     def _():
         spread_weights(w_ref, wide, hidden, cols)
+        swap[...] = swap_matrix(16)
 
     normed = layer_norm(pair_ref[0].reshape(rows * cols, channels)).astype(jnp.bfloat16)
     gate = sigmoid(dot(normed, w_ref[0, :, 4 * hidden :]))
     gate_ref[0] = gate.reshape(rows, cols, channels)
-    row_alive = alive_groups(chain_ref, (blocks[0, block] * n_chan + ids[1]) * rows, rows, hidden // cols)
-    k_alive = alive_rows(chain_ref, (blocks[1, block] * n_sub + ids[2]) * cols, cols)
-    taken = normed.reshape(rows, cols, channels)
-    make_operands(taken, wide, row_alive, k_alive, (left_refs, right_refs), laid, turned)
+    row_start, col_start = (blocks[0, block] * n_chan + ids[1]) * rows, (blocks[1, block] * n_sub + ids[2]) * cols
+    natural = normed.reshape(rows, cols, channels)
+    open_layer(0, natural, chain_ref, row_start, col_start, w_ref, left_refs, right_refs, wide, laid, turned, swap)
 
 
 def operand_scratch(rows, size, hidden):
     parts = hidden // size
     return [
         pltpu.VMEM((parts * hidden, 4 * parts * hidden), jnp.bfloat16),
-        pltpu.VMEM((2, rows // parts, parts * size, hidden), jnp.float32),
-        pltpu.VMEM((2, size * rows, hidden), jnp.float32),
+        pltpu.VMEM((2, rows // parts, parts * size, hidden), jnp.bfloat16),
+        pltpu.VMEM((size, rows, hidden), jnp.bfloat16),
+        pltpu.VMEM((256, 256), jnp.bfloat16),
     ]
 
 
@@ -529,7 +564,6 @@
     step = pl.program_id(0)
     turn = lax.rem(step, 2)
     _, halves, bands, rows, hidden = left_held.shape
-    cols = right_held.shape[3]
     parts = hidden // size
 
     @pl.when(step == 0)
@@ -583,15 +617,14 @@
     for n, piece in enumerate(pieces):
         copy(n, step, turn, piece[2]).wait()
 
-    group = lax.rem(lane_group((cols, halves * hidden), size), parts)
+    group = lane_group((size, hidden), size)
     for band in range(bands):
         left = jnp.concatenate([left_held[turn, h, band] for h in range(halves)], axis=1)
-        right = jnp.concatenate([right_held[turn, h, band] for h in range(halves)], axis=1)
-        apart = jnp.concatenate(
-            [jnp.where(group == part, right, jnp.zeros_like(right)) for part in range(parts)], axis=0
-        )
-        made = lax.dot_general(left, apart, (((1,), (1,)), ((), ())), preferred_element_type=jnp.float32)
-        out_ref[0, band] = made.astype(jnp.bfloat16)
+        apart = []
+        for h in range(halves):
+            right = right_held[turn, h, band]
+            apart += [jnp.where(group == part, right, jnp.zeros_like(right)) for part in range(parts)]
+        out_ref[0, band] = dot(left, jnp.concatenate(apart, axis=0)).astype(jnp.bfloat16)
 
 
 def banded_products(shift, ids, owners, slots, lefts, rights, capacity, slots_dev, terms, size):
@@ -609,7 +642,6 @@
         for half, (on, off) in enumerate(operands):
             pieces.append((side, half, index_of(on), index_of(off)))
     _, bands, rows, hidden = lefts[0][0].shape
-    cols = rights[0][0].shape[2]
     return pl.pallas_call(
         functools.partial(
             banded_kernel, shift, n_blk, slots_dev, terms, capacity, tuple(pieces), len(refs), size
@@ -621,7 +653,7 @@
             out_specs=pl.BlockSpec((1, bands, rows, hidden), lambda t, *_: (t, 0, 0, 0)),
             scratch_shapes=[
                 pltpu.VMEM((2, len(lefts), bands, rows, hidden), jnp.bfloat16),
-                pltpu.VMEM((2, len(rights), bands, cols, hidden), jnp.bfloat16),
+                pltpu.VMEM((2, len(rights), bands, size, hidden), jnp.bfloat16),
                 pltpu.SMEM((2 * capacity,), jnp.int32),
                 pltpu.SemaphoreType.DMA((2, len(pieces))),
             ],
@@ -637,16 +669,16 @@
     )(ids, owners, slots, *refs)
 
 
-def close_kernel(last, n_parts, n_blk, n_chan, n_sub, slots_dev, terms, capacity, ids, blocks, owners, *rest):
+def close_kernel(layer, last, n_parts, n_blk, n_chan, n_sub, slots_dev, terms, capacity, ids, blocks, owners, *rest):
     chunks = n_parts // n_blk
     arrived, rest = rest[:n_parts], rest[n_parts:]
     cur_ref, gate_ref, w_out_ref = rest[:3]
     if last:
-        out_ref, held, summed, wide_out, place, seen, sems = rest[3:]
+        out_ref, held, wide_out, place, seen, sems, swap = rest[3:]
     else:
         chain_ref, w_ref, out_ref, next_gate_ref = rest[3:7]
         left_refs, right_refs = rest[7 : 7 + chunks], rest[7 + chunks : 7 + 2 * chunks]
-        held, summed, wide_out, place, seen, sems, norm_ref, wide, laid, turned = rest[7 + 2 * chunks :]
+        held, wide_out, place, seen, sems, norm_ref, wide, laid, turned, swap = rest[7 + 2 * chunks :]
     step = pl.program_id(0)
     _, rows, cols, channels = cur_ref.shape
     _, bands, _, hidden = held.shape
@@ -681,29 +713,33 @@
                 wide_out[at : at + bands, a * channels : (a + 1) * channels] = w_out_ref[
                     0, part * bands : (part + 1) * bands, :
                 ]
+        swap[...] = swap_matrix(16)
         if not last:
             spread_weights(w_ref, wide, hidden, rows)
         for n in range(n_parts):
             arrival(n).wait()
 
-    span = 4
-    for band in range(0, bands, span):
-        taken = pl.ds(band, span)
-        total = held[place[step * terms], taken].astype(jnp.float32)
-        for t in range(1, terms):
-            total = total + held[place[step * terms + t], taken].astype(jnp.float32)
-        rounded = total.astype(jnp.bfloat16).astype(jnp.float32)
-        summed[pl.ds(band * rows, span * rows), :] = rounded.reshape(span * rows, hidden)
+    half = 16
+    by_row = [[] for _ in range(rows)]
+    for row in range(0, rows, half):
+        for band in range(0, bands, half):
+            taken = pl.ds(band, half), pl.ds(row, half)
+            total = held[(place[step * terms], *taken)].astype(jnp.float32)
+            for t in range(1, terms):
+                total = total + held[(place[step * terms + t], *taken)].astype(jnp.float32)
+            moved = swapped(total.astype(jnp.bfloat16), swap)
+            for r in range(half):
+                by_row[row + r].append(moved[r])
     groups = rows // parts
     pieces = []
     for g in range(groups):
-        block = jnp.concatenate([summed[pl.ds(g * parts + a, bands, stride=rows), :] for a in range(parts)]).T
+        block = jnp.concatenate([x for a in range(parts) for x in by_row[g * parts + a]]).T
         pieces.append(jnp.concatenate([block[p * cols : (p + 1) * cols] for p in range(parts)], axis=1))
     mixture = jnp.concatenate(pieces)
     together = (lane_group((hidden, hidden), size) == lax.broadcasted_iota(jnp.int32, (hidden, hidden), 0) // size)
     together = together.astype(jnp.float32).astype(jnp.bfloat16)
-    average = dot(mixture.astype(jnp.bfloat16), jnp.concatenate([together] * parts)) * (1.0 / hidden)
-    centred = [mixture[:, p * hidden : (p + 1) * hidden] - average for p in range(parts)]
+    average = dot(mixture, jnp.concatenate([together] * parts)) * (1.0 / hidden)
+    centred = [mixture[:, p * hidden : (p + 1) * hidden].astype(jnp.float32) - average for p in range(parts)]
     squares = sum(c * c for c in centred)
     high = squares.astype(jnp.bfloat16)
     low = (squares - high.astype(jnp.float32)).astype(jnp.bfloat16)
@@ -721,16 +757,16 @@
         result = (current + gate * change).astype(jnp.bfloat16)
         out_ref[0, taken] = result.reshape(parts, cols, channels)
         if not last:
-            norm = layer_norm(result)
-            norm_ref[pl.ds(g * parts * cols, parts * cols), :] = norm
-            next_gate = sigmoid(dot(norm.astype(jnp.bfloat16), w_ref[0, :, 4 * hidden :]))
+            norm = layer_norm(result).astype(jnp.bfloat16)
+            norm_ref[taken] = norm.reshape(parts, cols, channels)
+            next_gate = sigmoid(dot(norm, w_ref[0, :, 4 * hidden :]))
             next_gate_ref[0, taken] = next_gate.reshape(parts, cols, channels)
     if not last:
         block = ids[0] * slots_dev + step
-        k_alive = alive_rows(chain_ref, (blocks[0, block] * n_chan + ids[1]) * rows, rows)
-        col_alive = alive_groups(chain_ref, (blocks[1, block] * n_sub + ids[2]) * cols, cols, parts)
-        taken = jnp.stack([norm_ref[pl.ds(col, rows, stride=cols), :].astype(jnp.bfloat16) for col in range(cols)])
-        make_operands(taken, wide, col_alive, k_alive, (left_refs, right_refs), laid, turned)
+        starts = (blocks[0, block] * n_chan + ids[1]) * rows, (blocks[1, block] * n_sub + ids[2]) * cols
+        open_layer(
+            layer + 1, norm_ref[...], chain_ref, *starts, w_ref, left_refs, right_refs, wide, laid, turned, swap
+        )
 
 
 def close_layer(layer, arrived, ids, blocks, owners, current, gate, w_out, capacity, terms, chains, w_in, last, bands):
@@ -749,7 +785,6 @@
     out_specs = [whole]
     scratch = [
         pltpu.VMEM((n_blk * capacity, sum(bands), rows, hidden), jnp.bfloat16),
-        pltpu.VMEM((sum(bands) * rows, hidden), jnp.float32),
         pltpu.VMEM((hidden // cols * hidden, hidden // cols * channels), jnp.bfloat16),
         pltpu.SMEM((slots * terms,), jnp.int32),
         pltpu.SMEM((n_blk,), jnp.int32),
@@ -761,10 +796,12 @@
         made = [jax.ShapeDtypeStruct((slots, count, cols, hidden), jnp.bfloat16) for count in bands] * 2
         out_shape += [jax.ShapeDtypeStruct(current.shape, jnp.float32)] + made
         out_specs += [whole] + [pl.BlockSpec((1,) + o.shape[1:], lambda s, *_: (s, 0, 0, 0)) for o in made]
-        scratch += [pltpu.VMEM((rows * cols, channels), jnp.float32)] + operand_scratch(cols, rows, hidden)
+        scratch += [pltpu.VMEM((rows, cols, channels), jnp.bfloat16)] + operand_scratch(cols, rows, hidden)
+    else:
+        scratch += [pltpu.VMEM((256, 256), jnp.bfloat16)]
     out = pl.pallas_call(
         functools.partial(
-            close_kernel, last, len(flat), n_blk, lax.axis_size("chan"), lax.axis_size("sub"), slots, terms, capacity
+            close_kernel, layer, last, len(flat), n_blk, lax.axis_size("chan"), lax.axis_size("sub"), slots, terms, capacity
         ),
         grid_spec=pltpu.PrefetchScalarGridSpec(
             num_scalar_prefetch=3, grid=(slots,), in_specs=in_specs, out_specs=out_specs, scratch_shapes=scratch
@@ -817,7 +854,7 @@
     layers = w_in.shape[0]
     current = pair
     for layer in range(layers):
-        bands = [cols // 2, cols // 2]
+        bands = [cols // 4, cols // 4, cols // 2]
         if layer == 0:
             gate, lefts, rights = open_operands(ids, blocks, pair, chains, w_in, hidden, bands)
         exchange = exchange_bands_incoming if layer % 2 else exchange_bands_outgoing
@@ -857,7 +894,7 @@
     owners = term_owner.T
     slot_of = jnp.transpose(term_slots, (1, 2, 0))
     chains = chain_ids.reshape(-1, 128)
-    if fast and rows == cols and channels == hidden == 128 and hidden % cols == 0:
+    if fast and rows == cols == 32 and channels == hidden == 128:
         return banded(pair, ids, blocks, owners, slot_of, chains, w_in, w_out, capacity, terms, n_blk)
     shifts = [n_blk // 2] + [s for s in range(1, n_blk) if s != n_blk // 2] + [0]
 

time: 340 us -> 362 us (1.065)
  Pallas kernels: 157 us -> 177 us
  local copies, waits for them, and re-layouts: 7.8 us -> 3.7 us
    pallas_call x16 -> x24, Pallas kernels: 89 us -> 117 us  [banded_products(): pl.pallas_call(functools.partial(banded_kernel, shift, n_blk, slots_dev,...]
    ppermute x2 -> x3, waiting for transfers between devices: 29.1 us -> 5.45 us  [exchange_bands_incoming(): one = lax.ppermute(left, both, [(1, 3), (2, 0), (0, 1), (3, 2)])]
    ppermute x2 -> x3, waiting for transfers between devices: 9.21 us -> 21.4 us  [exchange_bands_incoming(): other = lax.ppermute(right, 'chan', [(0, 1), (1, 0)])]
    ppermute x2 -> x3, starting transfers between devices: 27.3 us -> 17.5 us  [exchange_bands_outgoing(): one = lax.ppermute(right, both, [(0, 2), (3, 1), (1, 0), (2, 3)])]
    ppermute x12 -> x18, waiting for transfers between devices: 77.5 us -> 86.3 us  [banded(): lax.ppermute(made, 'blk', [(p, (p + shift) % n_blk) for p in range(n_blk)])]
    ppermute x12 -> x18, starting transfers between devices: 13.7 us -> 21.3 us  [banded(): lax.ppermute(made, 'blk', [(p, (p + shift) % n_blk) for p in range(n_blk)])]
    pallas_call x2, Pallas kernels: 46.6 us -> 40.1 us  [close_layer(): pl.pallas_call(functools.partial(close_kernel, layer, last, len(flat), n_...]
    unnamed x50 -> x100, local copies, waits for them, and re-layouts: 7.8 us -> 3.7 us
  transfers between devices with their start and end apart: 24 -> 36, of which waited for: 12 -> 10; matrix products, arithmetic and copies ran while one was open for 0% -> 0% of each run, Pallas kernels for 26% -> 33%
where the time goes in v4:
time: 362 us; the launch traced here: 357 us
  Pallas kernels  177 us (49%)
  waiting for transfers between devices  115 us (32%)
  starting transfers between devices  59 us (16%)
  local copies, waits for them, and re-layouts  3.7 us (1%)
    pallas_call x24, Pallas kernels, banded_products(): pl.pallas_call(functools.partial(banded_kernel, shift, n_blk, slots_dev,...  117 us
    ppermute x18, waiting for transfers between devices, banded(): lax.ppermute(made, 'blk', [(p, (p + shift) % n_blk) for p in range(n_blk)])  86.3 us
    pallas_call x2, Pallas kernels, close_layer(): pl.pallas_call(functools.partial(close_kernel, layer, last, len(flat), n_...  40.1 us
    ppermute x3, waiting for transfers between devices, exchange_bands_incoming(): other = lax.ppermute(right, 'chan', [(0, 1), (1, 0)])  21.4 us
    ppermute x18, starting transfers between devices, banded(): lax.ppermute(made, 'blk', [(p, (p + shift) % n_blk) for p in range(n_blk)])  21.3 us
    pallas_call x1, Pallas kernels, open_operands(): pl.pallas_call(functools.partial(open_kernel, hidden, len(bands), lax.axi...  19.6 us
    ppermute x3, starting transfers between devices, exchange_bands_outgoing(): one = lax.ppermute(right, both, [(0, 2), (3, 1), (1, 0), (2, 3)])  17.5 us
    ppermute x3, starting transfers between devices, exchange_bands_incoming(): two = lax.ppermute(one, both, [(0, 1), (3, 2)])  10.4 us
  transfers between devices with their start and end apart: 36, of which 10 were waited for; matrix products, arithmetic and copies ran while one was open for 0% of the time, Pallas kernels for 33%

profile of v4, /device:TPU:11, one launch (start us, length us, event | category | flops | bytes accessed | tf_op | source)
XLA Modules:
  0.0 356.7 jit_solution(14112988199558910050)
XLA Ops:
  0.7 19.6 %open_operands.1 = (f32[8,32,32,128]{3,2,1,0:T(8,128)}, bf16[8,8,32,128]{3,2,1,0:T(8,128)(2,1)}, bf16[8,8,32,128]{3,2,1,0:T(8,128)(2,1)}, bf16[8,16,32,128]{3,2,...) custom-call(s32[4]{0:T(128)} %pad_add_fusion.ids, ...), custom_call_target="tpu_custom_call" | custom-call | tf_op jit(solution)/shard_map/open_operands/pallas_call | solution.py:540
  25.5 14.3 %collective-permute-start.7 = (bf16[8,8,32,128]{3,2,1,0:T(8,128)(2,1)}, bf16[8,8,32,128]{3,2,1,0:T(8,128)(2,1)S(1)}, u32[]{:S(2)}, u32[]{:S(2)}) collective-permute-start(bf16[8,8,32,128]{3,2,1,0:T(8,128)(2,1)} %get-tuple-element.30.rest_3_), channel_id=1, source_target_pairs={{0,2},{3,1},{1,0},{2,3},{4,6},{7,5},{5,4},{6,7},{8,10},{11,9},{9,8... | collective-permute-start | bytes 1572872 | tf_op jit(solution)/shard_map/ppermute | solution.py:831
  40.6 4.7 %banded_products.25 = bf16[4,8,32,128]{3,2,1,0:T(8,128)(2,1)} custom-call(s32[4]{0:T(128)} %pad_add_fusion.ids, s32[2,32]{1,0:T(2,128)} %bitcast.13, s32[2,2,32]{2,1,0:T(2,128)} %bitcast.39, bf16[8,8,32,128]{3,2,1,0:T(8,128)(2,1)} %copy-done.39, bf16[8,8,32,128]{3,2,1,0:T(8,128)(2,1)} %get-tuple-element.26.rest_1_, bf16[8,8,32,128]{3,2,1,0:T(8,128)(2,1)} %copy-done.40, ...), custom_call_target="tpu_custom_call" | custom-call | flops 3355443200 | bytes 1310720 | tf_op jit(solution)/shard_map/banded_products/pallas_call | solution.py:645
  51.3 4.7 %banded_products.26 = bf16[4,8,32,128]{3,2,1,0:T(8,128)(2,1)} custom-call(s32[4]{0:T(128)} %pad_add_fusion.ids, s32[2,32]{1,0:T(2,128)} %bitcast.15, s32[2,2,32]{2,1,0:T(2,128)} %bitcast.41, bf16[8,8,32,128]{3,2,1,0:T(8,128)(2,1)} %copy-done.39, bf16[8,8,32,128]{3,2,1,0:T(8,128)(2,1)} %get-tuple-element.26.rest_1_, bf16[8,8,32,128]{3,2,1,0:T(8,128)(2,1)} %copy-done.40, ...), custom_call_target="tpu_custom_call" | custom-call | flops 3355443200 | bytes 1310720 | tf_op jit(solution)/shard_map/banded_products/pallas_call | solution.py:645
  56.1 4.8 %banded_products.24.rest_0_ = bf16[4,8,32,128]{3,2,1,0:T(8,128)(2,1)} custom-call(s32[4]{0:T(128)} %pad_add_fusion.ids, s32[2,32]{1,0:T(2,128)} %bitcast.16, s32[2,2,32]{2,1,0:T(2,128)} %bitcast.42, bf16[8,8,32,128]{3,2,1,0:T(8,128)(2,1)} %copy-done.39, bf16[8,8,32,128]{3,2,1,0:T(8,128)(2,1)} %get-tuple-element.26.rest_1_, ...), custom_call_target="tpu_custom_call" | custom-call | flops 3355443200 | bytes 1310720 | tf_op jit(solution)/shard_map/banded_products/pallas_call | solution.py:645
  74.0 4.7 %banded_products.29 = bf16[4,8,32,128]{3,2,1,0:T(8,128)(2,1)} custom-call(s32[4]{0:T(128)} %pad_add_fusion.ids, s32[2,32]{1,0:T(2,128)} %bitcast.19, s32[2,2,32]{2,1,0:T(2,128)} %bitcast.45, bf16[8,8,32,128]{3,2,1,0:T(8,128)(2,1)} %copy-done.27, bf16[8,8,32,128]{3,2,1,0:T(8,128)(2,1)} %get-tuple-element.28.rest_1_, bf16[8,8,32,128]{3,2,1,0:T(8,128)(2,1)} %copy-done.36, ...), custom_call_target="tpu_custom_call" | custom-call | flops 3355443200 | bytes 1310720 | tf_op jit(solution)/shard_map/banded_products/pallas_call | solution.py:645
  78.8 4.8 %banded_products.28.rest_4_ = bf16[4,8,32,128]{3,2,1,0:T(8,128)(2,1)} custom-call(s32[4]{0:T(128)} %pad_add_fusion.ids, s32[2,32]{1,0:T(2,128)} %bitcast.20, s32[2,2,32]{2,1,0:T(2,128)} %bitcast.46, bf16[8,8,32,128]{3,2,1,0:T(8,128)(2,1)} %copy-done.27, bf16[8,8,32,128]{3,2,1,0:T(8,128)(2,1)} %get-tuple-element.28.rest_1_, ...), custom_call_target="tpu_custom_call" | custom-call | flops 3355443200 | bytes 1310720 | tf_op jit(solution)/shard_map/banded_products/pallas_call | solution.py:645
  89.1 5.2 %banded_products.35 = bf16[4,16,32,128]{3,2,1,0:T(8,128)(2,1)} custom-call(s32[4]{0:T(128)} %pad_add_fusion.ids, s32[2,32]{1,0:T(2,128)} %bitcast.21, s32[2,2,32]{2,1,0:T(2,128)} %bitcast.47, bf16[8,16,32,128]{3,2,1,0:T(8,128)(2,1)} %copy-done.20, bf16[8,16,32,128]{3,2,1,0:T(8,128)(2,1)} %get-tuple-element.31.rest_1_, bf16[8,16,32,128]{3,2,1,0:T(8,128)(2,1)} %copy-done.23, ...), custom_call_target="tpu_custom_call" | custom-call | flops 6710886400 | bytes 2621440 | tf_op jit(solution)/shard_map/banded_products/pallas_call | solution.py:645
  94.2 5.2 %banded_products.34 = bf16[4,16,32,128]{3,2,1,0:T(8,128)(2,1)} custom-call(s32[4]{0:T(128)} %pad_add_fusion.ids, s32[2,32]{1,0:T(2,128)} %bitcast.22, s32[2,2,32]{2,1,0:T(2,128)} %bitcast.48, bf16[8,16,32,128]{3,2,1,0:T(8,128)(2,1)} %copy-done.20, bf16[8,16,32,128]{3,2,1,0:T(8,128)(2,1)} %get-tuple-element.31.rest_1_, bf16[8,16,32,128]{3,2,1,0:T(8,128)(2,1)} %copy-done.23, ...), custom_call_target="tpu_custom_call" | custom-call | flops 6710886400 | bytes 2621440 | tf_op jit(solution)/shard_map/banded_products/pallas_call | solution.py:645
  99.4 5.3 %banded_products.33 = bf16[4,16,32,128]{3,2,1,0:T(8,128)(2,1)} custom-call(s32[4]{0:T(128)} %pad_add_fusion.ids, s32[2,32]{1,0:T(2,128)} %bitcast.23, s32[2,2,32]{2,1,0:T(2,128)} %bitcast.49, bf16[8,16,32,128]{3,2,1,0:T(8,128)(2,1)} %copy-done.20, bf16[8,16,32,128]{3,2,1,0:T(8,128)(2,1)} %get-tuple-element.31.rest_1_, bf16[8,16,32,128]{3,2,1,0:T(8,128)(2,1)} %copy-done.23, ...), custom_call_target="tpu_custom_call" | custom-call | flops 6710886400 | bytes 2621440 | tf_op jit(solution)/shard_map/banded_products/pallas_call | solution.py:645
  109.2 5.2 %banded_products.32.rest_8_ = bf16[4,16,32,128]{3,2,1,0:T(8,128)(2,1)} custom-call(s32[4]{0:T(128)} %pad_add_fusion.ids, s32[2,32]{1,0:T(2,128)} %bitcast.24, s32[2,2,32]{2,1,0:T(2,128)} %bitcast.50, bf16[8,16,32,128]{3,2,1,0:T(8,128)(2,1)} %copy-done.20, bf16[8,16,32,128]{3,2,1,0:T(8,128)(2,1)} %get-tuple-element.31.rest_1_, ...), custom_call_target="tpu_custom_call" | custom-call | flops 6710886400 | bytes 2621440 | tf_op jit(solution)/shard_map/banded_products/pallas_call | solution.py:645
  114.5 8.4 %collective-permute-done.11.rest_7_ = bf16[4,8,32,128]{3,2,1,0:T(8,128)(2,1)S(1)} collective-permute-done((bf16[4,8,32,128]{3,2,1,0:T(8,128)(2,1)S(1)}, bf16[4,8,32,128]{3,2,1,0:T(8,128)(2,1)S(1)}, u32[]{:S(2)}, u32[]{:S(2)}) %collective-permute-start.11) | collective-permute-done | bytes 262176 | tf_op jit(solution)/shard_map/ppermute | solution.py:867
  127.0 30.9 %collective-permute-done.16.rest_10_ = bf16[4,16,32,128]{3,2,1,0:T(8,128)(2,1)S(1)} collective-permute-done((bf16[4,16,32,128]{3,2,1,0:T(8,128)(2,1)S(1)}, bf16[4,16,32,128]{3,2,1,0:T(8,128)(2,1)S(1)}, u32[]{:S(2)}, u32[]{:S(2)}) %collective-permute-start.16) | collective-permute-done | bytes 524320 | tf_op jit(solution)/shard_map/ppermute | solution.py:867
  158.9 27.1 %close_layer.2 = (bf16[8,32,32,128]{3,2,1,0:T(8,128)(2,1)}, f32[8,32,32,128]{3,2,1,0:T(8,128)}, bf16[8,8,32,128]{3,2,1,0:T(8,128)(2,1)}, bf16[8,8,32,128]{3,2,1,...) custom-call(s32[4]{0:T(128)} %pad_add_fusion.ids, ...), custom_call_target="tpu_custom_call" | custom-call | tf_op jit(solution)/shard_map/close_layer/pallas_call | solution.py:802
  189.0 11.1 %collective-permute-done.20.rest_4_ = bf16[8,8,32,128]{3,2,1,0:T(8,128)(2,1)S(1)} collective-permute-done((bf16[8,8,32,128]{3,2,1,0:T(8,128)(2,1)}, bf16[8,8,32,128]{3,2,1,0:T(8,128)(2,1)S(1)}, u32[]{:S(2)}, u32[]{:S(2)}) %collective-permute-start.20) | collective-permute-done | bytes 524320 | tf_op jit(solution)/shard_map/ppermute | solution.py:845
  202.1 5.4 %collective-permute-done.18.rest_1_ = bf16[8,8,32,128]{3,2,1,0:T(8,128)(2,1)S(1)} collective-permute-done((bf16[8,8,32,128]{3,2,1,0:T(8,128)(2,1)}, bf16[8,8,32,128]{3,2,1,0:T(8,128)(2,1)S(1)}, u32[]{:S(2)}, u32[]{:S(2)}) %collective-permute-start.18) | collective-permute-done | bytes 524320 | tf_op jit(solution)/shard_map/ppermute | solution.py:843
  211.8 6.0 %collective-permute-done.26.rest_4_ = bf16[8,8,32,128]{3,2,1,0:T(8,128)(2,1)S(1)} collective-permute-done((bf16[8,8,32,128]{3,2,1,0:T(8,128)(2,1)}, bf16[8,8,32,128]{3,2,1,0:T(8,128)(2,1)S(1)}, u32[]{:S(2)}, u32[]{:S(2)}) %collective-permute-start.26) | collective-permute-done | bytes 524320 | tf_op jit(solution)/shard_map/ppermute | solution.py:845
  218.7 4.7 %banded_products.37 = bf16[4,8,32,128]{3,2,1,0:T(8,128)(2,1)} custom-call(s32[4]{0:T(128)} %pad_add_fusion.ids, s32[2,32]{1,0:T(2,128)} %bitcast.26, s32[2,2,32]{2,1,0:T(2,128)} %bitcast.51, bf16[8,8,32,128]{3,2,1,0:T(8,128)(2,1)} %get-tuple-element.35.rest_0_, bf16[8,8,32,128]{3,2,1,0:T(8,128)(2,1)} %copy-done.32, bf16[8,8,32,128]{3,2,1,0:T(8,128)(2,1)} %copy-done.38, ...), custom_call_target="tpu_custom_call" | custom-call | flops 3355443200 | bytes 1310720 | tf_op jit(solution)/shard_map/banded_products/pallas_call | solution.py:645
  223.5 4.7 %banded_products.38 = bf16[4,8,32,128]{3,2,1,0:T(8,128)(2,1)} custom-call(s32[4]{0:T(128)} %pad_add_fusion.ids, s32[2,32]{1,0:T(2,128)} %bitcast.27, s32[2,2,32]{2,1,0:T(2,128)} %bitcast.52, bf16[8,8,32,128]{3,2,1,0:T(8,128)(2,1)} %get-tuple-element.35.rest_0_, bf16[8,8,32,128]{3,2,1,0:T(8,128)(2,1)} %copy-done.32, bf16[8,8,32,128]{3,2,1,0:T(8,128)(2,1)} %copy-done.38, ...), custom_call_target="tpu_custom_call" | custom-call | flops 3355443200 | bytes 1310720 | tf_op jit(solution)/shard_map/banded_products/pallas_call | solution.py:645
  235.7 4.7 %banded_products.39 = bf16[4,8,32,128]{3,2,1,0:T(8,128)(2,1)} custom-call(s32[4]{0:T(128)} %pad_add_fusion.ids, s32[2,32]{1,0:T(2,128)} %bitcast.28, s32[2,2,32]{2,1,0:T(2,128)} %bitcast.53, bf16[8,8,32,128]{3,2,1,0:T(8,128)(2,1)} %get-tuple-element.35.rest_0_, bf16[8,8,32,128]{3,2,1,0:T(8,128)(2,1)} %copy-done.32, bf16[8,8,32,128]{3,2,1,0:T(8,128)(2,1)} %copy-done.38, ...), custom_call_target="tpu_custom_call" | custom-call | flops 3355443200 | bytes 1310720 | tf_op jit(solution)/shard_map/banded_products/pallas_call | solution.py:645
  242.4 4.7 %banded_products.36.rest_0_ = bf16[4,8,32,128]{3,2,1,0:T(8,128)(2,1)} custom-call(s32[4]{0:T(128)} %pad_add_fusion.ids, s32[2,32]{1,0:T(2,128)} %bitcast.29, s32[2,2,32]{2,1,0:T(2,128)} %bitcast.54, bf16[8,8,32,128]{3,2,1,0:T(8,128)(2,1)} %get-tuple-element.35.rest_0_, bf16[8,8,32,128]{3,2,1,0:T(8,128)(2,1)} %copy-done.32, ...), custom_call_target="tpu_custom_call" | custom-call | flops 3355443200 | bytes 1310720 | tf_op jit(solution)/shard_map/banded_products/pallas_call | solution.py:645
  248.9 4.7 %banded_products.43 = bf16[4,8,32,128]{3,2,1,0:T(8,128)(2,1)} custom-call(s32[4]{0:T(128)} %pad_add_fusion.ids, s32[2,32]{1,0:T(2,128)} %bitcast.30, s32[2,2,32]{2,1,0:T(2,128)} %bitcast.55, bf16[8,8,32,128]{3,2,1,0:T(8,128)(2,1)} %get-tuple-element.39.rest_0_, bf16[8,8,32,128]{3,2,1,0:T(8,128)(2,1)} %copy-done.28, bf16[8,8,32,128]{3,2,1,0:T(8,128)(2,1)} %copy-done.41, ...), custom_call_target="tpu_custom_call" | custom-call | flops 3355443200 | bytes 1310720 | tf_op jit(solution)/shard_map/banded_products/pallas_call | solution.py:645
  253.7 4.7 %banded_products.42 = bf16[4,8,32,128]{3,2,1,0:T(8,128)(2,1)} custom-call(s32[4]{0:T(128)} %pad_add_fusion.ids, s32[2,32]{1,0:T(2,128)} %bitcast.31, s32[2,2,32]{2,1,0:T(2,128)} %bitcast.56, bf16[8,8,32,128]{3,2,1,0:T(8,128)(2,1)} %get-tuple-element.39.rest_0_, bf16[8,8,32,128]{3,2,1,0:T(8,128)(2,1)} %copy-done.28, bf16[8,8,32,128]{3,2,1,0:T(8,128)(2,1)} %copy-done.41, ...), custom_call_target="tpu_custom_call" | custom-call | flops 3355443200 | bytes 1310720 | tf_op jit(solution)/shard_map/banded_products/pallas_call | solution.py:645
  258.4 4.7 %banded_products.41 = bf16[4,8,32,128]{3,2,1,0:T(8,128)(2,1)} custom-call(s32[4]{0:T(128)} %pad_add_fusion.ids, s32[2,32]{1,0:T(2,128)} %bitcast.32, s32[2,2,32]{2,1,0:T(2,128)} %bitcast.57, bf16[8,8,32,128]{3,2,1,0:T(8,128)(2,1)} %get-tuple-element.39.rest_0_, bf16[8,8,32,128]{3,2,1,0:T(8,128)(2,1)} %copy-done.28, bf16[8,8,32,128]{3,2,1,0:T(8,128)(2,1)} %copy-done.41, ...), custom_call_target="tpu_custom_call" | custom-call | flops 3355443200 | bytes 1310720 | tf_op jit(solution)/shard_map/banded_products/pallas_call | solution.py:645
  263.1 4.8 %banded_products.40.rest_4_ = bf16[4,8,32,128]{3,2,1,0:T(8,128)(2,1)} custom-call(s32[4]{0:T(128)} %pad_add_fusion.ids, s32[2,32]{1,0:T(2,128)} %bitcast.33, s32[2,2,32]{2,1,0:T(2,128)} %bitcast.58, bf16[8,8,32,128]{3,2,1,0:T(8,128)(2,1)} %get-tuple-element.39.rest_0_, bf16[8,8,32,128]{3,2,1,0:T(8,128)(2,1)} %copy-done.28, ...), custom_call_target="tpu_custom_call" | custom-call | flops 3355443200 | bytes 1310720 | tf_op jit(solution)/shard_map/banded_products/pallas_call | solution.py:645
  274.3 5.2 %banded_products.47 = bf16[4,16,32,128]{3,2,1,0:T(8,128)(2,1)} custom-call(s32[4]{0:T(128)} %pad_add_fusion.ids, s32[2,32]{1,0:T(2,128)} %bitcast.34, s32[2,2,32]{2,1,0:T(2,128)} %bitcast.59, bf16[8,16,32,128]{3,2,1,0:T(8,128)(2,1)} %get-tuple-element.43.rest_0_, bf16[8,16,32,128]{3,2,1,0:T(8,128)(2,1)} %copy-done.21, bf16[8,16,32,128]{3,2,1,0:T(8,128)(2,1)} %copy-done.25, ...), custom_call_target="tpu_custom_call" | custom-call | flops 6710886400 | bytes 2621440 | tf_op jit(solution)/shard_map/banded_products/pallas_call | solution.py:645
  279.5 5.2 %banded_products.46 = bf16[4,16,32,128]{3,2,1,0:T(8,128)(2,1)} custom-call(s32[4]{0:T(128)} %pad_add_fusion.ids, s32[2,32]{1,0:T(2,128)} %bitcast.35, s32[2,2,32]{2,1,0:T(2,128)} %bitcast.60, bf16[8,16,32,128]{3,2,1,0:T(8,128)(2,1)} %get-tuple-element.43.rest_0_, bf16[8,16,32,128]{3,2,1,0:T(8,128)(2,1)} %copy-done.21, bf16[8,16,32,128]{3,2,1,0:T(8,128)(2,1)} %copy-done.25, ...), custom_call_target="tpu_custom_call" | custom-call | flops 6710886400 | bytes 2621440 | tf_op jit(solution)/shard_map/banded_products/pallas_call | solution.py:645
  284.7 5.3 %banded_products.45 = bf16[4,16,32,128]{3,2,1,0:T(8,128)(2,1)} custom-call(s32[4]{0:T(128)} %pad_add_fusion.ids, s32[2,32]{1,0:T(2,128)} %bitcast.36, s32[2,2,32]{2,1,0:T(2,128)} %bitcast.61, bf16[8,16,32,128]{3,2,1,0:T(8,128)(2,1)} %get-tuple-element.43.rest_0_, bf16[8,16,32,128]{3,2,1,0:T(8,128)(2,1)} %copy-done.21, bf16[8,16,32,128]{3,2,1,0:T(8,128)(2,1)} %copy-done.25, ...), custom_call_target="tpu_custom_call" | custom-call | flops 6710886400 | bytes 2621440 | tf_op jit(solution)/shard_map/banded_products/pallas_call | solution.py:645
  294.5 5.2 %banded_products.44.rest_8_ = bf16[4,16,32,128]{3,2,1,0:T(8,128)(2,1)} custom-call(s32[4]{0:T(128)} %pad_add_fusion.ids, s32[2,32]{1,0:T(2,128)} %bitcast.37, s32[2,2,32]{2,1,0:T(2,128)} %bitcast.62, bf16[8,16,32,128]{3,2,1,0:T(8,128)(2,1)} %get-tuple-element.43.rest_0_, bf16[8,16,32,128]{3,2,1,0:T(8,128)(2,1)} %copy-done.21, ...), custom_call_target="tpu_custom_call" | custom-call | flops 6710886400 | bytes 2621440 | tf_op jit(solution)/shard_map/banded_products/pallas_call | solution.py:645
  299.8 9.5 %collective-permute-done.33.rest_9_ = bf16[4,16,32,128]{3,2,1,0:T(8,128)(2,1)S(1)} collective-permute-done((bf16[4,16,32,128]{3,2,1,0:T(8,128)(2,1)}, bf16[4,16,32,128]{3,2,1,0:T(8,128)(2,1)S(1)}, u32[]{:S(2)}, u32[]{:S(2)}) %collective-permute-start.33) | collective-permute-done | bytes 524320 | tf_op jit(solution)/shard_map/ppermute | solution.py:867
  309.4 33.2 %collective-permute-done.34.rest_10_ = bf16[4,16,32,128]{3,2,1,0:T(8,128)(2,1)S(1)} collective-permute-done((bf16[4,16,32,128]{3,2,1,0:T(8,128)(2,1)S(1)}, bf16[4,16,32,128]{3,2,1,0:T(8,128)(2,1)S(1)}, u32[]{:S(2)}, u32[]{:S(2)}) %collective-permute-start.34) | collective-permute-done | bytes 524320 | tf_op jit(solution)/shard_map/ppermute | solution.py:867
  343.6 13.0 %close_layer.3 = bf16[8,32,32,128]{3,2,1,0:T(8,128)(2,1)} custom-call(s32[4]{0:T(128)} %pad_add_fusion.ids, s32[2,32]{1,0:T(2,128)} %bitcast.12, s32[2,32]{1,0:T(2,128)} %bitcast.38, bf16[4,8,32,128]{3,2,1,0:T(8,128)(2,1)} %banded_products.36.rest_0_, bf16[4,8,32,128]{3,2,1,0:T(8,128)(2,1)} %copy-done.7, bf16[4,8,32,128]{3,2,1,0:T(8,128)(2,1)} %copy-done.8, ...), custom_call_target="tpu_custom_call" | custom-call | tf_op jit(solution)/shard_map/close_layer/pallas_call | solution.py:802
  (168 shorter events, 74.1 us)
Async XLA Ops:
  22.9 16.9 %collective-permute-start.1 = (bf16[8,8,32,128]{3,2,1,0:T(8,128)(2,1)}, bf16[8,8,32,128]{3,2,1,0:T(8,128)(2,1)S(1)}, u32[]{:S(2)}, u32[]{:S(2)}) collective-permute-start(bf16[8,8,32,128]{3,2,1,0:T(8,128)(2,1)} %get-tuple-element.27.rest_3_), channel_id=1, source_target_pairs={{0,2},{3,1},{1,0},{2,3},{4,6},{7,5},{5,4},{6,7},{8,10},{11,9},{9,8... | collective-permute-start | bytes 1572872 | tf_op jit(solution)/shard_map/ppermute | solution.py:831
  24.3 37.7 %collective-permute-start.6 = (bf16[8,8,32,128]{3,2,1,0:T(8,128)(2,1)}, bf16[8,8,32,128]{3,2,1,0:T(8,128)(2,1)S(1)}, u32[]{:S(2)}, u32[]{:S(2)}) collective-permute-start(bf16[8,8,32,128]{3,2,1,0:T(8,128)(2,1)} %get-tuple-element.28.rest_1_), channel_id=1, source_target_pairs={{0,1},{1,0},{2,3},{3,2},{4,5},{5,4},{6,7},{7,6},{8,9},{9,8},{10,11... | collective-permute-start | bytes 1572872 | tf_op jit(solution)/shard_map/ppermute | solution.py:830
  24.3 59.3 %collective-permute-start.12 = (bf16[8,16,32,128]{3,2,1,0:T(8,128)(2,1)}, bf16[8,16,32,128]{3,2,1,0:T(8,128)(2,1)S(1)}, u32[]{:S(2)}, u32[]{:S(2)}) collective-permute-start(bf16[8,16,32,128]{3,2,1,0:T(8,128)(2,1)} %get-tuple-element.31.rest_1_), channel_id=1, source_target_pairs={{0,1},{1,0},{2,3},{3,2},{4,5},{5,4},{6,7},{7,6},{8,9},{9,8},{10,11... | collective-permute-start | bytes 3145736 | tf_op jit(solution)/shard_map/ppermute | solution.py:830
  24.8 36.1 %collective-permute-start.8 = (bf16[8,8,32,128]{3,2,1,0:T(8,128)(2,1)}, bf16[8,8,32,128]{3,2,1,0:T(8,128)(2,1)S(1)}, u32[]{:S(2)}, u32[]{:S(2)}) collective-permute-start(bf16[8,8,32,128]{3,2,1,0:T(8,128)(2,1)} %get-tuple-element.30.rest_3_), channel_id=1, source_target_pairs={{1,2},{2,1},{5,6},{6,5},{9,10},{10,9},{13,14},{14,13},{17,18},{18,... | collective-permute-start | bytes 1572872 | tf_op jit(solution)/shard_map/ppermute | solution.py:832
  25.5 37.2 %collective-permute-start.7 = (bf16[8,8,32,128]{3,2,1,0:T(8,128)(2,1)}, bf16[8,8,32,128]{3,2,1,0:T(8,128)(2,1)S(1)}, u32[]{:S(2)}, u32[]{:S(2)}) collective-permute-start(bf16[8,8,32,128]{3,2,1,0:T(8,128)(2,1)} %get-tuple-element.30.rest_3_), channel_id=1, source_target_pairs={{0,2},{3,1},{1,0},{2,3},{4,6},{7,5},{5,4},{6,7},{8,10},{11,9},{9,8... | collective-permute-start | bytes 1572872 | tf_op jit(solution)/shard_map/ppermute | solution.py:831
  45.3 59.5 %collective-permute-start.3 = (bf16[4,8,32,128]{3,2,1,0:T(8,128)(2,1)}, bf16[4,8,32,128]{3,2,1,0:T(8,128)(2,1)S(1)}, u32[]{:S(2)}, u32[]{:S(2)}) collective-permute-start(bf16[4,8,32,128]{3,2,1,0:T(8,128)(2,1)} %banded_products.25), channel_id=1, source_target_pairs={{0,4},{4,8},{8,12},{12,0},{1,5},{5,9},{9,13},{13,1},{2,6},{6,10},{... | collective-permute-start | bytes 786440 | tf_op jit(solution)/shard_map/ppermute | solution.py:867
  60.9 45.0 %collective-permute-start.4 = (bf16[4,8,32,128]{3,2,1,0:T(8,128)(2,1)S(1)}, bf16[4,8,32,128]{3,2,1,0:T(8,128)(2,1)S(1)}, u32[]{:S(2)}, u32[]{:S(2)}) collective-permute-start(bf16[4,8,32,128]{3,2,1,0:T(8,128)(2,1)S(1)} %copy-done.45), channel_id=1, source_target_pairs={{0,8},{4,12},{8,0},{12,4},{1,9},{5,13},{9,1},{13,5},{2,10},{6,14},... | collective-permute-start | bytes 786440 | tf_op jit(solution)/shard_map/ppermute | solution.py:867
  62.0 23.2 %collective-permute-start.14 = (bf16[8,16,32,128]{3,2,1,0:T(8,128)(2,1)S(1)}, bf16[8,16,32,128]{3,2,1,0:T(8,128)(2,1)S(1)}, u32[]{:S(2)}, u32[]{:S(2)}) collective-permute-start(bf16[8,16,32,128]{3,2,1,0:T(8,128)(2,1)S(1)} %copy-done.19), channel_id=1, source_target_pairs={{1,2},{2,1},{5,6},{6,5},{9,10},{10,9},{13,14},{14,13},{17,18},{18,... | collective-permute-start | bytes 3145736 | tf_op jit(solution)/shard_map/ppermute | solution.py:832
  62.7 24.8 %collective-permute-start.13 = (bf16[8,16,32,128]{3,2,1,0:T(8,128)(2,1)S(1)}, bf16[8,16,32,128]{3,2,1,0:T(8,128)(2,1)S(1)}, u32[]{:S(2)}, u32[]{:S(2)}) collective-permute-start(bf16[8,16,32,128]{3,2,1,0:T(8,128)(2,1)S(1)} %copy-done.19), channel_id=1, source_target_pairs={{0,2},{3,1},{1,0},{2,3},{4,6},{7,5},{5,4},{6,7},{8,10},{11,9},{9,8... | collective-permute-start | bytes 3145736 | tf_op jit(solution)/shard_map/ppermute | solution.py:831
  83.6 22.7 %collective-permute-start.5 = (bf16[4,8,32,128]{3,2,1,0:T(8,128)(2,1)S(1)}, bf16[4,8,32,128]{3,2,1,0:T(8,128)(2,1)S(1)}, u32[]{:S(2)}, u32[]{:S(2)}) collective-permute-start(bf16[4,8,32,128]{3,2,1,0:T(8,128)(2,1)S(1)} %copy-done.42), channel_id=1, source_target_pairs={{0,12},{4,0},{8,4},{12,8},{1,13},{5,1},{9,5},{13,9},{2,14},{6,2},{... | collective-permute-start | bytes 786440 | tf_op jit(solution)/shard_map/ppermute | solution.py:867
  85.2 24.0 %collective-permute-start.9 = (bf16[4,8,32,128]{3,2,1,0:T(8,128)(2,1)S(1)}, bf16[4,8,32,128]{3,2,1,0:T(8,128)(2,1)S(1)}, u32[]{:S(2)}, u32[]{:S(2)}) collective-permute-start(bf16[4,8,32,128]{3,2,1,0:T(8,128)(2,1)S(1)} %copy-done.48), channel_id=1, source_target_pairs={{0,4},{4,8},{8,12},{12,0},{1,5},{5,9},{9,13},{13,1},{2,6},{6,10},{... | collective-permute-start | bytes 786440 | tf_op jit(solution)/shard_map/ppermute | solution.py:867
  87.6 26.9 %collective-permute-start.10 = (bf16[4,8,32,128]{3,2,1,0:T(8,128)(2,1)S(1)}, bf16[4,8,32,128]{3,2,1,0:T(8,128)(2,1)S(1)}, u32[]{:S(2)}, u32[]{:S(2)}) collective-permute-start(bf16[4,8,32,128]{3,2,1,0:T(8,128)(2,1)S(1)} %copy-done.44), channel_id=1, source_target_pairs={{0,8},{4,12},{8,0},{12,4},{1,9},{5,13},{9,1},{13,5},{2,10},{6,14},... | collective-permute-start | bytes 786440 | tf_op jit(solution)/shard_map/ppermute | solution.py:867
  104.8 18.1 %collective-permute-start.11 = (bf16[4,8,32,128]{3,2,1,0:T(8,128)(2,1)S(1)}, bf16[4,8,32,128]{3,2,1,0:T(8,128)(2,1)S(1)}, u32[]{:S(2)}, u32[]{:S(2)}) collective-permute-start(bf16[4,8,32,128]{3,2,1,0:T(8,128)(2,1)S(1)} %copy-done.43), channel_id=1, source_target_pairs={{0,12},{4,0},{8,4},{12,8},{1,13},{5,1},{9,5},{13,9},{2,14},{6,2},{... | collective-permute-start | bytes 786440 | tf_op jit(solution)/shard_map/ppermute | solution.py:867
  105.9 21.1 %collective-permute-start.15 = (bf16[4,16,32,128]{3,2,1,0:T(8,128)(2,1)}, bf16[4,16,32,128]{3,2,1,0:T(8,128)(2,1)S(1)}, u32[]{:S(2)}, u32[]{:S(2)}) collective-permute-start(bf16[4,16,32,128]{3,2,1,0:T(8,128)(2,1)} %banded_products.33), channel_id=1, source_target_pairs={{0,4},{4,8},{8,12},{12,0},{1,5},{5,9},{9,13},{13,1},{2,6},{6,10},{... | collective-permute-start | bytes 1572872 | tf_op jit(solution)/shard_map/ppermute | solution.py:867
  106.3 51.6 %collective-permute-start.16 = (bf16[4,16,32,128]{3,2,1,0:T(8,128)(2,1)S(1)}, bf16[4,16,32,128]{3,2,1,0:T(8,128)(2,1)S(1)}, u32[]{:S(2)}, u32[]{:S(2)}) collective-permute-start(bf16[4,16,32,128]{3,2,1,0:T(8,128)(2,1)S(1)} %copy-done.34), channel_id=1, source_target_pairs={{0,8},{4,12},{8,0},{12,4},{1,9},{5,13},{9,1},{13,5},{2,10},{6,14},... | collective-permute-start | bytes 1572872 | tf_op jit(solution)/shard_map/ppermute | solution.py:867
  109.2 48.8 %collective-permute-start.17 = (bf16[4,16,32,128]{3,2,1,0:T(8,128)(2,1)S(1)}, bf16[4,16,32,128]{3,2,1,0:T(8,128)(2,1)S(1)}, u32[]{:S(2)}, u32[]{:S(2)}) collective-permute-start(bf16[4,16,32,128]{3,2,1,0:T(8,128)(2,1)S(1)} %copy-done.30), channel_id=1, source_target_pairs={{0,12},{4,0},{8,4},{12,8},{1,13},{5,1},{9,5},{13,9},{2,14},{6,2},{... | collective-permute-start | bytes 1572872 | tf_op jit(solution)/shard_map/ppermute | solution.py:867
  185.9 14.2 %collective-permute-start.20 = (bf16[8,8,32,128]{3,2,1,0:T(8,128)(2,1)}, bf16[8,8,32,128]{3,2,1,0:T(8,128)(2,1)S(1)}, u32[]{:S(2)}, u32[]{:S(2)}) collective-permute-start(bf16[8,8,32,128]{3,2,1,0:T(8,128)(2,1)} %get-tuple-element.36.rest_3_), channel_id=1, source_target_pairs={{0,2},{2,0},{1,3},{3,1},{4,6},{6,4},{5,7},{7,5},{8,10},{10,8},{9,1... | collective-permute-start | bytes 1572872 | tf_op jit(solution)/shard_map/ppermute | solution.py:845
  188.6 19.0 %collective-permute-start.18 = (bf16[8,8,32,128]{3,2,1,0:T(8,128)(2,1)}, bf16[8,8,32,128]{3,2,1,0:T(8,128)(2,1)S(1)}, u32[]{:S(2)}, u32[]{:S(2)}) collective-permute-start(bf16[8,8,32,128]{3,2,1,0:T(8,128)(2,1)} %get-tuple-element.35.rest_0_), channel_id=1, source_target_pairs={{1,3},{2,0},{0,1},{3,2},{5,7},{6,4},{4,5},{7,6},{9,11},{10,8},{8,9... | collective-permute-start | bytes 1572872 | tf_op jit(solution)/shard_map/ppermute | solution.py:843
  200.1 17.7 %collective-permute-start.26 = (bf16[8,8,32,128]{3,2,1,0:T(8,128)(2,1)}, bf16[8,8,32,128]{3,2,1,0:T(8,128)(2,1)S(1)}, u32[]{:S(2)}, u32[]{:S(2)}) collective-permute-start(bf16[8,8,32,128]{3,2,1,0:T(8,128)(2,1)} %get-tuple-element.40.rest_3_), channel_id=1, source_target_pairs={{0,2},{2,0},{1,3},{3,1},{4,6},{6,4},{5,7},{7,5},{8,10},{10,8},{9,1... | collective-permute-start | bytes 1572872 | tf_op jit(solution)/shard_map/ppermute | solution.py:845
  211.8 19.4 %collective-permute-start.24 = (bf16[8,8,32,128]{3,2,1,0:T(8,128)(2,1)}, bf16[8,8,32,128]{3,2,1,0:T(8,128)(2,1)S(1)}, u32[]{:S(2)}, u32[]{:S(2)}) collective-permute-start(bf16[8,8,32,128]{3,2,1,0:T(8,128)(2,1)} %get-tuple-element.39.rest_0_), channel_id=1, source_target_pairs={{1,3},{2,0},{0,1},{3,2},{5,7},{6,4},{4,5},{7,6},{9,11},{10,8},{8,9... | collective-permute-start | bytes 1572872 | tf_op jit(solution)/shard_map/ppermute | solution.py:843
  217.8 29.4 %collective-permute-start.30 = (bf16[8,16,32,128]{3,2,1,0:T(8,128)(2,1)}, bf16[8,16,32,128]{3,2,1,0:T(8,128)(2,1)S(1)}, u32[]{:S(2)}, u32[]{:S(2)}) collective-permute-start(bf16[8,16,32,128]{3,2,1,0:T(8,128)(2,1)} %get-tuple-element.43.rest_0_), channel_id=1, source_target_pairs={{1,3},{2,0},{0,1},{3,2},{5,7},{6,4},{4,5},{7,6},{9,11},{10,8},{8,9... | collective-permute-start | bytes 3145736 | tf_op jit(solution)/shard_map/ppermute | solution.py:843
  223.5 66.6 %collective-permute-start.21 = (bf16[4,8,32,128]{3,2,1,0:T(8,128)(2,1)}, bf16[4,8,32,128]{3,2,1,0:T(8,128)(2,1)S(1)}, u32[]{:S(2)}, u32[]{:S(2)}) collective-permute-start(bf16[4,8,32,128]{3,2,1,0:T(8,128)(2,1)} %banded_products.37), channel_id=1, source_target_pairs={{0,4},{4,8},{8,12},{12,0},{1,5},{5,9},{9,13},{13,1},{2,6},{6,10},{... | collective-permute-start | bytes 786440 | tf_op jit(solution)/shard_map/ppermute | solution.py:867
  228.2 62.4 %collective-permute-start.22 = (bf16[4,8,32,128]{3,2,1,0:T(8,128)(2,1)}, bf16[4,8,32,128]{3,2,1,0:T(8,128)(2,1)S(1)}, u32[]{:S(2)}, u32[]{:S(2)}) collective-permute-start(bf16[4,8,32,128]{3,2,1,0:T(8,128)(2,1)} %banded_products.38), channel_id=1, source_target_pairs={{0,8},{4,12},{8,0},{12,4},{1,9},{5,13},{9,1},{13,5},{2,10},{6,14},... | collective-permute-start | bytes 786440 | tf_op jit(solution)/shard_map/ppermute | solution.py:867
  231.2 15.9 %collective-permute-start.25 = (bf16[8,8,32,128]{3,2,1,0:T(8,128)(2,1)S(1)}, bf16[8,8,32,128]{3,2,1,0:T(8,128)(2,1)S(1)}, u32[]{:S(2)}, u32[]{:S(2)}) collective-permute-start(bf16[8,8,32,128]{3,2,1,0:T(8,128)(2,1)S(1)} %collective-permute-done.24.rest_1_), channel_id=1, source_target_pairs={{0,1},{3,2},{4,5},{7,6},{8,9},{11,10},{12,13},{15,14},{16,17},{19,... | collective-permute-start | bytes 1572872 | tf_op jit(solution)/shard_map/ppermute | solution.py:844
  240.5 51.2 %collective-permute-start.23 = (bf16[4,8,32,128]{3,2,1,0:T(8,128)(2,1)}, bf16[4,8,32,128]{3,2,1,0:T(8,128)(2,1)S(1)}, u32[]{:S(2)}, u32[]{:S(2)}) collective-permute-start(bf16[4,8,32,128]{3,2,1,0:T(8,128)(2,1)} %banded_products.39), channel_id=1, source_target_pairs={{0,12},{4,0},{8,4},{12,8},{1,13},{5,1},{9,5},{13,9},{2,14},{6,2},{... | collective-permute-start | bytes 786440 | tf_op jit(solution)/shard_map/ppermute | solution.py:867
  247.1 25.2 %collective-permute-start.32 = (bf16[8,16,32,128]{3,2,1,0:T(8,128)(2,1)S(1)}, bf16[8,16,32,128]{3,2,1,0:T(8,128)(2,1)S(1)}, u32[]{:S(2)}, u32[]{:S(2)}) collective-permute-start(bf16[8,16,32,128]{3,2,1,0:T(8,128)(2,1)S(1)} %copy-done.18), channel_id=1, source_target_pairs={{0,2},{2,0},{1,3},{3,1},{4,6},{6,4},{5,7},{7,5},{8,10},{10,8},{9,1... | collective-permute-start | bytes 3145736 | tf_op jit(solution)/shard_map/ppermute | solution.py:845
  247.2 25.1 %collective-permute-start.31 = (bf16[8,16,32,128]{3,2,1,0:T(8,128)(2,1)S(1)}, bf16[8,16,32,128]{3,2,1,0:T(8,128)(2,1)S(1)}, u32[]{:S(2)}, u32[]{:S(2)}) collective-permute-start(bf16[8,16,32,128]{3,2,1,0:T(8,128)(2,1)S(1)} %collective-permute-done.30.rest_1_), channel_id=1, source_target_pairs={{0,1},{3,2},{4,5},{7,6},{8,9},{11,10},{12,13},{15,14},{16,17},{19,... | collective-permute-start | bytes 3145736 | tf_op jit(solution)/shard_map/ppermute | solution.py:844
  272.3 22.2 %collective-permute-start.27 = (bf16[4,8,32,128]{3,2,1,0:T(8,128)(2,1)S(1)}, bf16[4,8,32,128]{3,2,1,0:T(8,128)(2,1)S(1)}, u32[]{:S(2)}, u32[]{:S(2)}) collective-permute-start(bf16[4,8,32,128]{3,2,1,0:T(8,128)(2,1)S(1)} %copy-done.49), channel_id=1, source_target_pairs={{0,4},{4,8},{8,12},{12,0},{1,5},{5,9},{9,13},{13,1},{2,6},{6,10},{... | collective-permute-start | bytes 786440 | tf_op jit(solution)/shard_map/ppermute | solution.py:867
  272.3 27.4 %collective-permute-start.28 = (bf16[4,8,32,128]{3,2,1,0:T(8,128)(2,1)S(1)}, bf16[4,8,32,128]{3,2,1,0:T(8,128)(2,1)S(1)}, u32[]{:S(2)}, u32[]{:S(2)}) collective-permute-start(bf16[4,8,32,128]{3,2,1,0:T(8,128)(2,1)S(1)} %copy-done.47), channel_id=1, source_target_pairs={{0,8},{4,12},{8,0},{12,4},{1,9},{5,13},{9,1},{13,5},{2,10},{6,14},... | collective-permute-start | bytes 786440 | tf_op jit(solution)/shard_map/ppermute | solution.py:867
  290.7 18.7 %collective-permute-start.33 = (bf16[4,16,32,128]{3,2,1,0:T(8,128)(2,1)}, bf16[4,16,32,128]{3,2,1,0:T(8,128)(2,1)S(1)}, u32[]{:S(2)}, u32[]{:S(2)}) collective-permute-start(bf16[4,16,32,128]{3,2,1,0:T(8,128)(2,1)} %banded_products.45), channel_id=1, source_target_pairs={{0,4},{4,8},{8,12},{12,0},{1,5},{5,9},{9,13},{13,1},{2,6},{6,10},{... | collective-permute-start | bytes 1572872 | tf_op jit(solution)/shard_map/ppermute | solution.py:867
  291.6 51.0 %collective-permute-start.34 = (bf16[4,16,32,128]{3,2,1,0:T(8,128)(2,1)S(1)}, bf16[4,16,32,128]{3,2,1,0:T(8,128)(2,1)S(1)}, u32[]{:S(2)}, u32[]{:S(2)}) collective-permute-start(bf16[4,16,32,128]{3,2,1,0:T(8,128)(2,1)S(1)} %copy-done.35), channel_id=1, source_target_pairs={{0,8},{4,12},{8,0},{12,4},{1,9},{5,13},{9,1},{13,5},{2,10},{6,14},... | collective-permute-start | bytes 1572872 | tf_op jit(solution)/shard_map/ppermute | solution.py:867
  294.5 48.1 %collective-permute-start.35 = (bf16[4,16,32,128]{3,2,1,0:T(8,128)(2,1)S(1)}, bf16[4,16,32,128]{3,2,1,0:T(8,128)(2,1)S(1)}, u32[]{:S(2)}, u32[]{:S(2)}) collective-permute-start(bf16[4,16,32,128]{3,2,1,0:T(8,128)(2,1)S(1)} %copy-done.31), channel_id=1, source_target_pairs={{0,12},{4,0},{8,4},{12,8},{1,13},{5,1},{9,5},{13,9},{2,14},{6,2},{... | collective-permute-start | bytes 1572872 | tf_op jit(solution)/shard_map/ppermute | solution.py:867
  (54 other events, 529.9 us)

commit v5 on v4

--- a/solution.py
+++ b/solution.py
@@ -505,7 +505,7 @@
 
 def open_kernel(hidden, chunks, n_chan, n_sub, ids, blocks, pair_ref, chain_ref, w_ref, gate_ref, *rest):
     left_refs, right_refs = rest[:chunks], rest[chunks : 2 * chunks]
-    wide, laid, turned, swap = rest[2 * chunks :]
+    norm_ref, wide, laid, turned, swap = rest[2 * chunks :]
     slots = pl.num_programs(0)
     step = pl.program_id(0)
     _, rows, cols, channels = pair_ref.shape
@@ -516,12 +516,15 @@
         spread_weights(w_ref, wide, hidden, cols)
         swap[...] = swap_matrix(16)
 
-    normed = layer_norm(pair_ref[0].reshape(rows * cols, channels)).astype(jnp.bfloat16)
-    gate = sigmoid(dot(normed, w_ref[0, :, 4 * hidden :]))
-    gate_ref[0] = gate.reshape(rows, cols, channels)
+    group = hidden // cols
+    for start in range(0, rows, group):
+        at = pl.ds(start, group)
+        normed = layer_norm(pair_ref[0, at].reshape(group * cols, channels)).astype(jnp.bfloat16)
+        gate = sigmoid(dot(normed, w_ref[0, :, 4 * hidden :]))
+        gate_ref[0, at] = gate.reshape(group, cols, channels)
+        norm_ref[at] = normed.reshape(group, cols, channels)
     row_start, col_start = (blocks[0, block] * n_chan + ids[1]) * rows, (blocks[1, block] * n_sub + ids[2]) * cols
-    natural = normed.reshape(rows, cols, channels)
-    open_layer(0, natural, chain_ref, row_start, col_start, w_ref, left_refs, right_refs, wide, laid, turned, swap)
+    open_layer(0, norm_ref[...], chain_ref, row_start, col_start, w_ref, left_refs, right_refs, wide, laid, turned, swap)
 
 
 def operand_scratch(rows, size, hidden):
@@ -549,7 +552,7 @@
             ],
             out_specs=[pl.BlockSpec((1, rows, cols, channels), lambda s, *_: (s, 0, 0, 0))]
             + [pl.BlockSpec((1,) + o.shape[1:], lambda s, *_: (s, 0, 0, 0)) for o in operands],
-            scratch_shapes=operand_scratch(rows, cols, hidden),
+            scratch_shapes=[pltpu.VMEM((rows, cols, channels), jnp.bfloat16)] + operand_scratch(rows, cols, hidden),
         ),
         out_shape=[jax.ShapeDtypeStruct(pair.shape, jnp.float32)] + operands,
         compiler_params=pltpu.CompilerParams(vmem_limit_bytes=vmem_limit),
@@ -558,76 +561,73 @@
     return out[0], out[1 : 1 + len(bands)], out[1 + len(bands) :]
 
 
-def banded_kernel(shift, n_blk, slots_dev, terms, capacity, pieces, n_refs, size, ids, owners, slots, *rest):
-    refs = rest[:n_refs]
-    out_ref, left_held, right_held, chosen, sems = rest[n_refs:]
+def banded_kernel(shifts, n_blk, slots_dev, terms, capacity, pieces, n_refs, size, ids, owners, slots, *rest):
+    refs, rest = rest[:n_refs], rest[n_refs:]
+    out_refs, (left_held, right_held, chosen, sems) = rest[: len(shifts)], rest[len(shifts) :]
     step = pl.program_id(0)
-    turn = lax.rem(step, 2)
     _, halves, bands, rows, hidden = left_held.shape
     parts = hidden // size
+    count = len(shifts) * capacity
+
+    def copy(n, term, source):
+        side, half, *_ = pieces[n]
+        held = (left_held, right_held)[side]
+        return pltpu.make_async_copy(refs[source].at[chosen[2 * term + side]], held.at[term, half], sems.at[term, n])
+
+    def start(term):
+        for n, (_, _, on, off) in enumerate(pieces):
+            if on == off:
+                copy(n, term, on).start()
+            else:
+
+                @pl.when(ids[3] == 1)
+                def _(n=n, on=on):
+                    copy(n, term, on).start()
+
+                @pl.when(ids[3] == 0)
+                def _(n=n, off=off):
+                    copy(n, term, off).start()
 
     @pl.when(step == 0)
     def _():
-        target = lax.rem(ids[0] + shift, n_blk)
-        for e in range(2 * capacity):
+        for e in range(2 * count):
             chosen[e] = 0
-
-        def scan(e, count):
-            block, term = target * slots_dev + e // terms, lax.rem(e, terms)
-            here = jnp.logical_and(owners[term, block] == ids[0], count < capacity)
-
-            @pl.when(here)
-            def _():
-                chosen[2 * count] = slots[term, 0, block]
-                chosen[2 * count + 1] = slots[term, 1, block]
-
-            return count + here.astype(jnp.int32)
-
-        lax.fori_loop(0, slots_dev * terms, scan, jnp.int32(0))
-
-    def copy(n, term, buffer, source):
-        side, half, *_ = pieces[n]
-        held = (left_held, right_held)[side]
-        return pltpu.make_async_copy(
-            refs[source].at[chosen[2 * term + side]], held.at[buffer, half], sems.at[buffer, n]
-        )
-
-    def start(term, buffer):
-        for n, (_, _, on, off) in enumerate(pieces):
-            if on == off:
-                copy(n, term, buffer, on).start()
-            else:
-
-                @pl.when(ids[3] == 1)
-                def _(n=n, on=on):
-                    copy(n, term, buffer, on).start()
-
-                @pl.when(ids[3] == 0)
-                def _(n=n, off=off):
-                    copy(n, term, buffer, off).start()
-
-    @pl.when(step == 0)
-    def _():
-        start(0, 0)
-
-    @pl.when(step + 1 < capacity)
-    def _():
-        start(step + 1, 1 - turn)
+        for n, shift in enumerate(shifts):
+            target = lax.rem(ids[0] + shift, n_blk)
+
+            def scan(e, found):
+                block, term = target * slots_dev + e // terms, lax.rem(e, terms)
+                here = jnp.logical_and(owners[term, block] == ids[0], found < capacity)
+
+                @pl.when(here)
+                def _():
+                    chosen[2 * (n * capacity + found)] = slots[term, 0, block]
+                    chosen[2 * (n * capacity + found) + 1] = slots[term, 1, block]
+
+                return found + here.astype(jnp.int32)
+
+            lax.fori_loop(0, slots_dev * terms, scan, jnp.int32(0))
+        for term in range(count):
+            start(term)
 
     for n, piece in enumerate(pieces):
-        copy(n, step, turn, piece[2]).wait()
-
-    group = lane_group((size, hidden), size)
-    for band in range(bands):
-        left = jnp.concatenate([left_held[turn, h, band] for h in range(halves)], axis=1)
-        apart = []
-        for h in range(halves):
-            right = right_held[turn, h, band]
-            apart += [jnp.where(group == part, right, jnp.zeros_like(right)) for part in range(parts)]
-        out_ref[0, band] = dot(left, jnp.concatenate(apart, axis=0)).astype(jnp.bfloat16)
-
-
-def banded_products(shift, ids, owners, slots, lefts, rights, capacity, slots_dev, terms, size):
+        copy(n, step, piece[2]).wait()
+
+    for n, out_ref in enumerate(out_refs):
+
+        @pl.when(step // capacity == n)
+        def _(out_ref=out_ref):
+            group = lane_group((size, hidden), size)
+            for band in range(bands):
+                left = jnp.concatenate([left_held[step, h, band] for h in range(halves)], axis=1)
+                apart = []
+                for h in range(halves):
+                    right = right_held[step, h, band]
+                    apart += [jnp.where(group == part, right, jnp.zeros_like(right)) for part in range(parts)]
+                out_ref[0, band] = dot(left, jnp.concatenate(apart, axis=0)).astype(jnp.bfloat16)
+
+
+def banded_products(shifts, ids, owners, slots, lefts, rights, capacity, slots_dev, terms, size):
     n_blk = lax.axis_size("blk")
     refs, pieces = [], []
 
@@ -642,28 +642,33 @@
         for half, (on, off) in enumerate(operands):
             pieces.append((side, half, index_of(on), index_of(off)))
     _, bands, rows, hidden = lefts[0][0].shape
+    count = len(shifts) * capacity
+
+    def out_spec(n):
+        return pl.BlockSpec(
+            (1, bands, rows, hidden), lambda t, *_: (jnp.clip(t - n * capacity, 0, capacity - 1), 0, 0, 0)
+        )
+
     return pl.pallas_call(
         functools.partial(
-            banded_kernel, shift, n_blk, slots_dev, terms, capacity, tuple(pieces), len(refs), size
+            banded_kernel, shifts, n_blk, slots_dev, terms, capacity, tuple(pieces), len(refs), size
         ),
         grid_spec=pltpu.PrefetchScalarGridSpec(
             num_scalar_prefetch=3,
-            grid=(capacity,),
+            grid=(count,),
             in_specs=[pl.BlockSpec(memory_space=pl.ANY)] * len(refs),
-            out_specs=pl.BlockSpec((1, bands, rows, hidden), lambda t, *_: (t, 0, 0, 0)),
+            out_specs=[out_spec(n) for n in range(len(shifts))],
             scratch_shapes=[
-                pltpu.VMEM((2, len(lefts), bands, rows, hidden), jnp.bfloat16),
-                pltpu.VMEM((2, len(rights), bands, size, hidden), jnp.bfloat16),
-                pltpu.SMEM((2 * capacity,), jnp.int32),
-                pltpu.SemaphoreType.DMA((2, len(pieces))),
+                pltpu.VMEM((count, len(lefts), bands, rows, hidden), jnp.bfloat16),
+                pltpu.VMEM((count, len(rights), bands, size, hidden), jnp.bfloat16),
+                pltpu.SMEM((2 * count,), jnp.int32),
+                pltpu.SemaphoreType.DMA((count, len(pieces))),
             ],
         ),
-        out_shape=jax.ShapeDtypeStruct((capacity, bands, rows, hidden), jnp.bfloat16),
+        out_shape=[jax.ShapeDtypeStruct((capacity, bands, rows, hidden), jnp.bfloat16)] * len(shifts),
         compiler_params=pltpu.CompilerParams(vmem_limit_bytes=vmem_limit),
         cost_estimate=pl.CostEstimate(
-            flops=2 * capacity * bands * rows * hidden * hidden * len(lefts) * 50,
-            bytes_accessed=capacity * bands * rows * hidden * 2 * 5,
-            transcendentals=0,
+            flops=2 * count * bands * rows * hidden * hidden * len(lefts), bytes_accessed=1, transcendentals=0
         ),
         name="banded_products",
     )(ids, owners, slots, *refs)
@@ -784,7 +789,7 @@
     out_shape = [jax.ShapeDtypeStruct(current.shape, jnp.bfloat16)]
     out_specs = [whole]
     scratch = [
-        pltpu.VMEM((n_blk * capacity, sum(bands), rows, hidden), jnp.bfloat16),
+        pltpu.VMEM((n_blk * capacity, sum(bands[layer]), rows, hidden), jnp.bfloat16),
         pltpu.VMEM((hidden // cols * hidden, hidden // cols * channels), jnp.bfloat16),
         pltpu.SMEM((slots * terms,), jnp.int32),
         pltpu.SMEM((n_blk,), jnp.int32),
@@ -793,6 +798,7 @@
     if not last:
         operands += [chains, w_in]
         in_specs += [pl.BlockSpec(chains.shape, lambda s, *_: (0, 0)), layer_spec(w_in, layer + 1)]
+        bands = bands[layer + 1]
         made = [jax.ShapeDtypeStruct((slots, count, cols, hidden), jnp.bfloat16) for count in bands] * 2
         out_shape += [jax.ShapeDtypeStruct(current.shape, jnp.float32)] + made
         out_specs += [whole] + [pl.BlockSpec((1,) + o.shape[1:], lambda s, *_: (s, 0, 0, 0)) for o in made]
@@ -824,9 +830,9 @@
     made = []
     for left, right in zip(lefts, rights):
         if made:
-            (_, other_left), *_ = made[-1][0]
-            _, (_, two) = made[-1][1]
-            right = after(right, two)
+            (before, _), _ = made[-1][0]
+            (one, _), (_, two) = made[-1][1]
+            left, right = lax.optimization_barrier((left, right, before, one, two))[:2]
         other_left = lax.ppermute(left, "sub", [(0, 1), (1, 0)])
         one = lax.ppermute(right, both, [(0, 2), (3, 1), (1, 0), (2, 3)])
         two = lax.ppermute(right, both, [(1, 2), (2, 1)])
@@ -839,7 +845,8 @@
     made = []
     for left, right in zip(lefts, rights):
         if made:
-            right, left = lax.optimization_barrier((right, left, made[-1][1][1][0]))[:2]
+            before, other = made[-1][0][1][1], made[-1][1][1][0]
+            left, right = lax.optimization_barrier((left, right, before, other))[:2]
         one = lax.ppermute(left, both, [(1, 3), (2, 0), (0, 1), (3, 2)])
         two = lax.ppermute(one, both, [(0, 1), (3, 2)])
         other = lax.ppermute(right, "chan", [(0, 1), (1, 0)])
@@ -850,22 +857,29 @@
 def banded(pair, ids, blocks, owners, slot_of, chains, w_in, w_out, capacity, terms, n_blk):
     slots, rows, cols, channels = pair.shape
     hidden = w_out.shape[1]
-    shifts = [n_blk // 2] + [s for s in range(1, n_blk) if s != n_blk // 2] + [0]
+    far = n_blk // 2
+    calls = [[far], [s for s in range(1, n_blk) if s != far] + [0]]
     layers = w_in.shape[0]
     current = pair
+    bands = [[12, 20], [14, 18]]
     for layer in range(layers):
-        bands = [cols // 4, cols // 4, cols // 2]
         if layer == 0:
-            gate, lefts, rights = open_operands(ids, blocks, pair, chains, w_in, hidden, bands)
+            gate, lefts, rights = open_operands(ids, blocks, pair, chains, w_in, hidden, bands[0])
         exchange = exchange_bands_incoming if layer % 2 else exchange_bands_outgoing
-        arrived = []
+        arrived, last_made = [], None
         for left, right in exchange(lefts, rights):
             parts = [None] * n_blk
-            for shift in shifts:
-                made = banded_products(shift, ids, owners, slot_of, left, right, capacity, slots, terms, cols)
-                if shift:
-                    made = lax.ppermute(made, "blk", [(p, (p + shift) % n_blk) for p in range(n_blk)])
-                parts[shift] = made
+            for shifts in calls:
+                if last_made is not None:
+                    ids = after(ids, last_made)
+                made = banded_products(shifts, ids, owners, slot_of, left, right, capacity, slots, terms, cols)
+                last_made = made[-1]
+                for shift, part in zip(shifts, made):
+                    if shift:
+                        if arrived:
+                            part = after(part, arrived[-1][shift])
+                        part = lax.ppermute(part, "blk", [(p, (p + shift) % n_blk) for p in range(n_blk)])
+                    parts[shift] = part
             arrived.append(parts)
         last = layer == layers - 1
         out = close_layer(

time: 362 us -> 355 us (0.981)
  waiting for transfers between devices: 115 us -> 192 us
  Pallas kernels: 177 us -> 115 us
  starting transfers between devices: 59 us -> 39.3 us
    pallas_call x24 -> x8, Pallas kernels: 117 us -> 55.7 us  [banded_products(): pl.pallas_call(functools.partial(banded_kernel, shifts, n_blk, slots_dev,...]
    ppermute x3 -> x2, waiting for transfers between devices: 5.45 us -> 43.3 us  [exchange_bands_incoming(): one = lax.ppermute(left, both, [(1, 3), (2, 0), (0, 1), (3, 2)])]
    ppermute x18 -> x12, waiting for transfers between devices: 86.3 us -> 112 us  [banded(): lax.ppermute(part, 'blk', [(p, (p + shift) % n_blk) for p in range(n_blk)])]
    ppermute x3 -> x2, waiting for transfers between devices: 2.31 us -> 28.2 us  [exchange_bands_outgoing(): one = lax.ppermute(right, both, [(0, 2), (3, 1), (1, 0), (2, 3)])]
    ppermute x3 -> x2, waiting for transfers between devices: 21.4 us -> 8.19 us  [exchange_bands_incoming(): other = lax.ppermute(right, 'chan', [(0, 1), (1, 0)])]
    ppermute x3 -> x2, starting transfers between devices: 17.5 us -> 5.12 us  [exchange_bands_outgoing(): one = lax.ppermute(right, both, [(0, 2), (3, 1), (1, 0), (2, 3)])]
    ppermute x18 -> x12, starting transfers between devices: 21.3 us -> 17.9 us  [banded(): lax.ppermute(part, 'blk', [(p, (p + shift) % n_blk) for p in range(n_blk)])]
    ppermute x3 -> x2, starting transfers between devices: 10.4 us -> 7.55 us  [exchange_bands_incoming(): two = lax.ppermute(one, both, [(0, 1), (3, 2)])]
  transfers between devices with their start and end apart: 36 -> 24, of which waited for: 10 -> 14; matrix products, arithmetic and copies ran while one was open for 0% -> 0% of each run, Pallas kernels for 33% -> 16%
where the time goes in v5:
time: 355 us; the launch traced here: 353 us
  waiting for transfers between devices  192 us (54%)
  Pallas kernels  115 us (32%)
  starting transfers between devices  39.3 us (11%)
  local copies, waits for them, and re-layouts  4.89 us (1%)
    ppermute x12, waiting for transfers between devices, banded(): lax.ppermute(part, 'blk', [(p, (p + shift) % n_blk) for p in range(n_blk)])  112 us
    pallas_call x8, Pallas kernels, banded_products(): pl.pallas_call(functools.partial(banded_kernel, shifts, n_blk, slots_dev,...  55.7 us
    ppermute x2, waiting for transfers between devices, exchange_bands_incoming(): one = lax.ppermute(left, both, [(1, 3), (2, 0), (0, 1), (3, 2)])  43.3 us
    pallas_call x2, Pallas kernels, close_layer(): pl.pallas_call(functools.partial(close_kernel, layer, last, len(flat), n_...  40 us
    ppermute x2, waiting for transfers between devices, exchange_bands_outgoing(): one = lax.ppermute(right, both, [(0, 2), (3, 1), (1, 0), (2, 3)])  28.2 us
    pallas_call x1, Pallas kernels, open_operands(): pl.pallas_call(functools.partial(open_kernel, hidden, len(bands), lax.axi...  19.2 us
    ppermute x12, starting transfers between devices, banded(): lax.ppermute(part, 'blk', [(p, (p + shift) % n_blk) for p in range(n_blk)])  17.9 us
    ppermute x2, waiting for transfers between devices, exchange_bands_incoming(): other = lax.ppermute(right, 'chan', [(0, 1), (1, 0)])  8.19 us
  transfers between devices with their start and end apart: 24, of which 14 were waited for; matrix products, arithmetic and copies ran while one was open for 0% of the time, Pallas kernels for 16%

profile of v5, /device:TPU:11, one launch (start us, length us, event | category | flops | bytes accessed | tf_op | source)
XLA Modules:
  0.0 352.5 jit_solution(2158091678112967547)
XLA Ops:
  0.7 19.2 %open_operands.1 = (f32[8,32,32,128]{3,2,1,0:T(8,128)}, bf16[8,12,32,128]{3,2,1,0:T(8,128)(2,1)}, bf16[8,20,32,128]{3,2,1,0:T(8,128)(2,1)}, bf16[8,12,32,128]{3,2,1,0:T(8,128)(2,1)}, bf16[8,20,32,128]{3,2,1,0:T(8,128)(2,1)}) custom-call(s32[4]{0:T(128)} %pad_add_fusion.ids, s32[2,32]{1,0:T(2,128)} %bitcast.28, bf16[8,32,32,128]{3,2,1,0:T(8,128)(2,1)} %rest_8_.1, ...), custom_call_target="tpu_custom_call" | custom-call | tf_op jit(solution)/shard_map/open_operands/pallas_call | solution.py:543
  21.3 2.6 collective-permute-start.1
  23.9 17.1 %collective-permute-done.1.rest_2_ = bf16[8,12,32,128]{3,2,1,0:T(8,128)(2,1)S(1)} collective-permute-done((bf16[8,12,32,128]{3,2,1,0:T(8,128)(2,1)}, bf16[8,12,32,128]{3,2,1,0:T(8,128)(2,1)S(1)}, u32[]{:S(2)}, u32[]{:S(2)}) %collective-permute-start.1) | collective-permute-done | bytes 786464 | tf_op jit(solution)/shard_map/ppermute | solution.py:837
  43.3 2.5 collective-permute-start.4
  45.8 4.3 %banded_products.8 = bf16[4,12,32,128]{3,2,1,0:T(8,128)(2,1)} custom-call(s32[4]{0:T(128)} %pad_add_fusion.ids, s32[2,32]{1,0:T(2,128)} %bitcast.16, s32[2,2,32]{2,1,0:T(2,128)} %bitcast.8, bf16[8,12,32,128]{3,2,1,0:T(8,128)(2,1)} %copy-done.9, bf16[8,12,32,128]{3,2,1,0:T(8,128)(2,1)} %get-tuple-element.44.rest_1_, bf16[8,12,32,128]{3,2,1,0:T(8,128)(2,1)} %copy-done.11, ...), custom_call_target="tpu_custom_call" | custom-call | flops 100663296 | bytes 1 | tf_op jit(solution)/shard_map/banded_products/pallas_call | solution.py:652
  50.1 2.4 collective-permute-start.7
  52.5 9.0 %banded_products.9 = (bf16[4,12,32,128]{3,2,1,0:T(8,128)(2,1)}, bf16[4,12,32,128]{3,2,1,0:T(8,128)(2,1)}, bf16[4,12,32,128]{3,2,1,0:T(8,128)(2,1)}) custom-call(s32[4]{0:T(128)} %pad_add_fusion.ids, s32[2,32]{1,0:T(2,128)} %bitcast.17, s32[2,2,32]{2,1,0:T(2,128)} %bitcast.9, bf16[8,12,32,128]{3,2,1,0:T(8,128)(2,1)} %copy-done.9, ...), custom_call_target="tpu_custom_call" | custom-call | flops 301989888 | bytes 1 | tf_op jit(solution)/shard_map/banded_products/pallas_call | solution.py:652
  63.0 11.1 %collective-permute-done.4.rest_2_ = bf16[8,20,32,128]{3,2,1,0:T(8,128)(2,1)S(1)} collective-permute-done((bf16[8,20,32,128]{3,2,1,0:T(8,128)(2,1)}, bf16[8,20,32,128]{3,2,1,0:T(8,128)(2,1)S(1)}, u32[]{:S(2)}, u32[]{:S(2)}) %collective-permute-start.4) | collective-permute-done | bytes 1310752 | tf_op jit(solution)/shard_map/ppermute | solution.py:837
  75.3 4.7 %banded_products.10 = bf16[4,20,32,128]{3,2,1,0:T(8,128)(2,1)} custom-call(s32[4]{0:T(128)} %pad_add_fusion.ids, s32[2,32]{1,0:T(2,128)} %bitcast.18, s32[2,2,32]{2,1,0:T(2,128)} %bitcast.10, bf16[8,20,32,128]{3,2,1,0:T(8,128)(2,1)} %copy-done, bf16[8,20,32,128]{3,2,1,0:T(8,128)(2,1)} %get-tuple-element.51.rest_1_, bf16[8,20,32,128]{3,2,1,0:T(8,128)(2,1)} %copy-done.2, ...), custom_call_target="tpu_custom_call" | custom-call | flops 167772160 | bytes 1 | tf_op jit(solution)/shard_map/banded_products/pallas_call | solution.py:652
  80.0 9.9 %banded_products.11 = (bf16[4,20,32,128]{3,2,1,0:T(8,128)(2,1)}, bf16[4,20,32,128]{3,2,1,0:T(8,128)(2,1)}, bf16[4,20,32,128]{3,2,1,0:T(8,128)(2,1)}) custom-call(s32[4]{0:T(128)} %pad_add_fusion.ids, s32[2,32]{1,0:T(2,128)} %bitcast.19, s32[2,2,32]{2,1,0:T(2,128)} %bitcast.11, bf16[8,20,32,128]{3,2,1,0:T(8,128)(2,1)} %copy-done, ...), custom_call_target="tpu_custom_call" | custom-call | flops 503316480 | bytes 1 | tf_op jit(solution)/shard_map/banded_products/pallas_call | solution.py:652
  91.5 4.1 %collective-permute-start.10 = (bf16[4,20,32,128]{3,2,1,0:T(8,128)(2,1)S(1)}, bf16[4,20,32,128]{3,2,1,0:T(8,128)(2,1)S(1)}, u32[]{:S(2)}, u32[]{:S(2)}) collective-permute-start(bf16[4,20,32,128]{3,2,1,0:T(8,128)(2,1)S(1)} %copy-done.15), channel_id=1, source_target_pairs={{0,8},{4,12},{8,0},{12,4},{1,9},{5,13},{9,1},{13,5},{2,10},{6,14},... | collective-permute-start | bytes 1966088 | tf_op jit(solution)/shard_map/ppermute | solution.py:881
  95.6 9.3 %collective-permute-done.11.rest_7_ = bf16[4,20,32,128]{3,2,1,0:T(8,128)(2,1)S(1)} collective-permute-done((bf16[4,20,32,128]{3,2,1,0:T(8,128)(2,1)}, bf16[4,20,32,128]{3,2,1,0:T(8,128)(2,1)S(1)}, u32[]{:S(2)}, u32[]{:S(2)}) %collective-permute-start.11) | collective-permute-done | bytes 655392 | tf_op jit(solution)/shard_map/ppermute | solution.py:881
  104.9 16.1 %collective-permute-done.9.rest_5_ = bf16[4,20,32,128]{3,2,1,0:T(8,128)(2,1)S(1)} collective-permute-done((bf16[4,20,32,128]{3,2,1,0:T(8,128)(2,1)}, bf16[4,20,32,128]{3,2,1,0:T(8,128)(2,1)S(1)}, u32[]{:S(2)}, u32[]{:S(2)}) %collective-permute-start.9) | collective-permute-done | bytes 655392 | tf_op jit(solution)/shard_map/ppermute | solution.py:881
  121.0 25.4 %collective-permute-done.10.rest_6_ = bf16[4,20,32,128]{3,2,1,0:T(8,128)(2,1)S(1)} collective-permute-done((bf16[4,20,32,128]{3,2,1,0:T(8,128)(2,1)S(1)}, bf16[4,20,32,128]{3,2,1,0:T(8,128)(2,1)S(1)}, u32[]{:S(2)}, u32[]{:S(2)}) %collective-permute-start.10) | collective-permute-done | bytes 655392 | tf_op jit(solution)/shard_map/ppermute | solution.py:881
  147.3 27.0 %close_layer.2 = (bf16[8,32,32,128]{3,2,1,0:T(8,128)(2,1)}, f32[8,32,32,128]{3,2,1,0:T(8,128)}, bf16[8,14,32,128]{3,2,1,0:T(8,128)(2,1)}, bf16[8,18,32,128]{3,2,...) custom-call(s32[4]{0:T(128)} %pad_add_fusion.ids, s32[2,32]{1,0:T(2,128)} %bitcast.29, ...), custom_call_target="tpu_custom_call" | custom-call | tf_op jit(solution)/shard_map/close_layer/pallas_call | solution.py:808
  174.3 2.3 collective-permute-start.12
  178.0 19.4 %collective-permute-done.12.rest_1_ = bf16[8,14,32,128]{3,2,1,0:T(8,128)(2,1)S(1)} collective-permute-done((bf16[8,14,32,128]{3,2,1,0:T(8,128)(2,1)}, bf16[8,14,32,128]{3,2,1,0:T(8,128)(2,1)S(1)}, u32[]{:S(2)}, u32[]{:S(2)}) %collective-permute-start.12) | collective-permute-done | bytes 917536 | tf_op jit(solution)/shard_map/ppermute | solution.py:850
  197.3 3.0 collective-permute-start.13
  200.3 8.2 %collective-permute-done.14.rest_4_ = bf16[8,14,32,128]{3,2,1,0:T(8,128)(2,1)S(1)} collective-permute-done((bf16[8,14,32,128]{3,2,1,0:T(8,128)(2,1)}, bf16[8,14,32,128]{3,2,1,0:T(8,128)(2,1)S(1)}, u32[]{:S(2)}, u32[]{:S(2)}) %collective-permute-start.14) | collective-permute-done | bytes 917536 | tf_op jit(solution)/shard_map/ppermute | solution.py:852
  210.0 23.9 %collective-permute-done.15.rest_1_ = bf16[8,18,32,128]{3,2,1,0:T(8,128)(2,1)S(1)} collective-permute-done((bf16[8,18,32,128]{3,2,1,0:T(8,128)(2,1)}, bf16[8,18,32,128]{3,2,1,0:T(8,128)(2,1)S(1)}, u32[]{:S(2)}, u32[]{:S(2)}) %collective-permute-start.15) | collective-permute-done | bytes 1179680 | tf_op jit(solution)/shard_map/ppermute | solution.py:850
  233.9 4.5 %collective-permute-start.16 = (bf16[8,18,32,128]{3,2,1,0:T(8,128)(2,1)S(1)}, bf16[8,18,32,128]{3,2,1,0:T(8,128)(2,1)S(1)}, u32[]{:S(2)}, u32[]{:S(2)}) collective-permute-start(bf16[8,18,32,128]{3,2,1,0:T(8,128)(2,1)S(1)} %collective-permute-done.15.rest_1_), channel_id=1, source_target_pairs={{0,1},{3,2},{4,5},{7,6},{8,9},{11,10},{12,13},{15,14},{16,17},{19,... | collective-permute-start | bytes 3538952 | tf_op jit(solution)/shard_map/ppermute | solution.py:851
  238.5 4.4 %banded_products.12 = bf16[4,14,32,128]{3,2,1,0:T(8,128)(2,1)} custom-call(s32[4]{0:T(128)} %pad_add_fusion.ids, s32[2,32]{1,0:T(2,128)} %bitcast.21, s32[2,2,32]{2,1,0:T(2,128)} %bitcast.12, bf16[8,14,32,128]{3,2,1,0:T(8,128)(2,1)} %get-tuple-element.63.rest_0_, bf16[8,14,32,128]{3,2,1,0:T(8,128)(2,1)} %copy-done.6, bf16[8,14,32,128]{3,2,1,0:T(8,128)(2,1)} %copy-done.8, ...), custom_call_target="tpu_custom_call" | custom-call | flops 117440512 | bytes 1 | tf_op jit(solution)/shard_map/banded_products/pallas_call | solution.py:652
  243.0 2.9 collective-permute-start.19
  245.8 9.2 %banded_products.13 = (bf16[4,14,32,128]{3,2,1,0:T(8,128)(2,1)}, bf16[4,14,32,128]{3,2,1,0:T(8,128)(2,1)}, bf16[4,14,32,128]{3,2,1,0:T(8,128)(2,1)}) custom-call(s32[4]{0:T(128)} %pad_add_fusion.ids, s32[2,32]{1,0:T(2,128)} %bitcast.22, s32[2,2,32]{2,1,0:T(2,128)} %bitcast.13, bf16[8,14,32,128]{3,2,1,0:T(8,128)(2,1)} %get-tuple-element.63.rest_0_, ...), custom_call_target="tpu_custom_call" | custom-call | flops 352321536 | bytes 1 | tf_op jit(solution)/shard_map/banded_products/pallas_call | solution.py:652
  258.7 4.6 %banded_products.14 = bf16[4,18,32,128]{3,2,1,0:T(8,128)(2,1)} custom-call(s32[4]{0:T(128)} %pad_add_fusion.ids, s32[2,32]{1,0:T(2,128)} %bitcast.23, s32[2,2,32]{2,1,0:T(2,128)} %bitcast.14, bf16[8,18,32,128]{3,2,1,0:T(8,128)(2,1)} %get-tuple-element.70.rest_0_, bf16[8,18,32,128]{3,2,1,0:T(8,128)(2,1)} %copy-done.3, bf16[8,18,32,128]{3,2,1,0:T(8,128)(2,1)} %copy-done.5, ...), custom_call_target="tpu_custom_call" | custom-call | flops 150994944 | bytes 1 | tf_op jit(solution)/shard_map/banded_products/pallas_call | solution.py:652
  264.1 9.6 %banded_products.15 = (bf16[4,18,32,128]{3,2,1,0:T(8,128)(2,1)}, bf16[4,18,32,128]{3,2,1,0:T(8,128)(2,1)}, bf16[4,18,32,128]{3,2,1,0:T(8,128)(2,1)}) custom-call(s32[4]{0:T(128)} %pad_add_fusion.ids, s32[2,32]{1,0:T(2,128)} %bitcast.24, s32[2,2,32]{2,1,0:T(2,128)} %bitcast.15, bf16[8,18,32,128]{3,2,1,0:T(8,128)(2,1)} %get-tuple-element.70.rest_0_, ...), custom_call_target="tpu_custom_call" | custom-call | flops 452984832 | bytes 1 | tf_op jit(solution)/shard_map/banded_products/pallas_call | solution.py:652
  273.7 10.1 %collective-permute-done.18.rest_1_ = bf16[4,14,32,128]{3,2,1,0:T(8,128)(2,1)S(1)} collective-permute-done((bf16[4,14,32,128]{3,2,1,0:T(8,128)(2,1)}, bf16[4,14,32,128]{3,2,1,0:T(8,128)(2,1)S(1)}, u32[]{:S(2)}, u32[]{:S(2)}) %collective-permute-start.18) | collective-permute-done | bytes 458784 | tf_op jit(solution)/shard_map/ppermute | solution.py:881
  287.5 2.5 collective-permute-start.22
  290.0 11.2 %collective-permute-done.23.rest_7_ = bf16[4,18,32,128]{3,2,1,0:T(8,128)(2,1)S(1)} collective-permute-done((bf16[4,18,32,128]{3,2,1,0:T(8,128)(2,1)}, bf16[4,18,32,128]{3,2,1,0:T(8,128)(2,1)S(1)}, u32[]{:S(2)}, u32[]{:S(2)}) %collective-permute-start.23) | collective-permute-done | bytes 589856 | tf_op jit(solution)/shard_map/ppermute | solution.py:881
  301.2 12.7 %collective-permute-done.21.rest_5_ = bf16[4,18,32,128]{3,2,1,0:T(8,128)(2,1)S(1)} collective-permute-done((bf16[4,18,32,128]{3,2,1,0:T(8,128)(2,1)}, bf16[4,18,32,128]{3,2,1,0:T(8,128)(2,1)S(1)}, u32[]{:S(2)}, u32[]{:S(2)}) %collective-permute-start.21) | collective-permute-done | bytes 589856 | tf_op jit(solution)/shard_map/ppermute | solution.py:881
  313.9 24.6 %collective-permute-done.22.rest_6_ = bf16[4,18,32,128]{3,2,1,0:T(8,128)(2,1)S(1)} collective-permute-done((bf16[4,18,32,128]{3,2,1,0:T(8,128)(2,1)S(1)}, bf16[4,18,32,128]{3,2,1,0:T(8,128)(2,1)S(1)}, u32[]{:S(2)}, u32[]{:S(2)}) %collective-permute-start.22) | collective-permute-done | bytes 589856 | tf_op jit(solution)/shard_map/ppermute | solution.py:881
  339.4 13.0 %close_layer.3 = bf16[8,32,32,128]{3,2,1,0:T(8,128)(2,1)} custom-call(s32[4]{0:T(128)} %pad_add_fusion.ids, s32[2,32]{1,0:T(2,128)} %bitcast.30, s32[2,32]{1,0:T(2,128)} %bitcast.25, bf16[4,14,32,128]{3,2,1,0:T(8,128)(2,1)} %get-tuple-element.66.rest_0_, bf16[4,14,32,128]{3,2,1,0:T(8,128)(2,1)} %copy-done.21, bf16[4,14,32,128]{3,2,1,0:T(8,128)(2,1)} %copy-done.20, ...), custom_call_target="tpu_custom_call" | custom-call | tf_op jit(solution)/shard_map/close_layer/pallas_call | solution.py:808
  (80 shorter events, 21.1 us)
Async XLA Ops:
  19.9 4.0 %collective-permute-start = (bf16[8,12,32,128]{3,2,1,0:T(8,128)(2,1)}, bf16[8,12,32,128]{3,2,1,0:T(8,128)(2,1)S(1)}, u32[]{:S(2)}, u32[]{:S(2)}) collective-permute-start(bf16[8,12,32,128]{3,2,1,0:T(8,128)(2,1)} %get-tuple-element.44.rest_1_), channel_id=1, source_target_pairs={{0,1},{1,0},{2,3},{3,2},{4,5},{5,4},{6,7},{7,6},{8,9},{9,8},{10,11... | collective-permute-start | bytes 2359304 | tf_op jit(solution)/shard_map/ppermute | solution.py:836
  20.6 3.3 collective-permute-start.2
  21.3 19.7 %collective-permute-start.1 = (bf16[8,12,32,128]{3,2,1,0:T(8,128)(2,1)}, bf16[8,12,32,128]{3,2,1,0:T(8,128)(2,1)S(1)}, u32[]{:S(2)}, u32[]{:S(2)}) collective-permute-start(bf16[8,12,32,128]{3,2,1,0:T(8,128)(2,1)} %get-tuple-element.45.rest_3_), channel_id=1, source_target_pairs={{0,2},{3,1},{1,0},{2,3},{4,6},{7,5},{5,4},{6,7},{8,10},{11,9},{9,8... | collective-permute-start | bytes 2359304 | tf_op jit(solution)/shard_map/ppermute | solution.py:837
  41.0 20.6 %collective-permute-start.3 = (bf16[8,20,32,128]{3,2,1,0:T(8,128)(2,1)}, bf16[8,20,32,128]{3,2,1,0:T(8,128)(2,1)S(1)}, u32[]{:S(2)}, u32[]{:S(2)}) collective-permute-start(bf16[8,20,32,128]{3,2,1,0:T(8,128)(2,1)} %get-tuple-element.51.rest_1_), channel_id=1, source_target_pairs={{0,1},{1,0},{2,3},{3,2},{4,5},{5,4},{6,7},{7,6},{8,9},{9,8},{10,11... | collective-permute-start | bytes 3932168 | tf_op jit(solution)/shard_map/ppermute | solution.py:836
  42.6 20.5 %collective-permute-start.5 = (bf16[8,20,32,128]{3,2,1,0:T(8,128)(2,1)}, bf16[8,20,32,128]{3,2,1,0:T(8,128)(2,1)S(1)}, u32[]{:S(2)}, u32[]{:S(2)}) collective-permute-start(bf16[8,20,32,128]{3,2,1,0:T(8,128)(2,1)} %get-tuple-element.52.rest_3_), channel_id=1, source_target_pairs={{1,2},{2,1},{5,6},{6,5},{9,10},{10,9},{13,14},{14,13},{17,18},{18,... | collective-permute-start | bytes 3932168 | tf_op jit(solution)/shard_map/ppermute | solution.py:838
  43.3 30.9 %collective-permute-start.4 = (bf16[8,20,32,128]{3,2,1,0:T(8,128)(2,1)}, bf16[8,20,32,128]{3,2,1,0:T(8,128)(2,1)S(1)}, u32[]{:S(2)}, u32[]{:S(2)}) collective-permute-start(bf16[8,20,32,128]{3,2,1,0:T(8,128)(2,1)} %get-tuple-element.52.rest_3_), channel_id=1, source_target_pairs={{0,2},{3,1},{1,0},{2,3},{4,6},{7,5},{5,4},{6,7},{8,10},{11,9},{9,8... | collective-permute-start | bytes 3932168 | tf_op jit(solution)/shard_map/ppermute | solution.py:837
  50.1 29.8 %collective-permute-start.7 = (bf16[4,12,32,128]{3,2,1,0:T(8,128)(2,1)}, bf16[4,12,32,128]{3,2,1,0:T(8,128)(2,1)S(1)}, u32[]{:S(2)}, u32[]{:S(2)}) collective-permute-start(bf16[4,12,32,128]{3,2,1,0:T(8,128)(2,1)} %banded_products.8), channel_id=1, source_target_pairs={{0,8},{4,12},{8,0},{12,4},{1,9},{5,13},{9,1},{13,5},{2,10},{6,14},... | collective-permute-start | bytes 1179656 | tf_op jit(solution)/shard_map/ppermute | solution.py:881
  61.5 28.4 %collective-permute-start.6 = (bf16[4,12,32,128]{3,2,1,0:T(8,128)(2,1)}, bf16[4,12,32,128]{3,2,1,0:T(8,128)(2,1)S(1)}, u32[]{:S(2)}, u32[]{:S(2)}) collective-permute-start(bf16[4,12,32,128]{3,2,1,0:T(8,128)(2,1)} %get-tuple-element.54), channel_id=1, source_target_pairs={{0,4},{4,8},{8,12},{12,0},{1,5},{5,9},{9,13},{13,1},{2,6},{6,10},{... | collective-permute-start | bytes 1179656 | tf_op jit(solution)/shard_map/ppermute | solution.py:881
  61.6 28.3 %collective-permute-start.8 = (bf16[4,12,32,128]{3,2,1,0:T(8,128)(2,1)}, bf16[4,12,32,128]{3,2,1,0:T(8,128)(2,1)S(1)}, u32[]{:S(2)}, u32[]{:S(2)}) collective-permute-start(bf16[4,12,32,128]{3,2,1,0:T(8,128)(2,1)} %get-tuple-element.55), channel_id=1, source_target_pairs={{0,12},{4,0},{8,4},{12,8},{1,13},{5,1},{9,5},{13,9},{2,14},{6,2},{... | collective-permute-start | bytes 1179656 | tf_op jit(solution)/shard_map/ppermute | solution.py:881
  89.9 56.5 %copy-start.24 = (bf16[4,12,32,128]{3,2,1,0:T(8,128)(2,1)}, bf16[4,12,32,128]{3,2,1,0:T(8,128)(2,1)S(1)}, u32[]{:S(2)}) copy-start(bf16[4,12,32,128]{3,2,1,0:T(8,128)(2,1)S(1)} %collective-permute-done.6.rest_1_) | copy-start | bytes 1179652
  89.9 56.5 %copy-start.25 = (bf16[4,12,32,128]{3,2,1,0:T(8,128)(2,1)}, bf16[4,12,32,128]{3,2,1,0:T(8,128)(2,1)S(1)}, u32[]{:S(2)}) copy-start(bf16[4,12,32,128]{3,2,1,0:T(8,128)(2,1)S(1)} %collective-permute-done.8.rest_3_) | copy-start | bytes 1179652
  89.9 14.9 %collective-permute-start.11 = (bf16[4,20,32,128]{3,2,1,0:T(8,128)(2,1)}, bf16[4,20,32,128]{3,2,1,0:T(8,128)(2,1)S(1)}, u32[]{:S(2)}, u32[]{:S(2)}) collective-permute-start(bf16[4,20,32,128]{3,2,1,0:T(8,128)(2,1)} %get-tuple-element.61), channel_id=1, source_target_pairs={{0,12},{4,0},{8,4},{12,8},{1,13},{5,1},{9,5},{13,9},{2,14},{6,2},{... | collective-permute-start | bytes 1966088 | tf_op jit(solution)/shard_map/ppermute | solution.py:881
  90.0 31.0 %collective-permute-start.9 = (bf16[4,20,32,128]{3,2,1,0:T(8,128)(2,1)}, bf16[4,20,32,128]{3,2,1,0:T(8,128)(2,1)S(1)}, u32[]{:S(2)}, u32[]{:S(2)}) collective-permute-start(bf16[4,20,32,128]{3,2,1,0:T(8,128)(2,1)} %get-tuple-element.58), channel_id=1, source_target_pairs={{0,4},{4,8},{8,12},{12,0},{1,5},{5,9},{9,13},{13,1},{2,6},{6,10},{... | collective-permute-start | bytes 1966088 | tf_op jit(solution)/shard_map/ppermute | solution.py:881
  91.5 55.0 %collective-permute-start.10 = (bf16[4,20,32,128]{3,2,1,0:T(8,128)(2,1)S(1)}, bf16[4,20,32,128]{3,2,1,0:T(8,128)(2,1)S(1)}, u32[]{:S(2)}, u32[]{:S(2)}) collective-permute-start(bf16[4,20,32,128]{3,2,1,0:T(8,128)(2,1)S(1)} %copy-done.15), channel_id=1, source_target_pairs={{0,8},{4,12},{8,0},{12,4},{1,9},{5,13},{9,1},{13,5},{2,10},{6,14},... | collective-permute-start | bytes 1966088 | tf_op jit(solution)/shard_map/ppermute | solution.py:881
  104.9 41.6 %copy-start.12 = (bf16[4,20,32,128]{3,2,1,0:T(8,128)(2,1)}, bf16[4,20,32,128]{3,2,1,0:T(8,128)(2,1)S(1)}, u32[]{:S(2)}) copy-start(bf16[4,20,32,128]{3,2,1,0:T(8,128)(2,1)S(1)} %collective-permute-done.11.rest_7_) | copy-start | bytes 1966084
  174.3 23.0 %collective-permute-start.12 = (bf16[8,14,32,128]{3,2,1,0:T(8,128)(2,1)}, bf16[8,14,32,128]{3,2,1,0:T(8,128)(2,1)S(1)}, u32[]{:S(2)}, u32[]{:S(2)}) collective-permute-start(bf16[8,14,32,128]{3,2,1,0:T(8,128)(2,1)} %get-tuple-element.63.rest_0_), channel_id=1, source_target_pairs={{1,3},{2,0},{0,1},{3,2},{5,7},{6,4},{4,5},{7,6},{9,11},{10,8},{8,9... | collective-permute-start | bytes 2752520 | tf_op jit(solution)/shard_map/ppermute | solution.py:850
  176.6 31.9 %collective-permute-start.14 = (bf16[8,14,32,128]{3,2,1,0:T(8,128)(2,1)}, bf16[8,14,32,128]{3,2,1,0:T(8,128)(2,1)S(1)}, u32[]{:S(2)}, u32[]{:S(2)}) collective-permute-start(bf16[8,14,32,128]{3,2,1,0:T(8,128)(2,1)} %get-tuple-element.64.rest_3_), channel_id=1, source_target_pairs={{0,2},{2,0},{1,3},{3,1},{4,6},{6,4},{5,7},{7,5},{8,10},{10,8},{9,1... | collective-permute-start | bytes 2752520 | tf_op jit(solution)/shard_map/ppermute | solution.py:852
  197.3 41.2 %copy-start.6 = (bf16[8,14,32,128]{3,2,1,0:T(8,128)(2,1)}, bf16[8,14,32,128]{3,2,1,0:T(8,128)(2,1)S(1)}, u32[]{:S(2)}) copy-start(bf16[8,14,32,128]{3,2,1,0:T(8,128)(2,1)S(1)} %collective-permute-done.12.rest_1_) | copy-start | bytes 2752516
  197.3 11.2 %collective-permute-start.13 = (bf16[8,14,32,128]{3,2,1,0:T(8,128)(2,1)S(1)}, bf16[8,14,32,128]{3,2,1,0:T(8,128)(2,1)S(1)}, u32[]{:S(2)}, u32[]{:S(2)}) collective-permute-start(bf16[8,14,32,128]{3,2,1,0:T(8,128)(2,1)S(1)} %collective-permute-done.12.rest_1_), channel_id=1, source_target_pairs={{0,1},{3,2},{4,5},{7,6},{8,9},{11,10},{12,13},{15,14},{16,17},{19,... | collective-permute-start | bytes 2752520 | tf_op jit(solution)/shard_map/ppermute | solution.py:851
  208.5 30.0 %copy-start.8 = (bf16[8,14,32,128]{3,2,1,0:T(8,128)(2,1)}, bf16[8,14,32,128]{3,2,1,0:T(8,128)(2,1)S(1)}, u32[]{:S(2)}) copy-start(bf16[8,14,32,128]{3,2,1,0:T(8,128)(2,1)S(1)} %collective-permute-done.13.rest_2_) | copy-start | bytes 2752516
  208.5 25.4 %collective-permute-start.15 = (bf16[8,18,32,128]{3,2,1,0:T(8,128)(2,1)}, bf16[8,18,32,128]{3,2,1,0:T(8,128)(2,1)S(1)}, u32[]{:S(2)}, u32[]{:S(2)}) collective-permute-start(bf16[8,18,32,128]{3,2,1,0:T(8,128)(2,1)} %get-tuple-element.70.rest_0_), channel_id=1, source_target_pairs={{1,3},{2,0},{0,1},{3,2},{5,7},{6,4},{4,5},{7,6},{9,11},{10,8},{8,9... | collective-permute-start | bytes 3538952 | tf_op jit(solution)/shard_map/ppermute | solution.py:850
  208.6 48.0 %collective-permute-start.17 = (bf16[8,18,32,128]{3,2,1,0:T(8,128)(2,1)}, bf16[8,18,32,128]{3,2,1,0:T(8,128)(2,1)S(1)}, u32[]{:S(2)}, u32[]{:S(2)}) collective-permute-start(bf16[8,18,32,128]{3,2,1,0:T(8,128)(2,1)} %get-tuple-element.71.rest_3_), channel_id=1, source_target_pairs={{0,2},{2,0},{1,3},{3,1},{4,6},{6,4},{5,7},{7,5},{8,10},{10,8},{9,1... | collective-permute-start | bytes 3538952 | tf_op jit(solution)/shard_map/ppermute | solution.py:852
  233.9 22.6 %collective-permute-start.16 = (bf16[8,18,32,128]{3,2,1,0:T(8,128)(2,1)S(1)}, bf16[8,18,32,128]{3,2,1,0:T(8,128)(2,1)S(1)}, u32[]{:S(2)}, u32[]{:S(2)}) collective-permute-start(bf16[8,18,32,128]{3,2,1,0:T(8,128)(2,1)S(1)} %collective-permute-done.15.rest_1_), channel_id=1, source_target_pairs={{0,1},{3,2},{4,5},{7,6},{8,9},{11,10},{12,13},{15,14},{16,17},{19,... | collective-permute-start | bytes 3538952 | tf_op jit(solution)/shard_map/ppermute | solution.py:851
  243.0 21.2 %collective-permute-start.19 = (bf16[4,14,32,128]{3,2,1,0:T(8,128)(2,1)}, bf16[4,14,32,128]{3,2,1,0:T(8,128)(2,1)S(1)}, u32[]{:S(2)}, u32[]{:S(2)}) collective-permute-start(bf16[4,14,32,128]{3,2,1,0:T(8,128)(2,1)} %banded_products.12), channel_id=1, source_target_pairs={{0,8},{4,12},{8,0},{12,4},{1,9},{5,13},{9,1},{13,5},{2,10},{6,14},... | collective-permute-start | bytes 1376264 | tf_op jit(solution)/shard_map/ppermute | solution.py:881
  255.1 28.7 %collective-permute-start.18 = (bf16[4,14,32,128]{3,2,1,0:T(8,128)(2,1)}, bf16[4,14,32,128]{3,2,1,0:T(8,128)(2,1)S(1)}, u32[]{:S(2)}, u32[]{:S(2)}) collective-permute-start(bf16[4,14,32,128]{3,2,1,0:T(8,128)(2,1)} %get-tuple-element.73), channel_id=1, source_target_pairs={{0,4},{4,8},{8,12},{12,0},{1,5},{5,9},{9,13},{13,1},{2,6},{6,10},{... | collective-permute-start | bytes 1376264 | tf_op jit(solution)/shard_map/ppermute | solution.py:881
  255.1 30.9 %collective-permute-start.20 = (bf16[4,14,32,128]{3,2,1,0:T(8,128)(2,1)}, bf16[4,14,32,128]{3,2,1,0:T(8,128)(2,1)S(1)}, u32[]{:S(2)}, u32[]{:S(2)}) collective-permute-start(bf16[4,14,32,128]{3,2,1,0:T(8,128)(2,1)} %get-tuple-element.74), channel_id=1, source_target_pairs={{0,12},{4,0},{8,4},{12,8},{1,13},{5,1},{9,5},{13,9},{2,14},{6,2},{... | collective-permute-start | bytes 1376264 | tf_op jit(solution)/shard_map/ppermute | solution.py:881
  283.8 54.7 %copy-start.21 = (bf16[4,14,32,128]{3,2,1,0:T(8,128)(2,1)}, bf16[4,14,32,128]{3,2,1,0:T(8,128)(2,1)S(1)}, u32[]{:S(2)}) copy-start(bf16[4,14,32,128]{3,2,1,0:T(8,128)(2,1)S(1)} %collective-permute-done.18.rest_1_) | copy-start | bytes 1376260
  286.0 52.5 %copy-start.22 = (bf16[4,14,32,128]{3,2,1,0:T(8,128)(2,1)}, bf16[4,14,32,128]{3,2,1,0:T(8,128)(2,1)S(1)}, u32[]{:S(2)}) copy-start(bf16[4,14,32,128]{3,2,1,0:T(8,128)(2,1)S(1)} %collective-permute-done.20.rest_3_) | copy-start | bytes 1376260
  286.0 15.1 %collective-permute-start.23 = (bf16[4,18,32,128]{3,2,1,0:T(8,128)(2,1)}, bf16[4,18,32,128]{3,2,1,0:T(8,128)(2,1)S(1)}, u32[]{:S(2)}, u32[]{:S(2)}) collective-permute-start(bf16[4,18,32,128]{3,2,1,0:T(8,128)(2,1)} %get-tuple-element.80), channel_id=1, source_target_pairs={{0,12},{4,0},{8,4},{12,8},{1,13},{5,1},{9,5},{13,9},{2,14},{6,2},{... | collective-permute-start | bytes 1769480 | tf_op jit(solution)/shard_map/ppermute | solution.py:881
  287.3 26.6 %collective-permute-start.21 = (bf16[4,18,32,128]{3,2,1,0:T(8,128)(2,1)}, bf16[4,18,32,128]{3,2,1,0:T(8,128)(2,1)S(1)}, u32[]{:S(2)}, u32[]{:S(2)}) collective-permute-start(bf16[4,18,32,128]{3,2,1,0:T(8,128)(2,1)} %get-tuple-element.77), channel_id=1, source_target_pairs={{0,4},{4,8},{8,12},{12,0},{1,5},{5,9},{9,13},{13,1},{2,6},{6,10},{... | collective-permute-start | bytes 1769480 | tf_op jit(solution)/shard_map/ppermute | solution.py:881
  287.5 51.0 %collective-permute-start.22 = (bf16[4,18,32,128]{3,2,1,0:T(8,128)(2,1)S(1)}, bf16[4,18,32,128]{3,2,1,0:T(8,128)(2,1)S(1)}, u32[]{:S(2)}, u32[]{:S(2)}) collective-permute-start(bf16[4,18,32,128]{3,2,1,0:T(8,128)(2,1)S(1)} %copy-done.16), channel_id=1, source_target_pairs={{0,8},{4,12},{8,0},{12,4},{1,9},{5,13},{9,1},{13,5},{2,10},{6,14},... | collective-permute-start | bytes 1769480 | tf_op jit(solution)/shard_map/ppermute | solution.py:881
  301.2 37.4 %copy-start.17 = (bf16[4,18,32,128]{3,2,1,0:T(8,128)(2,1)}, bf16[4,18,32,128]{3,2,1,0:T(8,128)(2,1)S(1)}, u32[]{:S(2)}) copy-start(bf16[4,18,32,128]{3,2,1,0:T(8,128)(2,1)S(1)} %collective-permute-done.23.rest_7_) | copy-start | bytes 1769476
  (18 other events, 221.6 us)

commit v6 on v5

--- a/solution.py
+++ b/solution.py
@@ -414,19 +414,20 @@
     return lax.broadcasted_iota(jnp.int32, shape, 1) // size
 
 
-def spread_weights(w_ref, wide_ref, hidden, size):
-    parts = hidden // size
-    for side in range(2):
-        for kind in range(2):
-            start = (2 * side + kind) * hidden
-            weights = w_ref[0, :, start : start + hidden].astype(jnp.float32)
-            group = lane_group(weights.shape, size)
-            for part in range(parts):
-                kept = jnp.where(group == part, weights, 0.0)
-                at = ((side * parts + part) * 2 + kind) * hidden
-                for a in range(parts):
-                    moved = pltpu.roll(kept, ((a - part) % parts) * size, 1) if a != part else kept
-                    wide_ref[a * hidden : (a + 1) * hidden, at : at + hidden] = moved.astype(jnp.bfloat16)
+def exchange_groups(tiles, size):
+    tiles = list(tiles)
+    lanes = tiles[0].shape[1]
+    group = lane_group(tiles[0].shape, size)
+    distance = len(tiles) // 2
+    while distance:
+        low = lax.rem(group // distance, 2) == 0
+        for a in range(len(tiles)):
+            if not a & distance:
+                x, y = tiles[a], tiles[a + distance]
+                tiles[a] = jnp.where(low, x, pltpu.roll(y, distance * size, 1))
+                tiles[a + distance] = jnp.where(low, pltpu.roll(x, lanes - distance * size, 1), y)
+        distance //= 2
+    return tiles
 
 
 def swap_matrix(half):
@@ -449,19 +450,21 @@
             turned[y : y + half, x : x + half] = swapped(taken[x : x + half, y : y + half], swap_ref)
 
 
-def make_operand(side, taken, row_alive, inner_alive, wide_ref, out_refs, laid, swap_ref):
+def make_operand(side, taken, row_alive, inner_alive, w_ref, out_refs, laid, swap_ref):
     rows, size, hidden = taken.shape
     parts, bands, half = hidden // size, size, 16
     groups = rows // parts
-    stacked = jnp.concatenate(
-        [jnp.concatenate([taken[g * parts + a] for a in range(parts)], axis=1) for g in range(groups)], axis=0
-    )
-    mask = (row_alive[:, None, :] * inner_alive[None, :, :]).reshape(groups * size, hidden)
-    for part in range(parts):
-        at = (side * parts + part) * 2 * hidden
-        made = dot(stacked, wide_ref[:, at : at + 2 * hidden])
+    weights = w_ref[0, :, 2 * side * hidden : (2 * side + 2) * hidden]
+    step = 2 * parts
+    for start in range(0, rows, step):
+        made = dot(taken[start : start + step].reshape(step * size, hidden), weights)
+        mask = (row_alive[start : start + step, None, :] * inner_alive[None, :, :]).reshape(step * size, hidden)
         value = mask * sigmoid(made[:, hidden:]) * made[:, :hidden]
-        laid[side, :, part * size : (part + 1) * size, :] = value.astype(jnp.bfloat16).reshape(groups, size, hidden)
+        for first in range(0, step, parts):
+            tiles = [value[(first + a) * size : (first + a + 1) * size] for a in range(parts)]
+            for part, tile in enumerate(exchange_groups(tiles, size)):
+                at = slice(part * size, (part + 1) * size)
+                laid[side, (start + first) // parts, at, :] = tile.astype(jnp.bfloat16)
     blocks = [laid[side, g].T for g in range(groups)]
     starts = [sum(ref.shape[1] for ref in out_refs[:n]) for n in range(len(out_refs))]
     for first in range(0, bands, half):
@@ -477,35 +480,20 @@
                     ref[0, low - start : high - start, row : row + half] = moved[low - first : high - first]
 
 
-def alive_groups(chain_ref, start, rows, parts):
-    lanes = chain_ref.shape[1]
-    groups = rows // parts
-    line = chain_ref[pl.ds(start // lanes, 1), :] >= 0
-    row = lax.broadcasted_iota(jnp.int32, (groups, lanes), 1) - lax.rem(start, lanes)
-    group = lax.broadcasted_iota(jnp.int32, (groups, lanes), 0)
-    pick = jnp.logical_and(jnp.logical_and(row >= group * parts, row < (group + 1) * parts), line)
-    fold = lax.rem(lax.broadcasted_iota(jnp.int32, (lanes, lanes), 0), parts) == lane_group(
-        (lanes, lanes), lanes // parts
-    )
-    return dot(pick.astype(jnp.float32).astype(jnp.bfloat16), fold.astype(jnp.float32).astype(jnp.bfloat16))
-
-
-def open_layer(layer, natural, chain_ref, row_start, col_start, w_ref, left_refs, right_refs, wide, laid, turned, swap):
+def open_layer(layer, natural, chain_ref, row_start, col_start, w_ref, left_refs, right_refs, laid, turned, swap):
     rows, cols, hidden = natural.shape
-    parts = hidden // rows
     turn(natural, turned, swap)
-    row_mask = alive_groups(chain_ref, row_start, rows, parts), alive_rows(chain_ref, col_start, cols)
-    col_mask = alive_groups(chain_ref, col_start, cols, parts), alive_rows(chain_ref, row_start, rows)
+    row_alive, col_alive = alive_rows(chain_ref, row_start, rows), alive_rows(chain_ref, col_start, cols)
     for side, refs in ((0, left_refs), (1, right_refs)):
         if side == layer % 2:
-            make_operand(side, natural, *row_mask, wide, refs, laid, swap)
+            make_operand(side, natural, row_alive, col_alive, w_ref, refs, laid, swap)
         else:
-            make_operand(side, turned[...], *col_mask, wide, refs, laid, swap)
+            make_operand(side, turned[...], col_alive, row_alive, w_ref, refs, laid, swap)
 
 
 def open_kernel(hidden, chunks, n_chan, n_sub, ids, blocks, pair_ref, chain_ref, w_ref, gate_ref, *rest):
     left_refs, right_refs = rest[:chunks], rest[chunks : 2 * chunks]
-    norm_ref, wide, laid, turned, swap = rest[2 * chunks :]
+    norm_ref, laid, turned, swap = rest[2 * chunks :]
     slots = pl.num_programs(0)
     step = pl.program_id(0)
     _, rows, cols, channels = pair_ref.shape
@@ -513,7 +501,6 @@
 
     @pl.when(step == 0)
     def _():
-        spread_weights(w_ref, wide, hidden, cols)
         swap[...] = swap_matrix(16)
 
     group = hidden // cols
@@ -524,13 +511,12 @@
         gate_ref[0, at] = gate.reshape(group, cols, channels)
         norm_ref[at] = normed.reshape(group, cols, channels)
     row_start, col_start = (blocks[0, block] * n_chan + ids[1]) * rows, (blocks[1, block] * n_sub + ids[2]) * cols
-    open_layer(0, norm_ref[...], chain_ref, row_start, col_start, w_ref, left_refs, right_refs, wide, laid, turned, swap)
+    open_layer(0, norm_ref[...], chain_ref, row_start, col_start, w_ref, left_refs, right_refs, laid, turned, swap)
 
 
 def operand_scratch(rows, size, hidden):
     parts = hidden // size
     return [
-        pltpu.VMEM((parts * hidden, 4 * parts * hidden), jnp.bfloat16),
         pltpu.VMEM((2, rows // parts, parts * size, hidden), jnp.bfloat16),
         pltpu.VMEM((size, rows, hidden), jnp.bfloat16),
         pltpu.VMEM((256, 256), jnp.bfloat16),
@@ -561,74 +547,103 @@
     return out[0], out[1 : 1 + len(bands)], out[1 + len(bands) :]
 
 
-def banded_kernel(shifts, n_blk, slots_dev, terms, capacity, pieces, n_refs, size, ids, owners, slots, *rest):
+def plan_kernel(n_blk, slots_dev, terms, capacity, ids, owners, slots, chosen, place, seen):
+    for e in range(2 * n_blk * capacity):
+        chosen[e] = 0
+    for shift in range(n_blk):
+        seen[shift] = 0
+        target = lax.rem(ids[0] + shift, n_blk)
+
+        def scan(e, found):
+            block, term = target * slots_dev + e // terms, lax.rem(e, terms)
+            here = jnp.logical_and(owners[term, block] == ids[0], found < capacity)
+
+            @pl.when(here)
+            def _():
+                chosen[2 * (shift * capacity + found)] = slots[term, 0, block]
+                chosen[2 * (shift * capacity + found) + 1] = slots[term, 1, block]
+
+            return found + here.astype(jnp.int32)
+
+        lax.fori_loop(0, slots_dev * terms, scan, jnp.int32(0))
+
+    def own(e, carry):
+        owner = owners[lax.rem(e, terms), ids[0] * slots_dev + e // terms]
+        count = seen[owner]
+        seen[owner] = count + 1
+        place[e] = lax.rem(ids[0] - owner + n_blk, n_blk) * capacity + count
+        return carry
+
+    lax.fori_loop(0, slots_dev * terms, own, jnp.int32(0))
+
+
+def make_plan(ids, owners, slots, n_blk, slots_dev, terms, capacity):
+    scalars = pl.BlockSpec(memory_space=pltpu.SMEM)
+    return pl.pallas_call(
+        functools.partial(plan_kernel, n_blk, slots_dev, terms, capacity),
+        in_specs=[scalars] * 3,
+        out_specs=[scalars] * 2,
+        out_shape=[
+            jax.ShapeDtypeStruct((2 * n_blk * capacity,), jnp.int32),
+            jax.ShapeDtypeStruct((slots_dev * terms,), jnp.int32),
+        ],
+        scratch_shapes=[pltpu.SMEM((n_blk,), jnp.int32)],
+        name="make_plan",
+    )(ids, owners, slots)
+
+
+def banded_kernel(shifts, capacity, pieces, n_refs, size, ids, chosen, *rest):
     refs, rest = rest[:n_refs], rest[n_refs:]
-    out_refs, (left_held, right_held, chosen, sems) = rest[: len(shifts)], rest[len(shifts) :]
-    step = pl.program_id(0)
-    _, halves, bands, rows, hidden = left_held.shape
+    out_refs, (left_held, right_held, out_held, sems, out_sems) = rest[: len(shifts)], rest[len(shifts) :]
+    halves, _, bands, rows, hidden = left_held.shape
     parts = hidden // size
-    count = len(shifts) * capacity
-
-    def copy(n, term, source):
+
+    def copy(n, source):
         side, half, *_ = pieces[n]
-        held = (left_held, right_held)[side]
-        return pltpu.make_async_copy(refs[source].at[chosen[2 * term + side]], held.at[term, half], sems.at[term, n])
-
-    def start(term):
-        for n, (_, _, on, off) in enumerate(pieces):
-            if on == off:
-                copy(n, term, on).start()
-            else:
-
-                @pl.when(ids[3] == 1)
-                def _(n=n, on=on):
-                    copy(n, term, on).start()
-
-                @pl.when(ids[3] == 0)
-                def _(n=n, off=off):
-                    copy(n, term, off).start()
-
-    @pl.when(step == 0)
-    def _():
-        for e in range(2 * count):
-            chosen[e] = 0
-        for n, shift in enumerate(shifts):
-            target = lax.rem(ids[0] + shift, n_blk)
-
-            def scan(e, found):
-                block, term = target * slots_dev + e // terms, lax.rem(e, terms)
-                here = jnp.logical_and(owners[term, block] == ids[0], found < capacity)
-
-                @pl.when(here)
-                def _():
-                    chosen[2 * (n * capacity + found)] = slots[term, 0, block]
-                    chosen[2 * (n * capacity + found) + 1] = slots[term, 1, block]
-
-                return found + here.astype(jnp.int32)
-
-            lax.fori_loop(0, slots_dev * terms, scan, jnp.int32(0))
-        for term in range(count):
-            start(term)
+        return pltpu.make_async_copy(refs[source], (left_held, right_held)[side].at[half], sems.at[n])
+
+    for n, (_, _, on, off) in enumerate(pieces):
+        if on == off:
+            copy(n, on).start()
+        else:
+
+            @pl.when(ids[3] == 1)
+            def _(n=n, on=on):
+                copy(n, on).start()
+
+            @pl.when(ids[3] == 0)
+            def _(n=n, off=off):
+                copy(n, off).start()
 
     for n, piece in enumerate(pieces):
-        copy(n, step, piece[2]).wait()
-
-    for n, out_ref in enumerate(out_refs):
-
-        @pl.when(step // capacity == n)
-        def _(out_ref=out_ref):
+        copy(n, piece[2]).wait()
+
+    def leave(n):
+        return pltpu.make_async_copy(out_held.at[pl.ds(n * capacity, capacity)], out_refs[n], out_sems.at[n])
+
+    for n, shift in enumerate(shifts):
+
+        def one(term, carry, n=n, shift=shift):
+            at = 2 * (shift * capacity + term)
+            left_slot, right_slot = chosen[at], chosen[at + 1]
             group = lane_group((size, hidden), size)
             for band in range(bands):
-                left = jnp.concatenate([left_held[step, h, band] for h in range(halves)], axis=1)
+                left = jnp.concatenate([left_held[h, left_slot, band] for h in range(halves)], axis=1)
                 apart = []
                 for h in range(halves):
-                    right = right_held[step, h, band]
+                    right = right_held[h, right_slot, band]
                     apart += [jnp.where(group == part, right, jnp.zeros_like(right)) for part in range(parts)]
-                out_ref[0, band] = dot(left, jnp.concatenate(apart, axis=0)).astype(jnp.bfloat16)
-
-
-def banded_products(shifts, ids, owners, slots, lefts, rights, capacity, slots_dev, terms, size):
-    n_blk = lax.axis_size("blk")
+                made = dot(left, jnp.concatenate(apart, axis=0))
+                out_held[n * capacity + term, band] = made.astype(jnp.bfloat16)
+            return carry
+
+        lax.fori_loop(0, capacity, one, 0)
+        leave(n).start()
+    for n in range(len(shifts)):
+        leave(n).wait()
+
+
+def banded_products(shifts, ids, chosen, lefts, rights, capacity, size):
     refs, pieces = [], []
 
     def index_of(array):
@@ -641,28 +656,22 @@
     for side, operands in ((0, lefts), (1, rights)):
         for half, (on, off) in enumerate(operands):
             pieces.append((side, half, index_of(on), index_of(off)))
-    _, bands, rows, hidden = lefts[0][0].shape
+    slots, bands, rows, hidden = lefts[0][0].shape
     count = len(shifts) * capacity
-
-    def out_spec(n):
-        return pl.BlockSpec(
-            (1, bands, rows, hidden), lambda t, *_: (jnp.clip(t - n * capacity, 0, capacity - 1), 0, 0, 0)
-        )
-
+    anywhere = pl.BlockSpec(memory_space=pl.ANY)
     return pl.pallas_call(
-        functools.partial(
-            banded_kernel, shifts, n_blk, slots_dev, terms, capacity, tuple(pieces), len(refs), size
-        ),
+        functools.partial(banded_kernel, shifts, capacity, tuple(pieces), len(refs), size),
         grid_spec=pltpu.PrefetchScalarGridSpec(
-            num_scalar_prefetch=3,
-            grid=(count,),
-            in_specs=[pl.BlockSpec(memory_space=pl.ANY)] * len(refs),
-            out_specs=[out_spec(n) for n in range(len(shifts))],
+            num_scalar_prefetch=2,
+            grid=(),
+            in_specs=[anywhere] * len(refs),
+            out_specs=[anywhere] * len(shifts),
             scratch_shapes=[
-                pltpu.VMEM((count, len(lefts), bands, rows, hidden), jnp.bfloat16),
-                pltpu.VMEM((count, len(rights), bands, size, hidden), jnp.bfloat16),
-                pltpu.SMEM((2 * count,), jnp.int32),
-                pltpu.SemaphoreType.DMA((count, len(pieces))),
+                pltpu.VMEM((len(lefts), slots, bands, rows, hidden), jnp.bfloat16),
+                pltpu.VMEM((len(rights), slots, bands, size, hidden), jnp.bfloat16),
+                pltpu.VMEM((count, bands, rows, hidden), jnp.bfloat16),
+                pltpu.SemaphoreType.DMA((len(pieces),)),
+                pltpu.SemaphoreType.DMA((len(shifts),)),
             ],
         ),
         out_shape=[jax.ShapeDtypeStruct((capacity, bands, rows, hidden), jnp.bfloat16)] * len(shifts),
@@ -671,19 +680,19 @@
             flops=2 * count * bands * rows * hidden * hidden * len(lefts), bytes_accessed=1, transcendentals=0
         ),
         name="banded_products",
-    )(ids, owners, slots, *refs)
-
-
-def close_kernel(layer, last, n_parts, n_blk, n_chan, n_sub, slots_dev, terms, capacity, ids, blocks, owners, *rest):
+    )(ids, chosen, *refs)
+
+
+def close_kernel(layer, last, n_parts, n_blk, n_chan, n_sub, slots_dev, terms, capacity, ids, blocks, place, *rest):
     chunks = n_parts // n_blk
     arrived, rest = rest[:n_parts], rest[n_parts:]
     cur_ref, gate_ref, w_out_ref = rest[:3]
     if last:
-        out_ref, held, wide_out, place, seen, sems, swap = rest[3:]
+        out_ref, held, sems, swap = rest[3:]
     else:
         chain_ref, w_ref, out_ref, next_gate_ref = rest[3:7]
         left_refs, right_refs = rest[7 : 7 + chunks], rest[7 + chunks : 7 + 2 * chunks]
-        held, wide_out, place, seen, sems, norm_ref, wide, laid, turned, swap = rest[7 + 2 * chunks :]
+        held, sems, norm_ref, laid, turned, swap = rest[7 + 2 * chunks :]
     step = pl.program_id(0)
     _, rows, cols, channels = cur_ref.shape
     _, bands, _, hidden = held.shape
@@ -699,28 +708,7 @@
     def _():
         for n in range(n_parts):
             arrival(n).start()
-        for shift in range(n_blk):
-            seen[shift] = 0
-
-        def scan(e, carry):
-            owner = owners[lax.rem(e, terms), ids[0] * slots_dev + e // terms]
-            shift = lax.rem(ids[0] - owner + n_blk, n_blk)
-            count = seen[owner]
-            seen[owner] = count + 1
-            place[e] = shift * capacity + count
-            return carry
-
-        lax.fori_loop(0, slots_dev * terms, scan, jnp.int32(0))
-        wide_out[...] = jnp.zeros_like(wide_out)
-        for part in range(parts):
-            for a in range(parts):
-                at = (part * parts + a) * bands
-                wide_out[at : at + bands, a * channels : (a + 1) * channels] = w_out_ref[
-                    0, part * bands : (part + 1) * bands, :
-                ]
         swap[...] = swap_matrix(16)
-        if not last:
-            spread_weights(w_ref, wide, hidden, rows)
         for n in range(n_parts):
             arrival(n).wait()
 
@@ -735,28 +723,13 @@
             moved = swapped(total.astype(jnp.bfloat16), swap)
             for r in range(half):
                 by_row[row + r].append(moved[r])
-    groups = rows // parts
-    pieces = []
-    for g in range(groups):
+    for g in range(rows // parts):
         block = jnp.concatenate([x for a in range(parts) for x in by_row[g * parts + a]]).T
-        pieces.append(jnp.concatenate([block[p * cols : (p + 1) * cols] for p in range(parts)], axis=1))
-    mixture = jnp.concatenate(pieces)
-    together = (lane_group((hidden, hidden), size) == lax.broadcasted_iota(jnp.int32, (hidden, hidden), 0) // size)
-    together = together.astype(jnp.float32).astype(jnp.bfloat16)
-    average = dot(mixture, jnp.concatenate([together] * parts)) * (1.0 / hidden)
-    centred = [mixture[:, p * hidden : (p + 1) * hidden].astype(jnp.float32) - average for p in range(parts)]
-    squares = sum(c * c for c in centred)
-    high = squares.astype(jnp.bfloat16)
-    low = (squares - high.astype(jnp.float32)).astype(jnp.bfloat16)
-    variance = dot(jnp.concatenate([high, low], axis=1), jnp.concatenate([together] * 2)) * (1.0 / hidden)
-    scale = lax.rsqrt(variance + norm_epsilon)
-    normed = jnp.concatenate([(c * scale).astype(jnp.bfloat16) for c in centred], axis=1)
-    update = dot(normed, wide_out[...])
-    for g in range(groups):
+        block = block.astype(jnp.float32)
+        tiles = [block[p * cols : (p + 1) * cols] for p in range(parts)]
+        mixture = jnp.concatenate(exchange_groups(tiles, size))
+        change = dot(layer_norm(mixture).astype(jnp.bfloat16), w_out_ref[0])
         taken = pl.ds(g * parts, parts)
-        change = jnp.concatenate(
-            [update[g * cols : (g + 1) * cols, a * channels : (a + 1) * channels] for a in range(parts)]
-        )
         gate = gate_ref[0, taken].reshape(parts * cols, channels)
         current = cur_ref[0, taken].astype(jnp.float32).reshape(parts * cols, channels)
         result = (current + gate * change).astype(jnp.bfloat16)
@@ -769,12 +742,10 @@
     if not last:
         block = ids[0] * slots_dev + step
         starts = (blocks[0, block] * n_chan + ids[1]) * rows, (blocks[1, block] * n_sub + ids[2]) * cols
-        open_layer(
-            layer + 1, norm_ref[...], chain_ref, *starts, w_ref, left_refs, right_refs, wide, laid, turned, swap
-        )
-
-
-def close_layer(layer, arrived, ids, blocks, owners, current, gate, w_out, capacity, terms, chains, w_in, last, bands):
+        open_layer(layer + 1, norm_ref[...], chain_ref, *starts, w_ref, left_refs, right_refs, laid, turned, swap)
+
+
+def close_layer(layer, arrived, ids, blocks, place, current, gate, w_out, capacity, terms, chains, w_in, last, bands):
     n_blk = len(arrived[0])
     flat = [part for chunk in arrived for part in chunk]
     slots, rows, cols, channels = current.shape
@@ -790,9 +761,6 @@
     out_specs = [whole]
     scratch = [
         pltpu.VMEM((n_blk * capacity, sum(bands[layer]), rows, hidden), jnp.bfloat16),
-        pltpu.VMEM((hidden // cols * hidden, hidden // cols * channels), jnp.bfloat16),
-        pltpu.SMEM((slots * terms,), jnp.int32),
-        pltpu.SMEM((n_blk,), jnp.int32),
         pltpu.SemaphoreType.DMA((len(flat),)),
     ]
     if not last:
@@ -815,7 +783,7 @@
         out_shape=out_shape,
         compiler_params=pltpu.CompilerParams(vmem_limit_bytes=vmem_limit),
         name="close_layer",
-    )(ids, blocks, owners, *operands)
+    )(ids, blocks, place, *operands)
     if last:
         return out[0]
     return out[0], out[1], out[2 : 2 + len(bands)], out[2 + len(bands) :]
@@ -825,65 +793,57 @@
     return lax.optimization_barrier((value, *others))[0]
 
 
-def exchange_bands_outgoing(lefts, rights):
+def exchange_bands_outgoing(left, right, before):
     both = ("chan", "sub")
-    made = []
-    for left, right in zip(lefts, rights):
-        if made:
-            (before, _), _ = made[-1][0]
-            (one, _), (_, two) = made[-1][1]
-            left, right = lax.optimization_barrier((left, right, before, one, two))[:2]
-        other_left = lax.ppermute(left, "sub", [(0, 1), (1, 0)])
-        one = lax.ppermute(right, both, [(0, 2), (3, 1), (1, 0), (2, 3)])
-        two = lax.ppermute(right, both, [(1, 2), (2, 1)])
-        made.append(([(other_left, left), (left, other_left)], [(one, one), (right, two)]))
-    return made
-
-
-def exchange_bands_incoming(lefts, rights):
+    if before:
+        ((other, _), _), ((one, _), (_, two)) = before[0]
+        left, right = lax.optimization_barrier((left, right, other, one, two))[:2]
+    other = lax.ppermute(left, "sub", [(0, 1), (1, 0)])
+    one = lax.ppermute(right, both, [(0, 2), (3, 1), (1, 0), (2, 3)])
+    two = lax.ppermute(right, both, [(1, 2), (2, 1)])
+    return [(other, left), (left, other)], [(one, one), (right, two)]
+
+
+def exchange_bands_incoming(left, right, before):
     both = ("chan", "sub")
-    made = []
-    for left, right in zip(lefts, rights):
-        if made:
-            before, other = made[-1][0][1][1], made[-1][1][1][0]
-            left, right = lax.optimization_barrier((left, right, before, other))[:2]
-        one = lax.ppermute(left, both, [(1, 3), (2, 0), (0, 1), (3, 2)])
-        two = lax.ppermute(one, both, [(0, 1), (3, 2)])
-        other = lax.ppermute(right, "chan", [(0, 1), (1, 0)])
-        made.append(([(left, one), (one, two)], [(right, right), (other, other)]))
-    return made
+    if before:
+        (_, (_, two)), (_, (other, _)) = before[0]
+        left, right = lax.optimization_barrier((left, right, two, other))[:2]
+    one = lax.ppermute(left, both, [(1, 3), (2, 0), (0, 1), (3, 2)])
+    other = lax.ppermute(right, "chan", [(0, 1), (1, 0)])
+    two = lax.ppermute(after(one, before[1]) if before else one, both, [(0, 1), (3, 2)])
+    return [(left, one), (one, two)], [(right, right), (other, other)]
 
 
 def banded(pair, ids, blocks, owners, slot_of, chains, w_in, w_out, capacity, terms, n_blk):
     slots, rows, cols, channels = pair.shape
     hidden = w_out.shape[1]
     far = n_blk // 2
-    calls = [[far], [s for s in range(1, n_blk) if s != far] + [0]]
+    shifts = [far] + [s for s in range(1, n_blk) if s != far] + [0]
     layers = w_in.shape[0]
     current = pair
     bands = [[12, 20], [14, 18]]
+    chosen, place = make_plan(ids, owners, slot_of, n_blk, slots, terms, capacity)
     for layer in range(layers):
         if layer == 0:
             gate, lefts, rights = open_operands(ids, blocks, pair, chains, w_in, hidden, bands[0])
         exchange = exchange_bands_incoming if layer % 2 else exchange_bands_outgoing
-        arrived, last_made = [], None
-        for left, right in exchange(lefts, rights):
+        arrived, before = [], None
+        for left, right in zip(lefts, rights):
+            operands = exchange(left, right, before)
+            made = banded_products(shifts, ids, chosen, *operands, capacity, cols)
             parts = [None] * n_blk
-            for shifts in calls:
-                if last_made is not None:
-                    ids = after(ids, last_made)
-                made = banded_products(shifts, ids, owners, slot_of, left, right, capacity, slots, terms, cols)
-                last_made = made[-1]
-                for shift, part in zip(shifts, made):
-                    if shift:
-                        if arrived:
-                            part = after(part, arrived[-1][shift])
-                        part = lax.ppermute(part, "blk", [(p, (p + shift) % n_blk) for p in range(n_blk)])
-                    parts[shift] = part
+            for shift, part in zip(shifts, made):
+                if shift:
+                    if arrived:
+                        part = after(part, arrived[-1][shift])
+                    part = lax.ppermute(part, "blk", [(p, (p + shift) % n_blk) for p in range(n_blk)])
+                parts[shift] = part
             arrived.append(parts)
+            before = operands, parts[far]
         last = layer == layers - 1
         out = close_layer(
-            layer, arrived, ids, blocks, owners, current, gate, w_out, capacity, terms, chains, w_in, last, bands
+            layer, arrived, ids, blocks, place, current, gate, w_out, capacity, terms, chains, w_in, last, bands
         )
         if last:
             return out

time: 355 us -> 347 us (0.977)
  Pallas kernels: 115 us -> 104 us
  waiting for transfers between devices: 192 us -> 201 us
  starting transfers between devices: 39.3 us -> 34.7 us
    ppermute x12, waiting for transfers between devices: 112 us -> 137 us  [banded(): lax.ppermute(part, 'blk', [(p, (p + shift) % n_blk) for p in range(n_blk)])]
    ppermute x2, waiting for transfers between devices: 43.3 us -> 19.3 us  [exchange_bands_incoming(): one = lax.ppermute(left, both, [(1, 3), (2, 0), (0, 1), (3, 2)])]
    pallas_call x8 -> x5, Pallas kernels: 55.7 us -> 35.6 us  [the longest x4 32.8 us: banded_products(): pl.pallas_call(functools.partial(banded_kernel, shifts, capacity, tuple(p...]
    pallas_call x2, Pallas kernels: 40 us -> 49.3 us  [close_layer(): pl.pallas_call(functools.partial(close_kernel, layer, last, len(flat), n_...]
    ppermute x2, waiting for transfers between devices: 8.19 us -> 12.6 us  [exchange_bands_incoming(): other = lax.ppermute(right, 'chan', [(0, 1), (1, 0)])]
  transfers between devices with their start and end apart: 24 -> 24, of which waited for: 14 -> 15; matrix products, arithmetic and copies ran while one was open for 0% -> 0% of each run, Pallas kernels for 16% -> 10%
where the time goes in v6:
time: 347 us; the launch traced here: 345 us
  waiting for transfers between devices  201 us (58%)
  Pallas kernels  104 us (30%)
  starting transfers between devices  34.7 us (10%)
  local copies, waits for them, and re-layouts  4.95 us (1%)
    ppermute x12, waiting for transfers between devices, banded(): lax.ppermute(part, 'blk', [(p, (p + shift) % n_blk) for p in range(n_blk)])  137 us
    pallas_call x2, Pallas kernels, close_layer(): pl.pallas_call(functools.partial(close_kernel, layer, last, len(flat), n_...  49.3 us
    pallas_call x4, Pallas kernels, banded_products(): pl.pallas_call(functools.partial(banded_kernel, shifts, capacity, tuple(p...  32.8 us
    ppermute x2, waiting for transfers between devices, exchange_bands_outgoing(): one = lax.ppermute(right, both, [(0, 2), (3, 1), (1, 0), (2, 3)])  31.4 us
    ppermute x2, waiting for transfers between devices, exchange_bands_incoming(): one = lax.ppermute(left, both, [(1, 3), (2, 0), (0, 1), (3, 2)])  19.3 us
    pallas_call x1, Pallas kernels, open_operands(): pl.pallas_call(functools.partial(open_kernel, hidden, len(bands), lax.axi...  18.7 us
    ppermute x12, starting transfers between devices, banded(): lax.ppermute(part, 'blk', [(p, (p + shift) % n_blk) for p in range(n_blk)])  15.9 us
    ppermute x2, waiting for transfers between devices, exchange_bands_incoming(): other = lax.ppermute(right, 'chan', [(0, 1), (1, 0)])  12.6 us
  transfers between devices with their start and end apart: 24, of which 15 were waited for; matrix products, arithmetic and copies ran while one was open for 0% of the time, Pallas kernels for 10%

profile of v6, /device:TPU:11, one launch (start us, length us, event | category | flops | bytes accessed | tf_op | source)
XLA Modules:
  0.0 344.9 jit_solution(7121447144749751135)
XLA Ops:
  0.7 18.7 %open_operands.1 = (f32[8,32,32,128]{3,2,1,0:T(8,128)}, bf16[8,12,32,128]{3,2,1,0:T(8,128)(2,1)}, bf16[8,20,32,128]{3,2,1,0:T(8,128)(2,1)}, bf16[8,12,32,128]{3,2,1,0:T(8,128)(2,1)}, bf16[8,20,32,128]{3,2,1,0:T(8,128)(2,1)}) custom-call(s32[4]{0:T(128)} %pad_add_fusion.ids, s32[2,32]{1,0:T(2,128)} %bitcast.10, bf16[8,32,32,128]{3,2,1,0:T(8,128)(2,1)} %rest_8_.1, ...), custom_call_target="tpu_custom_call" | custom-call | tf_op jit(solution)/shard_map/open_operands/pallas_call | solution.py:529
  20.8 2.6 collective-permute-start.1
  23.4 17.1 %collective-permute-done.1.rest_2_ = bf16[8,12,32,128]{3,2,1,0:T(8,128)(2,1)S(1)} collective-permute-done((bf16[8,12,32,128]{3,2,1,0:T(8,128)(2,1)}, bf16[8,12,32,128]{3,2,1,0:T(8,128)(2,1)S(1)}, u32[]{:S(2)}, u32[]{:S(2)}) %collective-permute-start.1) | collective-permute-done | bytes 786464 | tf_op jit(solution)/shard_map/ppermute | solution.py:802
  40.4 1.6 collective-permute-start.6
  42.8 3.4 collective-permute-start.7
  46.2 2.8 make_plan.1
  49.1 7.3 %banded_products.4 = (bf16[4,12,32,128]{3,2,1,0:T(8,128)(2,1)}, bf16[4,12,32,128]{3,2,1,0:T(8,128)(2,1)}, bf16[4,12,32,128]{3,2,1,0:T(8,128)(2,1)}, bf16[4,12,32,128]{3,2,1,0:T(8,128)(2,1)}) custom-call(s32[4]{0:T(128)} %pad_add_fusion.ids, s32[32]{0:T(128)} %get-tuple-element.46.chosen, bf16[8,12,32,128]{3,2,1,0:T(8,128)(2,1)} %copy-done.9, ...), custom_call_target="tpu_custom_call" | custom-call | flops 402653184 | bytes 1 | tf_op jit(solution)/shard_map/banded_products/pallas_call | solution.py:662
  60.1 14.4 %collective-permute-done.7.rest_2_ = bf16[8,20,32,128]{3,2,1,0:T(8,128)(2,1)} collective-permute-done((bf16[8,20,32,128]{3,2,1,0:T(8,128)(2,1)}, bf16[8,20,32,128]{3,2,1,0:T(8,128)(2,1)}, u32[]{:S(2)}, u32[]{:S(2)}) %collective-permute-start.7) | collective-permute-done | bytes 1310752 | tf_op jit(solution)/shard_map/ppermute | solution.py:802
  74.5 9.1 %banded_products.5 = (bf16[4,20,32,128]{3,2,1,0:T(8,128)(2,1)}, bf16[4,20,32,128]{3,2,1,0:T(8,128)(2,1)}, bf16[4,20,32,128]{3,2,1,0:T(8,128)(2,1)}, bf16[4,20,32,128]{3,2,1,0:T(8,128)(2,1)}) custom-call(s32[4]{0:T(128)} %pad_add_fusion.ids, s32[32]{0:T(128)} %get-tuple-element.46.chosen, bf16[8,20,32,128]{3,2,1,0:T(8,128)(2,1)} %copy-done, ...), custom_call_target="tpu_custom_call" | custom-call | flops 671088640 | bytes 1 | tf_op jit(solution)/shard_map/banded_products/pallas_call | solution.py:662
  83.7 8.3 %collective-permute-done.4.rest_2_ = bf16[4,12,32,128]{3,2,1,0:T(8,128)(2,1)S(1)} collective-permute-done((bf16[4,12,32,128]{3,2,1,0:T(8,128)(2,1)}, bf16[4,12,32,128]{3,2,1,0:T(8,128)(2,1)S(1)}, u32[]{:S(2)}, u32[]{:S(2)}) %collective-permute-start.4) | collective-permute-done | bytes 393248 | tf_op jit(solution)/shard_map/ppermute | solution.py:840
  94.8 2.3 collective-permute-start.9
  97.1 12.4 %collective-permute-done.11.rest_7_ = bf16[4,20,32,128]{3,2,1,0:T(8,128)(2,1)S(1)} collective-permute-done((bf16[4,20,32,128]{3,2,1,0:T(8,128)(2,1)}, bf16[4,20,32,128]{3,2,1,0:T(8,128)(2,1)S(1)}, u32[]{:S(2)}, u32[]{:S(2)}) %collective-permute-start.11) | collective-permute-done | bytes 655392 | tf_op jit(solution)/shard_map/ppermute | solution.py:840
  109.5 27.5 %collective-permute-done.10.rest_6_ = bf16[4,20,32,128]{3,2,1,0:T(8,128)(2,1)S(1)} collective-permute-done((bf16[4,20,32,128]{3,2,1,0:T(8,128)(2,1)}, bf16[4,20,32,128]{3,2,1,0:T(8,128)(2,1)S(1)}, u32[]{:S(2)}, u32[]{:S(2)}) %collective-permute-start.10) | collective-permute-done | bytes 655392 | tf_op jit(solution)/shard_map/ppermute | solution.py:840
  137.0 14.0 %collective-permute-done.9.rest_5_ = bf16[4,20,32,128]{3,2,1,0:T(8,128)(2,1)S(1)} collective-permute-done((bf16[4,20,32,128]{3,2,1,0:T(8,128)(2,1)}, bf16[4,20,32,128]{3,2,1,0:T(8,128)(2,1)S(1)}, u32[]{:S(2)}, u32[]{:S(2)}) %collective-permute-start.9) | collective-permute-done | bytes 655392 | tf_op jit(solution)/shard_map/ppermute | solution.py:840
  151.9 34.0 %close_layer.2 = (bf16[8,32,32,128]{3,2,1,0:T(8,128)(2,1)}, f32[8,32,32,128]{3,2,1,0:T(8,128)}, bf16[8,14,32,128]{3,2,1,0:T(8,128)(2,1)}, bf16[8,18,32,128]{3,2,...) custom-call(s32[4]{0:T(128)} %pad_add_fusion.ids, s32[2,32]{1,0:T(2,128)} %bitcast.11, ...), custom_call_target="tpu_custom_call" | custom-call | tf_op jit(solution)/shard_map/close_layer/pallas_call | solution.py:776
  187.3 19.3 %collective-permute-done.12.rest_1_ = bf16[8,14,32,128]{3,2,1,0:T(8,128)(2,1)S(1)} collective-permute-done((bf16[8,14,32,128]{3,2,1,0:T(8,128)(2,1)}, bf16[8,14,32,128]{3,2,1,0:T(8,128)(2,1)S(1)}, u32[]{:S(2)}, u32[]{:S(2)}) %collective-permute-start.12) | collective-permute-done | bytes 917536 | tf_op jit(solution)/shard_map/ppermute | solution.py:812
  206.6 3.4 collective-permute-start.13
  210.0 7.9 %collective-permute-done.14.rest_4_ = bf16[8,14,32,128]{3,2,1,0:T(8,128)(2,1)S(1)} collective-permute-done((bf16[8,14,32,128]{3,2,1,0:T(8,128)(2,1)}, bf16[8,14,32,128]{3,2,1,0:T(8,128)(2,1)S(1)}, u32[]{:S(2)}, u32[]{:S(2)}) %collective-permute-start.14) | collective-permute-done | bytes 917536 | tf_op jit(solution)/shard_map/ppermute | solution.py:813
  219.2 7.7 %banded_products.6 = (bf16[4,14,32,128]{3,2,1,0:T(8,128)(2,1)}, bf16[4,14,32,128]{3,2,1,0:T(8,128)(2,1)}, bf16[4,14,32,128]{3,2,1,0:T(8,128)(2,1)}, bf16[4,14,32,128]{3,2,1,0:T(8,128)(2,1)}) custom-call(s32[4]{0:T(128)} %pad_add_fusion.ids, s32[32]{0:T(128)} %get-tuple-element.46.chosen, bf16[8,14,32,128]{3,2,1,0:T(8,128)(2,1)} %get-tuple-element.65.rest_0_, ...), custom_call_target="tpu_custom_call" | custom-call | flops 469762048 | bytes 1 | tf_op jit(solution)/shard_map/banded_products/pallas_call | solution.py:662
  227.3 18.7 %collective-permute-done.16.rest_2_ = bf16[4,14,32,128]{3,2,1,0:T(8,128)(2,1)S(1)} collective-permute-done((bf16[4,14,32,128]{3,2,1,0:T(8,128)(2,1)}, bf16[4,14,32,128]{3,2,1,0:T(8,128)(2,1)S(1)}, u32[]{:S(2)}, u32[]{:S(2)}) %collective-permute-start.16) | collective-permute-done | bytes 458784 | tf_op jit(solution)/shard_map/ppermute | solution.py:840
  246.1 3.8 %collective-permute-start.19 = (bf16[8,18,32,128]{3,2,1,0:T(8,128)(2,1)S(1)}, bf16[8,18,32,128]{3,2,1,0:T(8,128)(2,1)S(1)}, u32[]{:S(2)}, u32[]{:S(2)}) collective-permute-start(bf16[8,18,32,128]{3,2,1,0:T(8,128)(2,1)S(1)} %collective-permute-done.18.rest_1_), channel_id=1, source_target_pairs={{0,1},{3,2},{4,5},{7,6},{8,9},{11,10},{12,13},{15,14},{16,17},{19,... | collective-permute-start | bytes 3538952 | tf_op jit(solution)/shard_map/ppermute | solution.py:814
  249.8 2.4 collective-permute-start.15
  252.3 1.9 collective-permute-start.17
  254.1 4.7 %collective-permute-done.20.rest_4_ = bf16[8,18,32,128]{3,2,1,0:T(8,128)(2,1)S(1)} collective-permute-done((bf16[8,18,32,128]{3,2,1,0:T(8,128)(2,1)S(1)}, bf16[8,18,32,128]{3,2,1,0:T(8,128)(2,1)S(1)}, u32[]{:S(2)}, u32[]{:S(2)}) %collective-permute-start.20) | collective-permute-done | bytes 1179680 | tf_op jit(solution)/shard_map/ppermute | solution.py:813
  260.9 8.7 %banded_products.7 = (bf16[4,18,32,128]{3,2,1,0:T(8,128)(2,1)}, bf16[4,18,32,128]{3,2,1,0:T(8,128)(2,1)}, bf16[4,18,32,128]{3,2,1,0:T(8,128)(2,1)}, bf16[4,18,32,128]{3,2,1,0:T(8,128)(2,1)}) custom-call(s32[4]{0:T(128)} %pad_add_fusion.ids, s32[32]{0:T(128)} %get-tuple-element.46.chosen, bf16[8,18,32,128]{3,2,1,0:T(8,128)(2,1)} %get-tuple-element.73.rest_0_, ...), custom_call_target="tpu_custom_call" | custom-call | flops 603979776 | bytes 1 | tf_op jit(solution)/shard_map/banded_products/pallas_call | solution.py:662
  269.6 5.1 %collective-permute-done.17.rest_3_ = bf16[4,14,32,128]{3,2,1,0:T(8,128)(2,1)S(1)} collective-permute-done((bf16[4,14,32,128]{3,2,1,0:T(8,128)(2,1)}, bf16[4,14,32,128]{3,2,1,0:T(8,128)(2,1)S(1)}, u32[]{:S(2)}, u32[]{:S(2)}) %collective-permute-start.17) | collective-permute-done | bytes 458784 | tf_op jit(solution)/shard_map/ppermute | solution.py:840
  274.8 1.5 collective-permute-start.23
  276.3 2.1 collective-permute-start.22
  278.8 11.9 %collective-permute-done.23.rest_7_ = bf16[4,18,32,128]{3,2,1,0:T(8,128)(2,1)S(1)} collective-permute-done((bf16[4,18,32,128]{3,2,1,0:T(8,128)(2,1)}, bf16[4,18,32,128]{3,2,1,0:T(8,128)(2,1)S(1)}, u32[]{:S(2)}, u32[]{:S(2)}) %collective-permute-start.23) | collective-permute-done | bytes 589856 | tf_op jit(solution)/shard_map/ppermute | solution.py:840
  290.7 25.3 %collective-permute-done.22.rest_6_ = bf16[4,18,32,128]{3,2,1,0:T(8,128)(2,1)S(1)} collective-permute-done((bf16[4,18,32,128]{3,2,1,0:T(8,128)(2,1)}, bf16[4,18,32,128]{3,2,1,0:T(8,128)(2,1)S(1)}, u32[]{:S(2)}, u32[]{:S(2)}) %collective-permute-start.22) | collective-permute-done | bytes 589856 | tf_op jit(solution)/shard_map/ppermute | solution.py:840
  316.1 12.6 %collective-permute-done.21.rest_5_ = bf16[4,18,32,128]{3,2,1,0:T(8,128)(2,1)S(1)} collective-permute-done((bf16[4,18,32,128]{3,2,1,0:T(8,128)(2,1)}, bf16[4,18,32,128]{3,2,1,0:T(8,128)(2,1)S(1)}, u32[]{:S(2)}, u32[]{:S(2)}) %collective-permute-start.21) | collective-permute-done | bytes 589856 | tf_op jit(solution)/shard_map/ppermute | solution.py:840
  329.5 15.4 %close_layer.3 = bf16[8,32,32,128]{3,2,1,0:T(8,128)(2,1)} custom-call(s32[4]{0:T(128)} %pad_add_fusion.ids, s32[2,32]{1,0:T(2,128)} %bitcast.12, s32[16]{0:T(128)} %get-tuple-element.45.place, bf16[4,14,32,128]{3,2,1,0:T(8,128)(2,1)} %get-tuple-element.67.rest_0_, bf16[4,14,32,128]{3,2,1,0:T(8,128)(2,1)} %copy-done.19, bf16[4,14,32,128]{3,2,1,0:T(8,128)(2,1)} %copy-done.18, ...), custom_call_target="tpu_custom_call" | custom-call | tf_op jit(solution)/shard_map/close_layer/pallas_call | solution.py:776
  (73 shorter events, 16.9 us)
Async XLA Ops:
  19.4 4.0 %collective-permute-start = (bf16[8,12,32,128]{3,2,1,0:T(8,128)(2,1)}, bf16[8,12,32,128]{3,2,1,0:T(8,128)(2,1)S(1)}, u32[]{:S(2)}, u32[]{:S(2)}) collective-permute-start(bf16[8,12,32,128]{3,2,1,0:T(8,128)(2,1)} %get-tuple-element.47.rest_1_), channel_id=1, source_target_pairs={{0,1},{1,0},{2,3},{3,2},{4,5},{5,4},{6,7},{7,6},{8,9},{9,8},{10,11... | collective-permute-start | bytes 2359304 | tf_op jit(solution)/shard_map/ppermute | solution.py:801
  20.1 3.3 collective-permute-start.2
  20.8 19.7 %collective-permute-start.1 = (bf16[8,12,32,128]{3,2,1,0:T(8,128)(2,1)}, bf16[8,12,32,128]{3,2,1,0:T(8,128)(2,1)S(1)}, u32[]{:S(2)}, u32[]{:S(2)}) collective-permute-start(bf16[8,12,32,128]{3,2,1,0:T(8,128)(2,1)} %get-tuple-element.48.rest_3_), channel_id=1, source_target_pairs={{0,2},{3,1},{1,0},{2,3},{4,6},{7,5},{5,4},{6,7},{8,10},{11,9},{9,8... | collective-permute-start | bytes 2359304 | tf_op jit(solution)/shard_map/ppermute | solution.py:802
  40.4 18.3 %collective-permute-start.6 = (bf16[8,20,32,128]{3,2,1,0:T(8,128)(2,1)}, bf16[8,20,32,128]{3,2,1,0:T(8,128)(2,1)S(1)}, u32[]{:S(2)}, u32[]{:S(2)}) collective-permute-start(bf16[8,20,32,128]{3,2,1,0:T(8,128)(2,1)} %get-tuple-element.55.rest_1_), channel_id=1, source_target_pairs={{0,1},{1,0},{2,3},{3,2},{4,5},{5,4},{6,7},{7,6},{8,9},{9,8},{10,11... | collective-permute-start | bytes 3932168 | tf_op jit(solution)/shard_map/ppermute | solution.py:801
  42.0 18.1 %collective-permute-start.8 = (bf16[8,20,32,128]{3,2,1,0:T(8,128)(2,1)}, bf16[8,20,32,128]{3,2,1,0:T(8,128)(2,1)S(1)}, u32[]{:S(2)}, u32[]{:S(2)}) collective-permute-start(bf16[8,20,32,128]{3,2,1,0:T(8,128)(2,1)} %get-tuple-element.56.rest_3_), channel_id=1, source_target_pairs={{1,2},{2,1},{5,6},{6,5},{9,10},{10,9},{13,14},{14,13},{17,18},{18,... | collective-permute-start | bytes 3932168 | tf_op jit(solution)/shard_map/ppermute | solution.py:803
  42.8 31.7 %collective-permute-start.7 = (bf16[8,20,32,128]{3,2,1,0:T(8,128)(2,1)}, bf16[8,20,32,128]{3,2,1,0:T(8,128)(2,1)}, u32[]{:S(2)}, u32[]{:S(2)}) collective-permute-start(bf16[8,20,32,128]{3,2,1,0:T(8,128)(2,1)} %get-tuple-element.56.rest_3_), channel_id=1, source_target_pairs={{0,2},{3,1},{1,0},{2,3},{4,6},{7,5},{5,4},{6,7},{8,10},{11,9},{9,8... | collective-permute-start | bytes 3932168 | tf_op jit(solution)/shard_map/ppermute | solution.py:802
  56.3 27.3 %collective-permute-start.3 = (bf16[4,12,32,128]{3,2,1,0:T(8,128)(2,1)}, bf16[4,12,32,128]{3,2,1,0:T(8,128)(2,1)S(1)}, u32[]{:S(2)}, u32[]{:S(2)}) collective-permute-start(bf16[4,12,32,128]{3,2,1,0:T(8,128)(2,1)} %get-tuple-element.50), channel_id=1, source_target_pairs={{0,4},{4,8},{8,12},{12,0},{1,5},{5,9},{9,13},{13,1},{2,6},{6,10},{... | collective-permute-start | bytes 1179656 | tf_op jit(solution)/shard_map/ppermute | solution.py:840
  57.7 34.3 %collective-permute-start.4 = (bf16[4,12,32,128]{3,2,1,0:T(8,128)(2,1)}, bf16[4,12,32,128]{3,2,1,0:T(8,128)(2,1)S(1)}, u32[]{:S(2)}, u32[]{:S(2)}) collective-permute-start(bf16[4,12,32,128]{3,2,1,0:T(8,128)(2,1)} %get-tuple-element.51), channel_id=1, source_target_pairs={{0,8},{4,12},{8,0},{12,4},{1,9},{5,13},{9,1},{13,5},{2,10},{6,14},... | collective-permute-start | bytes 1179656 | tf_op jit(solution)/shard_map/ppermute | solution.py:840
  58.8 34.6 %collective-permute-start.5 = (bf16[4,12,32,128]{3,2,1,0:T(8,128)(2,1)}, bf16[4,12,32,128]{3,2,1,0:T(8,128)(2,1)S(1)}, u32[]{:S(2)}, u32[]{:S(2)}) collective-permute-start(bf16[4,12,32,128]{3,2,1,0:T(8,128)(2,1)} %get-tuple-element.52), channel_id=1, source_target_pairs={{0,12},{4,0},{8,4},{12,8},{1,13},{5,1},{9,5},{13,9},{2,14},{6,2},{... | collective-permute-start | bytes 1179656 | tf_op jit(solution)/shard_map/ppermute | solution.py:840
  83.7 67.4 %copy-start.21 = (bf16[4,12,32,128]{3,2,1,0:T(8,128)(2,1)}, bf16[4,12,32,128]{3,2,1,0:T(8,128)(2,1)S(1)}, u32[]{:S(2)}) copy-start(bf16[4,12,32,128]{3,2,1,0:T(8,128)(2,1)S(1)} %collective-permute-done.3.rest_1_) | copy-start | bytes 1179652
  91.9 59.1 %copy-start.22 = (bf16[4,12,32,128]{3,2,1,0:T(8,128)(2,1)}, bf16[4,12,32,128]{3,2,1,0:T(8,128)(2,1)S(1)}, u32[]{:S(2)}) copy-start(bf16[4,12,32,128]{3,2,1,0:T(8,128)(2,1)S(1)} %collective-permute-done.4.rest_2_) | copy-start | bytes 1179652
  93.4 57.7 %copy-start.23 = (bf16[4,12,32,128]{3,2,1,0:T(8,128)(2,1)}, bf16[4,12,32,128]{3,2,1,0:T(8,128)(2,1)S(1)}, u32[]{:S(2)}) copy-start(bf16[4,12,32,128]{3,2,1,0:T(8,128)(2,1)S(1)} %collective-permute-done.5.rest_3_) | copy-start | bytes 1179652
  93.4 16.1 %collective-permute-start.11 = (bf16[4,20,32,128]{3,2,1,0:T(8,128)(2,1)}, bf16[4,20,32,128]{3,2,1,0:T(8,128)(2,1)S(1)}, u32[]{:S(2)}, u32[]{:S(2)}) collective-permute-start(bf16[4,20,32,128]{3,2,1,0:T(8,128)(2,1)} %get-tuple-element.63), channel_id=1, source_target_pairs={{0,12},{4,0},{8,4},{12,8},{1,13},{5,1},{9,5},{13,9},{2,14},{6,2},{... | collective-permute-start | bytes 1966088 | tf_op jit(solution)/shard_map/ppermute | solution.py:840
  93.4 43.6 %collective-permute-start.10 = (bf16[4,20,32,128]{3,2,1,0:T(8,128)(2,1)}, bf16[4,20,32,128]{3,2,1,0:T(8,128)(2,1)S(1)}, u32[]{:S(2)}, u32[]{:S(2)}) collective-permute-start(bf16[4,20,32,128]{3,2,1,0:T(8,128)(2,1)} %get-tuple-element.61), channel_id=1, source_target_pairs={{0,8},{4,12},{8,0},{12,4},{1,9},{5,13},{9,1},{13,5},{2,10},{6,14},... | collective-permute-start | bytes 1966088 | tf_op jit(solution)/shard_map/ppermute | solution.py:840
  94.8 56.2 %collective-permute-start.9 = (bf16[4,20,32,128]{3,2,1,0:T(8,128)(2,1)}, bf16[4,20,32,128]{3,2,1,0:T(8,128)(2,1)S(1)}, u32[]{:S(2)}, u32[]{:S(2)}) collective-permute-start(bf16[4,20,32,128]{3,2,1,0:T(8,128)(2,1)} %get-tuple-element.59), channel_id=1, source_target_pairs={{0,4},{4,8},{8,12},{12,0},{1,5},{5,9},{9,13},{13,1},{2,6},{6,10},{... | collective-permute-start | bytes 1966088 | tf_op jit(solution)/shard_map/ppermute | solution.py:840
  109.5 41.5 %copy-start.12 = (bf16[4,20,32,128]{3,2,1,0:T(8,128)(2,1)}, bf16[4,20,32,128]{3,2,1,0:T(8,128)(2,1)S(1)}, u32[]{:S(2)}) copy-start(bf16[4,20,32,128]{3,2,1,0:T(8,128)(2,1)S(1)} %collective-permute-done.11.rest_7_) | copy-start | bytes 1966084
  185.8 20.8 %collective-permute-start.12 = (bf16[8,14,32,128]{3,2,1,0:T(8,128)(2,1)}, bf16[8,14,32,128]{3,2,1,0:T(8,128)(2,1)S(1)}, u32[]{:S(2)}, u32[]{:S(2)}) collective-permute-start(bf16[8,14,32,128]{3,2,1,0:T(8,128)(2,1)} %get-tuple-element.65.rest_0_), channel_id=1, source_target_pairs={{1,3},{2,0},{0,1},{3,2},{5,7},{6,4},{4,5},{7,6},{9,11},{10,8},{8,9... | collective-permute-start | bytes 2752520 | tf_op jit(solution)/shard_map/ppermute | solution.py:812
  187.1 30.9 %collective-permute-start.14 = (bf16[8,14,32,128]{3,2,1,0:T(8,128)(2,1)}, bf16[8,14,32,128]{3,2,1,0:T(8,128)(2,1)S(1)}, u32[]{:S(2)}, u32[]{:S(2)}) collective-permute-start(bf16[8,14,32,128]{3,2,1,0:T(8,128)(2,1)} %get-tuple-element.66.rest_3_), channel_id=1, source_target_pairs={{0,2},{2,0},{1,3},{3,1},{4,6},{6,4},{5,7},{7,5},{8,10},{10,8},{9,1... | collective-permute-start | bytes 2752520 | tf_op jit(solution)/shard_map/ppermute | solution.py:813
  206.6 11.4 %collective-permute-start.13 = (bf16[8,14,32,128]{3,2,1,0:T(8,128)(2,1)S(1)}, bf16[8,14,32,128]{3,2,1,0:T(8,128)(2,1)S(1)}, u32[]{:S(2)}, u32[]{:S(2)}) collective-permute-start(bf16[8,14,32,128]{3,2,1,0:T(8,128)(2,1)S(1)} %collective-permute-done.12.rest_1_), channel_id=1, source_target_pairs={{0,1},{3,2},{4,5},{7,6},{8,9},{11,10},{12,13},{15,14},{16,17},{19,... | collective-permute-start | bytes 2752520 | tf_op jit(solution)/shard_map/ppermute | solution.py:814
  218.0 28.1 %collective-permute-start.18 = (bf16[8,18,32,128]{3,2,1,0:T(8,128)(2,1)}, bf16[8,18,32,128]{3,2,1,0:T(8,128)(2,1)S(1)}, u32[]{:S(2)}, u32[]{:S(2)}) collective-permute-start(bf16[8,18,32,128]{3,2,1,0:T(8,128)(2,1)} %get-tuple-element.73.rest_0_), channel_id=1, source_target_pairs={{1,3},{2,0},{0,1},{3,2},{5,7},{6,4},{4,5},{7,6},{9,11},{10,8},{8,9... | collective-permute-start | bytes 3538952 | tf_op jit(solution)/shard_map/ppermute | solution.py:812
  226.9 19.1 %collective-permute-start.16 = (bf16[4,14,32,128]{3,2,1,0:T(8,128)(2,1)}, bf16[4,14,32,128]{3,2,1,0:T(8,128)(2,1)S(1)}, u32[]{:S(2)}, u32[]{:S(2)}) collective-permute-start(bf16[4,14,32,128]{3,2,1,0:T(8,128)(2,1)} %get-tuple-element.69), channel_id=1, source_target_pairs={{0,8},{4,12},{8,0},{12,4},{1,9},{5,13},{9,1},{13,5},{2,10},{6,14},... | collective-permute-start | bytes 1376264 | tf_op jit(solution)/shard_map/ppermute | solution.py:840
  227.0 31.8 %collective-permute-start.20 = (bf16[8,18,32,128]{3,2,1,0:T(8,128)(2,1)S(1)}, bf16[8,18,32,128]{3,2,1,0:T(8,128)(2,1)S(1)}, u32[]{:S(2)}, u32[]{:S(2)}) collective-permute-start(bf16[8,18,32,128]{3,2,1,0:T(8,128)(2,1)S(1)} %copy-done.2), channel_id=1, source_target_pairs={{0,2},{2,0},{1,3},{3,1},{4,6},{6,4},{5,7},{7,5},{8,10},{10,8},{9,1... | collective-permute-start | bytes 3538952 | tf_op jit(solution)/shard_map/ppermute | solution.py:813
  246.1 82.7 %copy-start.18 = (bf16[4,14,32,128]{3,2,1,0:T(8,128)(2,1)}, bf16[4,14,32,128]{3,2,1,0:T(8,128)(2,1)S(1)}, u32[]{:S(2)}) copy-start(bf16[4,14,32,128]{3,2,1,0:T(8,128)(2,1)S(1)} %collective-permute-done.16.rest_2_) | copy-start | bytes 1376260
  246.1 12.8 %collective-permute-start.19 = (bf16[8,18,32,128]{3,2,1,0:T(8,128)(2,1)S(1)}, bf16[8,18,32,128]{3,2,1,0:T(8,128)(2,1)S(1)}, u32[]{:S(2)}, u32[]{:S(2)}) collective-permute-start(bf16[8,18,32,128]{3,2,1,0:T(8,128)(2,1)S(1)} %collective-permute-done.18.rest_1_), channel_id=1, source_target_pairs={{0,1},{3,2},{4,5},{7,6},{8,9},{11,10},{12,13},{15,14},{16,17},{19,... | collective-permute-start | bytes 3538952 | tf_op jit(solution)/shard_map/ppermute | solution.py:814
  249.8 19.8 %collective-permute-start.15 = (bf16[4,14,32,128]{3,2,1,0:T(8,128)(2,1)}, bf16[4,14,32,128]{3,2,1,0:T(8,128)(2,1)S(1)}, u32[]{:S(2)}, u32[]{:S(2)}) collective-permute-start(bf16[4,14,32,128]{3,2,1,0:T(8,128)(2,1)} %get-tuple-element.68), channel_id=1, source_target_pairs={{0,4},{4,8},{8,12},{12,0},{1,5},{5,9},{9,13},{13,1},{2,6},{6,10},{... | collective-permute-start | bytes 1376264 | tf_op jit(solution)/shard_map/ppermute | solution.py:840
  252.3 22.5 %collective-permute-start.17 = (bf16[4,14,32,128]{3,2,1,0:T(8,128)(2,1)}, bf16[4,14,32,128]{3,2,1,0:T(8,128)(2,1)S(1)}, u32[]{:S(2)}, u32[]{:S(2)}) collective-permute-start(bf16[4,14,32,128]{3,2,1,0:T(8,128)(2,1)} %get-tuple-element.70), channel_id=1, source_target_pairs={{0,12},{4,0},{8,4},{12,8},{1,13},{5,1},{9,5},{13,9},{2,14},{6,2},{... | collective-permute-start | bytes 1376264 | tf_op jit(solution)/shard_map/ppermute | solution.py:840
  269.6 59.1 %copy-start.19 = (bf16[4,14,32,128]{3,2,1,0:T(8,128)(2,1)}, bf16[4,14,32,128]{3,2,1,0:T(8,128)(2,1)S(1)}, u32[]{:S(2)}) copy-start(bf16[4,14,32,128]{3,2,1,0:T(8,128)(2,1)S(1)} %collective-permute-done.15.rest_1_) | copy-start | bytes 1376260
  274.8 53.9 %copy-start.20 = (bf16[4,14,32,128]{3,2,1,0:T(8,128)(2,1)}, bf16[4,14,32,128]{3,2,1,0:T(8,128)(2,1)S(1)}, u32[]{:S(2)}) copy-start(bf16[4,14,32,128]{3,2,1,0:T(8,128)(2,1)S(1)} %collective-permute-done.17.rest_3_) | copy-start | bytes 1376260
  274.8 15.9 %collective-permute-start.23 = (bf16[4,18,32,128]{3,2,1,0:T(8,128)(2,1)}, bf16[4,18,32,128]{3,2,1,0:T(8,128)(2,1)S(1)}, u32[]{:S(2)}, u32[]{:S(2)}) collective-permute-start(bf16[4,18,32,128]{3,2,1,0:T(8,128)(2,1)} %get-tuple-element.82), channel_id=1, source_target_pairs={{0,12},{4,0},{8,4},{12,8},{1,13},{5,1},{9,5},{13,9},{2,14},{6,2},{... | collective-permute-start | bytes 1769480 | tf_op jit(solution)/shard_map/ppermute | solution.py:840
  276.3 39.8 %collective-permute-start.22 = (bf16[4,18,32,128]{3,2,1,0:T(8,128)(2,1)}, bf16[4,18,32,128]{3,2,1,0:T(8,128)(2,1)S(1)}, u32[]{:S(2)}, u32[]{:S(2)}) collective-permute-start(bf16[4,18,32,128]{3,2,1,0:T(8,128)(2,1)} %get-tuple-element.80), channel_id=1, source_target_pairs={{0,8},{4,12},{8,0},{12,4},{1,9},{5,13},{9,1},{13,5},{2,10},{6,14},... | collective-permute-start | bytes 1769480 | tf_op jit(solution)/shard_map/ppermute | solution.py:840
  278.3 50.4 %collective-permute-start.21 = (bf16[4,18,32,128]{3,2,1,0:T(8,128)(2,1)}, bf16[4,18,32,128]{3,2,1,0:T(8,128)(2,1)S(1)}, u32[]{:S(2)}, u32[]{:S(2)}) collective-permute-start(bf16[4,18,32,128]{3,2,1,0:T(8,128)(2,1)} %get-tuple-element.78), channel_id=1, source_target_pairs={{0,4},{4,8},{8,12},{12,0},{1,5},{5,9},{9,13},{13,1},{2,6},{6,10},{... | collective-permute-start | bytes 1769480 | tf_op jit(solution)/shard_map/ppermute | solution.py:840
  290.7 38.0 %copy-start.15 = (bf16[4,18,32,128]{3,2,1,0:T(8,128)(2,1)}, bf16[4,18,32,128]{3,2,1,0:T(8,128)(2,1)S(1)}, u32[]{:S(2)}) copy-start(bf16[4,18,32,128]{3,2,1,0:T(8,128)(2,1)S(1)} %collective-permute-done.23.rest_7_) | copy-start | bytes 1769476
  (16 other events, 140.3 us)

commit v7 on v6

--- a/solution.py
+++ b/solution.py
@@ -414,20 +414,19 @@
     return lax.broadcasted_iota(jnp.int32, shape, 1) // size
 
 
-def exchange_groups(tiles, size):
-    tiles = list(tiles)
-    lanes = tiles[0].shape[1]
-    group = lane_group(tiles[0].shape, size)
-    distance = len(tiles) // 2
-    while distance:
-        low = lax.rem(group // distance, 2) == 0
-        for a in range(len(tiles)):
-            if not a & distance:
-                x, y = tiles[a], tiles[a + distance]
-                tiles[a] = jnp.where(low, x, pltpu.roll(y, distance * size, 1))
-                tiles[a + distance] = jnp.where(low, pltpu.roll(x, lanes - distance * size, 1), y)
-        distance //= 2
-    return tiles
+def spread_weights(w_ref, wide_ref, hidden, size):
+    parts = hidden // size
+    for side in range(2):
+        for kind in range(2):
+            start = (2 * side + kind) * hidden
+            weights = w_ref[0, :, start : start + hidden].astype(jnp.float32)
+            group = lane_group(weights.shape, size)
+            for part in range(parts):
+                kept = jnp.where(group == part, weights, 0.0)
+                at = ((side * parts + part) * 2 + kind) * hidden
+                for a in range(parts):
+                    moved = pltpu.roll(kept, ((a - part) % parts) * size, 1) if a != part else kept
+                    wide_ref[a * hidden : (a + 1) * hidden, at : at + hidden] = moved.astype(jnp.bfloat16)
 
 
 def swap_matrix(half):
@@ -450,21 +449,19 @@
             turned[y : y + half, x : x + half] = swapped(taken[x : x + half, y : y + half], swap_ref)
 
 
-def make_operand(side, taken, row_alive, inner_alive, w_ref, out_refs, laid, swap_ref):
+def make_operand(side, taken, row_alive, inner_alive, wide_ref, out_refs, laid, swap_ref):
     rows, size, hidden = taken.shape
     parts, bands, half = hidden // size, size, 16
     groups = rows // parts
-    weights = w_ref[0, :, 2 * side * hidden : (2 * side + 2) * hidden]
-    step = 2 * parts
-    for start in range(0, rows, step):
-        made = dot(taken[start : start + step].reshape(step * size, hidden), weights)
-        mask = (row_alive[start : start + step, None, :] * inner_alive[None, :, :]).reshape(step * size, hidden)
+    stacked = jnp.concatenate(
+        [jnp.concatenate([taken[g * parts + a] for a in range(parts)], axis=1) for g in range(groups)], axis=0
+    )
+    mask = (row_alive[:, None, :] * inner_alive[None, :, :]).reshape(groups * size, hidden)
+    for part in range(parts):
+        at = (side * parts + part) * 2 * hidden
+        made = dot(stacked, wide_ref[:, at : at + 2 * hidden])
         value = mask * sigmoid(made[:, hidden:]) * made[:, :hidden]
-        for first in range(0, step, parts):
-            tiles = [value[(first + a) * size : (first + a + 1) * size] for a in range(parts)]
-            for part, tile in enumerate(exchange_groups(tiles, size)):
-                at = slice(part * size, (part + 1) * size)
-                laid[side, (start + first) // parts, at, :] = tile.astype(jnp.bfloat16)
+        laid[side, :, part * size : (part + 1) * size, :] = value.astype(jnp.bfloat16).reshape(groups, size, hidden)
     blocks = [laid[side, g].T for g in range(groups)]
     starts = [sum(ref.shape[1] for ref in out_refs[:n]) for n in range(len(out_refs))]
     for first in range(0, bands, half):
@@ -480,27 +477,41 @@
                     ref[0, low - start : high - start, row : row + half] = moved[low - first : high - first]
 
 
-def open_layer(layer, natural, chain_ref, row_start, col_start, w_ref, left_refs, right_refs, laid, turned, swap):
+def alive_groups(chain_ref, start, rows, parts):
+    lanes = chain_ref.shape[1]
+    groups = rows // parts
+    line = chain_ref[pl.ds(start // lanes, 1), :] >= 0
+    row = lax.broadcasted_iota(jnp.int32, (groups, lanes), 1) - lax.rem(start, lanes)
+    group = lax.broadcasted_iota(jnp.int32, (groups, lanes), 0)
+    pick = jnp.logical_and(jnp.logical_and(row >= group * parts, row < (group + 1) * parts), line)
+    fold = lax.rem(lax.broadcasted_iota(jnp.int32, (lanes, lanes), 0), parts) == lane_group(
+        (lanes, lanes), lanes // parts
+    )
+    return dot(pick.astype(jnp.float32).astype(jnp.bfloat16), fold.astype(jnp.float32).astype(jnp.bfloat16))
+
+
+def open_layer(layer, natural, chain_ref, row_start, col_start, w_ref, left_refs, right_refs, wide, laid, turned, swap):
     rows, cols, hidden = natural.shape
+    parts = hidden // rows
     turn(natural, turned, swap)
-    row_alive, col_alive = alive_rows(chain_ref, row_start, rows), alive_rows(chain_ref, col_start, cols)
+    row_mask = alive_groups(chain_ref, row_start, rows, parts), alive_rows(chain_ref, col_start, cols)
+    col_mask = alive_groups(chain_ref, col_start, cols, parts), alive_rows(chain_ref, row_start, rows)
     for side, refs in ((0, left_refs), (1, right_refs)):
         if side == layer % 2:
-            make_operand(side, natural, row_alive, col_alive, w_ref, refs, laid, swap)
+            make_operand(side, natural, *row_mask, wide, refs, laid, swap)
         else:
-            make_operand(side, turned[...], col_alive, row_alive, w_ref, refs, laid, swap)
-
-
-def open_kernel(hidden, chunks, n_chan, n_sub, ids, blocks, pair_ref, chain_ref, w_ref, gate_ref, *rest):
-    left_refs, right_refs = rest[:chunks], rest[chunks : 2 * chunks]
-    norm_ref, laid, turned, swap = rest[2 * chunks :]
-    slots = pl.num_programs(0)
+            make_operand(side, turned[...], *col_mask, wide, refs, laid, swap)
+
+
+def open_kernel(hidden, chunks, n_chan, n_sub, base, of, ids, blocks, pair_ref, chain_ref, w_ref, *rest):
+    gate_ref, *operand_refs, norm_ref, wide, laid, turned, swap = rest[-(2 * chunks + 6) :]
     step = pl.program_id(0)
     _, rows, cols, channels = pair_ref.shape
-    block = ids[0] * slots + step
+    block = ids[0] * of + base + step
 
     @pl.when(step == 0)
     def _():
+        spread_weights(w_ref, wide, hidden, cols)
         swap[...] = swap_matrix(16)
 
     group = hidden // cols
@@ -510,71 +521,86 @@
         gate = sigmoid(dot(normed, w_ref[0, :, 4 * hidden :]))
         gate_ref[0, at] = gate.reshape(group, cols, channels)
         norm_ref[at] = normed.reshape(group, cols, channels)
-    row_start, col_start = (blocks[0, block] * n_chan + ids[1]) * rows, (blocks[1, block] * n_sub + ids[2]) * cols
-    open_layer(0, norm_ref[...], chain_ref, row_start, col_start, w_ref, left_refs, right_refs, laid, turned, swap)
+    starts = (blocks[0, block] * n_chan + ids[1]) * rows, (blocks[1, block] * n_sub + ids[2]) * cols
+    lefts, rights = operand_refs[:chunks], operand_refs[chunks:]
+    open_layer(0, norm_ref[...], chain_ref, *starts, w_ref, lefts, rights, wide, laid, turned, swap)
 
 
 def operand_scratch(rows, size, hidden):
     parts = hidden // size
     return [
+        pltpu.VMEM((parts * hidden, 4 * parts * hidden), jnp.bfloat16),
         pltpu.VMEM((2, rows // parts, parts * size, hidden), jnp.bfloat16),
         pltpu.VMEM((size, rows, hidden), jnp.bfloat16),
         pltpu.VMEM((256, 256), jnp.bfloat16),
     ]
 
 
-def open_operands(ids, blocks, pair, chains, w_in, hidden, bands):
+def operand_outputs(slots, count, rows, hidden, bands):
+    kept = [count if n == 0 else slots for n in range(len(bands))] * 2
+    return [jax.ShapeDtypeStruct((k, b, rows, hidden), jnp.bfloat16) for k, b in zip(kept, bands * 2)]
+
+
+def slot_specs(arrays, slots, base):
+    def spec(array):
+        offset = base if array.shape[0] == slots else 0
+        return pl.BlockSpec((1,) + array.shape[1:], lambda s, *_: (s + offset, 0, 0, 0))
+
+    return [spec(a) for a in arrays]
+
+
+def fill(out_shape, earlier, slots, n_before):
+    if earlier is None:
+        return [], [], {}
+    shared = [n for n, o in enumerate(out_shape) if o.shape[0] == slots]
+    specs = [pl.BlockSpec(memory_space=pl.ANY)] * len(shared)
+    return [earlier[n] for n in shared], specs, {n_before + k: n for k, n in enumerate(shared)}
+
+
+def open_operands(ids, blocks, pair, chains, w_in, hidden, bands, base, count, earlier):
     slots, rows, cols, channels = pair.shape
-    operands = [jax.ShapeDtypeStruct((slots, count, rows, hidden), jnp.bfloat16) for count in bands] * 2
-    out = pl.pallas_call(
-        functools.partial(open_kernel, hidden, len(bands), lax.axis_size("chan"), lax.axis_size("sub")),
+    out_shape = [jax.ShapeDtypeStruct(pair.shape, jnp.float32)] + operand_outputs(slots, count, rows, hidden, bands)
+    more, more_specs, aliases = fill(out_shape, earlier, slots, 5)
+    return pl.pallas_call(
+        functools.partial(open_kernel, hidden, len(bands), lax.axis_size("chan"), lax.axis_size("sub"), base, slots),
         grid_spec=pltpu.PrefetchScalarGridSpec(
             num_scalar_prefetch=2,
-            grid=(slots,),
-            in_specs=[
-                pl.BlockSpec((1, rows, cols, channels), lambda s, *_: (s, 0, 0, 0)),
+            grid=(count,),
+            in_specs=slot_specs([pair], slots, base)
+            + [
                 pl.BlockSpec(chains.shape, lambda s, *_: (0, 0)),
                 pl.BlockSpec((1,) + w_in.shape[1:], lambda s, *_: (0, 0, 0)),
-            ],
-            out_specs=[pl.BlockSpec((1, rows, cols, channels), lambda s, *_: (s, 0, 0, 0))]
-            + [pl.BlockSpec((1,) + o.shape[1:], lambda s, *_: (s, 0, 0, 0)) for o in operands],
+            ]
+            + more_specs,
+            out_specs=slot_specs(out_shape, slots, base),
             scratch_shapes=[pltpu.VMEM((rows, cols, channels), jnp.bfloat16)] + operand_scratch(rows, cols, hidden),
         ),
-        out_shape=[jax.ShapeDtypeStruct(pair.shape, jnp.float32)] + operands,
+        out_shape=out_shape,
+        input_output_aliases=aliases,
         compiler_params=pltpu.CompilerParams(vmem_limit_bytes=vmem_limit),
+        cost_estimate=pl.CostEstimate(flops=1 << 33, bytes_accessed=1 << 20, transcendentals=0),
         name="open_operands",
-    )(ids, blocks, pair, chains, w_in)
-    return out[0], out[1 : 1 + len(bands)], out[1 + len(bands) :]
+    )(ids, blocks, pair, chains, w_in, *more)
 
 
 def plan_kernel(n_blk, slots_dev, terms, capacity, ids, owners, slots, chosen, place, seen):
-    for e in range(2 * n_blk * capacity):
-        chosen[e] = 0
     for shift in range(n_blk):
         seen[shift] = 0
         target = lax.rem(ids[0] + shift, n_blk)
-
-        def scan(e, found):
-            block, term = target * slots_dev + e // terms, lax.rem(e, terms)
-            here = jnp.logical_and(owners[term, block] == ids[0], found < capacity)
-
-            @pl.when(here)
-            def _():
-                chosen[2 * (shift * capacity + found)] = slots[term, 0, block]
-                chosen[2 * (shift * capacity + found) + 1] = slots[term, 1, block]
-
-            return found + here.astype(jnp.int32)
-
-        lax.fori_loop(0, slots_dev * terms, scan, jnp.int32(0))
-
-    def own(e, carry):
-        owner = owners[lax.rem(e, terms), ids[0] * slots_dev + e // terms]
+        for e in range(2 * (capacity + 1)):
+            chosen[2 * shift * (capacity + 1) + e] = 0
+        found = jnp.int32(0)
+        for e in range(slots_dev * terms):
+            block, term = target * slots_dev + e // terms, e % terms
+            at = 2 * (shift * (capacity + 1) + jnp.minimum(found, capacity))
+            chosen[at] = slots[term, 0, block]
+            chosen[at + 1] = slots[term, 1, block]
+            found = found + (owners[term, block] == ids[0]).astype(jnp.int32)
+    for e in range(slots_dev * terms):
+        owner = owners[e % terms, ids[0] * slots_dev + e // terms]
         count = seen[owner]
         seen[owner] = count + 1
         place[e] = lax.rem(ids[0] - owner + n_blk, n_blk) * capacity + count
-        return carry
-
-    lax.fori_loop(0, slots_dev * terms, own, jnp.int32(0))
 
 
 def make_plan(ids, owners, slots, n_blk, slots_dev, terms, capacity):
@@ -584,7 +610,7 @@
         in_specs=[scalars] * 3,
         out_specs=[scalars] * 2,
         out_shape=[
-            jax.ShapeDtypeStruct((2 * n_blk * capacity,), jnp.int32),
+            jax.ShapeDtypeStruct((2 * n_blk * (capacity + 1),), jnp.int32),
             jax.ShapeDtypeStruct((slots_dev * terms,), jnp.int32),
         ],
         scratch_shapes=[pltpu.SMEM((n_blk,), jnp.int32)],
@@ -599,10 +625,11 @@
     parts = hidden // size
 
     def copy(n, source):
-        side, half, *_ = pieces[n]
-        return pltpu.make_async_copy(refs[source], (left_held, right_held)[side].at[half], sems.at[n])
-
-    for n, (_, _, on, off) in enumerate(pieces):
+        side, half, base, *_ = pieces[n]
+        target = (left_held, right_held)[side].at[half, pl.ds(base, refs[source].shape[0])]
+        return pltpu.make_async_copy(refs[source], target, sems.at[n])
+
+    for n, (*_, on, off) in enumerate(pieces):
         if on == off:
             copy(n, on).start()
         else:
@@ -616,7 +643,7 @@
                 copy(n, off).start()
 
     for n, piece in enumerate(pieces):
-        copy(n, piece[2]).wait()
+        copy(n, piece[-1]).wait()
 
     def leave(n):
         return pltpu.make_async_copy(out_held.at[pl.ds(n * capacity, capacity)], out_refs[n], out_sems.at[n])
@@ -624,7 +651,7 @@
     for n, shift in enumerate(shifts):
 
         def one(term, carry, n=n, shift=shift):
-            at = 2 * (shift * capacity + term)
+            at = 2 * (shift * (capacity + 1) + term)
             left_slot, right_slot = chosen[at], chosen[at + 1]
             group = lane_group((size, hidden), size)
             for band in range(bands):
@@ -643,7 +670,7 @@
         leave(n).wait()
 
 
-def banded_products(shifts, ids, chosen, lefts, rights, capacity, size):
+def banded_products(shifts, ids, chosen, operands, capacity, size):
     refs, pieces = [], []
 
     def index_of(array):
@@ -653,10 +680,14 @@
         refs.append(array)
         return len(refs) - 1
 
-    for side, operands in ((0, lefts), (1, rights)):
-        for half, (on, off) in enumerate(operands):
-            pieces.append((side, half, index_of(on), index_of(off)))
-    slots, bands, rows, hidden = lefts[0][0].shape
+    slots = 0
+    for both in operands:
+        for side in range(2):
+            for half, (on, off) in enumerate(both[side]):
+                pieces.append((side, half, slots, index_of(on), index_of(off)))
+        slots += both[0][0][0].shape[0]
+    halves = len(operands[0][0])
+    _, bands, rows, hidden = operands[0][0][0][0].shape
     count = len(shifts) * capacity
     anywhere = pl.BlockSpec(memory_space=pl.ANY)
     return pl.pallas_call(
@@ -667,8 +698,8 @@
             in_specs=[anywhere] * len(refs),
             out_specs=[anywhere] * len(shifts),
             scratch_shapes=[
-                pltpu.VMEM((len(lefts), slots, bands, rows, hidden), jnp.bfloat16),
-                pltpu.VMEM((len(rights), slots, bands, size, hidden), jnp.bfloat16),
+                pltpu.VMEM((halves, slots, bands, rows, hidden), jnp.bfloat16),
+                pltpu.VMEM((halves, slots, bands, size, hidden), jnp.bfloat16),
                 pltpu.VMEM((count, bands, rows, hidden), jnp.bfloat16),
                 pltpu.SemaphoreType.DMA((len(pieces),)),
                 pltpu.SemaphoreType.DMA((len(shifts),)),
@@ -677,22 +708,24 @@
         out_shape=[jax.ShapeDtypeStruct((capacity, bands, rows, hidden), jnp.bfloat16)] * len(shifts),
         compiler_params=pltpu.CompilerParams(vmem_limit_bytes=vmem_limit),
         cost_estimate=pl.CostEstimate(
-            flops=2 * count * bands * rows * hidden * hidden * len(lefts), bytes_accessed=1, transcendentals=0
+            flops=2 * count * bands * rows * hidden * hidden * halves, bytes_accessed=1, transcendentals=0
         ),
         name="banded_products",
     )(ids, chosen, *refs)
 
 
-def close_kernel(layer, last, n_parts, n_blk, n_chan, n_sub, slots_dev, terms, capacity, ids, blocks, place, *rest):
+def close_kernel(layer, last, n_parts, n_blk, n_chan, n_sub, base, of, terms, capacity, ids, blocks, place, *rest):
     chunks = n_parts // n_blk
     arrived, rest = rest[:n_parts], rest[n_parts:]
     cur_ref, gate_ref, w_out_ref = rest[:3]
     if last:
-        out_ref, held, sems, swap = rest[3:]
+        out_ref, held, wide_out, sems, swap = rest[3:]
     else:
-        chain_ref, w_ref, out_ref, next_gate_ref = rest[3:7]
-        left_refs, right_refs = rest[7 : 7 + chunks], rest[7 + chunks : 7 + 2 * chunks]
-        held, sems, norm_ref, laid, turned, swap = rest[7 + 2 * chunks :]
+        chain_ref, w_ref = rest[3:5]
+        out_ref, next_gate_ref, *operand_refs, held, wide_out, sems, norm_ref, wide, laid, turned, swap = rest[
+            -(2 * chunks + 10) :
+        ]
+        left_refs, right_refs = operand_refs[:chunks], operand_refs[chunks:]
     step = pl.program_id(0)
     _, rows, cols, channels = cur_ref.shape
     _, bands, _, hidden = held.shape
@@ -708,7 +741,16 @@
     def _():
         for n in range(n_parts):
             arrival(n).start()
+        wide_out[...] = jnp.zeros_like(wide_out)
+        for part in range(parts):
+            for a in range(parts):
+                at = (part * parts + a) * bands
+                wide_out[at : at + bands, a * channels : (a + 1) * channels] = w_out_ref[
+                    0, part * bands : (part + 1) * bands, :
+                ]
         swap[...] = swap_matrix(16)
+        if not last:
+            spread_weights(w_ref, wide, hidden, rows)
         for n in range(n_parts):
             arrival(n).wait()
 
@@ -717,19 +759,34 @@
     for row in range(0, rows, half):
         for band in range(0, bands, half):
             taken = pl.ds(band, half), pl.ds(row, half)
-            total = held[(place[step * terms], *taken)].astype(jnp.float32)
+            total = held[(place[(base + step) * terms], *taken)].astype(jnp.float32)
             for t in range(1, terms):
-                total = total + held[(place[step * terms + t], *taken)].astype(jnp.float32)
+                total = total + held[(place[(base + step) * terms + t], *taken)].astype(jnp.float32)
             moved = swapped(total.astype(jnp.bfloat16), swap)
             for r in range(half):
                 by_row[row + r].append(moved[r])
-    for g in range(rows // parts):
+    groups = rows // parts
+    pieces = []
+    for g in range(groups):
         block = jnp.concatenate([x for a in range(parts) for x in by_row[g * parts + a]]).T
-        block = block.astype(jnp.float32)
-        tiles = [block[p * cols : (p + 1) * cols] for p in range(parts)]
-        mixture = jnp.concatenate(exchange_groups(tiles, size))
-        change = dot(layer_norm(mixture).astype(jnp.bfloat16), w_out_ref[0])
+        pieces.append(jnp.concatenate([block[p * cols : (p + 1) * cols] for p in range(parts)], axis=1))
+    mixture = jnp.concatenate(pieces)
+    together = (lane_group((hidden, hidden), size) == lax.broadcasted_iota(jnp.int32, (hidden, hidden), 0) // size)
+    together = together.astype(jnp.float32).astype(jnp.bfloat16)
+    average = dot(mixture, jnp.concatenate([together] * parts)) * (1.0 / hidden)
+    centred = [mixture[:, p * hidden : (p + 1) * hidden].astype(jnp.float32) - average for p in range(parts)]
+    squares = sum(c * c for c in centred)
+    high = squares.astype(jnp.bfloat16)
+    low = (squares - high.astype(jnp.float32)).astype(jnp.bfloat16)
+    variance = dot(jnp.concatenate([high, low], axis=1), jnp.concatenate([together] * 2)) * (1.0 / hidden)
+    scale = lax.rsqrt(variance + norm_epsilon)
+    normed = jnp.concatenate([(c * scale).astype(jnp.bfloat16) for c in centred], axis=1)
+    update = dot(normed, wide_out[...])
+    for g in range(groups):
         taken = pl.ds(g * parts, parts)
+        change = jnp.concatenate(
+            [update[g * cols : (g + 1) * cols, a * channels : (a + 1) * channels] for a in range(parts)]
+        )
         gate = gate_ref[0, taken].reshape(parts * cols, channels)
         current = cur_ref[0, taken].astype(jnp.float32).reshape(parts * cols, channels)
         result = (current + gate * change).astype(jnp.bfloat16)
@@ -740,78 +797,79 @@
             next_gate = sigmoid(dot(norm, w_ref[0, :, 4 * hidden :]))
             next_gate_ref[0, taken] = next_gate.reshape(parts, cols, channels)
     if not last:
-        block = ids[0] * slots_dev + step
+        block = ids[0] * of + base + step
         starts = (blocks[0, block] * n_chan + ids[1]) * rows, (blocks[1, block] * n_sub + ids[2]) * cols
-        open_layer(layer + 1, norm_ref[...], chain_ref, *starts, w_ref, left_refs, right_refs, laid, turned, swap)
-
-
-def close_layer(layer, arrived, ids, blocks, place, current, gate, w_out, capacity, terms, chains, w_in, last, bands):
+        open_layer(
+            layer + 1, norm_ref[...], chain_ref, *starts, w_ref, left_refs, right_refs, wide, laid, turned, swap
+        )
+
+
+def close_layer(
+    layer, arrived, ids, blocks, place, current, gate, w_out, capacity, terms, chains, w_in, last, bands, base, count, earlier
+):
     n_blk = len(arrived[0])
     flat = [part for chunk in arrived for part in chunk]
     slots, rows, cols, channels = current.shape
     hidden = w_out.shape[1]
-    whole = pl.BlockSpec((1, rows, cols, channels), lambda s, *_: (s, 0, 0, 0))
 
     def layer_spec(array, index):
         return pl.BlockSpec((1,) + array.shape[1:], lambda s, *_: (index, 0, 0))
 
-    in_specs = [pl.BlockSpec(memory_space=pl.ANY)] * len(flat) + [whole, whole, layer_spec(w_out, layer)]
+    in_specs = [pl.BlockSpec(memory_space=pl.ANY)] * len(flat)
+    in_specs += slot_specs([current, gate], slots, base) + [layer_spec(w_out, layer)]
     operands = [*flat, current, gate, w_out]
     out_shape = [jax.ShapeDtypeStruct(current.shape, jnp.bfloat16)]
-    out_specs = [whole]
     scratch = [
         pltpu.VMEM((n_blk * capacity, sum(bands[layer]), rows, hidden), jnp.bfloat16),
+        pltpu.VMEM((hidden // cols * hidden, hidden // cols * channels), jnp.bfloat16),
         pltpu.SemaphoreType.DMA((len(flat),)),
     ]
     if not last:
         operands += [chains, w_in]
         in_specs += [pl.BlockSpec(chains.shape, lambda s, *_: (0, 0)), layer_spec(w_in, layer + 1)]
-        bands = bands[layer + 1]
-        made = [jax.ShapeDtypeStruct((slots, count, cols, hidden), jnp.bfloat16) for count in bands] * 2
-        out_shape += [jax.ShapeDtypeStruct(current.shape, jnp.float32)] + made
-        out_specs += [whole] + [pl.BlockSpec((1,) + o.shape[1:], lambda s, *_: (s, 0, 0, 0)) for o in made]
+        out_shape += [jax.ShapeDtypeStruct(current.shape, jnp.float32)]
+        out_shape += operand_outputs(slots, count, cols, hidden, bands[layer + 1])
         scratch += [pltpu.VMEM((rows, cols, channels), jnp.bfloat16)] + operand_scratch(cols, rows, hidden)
     else:
         scratch += [pltpu.VMEM((256, 256), jnp.bfloat16)]
-    out = pl.pallas_call(
+    more, more_specs, aliases = fill(out_shape, earlier, slots, 3 + len(operands))
+    return pl.pallas_call(
         functools.partial(
-            close_kernel, layer, last, len(flat), n_blk, lax.axis_size("chan"), lax.axis_size("sub"), slots, terms, capacity
+            close_kernel,
+            *(layer, last, len(flat), n_blk, lax.axis_size("chan"), lax.axis_size("sub"), base, slots, terms, capacity),
         ),
         grid_spec=pltpu.PrefetchScalarGridSpec(
-            num_scalar_prefetch=3, grid=(slots,), in_specs=in_specs, out_specs=out_specs, scratch_shapes=scratch
+            num_scalar_prefetch=3,
+            grid=(count,),
+            in_specs=in_specs + more_specs,
+            out_specs=slot_specs(out_shape, slots, base),
+            scratch_shapes=scratch,
         ),
         out_shape=out_shape,
+        input_output_aliases=aliases,
         compiler_params=pltpu.CompilerParams(vmem_limit_bytes=vmem_limit),
+        cost_estimate=pl.CostEstimate(flops=1 << 33, bytes_accessed=1 << 20, transcendentals=0),
         name="close_layer",
-    )(ids, blocks, place, *operands)
-    if last:
-        return out[0]
-    return out[0], out[1], out[2 : 2 + len(bands)], out[2 + len(bands) :]
+    )(ids, blocks, place, *operands, *more)
 
 
 def after(value, *others):
     return lax.optimization_barrier((value, *others))[0]
 
 
-def exchange_bands_outgoing(left, right, before):
+def exchange_bands_outgoing(left, right, over):
     both = ("chan", "sub")
-    if before:
-        ((other, _), _), ((one, _), (_, two)) = before[0]
-        left, right = lax.optimization_barrier((left, right, other, one, two))[:2]
     other = lax.ppermute(left, "sub", [(0, 1), (1, 0)])
     one = lax.ppermute(right, both, [(0, 2), (3, 1), (1, 0), (2, 3)])
     two = lax.ppermute(right, both, [(1, 2), (2, 1)])
     return [(other, left), (left, other)], [(one, one), (right, two)]
 
 
-def exchange_bands_incoming(left, right, before):
+def exchange_bands_incoming(left, right, over):
     both = ("chan", "sub")
-    if before:
-        (_, (_, two)), (_, (other, _)) = before[0]
-        left, right = lax.optimization_barrier((left, right, two, other))[:2]
     one = lax.ppermute(left, both, [(1, 3), (2, 0), (0, 1), (3, 2)])
     other = lax.ppermute(right, "chan", [(0, 1), (1, 0)])
-    two = lax.ppermute(after(one, before[1]) if before else one, both, [(0, 1), (3, 2)])
+    two = lax.ppermute(after(one, over), both, [(0, 1), (3, 2)])
     return [(left, one), (one, two)], [(right, right), (other, other)]
 
 
@@ -824,14 +882,36 @@
     current = pair
     bands = [[12, 20], [14, 18]]
     chosen, place = make_plan(ids, owners, slot_of, n_blk, slots, terms, capacity)
+    half = slots // 2
+    halves = [(0, half), (half, slots - half)]
     for layer in range(layers):
+        count = len(bands[layer])
         if layer == 0:
-            gate, lefts, rights = open_operands(ids, blocks, pair, chains, w_in, hidden, bands[0])
+            calls = [None]
+            for base, size in halves:
+                calls.append(open_operands(ids, blocks, pair, chains, w_in, hidden, bands[0], base, size, calls[-1]))
+            gate = calls[-1][0]
+        operands = [call[-2 * count :] for call in calls[1:]]
         exchange = exchange_bands_incoming if layer % 2 else exchange_bands_outgoing
-        arrived, before = [], None
-        for left, right in zip(lefts, rights):
-            operands = exchange(left, right, before)
-            made = banded_products(shifts, ids, chosen, *operands, capacity, cols)
+        arrived = []
+        for chunk in range(count):
+            if chunk == 0:
+                exchanged = []
+                over = operands[-1][count]
+                for left, right in [(o[0], o[count]) for o in operands]:
+                    if exchanged and layer % 2:
+                        (_, (one, _)), (_, (other, _)) = exchanged[-1]
+                        left, right = lax.optimization_barrier((left, right, one, other))[:2]
+                    exchanged.append(exchange(left, right, over))
+            else:
+                left, right = operands[-1][chunk], operands[-1][count + chunk]
+                last_of = exchanged[-1]
+                left, right = lax.optimization_barrier(
+                    (left, right, last_of[0][1][1], last_of[0][0][0], last_of[1][0][1], last_of[1][1][1])
+                    + ((made[-1],) if layer % 2 == 0 else ())
+                )[:2]
+                exchanged = [exchange(left, right, arrived[-1][far])]
+            made = banded_products(shifts, ids, chosen, exchanged, capacity, cols)
             parts = [None] * n_blk
             for shift, part in zip(shifts, made):
                 if shift:
@@ -840,14 +920,18 @@
                     part = lax.ppermute(part, "blk", [(p, (p + shift) % n_blk) for p in range(n_blk)])
                 parts[shift] = part
             arrived.append(parts)
-            before = operands, parts[far]
         last = layer == layers - 1
-        out = close_layer(
-            layer, arrived, ids, blocks, place, current, gate, w_out, capacity, terms, chains, w_in, last, bands
-        )
+        calls = [None]
+        for base, size in [(0, slots)] if last else halves:
+            calls.append(
+                close_layer(
+                    *(layer, arrived, ids, blocks, place, current, gate, w_out, capacity, terms, chains, w_in, last),
+                    *(bands, base, size, calls[-1]),
+                )
+            )
         if last:
-            return out
-        current, gate, lefts, rights = out
+            return calls[-1][0]
+        current, gate = calls[-1][:2]
 
 
 def per_device(pair, block_list, term_owner, term_slots, chain_ids, w_in, w_out):

time: 347 us -> 334 us (0.963)
  waiting for transfers between devices: 201 us -> 177 us
  starting transfers between devices: 34.7 us -> 45.3 us
    ppermute x2 -> x3, waiting for transfers between devices: 19.3 us -> 8.5 us  [exchange_bands_incoming(): one = lax.ppermute(left, both, [(1, 3), (2, 0), (0, 1), (3, 2)])]
    ppermute x2 -> x3, waiting for transfers between devices: 12.6 us -> 3.58 us  [exchange_bands_incoming(): other = lax.ppermute(right, 'chan', [(0, 1), (1, 0)])]
    ppermute x12, waiting for transfers between devices: 137 us -> 133 us  [banded(): lax.ppermute(part, 'blk', [(p, (p + shift) % n_blk) for p in range(n_blk)])]
    ppermute x2 -> x3, starting transfers between devices: 7.19 us -> 11.6 us  [exchange_bands_incoming(): two = lax.ppermute(after(one, over), both, [(0, 1), (3, 2)])]
    pallas_call x2 -> x3, Pallas kernels: 49.3 us -> 45.1 us  [close_layer(): pl.pallas_call(functools.partial(close_kernel, *(layer, last, len(flat),...]
    pallas_call x1 -> x2, Pallas kernels: 18.7 us -> 22.3 us  [open_operands(): pl.pallas_call(functools.partial(open_kernel, hidden, len(bands), lax.axi...]
    ppermute x2 -> x3, starting transfers between devices: 6.02 us -> 8.45 us  [exchange_bands_outgoing(): one = lax.ppermute(right, both, [(0, 2), (3, 1), (1, 0), (2, 3)])]
    ppermute x2 -> x3, waiting for transfers between devices: 31.4 us -> 30.8 us  [exchange_bands_outgoing(): one = lax.ppermute(right, both, [(0, 2), (3, 1), (1, 0), (2, 3)])]
  transfers between devices with their start and end apart: 24 -> 30, of which waited for: 15 -> 14; matrix products, arithmetic and copies ran while one was open for 0% -> 0% of each run, Pallas kernels for 10% -> 16%
where the time goes in v7:
time: 334 us; the launch traced here: 332 us
  waiting for transfers between devices  177 us (53%)
  Pallas kernels  102 us (31%)
  starting transfers between devices  45.3 us (14%)
  local copies, waits for them, and re-layouts  6.46 us (2%)
    ppermute x12, waiting for transfers between devices, banded(): lax.ppermute(part, 'blk', [(p, (p + shift) % n_blk) for p in range(n_blk)])  133 us
    pallas_call x3, Pallas kernels, close_layer(): pl.pallas_call(functools.partial(close_kernel, *(layer, last, len(flat),...  45.1 us
    pallas_call x4, Pallas kernels, banded_products(): pl.pallas_call(functools.partial(banded_kernel, shifts, capacity, tuple(p...  33.1 us
    ppermute x3, waiting for transfers between devices, exchange_bands_outgoing(): one = lax.ppermute(right, both, [(0, 2), (3, 1), (1, 0), (2, 3)])  30.8 us
    pallas_call x2, Pallas kernels, open_operands(): pl.pallas_call(functools.partial(open_kernel, hidden, len(bands), lax.axi...  22.3 us
    ppermute x12, starting transfers between devices, banded(): lax.ppermute(part, 'blk', [(p, (p + shift) % n_blk) for p in range(n_blk)])  16.3 us
    ppermute x3, starting transfers between devices, exchange_bands_incoming(): two = lax.ppermute(after(one, over), both, [(0, 1), (3, 2)])  11.6 us
    ppermute x3, waiting for transfers between devices, exchange_bands_incoming(): one = lax.ppermute(left, both, [(1, 3), (2, 0), (0, 1), (3, 2)])  8.5 us
  transfers between devices with their start and end apart: 30, of which 14 were waited for; matrix products, arithmetic and copies ran while one was open for 0% of the time, Pallas kernels for 16%

profile of v7, /device:TPU:11, one launch (start us, length us, event | category | flops | bytes accessed | tf_op | source)
XLA Modules:
  0.0 332.3 jit_solution(5579532023283746393)
XLA Ops:
  0.6 11.1 %open_operands.2 = (f32[8,32,32,128]{3,2,1,0:T(8,128)}, bf16[4,12,32,128]{3,2,1,0:T(8,128)(2,1)}, bf16[8,20,32,128]{3,2,1,0:T(8,128)(2,1)}, bf16[4,12,32,128]{3,2,1,0:T(8,128)(2,1)}, bf16[8,20,32,128]{3,2,1,0:T(8,128)(2,1)}) custom-call(s32[4]{0:T(128)} %pad_add_fusion.ids, s32[2,32]{1,0:T(2,128)} %bitcast.14, bf16[8,32,32,128]{3,2,1,0:T(8,128)(2,1)} %rest_8_.3, ...), custom_call_target="tpu_custom_call" | custom-call | flops 8589934592 | bytes 1048576 | tf_op jit(solution)/shard_map/open_operands/pallas_call | solution.py:564
  12.4 3.3 collective-permute-start.1
  15.7 11.2 %open_operands.3 = (f32[8,32,32,128]{3,2,1,0:T(8,128)}, bf16[4,12,32,128]{3,2,1,0:T(8,128)(2,1)}, bf16[8,20,32,128]{3,2,1,0:T(8,128)(2,1)}, bf16[4,12,32,128]{3,2,1,0:T(8,128)(2,1)}, bf16[8,20,32,128]{3,2,1,0:T(8,128)(2,1)}) custom-call(s32[4]{0:T(128)} %pad_add_fusion.ids, ...), custom_call_target="tpu_custom_call", output_to_operand_aliasing={{0}: (5, {}), {2}: (6, {}), {4}: (7, {})} | custom-call | flops 8589934592 | bytes 1048576 | tf_op jit(solution)/shard_map/open_operands/pallas_call | solution.py:564
  28.1 2.6 collective-permute-start.4
  32.5 6.7 %collective-permute-done.4.rest_7_ = bf16[4,12,32,128]{3,2,1,0:T(8,128)(2,1)S(1)} collective-permute-done((bf16[4,12,32,128]{3,2,1,0:T(8,128)(2,1)}, bf16[4,12,32,128]{3,2,1,0:T(8,128)(2,1)S(1)}, u32[]{:S(2)}, u32[]{:S(2)}) %collective-permute-start.4) | collective-permute-done | bytes 393248 | tf_op jit(solution)/shard_map/ppermute | solution.py:863
  40.0 7.4 %banded_products.4 = (bf16[4,12,32,128]{3,2,1,0:T(8,128)(2,1)}, bf16[4,12,32,128]{3,2,1,0:T(8,128)(2,1)}, bf16[4,12,32,128]{3,2,1,0:T(8,128)(2,1)}, bf16[4,12,32,128]{3,2,1,0:T(8,128)(2,1)}) custom-call(s32[4]{0:T(128)} %pad_add_fusion.ids, s32[40]{0:T(128)} %get-tuple-element.61.chosen, bf16[4,12,32,128]{3,2,1,0:T(8,128)(2,1)} %copy-done.17, ...), custom_call_target="tpu_custom_call" | custom-call | flops 402653184 | bytes 1 | tf_op jit(solution)/shard_map/banded_products/pallas_call | solution.py:693
  50.0 2.6 collective-permute-start.10
  56.4 24.1 %collective-permute-done.10.rest_2_ = bf16[8,20,32,128]{3,2,1,0:T(8,128)(2,1)S(1)} collective-permute-done((bf16[8,20,32,128]{3,2,1,0:T(8,128)(2,1)S(1)}, bf16[8,20,32,128]{3,2,1,0:T(8,128)(2,1)S(1)}, u32[]{:S(2)}, u32[]{:S(2)}) %collective-permute-start.10) | collective-permute-done | bytes 1310752 | tf_op jit(solution)/shard_map/ppermute | solution.py:863
  81.5 9.2 %banded_products.5 = (bf16[4,20,32,128]{3,2,1,0:T(8,128)(2,1)}, bf16[4,20,32,128]{3,2,1,0:T(8,128)(2,1)}, bf16[4,20,32,128]{3,2,1,0:T(8,128)(2,1)}, bf16[4,20,32,128]{3,2,1,0:T(8,128)(2,1)}) custom-call(s32[4]{0:T(128)} %pad_add_fusion.ids, s32[40]{0:T(128)} %get-tuple-element.61.chosen, bf16[8,20,32,128]{3,2,1,0:T(8,128)(2,1)} %copy-done, ...), custom_call_target="tpu_custom_call" | custom-call | flops 671088640 | bytes 1 | tf_op jit(solution)/shard_map/banded_products/pallas_call | solution.py:693
  91.0 2.3 collective-permute-start.13
  93.3 2.2 collective-permute-start.12
  95.5 9.9 %collective-permute-done.14.rest_7_ = bf16[4,20,32,128]{3,2,1,0:T(8,128)(2,1)S(1)} collective-permute-done((bf16[4,20,32,128]{3,2,1,0:T(8,128)(2,1)}, bf16[4,20,32,128]{3,2,1,0:T(8,128)(2,1)S(1)}, u32[]{:S(2)}, u32[]{:S(2)}) %collective-permute-start.14) | collective-permute-done | bytes 655392 | tf_op jit(solution)/shard_map/ppermute | solution.py:920
  105.4 30.0 %collective-permute-done.13.rest_6_ = bf16[4,20,32,128]{3,2,1,0:T(8,128)(2,1)S(1)} collective-permute-done((bf16[4,20,32,128]{3,2,1,0:T(8,128)(2,1)}, bf16[4,20,32,128]{3,2,1,0:T(8,128)(2,1)S(1)}, u32[]{:S(2)}, u32[]{:S(2)}) %collective-permute-start.13) | collective-permute-done | bytes 655392 | tf_op jit(solution)/shard_map/ppermute | solution.py:920
  135.4 14.0 %collective-permute-done.12.rest_5_ = bf16[4,20,32,128]{3,2,1,0:T(8,128)(2,1)S(1)} collective-permute-done((bf16[4,20,32,128]{3,2,1,0:T(8,128)(2,1)}, bf16[4,20,32,128]{3,2,1,0:T(8,128)(2,1)S(1)}, u32[]{:S(2)}, u32[]{:S(2)}) %collective-permute-start.12) | collective-permute-done | bytes 655392 | tf_op jit(solution)/shard_map/ppermute | solution.py:920
  150.3 16.1 %close_layer.3 = (bf16[8,32,32,128]{3,2,1,0:T(8,128)(2,1)}, f32[8,32,32,128]{3,2,1,0:T(8,128)}, bf16[4,14,32,128]{3,2,1,0:T(8,128)(2,1)}, bf16[8,18,32,128]{3,2,...) custom-call(s32[4]{0:T(128)} %pad_add_fusion.ids, s32[2,32]{1,0:T(2,128)} %bitcast.16, ...), custom_call_target="tpu_custom_call" | custom-call | flops 8589934592 | bytes 1048576 | tf_op jit(solution)/shard_map/close_layer/pallas_call | solution.py:836
  169.2 16.0 %close_layer.4 = (bf16[8,32,32,128]{3,2,1,0:T(8,128)(2,1)}, f32[8,32,32,128]{3,2,1,0:T(8,128)}, bf16[4,14,32,128]{3,2,1,0:T(8,128)(2,1)}, bf16[8,18,32,128]{3,2,...) custom-call(s32[4]{0:T(128)} %pad_add_fusion.ids, ...), custom_call_target="tpu_custom_call", output_to_operand_aliasing={{0}: (16, {}), {1}: (17, {}), {3}: (18, {}), {5}: (19, {})} | custom-call | flops 8589934592 | bytes 1048576 | tf_op jit(solution)/shard_map/close_layer/pallas_call | solution.py:836
  186.8 8.5 %collective-permute-done.18.rest_6_ = bf16[4,14,32,128]{3,2,1,0:T(8,128)(2,1)S(1)} collective-permute-done((bf16[4,14,32,128]{3,2,1,0:T(8,128)(2,1)}, bf16[4,14,32,128]{3,2,1,0:T(8,128)(2,1)S(1)}, u32[]{:S(2)}, u32[]{:S(2)}) %collective-permute-start.18) | collective-permute-done | bytes 458784 | tf_op jit(solution)/shard_map/ppermute | solution.py:870
  195.3 4.5 %collective-permute-start.19 = (bf16[4,14,32,128]{3,2,1,0:T(8,128)(2,1)S(1)}, bf16[4,14,32,128]{3,2,1,0:T(8,128)(2,1)S(1)}, u32[]{:S(2)}, u32[]{:S(2)}) collective-permute-start(bf16[4,14,32,128]{3,2,1,0:T(8,128)(2,1)S(1)} %collective-permute-done.18.rest_6_), channel_id=1, source_target_pairs={{0,1},{3,2},{4,5},{7,6},{8,9},{11,10},{12,13},{15,14},{16,17},{19,... | collective-permute-start | bytes 1376264 | tf_op jit(solution)/shard_map/ppermute | solution.py:872
  199.8 2.9 collective-permute-done.20.rest_9_
  202.8 4.3 %collective-permute-start.16 = (bf16[4,14,32,128]{3,2,1,0:T(8,128)(2,1)S(1)}, bf16[4,14,32,128]{3,2,1,0:T(8,128)(2,1)S(1)}, u32[]{:S(2)}, u32[]{:S(2)}) collective-permute-start(bf16[4,14,32,128]{3,2,1,0:T(8,128)(2,1)S(1)} %collective-permute-done.15.rest_1_), channel_id=1, source_target_pairs={{0,1},{3,2},{4,5},{7,6},{8,9},{11,10},{12,13},{15,14},{16,17},{19,... | collective-permute-start | bytes 1376264 | tf_op jit(solution)/shard_map/ppermute | solution.py:872
  209.3 7.8 %banded_products.6 = (bf16[4,14,32,128]{3,2,1,0:T(8,128)(2,1)}, bf16[4,14,32,128]{3,2,1,0:T(8,128)(2,1)}, bf16[4,14,32,128]{3,2,1,0:T(8,128)(2,1)}, bf16[4,14,32,128]{3,2,1,0:T(8,128)(2,1)}) custom-call(s32[4]{0:T(128)} %pad_add_fusion.ids, s32[40]{0:T(128)} %get-tuple-element.61.chosen, bf16[4,14,32,128]{3,2,1,0:T(8,128)(2,1)} %get-tuple-element.85.rest_0_, ...), custom_call_target="tpu_custom_call" | custom-call | flops 469762048 | bytes 1 | tf_op jit(solution)/shard_map/banded_products/pallas_call | solution.py:693
  217.3 19.9 %collective-permute-done.22.rest_2_ = bf16[4,14,32,128]{3,2,1,0:T(8,128)(2,1)S(1)} collective-permute-done((bf16[4,14,32,128]{3,2,1,0:T(8,128)(2,1)}, bf16[4,14,32,128]{3,2,1,0:T(8,128)(2,1)S(1)}, u32[]{:S(2)}, u32[]{:S(2)}) %collective-permute-start.22) | collective-permute-done | bytes 458784 | tf_op jit(solution)/shard_map/ppermute | solution.py:920
  237.2 2.9 collective-permute-start.25
  240.0 1.9 collective-permute-start.21
  241.9 1.9 collective-permute-start.23
  246.5 8.7 %banded_products.7 = (bf16[4,18,32,128]{3,2,1,0:T(8,128)(2,1)}, bf16[4,18,32,128]{3,2,1,0:T(8,128)(2,1)}, bf16[4,18,32,128]{3,2,1,0:T(8,128)(2,1)}, bf16[4,18,32,128]{3,2,1,0:T(8,128)(2,1)}) custom-call(s32[4]{0:T(128)} %pad_add_fusion.ids, s32[40]{0:T(128)} %get-tuple-element.61.chosen, bf16[8,18,32,128]{3,2,1,0:T(8,128)(2,1)} %get-tuple-element.103.rest_0_, ...), custom_call_target="tpu_custom_call" | custom-call | flops 603979776 | bytes 1 | tf_op jit(solution)/shard_map/banded_products/pallas_call | solution.py:693
  255.3 9.2 %collective-permute-done.23.rest_3_ = bf16[4,14,32,128]{3,2,1,0:T(8,128)(2,1)S(1)} collective-permute-done((bf16[4,14,32,128]{3,2,1,0:T(8,128)(2,1)}, bf16[4,14,32,128]{3,2,1,0:T(8,128)(2,1)S(1)}, u32[]{:S(2)}, u32[]{:S(2)}) %collective-permute-start.23) | collective-permute-done | bytes 458784 | tf_op jit(solution)/shard_map/ppermute | solution.py:920
  265.9 2.1 collective-permute-start.28
  268.5 11.9 %collective-permute-done.29.rest_7_ = bf16[4,18,32,128]{3,2,1,0:T(8,128)(2,1)S(1)} collective-permute-done((bf16[4,18,32,128]{3,2,1,0:T(8,128)(2,1)}, bf16[4,18,32,128]{3,2,1,0:T(8,128)(2,1)S(1)}, u32[]{:S(2)}, u32[]{:S(2)}) %collective-permute-start.29) | collective-permute-done | bytes 589856 | tf_op jit(solution)/shard_map/ppermute | solution.py:920
  280.3 25.3 %collective-permute-done.28.rest_6_ = bf16[4,18,32,128]{3,2,1,0:T(8,128)(2,1)S(1)} collective-permute-done((bf16[4,18,32,128]{3,2,1,0:T(8,128)(2,1)}, bf16[4,18,32,128]{3,2,1,0:T(8,128)(2,1)S(1)}, u32[]{:S(2)}, u32[]{:S(2)}) %collective-permute-start.28) | collective-permute-done | bytes 589856 | tf_op jit(solution)/shard_map/ppermute | solution.py:920
  305.7 12.6 %collective-permute-done.27.rest_5_ = bf16[4,18,32,128]{3,2,1,0:T(8,128)(2,1)S(1)} collective-permute-done((bf16[4,18,32,128]{3,2,1,0:T(8,128)(2,1)}, bf16[4,18,32,128]{3,2,1,0:T(8,128)(2,1)S(1)}, u32[]{:S(2)}, u32[]{:S(2)}) %collective-permute-start.27) | collective-permute-done | bytes 589856 | tf_op jit(solution)/shard_map/ppermute | solution.py:920
  319.2 13.0 %close_layer.5 = bf16[8,32,32,128]{3,2,1,0:T(8,128)(2,1)} custom-call(s32[4]{0:T(128)} %pad_add_fusion.ids, s32[2,32]{1,0:T(2,128)} %bitcast.18, s32[16]{0:T(128)} %get-tuple-element.60.place, bf16[4,14,32,128]{3,2,1,0:T(8,128)(2,1)} %get-tuple-element.97.rest_0_, bf16[4,14,32,128]{3,2,1,0:T(8,128)(2,1)} %copy-done.28, bf16[4,14,32,128]{3,2,1,0:T(8,128)(2,1)} %copy-done.27, ...), custom_call_target="tpu_custom_call" | custom-call | flops 8589934592 | bytes 1048576 | tf_op jit(solution)/shard_map/close_layer/pallas_call | solution.py:836
  (105 shorter events, 25.7 us)
Async XLA Ops:
  11.8 20.7 %collective-permute-start.2 = (bf16[4,12,32,128]{3,2,1,0:T(8,128)(2,1)}, bf16[4,12,32,128]{3,2,1,0:T(8,128)(2,1)S(1)}, u32[]{:S(2)}, u32[]{:S(2)}) collective-permute-start(bf16[4,12,32,128]{3,2,1,0:T(8,128)(2,1)} %get-tuple-element.63.rest_3_), channel_id=1, source_target_pairs={{1,2},{2,1},{5,6},{6,5},{9,10},{10,9},{13,14},{14,13},{17,18},{18,... | collective-permute-start | bytes 1179656 | tf_op jit(solution)/shard_map/ppermute | solution.py:864
  12.4 20.0 %collective-permute-start.1 = (bf16[4,12,32,128]{3,2,1,0:T(8,128)(2,1)}, bf16[4,12,32,128]{3,2,1,0:T(8,128)(2,1)S(1)}, u32[]{:S(2)}, u32[]{:S(2)}) collective-permute-start(bf16[4,12,32,128]{3,2,1,0:T(8,128)(2,1)} %get-tuple-element.63.rest_3_), channel_id=1, source_target_pairs={{0,2},{3,1},{1,0},{2,3},{4,6},{7,5},{5,4},{6,7},{8,10},{11,9},{9,8... | collective-permute-start | bytes 1179656 | tf_op jit(solution)/shard_map/ppermute | solution.py:863
  15.7 12.4 %collective-permute-start = (bf16[4,12,32,128]{3,2,1,0:T(8,128)(2,1)}, bf16[4,12,32,128]{3,2,1,0:T(8,128)(2,1)S(1)}, u32[]{:S(2)}, u32[]{:S(2)}) collective-permute-start(bf16[4,12,32,128]{3,2,1,0:T(8,128)(2,1)} %get-tuple-element.62.rest_1_), channel_id=1, source_target_pairs={{0,1},{1,0},{2,3},{3,2},{4,5},{5,4},{6,7},{7,6},{8,9},{9,8},{10,11... | collective-permute-start | bytes 1179656 | tf_op jit(solution)/shard_map/ppermute | solution.py:862
  26.9 5.6 %collective-permute-start.3 = (bf16[4,12,32,128]{3,2,1,0:T(8,128)(2,1)}, bf16[4,12,32,128]{3,2,1,0:T(8,128)(2,1)S(1)}, u32[]{:S(2)}, u32[]{:S(2)}) collective-permute-start(bf16[4,12,32,128]{3,2,1,0:T(8,128)(2,1)} %get-tuple-element.67.rest_6_), channel_id=1, source_target_pairs={{0,1},{1,0},{2,3},{3,2},{4,5},{5,4},{6,7},{7,6},{8,9},{9,8},{10,11... | collective-permute-start | bytes 1179656 | tf_op jit(solution)/shard_map/ppermute | solution.py:862
  27.4 5.0 %collective-permute-start.5 = (bf16[4,12,32,128]{3,2,1,0:T(8,128)(2,1)}, bf16[4,12,32,128]{3,2,1,0:T(8,128)(2,1)S(1)}, u32[]{:S(2)}, u32[]{:S(2)}) collective-permute-start(bf16[4,12,32,128]{3,2,1,0:T(8,128)(2,1)} %get-tuple-element.68.rest_8_), channel_id=1, source_target_pairs={{1,2},{2,1},{5,6},{6,5},{9,10},{10,9},{13,14},{14,13},{17,18},{18,... | collective-permute-start | bytes 1179656 | tf_op jit(solution)/shard_map/ppermute | solution.py:864
  28.1 11.1 %collective-permute-start.4 = (bf16[4,12,32,128]{3,2,1,0:T(8,128)(2,1)}, bf16[4,12,32,128]{3,2,1,0:T(8,128)(2,1)S(1)}, u32[]{:S(2)}, u32[]{:S(2)}) collective-permute-start(bf16[4,12,32,128]{3,2,1,0:T(8,128)(2,1)} %get-tuple-element.68.rest_8_), channel_id=1, source_target_pairs={{0,2},{3,1},{1,0},{2,3},{4,6},{7,5},{5,4},{6,7},{8,10},{11,9},{9,8... | collective-permute-start | bytes 1179656 | tf_op jit(solution)/shard_map/ppermute | solution.py:863
  47.5 7.4 %collective-permute-start.9 = (bf16[8,20,32,128]{3,2,1,0:T(8,128)(2,1)S(1)}, bf16[8,20,32,128]{3,2,1,0:T(8,128)(2,1)S(1)}, u32[]{:S(2)}, u32[]{:S(2)}) collective-permute-start(bf16[8,20,32,128]{3,2,1,0:T(8,128)(2,1)S(1)} %copy-done.3), channel_id=1, source_target_pairs={{0,1},{1,0},{2,3},{3,2},{4,5},{5,4},{6,7},{7,6},{8,9},{9,8},{10,11... | collective-permute-start | bytes 3932168 | tf_op jit(solution)/shard_map/ppermute | solution.py:862
  49.3 7.1 %collective-permute-start.11 = (bf16[8,20,32,128]{3,2,1,0:T(8,128)(2,1)S(1)}, bf16[8,20,32,128]{3,2,1,0:T(8,128)(2,1)S(1)}, u32[]{:S(2)}, u32[]{:S(2)}) collective-permute-start(bf16[8,20,32,128]{3,2,1,0:T(8,128)(2,1)S(1)} %copy-done.4), channel_id=1, source_target_pairs={{1,2},{2,1},{5,6},{6,5},{9,10},{10,9},{13,14},{14,13},{17,18},{18,... | collective-permute-start | bytes 3932168 | tf_op jit(solution)/shard_map/ppermute | solution.py:864
  50.0 30.4 %collective-permute-start.10 = (bf16[8,20,32,128]{3,2,1,0:T(8,128)(2,1)S(1)}, bf16[8,20,32,128]{3,2,1,0:T(8,128)(2,1)S(1)}, u32[]{:S(2)}, u32[]{:S(2)}) collective-permute-start(bf16[8,20,32,128]{3,2,1,0:T(8,128)(2,1)S(1)} %copy-done.4), channel_id=1, source_target_pairs={{0,2},{3,1},{1,0},{2,3},{4,6},{7,5},{5,4},{6,7},{8,10},{11,9},{9,8... | collective-permute-start | bytes 3932168 | tf_op jit(solution)/shard_map/ppermute | solution.py:863
  52.6 38.1 %collective-permute-start.6 = (bf16[4,12,32,128]{3,2,1,0:T(8,128)(2,1)}, bf16[4,12,32,128]{3,2,1,0:T(8,128)(2,1)S(1)}, u32[]{:S(2)}, u32[]{:S(2)}) collective-permute-start(bf16[4,12,32,128]{3,2,1,0:T(8,128)(2,1)} %get-tuple-element.70), channel_id=1, source_target_pairs={{0,4},{4,8},{8,12},{12,0},{1,5},{5,9},{9,13},{13,1},{2,6},{6,10},{... | collective-permute-start | bytes 1179656 | tf_op jit(solution)/shard_map/ppermute | solution.py:920
  53.9 36.8 %collective-permute-start.7 = (bf16[4,12,32,128]{3,2,1,0:T(8,128)(2,1)}, bf16[4,12,32,128]{3,2,1,0:T(8,128)(2,1)S(1)}, u32[]{:S(2)}, u32[]{:S(2)}) collective-permute-start(bf16[4,12,32,128]{3,2,1,0:T(8,128)(2,1)} %get-tuple-element.71), channel_id=1, source_target_pairs={{0,8},{4,12},{8,0},{12,4},{1,9},{5,13},{9,1},{13,5},{2,10},{6,14},... | collective-permute-start | bytes 1179656 | tf_op jit(solution)/shard_map/ppermute | solution.py:920
  54.9 35.8 %collective-permute-start.8 = (bf16[4,12,32,128]{3,2,1,0:T(8,128)(2,1)}, bf16[4,12,32,128]{3,2,1,0:T(8,128)(2,1)S(1)}, u32[]{:S(2)}, u32[]{:S(2)}) collective-permute-start(bf16[4,12,32,128]{3,2,1,0:T(8,128)(2,1)} %get-tuple-element.72), channel_id=1, source_target_pairs={{0,12},{4,0},{8,4},{12,8},{1,13},{5,1},{9,5},{13,9},{2,14},{6,2},{... | collective-permute-start | bytes 1179656 | tf_op jit(solution)/shard_map/ppermute | solution.py:920
  90.8 14.7 %collective-permute-start.14 = (bf16[4,20,32,128]{3,2,1,0:T(8,128)(2,1)}, bf16[4,20,32,128]{3,2,1,0:T(8,128)(2,1)S(1)}, u32[]{:S(2)}, u32[]{:S(2)}) collective-permute-start(bf16[4,20,32,128]{3,2,1,0:T(8,128)(2,1)} %get-tuple-element.83), channel_id=1, source_target_pairs={{0,12},{4,0},{8,4},{12,8},{1,13},{5,1},{9,5},{13,9},{2,14},{6,2},{... | collective-permute-start | bytes 1966088 | tf_op jit(solution)/shard_map/ppermute | solution.py:920
  91.0 44.4 %collective-permute-start.13 = (bf16[4,20,32,128]{3,2,1,0:T(8,128)(2,1)}, bf16[4,20,32,128]{3,2,1,0:T(8,128)(2,1)S(1)}, u32[]{:S(2)}, u32[]{:S(2)}) collective-permute-start(bf16[4,20,32,128]{3,2,1,0:T(8,128)(2,1)} %get-tuple-element.81), channel_id=1, source_target_pairs={{0,8},{4,12},{8,0},{12,4},{1,9},{5,13},{9,1},{13,5},{2,10},{6,14},... | collective-permute-start | bytes 1966088 | tf_op jit(solution)/shard_map/ppermute | solution.py:920
  93.3 56.1 %collective-permute-start.12 = (bf16[4,20,32,128]{3,2,1,0:T(8,128)(2,1)}, bf16[4,20,32,128]{3,2,1,0:T(8,128)(2,1)S(1)}, u32[]{:S(2)}, u32[]{:S(2)}) collective-permute-start(bf16[4,20,32,128]{3,2,1,0:T(8,128)(2,1)} %get-tuple-element.79), channel_id=1, source_target_pairs={{0,4},{4,8},{8,12},{12,0},{1,5},{5,9},{9,13},{13,1},{2,6},{6,10},{... | collective-permute-start | bytes 1966088 | tf_op jit(solution)/shard_map/ppermute | solution.py:920
  166.4 18.9 %collective-permute-start.15 = (bf16[4,14,32,128]{3,2,1,0:T(8,128)(2,1)}, bf16[4,14,32,128]{3,2,1,0:T(8,128)(2,1)S(1)}, u32[]{:S(2)}, u32[]{:S(2)}) collective-permute-start(bf16[4,14,32,128]{3,2,1,0:T(8,128)(2,1)} %get-tuple-element.85.rest_0_), channel_id=1, source_target_pairs={{1,3},{2,0},{0,1},{3,2},{5,7},{6,4},{4,5},{7,6},{9,11},{10,8},{8,9... | collective-permute-start | bytes 1376264 | tf_op jit(solution)/shard_map/ppermute | solution.py:870
  167.7 17.6 %collective-permute-start.17 = (bf16[4,14,32,128]{3,2,1,0:T(8,128)(2,1)}, bf16[4,14,32,128]{3,2,1,0:T(8,128)(2,1)S(1)}, u32[]{:S(2)}, u32[]{:S(2)}) collective-permute-start(bf16[4,14,32,128]{3,2,1,0:T(8,128)(2,1)} %get-tuple-element.92.rest_3_), channel_id=1, source_target_pairs={{0,2},{2,0},{1,3},{3,1},{4,6},{6,4},{5,7},{7,5},{8,10},{10,8},{9,1... | collective-permute-start | bytes 1376264 | tf_op jit(solution)/shard_map/ppermute | solution.py:871
  185.3 10.0 %collective-permute-start.18 = (bf16[4,14,32,128]{3,2,1,0:T(8,128)(2,1)}, bf16[4,14,32,128]{3,2,1,0:T(8,128)(2,1)S(1)}, u32[]{:S(2)}, u32[]{:S(2)}) collective-permute-start(bf16[4,14,32,128]{3,2,1,0:T(8,128)(2,1)} %get-tuple-element.94.rest_5_), channel_id=1, source_target_pairs={{1,3},{2,0},{0,1},{3,2},{5,7},{6,4},{4,5},{7,6},{9,11},{10,8},{8,9... | collective-permute-start | bytes 1376264 | tf_op jit(solution)/shard_map/ppermute | solution.py:870
  186.0 16.7 %collective-permute-start.20 = (bf16[4,14,32,128]{3,2,1,0:T(8,128)(2,1)}, bf16[4,14,32,128]{3,2,1,0:T(8,128)(2,1)S(1)}, u32[]{:S(2)}, u32[]{:S(2)}) collective-permute-start(bf16[4,14,32,128]{3,2,1,0:T(8,128)(2,1)} %get-tuple-element.96.rest_8_), channel_id=1, source_target_pairs={{0,2},{2,0},{1,3},{3,1},{4,6},{6,4},{5,7},{7,5},{8,10},{10,8},{9,1... | collective-permute-start | bytes 1376264 | tf_op jit(solution)/shard_map/ppermute | solution.py:871
  195.3 7.4 %collective-permute-start.19 = (bf16[4,14,32,128]{3,2,1,0:T(8,128)(2,1)S(1)}, bf16[4,14,32,128]{3,2,1,0:T(8,128)(2,1)S(1)}, u32[]{:S(2)}, u32[]{:S(2)}) collective-permute-start(bf16[4,14,32,128]{3,2,1,0:T(8,128)(2,1)S(1)} %collective-permute-done.18.rest_6_), channel_id=1, source_target_pairs={{0,1},{3,2},{4,5},{7,6},{8,9},{11,10},{12,13},{15,14},{16,17},{19,... | collective-permute-start | bytes 1376264 | tf_op jit(solution)/shard_map/ppermute | solution.py:872
  202.7 34.4 %collective-permute-start.24 = (bf16[8,18,32,128]{3,2,1,0:T(8,128)(2,1)}, bf16[8,18,32,128]{3,2,1,0:T(8,128)(2,1)S(1)}, u32[]{:S(2)}, u32[]{:S(2)}) collective-permute-start(bf16[8,18,32,128]{3,2,1,0:T(8,128)(2,1)} %get-tuple-element.103.rest_0_), channel_id=1, source_target_pairs={{1,3},{2,0},{0,1},{3,2},{5,7},{6,4},{4,5},{7,6},{9,11},{10,8},{8,9... | collective-permute-start | bytes 3538952 | tf_op jit(solution)/shard_map/ppermute | solution.py:870
  202.8 5.7 %collective-permute-start.16 = (bf16[4,14,32,128]{3,2,1,0:T(8,128)(2,1)S(1)}, bf16[4,14,32,128]{3,2,1,0:T(8,128)(2,1)S(1)}, u32[]{:S(2)}, u32[]{:S(2)}) collective-permute-start(bf16[4,14,32,128]{3,2,1,0:T(8,128)(2,1)S(1)} %collective-permute-done.15.rest_1_), channel_id=1, source_target_pairs={{0,1},{3,2},{4,5},{7,6},{8,9},{11,10},{12,13},{15,14},{16,17},{19,... | collective-permute-start | bytes 1376264 | tf_op jit(solution)/shard_map/ppermute | solution.py:872
  217.1 20.1 %collective-permute-start.22 = (bf16[4,14,32,128]{3,2,1,0:T(8,128)(2,1)}, bf16[4,14,32,128]{3,2,1,0:T(8,128)(2,1)S(1)}, u32[]{:S(2)}, u32[]{:S(2)}) collective-permute-start(bf16[4,14,32,128]{3,2,1,0:T(8,128)(2,1)} %get-tuple-element.99), channel_id=1, source_target_pairs={{0,8},{4,12},{8,0},{12,4},{1,9},{5,13},{9,1},{13,5},{2,10},{6,14},... | collective-permute-start | bytes 1376264 | tf_op jit(solution)/shard_map/ppermute | solution.py:920
  217.2 27.2 %collective-permute-start.26 = (bf16[8,18,32,128]{3,2,1,0:T(8,128)(2,1)S(1)}, bf16[8,18,32,128]{3,2,1,0:T(8,128)(2,1)S(1)}, u32[]{:S(2)}, u32[]{:S(2)}) collective-permute-start(bf16[8,18,32,128]{3,2,1,0:T(8,128)(2,1)S(1)} %copy-done.7), channel_id=1, source_target_pairs={{0,2},{2,0},{1,3},{3,1},{4,6},{6,4},{5,7},{7,5},{8,10},{10,8},{9,1... | collective-permute-start | bytes 3538952 | tf_op jit(solution)/shard_map/ppermute | solution.py:871
  237.2 81.2 %copy-start.27 = (bf16[4,14,32,128]{3,2,1,0:T(8,128)(2,1)}, bf16[4,14,32,128]{3,2,1,0:T(8,128)(2,1)S(1)}, u32[]{:S(2)}) copy-start(bf16[4,14,32,128]{3,2,1,0:T(8,128)(2,1)S(1)} %collective-permute-done.22.rest_2_) | copy-start | bytes 1376260
  237.2 7.3 %collective-permute-start.25 = (bf16[8,18,32,128]{3,2,1,0:T(8,128)(2,1)S(1)}, bf16[8,18,32,128]{3,2,1,0:T(8,128)(2,1)S(1)}, u32[]{:S(2)}, u32[]{:S(2)}) collective-permute-start(bf16[8,18,32,128]{3,2,1,0:T(8,128)(2,1)S(1)} %collective-permute-done.24.rest_1_), channel_id=1, source_target_pairs={{0,1},{3,2},{4,5},{7,6},{8,9},{11,10},{12,13},{15,14},{16,17},{19,... | collective-permute-start | bytes 3538952 | tf_op jit(solution)/shard_map/ppermute | solution.py:872
  240.0 15.2 %collective-permute-start.21 = (bf16[4,14,32,128]{3,2,1,0:T(8,128)(2,1)}, bf16[4,14,32,128]{3,2,1,0:T(8,128)(2,1)S(1)}, u32[]{:S(2)}, u32[]{:S(2)}) collective-permute-start(bf16[4,14,32,128]{3,2,1,0:T(8,128)(2,1)} %get-tuple-element.98), channel_id=1, source_target_pairs={{0,4},{4,8},{8,12},{12,0},{1,5},{5,9},{9,13},{13,1},{2,6},{6,10},{... | collective-permute-start | bytes 1376264 | tf_op jit(solution)/shard_map/ppermute | solution.py:920
  241.9 22.6 %collective-permute-start.23 = (bf16[4,14,32,128]{3,2,1,0:T(8,128)(2,1)}, bf16[4,14,32,128]{3,2,1,0:T(8,128)(2,1)S(1)}, u32[]{:S(2)}, u32[]{:S(2)}) collective-permute-start(bf16[4,14,32,128]{3,2,1,0:T(8,128)(2,1)} %get-tuple-element.100), channel_id=1, source_target_pairs={{0,12},{4,0},{8,4},{12,8},{1,13},{5,1},{9,5},{13,9},{2,14},{6,2},{... | collective-permute-start | bytes 1376264 | tf_op jit(solution)/shard_map/ppermute | solution.py:920
  255.3 63.1 %copy-start.28 = (bf16[4,14,32,128]{3,2,1,0:T(8,128)(2,1)}, bf16[4,14,32,128]{3,2,1,0:T(8,128)(2,1)S(1)}, u32[]{:S(2)}) copy-start(bf16[4,14,32,128]{3,2,1,0:T(8,128)(2,1)S(1)} %collective-permute-done.21.rest_1_) | copy-start | bytes 1376260
  264.4 15.9 %collective-permute-start.29 = (bf16[4,18,32,128]{3,2,1,0:T(8,128)(2,1)}, bf16[4,18,32,128]{3,2,1,0:T(8,128)(2,1)S(1)}, u32[]{:S(2)}, u32[]{:S(2)}) collective-permute-start(bf16[4,18,32,128]{3,2,1,0:T(8,128)(2,1)} %get-tuple-element.112), channel_id=1, source_target_pairs={{0,12},{4,0},{8,4},{12,8},{1,13},{5,1},{9,5},{13,9},{2,14},{6,2},{... | collective-permute-start | bytes 1769480 | tf_op jit(solution)/shard_map/ppermute | solution.py:920
  265.9 39.8 %collective-permute-start.28 = (bf16[4,18,32,128]{3,2,1,0:T(8,128)(2,1)}, bf16[4,18,32,128]{3,2,1,0:T(8,128)(2,1)S(1)}, u32[]{:S(2)}, u32[]{:S(2)}) collective-permute-start(bf16[4,18,32,128]{3,2,1,0:T(8,128)(2,1)} %get-tuple-element.110), channel_id=1, source_target_pairs={{0,8},{4,12},{8,0},{12,4},{1,9},{5,13},{9,1},{13,5},{2,10},{6,14},... | collective-permute-start | bytes 1769480 | tf_op jit(solution)/shard_map/ppermute | solution.py:920
  267.9 50.4 %collective-permute-start.27 = (bf16[4,18,32,128]{3,2,1,0:T(8,128)(2,1)}, bf16[4,18,32,128]{3,2,1,0:T(8,128)(2,1)S(1)}, u32[]{:S(2)}, u32[]{:S(2)}) collective-permute-start(bf16[4,18,32,128]{3,2,1,0:T(8,128)(2,1)} %get-tuple-element.108), channel_id=1, source_target_pairs={{0,4},{4,8},{8,12},{12,0},{1,5},{5,9},{9,13},{13,1},{2,6},{6,10},{... | collective-permute-start | bytes 1769480 | tf_op jit(solution)/shard_map/ppermute | solution.py:920
  (31 other events, 545.8 us)

commit v8 on v7

--- a/solution.py
+++ b/solution.py
@@ -8,7 +8,8 @@
 from jax.sharding import PartitionSpec as P
 
 norm_epsilon = 1e-05
-vmem_limit = 56 * 1024 * 1024
+mebi = 1024 * 1024
+vmem_limit = 56 * mebi
 
 
 def sigmoid(values):
@@ -414,12 +415,13 @@
     return lax.broadcasted_iota(jnp.int32, shape, 1) // size
 
 
-def spread_weights(w_ref, wide_ref, hidden, size):
+def spread_kernel(size, w_ref, wide_ref):
+    hidden = w_ref.shape[1]
     parts = hidden // size
     for side in range(2):
         for kind in range(2):
             start = (2 * side + kind) * hidden
-            weights = w_ref[0, :, start : start + hidden].astype(jnp.float32)
+            weights = 0.5 * w_ref[0, :, start : start + hidden].astype(jnp.float32)
             group = lane_group(weights.shape, size)
             for part in range(parts):
                 kept = jnp.where(group == part, weights, 0.0)
@@ -429,6 +431,22 @@
                     wide_ref[a * hidden : (a + 1) * hidden, at : at + hidden] = moved.astype(jnp.bfloat16)
 
 
+def spread_weights(w_in, layer, size):
+    hidden = w_in.shape[1]
+    parts = hidden // size
+    shape = (parts * hidden, 4 * parts * hidden)
+    return pl.pallas_call(
+        functools.partial(spread_kernel, size),
+        grid=(1,),
+        in_specs=[pl.BlockSpec((1,) + w_in.shape[1:], lambda s: (layer, 0, 0))],
+        out_specs=pl.BlockSpec(shape, lambda s: (0, 0)),
+        out_shape=jax.ShapeDtypeStruct(shape, jnp.bfloat16),
+        compiler_params=pltpu.CompilerParams(vmem_limit_bytes=16 * mebi),
+        cost_estimate=pl.CostEstimate(flops=1 << 30, bytes_accessed=1 << 20, transcendentals=0),
+        name="spread_weights",
+    )(w_in)
+
+
 def swap_matrix(half):
     shape = (half * half, half * half)
     to, of = lax.broadcasted_iota(jnp.int32, shape, 0), lax.broadcasted_iota(jnp.int32, shape, 1)
@@ -449,18 +467,17 @@
             turned[y : y + half, x : x + half] = swapped(taken[x : x + half, y : y + half], swap_ref)
 
 
-def make_operand(side, taken, row_alive, inner_alive, wide_ref, out_refs, laid, swap_ref):
+def make_operand(side, taken, wide_ref, out_refs, laid, swap_ref):
     rows, size, hidden = taken.shape
     parts, bands, half = hidden // size, size, 16
     groups = rows // parts
     stacked = jnp.concatenate(
         [jnp.concatenate([taken[g * parts + a] for a in range(parts)], axis=1) for g in range(groups)], axis=0
     )
-    mask = (row_alive[:, None, :] * inner_alive[None, :, :]).reshape(groups * size, hidden)
     for part in range(parts):
         at = (side * parts + part) * 2 * hidden
         made = dot(stacked, wide_ref[:, at : at + 2 * hidden])
-        value = mask * sigmoid(made[:, hidden:]) * made[:, :hidden]
+        value = made[:, :hidden] * (1.0 + jnp.tanh(made[:, hidden:]))
         laid[side, :, part * size : (part + 1) * size, :] = value.astype(jnp.bfloat16).reshape(groups, size, hidden)
     blocks = [laid[side, g].T for g in range(groups)]
     starts = [sum(ref.shape[1] for ref in out_refs[:n]) for n in range(len(out_refs))]
@@ -477,59 +494,44 @@
                     ref[0, low - start : high - start, row : row + half] = moved[low - first : high - first]
 
 
-def alive_groups(chain_ref, start, rows, parts):
-    lanes = chain_ref.shape[1]
-    groups = rows // parts
-    line = chain_ref[pl.ds(start // lanes, 1), :] >= 0
-    row = lax.broadcasted_iota(jnp.int32, (groups, lanes), 1) - lax.rem(start, lanes)
-    group = lax.broadcasted_iota(jnp.int32, (groups, lanes), 0)
-    pick = jnp.logical_and(jnp.logical_and(row >= group * parts, row < (group + 1) * parts), line)
-    fold = lax.rem(lax.broadcasted_iota(jnp.int32, (lanes, lanes), 0), parts) == lane_group(
-        (lanes, lanes), lanes // parts
-    )
-    return dot(pick.astype(jnp.float32).astype(jnp.bfloat16), fold.astype(jnp.float32).astype(jnp.bfloat16))
-
-
-def open_layer(layer, natural, chain_ref, row_start, col_start, w_ref, left_refs, right_refs, wide, laid, turned, swap):
-    rows, cols, hidden = natural.shape
-    parts = hidden // rows
+def open_layer(layer, natural, left_refs, right_refs, wide, laid, turned, swap):
     turn(natural, turned, swap)
-    row_mask = alive_groups(chain_ref, row_start, rows, parts), alive_rows(chain_ref, col_start, cols)
-    col_mask = alive_groups(chain_ref, col_start, cols, parts), alive_rows(chain_ref, row_start, rows)
     for side, refs in ((0, left_refs), (1, right_refs)):
-        if side == layer % 2:
-            make_operand(side, natural, *row_mask, wide, refs, laid, swap)
-        else:
-            make_operand(side, turned[...], *col_mask, wide, refs, laid, swap)
-
-
-def open_kernel(hidden, chunks, n_chan, n_sub, base, of, ids, blocks, pair_ref, chain_ref, w_ref, *rest):
-    gate_ref, *operand_refs, norm_ref, wide, laid, turned, swap = rest[-(2 * chunks + 6) :]
+        make_operand(side, natural if side == layer % 2 else turned[...], wide, refs, laid, swap)
+
+
+def norm_and_gate(values, row_alive, col_alive, w_ref, at, norm_ref, gate_ref):
+    _, cols, channels = norm_ref.shape
+    rows = values.shape[0] // cols
+    normed = layer_norm(values)
+    gate = sigmoid(dot(normed.astype(jnp.bfloat16), w_ref[0, :, -channels:]))
+    gate_ref[0, pl.ds(at, rows)] = gate.reshape(rows, cols, channels)
+    mask = row_alive[at : at + rows, None, :] * col_alive[None, :, :]
+    norm_ref[pl.ds(at, rows)] = (normed.reshape(rows, cols, channels) * mask).astype(jnp.bfloat16)
+
+
+def open_kernel(hidden, chunks, n_chan, n_sub, base, of, ids, blocks, pair_ref, chain_ref, w_ref, wide, *rest):
+    gate_ref, *operand_refs, norm_ref, laid, turned, swap = rest[-(2 * chunks + 5) :]
     step = pl.program_id(0)
     _, rows, cols, channels = pair_ref.shape
     block = ids[0] * of + base + step
 
     @pl.when(step == 0)
     def _():
-        spread_weights(w_ref, wide, hidden, cols)
         swap[...] = swap_matrix(16)
 
+    row_alive = alive_rows(chain_ref, (blocks[0, block] * n_chan + ids[1]) * rows, rows)
+    col_alive = alive_rows(chain_ref, (blocks[1, block] * n_sub + ids[2]) * cols, cols)
     group = hidden // cols
-    for start in range(0, rows, group):
-        at = pl.ds(start, group)
-        normed = layer_norm(pair_ref[0, at].reshape(group * cols, channels)).astype(jnp.bfloat16)
-        gate = sigmoid(dot(normed, w_ref[0, :, 4 * hidden :]))
-        gate_ref[0, at] = gate.reshape(group, cols, channels)
-        norm_ref[at] = normed.reshape(group, cols, channels)
-    starts = (blocks[0, block] * n_chan + ids[1]) * rows, (blocks[1, block] * n_sub + ids[2]) * cols
-    lefts, rights = operand_refs[:chunks], operand_refs[chunks:]
-    open_layer(0, norm_ref[...], chain_ref, *starts, w_ref, lefts, rights, wide, laid, turned, swap)
+    for at in range(0, rows, group):
+        values = pair_ref[0, pl.ds(at, group)].reshape(group * cols, channels)
+        norm_and_gate(values, row_alive, col_alive, w_ref, at, norm_ref, gate_ref)
+    open_layer(0, norm_ref[...], operand_refs[:chunks], operand_refs[chunks:], wide, laid, turned, swap)
 
 
 def operand_scratch(rows, size, hidden):
     parts = hidden // size
     return [
-        pltpu.VMEM((parts * hidden, 4 * parts * hidden), jnp.bfloat16),
         pltpu.VMEM((2, rows // parts, parts * size, hidden), jnp.bfloat16),
         pltpu.VMEM((size, rows, hidden), jnp.bfloat16),
         pltpu.VMEM((256, 256), jnp.bfloat16),
@@ -557,10 +559,10 @@
     return [earlier[n] for n in shared], specs, {n_before + k: n for k, n in enumerate(shared)}
 
 
-def open_operands(ids, blocks, pair, chains, w_in, hidden, bands, base, count, earlier):
+def open_operands(ids, blocks, pair, chains, w_in, wide, hidden, bands, base, count, earlier):
     slots, rows, cols, channels = pair.shape
     out_shape = [jax.ShapeDtypeStruct(pair.shape, jnp.float32)] + operand_outputs(slots, count, rows, hidden, bands)
-    more, more_specs, aliases = fill(out_shape, earlier, slots, 5)
+    more, more_specs, aliases = fill(out_shape, earlier, slots, 6)
     return pl.pallas_call(
         functools.partial(open_kernel, hidden, len(bands), lax.axis_size("chan"), lax.axis_size("sub"), base, slots),
         grid_spec=pltpu.PrefetchScalarGridSpec(
@@ -570,6 +572,7 @@
             + [
                 pl.BlockSpec(chains.shape, lambda s, *_: (0, 0)),
                 pl.BlockSpec((1,) + w_in.shape[1:], lambda s, *_: (0, 0, 0)),
+                pl.BlockSpec(wide.shape, lambda s, *_: (0, 0)),
             ]
             + more_specs,
             out_specs=slot_specs(out_shape, slots, base),
@@ -577,10 +580,10 @@
         ),
         out_shape=out_shape,
         input_output_aliases=aliases,
-        compiler_params=pltpu.CompilerParams(vmem_limit_bytes=vmem_limit),
+        compiler_params=pltpu.CompilerParams(vmem_limit_bytes=28 * mebi),
         cost_estimate=pl.CostEstimate(flops=1 << 33, bytes_accessed=1 << 20, transcendentals=0),
         name="open_operands",
-    )(ids, blocks, pair, chains, w_in, *more)
+    )(ids, blocks, pair, chains, w_in, wide, *more)
 
 
 def plan_kernel(n_blk, slots_dev, terms, capacity, ids, owners, slots, chosen, place, seen):
@@ -706,7 +709,7 @@
             ],
         ),
         out_shape=[jax.ShapeDtypeStruct((capacity, bands, rows, hidden), jnp.bfloat16)] * len(shifts),
-        compiler_params=pltpu.CompilerParams(vmem_limit_bytes=vmem_limit),
+        compiler_params=pltpu.CompilerParams(vmem_limit_bytes=14 * mebi),
         cost_estimate=pl.CostEstimate(
             flops=2 * count * bands * rows * hidden * hidden * halves, bytes_accessed=1, transcendentals=0
         ),
@@ -721,9 +724,9 @@
     if last:
         out_ref, held, wide_out, sems, swap = rest[3:]
     else:
-        chain_ref, w_ref = rest[3:5]
-        out_ref, next_gate_ref, *operand_refs, held, wide_out, sems, norm_ref, wide, laid, turned, swap = rest[
-            -(2 * chunks + 10) :
+        chain_ref, w_ref, wide = rest[3:6]
+        out_ref, next_gate_ref, *operand_refs, held, wide_out, sems, norm_ref, laid, turned, swap = rest[
+            -(2 * chunks + 9) :
         ]
         left_refs, right_refs = operand_refs[:chunks], operand_refs[chunks:]
     step = pl.program_id(0)
@@ -749,11 +752,13 @@
                     0, part * bands : (part + 1) * bands, :
                 ]
         swap[...] = swap_matrix(16)
-        if not last:
-            spread_weights(w_ref, wide, hidden, rows)
         for n in range(n_parts):
             arrival(n).wait()
 
+    if not last:
+        block = ids[0] * of + base + step
+        row_alive = alive_rows(chain_ref, (blocks[0, block] * n_chan + ids[1]) * rows, rows)
+        col_alive = alive_rows(chain_ref, (blocks[1, block] * n_sub + ids[2]) * cols, cols)
     half = 16
     by_row = [[] for _ in range(rows)]
     for row in range(0, rows, half):
@@ -792,20 +797,13 @@
         result = (current + gate * change).astype(jnp.bfloat16)
         out_ref[0, taken] = result.reshape(parts, cols, channels)
         if not last:
-            norm = layer_norm(result).astype(jnp.bfloat16)
-            norm_ref[taken] = norm.reshape(parts, cols, channels)
-            next_gate = sigmoid(dot(norm, w_ref[0, :, 4 * hidden :]))
-            next_gate_ref[0, taken] = next_gate.reshape(parts, cols, channels)
+            norm_and_gate(result, row_alive, col_alive, w_ref, g * parts, norm_ref, next_gate_ref)
     if not last:
-        block = ids[0] * of + base + step
-        starts = (blocks[0, block] * n_chan + ids[1]) * rows, (blocks[1, block] * n_sub + ids[2]) * cols
-        open_layer(
-            layer + 1, norm_ref[...], chain_ref, *starts, w_ref, left_refs, right_refs, wide, laid, turned, swap
-        )
+        open_layer(layer + 1, norm_ref[...], left_refs, right_refs, wide, laid, turned, swap)
 
 
 def close_layer(
-    layer, arrived, ids, blocks, place, current, gate, w_out, capacity, terms, chains, w_in, last, bands, base, count, earlier
+    layer, arrived, ids, blocks, place, current, gate, w_out, capacity, terms, chains, w_in, wide, last, bands, base, count, earlier
 ):
     n_blk = len(arrived[0])
     flat = [part for chunk in arrived for part in chunk]
@@ -825,8 +823,9 @@
         pltpu.SemaphoreType.DMA((len(flat),)),
     ]
     if not last:
-        operands += [chains, w_in]
+        operands += [chains, w_in, wide]
         in_specs += [pl.BlockSpec(chains.shape, lambda s, *_: (0, 0)), layer_spec(w_in, layer + 1)]
+        in_specs += [pl.BlockSpec(wide.shape, lambda s, *_: (0, 0))]
         out_shape += [jax.ShapeDtypeStruct(current.shape, jnp.float32)]
         out_shape += operand_outputs(slots, count, cols, hidden, bands[layer + 1])
         scratch += [pltpu.VMEM((rows, cols, channels), jnp.bfloat16)] + operand_scratch(cols, rows, hidden)
@@ -847,7 +846,7 @@
         ),
         out_shape=out_shape,
         input_output_aliases=aliases,
-        compiler_params=pltpu.CompilerParams(vmem_limit_bytes=vmem_limit),
+        compiler_params=pltpu.CompilerParams(vmem_limit_bytes=32 * mebi),
         cost_estimate=pl.CostEstimate(flops=1 << 33, bytes_accessed=1 << 20, transcendentals=0),
         name="close_layer",
     )(ids, blocks, place, *operands, *more)
@@ -887,9 +886,9 @@
     for layer in range(layers):
         count = len(bands[layer])
         if layer == 0:
-            calls = [None]
+            calls, wide = [None], spread_weights(w_in, 0, cols)
             for base, size in halves:
-                calls.append(open_operands(ids, blocks, pair, chains, w_in, hidden, bands[0], base, size, calls[-1]))
+                calls.append(open_operands(ids, blocks, pair, chains, w_in, wide, hidden, bands[0], base, size, calls[-1]))
             gate = calls[-1][0]
         operands = [call[-2 * count :] for call in calls[1:]]
         exchange = exchange_bands_incoming if layer % 2 else exchange_bands_outgoing
@@ -902,6 +901,9 @@
                     if exchanged and layer % 2:
                         (_, (one, _)), (_, (other, _)) = exchanged[-1]
                         left, right = lax.optimization_barrier((left, right, one, other))[:2]
+                    elif exchanged:
+                        ((other, _), _), ((one, _), (_, two)) = exchanged[-1]
+                        left, right = lax.optimization_barrier((left, right, other, one, two))[:2]
                     exchanged.append(exchange(left, right, over))
             else:
                 left, right = operands[-1][chunk], operands[-1][count + chunk]
@@ -922,10 +924,12 @@
             arrived.append(parts)
         last = layer == layers - 1
         calls = [None]
+        if not last:
+            wide = spread_weights(after(w_in, made[-1]), layer + 1, cols)
         for base, size in [(0, slots)] if last else halves:
             calls.append(
                 close_layer(
-                    *(layer, arrived, ids, blocks, place, current, gate, w_out, capacity, terms, chains, w_in, last),
+                    *(layer, arrived, ids, blocks, place, current, gate, w_out, capacity, terms, chains, w_in, wide, last),
                     *(bands, base, size, calls[-1]),
                 )
             )

time: 334 us -> 325 us (0.973)
  Pallas kernels: 102 us -> 83.5 us
  waiting for transfers between devices: 177 us -> 184 us
  local copies, waits for them, and re-layouts: 6.46 us -> 10.5 us
    pallas_call x3, Pallas kernels: 45.1 us -> 34.1 us  [close_layer(): pl.pallas_call(functools.partial(close_kernel, *(layer, last, len(flat),...]
    pallas_call x2, Pallas kernels: 22.3 us -> 17.2 us  [open_operands(): pl.pallas_call(functools.partial(open_kernel, hidden, len(bands), lax.axi...]
    ppermute x12, waiting for transfers between devices: 133 us -> 137 us  [banded(): lax.ppermute(part, 'blk', [(p, (p + shift) % n_blk) for p in range(n_blk)])]
    unnamed x66 -> x44, local copies, waits for them, and re-layouts: 6.46 us -> 10.5 us
    pallas_call x4, Pallas kernels: 33.1 us -> 29.4 us  [banded_products(): pl.pallas_call(functools.partial(banded_kernel, shifts, capacity, tuple(p...]
  transfers between devices with their start and end apart: 30 -> 30, of which waited for: 14 -> 18; matrix products, arithmetic and copies ran while one was open for 0% -> 0% of each run, Pallas kernels for 16% -> 14%
where the time goes in v8:
time: 325 us; the launch traced here: 323 us
  waiting for transfers between devices  184 us (57%)
  Pallas kernels  83.5 us (26%)
  starting transfers between devices  44.7 us (14%)
  local copies, waits for them, and re-layouts  10.5 us (3%)
    ppermute x12, waiting for transfers between devices, banded(): lax.ppermute(part, 'blk', [(p, (p + shift) % n_blk) for p in range(n_blk)])  137 us
    pallas_call x3, Pallas kernels, close_layer(): pl.pallas_call(functools.partial(close_kernel, *(layer, last, len(flat),...  34.1 us
    ppermute x3, waiting for transfers between devices, exchange_bands_outgoing(): one = lax.ppermute(right, both, [(0, 2), (3, 1), (1, 0), (2, 3)])  30.9 us
    pallas_call x4, Pallas kernels, banded_products(): pl.pallas_call(functools.partial(banded_kernel, shifts, capacity, tuple(p...  29.4 us
    pallas_call x2, Pallas kernels, open_operands(): pl.pallas_call(functools.partial(open_kernel, hidden, len(bands), lax.axi...  17.2 us
    ppermute x12, starting transfers between devices, banded(): lax.ppermute(part, 'blk', [(p, (p + shift) % n_blk) for p in range(n_blk)])  15.9 us
    ppermute x3, starting transfers between devices, exchange_bands_incoming(): two = lax.ppermute(after(one, over), both, [(0, 1), (3, 2)])  11.8 us
    unnamed x44, local copies, waits for them, and re-layouts  10.5 us
  transfers between devices with their start and end apart: 30, of which 18 were waited for; matrix products, arithmetic and copies ran while one was open for 0% of the time, Pallas kernels for 14%

profile of v8, /device:TPU:11, one launch (start us, length us, event | category | flops | bytes accessed | tf_op | source)
XLA Modules:
  0.0 322.9 jit_solution(13672713323708306652)
XLA Ops:
  2.6 8.3 %open_operands.2 = (f32[8,32,32,128]{3,2,1,0:T(8,128)S(1)}, bf16[4,12,32,128]{3,2,1,0:T(8,128)(2,1)S(1)}, bf16[8,20,32,128]{3,2,1,0:T(8,128)(2,1)S(1)}, bf16[4,1...) custom-call(s32[4]{0:T(128)S(1)} %pad_add_fusion.ids, s32[2,32]{1,0:T(2,128)S(1)} %bitcast.12, ...), custom_call_target="tpu_custom_call" | custom-call | flops 8589934592 | bytes 1048576 | tf_op jit(solution)/shard_map/open_operands/pallas_call | solution.py:566
  11.6 3.3 %collective-permute-start.1 = (bf16[4,12,32,128]{3,2,1,0:T(8,128)(2,1)S(1)}, bf16[4,12,32,128]{3,2,1,0:T(8,128)(2,1)S(1)}, u32[]{:S(2)}, u32[]{:S(2)}) collective-permute-start(bf16[4,12,32,128]{3,2,1,0:T(8,128)(2,1)S(1)} %get-tuple-element.66.rest_3_), channel_id=1, source_target_pairs={{0,2},{3,1},{1,0},{2,3},{4,6},{7,5},{5,4},{6,7},{8,10},{11,9},{9,8... | collective-permute-start | bytes 1179656 | tf_op jit(solution)/shard_map/ppermute | solution.py:862
  14.9 9.0 %open_operands.3 = (f32[8,32,32,128]{3,2,1,0:T(8,128)S(1)}, bf16[4,12,32,128]{3,2,1,0:T(8,128)(2,1)}, bf16[8,20,32,128]{3,2,1,0:T(8,128)(2,1)S(1)}, bf16[4,12,32...) custom-call(s32[4]{0:T(128)S(1)} %pad_add_fusion.ids, ...), custom_call_target="tpu_custom_call", output_to_operand_aliasing={{0}: (6, {}), {2}: (7, {}), {4}: (8, {})} | custom-call | flops 8589934592 | bytes 1048576 | tf_op jit(solution)/shard_map/open_operands/pallas_call | solution.py:566
  23.8 2.0 copy-done.20
  33.5 6.8 %collective-permute-done.4.rest_7_ = bf16[4,12,32,128]{3,2,1,0:T(8,128)(2,1)} collective-permute-done((bf16[4,12,32,128]{3,2,1,0:T(8,128)(2,1)}, bf16[4,12,32,128]{3,2,1,0:T(8,128)(2,1)}, u32[]{:S(2)}, u32[]{:S(2)}) %collective-permute-start.4) | collective-permute-done | bytes 393248 | tf_op jit(solution)/shard_map/ppermute | solution.py:862
  44.6 7.5 %banded_products.4 = (bf16[4,12,32,128]{3,2,1,0:T(8,128)(2,1)S(1)}, bf16[4,12,32,128]{3,2,1,0:T(8,128)(2,1)S(1)}, bf16[4,12,32,128]{3,2,1,0:T(8,128)(2,1)S(1)}, bf16[4,12,32,128]{3,2,1,0:T(8,128)(2,1)S(1)}) custom-call(s32[4]{0:T(128)S(1)} %copy-done.7, s32[40]{0:T(128)S(1)} %copy-done.9, bf16[4,12,32,128]{3,2,1,0:T(8,128)(2,1)S(1)} %copy-done.5, ...), custom_call_target="tpu_custom_call" | custom-call | flops 402653184 | bytes 1 | tf_op jit(solution)/shard_map/banded_products/pallas_call | solution.py:696
  54.7 2.6 collective-permute-start.10
  61.1 24.1 %collective-permute-done.10.rest_2_ = bf16[8,20,32,128]{3,2,1,0:T(8,128)(2,1)S(1)} collective-permute-done((bf16[8,20,32,128]{3,2,1,0:T(8,128)(2,1)S(1)}, bf16[8,20,32,128]{3,2,1,0:T(8,128)(2,1)S(1)}, u32[]{:S(2)}, u32[]{:S(2)}) %collective-permute-start.10) | collective-permute-done | bytes 1310752 | tf_op jit(solution)/shard_map/ppermute | solution.py:862
  85.2 6.9 %banded_products.5 = (bf16[4,20,32,128]{3,2,1,0:T(8,128)(2,1)S(1)}, bf16[4,20,32,128]{3,2,1,0:T(8,128)(2,1)S(1)}, bf16[4,20,32,128]{3,2,1,0:T(8,128)(2,1)S(1)}, bf16[4,20,32,128]{3,2,1,0:T(8,128)(2,1)S(1)}) custom-call(s32[4]{0:T(128)S(1)} %copy-done.7, s32[40]{0:T(128)S(1)} %copy-done.9, bf16[8,20,32,128]{3,2,1,0:T(8,128)(2,1)S(1)} %collective-permute-done.9.rest_0_, ...), custom_call_target="tpu_custom_call" | custom-call | flops 671088640 | bytes 1 | tf_op jit(solution)/shard_map/banded_products/pallas_call | solution.py:696
  95.3 2.4 collective-permute-start.12
  98.2 13.0 %collective-permute-done.14.rest_7_ = bf16[4,20,32,128]{3,2,1,0:T(8,128)(2,1)S(1)} collective-permute-done((bf16[4,20,32,128]{3,2,1,0:T(8,128)(2,1)S(1)}, bf16[4,20,32,128]{3,2,1,0:T(8,128)(2,1)S(1)}, u32[]{:S(2)}, u32[]{:S(2)}) %collective-permute-start.14) | collective-permute-done | bytes 655392 | tf_op jit(solution)/shard_map/ppermute | solution.py:922
  111.2 25.7 %collective-permute-done.13.rest_6_ = bf16[4,20,32,128]{3,2,1,0:T(8,128)(2,1)S(1)} collective-permute-done((bf16[4,20,32,128]{3,2,1,0:T(8,128)(2,1)S(1)}, bf16[4,20,32,128]{3,2,1,0:T(8,128)(2,1)S(1)}, u32[]{:S(2)}, u32[]{:S(2)}) %collective-permute-start.13) | collective-permute-done | bytes 655392 | tf_op jit(solution)/shard_map/ppermute | solution.py:922
  136.9 14.0 %collective-permute-done.12.rest_5_ = bf16[4,20,32,128]{3,2,1,0:T(8,128)(2,1)S(1)} collective-permute-done((bf16[4,20,32,128]{3,2,1,0:T(8,128)(2,1)S(1)}, bf16[4,20,32,128]{3,2,1,0:T(8,128)(2,1)S(1)}, u32[]{:S(2)}, u32[]{:S(2)}) %collective-permute-start.12) | collective-permute-done | bytes 655392 | tf_op jit(solution)/shard_map/ppermute | solution.py:922
  151.0 12.5 %close_layer.3 = (bf16[8,32,32,128]{3,2,1,0:T(8,128)(2,1)S(1)}, f32[8,32,32,128]{3,2,1,0:T(8,128)S(1)}, bf16[4,14,32,128]{3,2,1,0:T(8,128)(2,1)S(1)}, bf16[8,18,...) custom-call(s32[4]{0:T(128)S(1)} %copy-done.8, ...), custom_call_target="tpu_custom_call" | custom-call | flops 8589934592 | bytes 1048576 | tf_op jit(solution)/shard_map/close_layer/pallas_call | solution.py:835
  166.0 12.6 %close_layer.4 = (bf16[8,32,32,128]{3,2,1,0:T(8,128)(2,1)S(1)}, f32[8,32,32,128]{3,2,1,0:T(8,128)S(1)}, bf16[4,14,32,128]{3,2,1,0:T(8,128)(2,1)S(1)}, bf16[8,18,...) custom-call(s32[4]{0:T(128)S(1)} %copy-done.8, ...), custom_call_target="tpu_custom_call", output_to_operand_aliasing={{0}: (17, {}), {1}: (18, {}), {3}: (19, {}), {5}: (20, {})} | custom-call | flops 8589934592 | bytes 1048576 | tf_op jit(solution)/shard_map/close_layer/pallas_call | solution.py:835
  178.6 3.0 collective-permute-done.17.rest_4_
  183.1 8.0 %collective-permute-done.18.rest_6_ = bf16[4,14,32,128]{3,2,1,0:T(8,128)(2,1)S(1)} collective-permute-done((bf16[4,14,32,128]{3,2,1,0:T(8,128)(2,1)S(1)}, bf16[4,14,32,128]{3,2,1,0:T(8,128)(2,1)S(1)}, u32[]{:S(2)}, u32[]{:S(2)}) %collective-permute-start.18) | collective-permute-done | bytes 458784 | tf_op jit(solution)/shard_map/ppermute | solution.py:869
  191.1 4.6 %collective-permute-start.19 = (bf16[4,14,32,128]{3,2,1,0:T(8,128)(2,1)S(1)}, bf16[4,14,32,128]{3,2,1,0:T(8,128)(2,1)S(1)}, u32[]{:S(2)}, u32[]{:S(2)}) collective-permute-start(bf16[4,14,32,128]{3,2,1,0:T(8,128)(2,1)S(1)} %collective-permute-done.18.rest_6_), channel_id=1, source_target_pairs={{0,1},{3,2},{4,5},{7,6},{8,9},{11,10},{12,13},{15,14},{16,17},{19,... | collective-permute-start | bytes 1376264 | tf_op jit(solution)/shard_map/ppermute | solution.py:871
  195.8 3.0 collective-permute-done.20.rest_9_
  198.8 4.4 %collective-permute-start.16 = (bf16[4,14,32,128]{3,2,1,0:T(8,128)(2,1)S(1)}, bf16[4,14,32,128]{3,2,1,0:T(8,128)(2,1)S(1)}, u32[]{:S(2)}, u32[]{:S(2)}) collective-permute-start(bf16[4,14,32,128]{3,2,1,0:T(8,128)(2,1)S(1)} %collective-permute-done.15.rest_1_), channel_id=1, source_target_pairs={{0,1},{3,2},{4,5},{7,6},{8,9},{11,10},{12,13},{15,14},{16,17},{19,... | collective-permute-start | bytes 1376264 | tf_op jit(solution)/shard_map/ppermute | solution.py:871
  204.6 8.2 %banded_products.6 = (bf16[4,14,32,128]{3,2,1,0:T(8,128)(2,1)S(1)}, bf16[4,14,32,128]{3,2,1,0:T(8,128)(2,1)S(1)}, bf16[4,14,32,128]{3,2,1,0:T(8,128)(2,1)S(1)}, bf16[4,14,32,128]{3,2,1,0:T(8,128)(2,1)S(1)}) custom-call(s32[4]{0:T(128)S(1)} %copy-done.8, s32[40]{0:T(128)S(1)} %copy-done.10, bf16[4,14,32,128]{3,2,1,0:T(8,128)(2,1)S(1)} %get-tuple-element.91.rest_0_, ...), custom_call_target="tpu_custom_call" | custom-call | flops 469762048 | bytes 1 | tf_op jit(solution)/shard_map/banded_products/pallas_call | solution.py:696
  212.9 19.6 %collective-permute-done.22.rest_2_ = bf16[4,14,32,128]{3,2,1,0:T(8,128)(2,1)S(1)} collective-permute-done((bf16[4,14,32,128]{3,2,1,0:T(8,128)(2,1)S(1)}, bf16[4,14,32,128]{3,2,1,0:T(8,128)(2,1)S(1)}, u32[]{:S(2)}, u32[]{:S(2)}) %collective-permute-start.22) | collective-permute-done | bytes 458784 | tf_op jit(solution)/shard_map/ppermute | solution.py:922
  232.5 2.9 collective-permute-start.25
  235.3 2.4 collective-permute-start.21
  240.1 6.9 %banded_products.7 = (bf16[4,18,32,128]{3,2,1,0:T(8,128)(2,1)S(1)}, bf16[4,18,32,128]{3,2,1,0:T(8,128)(2,1)S(1)}, bf16[4,18,32,128]{3,2,1,0:T(8,128)(2,1)S(1)}, bf16[4,18,32,128]{3,2,1,0:T(8,128)(2,1)S(1)}) custom-call(s32[4]{0:T(128)S(1)} %copy-done.8, s32[40]{0:T(128)S(1)} %copy-done.10, bf16[8,18,32,128]{3,2,1,0:T(8,128)(2,1)S(1)} %get-tuple-element.109.rest_0_, ...), custom_call_target="tpu_custom_call" | custom-call | flops 603979776 | bytes 1 | tf_op jit(solution)/shard_map/banded_products/pallas_call | solution.py:696
  246.9 3.8 %collective-permute-done.21.rest_1_ = bf16[4,14,32,128]{3,2,1,0:T(8,128)(2,1)S(1)} collective-permute-done((bf16[4,14,32,128]{3,2,1,0:T(8,128)(2,1)S(1)}, bf16[4,14,32,128]{3,2,1,0:T(8,128)(2,1)S(1)}, u32[]{:S(2)}, u32[]{:S(2)}) %collective-permute-start.21) | collective-permute-done | bytes 458784 | tf_op jit(solution)/shard_map/ppermute | solution.py:922
  250.7 9.4 %collective-permute-done.23.rest_3_ = bf16[4,14,32,128]{3,2,1,0:T(8,128)(2,1)S(1)} collective-permute-done((bf16[4,14,32,128]{3,2,1,0:T(8,128)(2,1)S(1)}, bf16[4,14,32,128]{3,2,1,0:T(8,128)(2,1)S(1)}, u32[]{:S(2)}, u32[]{:S(2)}) %collective-permute-start.23) | collective-permute-done | bytes 458784 | tf_op jit(solution)/shard_map/ppermute | solution.py:922
  261.7 2.1 collective-permute-start.28
  264.2 11.7 %collective-permute-done.29.rest_7_ = bf16[4,18,32,128]{3,2,1,0:T(8,128)(2,1)S(1)} collective-permute-done((bf16[4,18,32,128]{3,2,1,0:T(8,128)(2,1)S(1)}, bf16[4,18,32,128]{3,2,1,0:T(8,128)(2,1)S(1)}, u32[]{:S(2)}, u32[]{:S(2)}) %collective-permute-start.29) | collective-permute-done | bytes 589856 | tf_op jit(solution)/shard_map/ppermute | solution.py:922
  275.9 25.2 %collective-permute-done.28.rest_6_ = bf16[4,18,32,128]{3,2,1,0:T(8,128)(2,1)S(1)} collective-permute-done((bf16[4,18,32,128]{3,2,1,0:T(8,128)(2,1)S(1)}, bf16[4,18,32,128]{3,2,1,0:T(8,128)(2,1)S(1)}, u32[]{:S(2)}, u32[]{:S(2)}) %collective-permute-start.28) | collective-permute-done | bytes 589856 | tf_op jit(solution)/shard_map/ppermute | solution.py:922
  301.1 12.6 %collective-permute-done.27.rest_5_ = bf16[4,18,32,128]{3,2,1,0:T(8,128)(2,1)S(1)} collective-permute-done((bf16[4,18,32,128]{3,2,1,0:T(8,128)(2,1)S(1)}, bf16[4,18,32,128]{3,2,1,0:T(8,128)(2,1)S(1)}, u32[]{:S(2)}, u32[]{:S(2)}) %collective-permute-start.27) | collective-permute-done | bytes 589856 | tf_op jit(solution)/shard_map/ppermute | solution.py:922
  313.8 9.0 %close_layer.5 = bf16[8,32,32,128]{3,2,1,0:T(8,128)(2,1)} custom-call(s32[4]{0:T(128)S(1)} %copy-done.8, s32[2,32]{1,0:T(2,128)S(1)} %bitcast.16, s32[16]{0:T(128)S(1)} %copy-done.19, bf16[4,14,32,128]{3,2,1,0:T(8,128)(2,1)S(1)} %get-tuple-element.103.rest_0_, bf16[4,14,32,128]{3,2,1,0:T(8,128)(2,1)S(1)} %collective-permute-done.21.rest_1_, ...), custom_call_target="tpu_custom_call" | custom-call | flops 8589934592 | bytes 1048576 | tf_op jit(solution)/shard_map/close_layer/pallas_call | solution.py:835
  (85 shorter events, 35.4 us)
Async XLA Ops:
  10.9 15.7 %collective-permute-start.2 = (bf16[4,12,32,128]{3,2,1,0:T(8,128)(2,1)S(1)}, bf16[4,12,32,128]{3,2,1,0:T(8,128)(2,1)S(1)}, u32[]{:S(2)}, u32[]{:S(2)}) collective-permute-start(bf16[4,12,32,128]{3,2,1,0:T(8,128)(2,1)S(1)} %get-tuple-element.66.rest_3_), channel_id=1, source_target_pairs={{1,2},{2,1},{5,6},{6,5},{9,10},{10,9},{13,14},{14,13},{17,18},{18,... | collective-permute-start | bytes 1179656 | tf_op jit(solution)/shard_map/ppermute | solution.py:863
  11.6 15.7 %collective-permute-start.1 = (bf16[4,12,32,128]{3,2,1,0:T(8,128)(2,1)S(1)}, bf16[4,12,32,128]{3,2,1,0:T(8,128)(2,1)S(1)}, u32[]{:S(2)}, u32[]{:S(2)}) collective-permute-start(bf16[4,12,32,128]{3,2,1,0:T(8,128)(2,1)S(1)} %get-tuple-element.66.rest_3_), channel_id=1, source_target_pairs={{0,2},{3,1},{1,0},{2,3},{4,6},{7,5},{5,4},{6,7},{8,10},{11,9},{9,8... | collective-permute-start | bytes 1179656 | tf_op jit(solution)/shard_map/ppermute | solution.py:862
  14.8 11.0 %collective-permute-start = (bf16[4,12,32,128]{3,2,1,0:T(8,128)(2,1)S(1)}, bf16[4,12,32,128]{3,2,1,0:T(8,128)(2,1)S(1)}, u32[]{:S(2)}, u32[]{:S(2)}) collective-permute-start(bf16[4,12,32,128]{3,2,1,0:T(8,128)(2,1)S(1)} %get-tuple-element.65.rest_1_), channel_id=1, source_target_pairs={{0,1},{1,0},{2,3},{3,2},{4,5},{5,4},{6,7},{7,6},{8,9},{9,8},{10,11... | collective-permute-start | bytes 1179656 | tf_op jit(solution)/shard_map/ppermute | solution.py:861
  28.0 5.5 %collective-permute-start.3 = (bf16[4,12,32,128]{3,2,1,0:T(8,128)(2,1)}, bf16[4,12,32,128]{3,2,1,0:T(8,128)(2,1)}, u32[]{:S(2)}, u32[]{:S(2)}) collective-permute-start(bf16[4,12,32,128]{3,2,1,0:T(8,128)(2,1)} %get-tuple-element.72.rest_6_), channel_id=1, source_target_pairs={{0,1},{1,0},{2,3},{3,2},{4,5},{5,4},{6,7},{7,6},{8,9},{9,8},{10,11... | collective-permute-start | bytes 1179656 | tf_op jit(solution)/shard_map/ppermute | solution.py:861
  28.5 5.0 %collective-permute-start.5 = (bf16[4,12,32,128]{3,2,1,0:T(8,128)(2,1)}, bf16[4,12,32,128]{3,2,1,0:T(8,128)(2,1)}, u32[]{:S(2)}, u32[]{:S(2)}) collective-permute-start(bf16[4,12,32,128]{3,2,1,0:T(8,128)(2,1)} %get-tuple-element.73.rest_8_), channel_id=1, source_target_pairs={{1,2},{2,1},{5,6},{6,5},{9,10},{10,9},{13,14},{14,13},{17,18},{18,... | collective-permute-start | bytes 1179656 | tf_op jit(solution)/shard_map/ppermute | solution.py:863
  30.0 10.4 %collective-permute-start.4 = (bf16[4,12,32,128]{3,2,1,0:T(8,128)(2,1)}, bf16[4,12,32,128]{3,2,1,0:T(8,128)(2,1)}, u32[]{:S(2)}, u32[]{:S(2)}) collective-permute-start(bf16[4,12,32,128]{3,2,1,0:T(8,128)(2,1)} %get-tuple-element.73.rest_8_), channel_id=1, source_target_pairs={{0,2},{3,1},{1,0},{2,3},{4,6},{7,5},{5,4},{6,7},{8,10},{11,9},{9,8... | collective-permute-start | bytes 1179656 | tf_op jit(solution)/shard_map/ppermute | solution.py:862
  52.1 7.5 %collective-permute-start.9 = (bf16[8,20,32,128]{3,2,1,0:T(8,128)(2,1)S(1)}, bf16[8,20,32,128]{3,2,1,0:T(8,128)(2,1)S(1)}, u32[]{:S(2)}, u32[]{:S(2)}) collective-permute-start(bf16[8,20,32,128]{3,2,1,0:T(8,128)(2,1)S(1)} %get-tuple-element.80.rest_1_), channel_id=1, source_target_pairs={{0,1},{1,0},{2,3},{3,2},{4,5},{5,4},{6,7},{7,6},{8,9},{9,8},{10,11... | collective-permute-start | bytes 3932168 | tf_op jit(solution)/shard_map/ppermute | solution.py:861
  54.0 7.1 %collective-permute-start.11 = (bf16[8,20,32,128]{3,2,1,0:T(8,128)(2,1)S(1)}, bf16[8,20,32,128]{3,2,1,0:T(8,128)(2,1)S(1)}, u32[]{:S(2)}, u32[]{:S(2)}) collective-permute-start(bf16[8,20,32,128]{3,2,1,0:T(8,128)(2,1)S(1)} %get-tuple-element.81.rest_3_), channel_id=1, source_target_pairs={{1,2},{2,1},{5,6},{6,5},{9,10},{10,9},{13,14},{14,13},{17,18},{18,... | collective-permute-start | bytes 3932168 | tf_op jit(solution)/shard_map/ppermute | solution.py:863
  54.7 30.4 %collective-permute-start.10 = (bf16[8,20,32,128]{3,2,1,0:T(8,128)(2,1)S(1)}, bf16[8,20,32,128]{3,2,1,0:T(8,128)(2,1)S(1)}, u32[]{:S(2)}, u32[]{:S(2)}) collective-permute-start(bf16[8,20,32,128]{3,2,1,0:T(8,128)(2,1)S(1)} %get-tuple-element.81.rest_3_), channel_id=1, source_target_pairs={{0,2},{3,1},{1,0},{2,3},{4,6},{7,5},{5,4},{6,7},{8,10},{11,9},{9,8... | collective-permute-start | bytes 3932168 | tf_op jit(solution)/shard_map/ppermute | solution.py:862
  57.3 34.8 %collective-permute-start.6 = (bf16[4,12,32,128]{3,2,1,0:T(8,128)(2,1)S(1)}, bf16[4,12,32,128]{3,2,1,0:T(8,128)(2,1)S(1)}, u32[]{:S(2)}, u32[]{:S(2)}) collective-permute-start(bf16[4,12,32,128]{3,2,1,0:T(8,128)(2,1)S(1)} %get-tuple-element.75), channel_id=1, source_target_pairs={{0,4},{4,8},{8,12},{12,0},{1,5},{5,9},{9,13},{13,1},{2,6},{6,10},{... | collective-permute-start | bytes 1179656 | tf_op jit(solution)/shard_map/ppermute | solution.py:922
  58.6 33.9 %collective-permute-start.7 = (bf16[4,12,32,128]{3,2,1,0:T(8,128)(2,1)S(1)}, bf16[4,12,32,128]{3,2,1,0:T(8,128)(2,1)S(1)}, u32[]{:S(2)}, u32[]{:S(2)}) collective-permute-start(bf16[4,12,32,128]{3,2,1,0:T(8,128)(2,1)S(1)} %get-tuple-element.76), channel_id=1, source_target_pairs={{0,8},{4,12},{8,0},{12,4},{1,9},{5,13},{9,1},{13,5},{2,10},{6,14},... | collective-permute-start | bytes 1179656 | tf_op jit(solution)/shard_map/ppermute | solution.py:922
  59.6 34.6 %collective-permute-start.8 = (bf16[4,12,32,128]{3,2,1,0:T(8,128)(2,1)S(1)}, bf16[4,12,32,128]{3,2,1,0:T(8,128)(2,1)S(1)}, u32[]{:S(2)}, u32[]{:S(2)}) collective-permute-start(bf16[4,12,32,128]{3,2,1,0:T(8,128)(2,1)S(1)} %get-tuple-element.77), channel_id=1, source_target_pairs={{0,12},{4,0},{8,4},{12,8},{1,13},{5,1},{9,5},{13,9},{2,14},{6,2},{... | collective-permute-start | bytes 1179656 | tf_op jit(solution)/shard_map/ppermute | solution.py:922
  85.2 65.8 %copy-start.21 = (f32[8,32,32,128]{3,2,1,0:T(8,128)S(1)}, f32[8,32,32,128]{3,2,1,0:T(8,128)}, u32[]{:S(2)}) copy-start(f32[8,32,32,128]{3,2,1,0:T(8,128)} %copy-done.20) | copy-start | bytes 12582916
  94.2 17.1 %collective-permute-start.14 = (bf16[4,20,32,128]{3,2,1,0:T(8,128)(2,1)S(1)}, bf16[4,20,32,128]{3,2,1,0:T(8,128)(2,1)S(1)}, u32[]{:S(2)}, u32[]{:S(2)}) collective-permute-start(bf16[4,20,32,128]{3,2,1,0:T(8,128)(2,1)S(1)} %get-tuple-element.88), channel_id=1, source_target_pairs={{0,12},{4,0},{8,4},{12,8},{1,13},{5,1},{9,5},{13,9},{2,14},{6,2},{... | collective-permute-start | bytes 1966088 | tf_op jit(solution)/shard_map/ppermute | solution.py:922
  94.2 42.7 %collective-permute-start.13 = (bf16[4,20,32,128]{3,2,1,0:T(8,128)(2,1)S(1)}, bf16[4,20,32,128]{3,2,1,0:T(8,128)(2,1)S(1)}, u32[]{:S(2)}, u32[]{:S(2)}) collective-permute-start(bf16[4,20,32,128]{3,2,1,0:T(8,128)(2,1)S(1)} %get-tuple-element.86), channel_id=1, source_target_pairs={{0,8},{4,12},{8,0},{12,4},{1,9},{5,13},{9,1},{13,5},{2,10},{6,14},... | collective-permute-start | bytes 1966088 | tf_op jit(solution)/shard_map/ppermute | solution.py:922
  95.3 55.7 %collective-permute-start.12 = (bf16[4,20,32,128]{3,2,1,0:T(8,128)(2,1)S(1)}, bf16[4,20,32,128]{3,2,1,0:T(8,128)(2,1)S(1)}, u32[]{:S(2)}, u32[]{:S(2)}) collective-permute-start(bf16[4,20,32,128]{3,2,1,0:T(8,128)(2,1)S(1)} %get-tuple-element.84), channel_id=1, source_target_pairs={{0,4},{4,8},{8,12},{12,0},{1,5},{5,9},{9,13},{13,1},{2,6},{6,10},{... | collective-permute-start | bytes 1966088 | tf_op jit(solution)/shard_map/ppermute | solution.py:922
  97.7 53.3 %copy-start.19 = (s32[16]{0:T(128)S(1)}, s32[16]{0:T(128)}, u32[]{:S(2)}) copy-start(s32[16]{0:T(128)} %get-tuple-element.63.place) | copy-start | bytes 196
  163.5 15.1 %collective-permute-start.15 = (bf16[4,14,32,128]{3,2,1,0:T(8,128)(2,1)S(1)}, bf16[4,14,32,128]{3,2,1,0:T(8,128)(2,1)S(1)}, u32[]{:S(2)}, u32[]{:S(2)}) collective-permute-start(bf16[4,14,32,128]{3,2,1,0:T(8,128)(2,1)S(1)} %get-tuple-element.91.rest_0_), channel_id=1, source_target_pairs={{1,3},{2,0},{0,1},{3,2},{5,7},{6,4},{4,5},{7,6},{9,11},{10,8},{8,9... | collective-permute-start | bytes 1376264 | tf_op jit(solution)/shard_map/ppermute | solution.py:869
  165.0 16.6 %collective-permute-start.17 = (bf16[4,14,32,128]{3,2,1,0:T(8,128)(2,1)S(1)}, bf16[4,14,32,128]{3,2,1,0:T(8,128)(2,1)S(1)}, u32[]{:S(2)}, u32[]{:S(2)}) collective-permute-start(bf16[4,14,32,128]{3,2,1,0:T(8,128)(2,1)S(1)} %get-tuple-element.98.rest_3_), channel_id=1, source_target_pairs={{0,2},{2,0},{1,3},{3,1},{4,6},{6,4},{5,7},{7,5},{8,10},{10,8},{9,1... | collective-permute-start | bytes 1376264 | tf_op jit(solution)/shard_map/ppermute | solution.py:870
  181.6 9.5 %collective-permute-start.18 = (bf16[4,14,32,128]{3,2,1,0:T(8,128)(2,1)S(1)}, bf16[4,14,32,128]{3,2,1,0:T(8,128)(2,1)S(1)}, u32[]{:S(2)}, u32[]{:S(2)}) collective-permute-start(bf16[4,14,32,128]{3,2,1,0:T(8,128)(2,1)S(1)} %get-tuple-element.100.rest_5_), channel_id=1, source_target_pairs={{1,3},{2,0},{0,1},{3,2},{5,7},{6,4},{4,5},{7,6},{9,11},{10,8},{8,9... | collective-permute-start | bytes 1376264 | tf_op jit(solution)/shard_map/ppermute | solution.py:869
  181.7 17.1 %collective-permute-start.20 = (bf16[4,14,32,128]{3,2,1,0:T(8,128)(2,1)S(1)}, bf16[4,14,32,128]{3,2,1,0:T(8,128)(2,1)S(1)}, u32[]{:S(2)}, u32[]{:S(2)}) collective-permute-start(bf16[4,14,32,128]{3,2,1,0:T(8,128)(2,1)S(1)} %get-tuple-element.102.rest_8_), channel_id=1, source_target_pairs={{0,2},{2,0},{1,3},{3,1},{4,6},{6,4},{5,7},{7,5},{8,10},{10,8},{9,1... | collective-permute-start | bytes 1376264 | tf_op jit(solution)/shard_map/ppermute | solution.py:870
  191.1 7.7 %collective-permute-start.19 = (bf16[4,14,32,128]{3,2,1,0:T(8,128)(2,1)S(1)}, bf16[4,14,32,128]{3,2,1,0:T(8,128)(2,1)S(1)}, u32[]{:S(2)}, u32[]{:S(2)}) collective-permute-start(bf16[4,14,32,128]{3,2,1,0:T(8,128)(2,1)S(1)} %collective-permute-done.18.rest_6_), channel_id=1, source_target_pairs={{0,1},{3,2},{4,5},{7,6},{8,9},{11,10},{12,13},{15,14},{16,17},{19,... | collective-permute-start | bytes 1376264 | tf_op jit(solution)/shard_map/ppermute | solution.py:871
  198.8 33.7 %collective-permute-start.24 = (bf16[8,18,32,128]{3,2,1,0:T(8,128)(2,1)S(1)}, bf16[8,18,32,128]{3,2,1,0:T(8,128)(2,1)S(1)}, u32[]{:S(2)}, u32[]{:S(2)}) collective-permute-start(bf16[8,18,32,128]{3,2,1,0:T(8,128)(2,1)S(1)} %get-tuple-element.109.rest_0_), channel_id=1, source_target_pairs={{1,3},{2,0},{0,1},{3,2},{5,7},{6,4},{4,5},{7,6},{9,11},{10,8},{8,9... | collective-permute-start | bytes 3538952 | tf_op jit(solution)/shard_map/ppermute | solution.py:869
  198.8 5.8 %collective-permute-start.16 = (bf16[4,14,32,128]{3,2,1,0:T(8,128)(2,1)S(1)}, bf16[4,14,32,128]{3,2,1,0:T(8,128)(2,1)S(1)}, u32[]{:S(2)}, u32[]{:S(2)}) collective-permute-start(bf16[4,14,32,128]{3,2,1,0:T(8,128)(2,1)S(1)} %collective-permute-done.15.rest_1_), channel_id=1, source_target_pairs={{0,1},{3,2},{4,5},{7,6},{8,9},{11,10},{12,13},{15,14},{16,17},{19,... | collective-permute-start | bytes 1376264 | tf_op jit(solution)/shard_map/ppermute | solution.py:871
  212.7 19.8 %collective-permute-start.22 = (bf16[4,14,32,128]{3,2,1,0:T(8,128)(2,1)S(1)}, bf16[4,14,32,128]{3,2,1,0:T(8,128)(2,1)S(1)}, u32[]{:S(2)}, u32[]{:S(2)}) collective-permute-start(bf16[4,14,32,128]{3,2,1,0:T(8,128)(2,1)S(1)} %get-tuple-element.105), channel_id=1, source_target_pairs={{0,8},{4,12},{8,0},{12,4},{1,9},{5,13},{9,1},{13,5},{2,10},{6,14},... | collective-permute-start | bytes 1376264 | tf_op jit(solution)/shard_map/ppermute | solution.py:922
  212.8 27.2 %collective-permute-start.26 = (bf16[8,18,32,128]{3,2,1,0:T(8,128)(2,1)S(1)}, bf16[8,18,32,128]{3,2,1,0:T(8,128)(2,1)S(1)}, u32[]{:S(2)}, u32[]{:S(2)}) collective-permute-start(bf16[8,18,32,128]{3,2,1,0:T(8,128)(2,1)S(1)} %get-tuple-element.111.rest_3_), channel_id=1, source_target_pairs={{0,2},{2,0},{1,3},{3,1},{4,6},{6,4},{5,7},{7,5},{8,10},{10,8},{9,1... | collective-permute-start | bytes 3538952 | tf_op jit(solution)/shard_map/ppermute | solution.py:870
  232.5 7.6 %collective-permute-start.25 = (bf16[8,18,32,128]{3,2,1,0:T(8,128)(2,1)S(1)}, bf16[8,18,32,128]{3,2,1,0:T(8,128)(2,1)S(1)}, u32[]{:S(2)}, u32[]{:S(2)}) collective-permute-start(bf16[8,18,32,128]{3,2,1,0:T(8,128)(2,1)S(1)} %collective-permute-done.24.rest_1_), channel_id=1, source_target_pairs={{0,1},{3,2},{4,5},{7,6},{8,9},{11,10},{12,13},{15,14},{16,17},{19,... | collective-permute-start | bytes 3538952 | tf_op jit(solution)/shard_map/ppermute | solution.py:871
  235.3 15.3 %collective-permute-start.21 = (bf16[4,14,32,128]{3,2,1,0:T(8,128)(2,1)S(1)}, bf16[4,14,32,128]{3,2,1,0:T(8,128)(2,1)S(1)}, u32[]{:S(2)}, u32[]{:S(2)}) collective-permute-start(bf16[4,14,32,128]{3,2,1,0:T(8,128)(2,1)S(1)} %get-tuple-element.104), channel_id=1, source_target_pairs={{0,4},{4,8},{8,12},{12,0},{1,5},{5,9},{9,13},{13,1},{2,6},{6,10},{... | collective-permute-start | bytes 1376264 | tf_op jit(solution)/shard_map/ppermute | solution.py:922
  237.8 22.3 %collective-permute-start.23 = (bf16[4,14,32,128]{3,2,1,0:T(8,128)(2,1)S(1)}, bf16[4,14,32,128]{3,2,1,0:T(8,128)(2,1)S(1)}, u32[]{:S(2)}, u32[]{:S(2)}) collective-permute-start(bf16[4,14,32,128]{3,2,1,0:T(8,128)(2,1)S(1)} %get-tuple-element.106), channel_id=1, source_target_pairs={{0,12},{4,0},{8,4},{12,8},{1,13},{5,1},{9,5},{13,9},{2,14},{6,2},{... | collective-permute-start | bytes 1376264 | tf_op jit(solution)/shard_map/ppermute | solution.py:922
  260.1 15.8 %collective-permute-start.29 = (bf16[4,18,32,128]{3,2,1,0:T(8,128)(2,1)S(1)}, bf16[4,18,32,128]{3,2,1,0:T(8,128)(2,1)S(1)}, u32[]{:S(2)}, u32[]{:S(2)}) collective-permute-start(bf16[4,18,32,128]{3,2,1,0:T(8,128)(2,1)S(1)} %get-tuple-element.118), channel_id=1, source_target_pairs={{0,12},{4,0},{8,4},{12,8},{1,13},{5,1},{9,5},{13,9},{2,14},{6,2},{... | collective-permute-start | bytes 1769480 | tf_op jit(solution)/shard_map/ppermute | solution.py:922
  261.7 39.5 %collective-permute-start.28 = (bf16[4,18,32,128]{3,2,1,0:T(8,128)(2,1)S(1)}, bf16[4,18,32,128]{3,2,1,0:T(8,128)(2,1)S(1)}, u32[]{:S(2)}, u32[]{:S(2)}) collective-permute-start(bf16[4,18,32,128]{3,2,1,0:T(8,128)(2,1)S(1)} %get-tuple-element.116), channel_id=1, source_target_pairs={{0,8},{4,12},{8,0},{12,4},{1,9},{5,13},{9,1},{13,5},{2,10},{6,14},... | collective-permute-start | bytes 1769480 | tf_op jit(solution)/shard_map/ppermute | solution.py:922
  263.7 50.1 %collective-permute-start.27 = (bf16[4,18,32,128]{3,2,1,0:T(8,128)(2,1)S(1)}, bf16[4,18,32,128]{3,2,1,0:T(8,128)(2,1)S(1)}, u32[]{:S(2)}, u32[]{:S(2)}) collective-permute-start(bf16[4,18,32,128]{3,2,1,0:T(8,128)(2,1)S(1)} %get-tuple-element.114), channel_id=1, source_target_pairs={{0,4},{4,8},{8,12},{12,0},{1,5},{5,9},{9,13},{13,1},{2,6},{6,10},{... | collective-permute-start | bytes 1769480 | tf_op jit(solution)/shard_map/ppermute | solution.py:922
  (20 other events, 265.6 us)

commit v9 on v8

--- a/solution.py
+++ b/solution.py
@@ -617,6 +617,7 @@
             jax.ShapeDtypeStruct((slots_dev * terms,), jnp.int32),
         ],
         scratch_shapes=[pltpu.SMEM((n_blk,), jnp.int32)],
+        compiler_params=pltpu.CompilerParams(vmem_limit_bytes=mebi),
         name="make_plan",
     )(ids, owners, slots)
 
@@ -626,6 +627,7 @@
     out_refs, (left_held, right_held, out_held, sems, out_sems) = rest[: len(shifts)], rest[len(shifts) :]
     halves, _, bands, rows, hidden = left_held.shape
     parts = hidden // size
+    at_once = 2 if capacity % 2 == 0 else 1
 
     def copy(n, source):
         side, half, base, *_ = pieces[n]
@@ -653,21 +655,22 @@
 
     for n, shift in enumerate(shifts):
 
-        def one(term, carry, n=n, shift=shift):
-            at = 2 * (shift * (capacity + 1) + term)
-            left_slot, right_slot = chosen[at], chosen[at + 1]
+        def one(turn, carry, n=n, shift=shift):
             group = lane_group((size, hidden), size)
-            for band in range(bands):
-                left = jnp.concatenate([left_held[h, left_slot, band] for h in range(halves)], axis=1)
-                apart = []
-                for h in range(halves):
-                    right = right_held[h, right_slot, band]
-                    apart += [jnp.where(group == part, right, jnp.zeros_like(right)) for part in range(parts)]
-                made = dot(left, jnp.concatenate(apart, axis=0))
-                out_held[n * capacity + term, band] = made.astype(jnp.bfloat16)
+            for term in [turn * at_once + t for t in range(at_once)]:
+                at = 2 * (shift * (capacity + 1) + term)
+                left_slot, right_slot = chosen[at], chosen[at + 1]
+                for band in range(bands):
+                    left = jnp.concatenate([left_held[h, left_slot, band] for h in range(halves)], axis=1)
+                    apart = []
+                    for h in range(halves):
+                        right = right_held[h, right_slot, band]
+                        apart += [jnp.where(group == part, right, jnp.zeros_like(right)) for part in range(parts)]
+                    made = dot(left, jnp.concatenate(apart, axis=0))
+                    out_held[n * capacity + term, band] = made.astype(jnp.bfloat16)
             return carry
 
-        lax.fori_loop(0, capacity, one, 0)
+        lax.fori_loop(0, capacity // at_once, one, 0)
         leave(n).start()
     for n in range(len(shifts)):
         leave(n).wait()
@@ -907,11 +910,13 @@
                     exchanged.append(exchange(left, right, over))
             else:
                 left, right = operands[-1][chunk], operands[-1][count + chunk]
-                last_of = exchanged[-1]
-                left, right = lax.optimization_barrier(
-                    (left, right, last_of[0][1][1], last_of[0][0][0], last_of[1][0][1], last_of[1][1][1])
-                    + ((made[-1],) if layer % 2 == 0 else ())
-                )[:2]
+                if layer % 2:
+                    (_, (_, two)), (_, (other, _)) = exchanged[-1]
+                    left, right = lax.optimization_barrier((left, right, two, other))[:2]
+                else:
+                    ((other, _), _), ((one, _), (_, two)) = exchanged[-1]
+                    left = after(left, other)
+                    right = after(right, one, two, made[-1])
                 exchanged = [exchange(left, right, arrived[-1][far])]
             made = banded_products(shifts, ids, chosen, exchanged, capacity, cols)
             parts = [None] * n_blk

time: 325 us -> 312 us (0.960)
  local copies, waits for them, and re-layouts: 10.5 us -> 1.95 us
  Pallas kernels: 83.5 us -> 77.7 us
    unnamed x44 -> x16, local copies, waits for them, and re-layouts: 10.5 us -> 1.95 us
    pallas_call x4, Pallas kernels: 29.4 us -> 24.2 us  [banded_products(): pl.pallas_call(functools.partial(banded_kernel, shifts, capacity, tuple(p...]
  transfers between devices with their start and end apart: 30 -> 30, of which waited for: 18 -> 17; matrix products, arithmetic and copies ran while one was open for 0% -> 0% of each run, Pallas kernels for 14% -> 13%
where the time goes in v9:
time: 312 us; the launch traced here: 311 us
  waiting for transfers between devices  185 us (59%)
  Pallas kernels  77.7 us (25%)
  starting transfers between devices  45.6 us (15%)
    ppermute x12, waiting for transfers between devices, banded(): lax.ppermute(part, 'blk', [(p, (p + shift) % n_blk) for p in range(n_blk)])  139 us
    pallas_call x3, Pallas kernels, close_layer(): pl.pallas_call(functools.partial(close_kernel, *(layer, last, len(flat),...  34.1 us
    ppermute x3, waiting for transfers between devices, exchange_bands_outgoing(): one = lax.ppermute(right, both, [(0, 2), (3, 1), (1, 0), (2, 3)])  29.7 us
    pallas_call x4, Pallas kernels, banded_products(): pl.pallas_call(functools.partial(banded_kernel, shifts, capacity, tuple(p...  24.2 us
    pallas_call x2, Pallas kernels, open_operands(): pl.pallas_call(functools.partial(open_kernel, hidden, len(bands), lax.axi...  16.7 us
    ppermute x12, starting transfers between devices, banded(): lax.ppermute(part, 'blk', [(p, (p + shift) % n_blk) for p in range(n_blk)])  16.5 us
    ppermute x3, starting transfers between devices, exchange_bands_incoming(): two = lax.ppermute(after(one, over), both, [(0, 1), (3, 2)])  11.7 us
    ppermute x3, starting transfers between devices, exchange_bands_outgoing(): one = lax.ppermute(right, both, [(0, 2), (3, 1), (1, 0), (2, 3)])  10.7 us
  transfers between devices with their start and end apart: 30, of which 17 were waited for; matrix products, arithmetic and copies ran while one was open for 0% of the time, Pallas kernels for 13%

profile of v9, /device:TPU:11, one launch (start us, length us, event | category | flops | bytes accessed | tf_op | source)
XLA Modules:
  0.0 310.8 jit_solution(3355725672630489863)
XLA Ops:
  2.6 8.3 %open_operands.2 = (f32[8,32,32,128]{3,2,1,0:T(8,128)S(1)}, bf16[4,12,32,128]{3,2,1,0:T(8,128)(2,1)S(1)}, bf16[8,20,32,128]{3,2,1,0:T(8,128)(2,1)S(1)}, bf16[4,1...) custom-call(s32[4]{0:T(128)S(1)} %pad_add_fusion.ids, s32[2,32]{1,0:T(2,128)S(1)} %bitcast.14, ...), custom_call_target="tpu_custom_call" | custom-call | flops 8589934592 | bytes 1048576 | tf_op jit(solution)/shard_map/open_operands/pallas_call | solution.py:566
  11.6 3.3 %collective-permute-start.1 = (bf16[4,12,32,128]{3,2,1,0:T(8,128)(2,1)S(1)}, bf16[4,12,32,128]{3,2,1,0:T(8,128)(2,1)S(1)}, u32[]{:S(2)}, u32[]{:S(2)}) collective-permute-start(bf16[4,12,32,128]{3,2,1,0:T(8,128)(2,1)S(1)} %get-tuple-element.66.rest_3_), channel_id=1, source_target_pairs={{0,2},{3,1},{1,0},{2,3},{4,6},{7,5},{5,4},{6,7},{8,10},{11,9},{9,8... | collective-permute-start | bytes 1179656 | tf_op jit(solution)/shard_map/ppermute | solution.py:865
  14.9 8.3 %open_operands.3 = (f32[8,32,32,128]{3,2,1,0:T(8,128)S(1)}, bf16[4,12,32,128]{3,2,1,0:T(8,128)(2,1)S(1)}, bf16[8,20,32,128]{3,2,1,0:T(8,128)(2,1)S(1)}, bf16[4,1...) custom-call(s32[4]{0:T(128)S(1)} %pad_add_fusion.ids, ...), custom_call_target="tpu_custom_call", output_to_operand_aliasing={{0}: (6, {}), {2}: (7, {}), {4}: (8, {})} | custom-call | flops 8589934592 | bytes 1048576 | tf_op jit(solution)/shard_map/open_operands/pallas_call | solution.py:566
  25.6 2.6 collective-permute-start.4
  29.8 6.1 %collective-permute-done.4.rest_7_ = bf16[4,12,32,128]{3,2,1,0:T(8,128)(2,1)S(1)} collective-permute-done((bf16[4,12,32,128]{3,2,1,0:T(8,128)(2,1)S(1)}, bf16[4,12,32,128]{3,2,1,0:T(8,128)(2,1)S(1)}, u32[]{:S(2)}, u32[]{:S(2)}) %collective-permute-start.4) | collective-permute-done | bytes 393248 | tf_op jit(solution)/shard_map/ppermute | solution.py:865
  35.9 5.8 %banded_products.4 = (bf16[4,12,32,128]{3,2,1,0:T(8,128)(2,1)S(1)}, bf16[4,12,32,128]{3,2,1,0:T(8,128)(2,1)S(1)}, bf16[4,12,32,128]{3,2,1,0:T(8,128)(2,1)S(1)}, bf16[4,12,32,128]{3,2,1,0:T(8,128)(2,1)S(1)}) custom-call(s32[4]{0:T(128)S(1)} %pad_add_fusion.ids, s32[40]{0:T(128)S(1)} %get-tuple-element.64.chosen, ...), custom_call_target="tpu_custom_call" | custom-call | flops 402653184 | bytes 1 | tf_op jit(solution)/shard_map/banded_products/pallas_call | solution.py:699
  42.5 4.8 %collective-permute-start.10 = (bf16[8,20,32,128]{3,2,1,0:T(8,128)(2,1)S(1)}, bf16[8,20,32,128]{3,2,1,0:T(8,128)(2,1)S(1)}, u32[]{:S(2)}, u32[]{:S(2)}) collective-permute-start(bf16[8,20,32,128]{3,2,1,0:T(8,128)(2,1)S(1)} %get-tuple-element.81.rest_3_), channel_id=1, source_target_pairs={{0,2},{3,1},{1,0},{2,3},{4,6},{7,5},{5,4},{6,7},{8,10},{11,9},{9,8... | collective-permute-start | bytes 3932168 | tf_op jit(solution)/shard_map/ppermute | solution.py:865
  51.1 23.6 %collective-permute-done.10.rest_2_ = bf16[8,20,32,128]{3,2,1,0:T(8,128)(2,1)S(1)} collective-permute-done((bf16[8,20,32,128]{3,2,1,0:T(8,128)(2,1)S(1)}, bf16[8,20,32,128]{3,2,1,0:T(8,128)(2,1)S(1)}, u32[]{:S(2)}, u32[]{:S(2)}) %collective-permute-start.10) | collective-permute-done | bytes 1310752 | tf_op jit(solution)/shard_map/ppermute | solution.py:865
  74.7 5.7 %banded_products.5 = (bf16[4,20,32,128]{3,2,1,0:T(8,128)(2,1)S(1)}, bf16[4,20,32,128]{3,2,1,0:T(8,128)(2,1)S(1)}, bf16[4,20,32,128]{3,2,1,0:T(8,128)(2,1)S(1)}, bf16[4,20,32,128]{3,2,1,0:T(8,128)(2,1)S(1)}) custom-call(s32[4]{0:T(128)S(1)} %pad_add_fusion.ids, s32[40]{0:T(128)S(1)} %get-tuple-element.64.chosen, ...), custom_call_target="tpu_custom_call" | custom-call | flops 671088640 | bytes 1 | tf_op jit(solution)/shard_map/banded_products/pallas_call | solution.py:699
  83.0 2.2 collective-permute-start.12
  85.7 9.7 %collective-permute-done.14.rest_7_ = bf16[4,20,32,128]{3,2,1,0:T(8,128)(2,1)S(1)} collective-permute-done((bf16[4,20,32,128]{3,2,1,0:T(8,128)(2,1)S(1)}, bf16[4,20,32,128]{3,2,1,0:T(8,128)(2,1)S(1)}, u32[]{:S(2)}, u32[]{:S(2)}) %collective-permute-start.14) | collective-permute-done | bytes 655392 | tf_op jit(solution)/shard_map/ppermute | solution.py:927
  95.4 31.4 %collective-permute-done.13.rest_6_ = bf16[4,20,32,128]{3,2,1,0:T(8,128)(2,1)S(1)} collective-permute-done((bf16[4,20,32,128]{3,2,1,0:T(8,128)(2,1)S(1)}, bf16[4,20,32,128]{3,2,1,0:T(8,128)(2,1)S(1)}, u32[]{:S(2)}, u32[]{:S(2)}) %collective-permute-start.13) | collective-permute-done | bytes 655392 | tf_op jit(solution)/shard_map/ppermute | solution.py:927
  126.9 14.0 %collective-permute-done.12.rest_5_ = bf16[4,20,32,128]{3,2,1,0:T(8,128)(2,1)S(1)} collective-permute-done((bf16[4,20,32,128]{3,2,1,0:T(8,128)(2,1)S(1)}, bf16[4,20,32,128]{3,2,1,0:T(8,128)(2,1)S(1)}, u32[]{:S(2)}, u32[]{:S(2)}) %collective-permute-start.12) | collective-permute-done | bytes 655392 | tf_op jit(solution)/shard_map/ppermute | solution.py:927
  140.9 12.6 %close_layer.3 = (bf16[8,32,32,128]{3,2,1,0:T(8,128)(2,1)S(1)}, f32[8,32,32,128]{3,2,1,0:T(8,128)S(1)}, bf16[4,14,32,128]{3,2,1,0:T(8,128)(2,1)S(1)}, bf16[8,18,...) custom-call(s32[4]{0:T(128)S(1)} %pad_add_fusion.ids, ...), custom_call_target="tpu_custom_call" | custom-call | flops 8589934592 | bytes 1048576 | tf_op jit(solution)/shard_map/close_layer/pallas_call | solution.py:838
  154.9 12.6 %close_layer.4 = (bf16[8,32,32,128]{3,2,1,0:T(8,128)(2,1)S(1)}, f32[8,32,32,128]{3,2,1,0:T(8,128)S(1)}, bf16[4,14,32,128]{3,2,1,0:T(8,128)(2,1)S(1)}, bf16[8,18,...) custom-call(s32[4]{0:T(128)S(1)} %pad_add_fusion.ids, ...), custom_call_target="tpu_custom_call", output_to_operand_aliasing={{0}: (17, {}), {1}: (18, {}), {3}: (19, {}), {5}: (20, {})} | custom-call | flops 8589934592 | bytes 1048576 | tf_op jit(solution)/shard_map/close_layer/pallas_call | solution.py:838
  167.5 3.1 collective-permute-done.17.rest_4_
  172.1 8.2 %collective-permute-done.18.rest_6_ = bf16[4,14,32,128]{3,2,1,0:T(8,128)(2,1)S(1)} collective-permute-done((bf16[4,14,32,128]{3,2,1,0:T(8,128)(2,1)S(1)}, bf16[4,14,32,128]{3,2,1,0:T(8,128)(2,1)S(1)}, u32[]{:S(2)}, u32[]{:S(2)}) %collective-permute-start.18) | collective-permute-done | bytes 458784 | tf_op jit(solution)/shard_map/ppermute | solution.py:872
  180.3 4.5 %collective-permute-start.19 = (bf16[4,14,32,128]{3,2,1,0:T(8,128)(2,1)S(1)}, bf16[4,14,32,128]{3,2,1,0:T(8,128)(2,1)S(1)}, u32[]{:S(2)}, u32[]{:S(2)}) collective-permute-start(bf16[4,14,32,128]{3,2,1,0:T(8,128)(2,1)S(1)} %collective-permute-done.18.rest_6_), channel_id=1, source_target_pairs={{0,1},{3,2},{4,5},{7,6},{8,9},{11,10},{12,13},{15,14},{16,17},{19,... | collective-permute-start | bytes 1376264 | tf_op jit(solution)/shard_map/ppermute | solution.py:874
  184.8 3.0 collective-permute-done.20.rest_9_
  187.8 4.4 %collective-permute-start.16 = (bf16[4,14,32,128]{3,2,1,0:T(8,128)(2,1)S(1)}, bf16[4,14,32,128]{3,2,1,0:T(8,128)(2,1)S(1)}, u32[]{:S(2)}, u32[]{:S(2)}) collective-permute-start(bf16[4,14,32,128]{3,2,1,0:T(8,128)(2,1)S(1)} %collective-permute-done.15.rest_1_), channel_id=1, source_target_pairs={{0,1},{3,2},{4,5},{7,6},{8,9},{11,10},{12,13},{15,14},{16,17},{19,... | collective-permute-start | bytes 1376264 | tf_op jit(solution)/shard_map/ppermute | solution.py:874
  193.6 7.0 %banded_products.6 = (bf16[4,14,32,128]{3,2,1,0:T(8,128)(2,1)S(1)}, bf16[4,14,32,128]{3,2,1,0:T(8,128)(2,1)S(1)}, bf16[4,14,32,128]{3,2,1,0:T(8,128)(2,1)S(1)}, bf16[4,14,32,128]{3,2,1,0:T(8,128)(2,1)S(1)}) custom-call(s32[4]{0:T(128)S(1)} %pad_add_fusion.ids, s32[40]{0:T(128)S(1)} %get-tuple-element.64.chosen, ...), custom_call_target="tpu_custom_call" | custom-call | flops 469762048 | bytes 1 | tf_op jit(solution)/shard_map/banded_products/pallas_call | solution.py:699
  200.8 19.6 %collective-permute-done.22.rest_2_ = bf16[4,14,32,128]{3,2,1,0:T(8,128)(2,1)S(1)} collective-permute-done((bf16[4,14,32,128]{3,2,1,0:T(8,128)(2,1)S(1)}, bf16[4,14,32,128]{3,2,1,0:T(8,128)(2,1)S(1)}, u32[]{:S(2)}, u32[]{:S(2)}) %collective-permute-start.22) | collective-permute-done | bytes 458784 | tf_op jit(solution)/shard_map/ppermute | solution.py:927
  220.4 2.9 collective-permute-start.25
  223.2 2.4 collective-permute-start.21
  227.9 5.7 %banded_products.7 = (bf16[4,18,32,128]{3,2,1,0:T(8,128)(2,1)S(1)}, bf16[4,18,32,128]{3,2,1,0:T(8,128)(2,1)S(1)}, bf16[4,18,32,128]{3,2,1,0:T(8,128)(2,1)S(1)}, bf16[4,18,32,128]{3,2,1,0:T(8,128)(2,1)S(1)}) custom-call(s32[4]{0:T(128)S(1)} %pad_add_fusion.ids, s32[40]{0:T(128)S(1)} %get-tuple-element.64.chosen, ...), custom_call_target="tpu_custom_call" | custom-call | flops 603979776 | bytes 1 | tf_op jit(solution)/shard_map/banded_products/pallas_call | solution.py:699
  233.6 4.9 %collective-permute-done.21.rest_1_ = bf16[4,14,32,128]{3,2,1,0:T(8,128)(2,1)S(1)} collective-permute-done((bf16[4,14,32,128]{3,2,1,0:T(8,128)(2,1)S(1)}, bf16[4,14,32,128]{3,2,1,0:T(8,128)(2,1)S(1)}, u32[]{:S(2)}, u32[]{:S(2)}) %collective-permute-start.21) | collective-permute-done | bytes 458784 | tf_op jit(solution)/shard_map/ppermute | solution.py:927
  238.5 9.4 %collective-permute-done.23.rest_3_ = bf16[4,14,32,128]{3,2,1,0:T(8,128)(2,1)S(1)} collective-permute-done((bf16[4,14,32,128]{3,2,1,0:T(8,128)(2,1)S(1)}, bf16[4,14,32,128]{3,2,1,0:T(8,128)(2,1)S(1)}, u32[]{:S(2)}, u32[]{:S(2)}) %collective-permute-start.23) | collective-permute-done | bytes 458784 | tf_op jit(solution)/shard_map/ppermute | solution.py:927
  249.5 2.1 collective-permute-start.28
  252.1 11.7 %collective-permute-done.29.rest_7_ = bf16[4,18,32,128]{3,2,1,0:T(8,128)(2,1)S(1)} collective-permute-done((bf16[4,18,32,128]{3,2,1,0:T(8,128)(2,1)S(1)}, bf16[4,18,32,128]{3,2,1,0:T(8,128)(2,1)S(1)}, u32[]{:S(2)}, u32[]{:S(2)}) %collective-permute-start.29) | collective-permute-done | bytes 589856 | tf_op jit(solution)/shard_map/ppermute | solution.py:927
  263.8 25.2 %collective-permute-done.28.rest_6_ = bf16[4,18,32,128]{3,2,1,0:T(8,128)(2,1)S(1)} collective-permute-done((bf16[4,18,32,128]{3,2,1,0:T(8,128)(2,1)S(1)}, bf16[4,18,32,128]{3,2,1,0:T(8,128)(2,1)S(1)}, u32[]{:S(2)}, u32[]{:S(2)}) %collective-permute-start.28) | collective-permute-done | bytes 589856 | tf_op jit(solution)/shard_map/ppermute | solution.py:927
  289.0 12.6 %collective-permute-done.27.rest_5_ = bf16[4,18,32,128]{3,2,1,0:T(8,128)(2,1)S(1)} collective-permute-done((bf16[4,18,32,128]{3,2,1,0:T(8,128)(2,1)S(1)}, bf16[4,18,32,128]{3,2,1,0:T(8,128)(2,1)S(1)}, u32[]{:S(2)}, u32[]{:S(2)}) %collective-permute-start.27) | collective-permute-done | bytes 589856 | tf_op jit(solution)/shard_map/ppermute | solution.py:927
  301.6 9.0 %close_layer.5 = bf16[8,32,32,128]{3,2,1,0:T(8,128)(2,1)} custom-call(s32[4]{0:T(128)S(1)} %pad_add_fusion.ids, s32[2,32]{1,0:T(2,128)S(1)} %bitcast.18, s32[16]{0:T(128)S(1)} %get-tuple-element.63.place, bf16[4,14,32,128]{3,2,1,0:T(8,128)(2,1)S(1)} %get-tuple-element.103.rest_0_, bf16[4,14,32,128]{3,2,1,0:T(8,128)(2,1)S(1)} %collective-permute-done.21.rest_1_, ...), custom_call_target="tpu_custom_call" | custom-call | flops 8589934592 | bytes 1048576 | tf_op jit(solution)/shard_map/close_layer/pallas_call | solution.py:838
  (57 shorter events, 23.7 us)
Async XLA Ops:
  10.9 12.4 %collective-permute-start.2 = (bf16[4,12,32,128]{3,2,1,0:T(8,128)(2,1)S(1)}, bf16[4,12,32,128]{3,2,1,0:T(8,128)(2,1)S(1)}, u32[]{:S(2)}, u32[]{:S(2)}) collective-permute-start(bf16[4,12,32,128]{3,2,1,0:T(8,128)(2,1)S(1)} %get-tuple-element.66.rest_3_), channel_id=1, source_target_pairs={{1,2},{2,1},{5,6},{6,5},{9,10},{10,9},{13,14},{14,13},{17,18},{18,... | collective-permute-start | bytes 1179656 | tf_op jit(solution)/shard_map/ppermute | solution.py:866
  11.6 11.7 %collective-permute-start.1 = (bf16[4,12,32,128]{3,2,1,0:T(8,128)(2,1)S(1)}, bf16[4,12,32,128]{3,2,1,0:T(8,128)(2,1)S(1)}, u32[]{:S(2)}, u32[]{:S(2)}) collective-permute-start(bf16[4,12,32,128]{3,2,1,0:T(8,128)(2,1)S(1)} %get-tuple-element.66.rest_3_), channel_id=1, source_target_pairs={{0,2},{3,1},{1,0},{2,3},{4,6},{7,5},{5,4},{6,7},{8,10},{11,9},{9,8... | collective-permute-start | bytes 1179656 | tf_op jit(solution)/shard_map/ppermute | solution.py:865
  14.9 8.4 %collective-permute-start = (bf16[4,12,32,128]{3,2,1,0:T(8,128)(2,1)S(1)}, bf16[4,12,32,128]{3,2,1,0:T(8,128)(2,1)S(1)}, u32[]{:S(2)}, u32[]{:S(2)}) collective-permute-start(bf16[4,12,32,128]{3,2,1,0:T(8,128)(2,1)S(1)} %get-tuple-element.65.rest_1_), channel_id=1, source_target_pairs={{0,1},{1,0},{2,3},{3,2},{4,5},{5,4},{6,7},{7,6},{8,9},{9,8},{10,11... | collective-permute-start | bytes 1179656 | tf_op jit(solution)/shard_map/ppermute | solution.py:864
  14.9 13.3 %copy-start.1 = (s32[32,2]{0,1:T(2,128)S(1)}, s32[32,2]{0,1:T(2,128)}, u32[]{:S(2)}) copy-start(s32[32,2]{0,1:T(2,128)} %param.9) | copy-start | bytes 772
  23.3 6.5 %collective-permute-start.3 = (bf16[4,12,32,128]{3,2,1,0:T(8,128)(2,1)S(1)}, bf16[4,12,32,128]{3,2,1,0:T(8,128)(2,1)S(1)}, u32[]{:S(2)}, u32[]{:S(2)}) collective-permute-start(bf16[4,12,32,128]{3,2,1,0:T(8,128)(2,1)S(1)} %get-tuple-element.72.rest_6_), channel_id=1, source_target_pairs={{0,1},{1,0},{2,3},{3,2},{4,5},{5,4},{6,7},{7,6},{8,9},{9,8},{10,11... | collective-permute-start | bytes 1179656 | tf_op jit(solution)/shard_map/ppermute | solution.py:864
  24.9 4.9 %collective-permute-start.5 = (bf16[4,12,32,128]{3,2,1,0:T(8,128)(2,1)S(1)}, bf16[4,12,32,128]{3,2,1,0:T(8,128)(2,1)S(1)}, u32[]{:S(2)}, u32[]{:S(2)}) collective-permute-start(bf16[4,12,32,128]{3,2,1,0:T(8,128)(2,1)S(1)} %get-tuple-element.73.rest_8_), channel_id=1, source_target_pairs={{1,2},{2,1},{5,6},{6,5},{9,10},{10,9},{13,14},{14,13},{17,18},{18,... | collective-permute-start | bytes 1179656 | tf_op jit(solution)/shard_map/ppermute | solution.py:866
  25.6 10.3 %collective-permute-start.4 = (bf16[4,12,32,128]{3,2,1,0:T(8,128)(2,1)S(1)}, bf16[4,12,32,128]{3,2,1,0:T(8,128)(2,1)S(1)}, u32[]{:S(2)}, u32[]{:S(2)}) collective-permute-start(bf16[4,12,32,128]{3,2,1,0:T(8,128)(2,1)S(1)} %get-tuple-element.73.rest_8_), channel_id=1, source_target_pairs={{0,2},{3,1},{1,0},{2,3},{4,6},{7,5},{5,4},{6,7},{8,10},{11,9},{9,8... | collective-permute-start | bytes 1179656 | tf_op jit(solution)/shard_map/ppermute | solution.py:865
  41.7 7.9 %collective-permute-start.11 = (bf16[8,20,32,128]{3,2,1,0:T(8,128)(2,1)S(1)}, bf16[8,20,32,128]{3,2,1,0:T(8,128)(2,1)S(1)}, u32[]{:S(2)}, u32[]{:S(2)}) collective-permute-start(bf16[8,20,32,128]{3,2,1,0:T(8,128)(2,1)S(1)} %get-tuple-element.81.rest_3_), channel_id=1, source_target_pairs={{1,2},{2,1},{5,6},{6,5},{9,10},{10,9},{13,14},{14,13},{17,18},{18,... | collective-permute-start | bytes 3932168 | tf_op jit(solution)/shard_map/ppermute | solution.py:866
  42.5 32.2 %collective-permute-start.10 = (bf16[8,20,32,128]{3,2,1,0:T(8,128)(2,1)S(1)}, bf16[8,20,32,128]{3,2,1,0:T(8,128)(2,1)S(1)}, u32[]{:S(2)}, u32[]{:S(2)}) collective-permute-start(bf16[8,20,32,128]{3,2,1,0:T(8,128)(2,1)S(1)} %get-tuple-element.81.rest_3_), channel_id=1, source_target_pairs={{0,2},{3,1},{1,0},{2,3},{4,6},{7,5},{5,4},{6,7},{8,10},{11,9},{9,8... | collective-permute-start | bytes 3932168 | tf_op jit(solution)/shard_map/ppermute | solution.py:865
  47.3 27.4 %collective-permute-start.9 = (bf16[8,20,32,128]{3,2,1,0:T(8,128)(2,1)S(1)}, bf16[8,20,32,128]{3,2,1,0:T(8,128)(2,1)S(1)}, u32[]{:S(2)}, u32[]{:S(2)}) collective-permute-start(bf16[8,20,32,128]{3,2,1,0:T(8,128)(2,1)S(1)} %get-tuple-element.79.rest_1_), channel_id=1, source_target_pairs={{0,1},{1,0},{2,3},{3,2},{4,5},{5,4},{6,7},{7,6},{8,9},{9,8},{10,11... | collective-permute-start | bytes 3932168 | tf_op jit(solution)/shard_map/ppermute | solution.py:864
  47.3 33.1 %collective-permute-start.6 = (bf16[4,12,32,128]{3,2,1,0:T(8,128)(2,1)S(1)}, bf16[4,12,32,128]{3,2,1,0:T(8,128)(2,1)S(1)}, u32[]{:S(2)}, u32[]{:S(2)}) collective-permute-start(bf16[4,12,32,128]{3,2,1,0:T(8,128)(2,1)S(1)} %get-tuple-element.75), channel_id=1, source_target_pairs={{0,4},{4,8},{8,12},{12,0},{1,5},{5,9},{9,13},{13,1},{2,6},{6,10},{... | collective-permute-start | bytes 1179656 | tf_op jit(solution)/shard_map/ppermute | solution.py:927
  48.6 31.9 %collective-permute-start.7 = (bf16[4,12,32,128]{3,2,1,0:T(8,128)(2,1)S(1)}, bf16[4,12,32,128]{3,2,1,0:T(8,128)(2,1)S(1)}, u32[]{:S(2)}, u32[]{:S(2)}) collective-permute-start(bf16[4,12,32,128]{3,2,1,0:T(8,128)(2,1)S(1)} %get-tuple-element.76), channel_id=1, source_target_pairs={{0,8},{4,12},{8,0},{12,4},{1,9},{5,13},{9,1},{13,5},{2,10},{6,14},... | collective-permute-start | bytes 1179656 | tf_op jit(solution)/shard_map/ppermute | solution.py:927
  49.6 31.5 %collective-permute-start.8 = (bf16[4,12,32,128]{3,2,1,0:T(8,128)(2,1)S(1)}, bf16[4,12,32,128]{3,2,1,0:T(8,128)(2,1)S(1)}, u32[]{:S(2)}, u32[]{:S(2)}) collective-permute-start(bf16[4,12,32,128]{3,2,1,0:T(8,128)(2,1)S(1)} %get-tuple-element.77), channel_id=1, source_target_pairs={{0,12},{4,0},{8,4},{12,8},{1,13},{5,1},{9,5},{13,9},{2,14},{6,2},{... | collective-permute-start | bytes 1179656 | tf_op jit(solution)/shard_map/ppermute | solution.py:927
  81.1 14.3 %collective-permute-start.14 = (bf16[4,20,32,128]{3,2,1,0:T(8,128)(2,1)S(1)}, bf16[4,20,32,128]{3,2,1,0:T(8,128)(2,1)S(1)}, u32[]{:S(2)}, u32[]{:S(2)}) collective-permute-start(bf16[4,20,32,128]{3,2,1,0:T(8,128)(2,1)S(1)} %get-tuple-element.88), channel_id=1, source_target_pairs={{0,12},{4,0},{8,4},{12,8},{1,13},{5,1},{9,5},{13,9},{2,14},{6,2},{... | collective-permute-start | bytes 1966088 | tf_op jit(solution)/shard_map/ppermute | solution.py:927
  81.1 45.8 %collective-permute-start.13 = (bf16[4,20,32,128]{3,2,1,0:T(8,128)(2,1)S(1)}, bf16[4,20,32,128]{3,2,1,0:T(8,128)(2,1)S(1)}, u32[]{:S(2)}, u32[]{:S(2)}) collective-permute-start(bf16[4,20,32,128]{3,2,1,0:T(8,128)(2,1)S(1)} %get-tuple-element.86), channel_id=1, source_target_pairs={{0,8},{4,12},{8,0},{12,4},{1,9},{5,13},{9,1},{13,5},{2,10},{6,14},... | collective-permute-start | bytes 1966088 | tf_op jit(solution)/shard_map/ppermute | solution.py:927
  83.0 57.9 %collective-permute-start.12 = (bf16[4,20,32,128]{3,2,1,0:T(8,128)(2,1)S(1)}, bf16[4,20,32,128]{3,2,1,0:T(8,128)(2,1)S(1)}, u32[]{:S(2)}, u32[]{:S(2)}) collective-permute-start(bf16[4,20,32,128]{3,2,1,0:T(8,128)(2,1)S(1)} %get-tuple-element.84), channel_id=1, source_target_pairs={{0,4},{4,8},{8,12},{12,0},{1,5},{5,9},{9,13},{13,1},{2,6},{6,10},{... | collective-permute-start | bytes 1966088 | tf_op jit(solution)/shard_map/ppermute | solution.py:927
  85.2 55.7 %copy-start.5 = (bf16[2,128,128]{2,1,0:T(8,128)(2,1)S(1)}, bf16[2,128,128]{2,1,0:T(8,128)(2,1)}, u32[]{:S(2)}) copy-start(bf16[2,128,128]{2,1,0:T(8,128)(2,1)} %rest_10_.5) | copy-start | bytes 196612
  153.5 14.1 %collective-permute-start.15 = (bf16[4,14,32,128]{3,2,1,0:T(8,128)(2,1)S(1)}, bf16[4,14,32,128]{3,2,1,0:T(8,128)(2,1)S(1)}, u32[]{:S(2)}, u32[]{:S(2)}) collective-permute-start(bf16[4,14,32,128]{3,2,1,0:T(8,128)(2,1)S(1)} %get-tuple-element.91.rest_0_), channel_id=1, source_target_pairs={{1,3},{2,0},{0,1},{3,2},{5,7},{6,4},{4,5},{7,6},{9,11},{10,8},{8,9... | collective-permute-start | bytes 1376264 | tf_op jit(solution)/shard_map/ppermute | solution.py:872
  154.0 16.7 %collective-permute-start.17 = (bf16[4,14,32,128]{3,2,1,0:T(8,128)(2,1)S(1)}, bf16[4,14,32,128]{3,2,1,0:T(8,128)(2,1)S(1)}, u32[]{:S(2)}, u32[]{:S(2)}) collective-permute-start(bf16[4,14,32,128]{3,2,1,0:T(8,128)(2,1)S(1)} %get-tuple-element.98.rest_3_), channel_id=1, source_target_pairs={{0,2},{2,0},{1,3},{3,1},{4,6},{6,4},{5,7},{7,5},{8,10},{10,8},{9,1... | collective-permute-start | bytes 1376264 | tf_op jit(solution)/shard_map/ppermute | solution.py:873
  170.6 9.7 %collective-permute-start.18 = (bf16[4,14,32,128]{3,2,1,0:T(8,128)(2,1)S(1)}, bf16[4,14,32,128]{3,2,1,0:T(8,128)(2,1)S(1)}, u32[]{:S(2)}, u32[]{:S(2)}) collective-permute-start(bf16[4,14,32,128]{3,2,1,0:T(8,128)(2,1)S(1)} %get-tuple-element.100.rest_5_), channel_id=1, source_target_pairs={{1,3},{2,0},{0,1},{3,2},{5,7},{6,4},{4,5},{7,6},{9,11},{10,8},{8,9... | collective-permute-start | bytes 1376264 | tf_op jit(solution)/shard_map/ppermute | solution.py:872
  170.6 17.2 %collective-permute-start.20 = (bf16[4,14,32,128]{3,2,1,0:T(8,128)(2,1)S(1)}, bf16[4,14,32,128]{3,2,1,0:T(8,128)(2,1)S(1)}, u32[]{:S(2)}, u32[]{:S(2)}) collective-permute-start(bf16[4,14,32,128]{3,2,1,0:T(8,128)(2,1)S(1)} %get-tuple-element.102.rest_8_), channel_id=1, source_target_pairs={{0,2},{2,0},{1,3},{3,1},{4,6},{6,4},{5,7},{7,5},{8,10},{10,8},{9,1... | collective-permute-start | bytes 1376264 | tf_op jit(solution)/shard_map/ppermute | solution.py:873
  180.3 7.5 %collective-permute-start.19 = (bf16[4,14,32,128]{3,2,1,0:T(8,128)(2,1)S(1)}, bf16[4,14,32,128]{3,2,1,0:T(8,128)(2,1)S(1)}, u32[]{:S(2)}, u32[]{:S(2)}) collective-permute-start(bf16[4,14,32,128]{3,2,1,0:T(8,128)(2,1)S(1)} %collective-permute-done.18.rest_6_), channel_id=1, source_target_pairs={{0,1},{3,2},{4,5},{7,6},{8,9},{11,10},{12,13},{15,14},{16,17},{19,... | collective-permute-start | bytes 1376264 | tf_op jit(solution)/shard_map/ppermute | solution.py:874
  187.8 32.5 %collective-permute-start.24 = (bf16[8,18,32,128]{3,2,1,0:T(8,128)(2,1)S(1)}, bf16[8,18,32,128]{3,2,1,0:T(8,128)(2,1)S(1)}, u32[]{:S(2)}, u32[]{:S(2)}) collective-permute-start(bf16[8,18,32,128]{3,2,1,0:T(8,128)(2,1)S(1)} %get-tuple-element.109.rest_0_), channel_id=1, source_target_pairs={{1,3},{2,0},{0,1},{3,2},{5,7},{6,4},{4,5},{7,6},{9,11},{10,8},{8,9... | collective-permute-start | bytes 3538952 | tf_op jit(solution)/shard_map/ppermute | solution.py:872
  187.8 5.8 %collective-permute-start.16 = (bf16[4,14,32,128]{3,2,1,0:T(8,128)(2,1)S(1)}, bf16[4,14,32,128]{3,2,1,0:T(8,128)(2,1)S(1)}, u32[]{:S(2)}, u32[]{:S(2)}) collective-permute-start(bf16[4,14,32,128]{3,2,1,0:T(8,128)(2,1)S(1)} %collective-permute-done.15.rest_1_), channel_id=1, source_target_pairs={{0,1},{3,2},{4,5},{7,6},{8,9},{11,10},{12,13},{15,14},{16,17},{19,... | collective-permute-start | bytes 1376264 | tf_op jit(solution)/shard_map/ppermute | solution.py:874
  200.6 19.8 %collective-permute-start.22 = (bf16[4,14,32,128]{3,2,1,0:T(8,128)(2,1)S(1)}, bf16[4,14,32,128]{3,2,1,0:T(8,128)(2,1)S(1)}, u32[]{:S(2)}, u32[]{:S(2)}) collective-permute-start(bf16[4,14,32,128]{3,2,1,0:T(8,128)(2,1)S(1)} %get-tuple-element.105), channel_id=1, source_target_pairs={{0,8},{4,12},{8,0},{12,4},{1,9},{5,13},{9,1},{13,5},{2,10},{6,14},... | collective-permute-start | bytes 1376264 | tf_op jit(solution)/shard_map/ppermute | solution.py:927
  200.7 27.2 %collective-permute-start.26 = (bf16[8,18,32,128]{3,2,1,0:T(8,128)(2,1)S(1)}, bf16[8,18,32,128]{3,2,1,0:T(8,128)(2,1)S(1)}, u32[]{:S(2)}, u32[]{:S(2)}) collective-permute-start(bf16[8,18,32,128]{3,2,1,0:T(8,128)(2,1)S(1)} %get-tuple-element.111.rest_3_), channel_id=1, source_target_pairs={{0,2},{2,0},{1,3},{3,1},{4,6},{6,4},{5,7},{7,5},{8,10},{10,8},{9,1... | collective-permute-start | bytes 3538952 | tf_op jit(solution)/shard_map/ppermute | solution.py:873
  220.4 7.6 %collective-permute-start.25 = (bf16[8,18,32,128]{3,2,1,0:T(8,128)(2,1)S(1)}, bf16[8,18,32,128]{3,2,1,0:T(8,128)(2,1)S(1)}, u32[]{:S(2)}, u32[]{:S(2)}) collective-permute-start(bf16[8,18,32,128]{3,2,1,0:T(8,128)(2,1)S(1)} %collective-permute-done.24.rest_1_), channel_id=1, source_target_pairs={{0,1},{3,2},{4,5},{7,6},{8,9},{11,10},{12,13},{15,14},{16,17},{19,... | collective-permute-start | bytes 3538952 | tf_op jit(solution)/shard_map/ppermute | solution.py:874
  223.2 15.3 %collective-permute-start.21 = (bf16[4,14,32,128]{3,2,1,0:T(8,128)(2,1)S(1)}, bf16[4,14,32,128]{3,2,1,0:T(8,128)(2,1)S(1)}, u32[]{:S(2)}, u32[]{:S(2)}) collective-permute-start(bf16[4,14,32,128]{3,2,1,0:T(8,128)(2,1)S(1)} %get-tuple-element.104), channel_id=1, source_target_pairs={{0,4},{4,8},{8,12},{12,0},{1,5},{5,9},{9,13},{13,1},{2,6},{6,10},{... | collective-permute-start | bytes 1376264 | tf_op jit(solution)/shard_map/ppermute | solution.py:927
  225.6 22.3 %collective-permute-start.23 = (bf16[4,14,32,128]{3,2,1,0:T(8,128)(2,1)S(1)}, bf16[4,14,32,128]{3,2,1,0:T(8,128)(2,1)S(1)}, u32[]{:S(2)}, u32[]{:S(2)}) collective-permute-start(bf16[4,14,32,128]{3,2,1,0:T(8,128)(2,1)S(1)} %get-tuple-element.106), channel_id=1, source_target_pairs={{0,12},{4,0},{8,4},{12,8},{1,13},{5,1},{9,5},{13,9},{2,14},{6,2},{... | collective-permute-start | bytes 1376264 | tf_op jit(solution)/shard_map/ppermute | solution.py:927
  247.9 15.8 %collective-permute-start.29 = (bf16[4,18,32,128]{3,2,1,0:T(8,128)(2,1)S(1)}, bf16[4,18,32,128]{3,2,1,0:T(8,128)(2,1)S(1)}, u32[]{:S(2)}, u32[]{:S(2)}) collective-permute-start(bf16[4,18,32,128]{3,2,1,0:T(8,128)(2,1)S(1)} %get-tuple-element.118), channel_id=1, source_target_pairs={{0,12},{4,0},{8,4},{12,8},{1,13},{5,1},{9,5},{13,9},{2,14},{6,2},{... | collective-permute-start | bytes 1769480 | tf_op jit(solution)/shard_map/ppermute | solution.py:927
  249.5 39.5 %collective-permute-start.28 = (bf16[4,18,32,128]{3,2,1,0:T(8,128)(2,1)S(1)}, bf16[4,18,32,128]{3,2,1,0:T(8,128)(2,1)S(1)}, u32[]{:S(2)}, u32[]{:S(2)}) collective-permute-start(bf16[4,18,32,128]{3,2,1,0:T(8,128)(2,1)S(1)} %get-tuple-element.116), channel_id=1, source_target_pairs={{0,8},{4,12},{8,0},{12,4},{1,9},{5,13},{9,1},{13,5},{2,10},{6,14},... | collective-permute-start | bytes 1769480 | tf_op jit(solution)/shard_map/ppermute | solution.py:927
  251.6 50.1 %collective-permute-start.27 = (bf16[4,18,32,128]{3,2,1,0:T(8,128)(2,1)S(1)}, bf16[4,18,32,128]{3,2,1,0:T(8,128)(2,1)S(1)}, u32[]{:S(2)}, u32[]{:S(2)}) collective-permute-start(bf16[4,18,32,128]{3,2,1,0:T(8,128)(2,1)S(1)} %get-tuple-element.114), channel_id=1, source_target_pairs={{0,4},{4,8},{8,12},{12,0},{1,5},{5,9},{9,13},{13,1},{2,6},{6,10},{... | collective-permute-start | bytes 1769480 | tf_op jit(solution)/shard_map/ppermute | solution.py:927
  (6 other events, 20.7 us)

commit v10 on v9

--- a/solution.py
+++ b/solution.py
@@ -882,7 +882,7 @@
     shifts = [far] + [s for s in range(1, n_blk) if s != far] + [0]
     layers = w_in.shape[0]
     current = pair
-    bands = [[12, 20], [14, 18]]
+    bands = [[8, 24], [12, 20]]
     chosen, place = make_plan(ids, owners, slot_of, n_blk, slots, terms, capacity)
     half = slots // 2
     halves = [(0, half), (half, slots - half)]
@@ -902,8 +902,9 @@
                 over = operands[-1][count]
                 for left, right in [(o[0], o[count]) for o in operands]:
                     if exchanged and layer % 2:
-                        (_, (one, _)), (_, (other, _)) = exchanged[-1]
+                        (_, (one, two)), (_, (other, _)) = exchanged[-1]
                         left, right = lax.optimization_barrier((left, right, one, other))[:2]
+                        right = after(right, two)
                     elif exchanged:
                         ((other, _), _), ((one, _), (_, two)) = exchanged[-1]
                         left, right = lax.optimization_barrier((left, right, other, one, two))[:2]
@@ -916,7 +917,7 @@
                 else:
                     ((other, _), _), ((one, _), (_, two)) = exchanged[-1]
                     left = after(left, other)
-                    right = after(right, one, two, made[-1])
+                    right = after(right, one, two, chosen)
                 exchanged = [exchange(left, right, arrived[-1][far])]
             made = banded_products(shifts, ids, chosen, exchanged, capacity, cols)
             parts = [None] * n_blk

time: 312 us -> 312 us (level)
  Pallas kernels: 77.7 us -> 73.2 us
    ppermute x3, waiting for transfers between devices: 6.45 us -> 17.3 us  [exchange_bands_incoming(): other = lax.ppermute(right, 'chan', [(0, 1), (1, 0)])]
    ppermute x12, waiting for transfers between devices: 139 us -> 131 us  [banded(): lax.ppermute(part, 'blk', [(p, (p + shift) % n_blk) for p in range(n_blk)])]
    pallas_call x4, Pallas kernels: 24.2 us -> 20.4 us  [banded_products(): pl.pallas_call(functools.partial(banded_kernel, shifts, capacity, tuple(p...]
  transfers between devices with their start and end apart: 30 -> 30, of which waited for: 17 -> 14; matrix products, arithmetic and copies ran while one was open for 0% -> 0% of each run, Pallas kernels for 13% -> 14%
where the time goes in v10:
time: 312 us; the launch traced here: 308 us
  waiting for transfers between devices  188 us (60%)
  Pallas kernels  73.2 us (23%)
  starting transfers between devices  44.5 us (14%)
    ppermute x12, waiting for transfers between devices, banded(): lax.ppermute(part, 'blk', [(p, (p + shift) % n_blk) for p in range(n_blk)])  131 us
    pallas_call x3, Pallas kernels, close_layer(): pl.pallas_call(functools.partial(close_kernel, *(layer, last, len(flat),...  33.4 us
    ppermute x3, waiting for transfers between devices, exchange_bands_outgoing(): one = lax.ppermute(right, both, [(0, 2), (3, 1), (1, 0), (2, 3)])  29.8 us
    pallas_call x4, Pallas kernels, banded_products(): pl.pallas_call(functools.partial(banded_kernel, shifts, capacity, tuple(p...  20.4 us
    ppermute x3, waiting for transfers between devices, exchange_bands_incoming(): other = lax.ppermute(right, 'chan', [(0, 1), (1, 0)])  17.3 us
    pallas_call x2, Pallas kernels, open_operands(): pl.pallas_call(functools.partial(open_kernel, hidden, len(bands), lax.axi...  16.7 us
    ppermute x12, starting transfers between devices, banded(): lax.ppermute(part, 'blk', [(p, (p + shift) % n_blk) for p in range(n_blk)])  14.2 us
    ppermute x3, starting transfers between devices, exchange_bands_incoming(): two = lax.ppermute(after(one, over), both, [(0, 1), (3, 2)])  12.1 us
  transfers between devices with their start and end apart: 30, of which 14 were waited for; matrix products, arithmetic and copies ran while one was open for 0% of the time, Pallas kernels for 14%

profile of v10, /device:TPU:11, one launch (start us, length us, event | category | flops | bytes accessed | tf_op | source)
XLA Modules:
  0.0 308.0 jit_solution(12112738467958807811)
XLA Ops:
  2.6 8.3 %open_operands.2 = (f32[8,32,32,128]{3,2,1,0:T(8,128)S(1)}, bf16[4,8,32,128]{3,2,1,0:T(8,128)(2,1)S(1)}, bf16[8,24,32,128]{3,2,1,0:T(8,128)(2,1)S(1)}, bf16[4,8,...) custom-call(s32[4]{0:T(128)S(1)} %pad_add_fusion.ids, s32[2,32]{1,0:T(2,128)S(1)} %bitcast.14, ...), custom_call_target="tpu_custom_call" | custom-call | flops 8589934592 | bytes 1048576 | tf_op jit(solution)/shard_map/open_operands/pallas_call | solution.py:566
  11.6 3.3 %collective-permute-start.1 = (bf16[4,8,32,128]{3,2,1,0:T(8,128)(2,1)S(1)}, bf16[4,8,32,128]{3,2,1,0:T(8,128)(2,1)S(1)}, u32[]{:S(2)}, u32[]{:S(2)}) collective-permute-start(bf16[4,8,32,128]{3,2,1,0:T(8,128)(2,1)S(1)} %get-tuple-element.67.rest_3_), channel_id=1, source_target_pairs={{0,2},{3,1},{1,0},{2,3},{4,6},{7,5},{5,4},{6,7},{8,10},{11,9},{9,8... | collective-permute-start | bytes 786440 | tf_op jit(solution)/shard_map/ppermute | solution.py:865
  14.9 8.3 %open_operands.3 = (f32[8,32,32,128]{3,2,1,0:T(8,128)S(1)}, bf16[4,8,32,128]{3,2,1,0:T(8,128)(2,1)S(1)}, bf16[8,24,32,128]{3,2,1,0:T(8,128)(2,1)S(1)}, bf16[4,8,...) custom-call(s32[4]{0:T(128)S(1)} %pad_add_fusion.ids, ...), custom_call_target="tpu_custom_call", output_to_operand_aliasing={{0}: (6, {}), {2}: (7, {}), {4}: (8, {})} | custom-call | flops 8589934592 | bytes 1048576 | tf_op jit(solution)/shard_map/open_operands/pallas_call | solution.py:566
  24.0 3.1 %collective-permute-start.4 = (bf16[4,8,32,128]{3,2,1,0:T(8,128)(2,1)S(1)}, bf16[4,8,32,128]{3,2,1,0:T(8,128)(2,1)S(1)}, u32[]{:S(2)}, u32[]{:S(2)}) collective-permute-start(bf16[4,8,32,128]{3,2,1,0:T(8,128)(2,1)S(1)} %get-tuple-element.74.rest_8_), channel_id=1, source_target_pairs={{0,2},{3,1},{1,0},{2,3},{4,6},{7,5},{5,4},{6,7},{8,10},{11,9},{9,8... | collective-permute-start | bytes 786440 | tf_op jit(solution)/shard_map/ppermute | solution.py:865
  28.7 3.6 %collective-permute-done.4.rest_7_ = bf16[4,8,32,128]{3,2,1,0:T(8,128)(2,1)S(1)} collective-permute-done((bf16[4,8,32,128]{3,2,1,0:T(8,128)(2,1)S(1)}, bf16[4,8,32,128]{3,2,1,0:T(8,128)(2,1)S(1)}, u32[]{:S(2)}, u32[]{:S(2)}) %collective-permute-start.4) | collective-permute-done | bytes 262176 | tf_op jit(solution)/shard_map/ppermute | solution.py:865
  33.0 4.5 %collective-permute-start.10 = (bf16[8,24,32,128]{3,2,1,0:T(8,128)(2,1)S(1)}, bf16[8,24,32,128]{3,2,1,0:T(8,128)(2,1)S(1)}, u32[]{:S(2)}, u32[]{:S(2)}) collective-permute-start(bf16[8,24,32,128]{3,2,1,0:T(8,128)(2,1)S(1)} %get-tuple-element.82.rest_3_), channel_id=1, source_target_pairs={{0,2},{3,1},{1,0},{2,3},{4,6},{7,5},{5,4},{6,7},{8,10},{11,9},{9,8... | collective-permute-start | bytes 4718600 | tf_op jit(solution)/shard_map/ppermute | solution.py:865
  37.6 3.2 %banded_products.4 = (bf16[4,8,32,128]{3,2,1,0:T(8,128)(2,1)S(1)}, bf16[4,8,32,128]{3,2,1,0:T(8,128)(2,1)S(1)}, bf16[4,8,32,128]{3,2,1,0:T(8,128)(2,1)S(1)}, bf16[4,8,32,128]{3,2,1,0:T(8,128)(2,1)S(1)}) custom-call(s32[4]{0:T(128)S(1)} %pad_add_fusion.ids, s32[40]{0:T(128)S(1)} %get-tuple-element.65.chosen, ...), custom_call_target="tpu_custom_call" | custom-call | flops 268435456 | bytes 1 | tf_op jit(solution)/shard_map/banded_products/pallas_call | solution.py:699
  44.6 26.3 %collective-permute-done.10.rest_2_ = bf16[8,24,32,128]{3,2,1,0:T(8,128)(2,1)S(1)} collective-permute-done((bf16[8,24,32,128]{3,2,1,0:T(8,128)(2,1)S(1)}, bf16[8,24,32,128]{3,2,1,0:T(8,128)(2,1)S(1)}, u32[]{:S(2)}, u32[]{:S(2)}) %collective-permute-start.10) | collective-permute-done | bytes 1572896 | tf_op jit(solution)/shard_map/ppermute | solution.py:865
  70.9 5.8 %banded_products.5 = (bf16[4,24,32,128]{3,2,1,0:T(8,128)(2,1)S(1)}, bf16[4,24,32,128]{3,2,1,0:T(8,128)(2,1)S(1)}, bf16[4,24,32,128]{3,2,1,0:T(8,128)(2,1)S(1)}, bf16[4,24,32,128]{3,2,1,0:T(8,128)(2,1)S(1)}) custom-call(s32[4]{0:T(128)S(1)} %pad_add_fusion.ids, s32[40]{0:T(128)S(1)} %get-tuple-element.65.chosen, ...), custom_call_target="tpu_custom_call" | custom-call | flops 805306368 | bytes 1 | tf_op jit(solution)/shard_map/banded_products/pallas_call | solution.py:699
  76.9 2.3 collective-permute-start.13
  79.2 2.2 collective-permute-start.12
  81.9 11.8 %collective-permute-done.14.rest_7_ = bf16[4,24,32,128]{3,2,1,0:T(8,128)(2,1)S(1)} collective-permute-done((bf16[4,24,32,128]{3,2,1,0:T(8,128)(2,1)S(1)}, bf16[4,24,32,128]{3,2,1,0:T(8,128)(2,1)S(1)}, u32[]{:S(2)}, u32[]{:S(2)}) %collective-permute-start.14) | collective-permute-done | bytes 786464 | tf_op jit(solution)/shard_map/ppermute | solution.py:928
  93.7 35.6 %collective-permute-done.13.rest_6_ = bf16[4,24,32,128]{3,2,1,0:T(8,128)(2,1)S(1)} collective-permute-done((bf16[4,24,32,128]{3,2,1,0:T(8,128)(2,1)S(1)}, bf16[4,24,32,128]{3,2,1,0:T(8,128)(2,1)S(1)}, u32[]{:S(2)}, u32[]{:S(2)}) %collective-permute-start.13) | collective-permute-done | bytes 786464 | tf_op jit(solution)/shard_map/ppermute | solution.py:928
  129.4 16.9 %collective-permute-done.12.rest_5_ = bf16[4,24,32,128]{3,2,1,0:T(8,128)(2,1)S(1)} collective-permute-done((bf16[4,24,32,128]{3,2,1,0:T(8,128)(2,1)S(1)}, bf16[4,24,32,128]{3,2,1,0:T(8,128)(2,1)S(1)}, u32[]{:S(2)}, u32[]{:S(2)}) %collective-permute-start.12) | collective-permute-done | bytes 786464 | tf_op jit(solution)/shard_map/ppermute | solution.py:928
  146.2 12.2 %close_layer.3 = (bf16[8,32,32,128]{3,2,1,0:T(8,128)(2,1)S(1)}, f32[8,32,32,128]{3,2,1,0:T(8,128)S(1)}, bf16[4,12,32,128]{3,2,1,0:T(8,128)(2,1)S(1)}, bf16[8,20,...) custom-call(s32[4]{0:T(128)S(1)} %pad_add_fusion.ids, ...), custom_call_target="tpu_custom_call" | custom-call | flops 8589934592 | bytes 1048576 | tf_op jit(solution)/shard_map/close_layer/pallas_call | solution.py:838
  159.8 1.7 collective-permute-start.17
  161.5 12.2 %close_layer.4 = (bf16[8,32,32,128]{3,2,1,0:T(8,128)(2,1)S(1)}, f32[8,32,32,128]{3,2,1,0:T(8,128)S(1)}, bf16[4,12,32,128]{3,2,1,0:T(8,128)(2,1)S(1)}, bf16[8,20,...) custom-call(s32[4]{0:T(128)S(1)} %pad_add_fusion.ids, ...), custom_call_target="tpu_custom_call", output_to_operand_aliasing={{0}: (17, {}), {1}: (18, {}), {3}: (19, {}), {5}: (20, {})} | custom-call | flops 8589934592 | bytes 1048576 | tf_op jit(solution)/shard_map/close_layer/pallas_call | solution.py:838
  173.8 2.6 collective-permute-start.16
  178.5 6.9 %collective-permute-done.18.rest_6_ = bf16[4,12,32,128]{3,2,1,0:T(8,128)(2,1)S(1)} collective-permute-done((bf16[4,12,32,128]{3,2,1,0:T(8,128)(2,1)S(1)}, bf16[4,12,32,128]{3,2,1,0:T(8,128)(2,1)S(1)}, u32[]{:S(2)}, u32[]{:S(2)}) %collective-permute-start.18) | collective-permute-done | bytes 393248 | tf_op jit(solution)/shard_map/ppermute | solution.py:872
  185.4 3.0 collective-permute-start.19
  188.4 3.1 %collective-permute-done.20.rest_9_ = bf16[4,12,32,128]{3,2,1,0:T(8,128)(2,1)S(1)} collective-permute-done((bf16[4,12,32,128]{3,2,1,0:T(8,128)(2,1)S(1)}, bf16[4,12,32,128]{3,2,1,0:T(8,128)(2,1)S(1)}, u32[]{:S(2)}, u32[]{:S(2)}) %collective-permute-start.20) | collective-permute-done | bytes 393248 | tf_op jit(solution)/shard_map/ppermute | solution.py:873
  191.5 5.7 %banded_products.6 = (bf16[4,12,32,128]{3,2,1,0:T(8,128)(2,1)S(1)}, bf16[4,12,32,128]{3,2,1,0:T(8,128)(2,1)S(1)}, bf16[4,12,32,128]{3,2,1,0:T(8,128)(2,1)S(1)}, bf16[4,12,32,128]{3,2,1,0:T(8,128)(2,1)S(1)}) custom-call(s32[4]{0:T(128)S(1)} %pad_add_fusion.ids, s32[40]{0:T(128)S(1)} %get-tuple-element.65.chosen, ...), custom_call_target="tpu_custom_call" | custom-call | flops 402653184 | bytes 1 | tf_op jit(solution)/shard_map/banded_products/pallas_call | solution.py:699
  198.9 13.3 %collective-permute-done.22.rest_2_ = bf16[4,12,32,128]{3,2,1,0:T(8,128)(2,1)S(1)} collective-permute-done((bf16[4,12,32,128]{3,2,1,0:T(8,128)(2,1)S(1)}, bf16[4,12,32,128]{3,2,1,0:T(8,128)(2,1)S(1)}, u32[]{:S(2)}, u32[]{:S(2)}) %collective-permute-start.22) | collective-permute-done | bytes 393248 | tf_op jit(solution)/shard_map/ppermute | solution.py:928
  213.6 6.4 %collective-permute-start.25 = (bf16[8,20,32,128]{3,2,1,0:T(8,128)(2,1)S(1)}, bf16[8,20,32,128]{3,2,1,0:T(8,128)(2,1)S(1)}, u32[]{:S(2)}, u32[]{:S(2)}) collective-permute-start(bf16[8,20,32,128]{3,2,1,0:T(8,128)(2,1)S(1)} %collective-permute-done.24.rest_1_), channel_id=1, source_target_pairs={{0,1},{3,2},{4,5},{7,6},{8,9},{11,10},{12,13},{15,14},{16,17},{19,... | collective-permute-start | bytes 3932168 | tf_op jit(solution)/shard_map/ppermute | solution.py:874
  220.0 2.2 collective-permute-start.21
  222.2 14.1 %collective-permute-done.26.rest_4_ = bf16[8,20,32,128]{3,2,1,0:T(8,128)(2,1)S(1)} collective-permute-done((bf16[8,20,32,128]{3,2,1,0:T(8,128)(2,1)S(1)}, bf16[8,20,32,128]{3,2,1,0:T(8,128)(2,1)S(1)}, u32[]{:S(2)}, u32[]{:S(2)}) %collective-permute-start.26) | collective-permute-done | bytes 1310752 | tf_op jit(solution)/shard_map/ppermute | solution.py:873
  236.4 5.7 %banded_products.7 = (bf16[4,20,32,128]{3,2,1,0:T(8,128)(2,1)S(1)}, bf16[4,20,32,128]{3,2,1,0:T(8,128)(2,1)S(1)}, bf16[4,20,32,128]{3,2,1,0:T(8,128)(2,1)S(1)}, bf16[4,20,32,128]{3,2,1,0:T(8,128)(2,1)S(1)}) custom-call(s32[4]{0:T(128)S(1)} %pad_add_fusion.ids, s32[40]{0:T(128)S(1)} %get-tuple-element.65.chosen, ...), custom_call_target="tpu_custom_call" | custom-call | flops 671088640 | bytes 1 | tf_op jit(solution)/shard_map/banded_products/pallas_call | solution.py:699
  242.6 2.9 collective-permute-start.28
  245.5 13.3 %collective-permute-done.29.rest_7_ = bf16[4,20,32,128]{3,2,1,0:T(8,128)(2,1)S(1)} collective-permute-done((bf16[4,20,32,128]{3,2,1,0:T(8,128)(2,1)S(1)}, bf16[4,20,32,128]{3,2,1,0:T(8,128)(2,1)S(1)}, u32[]{:S(2)}, u32[]{:S(2)}) %collective-permute-start.29) | collective-permute-done | bytes 655392 | tf_op jit(solution)/shard_map/ppermute | solution.py:928
  258.8 26.1 %collective-permute-done.28.rest_6_ = bf16[4,20,32,128]{3,2,1,0:T(8,128)(2,1)S(1)} collective-permute-done((bf16[4,20,32,128]{3,2,1,0:T(8,128)(2,1)S(1)}, bf16[4,20,32,128]{3,2,1,0:T(8,128)(2,1)S(1)}, u32[]{:S(2)}, u32[]{:S(2)}) %collective-permute-start.28) | collective-permute-done | bytes 655392 | tf_op jit(solution)/shard_map/ppermute | solution.py:928
  284.9 14.0 %collective-permute-done.27.rest_5_ = bf16[4,20,32,128]{3,2,1,0:T(8,128)(2,1)S(1)} collective-permute-done((bf16[4,20,32,128]{3,2,1,0:T(8,128)(2,1)S(1)}, bf16[4,20,32,128]{3,2,1,0:T(8,128)(2,1)S(1)}, u32[]{:S(2)}, u32[]{:S(2)}) %collective-permute-start.27) | collective-permute-done | bytes 655392 | tf_op jit(solution)/shard_map/ppermute | solution.py:928
  298.9 8.9 %close_layer.5 = bf16[8,32,32,128]{3,2,1,0:T(8,128)(2,1)} custom-call(s32[4]{0:T(128)S(1)} %pad_add_fusion.ids, s32[2,32]{1,0:T(2,128)S(1)} %bitcast.18, s32[16]{0:T(128)S(1)} %get-tuple-element.64.place, bf16[4,12,32,128]{3,2,1,0:T(8,128)(2,1)S(1)} %get-tuple-element.105.rest_0_, bf16[4,12,32,128]{3,2,1,0:T(8,128)(2,1)S(1)} %collective-permute-done.21.rest_1_, ...), custom_call_target="tpu_custom_call" | custom-call | flops 8589934592 | bytes 1048576 | tf_op jit(solution)/shard_map/close_layer/pallas_call | solution.py:838
  (57 shorter events, 17.8 us)
Async XLA Ops:
  10.9 12.4 %collective-permute-start.2 = (bf16[4,8,32,128]{3,2,1,0:T(8,128)(2,1)S(1)}, bf16[4,8,32,128]{3,2,1,0:T(8,128)(2,1)S(1)}, u32[]{:S(2)}, u32[]{:S(2)}) collective-permute-start(bf16[4,8,32,128]{3,2,1,0:T(8,128)(2,1)S(1)} %get-tuple-element.67.rest_3_), channel_id=1, source_target_pairs={{1,2},{2,1},{5,6},{6,5},{9,10},{10,9},{13,14},{14,13},{17,18},{18,... | collective-permute-start | bytes 786440 | tf_op jit(solution)/shard_map/ppermute | solution.py:866
  11.6 11.7 %collective-permute-start.1 = (bf16[4,8,32,128]{3,2,1,0:T(8,128)(2,1)S(1)}, bf16[4,8,32,128]{3,2,1,0:T(8,128)(2,1)S(1)}, u32[]{:S(2)}, u32[]{:S(2)}) collective-permute-start(bf16[4,8,32,128]{3,2,1,0:T(8,128)(2,1)S(1)} %get-tuple-element.67.rest_3_), channel_id=1, source_target_pairs={{0,2},{3,1},{1,0},{2,3},{4,6},{7,5},{5,4},{6,7},{8,10},{11,9},{9,8... | collective-permute-start | bytes 786440 | tf_op jit(solution)/shard_map/ppermute | solution.py:865
  14.9 8.4 %collective-permute-start = (bf16[4,8,32,128]{3,2,1,0:T(8,128)(2,1)S(1)}, bf16[4,8,32,128]{3,2,1,0:T(8,128)(2,1)S(1)}, u32[]{:S(2)}, u32[]{:S(2)}) collective-permute-start(bf16[4,8,32,128]{3,2,1,0:T(8,128)(2,1)S(1)} %get-tuple-element.66.rest_1_), channel_id=1, source_target_pairs={{0,1},{1,0},{2,3},{3,2},{4,5},{5,4},{6,7},{7,6},{8,9},{9,8},{10,11... | collective-permute-start | bytes 786440 | tf_op jit(solution)/shard_map/ppermute | solution.py:864
  14.9 12.2 %copy-start.1 = (s32[32,2]{0,1:T(2,128)S(1)}, s32[32,2]{0,1:T(2,128)}, u32[]{:S(2)}) copy-start(s32[32,2]{0,1:T(2,128)} %param.9) | copy-start | bytes 772
  23.3 5.4 %collective-permute-start.5 = (bf16[4,8,32,128]{3,2,1,0:T(8,128)(2,1)S(1)}, bf16[4,8,32,128]{3,2,1,0:T(8,128)(2,1)S(1)}, u32[]{:S(2)}, u32[]{:S(2)}) collective-permute-start(bf16[4,8,32,128]{3,2,1,0:T(8,128)(2,1)S(1)} %get-tuple-element.74.rest_8_), channel_id=1, source_target_pairs={{1,2},{2,1},{5,6},{6,5},{9,10},{10,9},{13,14},{14,13},{17,18},{18,... | collective-permute-start | bytes 786440 | tf_op jit(solution)/shard_map/ppermute | solution.py:866
  24.0 8.3 %collective-permute-start.4 = (bf16[4,8,32,128]{3,2,1,0:T(8,128)(2,1)S(1)}, bf16[4,8,32,128]{3,2,1,0:T(8,128)(2,1)S(1)}, u32[]{:S(2)}, u32[]{:S(2)}) collective-permute-start(bf16[4,8,32,128]{3,2,1,0:T(8,128)(2,1)S(1)} %get-tuple-element.74.rest_8_), channel_id=1, source_target_pairs={{0,2},{3,1},{1,0},{2,3},{4,6},{7,5},{5,4},{6,7},{8,10},{11,9},{9,8... | collective-permute-start | bytes 786440 | tf_op jit(solution)/shard_map/ppermute | solution.py:865
  27.1 10.5 %collective-permute-start.3 = (bf16[4,8,32,128]{3,2,1,0:T(8,128)(2,1)S(1)}, bf16[4,8,32,128]{3,2,1,0:T(8,128)(2,1)S(1)}, u32[]{:S(2)}, u32[]{:S(2)}) collective-permute-start(bf16[4,8,32,128]{3,2,1,0:T(8,128)(2,1)S(1)} %get-tuple-element.73.rest_6_), channel_id=1, source_target_pairs={{0,1},{1,0},{2,3},{3,2},{4,5},{5,4},{6,7},{7,6},{8,9},{9,8},{10,11... | collective-permute-start | bytes 786440 | tf_op jit(solution)/shard_map/ppermute | solution.py:864
  32.3 10.9 %collective-permute-start.11 = (bf16[8,24,32,128]{3,2,1,0:T(8,128)(2,1)S(1)}, bf16[8,24,32,128]{3,2,1,0:T(8,128)(2,1)S(1)}, u32[]{:S(2)}, u32[]{:S(2)}) collective-permute-start(bf16[8,24,32,128]{3,2,1,0:T(8,128)(2,1)S(1)} %get-tuple-element.82.rest_3_), channel_id=1, source_target_pairs={{1,2},{2,1},{5,6},{6,5},{9,10},{10,9},{13,14},{14,13},{17,18},{18,... | collective-permute-start | bytes 4718600 | tf_op jit(solution)/shard_map/ppermute | solution.py:866
  33.0 37.8 %collective-permute-start.10 = (bf16[8,24,32,128]{3,2,1,0:T(8,128)(2,1)S(1)}, bf16[8,24,32,128]{3,2,1,0:T(8,128)(2,1)S(1)}, u32[]{:S(2)}, u32[]{:S(2)}) collective-permute-start(bf16[8,24,32,128]{3,2,1,0:T(8,128)(2,1)S(1)} %get-tuple-element.82.rest_3_), channel_id=1, source_target_pairs={{0,2},{3,1},{1,0},{2,3},{4,6},{7,5},{5,4},{6,7},{8,10},{11,9},{9,8... | collective-permute-start | bytes 4718600 | tf_op jit(solution)/shard_map/ppermute | solution.py:865
  37.6 33.3 %collective-permute-start.9 = (bf16[8,24,32,128]{3,2,1,0:T(8,128)(2,1)S(1)}, bf16[8,24,32,128]{3,2,1,0:T(8,128)(2,1)S(1)}, u32[]{:S(2)}, u32[]{:S(2)}) collective-permute-start(bf16[8,24,32,128]{3,2,1,0:T(8,128)(2,1)S(1)} %get-tuple-element.80.rest_1_), channel_id=1, source_target_pairs={{0,1},{1,0},{2,3},{3,2},{4,5},{5,4},{6,7},{7,6},{8,9},{9,8},{10,11... | collective-permute-start | bytes 4718600 | tf_op jit(solution)/shard_map/ppermute | solution.py:864
  40.8 35.9 %collective-permute-start.6 = (bf16[4,8,32,128]{3,2,1,0:T(8,128)(2,1)S(1)}, bf16[4,8,32,128]{3,2,1,0:T(8,128)(2,1)S(1)}, u32[]{:S(2)}, u32[]{:S(2)}) collective-permute-start(bf16[4,8,32,128]{3,2,1,0:T(8,128)(2,1)S(1)} %get-tuple-element.76), channel_id=1, source_target_pairs={{0,4},{4,8},{8,12},{12,0},{1,5},{5,9},{9,13},{13,1},{2,6},{6,10},{... | collective-permute-start | bytes 786440 | tf_op jit(solution)/shard_map/ppermute | solution.py:928
  42.1 34.5 %collective-permute-start.7 = (bf16[4,8,32,128]{3,2,1,0:T(8,128)(2,1)S(1)}, bf16[4,8,32,128]{3,2,1,0:T(8,128)(2,1)S(1)}, u32[]{:S(2)}, u32[]{:S(2)}) collective-permute-start(bf16[4,8,32,128]{3,2,1,0:T(8,128)(2,1)S(1)} %get-tuple-element.77), channel_id=1, source_target_pairs={{0,8},{4,12},{8,0},{12,4},{1,9},{5,13},{9,1},{13,5},{2,10},{6,14},... | collective-permute-start | bytes 786440 | tf_op jit(solution)/shard_map/ppermute | solution.py:928
  43.2 33.5 %collective-permute-start.8 = (bf16[4,8,32,128]{3,2,1,0:T(8,128)(2,1)S(1)}, bf16[4,8,32,128]{3,2,1,0:T(8,128)(2,1)S(1)}, u32[]{:S(2)}, u32[]{:S(2)}) collective-permute-start(bf16[4,8,32,128]{3,2,1,0:T(8,128)(2,1)S(1)} %get-tuple-element.78), channel_id=1, source_target_pairs={{0,12},{4,0},{8,4},{12,8},{1,13},{5,1},{9,5},{13,9},{2,14},{6,2},{... | collective-permute-start | bytes 786440 | tf_op jit(solution)/shard_map/ppermute | solution.py:928
  76.7 17.1 %collective-permute-start.14 = (bf16[4,24,32,128]{3,2,1,0:T(8,128)(2,1)S(1)}, bf16[4,24,32,128]{3,2,1,0:T(8,128)(2,1)S(1)}, u32[]{:S(2)}, u32[]{:S(2)}) collective-permute-start(bf16[4,24,32,128]{3,2,1,0:T(8,128)(2,1)S(1)} %get-tuple-element.89), channel_id=1, source_target_pairs={{0,12},{4,0},{8,4},{12,8},{1,13},{5,1},{9,5},{13,9},{2,14},{6,2},{... | collective-permute-start | bytes 2359304 | tf_op jit(solution)/shard_map/ppermute | solution.py:928
  76.9 52.5 %collective-permute-start.13 = (bf16[4,24,32,128]{3,2,1,0:T(8,128)(2,1)S(1)}, bf16[4,24,32,128]{3,2,1,0:T(8,128)(2,1)S(1)}, u32[]{:S(2)}, u32[]{:S(2)}) collective-permute-start(bf16[4,24,32,128]{3,2,1,0:T(8,128)(2,1)S(1)} %get-tuple-element.87), channel_id=1, source_target_pairs={{0,8},{4,12},{8,0},{12,4},{1,9},{5,13},{9,1},{13,5},{2,10},{6,14},... | collective-permute-start | bytes 2359304 | tf_op jit(solution)/shard_map/ppermute | solution.py:928
  79.2 67.1 %collective-permute-start.12 = (bf16[4,24,32,128]{3,2,1,0:T(8,128)(2,1)S(1)}, bf16[4,24,32,128]{3,2,1,0:T(8,128)(2,1)S(1)}, u32[]{:S(2)}, u32[]{:S(2)}) collective-permute-start(bf16[4,24,32,128]{3,2,1,0:T(8,128)(2,1)S(1)} %get-tuple-element.85), channel_id=1, source_target_pairs={{0,4},{4,8},{8,12},{12,0},{1,5},{5,9},{9,13},{13,1},{2,6},{6,10},{... | collective-permute-start | bytes 2359304 | tf_op jit(solution)/shard_map/ppermute | solution.py:928
  81.4 64.9 %copy-start.5 = (bf16[2,128,128]{2,1,0:T(8,128)(2,1)S(1)}, bf16[2,128,128]{2,1,0:T(8,128)(2,1)}, u32[]{:S(2)}) copy-start(bf16[2,128,128]{2,1,0:T(8,128)(2,1)} %rest_10_.5) | copy-start | bytes 196612
  158.5 15.3 %collective-permute-start.15 = (bf16[4,12,32,128]{3,2,1,0:T(8,128)(2,1)S(1)}, bf16[4,12,32,128]{3,2,1,0:T(8,128)(2,1)S(1)}, u32[]{:S(2)}, u32[]{:S(2)}) collective-permute-start(bf16[4,12,32,128]{3,2,1,0:T(8,128)(2,1)S(1)} %get-tuple-element.92.rest_0_), channel_id=1, source_target_pairs={{1,3},{2,0},{0,1},{3,2},{5,7},{6,4},{4,5},{7,6},{9,11},{10,8},{8,9... | collective-permute-start | bytes 1179656 | tf_op jit(solution)/shard_map/ppermute | solution.py:872
  159.8 16.6 %collective-permute-start.17 = (bf16[4,12,32,128]{3,2,1,0:T(8,128)(2,1)S(1)}, bf16[4,12,32,128]{3,2,1,0:T(8,128)(2,1)S(1)}, u32[]{:S(2)}, u32[]{:S(2)}) collective-permute-start(bf16[4,12,32,128]{3,2,1,0:T(8,128)(2,1)S(1)} %get-tuple-element.99.rest_3_), channel_id=1, source_target_pairs={{0,2},{2,0},{1,3},{3,1},{4,6},{6,4},{5,7},{7,5},{8,10},{10,8},{9,1... | collective-permute-start | bytes 1179656 | tf_op jit(solution)/shard_map/ppermute | solution.py:873
  173.8 4.0 %collective-permute-start.16 = (bf16[4,12,32,128]{3,2,1,0:T(8,128)(2,1)S(1)}, bf16[4,12,32,128]{3,2,1,0:T(8,128)(2,1)S(1)}, u32[]{:S(2)}, u32[]{:S(2)}) collective-permute-start(bf16[4,12,32,128]{3,2,1,0:T(8,128)(2,1)S(1)} %collective-permute-done.15.rest_1_), channel_id=1, source_target_pairs={{0,1},{3,2},{4,5},{7,6},{8,9},{11,10},{12,13},{15,14},{16,17},{19,... | collective-permute-start | bytes 1179656 | tf_op jit(solution)/shard_map/ppermute | solution.py:874
  176.4 9.0 %collective-permute-start.18 = (bf16[4,12,32,128]{3,2,1,0:T(8,128)(2,1)S(1)}, bf16[4,12,32,128]{3,2,1,0:T(8,128)(2,1)S(1)}, u32[]{:S(2)}, u32[]{:S(2)}) collective-permute-start(bf16[4,12,32,128]{3,2,1,0:T(8,128)(2,1)S(1)} %get-tuple-element.101.rest_5_), channel_id=1, source_target_pairs={{1,3},{2,0},{0,1},{3,2},{5,7},{6,4},{4,5},{7,6},{9,11},{10,8},{8,9... | collective-permute-start | bytes 1179656 | tf_op jit(solution)/shard_map/ppermute | solution.py:872
  177.7 13.8 %collective-permute-start.20 = (bf16[4,12,32,128]{3,2,1,0:T(8,128)(2,1)S(1)}, bf16[4,12,32,128]{3,2,1,0:T(8,128)(2,1)S(1)}, u32[]{:S(2)}, u32[]{:S(2)}) collective-permute-start(bf16[4,12,32,128]{3,2,1,0:T(8,128)(2,1)S(1)} %get-tuple-element.104.rest_8_), channel_id=1, source_target_pairs={{0,2},{2,0},{1,3},{3,1},{4,6},{6,4},{5,7},{7,5},{8,10},{10,8},{9,1... | collective-permute-start | bytes 1179656 | tf_op jit(solution)/shard_map/ppermute | solution.py:873
  185.4 6.1 %collective-permute-start.19 = (bf16[4,12,32,128]{3,2,1,0:T(8,128)(2,1)S(1)}, bf16[4,12,32,128]{3,2,1,0:T(8,128)(2,1)S(1)}, u32[]{:S(2)}, u32[]{:S(2)}) collective-permute-start(bf16[4,12,32,128]{3,2,1,0:T(8,128)(2,1)S(1)} %collective-permute-done.18.rest_6_), channel_id=1, source_target_pairs={{0,1},{3,2},{4,5},{7,6},{8,9},{11,10},{12,13},{15,14},{16,17},{19,... | collective-permute-start | bytes 1179656 | tf_op jit(solution)/shard_map/ppermute | solution.py:874
  191.5 22.1 %collective-permute-start.24 = (bf16[8,20,32,128]{3,2,1,0:T(8,128)(2,1)S(1)}, bf16[8,20,32,128]{3,2,1,0:T(8,128)(2,1)S(1)}, u32[]{:S(2)}, u32[]{:S(2)}) collective-permute-start(bf16[8,20,32,128]{3,2,1,0:T(8,128)(2,1)S(1)} %get-tuple-element.111.rest_0_), channel_id=1, source_target_pairs={{1,3},{2,0},{0,1},{3,2},{5,7},{6,4},{4,5},{7,6},{9,11},{10,8},{8,9... | collective-permute-start | bytes 3932168 | tf_op jit(solution)/shard_map/ppermute | solution.py:872
  197.3 14.9 %collective-permute-start.22 = (bf16[4,12,32,128]{3,2,1,0:T(8,128)(2,1)S(1)}, bf16[4,12,32,128]{3,2,1,0:T(8,128)(2,1)S(1)}, u32[]{:S(2)}, u32[]{:S(2)}) collective-permute-start(bf16[4,12,32,128]{3,2,1,0:T(8,128)(2,1)S(1)} %get-tuple-element.107), channel_id=1, source_target_pairs={{0,8},{4,12},{8,0},{12,4},{1,9},{5,13},{9,1},{13,5},{2,10},{6,14},... | collective-permute-start | bytes 1179656 | tf_op jit(solution)/shard_map/ppermute | solution.py:928
  197.3 39.0 %collective-permute-start.26 = (bf16[8,20,32,128]{3,2,1,0:T(8,128)(2,1)S(1)}, bf16[8,20,32,128]{3,2,1,0:T(8,128)(2,1)S(1)}, u32[]{:S(2)}, u32[]{:S(2)}) collective-permute-start(bf16[8,20,32,128]{3,2,1,0:T(8,128)(2,1)S(1)} %get-tuple-element.113.rest_3_), channel_id=1, source_target_pairs={{0,2},{2,0},{1,3},{3,1},{4,6},{6,4},{5,7},{7,5},{8,10},{10,8},{9,1... | collective-permute-start | bytes 3932168 | tf_op jit(solution)/shard_map/ppermute | solution.py:873
  213.6 22.8 %collective-permute-start.25 = (bf16[8,20,32,128]{3,2,1,0:T(8,128)(2,1)S(1)}, bf16[8,20,32,128]{3,2,1,0:T(8,128)(2,1)S(1)}, u32[]{:S(2)}, u32[]{:S(2)}) collective-permute-start(bf16[8,20,32,128]{3,2,1,0:T(8,128)(2,1)S(1)} %collective-permute-done.24.rest_1_), channel_id=1, source_target_pairs={{0,1},{3,2},{4,5},{7,6},{8,9},{11,10},{12,13},{15,14},{16,17},{19,... | collective-permute-start | bytes 3932168 | tf_op jit(solution)/shard_map/ppermute | solution.py:874
  220.0 22.1 %collective-permute-start.21 = (bf16[4,12,32,128]{3,2,1,0:T(8,128)(2,1)S(1)}, bf16[4,12,32,128]{3,2,1,0:T(8,128)(2,1)S(1)}, u32[]{:S(2)}, u32[]{:S(2)}) collective-permute-start(bf16[4,12,32,128]{3,2,1,0:T(8,128)(2,1)S(1)} %get-tuple-element.106), channel_id=1, source_target_pairs={{0,4},{4,8},{8,12},{12,0},{1,5},{5,9},{9,13},{13,1},{2,6},{6,10},{... | collective-permute-start | bytes 1179656 | tf_op jit(solution)/shard_map/ppermute | solution.py:928
  222.2 19.9 %collective-permute-start.23 = (bf16[4,12,32,128]{3,2,1,0:T(8,128)(2,1)S(1)}, bf16[4,12,32,128]{3,2,1,0:T(8,128)(2,1)S(1)}, u32[]{:S(2)}, u32[]{:S(2)}) collective-permute-start(bf16[4,12,32,128]{3,2,1,0:T(8,128)(2,1)S(1)} %get-tuple-element.108), channel_id=1, source_target_pairs={{0,12},{4,0},{8,4},{12,8},{1,13},{5,1},{9,5},{13,9},{2,14},{6,2},{... | collective-permute-start | bytes 1179656 | tf_op jit(solution)/shard_map/ppermute | solution.py:928
  242.1 16.7 %collective-permute-start.29 = (bf16[4,20,32,128]{3,2,1,0:T(8,128)(2,1)S(1)}, bf16[4,20,32,128]{3,2,1,0:T(8,128)(2,1)S(1)}, u32[]{:S(2)}, u32[]{:S(2)}) collective-permute-start(bf16[4,20,32,128]{3,2,1,0:T(8,128)(2,1)S(1)} %get-tuple-element.120), channel_id=1, source_target_pairs={{0,12},{4,0},{8,4},{12,8},{1,13},{5,1},{9,5},{13,9},{2,14},{6,2},{... | collective-permute-start | bytes 1966088 | tf_op jit(solution)/shard_map/ppermute | solution.py:928
  242.6 42.3 %collective-permute-start.28 = (bf16[4,20,32,128]{3,2,1,0:T(8,128)(2,1)S(1)}, bf16[4,20,32,128]{3,2,1,0:T(8,128)(2,1)S(1)}, u32[]{:S(2)}, u32[]{:S(2)}) collective-permute-start(bf16[4,20,32,128]{3,2,1,0:T(8,128)(2,1)S(1)} %get-tuple-element.118), channel_id=1, source_target_pairs={{0,8},{4,12},{8,0},{12,4},{1,9},{5,13},{9,1},{13,5},{2,10},{6,14},... | collective-permute-start | bytes 1966088 | tf_op jit(solution)/shard_map/ppermute | solution.py:928
  245.5 53.4 %collective-permute-start.27 = (bf16[4,20,32,128]{3,2,1,0:T(8,128)(2,1)S(1)}, bf16[4,20,32,128]{3,2,1,0:T(8,128)(2,1)S(1)}, u32[]{:S(2)}, u32[]{:S(2)}) collective-permute-start(bf16[4,20,32,128]{3,2,1,0:T(8,128)(2,1)S(1)} %get-tuple-element.116), channel_id=1, source_target_pairs={{0,4},{4,8},{8,12},{12,0},{1,5},{5,9},{9,13},{13,1},{2,6},{6,10},{... | collective-permute-start | bytes 1966088 | tf_op jit(solution)/shard_map/ppermute | solution.py:928
  (6 other events, 19.5 us)

commit v11 on v10

--- a/solution.py
+++ b/solution.py
@@ -500,12 +500,13 @@
         make_operand(side, natural if side == layer % 2 else turned[...], wide, refs, laid, swap)
 
 
-def norm_and_gate(values, row_alive, col_alive, w_ref, at, norm_ref, gate_ref):
+def norm_and_gate(values, row_alive, col_alive, at, norm_ref, w_ref=None, gate_ref=None):
     _, cols, channels = norm_ref.shape
     rows = values.shape[0] // cols
     normed = layer_norm(values)
-    gate = sigmoid(dot(normed.astype(jnp.bfloat16), w_ref[0, :, -channels:]))
-    gate_ref[0, pl.ds(at, rows)] = gate.reshape(rows, cols, channels)
+    if gate_ref is not None:
+        gate = sigmoid(dot(normed.astype(jnp.bfloat16), w_ref[0, :, -channels:]))
+        gate_ref[0, pl.ds(at, rows)] = gate.reshape(rows, cols, channels)
     mask = row_alive[at : at + rows, None, :] * col_alive[None, :, :]
     norm_ref[pl.ds(at, rows)] = (normed.reshape(rows, cols, channels) * mask).astype(jnp.bfloat16)
 
@@ -525,7 +526,7 @@
     group = hidden // cols
     for at in range(0, rows, group):
         values = pair_ref[0, pl.ds(at, group)].reshape(group * cols, channels)
-        norm_and_gate(values, row_alive, col_alive, w_ref, at, norm_ref, gate_ref)
+        norm_and_gate(values, row_alive, col_alive, at, norm_ref, w_ref, gate_ref)
     open_layer(0, norm_ref[...], operand_refs[:chunks], operand_refs[chunks:], wide, laid, turned, swap)
 
 
@@ -586,7 +587,68 @@
     )(ids, blocks, pair, chains, w_in, wide, *more)
 
 
-def plan_kernel(n_blk, slots_dev, terms, capacity, ids, owners, slots, chosen, place, seen):
+def far_kernel(layer, n_blk, far, n_chan, n_sub, of, bases, ids, blocks, mine, *rest):
+    sources, (chain_ref, wide, left_ref, right_ref, norm_ref, laid, turned, swap) = rest[:-8], rest[-8:]
+    step = pl.program_id(0)
+    rows, cols, channels = norm_ref.shape
+    holder = lax.rem(ids[0] - far + n_blk, n_blk)
+
+    @pl.when(step == 0)
+    def _():
+        swap[...] = swap_matrix(16)
+
+    group = channels // cols
+    for side, out_ref in ((0, left_ref), (1, right_ref)):
+        slot = mine[2 * step + side]
+        refs = sources[side * len(bases) : (side + 1) * len(bases)]
+        block = holder * of + slot
+        row_alive = alive_rows(chain_ref, (blocks[0, block] * n_chan + ids[1]) * rows, rows)
+        col_alive = alive_rows(chain_ref, (blocks[1, block] * n_sub + ids[2]) * cols, cols)
+        for at in range(0, rows, group):
+            values = refs[0][0, pl.ds(at, group)]
+            for base, ref in zip(bases[1:], refs[1:]):
+                values = jnp.where(slot >= base, ref[0, pl.ds(at, group)], values)
+            norm_and_gate(values.reshape(group * cols, channels), row_alive, col_alive, at, norm_ref)
+        if side == layer % 2:
+            make_operand(side, norm_ref[...], wide, [out_ref], laid, swap)
+        else:
+            turn(norm_ref[...], turned, swap)
+            make_operand(side, turned[...], wide, [out_ref], laid, swap)
+
+
+def far_operands(layer, ids, blocks, mine, sources, chains, wide, far, capacity, of, hidden):
+    n_blk = lax.axis_size("blk")
+    _, rows, cols, channels = sources[0].shape
+    bases = [sum(a.shape[0] for a in sources[:n]) for n in range(len(sources))]
+
+    def source_spec(side, base, size):
+        def place(t, ids, blocks, mine):
+            return jnp.clip(mine[2 * t + side] - base, 0, size - 1), 0, 0, 0
+
+        return pl.BlockSpec((1, rows, cols, channels), place)
+
+    in_specs = [source_spec(side, b, a.shape[0]) for side in range(2) for b, a in zip(bases, sources)]
+    in_specs += [pl.BlockSpec(chains.shape, lambda t, *_: (0, 0)), pl.BlockSpec(wide.shape, lambda t, *_: (0, 0))]
+    shape = (capacity, hidden // (hidden // cols), rows, hidden)
+    return pl.pallas_call(
+        functools.partial(
+            far_kernel, layer, n_blk, far, lax.axis_size("chan"), lax.axis_size("sub"), of, tuple(bases)
+        ),
+        grid_spec=pltpu.PrefetchScalarGridSpec(
+            num_scalar_prefetch=3,
+            grid=(capacity,),
+            in_specs=in_specs,
+            out_specs=[pl.BlockSpec((1,) + shape[1:], lambda t, *_: (t, 0, 0, 0))] * 2,
+            scratch_shapes=[pltpu.VMEM((rows, cols, channels), jnp.bfloat16)] + operand_scratch(rows, cols, hidden),
+        ),
+        out_shape=[jax.ShapeDtypeStruct(shape, jnp.bfloat16)] * 2,
+        compiler_params=pltpu.CompilerParams(vmem_limit_bytes=20 * mebi),
+        cost_estimate=pl.CostEstimate(flops=1 << 33, bytes_accessed=1 << 20, transcendentals=0),
+        name="far_operands",
+    )(ids, blocks, mine, *sources, *sources, chains, wide)
+
+
+def plan_kernel(n_blk, far, slots_dev, terms, capacity, ids, owners, slots, chosen, place, mine, seen):
     for shift in range(n_blk):
         seen[shift] = 0
         target = lax.rem(ids[0] + shift, n_blk)
@@ -604,17 +666,27 @@
         count = seen[owner]
         seen[owner] = count + 1
         place[e] = lax.rem(ids[0] - owner + n_blk, n_blk) * capacity + count
-
-
-def make_plan(ids, owners, slots, n_blk, slots_dev, terms, capacity):
+    for e in range(2 * (capacity + 1)):
+        mine[e] = 0
+    found = jnp.int32(0)
+    for e in range(slots_dev * terms):
+        block, term = ids[0] * slots_dev + e // terms, e % terms
+        at = 2 * jnp.minimum(found, capacity)
+        mine[at] = slots[term, 0, block]
+        mine[at + 1] = slots[term, 1, block]
+        found = found + (owners[term, block] == lax.rem(ids[0] - far + n_blk, n_blk)).astype(jnp.int32)
+
+
+def make_plan(ids, owners, slots, n_blk, far, slots_dev, terms, capacity):
     scalars = pl.BlockSpec(memory_space=pltpu.SMEM)
     return pl.pallas_call(
-        functools.partial(plan_kernel, n_blk, slots_dev, terms, capacity),
+        functools.partial(plan_kernel, n_blk, far, slots_dev, terms, capacity),
         in_specs=[scalars] * 3,
-        out_specs=[scalars] * 2,
+        out_specs=[scalars] * 3,
         out_shape=[
             jax.ShapeDtypeStruct((2 * n_blk * (capacity + 1),), jnp.int32),
             jax.ShapeDtypeStruct((slots_dev * terms,), jnp.int32),
+            jax.ShapeDtypeStruct((2 * (capacity + 1),), jnp.int32),
         ],
         scratch_shapes=[pltpu.SMEM((n_blk,), jnp.int32)],
         compiler_params=pltpu.CompilerParams(vmem_limit_bytes=mebi),
@@ -720,16 +792,16 @@
     )(ids, chosen, *refs)
 
 
-def close_kernel(layer, last, n_parts, n_blk, n_chan, n_sub, base, of, terms, capacity, ids, blocks, place, *rest):
-    chunks = n_parts // n_blk
+def close_kernel(layer, last, spots, chunks, n_chan, n_sub, base, of, terms, capacity, ids, blocks, place, *rest):
+    n_parts = len(spots)
     arrived, rest = rest[:n_parts], rest[n_parts:]
     cur_ref, gate_ref, w_out_ref = rest[:3]
     if last:
         out_ref, held, wide_out, sems, swap = rest[3:]
     else:
         chain_ref, w_ref, wide = rest[3:6]
-        out_ref, next_gate_ref, *operand_refs, held, wide_out, sems, norm_ref, laid, turned, swap = rest[
-            -(2 * chunks + 9) :
+        out_ref, next_gate_ref, sent_ref, *operand_refs, held, wide_out, sems, norm_ref, laid, turned, swap = rest[
+            -(2 * chunks + 10) :
         ]
         left_refs, right_refs = operand_refs[:chunks], operand_refs[chunks:]
     step = pl.program_id(0)
@@ -738,9 +810,8 @@
     parts, size = hidden // bands, bands
 
     def arrival(n):
-        at = sum(arrived[m * n_blk].shape[1] for m in range(n // n_blk))
-        count = arrived[n].shape[1]
-        target = held.at[pl.ds(n % n_blk * capacity, capacity), pl.ds(at, count)]
+        shift, at = spots[n]
+        target = held.at[pl.ds(shift * capacity, capacity), pl.ds(at, arrived[n].shape[1])]
         return pltpu.make_async_copy(arrived[n], target, sems.at[n])
 
     @pl.when(step == 0)
@@ -800,7 +871,8 @@
         result = (current + gate * change).astype(jnp.bfloat16)
         out_ref[0, taken] = result.reshape(parts, cols, channels)
         if not last:
-            norm_and_gate(result, row_alive, col_alive, w_ref, g * parts, norm_ref, next_gate_ref)
+            sent_ref[0, taken] = result.reshape(parts, cols, channels)
+            norm_and_gate(result, row_alive, col_alive, g * parts, norm_ref, w_ref, next_gate_ref)
     if not last:
         open_layer(layer + 1, norm_ref[...], left_refs, right_refs, wide, laid, turned, swap)
 
@@ -808,8 +880,8 @@
 def close_layer(
     layer, arrived, ids, blocks, place, current, gate, w_out, capacity, terms, chains, w_in, wide, last, bands, base, count, earlier
 ):
-    n_blk = len(arrived[0])
-    flat = [part for chunk in arrived for part in chunk]
+    flat, spots = [part for part, *_ in arrived], tuple((shift, at) for _, shift, at in arrived)
+    n_blk = lax.axis_size("blk")
     slots, rows, cols, channels = current.shape
     hidden = w_out.shape[1]
 
@@ -830,6 +902,7 @@
         in_specs += [pl.BlockSpec(chains.shape, lambda s, *_: (0, 0)), layer_spec(w_in, layer + 1)]
         in_specs += [pl.BlockSpec(wide.shape, lambda s, *_: (0, 0))]
         out_shape += [jax.ShapeDtypeStruct(current.shape, jnp.float32)]
+        out_shape += [jax.ShapeDtypeStruct((count,) + current.shape[1:], jnp.bfloat16)]
         out_shape += operand_outputs(slots, count, cols, hidden, bands[layer + 1])
         scratch += [pltpu.VMEM((rows, cols, channels), jnp.bfloat16)] + operand_scratch(cols, rows, hidden)
     else:
@@ -838,7 +911,8 @@
     return pl.pallas_call(
         functools.partial(
             close_kernel,
-            *(layer, last, len(flat), n_blk, lax.axis_size("chan"), lax.axis_size("sub"), base, slots, terms, capacity),
+            *(layer, last, spots, 0 if last else len(bands[layer + 1]), lax.axis_size("chan"), lax.axis_size("sub")),
+            *(base, slots, terms, capacity),
         ),
         grid_spec=pltpu.PrefetchScalarGridSpec(
             num_scalar_prefetch=3,
@@ -871,7 +945,7 @@
     both = ("chan", "sub")
     one = lax.ppermute(left, both, [(1, 3), (2, 0), (0, 1), (3, 2)])
     other = lax.ppermute(right, "chan", [(0, 1), (1, 0)])
-    two = lax.ppermute(after(one, over), both, [(0, 1), (3, 2)])
+    two = lax.ppermute(one if over is None else after(one, over), both, [(0, 1), (3, 2)])
     return [(left, one), (one, two)], [(right, right), (other, other)]
 
 
@@ -879,23 +953,35 @@
     slots, rows, cols, channels = pair.shape
     hidden = w_out.shape[1]
     far = n_blk // 2
-    shifts = [far] + [s for s in range(1, n_blk) if s != far] + [0]
+    near = [s for s in range(1, n_blk) if s != far] + [0]
     layers = w_in.shape[0]
     current = pair
-    bands = [[8, 24], [12, 20]]
-    chosen, place = make_plan(ids, owners, slot_of, n_blk, slots, terms, capacity)
+    bands = [[14, 18], [14, 18]]
+    chosen, place, mine = make_plan(ids, owners, slot_of, n_blk, far, slots, terms, capacity)
+    in_order = jnp.repeat(jnp.arange(capacity, dtype=jnp.int32), 2)
     half = slots // 2
     halves = [(0, half), (half, slots - half)]
+
+    def over_blk(value, shift):
+        return lax.ppermute(value, "blk", [(p, (p + shift) % n_blk) for p in range(n_blk)])
+
     for layer in range(layers):
         count = len(bands[layer])
         if layer == 0:
+            raw = [over_blk(pair, far)]
             calls, wide = [None], spread_weights(w_in, 0, cols)
             for base, size in halves:
-                calls.append(open_operands(ids, blocks, pair, chains, w_in, wide, hidden, bands[0], base, size, calls[-1]))
+                calls.append(
+                    open_operands(ids, blocks, pair, chains, w_in, wide, hidden, bands[0], base, size, calls[-1])
+                )
             gate = calls[-1][0]
+        else:
+            raw = []
+            for call in calls[1:]:
+                raw.append(over_blk(after(call[2], *raw) if raw else call[2], far))
         operands = [call[-2 * count :] for call in calls[1:]]
         exchange = exchange_bands_incoming if layer % 2 else exchange_bands_outgoing
-        arrived = []
+        arrived, by_shift = [], {}
         for chunk in range(count):
             if chunk == 0:
                 exchanged = []
@@ -918,16 +1004,23 @@
                     ((other, _), _), ((one, _), (_, two)) = exchanged[-1]
                     left = after(left, other)
                     right = after(right, one, two, chosen)
-                exchanged = [exchange(left, right, arrived[-1][far])]
-            made = banded_products(shifts, ids, chosen, exchanged, capacity, cols)
-            parts = [None] * n_blk
-            for shift, part in zip(shifts, made):
+                exchanged = [exchange(left, right, by_shift[near[0]])]
+                ids = after(ids, *by_shift.values())
+            made = banded_products(near, ids, chosen, exchanged, capacity, cols)
+            start = sum(bands[layer][:chunk])
+            for shift, part in zip(near, made):
                 if shift:
-                    if arrived:
-                        part = after(part, arrived[-1][shift])
-                    part = lax.ppermute(part, "blk", [(p, (p + shift) % n_blk) for p in range(n_blk)])
-                parts[shift] = part
-            arrived.append(parts)
+                    part = over_blk(after(part, by_shift.get(shift, raw[-1])), shift)
+                    by_shift[shift] = part
+                arrived.append((part, shift, start))
+            if chunk == 0:
+                sources = list(lax.optimization_barrier((*raw, made[-1]))[:-1])
+                far_left, far_right = far_operands(
+                    layer, ids, blocks, mine, sources, chains, wide, far, capacity, slots, hidden
+                )
+        far_exchanged = [exchange(far_left, far_right, made[-1])]
+        (part,) = banded_products([0], ids, in_order, far_exchanged, capacity, cols)
+        arrived.append((part, far, 0))
         last = layer == layers - 1
         calls = [None]
         if not last:
@@ -962,7 +1055,7 @@
     owners = term_owner.T
     slot_of = jnp.transpose(term_slots, (1, 2, 0))
     chains = chain_ids.reshape(-1, 128)
-    if fast and rows == cols == 32 and channels == hidden == 128:
+    if fast and n_blk > 1 and rows == cols == 32 and channels == hidden == 128:
         return banded(pair, ids, blocks, owners, slot_of, chains, w_in, w_out, capacity, terms, n_blk)
     shifts = [n_blk // 2] + [s for s in range(1, n_blk) if s != n_blk // 2] + [0]
 

time: 312 us -> 355 us (1.14)
  Pallas kernels: 73.2 us -> 104 us
  starting transfers between devices: 44.5 us -> 59.6 us
  local copies, waits for them, and re-layouts: 1.95 us -> 8.14 us
  waiting for transfers between devices: 188 us -> 182 us
    pallas_call x4 -> x6, Pallas kernels: 35 us -> 58.9 us  [the longest x3 37.8 us: close_layer(): pl.pallas_call(functools.partial(close_kernel, *(layer, last, spots, 0 if...]
    ppermute x3 -> x4, waiting for transfers between devices: 29.8 us -> 16.2 us  [exchange_bands_outgoing(): one = lax.ppermute(right, both, [(0, 2), (3, 1), (1, 0), (2, 3)])]
    ppermute x15, waiting for transfers between devices: 132 us -> 145 us  [the longest x11 144 us: over_blk(): lax.ppermute(value, 'blk', [(p, (p + shift) % n_blk) for p in range(n_blk)])]
    ppermute x3 -> x4, waiting for transfers between devices: 17.3 us -> 7.43 us  [exchange_bands_incoming(): other = lax.ppermute(right, 'chan', [(0, 1), (1, 0)])]
    pallas_call x4 -> x6, Pallas kernels: 20.4 us -> 26.9 us  [banded_products(): pl.pallas_call(functools.partial(banded_kernel, shifts, capacity, tuple(p...]
    ppermute x15, starting transfers between devices: 26.2 us -> 32.7 us  [the longest x11 18.2 us: over_blk(): lax.ppermute(value, 'blk', [(p, (p + shift) % n_blk) for p in range(n_blk)])]
    unnamed x16 -> x40, local copies, waits for them, and re-layouts: 1.95 us -> 8.05 us
    ppermute x3 -> x4, waiting for transfers between devices: 8.37 us -> 13.6 us  [exchange_bands_incoming(): one = lax.ppermute(left, both, [(1, 3), (2, 0), (0, 1), (3, 2)])]
  transfers between devices with their start and end apart: 30 -> 35, of which waited for: 14 -> 17; matrix products, arithmetic and copies ran while one was open for 0% -> 0% of each run, Pallas kernels for 14% -> 23%
where the time goes in v11:
time: 355 us; the launch traced here: 354 us
  waiting for transfers between devices  182 us (51%)
  Pallas kernels  104 us (29%)
  starting transfers between devices  59.6 us (17%)
  local copies, waits for them, and re-layouts  8.14 us (2%)
    ppermute x11, waiting for transfers between devices, over_blk(): lax.ppermute(value, 'blk', [(p, (p + shift) % n_blk) for p in range(n_blk)])  144 us
    pallas_call x3, Pallas kernels, close_layer(): pl.pallas_call(functools.partial(close_kernel, *(layer, last, spots, 0 if...  37.8 us
    pallas_call x6, Pallas kernels, banded_products(): pl.pallas_call(functools.partial(banded_kernel, shifts, capacity, tuple(p...  26.9 us
    pallas_call x2, Pallas kernels, far_operands(): pl.pallas_call(functools.partial(far_kernel, layer, n_blk, far, lax.axis_...  19.5 us
    ppermute x11, starting transfers between devices, over_blk(): lax.ppermute(value, 'blk', [(p, (p + shift) % n_blk) for p in range(n_blk)])  18.2 us
    pallas_call x2, Pallas kernels, open_operands(): pl.pallas_call(functools.partial(open_kernel, hidden, len(bands), lax.axi...  16.7 us
    ppermute x4, waiting for transfers between devices, exchange_bands_outgoing(): one = lax.ppermute(right, both, [(0, 2), (3, 1), (1, 0), (2, 3)])  16.2 us
    ppermute x4, starting transfers between devices, exchange_bands_incoming(): lax.ppermute(one if over is None else after(one, over), both, [(0, 1), (3...  14.4 us
  transfers between devices with their start and end apart: 35, of which 17 were waited for; matrix products, arithmetic and copies ran while one was open for 0% of the time, Pallas kernels for 23%

profile of v11, /device:TPU:11, one launch (start us, length us, event | category | flops | bytes accessed | tf_op | source)
XLA Modules:
  0.0 354.5 jit_solution(16803340449533219141)
XLA Ops:
  4.9 8.4 %open_operands.2 = (f32[8,32,32,128]{3,2,1,0:T(8,128)S(1)}, bf16[4,14,32,128]{3,2,1,0:T(8,128)(2,1)S(1)}, bf16[8,18,32,128]{3,2,1,0:T(8,128)(2,1)S(1)}, bf16[4,1...) custom-call(s32[4]{0:T(128)S(1)} %pad_add_fusion.ids, s32[2,32]{1,0:T(2,128)S(1)} %bitcast.16, ...), custom_call_target="tpu_custom_call" | custom-call | flops 8589934592 | bytes 1048576 | tf_op jit(solution)/shard_map/open_operands/pallas_call | solution.py:567
  14.0 3.5 collective-permute-start.1
  17.5 8.3 %open_operands.3 = (f32[8,32,32,128]{3,2,1,0:T(8,128)S(1)}, bf16[4,14,32,128]{3,2,1,0:T(8,128)(2,1)S(1)}, bf16[8,18,32,128]{3,2,1,0:T(8,128)(2,1)S(1)}, bf16[4,1...) custom-call(s32[4]{0:T(128)S(1)} %pad_add_fusion.ids, ...), custom_call_target="tpu_custom_call", output_to_operand_aliasing={{0}: (6, {}), {2}: (7, {}), {4}: (8, {})} | custom-call | flops 8589934592 | bytes 1048576 | tf_op jit(solution)/shard_map/open_operands/pallas_call | solution.py:567
  27.3 4.9 %collective-permute-start.4 = (bf16[4,14,32,128]{3,2,1,0:T(8,128)(2,1)S(1)}, bf16[4,14,32,128]{3,2,1,0:T(8,128)(2,1)S(1)}, u32[]{:S(2)}, u32[]{:S(2)}) collective-permute-start(bf16[4,14,32,128]{3,2,1,0:T(8,128)(2,1)S(1)} %get-tuple-element.85.rest_8_), channel_id=1, source_target_pairs={{0,2},{3,1},{1,0},{2,3},{4,6},{7,5},{5,4},{6,7},{8,10},{11,9},{9,8... | collective-permute-start | bytes 1376264 | tf_op jit(solution)/shard_map/ppermute | solution.py:939
  33.9 7.7 %collective-permute-done.4.rest_7_ = bf16[4,14,32,128]{3,2,1,0:T(8,128)(2,1)S(1)} collective-permute-done((bf16[4,14,32,128]{3,2,1,0:T(8,128)(2,1)S(1)}, bf16[4,14,32,128]{3,2,1,0:T(8,128)(2,1)S(1)}, u32[]{:S(2)}, u32[]{:S(2)}) %collective-permute-start.4) | collective-permute-done | bytes 458784 | tf_op jit(solution)/shard_map/ppermute | solution.py:939
  42.4 4.5 %collective-permute-start.10 = (bf16[8,18,32,128]{3,2,1,0:T(8,128)(2,1)S(1)}, bf16[8,18,32,128]{3,2,1,0:T(8,128)(2,1)S(1)}, u32[]{:S(2)}, u32[]{:S(2)}) collective-permute-start(bf16[8,18,32,128]{3,2,1,0:T(8,128)(2,1)S(1)} %get-tuple-element.96.rest_3_), channel_id=1, source_target_pairs={{0,2},{3,1},{1,0},{2,3},{4,6},{7,5},{5,4},{6,7},{8,10},{11,9},{9,8... | collective-permute-start | bytes 3538952 | tf_op jit(solution)/shard_map/ppermute | solution.py:939
  46.9 6.0 %banded_products.6 = (bf16[4,14,32,128]{3,2,1,0:T(8,128)(2,1)S(1)}, bf16[4,14,32,128]{3,2,1,0:T(8,128)(2,1)S(1)}, bf16[4,14,32,128]{3,2,1,0:T(8,128)(2,1)S(1)}) custom-call(s32[4]{0:T(128)S(1)} %pad_add_fusion.ids, s32[40]{0:T(128)S(1)} %get-tuple-element.76.chosen, bf16[4,14,32,128]{3,2,1,0:T(8,128)(2,1)S(1)} %collective-permute-done.rest_0_, ...), custom_call_target="tpu_custom_call" | custom-call | flops 352321536 | bytes 1 | tf_op jit(solution)/shard_map/banded_products/pallas_call | solution.py:771
  53.7 39.1 %collective-permute-done.6.rest_0_.rest_1_ = bf16[8,32,32,128]{3,2,1,0:T(8,128)(2,1)S(1)} collective-permute-done((bf16[8,32,32,128]{3,2,1,0:T(8,128)(2,1)}, bf16[8,32,32,128]{3,2,1,0:T(8,128)(2,1)S(1)}, u32[]{:S(2)}, u32[]{:S(2)}) %collective-permute-start.6) | collective-permute-done | bytes 2097184 | tf_op jit(solution)/shard_map/ppermute | solution.py:966
  97.2 9.8 %far_operands.2 = (bf16[4,32,32,128]{3,2,1,0:T(8,128)(2,1)S(1)}, bf16[4,32,32,128]{3,2,1,0:T(8,128)(2,1)S(1)}) custom-call(s32[4]{0:T(128)S(1)} %pad_add_fusion.ids, s32[2,32]{1,0:T(2,128)S(1)} %bitcast.18, s32[10]{0:T(128)S(1)} %get-tuple-element.102.mine, bf16[8,32,32,128]{3,2,1,0:T(8,128)(2,1)S(1)} %copy-done.5, bf16[8,32,32,128]{3,2,1,0:T(8,128)(2,1)S(1)} %copy-done.5, ...), custom_call_target="tpu_custom_call" | custom-call | flops 8589934592 | bytes 1048576 | tf_op jit(solution)/shard_map/far_operands/pallas_call | solution.py:633
  110.6 7.8 %collective-permute-done.7.rest_0_ = bf16[4,14,32,128]{3,2,1,0:T(8,128)(2,1)S(1)} collective-permute-done((bf16[4,14,32,128]{3,2,1,0:T(8,128)(2,1)S(1)}, bf16[4,14,32,128]{3,2,1,0:T(8,128)(2,1)S(1)}, u32[]{:S(2)}, u32[]{:S(2)}) %collective-permute-start.7) | collective-permute-done | bytes 458784 | tf_op jit(solution)/shard_map/ppermute | solution.py:966
  119.4 4.4 %banded_products.7 = (bf16[4,18,32,128]{3,2,1,0:T(8,128)(2,1)}, bf16[4,18,32,128]{3,2,1,0:T(8,128)(2,1)}, bf16[4,18,32,128]{3,2,1,0:T(8,128)(2,1)S(1)}) custom-call(s32[4]{0:T(128)S(1)} %pad_add_fusion.ids, s32[40]{0:T(128)S(1)} %get-tuple-element.76.chosen, bf16[8,18,32,128]{3,2,1,0:T(8,128)(2,1)S(1)} %collective-permute-done.9.rest_0_, ...), custom_call_target="tpu_custom_call" | custom-call | flops 452984832 | bytes 1 | tf_op jit(solution)/shard_map/banded_products/pallas_call | solution.py:771
  126.8 7.8 %collective-permute-done.15.rest_2_ = bf16[4,32,32,128]{3,2,1,0:T(8,128)(2,1)} collective-permute-done((bf16[4,32,32,128]{3,2,1,0:T(8,128)(2,1)S(1)}, bf16[4,32,32,128]{3,2,1,0:T(8,128)(2,1)}, u32[]{:S(2)}, u32[]{:S(2)}) %collective-permute-start.15) | collective-permute-done | bytes 1048608 | tf_op jit(solution)/shard_map/ppermute | solution.py:939
  134.6 3.4 banded_products.8.rest_6_
  139.6 12.2 %collective-permute-done.12.rest_3_ = bf16[4,18,32,128]{3,2,1,0:T(8,128)(2,1)} collective-permute-done((bf16[4,18,32,128]{3,2,1,0:T(8,128)(2,1)}, bf16[4,18,32,128]{3,2,1,0:T(8,128)(2,1)}, u32[]{:S(2)}, u32[]{:S(2)}) %collective-permute-start.12) | collective-permute-done | bytes 589856 | tf_op jit(solution)/shard_map/ppermute | solution.py:966
  151.8 14.4 %close_layer.3 = (bf16[8,32,32,128]{3,2,1,0:T(8,128)(2,1)S(1)}, f32[8,32,32,128]{3,2,1,0:T(8,128)S(1)}, bf16[4,32,32,128]{3,2,1,0:T(8,128)(2,1)S(1)}, bf16[4,14,...) custom-call(s32[4]{0:T(128)S(1)} %pad_add_fusion.ids, ...), custom_call_target="tpu_custom_call" | custom-call | flops 8589934592 | bytes 1048576 | tf_op jit(solution)/shard_map/close_layer/pallas_call | solution.py:911
  169.1 14.4 %close_layer.4 = (bf16[8,32,32,128]{3,2,1,0:T(8,128)(2,1)S(1)}, f32[8,32,32,128]{3,2,1,0:T(8,128)S(1)}, bf16[4,32,32,128]{3,2,1,0:T(8,128)(2,1)S(1)}, bf16[4,14,...) custom-call(s32[4]{0:T(128)S(1)} %pad_add_fusion.ids, ...), custom_call_target="tpu_custom_call", output_to_operand_aliasing={{0}: (16, {}), {1}: (17, {}), {4}: (18, {}), {6}: (19, {})} | custom-call | flops 8589934592 | bytes 1048576 | tf_op jit(solution)/shard_map/close_layer/pallas_call | solution.py:911
  183.5 3.9 %collective-permute-start.18 = (bf16[4,14,32,128]{3,2,1,0:T(8,128)(2,1)S(1)}, bf16[4,14,32,128]{3,2,1,0:T(8,128)(2,1)S(1)}, u32[]{:S(2)}, u32[]{:S(2)}) collective-permute-start(bf16[4,14,32,128]{3,2,1,0:T(8,128)(2,1)S(1)} %collective-permute-done.17.rest_1_), channel_id=1, source_target_pairs={{0,1},{3,2},{4,5},{7,6},{8,9},{11,10},{12,13},{15,14},{16,17},{19,... | collective-permute-start | bytes 1376264 | tf_op jit(solution)/shard_map/ppermute | solution.py:948
  189.7 8.0 %collective-permute-done.20.rest_6_ = bf16[4,14,32,128]{3,2,1,0:T(8,128)(2,1)S(1)} collective-permute-done((bf16[4,14,32,128]{3,2,1,0:T(8,128)(2,1)S(1)}, bf16[4,14,32,128]{3,2,1,0:T(8,128)(2,1)S(1)}, u32[]{:S(2)}, u32[]{:S(2)}) %collective-permute-start.20) | collective-permute-done | bytes 458784 | tf_op jit(solution)/shard_map/ppermute | solution.py:946
  200.9 11.7 %collective-permute-done.23.rest_0_.rest_2_ = bf16[4,32,32,128]{3,2,1,0:T(8,128)(2,1)S(1)} collective-permute-done((bf16[4,32,32,128]{3,2,1,0:T(8,128)(2,1)S(1)}, bf16[4,32,32,128]{3,2,1,0:T(8,128)(2,1)S(1)}, u32[]{:S(2)}, u32[]{:S(2)}) %collective-permute-start.23) | collective-permute-done | bytes 1048608 | tf_op jit(solution)/shard_map/ppermute | solution.py:966
  218.3 6.0 %banded_products.9 = (bf16[4,14,32,128]{3,2,1,0:T(8,128)(2,1)S(1)}, bf16[4,14,32,128]{3,2,1,0:T(8,128)(2,1)S(1)}, bf16[4,14,32,128]{3,2,1,0:T(8,128)(2,1)S(1)}) custom-call(s32[4]{0:T(128)S(1)} %pad_add_fusion.ids, s32[40]{0:T(128)S(1)} %get-tuple-element.76.chosen, bf16[4,14,32,128]{3,2,1,0:T(8,128)(2,1)S(1)} %get-tuple-element.108.rest_0_, ...), custom_call_target="tpu_custom_call" | custom-call | flops 352321536 | bytes 1 | tf_op jit(solution)/shard_map/banded_products/pallas_call | solution.py:771
  224.3 35.7 %collective-permute-done.24.rest_1_.rest_3_ = bf16[4,32,32,128]{3,2,1,0:T(8,128)(2,1)S(1)} collective-permute-done((bf16[4,32,32,128]{3,2,1,0:T(8,128)(2,1)S(1)}, bf16[4,32,32,128]{3,2,1,0:T(8,128)(2,1)S(1)}, u32[]{:S(2)}, u32[]{:S(2)}) %collective-permute-start.24) | collective-permute-done | bytes 1048608 | tf_op jit(solution)/shard_map/ppermute | solution.py:966
  263.4 10.0 %collective-permute-done.25.rest_0_ = bf16[4,14,32,128]{3,2,1,0:T(8,128)(2,1)S(1)} collective-permute-done((bf16[4,14,32,128]{3,2,1,0:T(8,128)(2,1)S(1)}, bf16[4,14,32,128]{3,2,1,0:T(8,128)(2,1)S(1)}, u32[]{:S(2)}, u32[]{:S(2)}) %collective-permute-start.25) | collective-permute-done | bytes 458784 | tf_op jit(solution)/shard_map/ppermute | solution.py:966
  276.4 9.7 %far_operands.3 = (bf16[4,32,32,128]{3,2,1,0:T(8,128)(2,1)S(1)}, bf16[4,32,32,128]{3,2,1,0:T(8,128)(2,1)S(1)}) custom-call(s32[4]{0:T(128)S(1)} %pad_add_fusion.ids, s32[2,32]{1,0:T(2,128)S(1)} %bitcast.21, s32[10]{0:T(128)S(1)} %get-tuple-element.102.mine, bf16[4,32,32,128]{3,2,1,0:T(8,128)(2,1)S(1)} %collective-permute-done.23.rest_0_.rest_2_, ...), custom_call_target="tpu_custom_call" | custom-call | flops 8589934592 | bytes 1048576 | tf_op jit(solution)/shard_map/far_operands/pallas_call | solution.py:633
  286.1 3.3 collective-permute-start.26
  290.8 6.4 %collective-permute-done.26.rest_1_ = bf16[4,14,32,128]{3,2,1,0:T(8,128)(2,1)S(1)} collective-permute-done((bf16[4,14,32,128]{3,2,1,0:T(8,128)(2,1)S(1)}, bf16[4,14,32,128]{3,2,1,0:T(8,128)(2,1)S(1)}, u32[]{:S(2)}, u32[]{:S(2)}) %collective-permute-start.26) | collective-permute-done | bytes 458784 | tf_op jit(solution)/shard_map/ppermute | solution.py:966
  297.2 4.7 %banded_products.10 = (bf16[4,18,32,128]{3,2,1,0:T(8,128)(2,1)S(1)}, bf16[4,18,32,128]{3,2,1,0:T(8,128)(2,1)S(1)}, bf16[4,18,32,128]{3,2,1,0:T(8,128)(2,1)S(1)}) custom-call(s32[4]{0:T(128)S(1)} %pad_add_fusion.ids, s32[40]{0:T(128)S(1)} %get-tuple-element.76.chosen, bf16[8,18,32,128]{3,2,1,0:T(8,128)(2,1)S(1)} %get-tuple-element.132.rest_0_, ...), custom_call_target="tpu_custom_call" | custom-call | flops 452984832 | bytes 1 | tf_op jit(solution)/shard_map/banded_products/pallas_call | solution.py:771
  301.9 5.6 %collective-permute-done.32.rest_1_ = bf16[4,32,32,128]{3,2,1,0:T(8,128)(2,1)S(1)} collective-permute-done((bf16[4,32,32,128]{3,2,1,0:T(8,128)(2,1)S(1)}, bf16[4,32,32,128]{3,2,1,0:T(8,128)(2,1)S(1)}, u32[]{:S(2)}, u32[]{:S(2)}) %collective-permute-start.32) | collective-permute-done | bytes 1048608 | tf_op jit(solution)/shard_map/ppermute | solution.py:946
  307.5 4.4 %collective-permute-start.33 = (bf16[4,32,32,128]{3,2,1,0:T(8,128)(2,1)S(1)}, bf16[4,32,32,128]{3,2,1,0:T(8,128)(2,1)S(1)}, u32[]{:S(2)}, u32[]{:S(2)}) collective-permute-start(bf16[4,32,32,128]{3,2,1,0:T(8,128)(2,1)S(1)} %collective-permute-done.32.rest_1_), channel_id=1, source_target_pairs={{0,1},{3,2},{4,5},{7,6},{8,9},{11,10},{12,13},{15,14},{16,17},{19,... | collective-permute-start | bytes 3145736 | tf_op jit(solution)/shard_map/ppermute | solution.py:948
  311.9 4.3 %collective-permute-start.31 = (bf16[4,18,32,128]{3,2,1,0:T(8,128)(2,1)S(1)}, bf16[4,18,32,128]{3,2,1,0:T(8,128)(2,1)S(1)}, u32[]{:S(2)}, u32[]{:S(2)}) collective-permute-start(bf16[4,18,32,128]{3,2,1,0:T(8,128)(2,1)S(1)} %get-tuple-element.138), channel_id=1, source_target_pairs={{0,12},{4,0},{8,4},{12,8},{1,13},{5,1},{9,5},{13,9},{2,14},{6,2},{... | collective-permute-start | bytes 1769480 | tf_op jit(solution)/shard_map/ppermute | solution.py:966
  316.2 7.4 %collective-permute-done.34.rest_4_ = bf16[4,32,32,128]{3,2,1,0:T(8,128)(2,1)S(1)} collective-permute-done((bf16[4,32,32,128]{3,2,1,0:T(8,128)(2,1)S(1)}, bf16[4,32,32,128]{3,2,1,0:T(8,128)(2,1)S(1)}, u32[]{:S(2)}, u32[]{:S(2)}) %collective-permute-start.34) | collective-permute-done | bytes 1048608 | tf_op jit(solution)/shard_map/ppermute | solution.py:947
  329.3 16.1 %collective-permute-done.30.rest_3_ = bf16[4,18,32,128]{3,2,1,0:T(8,128)(2,1)S(1)} collective-permute-done((bf16[4,18,32,128]{3,2,1,0:T(8,128)(2,1)S(1)}, bf16[4,18,32,128]{3,2,1,0:T(8,128)(2,1)S(1)}, u32[]{:S(2)}, u32[]{:S(2)}) %collective-permute-start.30) | collective-permute-done | bytes 589856 | tf_op jit(solution)/shard_map/ppermute | solution.py:966
  345.4 8.9 %close_layer.5 = bf16[8,32,32,128]{3,2,1,0:T(8,128)(2,1)} custom-call(s32[4]{0:T(128)S(1)} %pad_add_fusion.ids, s32[2,32]{1,0:T(2,128)S(1)} %bitcast.22, s32[16]{0:T(128)S(1)} %get-tuple-element.91.place, bf16[4,14,32,128]{3,2,1,0:T(8,128)(2,1)S(1)} %collective-permute-done.25.rest_0_, bf16[4,14,32,128]{3,2,1,0:T(8,128)(2,1)S(1)} %collective-permute-done.26.rest_1_, ...), custom_call_target="tpu_custom_call" | custom-call | flops 8589934592 | bytes 1048576 | tf_op jit(solution)/shard_map/close_layer/pallas_call | solution.py:911
  (97 shorter events, 51.1 us)
Async XLA Ops:
  0.0 92.8 %collective-permute-start.6 = (bf16[8,32,32,128]{3,2,1,0:T(8,128)(2,1)}, bf16[8,32,32,128]{3,2,1,0:T(8,128)(2,1)S(1)}, u32[]{:S(2)}, u32[]{:S(2)}) collective-permute-start(bf16[8,32,32,128]{3,2,1,0:T(8,128)(2,1)} %rest_7_.3), channel_id=1, source_target_pairs={{0,8},{4,12},{8,0},{12,4},{1,9},{5,13},{9,1},{13,5},{2,10},{6,14},... | collective-permute-start | bytes 6291464 | tf_op jit(solution)/shard_map/ppermute | solution.py:966
  13.3 12.6 %collective-permute-start.2 = (bf16[4,14,32,128]{3,2,1,0:T(8,128)(2,1)S(1)}, bf16[4,14,32,128]{3,2,1,0:T(8,128)(2,1)S(1)}, u32[]{:S(2)}, u32[]{:S(2)}) collective-permute-start(bf16[4,14,32,128]{3,2,1,0:T(8,128)(2,1)S(1)} %get-tuple-element.78.rest_3_), channel_id=1, source_target_pairs={{1,2},{2,1},{5,6},{6,5},{9,10},{10,9},{13,14},{14,13},{17,18},{18,... | collective-permute-start | bytes 1376264 | tf_op jit(solution)/shard_map/ppermute | solution.py:940
  14.0 12.7 %collective-permute-start.1 = (bf16[4,14,32,128]{3,2,1,0:T(8,128)(2,1)S(1)}, bf16[4,14,32,128]{3,2,1,0:T(8,128)(2,1)S(1)}, u32[]{:S(2)}, u32[]{:S(2)}) collective-permute-start(bf16[4,14,32,128]{3,2,1,0:T(8,128)(2,1)S(1)} %get-tuple-element.78.rest_3_), channel_id=1, source_target_pairs={{0,2},{3,1},{1,0},{2,3},{4,6},{7,5},{5,4},{6,7},{8,10},{11,9},{9,8... | collective-permute-start | bytes 1376264 | tf_op jit(solution)/shard_map/ppermute | solution.py:939
  27.3 14.3 %collective-permute-start.4 = (bf16[4,14,32,128]{3,2,1,0:T(8,128)(2,1)S(1)}, bf16[4,14,32,128]{3,2,1,0:T(8,128)(2,1)S(1)}, u32[]{:S(2)}, u32[]{:S(2)}) collective-permute-start(bf16[4,14,32,128]{3,2,1,0:T(8,128)(2,1)S(1)} %get-tuple-element.85.rest_8_), channel_id=1, source_target_pairs={{0,2},{3,1},{1,0},{2,3},{4,6},{7,5},{5,4},{6,7},{8,10},{11,9},{9,8... | collective-permute-start | bytes 1376264 | tf_op jit(solution)/shard_map/ppermute | solution.py:939
  32.2 14.7 %collective-permute-start.3 = (bf16[4,14,32,128]{3,2,1,0:T(8,128)(2,1)S(1)}, bf16[4,14,32,128]{3,2,1,0:T(8,128)(2,1)S(1)}, u32[]{:S(2)}, u32[]{:S(2)}) collective-permute-start(bf16[4,14,32,128]{3,2,1,0:T(8,128)(2,1)S(1)} %get-tuple-element.84.rest_6_), channel_id=1, source_target_pairs={{0,1},{1,0},{2,3},{3,2},{4,5},{5,4},{6,7},{7,6},{8,9},{9,8},{10,11... | collective-permute-start | bytes 1376264 | tf_op jit(solution)/shard_map/ppermute | solution.py:938
  41.6 65.4 %collective-permute-start.11 = (bf16[8,18,32,128]{3,2,1,0:T(8,128)(2,1)S(1)}, bf16[8,18,32,128]{3,2,1,0:T(8,128)(2,1)S(1)}, u32[]{:S(2)}, u32[]{:S(2)}) collective-permute-start(bf16[8,18,32,128]{3,2,1,0:T(8,128)(2,1)S(1)} %get-tuple-element.96.rest_3_), channel_id=1, source_target_pairs={{1,2},{2,1},{5,6},{6,5},{9,10},{10,9},{13,14},{14,13},{17,18},{18,... | collective-permute-start | bytes 3538952 | tf_op jit(solution)/shard_map/ppermute | solution.py:940
  42.4 77.0 %collective-permute-start.10 = (bf16[8,18,32,128]{3,2,1,0:T(8,128)(2,1)S(1)}, bf16[8,18,32,128]{3,2,1,0:T(8,128)(2,1)S(1)}, u32[]{:S(2)}, u32[]{:S(2)}) collective-permute-start(bf16[8,18,32,128]{3,2,1,0:T(8,128)(2,1)S(1)} %get-tuple-element.96.rest_3_), channel_id=1, source_target_pairs={{0,2},{3,1},{1,0},{2,3},{4,6},{7,5},{5,4},{6,7},{8,10},{11,9},{9,8... | collective-permute-start | bytes 3538952 | tf_op jit(solution)/shard_map/ppermute | solution.py:939
  46.9 72.5 %collective-permute-start.9 = (bf16[8,18,32,128]{3,2,1,0:T(8,128)(2,1)S(1)}, bf16[8,18,32,128]{3,2,1,0:T(8,128)(2,1)S(1)}, u32[]{:S(2)}, u32[]{:S(2)}) collective-permute-start(bf16[8,18,32,128]{3,2,1,0:T(8,128)(2,1)S(1)} %get-tuple-element.94.rest_1_), channel_id=1, source_target_pairs={{0,1},{1,0},{2,3},{3,2},{4,5},{5,4},{6,7},{7,6},{8,9},{9,8},{10,11... | collective-permute-start | bytes 3538952 | tf_op jit(solution)/shard_map/ppermute | solution.py:938
  94.1 14.0 %collective-permute-start.8 = (bf16[4,14,32,128]{3,2,1,0:T(8,128)(2,1)S(1)}, bf16[4,14,32,128]{3,2,1,0:T(8,128)(2,1)S(1)}, u32[]{:S(2)}, u32[]{:S(2)}) collective-permute-start(bf16[4,14,32,128]{3,2,1,0:T(8,128)(2,1)S(1)} %get-tuple-element.89), channel_id=1, source_target_pairs={{0,12},{4,0},{8,4},{12,8},{1,13},{5,1},{9,5},{13,9},{2,14},{6,2},{... | collective-permute-start | bytes 1376264 | tf_op jit(solution)/shard_map/ppermute | solution.py:966
  94.1 24.3 %collective-permute-start.7 = (bf16[4,14,32,128]{3,2,1,0:T(8,128)(2,1)S(1)}, bf16[4,14,32,128]{3,2,1,0:T(8,128)(2,1)S(1)}, u32[]{:S(2)}, u32[]{:S(2)}) collective-permute-start(bf16[4,14,32,128]{3,2,1,0:T(8,128)(2,1)S(1)} %get-tuple-element.87), channel_id=1, source_target_pairs={{0,4},{4,8},{8,12},{12,0},{1,5},{5,9},{9,13},{13,1},{2,6},{6,10},{... | collective-permute-start | bytes 1376264 | tf_op jit(solution)/shard_map/ppermute | solution.py:966
  107.0 19.8 %collective-permute-start.14 = (bf16[4,32,32,128]{3,2,1,0:T(8,128)(2,1)S(1)}, bf16[4,32,32,128]{3,2,1,0:T(8,128)(2,1)S(1)}, u32[]{:S(2)}, u32[]{:S(2)}) collective-permute-start(bf16[4,32,32,128]{3,2,1,0:T(8,128)(2,1)S(1)} %get-tuple-element.104.rest_1_), channel_id=1, source_target_pairs={{0,1},{1,0},{2,3},{3,2},{4,5},{5,4},{6,7},{7,6},{8,9},{9,8},{10,11... | collective-permute-start | bytes 3145736 | tf_op jit(solution)/shard_map/ppermute | solution.py:938
  108.9 17.9 %collective-permute-start.16 = (bf16[4,32,32,128]{3,2,1,0:T(8,128)(2,1)S(1)}, bf16[4,32,32,128]{3,2,1,0:T(8,128)(2,1)}, u32[]{:S(2)}, u32[]{:S(2)}) collective-permute-start(bf16[4,32,32,128]{3,2,1,0:T(8,128)(2,1)S(1)} %get-tuple-element.105.rest_3_), channel_id=1, source_target_pairs={{1,2},{2,1},{5,6},{6,5},{9,10},{10,9},{13,14},{14,13},{17,18},{18,... | collective-permute-start | bytes 3145736 | tf_op jit(solution)/shard_map/ppermute | solution.py:940
  119.2 15.4 %collective-permute-start.15 = (bf16[4,32,32,128]{3,2,1,0:T(8,128)(2,1)S(1)}, bf16[4,32,32,128]{3,2,1,0:T(8,128)(2,1)}, u32[]{:S(2)}, u32[]{:S(2)}) collective-permute-start(bf16[4,32,32,128]{3,2,1,0:T(8,128)(2,1)S(1)} %get-tuple-element.105.rest_3_), channel_id=1, source_target_pairs={{0,2},{3,1},{1,0},{2,3},{4,6},{7,5},{5,4},{6,7},{8,10},{11,9},{9,8... | collective-permute-start | bytes 3145736 | tf_op jit(solution)/shard_map/ppermute | solution.py:939
  124.7 15.0 %collective-permute-start.13 = (bf16[4,18,32,128]{3,2,1,0:T(8,128)(2,1)}, bf16[4,18,32,128]{3,2,1,0:T(8,128)(2,1)}, u32[]{:S(2)}, u32[]{:S(2)}) collective-permute-start(bf16[4,18,32,128]{3,2,1,0:T(8,128)(2,1)} %get-tuple-element.100), channel_id=1, source_target_pairs={{0,12},{4,0},{8,4},{12,8},{1,13},{5,1},{9,5},{13,9},{2,14},{6,2},{... | collective-permute-start | bytes 1769480 | tf_op jit(solution)/shard_map/ppermute | solution.py:966
  124.9 26.9 %collective-permute-start.12 = (bf16[4,18,32,128]{3,2,1,0:T(8,128)(2,1)}, bf16[4,18,32,128]{3,2,1,0:T(8,128)(2,1)}, u32[]{:S(2)}, u32[]{:S(2)}) collective-permute-start(bf16[4,18,32,128]{3,2,1,0:T(8,128)(2,1)} %get-tuple-element.98), channel_id=1, source_target_pairs={{0,4},{4,8},{8,12},{12,0},{1,5},{5,9},{9,13},{13,1},{2,6},{6,10},{... | collective-permute-start | bytes 1769480 | tf_op jit(solution)/shard_map/ppermute | solution.py:966
  166.3 17.2 %collective-permute-start.17 = (bf16[4,14,32,128]{3,2,1,0:T(8,128)(2,1)S(1)}, bf16[4,14,32,128]{3,2,1,0:T(8,128)(2,1)S(1)}, u32[]{:S(2)}, u32[]{:S(2)}) collective-permute-start(bf16[4,14,32,128]{3,2,1,0:T(8,128)(2,1)S(1)} %get-tuple-element.108.rest_0_), channel_id=1, source_target_pairs={{1,3},{2,0},{0,1},{3,2},{5,7},{6,4},{4,5},{7,6},{9,11},{10,8},{8,9... | collective-permute-start | bytes 1376264 | tf_op jit(solution)/shard_map/ppermute | solution.py:946
  167.9 19.6 %collective-permute-start.19 = (bf16[4,14,32,128]{3,2,1,0:T(8,128)(2,1)S(1)}, bf16[4,14,32,128]{3,2,1,0:T(8,128)(2,1)S(1)}, u32[]{:S(2)}, u32[]{:S(2)}) collective-permute-start(bf16[4,14,32,128]{3,2,1,0:T(8,128)(2,1)S(1)} %get-tuple-element.115.rest_3_), channel_id=1, source_target_pairs={{0,2},{2,0},{1,3},{3,1},{4,6},{6,4},{5,7},{7,5},{8,10},{10,8},{9,1... | collective-permute-start | bytes 1376264 | tf_op jit(solution)/shard_map/ppermute | solution.py:947
  167.9 44.7 %collective-permute-start.23 = (bf16[4,32,32,128]{3,2,1,0:T(8,128)(2,1)S(1)}, bf16[4,32,32,128]{3,2,1,0:T(8,128)(2,1)S(1)}, u32[]{:S(2)}, u32[]{:S(2)}) collective-permute-start(bf16[4,32,32,128]{3,2,1,0:T(8,128)(2,1)S(1)} %get-tuple-element.123), channel_id=1, source_target_pairs={{0,8},{4,12},{8,0},{12,4},{1,9},{5,13},{9,1},{13,5},{2,10},{6,14},... | collective-permute-start | bytes 3145736 | tf_op jit(solution)/shard_map/ppermute | solution.py:966
  187.4 10.3 %collective-permute-start.20 = (bf16[4,14,32,128]{3,2,1,0:T(8,128)(2,1)S(1)}, bf16[4,14,32,128]{3,2,1,0:T(8,128)(2,1)S(1)}, u32[]{:S(2)}, u32[]{:S(2)}) collective-permute-start(bf16[4,14,32,128]{3,2,1,0:T(8,128)(2,1)S(1)} %get-tuple-element.117.rest_5_), channel_id=1, source_target_pairs={{1,3},{2,0},{0,1},{3,2},{5,7},{6,4},{4,5},{7,6},{9,11},{10,8},{8,9... | collective-permute-start | bytes 1376264 | tf_op jit(solution)/shard_map/ppermute | solution.py:946
  188.8 26.9 %collective-permute-start.22 = (bf16[4,14,32,128]{3,2,1,0:T(8,128)(2,1)S(1)}, bf16[4,14,32,128]{3,2,1,0:T(8,128)(2,1)S(1)}, u32[]{:S(2)}, u32[]{:S(2)}) collective-permute-start(bf16[4,14,32,128]{3,2,1,0:T(8,128)(2,1)S(1)} %get-tuple-element.120.rest_8_), channel_id=1, source_target_pairs={{0,2},{2,0},{1,3},{3,1},{4,6},{6,4},{5,7},{7,5},{8,10},{10,8},{9,1... | collective-permute-start | bytes 1376264 | tf_op jit(solution)/shard_map/ppermute | solution.py:947
  197.7 18.0 %collective-permute-start.21 = (bf16[4,14,32,128]{3,2,1,0:T(8,128)(2,1)S(1)}, bf16[4,14,32,128]{3,2,1,0:T(8,128)(2,1)S(1)}, u32[]{:S(2)}, u32[]{:S(2)}) collective-permute-start(bf16[4,14,32,128]{3,2,1,0:T(8,128)(2,1)S(1)} %collective-permute-done.20.rest_6_), channel_id=1, source_target_pairs={{0,1},{3,2},{4,5},{7,6},{8,9},{11,10},{12,13},{15,14},{16,17},{19,... | collective-permute-start | bytes 1376264 | tf_op jit(solution)/shard_map/ppermute | solution.py:948
  212.6 47.4 %collective-permute-start.24 = (bf16[4,32,32,128]{3,2,1,0:T(8,128)(2,1)S(1)}, bf16[4,32,32,128]{3,2,1,0:T(8,128)(2,1)S(1)}, u32[]{:S(2)}, u32[]{:S(2)}) collective-permute-start(bf16[4,32,32,128]{3,2,1,0:T(8,128)(2,1)S(1)} %get-tuple-element.124), channel_id=1, source_target_pairs={{0,8},{4,12},{8,0},{12,4},{1,9},{5,13},{9,1},{13,5},{2,10},{6,14},... | collective-permute-start | bytes 3145736 | tf_op jit(solution)/shard_map/ppermute | solution.py:966
  215.7 57.7 %collective-permute-start.27 = (bf16[8,18,32,128]{3,2,1,0:T(8,128)(2,1)S(1)}, bf16[8,18,32,128]{3,2,1,0:T(8,128)(2,1)S(1)}, u32[]{:S(2)}, u32[]{:S(2)}) collective-permute-start(bf16[8,18,32,128]{3,2,1,0:T(8,128)(2,1)S(1)} %get-tuple-element.132.rest_0_), channel_id=1, source_target_pairs={{1,3},{2,0},{0,1},{3,2},{5,7},{6,4},{4,5},{7,6},{9,11},{10,8},{8,9... | collective-permute-start | bytes 3538952 | tf_op jit(solution)/shard_map/ppermute | solution.py:946
  260.0 13.4 %collective-permute-start.25 = (bf16[4,14,32,128]{3,2,1,0:T(8,128)(2,1)S(1)}, bf16[4,14,32,128]{3,2,1,0:T(8,128)(2,1)S(1)}, u32[]{:S(2)}, u32[]{:S(2)}) collective-permute-start(bf16[4,14,32,128]{3,2,1,0:T(8,128)(2,1)S(1)} %get-tuple-element.125), channel_id=1, source_target_pairs={{0,4},{4,8},{8,12},{12,0},{1,5},{5,9},{9,13},{13,1},{2,6},{6,10},{... | collective-permute-start | bytes 1376264 | tf_op jit(solution)/shard_map/ppermute | solution.py:966
  261.0 36.2 %collective-permute-start.29 = (bf16[8,18,32,128]{3,2,1,0:T(8,128)(2,1)S(1)}, bf16[8,18,32,128]{3,2,1,0:T(8,128)(2,1)S(1)}, u32[]{:S(2)}, u32[]{:S(2)}) collective-permute-start(bf16[8,18,32,128]{3,2,1,0:T(8,128)(2,1)S(1)} %get-tuple-element.134.rest_3_), channel_id=1, source_target_pairs={{0,2},{2,0},{1,3},{3,1},{4,6},{6,4},{5,7},{7,5},{8,10},{10,8},{9,1... | collective-permute-start | bytes 3538952 | tf_op jit(solution)/shard_map/ppermute | solution.py:947
  273.4 23.8 %collective-permute-start.28 = (bf16[8,18,32,128]{3,2,1,0:T(8,128)(2,1)S(1)}, bf16[8,18,32,128]{3,2,1,0:T(8,128)(2,1)S(1)}, u32[]{:S(2)}, u32[]{:S(2)}) collective-permute-start(bf16[8,18,32,128]{3,2,1,0:T(8,128)(2,1)S(1)} %collective-permute-done.27.rest_1_), channel_id=1, source_target_pairs={{0,1},{3,2},{4,5},{7,6},{8,9},{11,10},{12,13},{15,14},{16,17},{19,... | collective-permute-start | bytes 3538952 | tf_op jit(solution)/shard_map/ppermute | solution.py:948
  286.1 21.4 %collective-permute-start.32 = (bf16[4,32,32,128]{3,2,1,0:T(8,128)(2,1)S(1)}, bf16[4,32,32,128]{3,2,1,0:T(8,128)(2,1)S(1)}, u32[]{:S(2)}, u32[]{:S(2)}) collective-permute-start(bf16[4,32,32,128]{3,2,1,0:T(8,128)(2,1)S(1)} %get-tuple-element.142.rest_0_), channel_id=1, source_target_pairs={{1,3},{2,0},{0,1},{3,2},{5,7},{6,4},{4,5},{7,6},{9,11},{10,8},{8,9... | collective-permute-start | bytes 3145736 | tf_op jit(solution)/shard_map/ppermute | solution.py:946
  286.1 11.1 %collective-permute-start.26 = (bf16[4,14,32,128]{3,2,1,0:T(8,128)(2,1)S(1)}, bf16[4,14,32,128]{3,2,1,0:T(8,128)(2,1)S(1)}, u32[]{:S(2)}, u32[]{:S(2)}) collective-permute-start(bf16[4,14,32,128]{3,2,1,0:T(8,128)(2,1)S(1)} %get-tuple-element.127), channel_id=1, source_target_pairs={{0,12},{4,0},{8,4},{12,8},{1,13},{5,1},{9,5},{13,9},{2,14},{6,2},{... | collective-permute-start | bytes 1376264 | tf_op jit(solution)/shard_map/ppermute | solution.py:966
  289.4 34.3 %collective-permute-start.34 = (bf16[4,32,32,128]{3,2,1,0:T(8,128)(2,1)S(1)}, bf16[4,32,32,128]{3,2,1,0:T(8,128)(2,1)S(1)}, u32[]{:S(2)}, u32[]{:S(2)}) collective-permute-start(bf16[4,32,32,128]{3,2,1,0:T(8,128)(2,1)S(1)} %get-tuple-element.144.rest_3_), channel_id=1, source_target_pairs={{0,2},{2,0},{1,3},{3,1},{4,6},{6,4},{5,7},{7,5},{8,10},{10,8},{9,1... | collective-permute-start | bytes 3145736 | tf_op jit(solution)/shard_map/ppermute | solution.py:947
  307.5 16.2 %collective-permute-start.33 = (bf16[4,32,32,128]{3,2,1,0:T(8,128)(2,1)S(1)}, bf16[4,32,32,128]{3,2,1,0:T(8,128)(2,1)S(1)}, u32[]{:S(2)}, u32[]{:S(2)}) collective-permute-start(bf16[4,32,32,128]{3,2,1,0:T(8,128)(2,1)S(1)} %collective-permute-done.32.rest_1_), channel_id=1, source_target_pairs={{0,1},{3,2},{4,5},{7,6},{8,9},{11,10},{12,13},{15,14},{16,17},{19,... | collective-permute-start | bytes 3145736 | tf_op jit(solution)/shard_map/ppermute | solution.py:948
  311.9 17.4 %collective-permute-start.31 = (bf16[4,18,32,128]{3,2,1,0:T(8,128)(2,1)S(1)}, bf16[4,18,32,128]{3,2,1,0:T(8,128)(2,1)S(1)}, u32[]{:S(2)}, u32[]{:S(2)}) collective-permute-start(bf16[4,18,32,128]{3,2,1,0:T(8,128)(2,1)S(1)} %get-tuple-element.138), channel_id=1, source_target_pairs={{0,12},{4,0},{8,4},{12,8},{1,13},{5,1},{9,5},{13,9},{2,14},{6,2},{... | collective-permute-start | bytes 1769480 | tf_op jit(solution)/shard_map/ppermute | solution.py:966
  316.2 29.2 %collective-permute-start.30 = (bf16[4,18,32,128]{3,2,1,0:T(8,128)(2,1)S(1)}, bf16[4,18,32,128]{3,2,1,0:T(8,128)(2,1)S(1)}, u32[]{:S(2)}, u32[]{:S(2)}) collective-permute-start(bf16[4,18,32,128]{3,2,1,0:T(8,128)(2,1)S(1)} %get-tuple-element.136), channel_id=1, source_target_pairs={{0,4},{4,8},{8,12},{12,0},{1,5},{5,9},{9,13},{13,1},{2,6},{6,10},{... | collective-permute-start | bytes 1769480 | tf_op jit(solution)/shard_map/ppermute | solution.py:966
  (23 other events, 241.0 us)

commit v12 on v11

--- a/solution.py
+++ b/solution.py
@@ -581,7 +581,7 @@
         ),
         out_shape=out_shape,
         input_output_aliases=aliases,
-        compiler_params=pltpu.CompilerParams(vmem_limit_bytes=28 * mebi),
+        compiler_params=pltpu.CompilerParams(vmem_limit_bytes=18 * mebi),
         cost_estimate=pl.CostEstimate(flops=1 << 33, bytes_accessed=1 << 20, transcendentals=0),
         name="open_operands",
     )(ids, blocks, pair, chains, w_in, wide, *more)
@@ -642,7 +642,7 @@
             scratch_shapes=[pltpu.VMEM((rows, cols, channels), jnp.bfloat16)] + operand_scratch(rows, cols, hidden),
         ),
         out_shape=[jax.ShapeDtypeStruct(shape, jnp.bfloat16)] * 2,
-        compiler_params=pltpu.CompilerParams(vmem_limit_bytes=20 * mebi),
+        compiler_params=pltpu.CompilerParams(vmem_limit_bytes=14 * mebi),
         cost_estimate=pl.CostEstimate(flops=1 << 33, bytes_accessed=1 << 20, transcendentals=0),
         name="far_operands",
     )(ids, blocks, mine, *sources, *sources, chains, wide)
@@ -923,7 +923,7 @@
         ),
         out_shape=out_shape,
         input_output_aliases=aliases,
-        compiler_params=pltpu.CompilerParams(vmem_limit_bytes=32 * mebi),
+        compiler_params=pltpu.CompilerParams(vmem_limit_bytes=24 * mebi),
         cost_estimate=pl.CostEstimate(flops=1 << 33, bytes_accessed=1 << 20, transcendentals=0),
         name="close_layer",
     )(ids, blocks, place, *operands, *more)
@@ -952,11 +952,13 @@
 def banded(pair, ids, blocks, owners, slot_of, chains, w_in, w_out, capacity, terms, n_blk):
     slots, rows, cols, channels = pair.shape
     hidden = w_out.shape[1]
-    far = n_blk // 2
-    near = [s for s in range(1, n_blk) if s != far] + [0]
+    far = 1
+    middle = n_blk // 2
+    near = [s for s in (middle, *range(1, n_blk)) if s != far]
+    near = [s for n, s in enumerate(near) if s not in near[:n]] + [0]
     layers = w_in.shape[0]
     current = pair
-    bands = [[14, 18], [14, 18]]
+    bands = [[12, 20], [14, 18]]
     chosen, place, mine = make_plan(ids, owners, slot_of, n_blk, far, slots, terms, capacity)
     in_order = jnp.repeat(jnp.arange(capacity, dtype=jnp.int32), 2)
     half = slots // 2
@@ -1004,7 +1006,7 @@
                     ((other, _), _), ((one, _), (_, two)) = exchanged[-1]
                     left = after(left, other)
                     right = after(right, one, two, chosen)
-                exchanged = [exchange(left, right, by_shift[near[0]])]
+                exchanged = [exchange(left, right, list(by_shift.values())[-1] if by_shift else made[-1])]
                 ids = after(ids, *by_shift.values())
             made = banded_products(near, ids, chosen, exchanged, capacity, cols)
             start = sum(bands[layer][:chunk])

time: 355 us -> 306 us (0.86)
  waiting for transfers between devices: 182 us -> 136 us
  Pallas kernels: 104 us -> 100 us
    ppermute x11, waiting for transfers between devices: 144 us -> 104 us  [over_blk(): lax.ppermute(value, 'blk', [(p, (p + shift) % n_blk) for p in range(n_blk)])]
    ppermute x4, starting transfers between devices: 1.13 us -> 8.37 us  [exchange_bands_outgoing(): other = lax.ppermute(left, 'sub', [(0, 1), (1, 0)])]
    ppermute x4, waiting for transfers between devices: 13.6 us -> 8.55 us  [exchange_bands_incoming(): one = lax.ppermute(left, both, [(1, 3), (2, 0), (0, 1), (3, 2)])]
    ppermute x4, starting transfers between devices: 4.25 us -> 0.33 us  [exchange_bands_incoming(): one = lax.ppermute(left, both, [(1, 3), (2, 0), (0, 1), (3, 2)])]
    unnamed x40 -> x52, local copies, waits for them, and re-layouts: 8.05 us -> 9.37 us
  transfers between devices with their start and end apart: 35 -> 35, of which waited for: 17 -> 14; matrix products, arithmetic and copies ran while one was open for 0% -> 0% of each run, Pallas kernels for 23% -> 25%
where the time goes in v12:
time: 306 us; the launch traced here: 305 us
  waiting for transfers between devices  136 us (44%)
  Pallas kernels  100 us (33%)
  starting transfers between devices  58.1 us (19%)
  local copies, waits for them, and re-layouts  10.6 us (3%)
    ppermute x11, waiting for transfers between devices, over_blk(): lax.ppermute(value, 'blk', [(p, (p + shift) % n_blk) for p in range(n_blk)])  104 us
    pallas_call x3, Pallas kernels, close_layer(): pl.pallas_call(functools.partial(close_kernel, *(layer, last, spots, 0 if...  35.8 us
    pallas_call x6, Pallas kernels, banded_products(): pl.pallas_call(functools.partial(banded_kernel, shifts, capacity, tuple(p...  25.5 us
    pallas_call x2, Pallas kernels, far_operands(): pl.pallas_call(functools.partial(far_kernel, layer, n_blk, far, lax.axis_...  19.4 us
    ppermute x11, starting transfers between devices, over_blk(): lax.ppermute(value, 'blk', [(p, (p + shift) % n_blk) for p in range(n_blk)])  18.8 us
    pallas_call x2, Pallas kernels, open_operands(): pl.pallas_call(functools.partial(open_kernel, hidden, len(bands), lax.axi...  16.6 us
    ppermute x4, waiting for transfers between devices, exchange_bands_outgoing(): one = lax.ppermute(right, both, [(0, 2), (3, 1), (1, 0), (2, 3)])  14.6 us
    ppermute x4, starting transfers between devices, exchange_bands_outgoing(): one = lax.ppermute(right, both, [(0, 2), (3, 1), (1, 0), (2, 3)])  12.2 us
  transfers between devices with their start and end apart: 35, of which 14 were waited for; matrix products, arithmetic and copies ran while one was open for 0% of the time, Pallas kernels for 25%

profile of v12, /device:TPU:11, one launch (start us, length us, event | category | flops | bytes accessed | tf_op | source)
XLA Modules:
  0.0 305.0 jit_solution(16493242471045995708)
XLA Ops:
  3.9 8.3 %open_operands.2 = (f32[8,32,32,128]{3,2,1,0:T(8,128)S(1)}, bf16[4,12,32,128]{3,2,1,0:T(8,128)(2,1)S(1)}, bf16[8,20,32,128]{3,2,1,0:T(8,128)(2,1)S(1)}, bf16[4,1...) custom-call(s32[4]{0:T(128)S(1)} %pad_add_fusion.ids, s32[2,32]{1,0:T(2,128)S(1)} %bitcast.16, ...), custom_call_target="tpu_custom_call" | custom-call | flops 8589934592 | bytes 1048576 | tf_op jit(solution)/shard_map/open_operands/pallas_call | solution.py:567
  12.9 3.5 %collective-permute-start.1 = (bf16[4,12,32,128]{3,2,1,0:T(8,128)(2,1)S(1)}, bf16[4,12,32,128]{3,2,1,0:T(8,128)(2,1)S(1)}, u32[]{:S(2)}, u32[]{:S(2)}) collective-permute-start(bf16[4,12,32,128]{3,2,1,0:T(8,128)(2,1)S(1)} %get-tuple-element.78.rest_3_), channel_id=1, source_target_pairs={{0,2},{3,1},{1,0},{2,3},{4,6},{7,5},{5,4},{6,7},{8,10},{11,9},{9,8... | collective-permute-start | bytes 1179656 | tf_op jit(solution)/shard_map/ppermute | solution.py:939
  16.5 8.3 %open_operands.3 = (f32[8,32,32,128]{3,2,1,0:T(8,128)S(1)}, bf16[4,12,32,128]{3,2,1,0:T(8,128)(2,1)S(1)}, bf16[8,20,32,128]{3,2,1,0:T(8,128)(2,1)S(1)}, bf16[4,1...) custom-call(s32[4]{0:T(128)S(1)} %pad_add_fusion.ids, ...), custom_call_target="tpu_custom_call", output_to_operand_aliasing={{0}: (6, {}), {2}: (7, {}), {4}: (8, {})} | custom-call | flops 8589934592 | bytes 1048576 | tf_op jit(solution)/shard_map/open_operands/pallas_call | solution.py:567
  27.5 3.1 %collective-permute-start.4 = (bf16[4,12,32,128]{3,2,1,0:T(8,128)(2,1)S(1)}, bf16[4,12,32,128]{3,2,1,0:T(8,128)(2,1)S(1)}, u32[]{:S(2)}, u32[]{:S(2)}) collective-permute-start(bf16[4,12,32,128]{3,2,1,0:T(8,128)(2,1)S(1)} %get-tuple-element.85.rest_8_), channel_id=1, source_target_pairs={{0,2},{3,1},{1,0},{2,3},{4,6},{7,5},{5,4},{6,7},{8,10},{11,9},{9,8... | collective-permute-start | bytes 1179656 | tf_op jit(solution)/shard_map/ppermute | solution.py:939
  32.9 5.7 %collective-permute-done.4.rest_7_ = bf16[4,12,32,128]{3,2,1,0:T(8,128)(2,1)S(1)} collective-permute-done((bf16[4,12,32,128]{3,2,1,0:T(8,128)(2,1)S(1)}, bf16[4,12,32,128]{3,2,1,0:T(8,128)(2,1)S(1)}, u32[]{:S(2)}, u32[]{:S(2)}) %collective-permute-start.4) | collective-permute-done | bytes 393248 | tf_op jit(solution)/shard_map/ppermute | solution.py:939
  39.3 4.5 %collective-permute-start.10 = (bf16[8,20,32,128]{3,2,1,0:T(8,128)(2,1)S(1)}, bf16[8,20,32,128]{3,2,1,0:T(8,128)(2,1)S(1)}, u32[]{:S(2)}, u32[]{:S(2)}) collective-permute-start(bf16[8,20,32,128]{3,2,1,0:T(8,128)(2,1)S(1)} %get-tuple-element.96.rest_3_), channel_id=1, source_target_pairs={{0,2},{3,1},{1,0},{2,3},{4,6},{7,5},{5,4},{6,7},{8,10},{11,9},{9,8... | collective-permute-start | bytes 3932168 | tf_op jit(solution)/shard_map/ppermute | solution.py:939
  43.9 4.9 %banded_products.6 = (bf16[4,12,32,128]{3,2,1,0:T(8,128)(2,1)S(1)}, bf16[4,12,32,128]{3,2,1,0:T(8,128)(2,1)S(1)}, bf16[4,12,32,128]{3,2,1,0:T(8,128)(2,1)S(1)}) custom-call(s32[4]{0:T(128)S(1)} %pad_add_fusion.ids, s32[40]{0:T(128)S(1)} %get-tuple-element.76.chosen, bf16[4,12,32,128]{3,2,1,0:T(8,128)(2,1)S(1)} %collective-permute-done.rest_0_, ...), custom_call_target="tpu_custom_call" | custom-call | flops 301989888 | bytes 1 | tf_op jit(solution)/shard_map/banded_products/pallas_call | solution.py:771
  54.2 9.8 %far_operands.2 = (bf16[4,32,32,128]{3,2,1,0:T(8,128)(2,1)S(1)}, bf16[4,32,32,128]{3,2,1,0:T(8,128)(2,1)S(1)}) custom-call(s32[4]{0:T(128)S(1)} %pad_add_fusion.ids, s32[2,32]{1,0:T(2,128)S(1)} %bitcast.18, s32[10]{0:T(128)S(1)} %get-tuple-element.102.mine, bf16[8,32,32,128]{3,2,1,0:T(8,128)(2,1)S(1)} %copy-done.5, bf16[8,32,32,128]{3,2,1,0:T(8,128)(2,1)S(1)} %copy-done.5, ...), custom_call_target="tpu_custom_call" | custom-call | flops 8589934592 | bytes 1048576 | tf_op jit(solution)/shard_map/far_operands/pallas_call | solution.py:633
  64.0 8.4 %collective-permute-start.14 = (bf16[4,32,32,128]{3,2,1,0:T(8,128)(2,1)S(1)}, bf16[4,32,32,128]{3,2,1,0:T(8,128)(2,1)S(1)}, u32[]{:S(2)}, u32[]{:S(2)}) collective-permute-start(bf16[4,32,32,128]{3,2,1,0:T(8,128)(2,1)S(1)} %get-tuple-element.104.rest_1_), channel_id=1, source_target_pairs={{0,1},{1,0},{2,3},{3,2},{4,5},{5,4},{6,7},{7,6},{8,9},{9,8},{10,11... | collective-permute-start | bytes 3145736 | tf_op jit(solution)/shard_map/ppermute | solution.py:938
  74.0 3.6 %collective-permute-done.7.rest_0_ = bf16[4,12,32,128]{3,2,1,0:T(8,128)(2,1)S(1)} collective-permute-done((bf16[4,12,32,128]{3,2,1,0:T(8,128)(2,1)S(1)}, bf16[4,12,32,128]{3,2,1,0:T(8,128)(2,1)S(1)}, u32[]{:S(2)}, u32[]{:S(2)}) %collective-permute-start.7) | collective-permute-done | bytes 393248 | tf_op jit(solution)/shard_map/ppermute | solution.py:968
  78.7 4.1 %banded_products.7 = (bf16[4,20,32,128]{3,2,1,0:T(8,128)(2,1)}, bf16[4,20,32,128]{3,2,1,0:T(8,128)(2,1)}, bf16[4,20,32,128]{3,2,1,0:T(8,128)(2,1)S(1)}) custom-call(s32[4]{0:T(128)S(1)} %pad_add_fusion.ids, s32[40]{0:T(128)S(1)} %get-tuple-element.76.chosen, bf16[8,20,32,128]{3,2,1,0:T(8,128)(2,1)S(1)} %collective-permute-done.9.rest_0_, ...), custom_call_target="tpu_custom_call" | custom-call | flops 503316480 | bytes 1 | tf_op jit(solution)/shard_map/banded_products/pallas_call | solution.py:771
  89.7 8.9 %collective-permute-done.15.rest_2_ = bf16[4,32,32,128]{3,2,1,0:T(8,128)(2,1)} collective-permute-done((bf16[4,32,32,128]{3,2,1,0:T(8,128)(2,1)S(1)}, bf16[4,32,32,128]{3,2,1,0:T(8,128)(2,1)}, u32[]{:S(2)}, u32[]{:S(2)}) %collective-permute-start.15) | collective-permute-done | bytes 1048608 | tf_op jit(solution)/shard_map/ppermute | solution.py:939
  98.7 3.4 %banded_products.8.rest_6_ = bf16[4,32,32,128]{3,2,1,0:T(8,128)(2,1)S(1)} custom-call(s32[4]{0:T(128)S(1)} %pad_add_fusion.ids, s32[8]{0:T(128)S(1)} %reshape.9.chosen, bf16[4,32,32,128]{3,2,1,0:T(8,128)(2,1)S(1)} %collective-permute-done.14.rest_0_, bf16[4,32,32,128]{3,2,1,0:T(8,128)(2,1)S(1)} %get-tuple-element.104.rest_1_, ...), custom_call_target="tpu_custom_call" | custom-call | flops 268435456 | bytes 1 | tf_op jit(solution)/shard_map/banded_products/pallas_call | solution.py:771
  102.1 27.7 %collective-permute-done.12.rest_3_ = bf16[4,20,32,128]{3,2,1,0:T(8,128)(2,1)} collective-permute-done((bf16[4,20,32,128]{3,2,1,0:T(8,128)(2,1)}, bf16[4,20,32,128]{3,2,1,0:T(8,128)(2,1)}, u32[]{:S(2)}, u32[]{:S(2)}) %collective-permute-start.12) | collective-permute-done | bytes 655392 | tf_op jit(solution)/shard_map/ppermute | solution.py:968
  129.9 13.4 %close_layer.3 = (bf16[8,32,32,128]{3,2,1,0:T(8,128)(2,1)S(1)}, f32[8,32,32,128]{3,2,1,0:T(8,128)S(1)}, bf16[4,32,32,128]{3,2,1,0:T(8,128)(2,1)S(1)}, bf16[4,14,...) custom-call(s32[4]{0:T(128)S(1)} %pad_add_fusion.ids, ...), custom_call_target="tpu_custom_call" | custom-call | flops 8589934592 | bytes 1048576 | tf_op jit(solution)/shard_map/close_layer/pallas_call | solution.py:911
  144.8 13.4 %close_layer.4 = (bf16[8,32,32,128]{3,2,1,0:T(8,128)(2,1)S(1)}, f32[8,32,32,128]{3,2,1,0:T(8,128)S(1)}, bf16[4,32,32,128]{3,2,1,0:T(8,128)(2,1)S(1)}, bf16[4,14,...) custom-call(s32[4]{0:T(128)S(1)} %pad_add_fusion.ids, ...), custom_call_target="tpu_custom_call", output_to_operand_aliasing={{0}: (16, {}), {1}: (17, {}), {4}: (18, {}), {6}: (19, {})} | custom-call | flops 8589934592 | bytes 1048576 | tf_op jit(solution)/shard_map/close_layer/pallas_call | solution.py:911
  162.2 8.5 %collective-permute-done.20.rest_6_ = bf16[4,14,32,128]{3,2,1,0:T(8,128)(2,1)S(1)} collective-permute-done((bf16[4,14,32,128]{3,2,1,0:T(8,128)(2,1)S(1)}, bf16[4,14,32,128]{3,2,1,0:T(8,128)(2,1)S(1)}, u32[]{:S(2)}, u32[]{:S(2)}) %collective-permute-start.20) | collective-permute-done | bytes 458784 | tf_op jit(solution)/shard_map/ppermute | solution.py:946
  170.8 4.1 %collective-permute-start.21 = (bf16[4,14,32,128]{3,2,1,0:T(8,128)(2,1)S(1)}, bf16[4,14,32,128]{3,2,1,0:T(8,128)(2,1)S(1)}, u32[]{:S(2)}, u32[]{:S(2)}) collective-permute-start(bf16[4,14,32,128]{3,2,1,0:T(8,128)(2,1)S(1)} %collective-permute-done.20.rest_6_), channel_id=1, source_target_pairs={{0,1},{3,2},{4,5},{7,6},{8,9},{11,10},{12,13},{15,14},{16,17},{19,... | collective-permute-start | bytes 1376264 | tf_op jit(solution)/shard_map/ppermute | solution.py:948
  178.2 6.0 %banded_products.9 = (bf16[4,14,32,128]{3,2,1,0:T(8,128)(2,1)S(1)}, bf16[4,14,32,128]{3,2,1,0:T(8,128)(2,1)S(1)}, bf16[4,14,32,128]{3,2,1,0:T(8,128)(2,1)S(1)}) custom-call(s32[4]{0:T(128)S(1)} %pad_add_fusion.ids, s32[40]{0:T(128)S(1)} %get-tuple-element.76.chosen, bf16[4,14,32,128]{3,2,1,0:T(8,128)(2,1)S(1)} %get-tuple-element.108.rest_0_, ...), custom_call_target="tpu_custom_call" | custom-call | flops 352321536 | bytes 1 | tf_op jit(solution)/shard_map/banded_products/pallas_call | solution.py:771
  184.2 15.6 %collective-permute-done.24.rest_1_.rest_3_ = bf16[4,32,32,128]{3,2,1,0:T(8,128)(2,1)S(1)} collective-permute-done((bf16[4,32,32,128]{3,2,1,0:T(8,128)(2,1)S(1)}, bf16[4,32,32,128]{3,2,1,0:T(8,128)(2,1)S(1)}, u32[]{:S(2)}, u32[]{:S(2)}) %collective-permute-start.24) | collective-permute-done | bytes 1048608 | tf_op jit(solution)/shard_map/ppermute | solution.py:968
  202.2 10.3 %collective-permute-done.26.rest_1_ = bf16[4,14,32,128]{3,2,1,0:T(8,128)(2,1)S(1)} collective-permute-done((bf16[4,14,32,128]{3,2,1,0:T(8,128)(2,1)S(1)}, bf16[4,14,32,128]{3,2,1,0:T(8,128)(2,1)S(1)}, u32[]{:S(2)}, u32[]{:S(2)}) %collective-permute-start.26) | collective-permute-done | bytes 458784 | tf_op jit(solution)/shard_map/ppermute | solution.py:968
  212.4 2.9 collective-permute-start.28
  215.3 9.6 %far_operands.3 = (bf16[4,32,32,128]{3,2,1,0:T(8,128)(2,1)S(1)}, bf16[4,32,32,128]{3,2,1,0:T(8,128)(2,1)S(1)}) custom-call(s32[4]{0:T(128)S(1)} %pad_add_fusion.ids, s32[2,32]{1,0:T(2,128)S(1)} %bitcast.21, s32[10]{0:T(128)S(1)} %copy-done.23, bf16[4,32,32,128]{3,2,1,0:T(8,128)(2,1)S(1)} %collective-permute-done.23.rest_0_.rest_2_, ...), custom_call_target="tpu_custom_call" | custom-call | flops 8589934592 | bytes 1048576 | tf_op jit(solution)/shard_map/far_operands/pallas_call | solution.py:633
  225.0 4.3 %collective-permute-start.25 = (bf16[4,14,32,128]{3,2,1,0:T(8,128)(2,1)S(1)}, bf16[4,14,32,128]{3,2,1,0:T(8,128)(2,1)S(1)}, u32[]{:S(2)}, u32[]{:S(2)}) collective-permute-start(bf16[4,14,32,128]{3,2,1,0:T(8,128)(2,1)S(1)} %get-tuple-element.125), channel_id=1, source_target_pairs={{0,8},{4,12},{8,0},{12,4},{1,9},{5,13},{9,1},{13,5},{2,10},{6,14},... | collective-permute-start | bytes 1376264 | tf_op jit(solution)/shard_map/ppermute | solution.py:968
  230.7 16.7 %collective-permute-done.25.rest_0_ = bf16[4,14,32,128]{3,2,1,0:T(8,128)(2,1)S(1)} collective-permute-done((bf16[4,14,32,128]{3,2,1,0:T(8,128)(2,1)S(1)}, bf16[4,14,32,128]{3,2,1,0:T(8,128)(2,1)S(1)}, u32[]{:S(2)}, u32[]{:S(2)}) %collective-permute-start.25) | collective-permute-done | bytes 458784 | tf_op jit(solution)/shard_map/ppermute | solution.py:968
  247.4 4.7 %banded_products.10 = (bf16[4,18,32,128]{3,2,1,0:T(8,128)(2,1)S(1)}, bf16[4,18,32,128]{3,2,1,0:T(8,128)(2,1)S(1)}, bf16[4,18,32,128]{3,2,1,0:T(8,128)(2,1)S(1)}) custom-call(s32[4]{0:T(128)S(1)} %pad_add_fusion.ids, s32[40]{0:T(128)S(1)} %get-tuple-element.76.chosen, bf16[8,18,32,128]{3,2,1,0:T(8,128)(2,1)S(1)} %get-tuple-element.132.rest_0_, ...), custom_call_target="tpu_custom_call" | custom-call | flops 452984832 | bytes 1 | tf_op jit(solution)/shard_map/banded_products/pallas_call | solution.py:771
  254.4 2.3 collective-permute-start.31
  257.7 6.2 %collective-permute-done.34.rest_4_ = bf16[4,32,32,128]{3,2,1,0:T(8,128)(2,1)S(1)} collective-permute-done((bf16[4,32,32,128]{3,2,1,0:T(8,128)(2,1)S(1)}, bf16[4,32,32,128]{3,2,1,0:T(8,128)(2,1)S(1)}, u32[]{:S(2)}, u32[]{:S(2)}) %collective-permute-start.34) | collective-permute-done | bytes 1048608 | tf_op jit(solution)/shard_map/ppermute | solution.py:947
  263.9 2.4 banded_products.11.rest_6_
  266.2 4.9 %collective-permute-done.31.rest_4_ = bf16[4,18,32,128]{3,2,1,0:T(8,128)(2,1)S(1)} collective-permute-done((bf16[4,18,32,128]{3,2,1,0:T(8,128)(2,1)S(1)}, bf16[4,18,32,128]{3,2,1,0:T(8,128)(2,1)S(1)}, u32[]{:S(2)}, u32[]{:S(2)}) %collective-permute-start.31) | collective-permute-done | bytes 589856 | tf_op jit(solution)/shard_map/ppermute | solution.py:968
  271.1 24.7 %collective-permute-done.30.rest_3_ = bf16[4,18,32,128]{3,2,1,0:T(8,128)(2,1)S(1)} collective-permute-done((bf16[4,18,32,128]{3,2,1,0:T(8,128)(2,1)S(1)}, bf16[4,18,32,128]{3,2,1,0:T(8,128)(2,1)S(1)}, u32[]{:S(2)}, u32[]{:S(2)}) %collective-permute-start.30) | collective-permute-done | bytes 589856 | tf_op jit(solution)/shard_map/ppermute | solution.py:968
  295.9 9.0 %close_layer.5 = bf16[8,32,32,128]{3,2,1,0:T(8,128)(2,1)} custom-call(s32[4]{0:T(128)S(1)} %pad_add_fusion.ids, s32[2,32]{1,0:T(2,128)S(1)} %bitcast.22, s32[16]{0:T(128)S(1)} %copy-done.21, bf16[4,14,32,128]{3,2,1,0:T(8,128)(2,1)S(1)} %collective-permute-done.25.rest_0_, bf16[4,14,32,128]{3,2,1,0:T(8,128)(2,1)S(1)} %collective-permute-done.26.rest_1_, ...), custom_call_target="tpu_custom_call" | custom-call | flops 8589934592 | bytes 1048576 | tf_op jit(solution)/shard_map/close_layer/pallas_call | solution.py:911
  (109 shorter events, 41.0 us)
Async XLA Ops:
  0.0 48.8 %collective-permute-start.6 = (bf16[8,32,32,128]{3,2,1,0:T(8,128)(2,1)}, bf16[8,32,32,128]{3,2,1,0:T(8,128)(2,1)S(1)}, u32[]{:S(2)}, u32[]{:S(2)}) collective-permute-start(bf16[8,32,32,128]{3,2,1,0:T(8,128)(2,1)} %rest_7_.3), channel_id=1, source_target_pairs={{0,4},{4,8},{8,12},{12,0},{1,5},{5,9},{9,13},{13,1},{2,6},{6,10},{... | collective-permute-start | bytes 6291464 | tf_op jit(solution)/shard_map/ppermute | solution.py:968
  12.2 14.6 %collective-permute-start.2 = (bf16[4,12,32,128]{3,2,1,0:T(8,128)(2,1)S(1)}, bf16[4,12,32,128]{3,2,1,0:T(8,128)(2,1)S(1)}, u32[]{:S(2)}, u32[]{:S(2)}) collective-permute-start(bf16[4,12,32,128]{3,2,1,0:T(8,128)(2,1)S(1)} %get-tuple-element.78.rest_3_), channel_id=1, source_target_pairs={{1,2},{2,1},{5,6},{6,5},{9,10},{10,9},{13,14},{14,13},{17,18},{18,... | collective-permute-start | bytes 1179656 | tf_op jit(solution)/shard_map/ppermute | solution.py:940
  12.9 13.9 %collective-permute-start.1 = (bf16[4,12,32,128]{3,2,1,0:T(8,128)(2,1)S(1)}, bf16[4,12,32,128]{3,2,1,0:T(8,128)(2,1)S(1)}, u32[]{:S(2)}, u32[]{:S(2)}) collective-permute-start(bf16[4,12,32,128]{3,2,1,0:T(8,128)(2,1)S(1)} %get-tuple-element.78.rest_3_), channel_id=1, source_target_pairs={{0,2},{3,1},{1,0},{2,3},{4,6},{7,5},{5,4},{6,7},{8,10},{11,9},{9,8... | collective-permute-start | bytes 1179656 | tf_op jit(solution)/shard_map/ppermute | solution.py:939
  16.5 10.3 %collective-permute-start = (bf16[4,12,32,128]{3,2,1,0:T(8,128)(2,1)S(1)}, bf16[4,12,32,128]{3,2,1,0:T(8,128)(2,1)S(1)}, u32[]{:S(2)}, u32[]{:S(2)}) collective-permute-start(bf16[4,12,32,128]{3,2,1,0:T(8,128)(2,1)S(1)} %get-tuple-element.77.rest_1_), channel_id=1, source_target_pairs={{0,1},{1,0},{2,3},{3,2},{4,5},{5,4},{6,7},{7,6},{8,9},{9,8},{10,11... | collective-permute-start | bytes 1179656 | tf_op jit(solution)/shard_map/ppermute | solution.py:938
  27.5 11.1 %collective-permute-start.4 = (bf16[4,12,32,128]{3,2,1,0:T(8,128)(2,1)S(1)}, bf16[4,12,32,128]{3,2,1,0:T(8,128)(2,1)S(1)}, u32[]{:S(2)}, u32[]{:S(2)}) collective-permute-start(bf16[4,12,32,128]{3,2,1,0:T(8,128)(2,1)S(1)} %get-tuple-element.85.rest_8_), channel_id=1, source_target_pairs={{0,2},{3,1},{1,0},{2,3},{4,6},{7,5},{5,4},{6,7},{8,10},{11,9},{9,8... | collective-permute-start | bytes 1179656 | tf_op jit(solution)/shard_map/ppermute | solution.py:939
  30.6 13.3 %collective-permute-start.3 = (bf16[4,12,32,128]{3,2,1,0:T(8,128)(2,1)S(1)}, bf16[4,12,32,128]{3,2,1,0:T(8,128)(2,1)S(1)}, u32[]{:S(2)}, u32[]{:S(2)}) collective-permute-start(bf16[4,12,32,128]{3,2,1,0:T(8,128)(2,1)S(1)} %get-tuple-element.84.rest_6_), channel_id=1, source_target_pairs={{0,1},{1,0},{2,3},{3,2},{4,5},{5,4},{6,7},{7,6},{8,9},{9,8},{10,11... | collective-permute-start | bytes 1179656 | tf_op jit(solution)/shard_map/ppermute | solution.py:938
  38.6 25.4 %collective-permute-start.11 = (bf16[8,20,32,128]{3,2,1,0:T(8,128)(2,1)S(1)}, bf16[8,20,32,128]{3,2,1,0:T(8,128)(2,1)S(1)}, u32[]{:S(2)}, u32[]{:S(2)}) collective-permute-start(bf16[8,20,32,128]{3,2,1,0:T(8,128)(2,1)S(1)} %get-tuple-element.96.rest_3_), channel_id=1, source_target_pairs={{1,2},{2,1},{5,6},{6,5},{9,10},{10,9},{13,14},{14,13},{17,18},{18,... | collective-permute-start | bytes 3932168 | tf_op jit(solution)/shard_map/ppermute | solution.py:940
  39.3 39.3 %collective-permute-start.10 = (bf16[8,20,32,128]{3,2,1,0:T(8,128)(2,1)S(1)}, bf16[8,20,32,128]{3,2,1,0:T(8,128)(2,1)S(1)}, u32[]{:S(2)}, u32[]{:S(2)}) collective-permute-start(bf16[8,20,32,128]{3,2,1,0:T(8,128)(2,1)S(1)} %get-tuple-element.96.rest_3_), channel_id=1, source_target_pairs={{0,2},{3,1},{1,0},{2,3},{4,6},{7,5},{5,4},{6,7},{8,10},{11,9},{9,8... | collective-permute-start | bytes 3932168 | tf_op jit(solution)/shard_map/ppermute | solution.py:939
  43.9 34.8 %collective-permute-start.9 = (bf16[8,20,32,128]{3,2,1,0:T(8,128)(2,1)S(1)}, bf16[8,20,32,128]{3,2,1,0:T(8,128)(2,1)S(1)}, u32[]{:S(2)}, u32[]{:S(2)}) collective-permute-start(bf16[8,20,32,128]{3,2,1,0:T(8,128)(2,1)S(1)} %get-tuple-element.94.rest_1_), channel_id=1, source_target_pairs={{0,1},{1,0},{2,3},{3,2},{4,5},{5,4},{6,7},{7,6},{8,9},{9,8},{10,11... | collective-permute-start | bytes 3932168 | tf_op jit(solution)/shard_map/ppermute | solution.py:938
  50.1 22.2 %collective-permute-start.8 = (bf16[4,12,32,128]{3,2,1,0:T(8,128)(2,1)S(1)}, bf16[4,12,32,128]{3,2,1,0:T(8,128)(2,1)S(1)}, u32[]{:S(2)}, u32[]{:S(2)}) collective-permute-start(bf16[4,12,32,128]{3,2,1,0:T(8,128)(2,1)S(1)} %get-tuple-element.89), channel_id=1, source_target_pairs={{0,12},{4,0},{8,4},{12,8},{1,13},{5,1},{9,5},{13,9},{2,14},{6,2},{... | collective-permute-start | bytes 1179656 | tf_op jit(solution)/shard_map/ppermute | solution.py:968
  50.3 27.4 %collective-permute-start.7 = (bf16[4,12,32,128]{3,2,1,0:T(8,128)(2,1)S(1)}, bf16[4,12,32,128]{3,2,1,0:T(8,128)(2,1)S(1)}, u32[]{:S(2)}, u32[]{:S(2)}) collective-permute-start(bf16[4,12,32,128]{3,2,1,0:T(8,128)(2,1)S(1)} %get-tuple-element.87), channel_id=1, source_target_pairs={{0,8},{4,12},{8,0},{12,4},{1,9},{5,13},{9,1},{13,5},{2,10},{6,14},... | collective-permute-start | bytes 1179656 | tf_op jit(solution)/shard_map/ppermute | solution.py:968
  64.0 25.7 %collective-permute-start.14 = (bf16[4,32,32,128]{3,2,1,0:T(8,128)(2,1)S(1)}, bf16[4,32,32,128]{3,2,1,0:T(8,128)(2,1)S(1)}, u32[]{:S(2)}, u32[]{:S(2)}) collective-permute-start(bf16[4,32,32,128]{3,2,1,0:T(8,128)(2,1)S(1)} %get-tuple-element.104.rest_1_), channel_id=1, source_target_pairs={{0,1},{1,0},{2,3},{3,2},{4,5},{5,4},{6,7},{7,6},{8,9},{9,8},{10,11... | collective-permute-start | bytes 3145736 | tf_op jit(solution)/shard_map/ppermute | solution.py:938
  72.4 17.4 %collective-permute-start.16 = (bf16[4,32,32,128]{3,2,1,0:T(8,128)(2,1)S(1)}, bf16[4,32,32,128]{3,2,1,0:T(8,128)(2,1)}, u32[]{:S(2)}, u32[]{:S(2)}) collective-permute-start(bf16[4,32,32,128]{3,2,1,0:T(8,128)(2,1)S(1)} %get-tuple-element.105.rest_3_), channel_id=1, source_target_pairs={{1,2},{2,1},{5,6},{6,5},{9,10},{10,9},{13,14},{14,13},{17,18},{18,... | collective-permute-start | bytes 3145736 | tf_op jit(solution)/shard_map/ppermute | solution.py:940
  77.7 21.0 %collective-permute-start.15 = (bf16[4,32,32,128]{3,2,1,0:T(8,128)(2,1)S(1)}, bf16[4,32,32,128]{3,2,1,0:T(8,128)(2,1)}, u32[]{:S(2)}, u32[]{:S(2)}) collective-permute-start(bf16[4,32,32,128]{3,2,1,0:T(8,128)(2,1)S(1)} %get-tuple-element.105.rest_3_), channel_id=1, source_target_pairs={{0,2},{3,1},{1,0},{2,3},{4,6},{7,5},{5,4},{6,7},{8,10},{11,9},{9,8... | collective-permute-start | bytes 3145736 | tf_op jit(solution)/shard_map/ppermute | solution.py:939
  83.8 18.3 %collective-permute-start.13 = (bf16[4,20,32,128]{3,2,1,0:T(8,128)(2,1)}, bf16[4,20,32,128]{3,2,1,0:T(8,128)(2,1)}, u32[]{:S(2)}, u32[]{:S(2)}) collective-permute-start(bf16[4,20,32,128]{3,2,1,0:T(8,128)(2,1)} %get-tuple-element.100), channel_id=1, source_target_pairs={{0,12},{4,0},{8,4},{12,8},{1,13},{5,1},{9,5},{13,9},{2,14},{6,2},{... | collective-permute-start | bytes 1966088 | tf_op jit(solution)/shard_map/ppermute | solution.py:968
  85.0 44.9 %collective-permute-start.12 = (bf16[4,20,32,128]{3,2,1,0:T(8,128)(2,1)}, bf16[4,20,32,128]{3,2,1,0:T(8,128)(2,1)}, u32[]{:S(2)}, u32[]{:S(2)}) collective-permute-start(bf16[4,20,32,128]{3,2,1,0:T(8,128)(2,1)} %get-tuple-element.98), channel_id=1, source_target_pairs={{0,8},{4,12},{8,0},{12,4},{1,9},{5,13},{9,1},{13,5},{2,10},{6,14},... | collective-permute-start | bytes 1966088 | tf_op jit(solution)/shard_map/ppermute | solution.py:968
  143.3 14.9 %collective-permute-start.17 = (bf16[4,14,32,128]{3,2,1,0:T(8,128)(2,1)S(1)}, bf16[4,14,32,128]{3,2,1,0:T(8,128)(2,1)S(1)}, u32[]{:S(2)}, u32[]{:S(2)}) collective-permute-start(bf16[4,14,32,128]{3,2,1,0:T(8,128)(2,1)S(1)} %get-tuple-element.108.rest_0_), channel_id=1, source_target_pairs={{1,3},{2,0},{0,1},{3,2},{5,7},{6,4},{4,5},{7,6},{9,11},{10,8},{8,9... | collective-permute-start | bytes 1376264 | tf_op jit(solution)/shard_map/ppermute | solution.py:946
  143.6 17.2 %collective-permute-start.19 = (bf16[4,14,32,128]{3,2,1,0:T(8,128)(2,1)S(1)}, bf16[4,14,32,128]{3,2,1,0:T(8,128)(2,1)S(1)}, u32[]{:S(2)}, u32[]{:S(2)}) collective-permute-start(bf16[4,14,32,128]{3,2,1,0:T(8,128)(2,1)S(1)} %get-tuple-element.115.rest_3_), channel_id=1, source_target_pairs={{0,2},{2,0},{1,3},{3,1},{4,6},{6,4},{5,7},{7,5},{8,10},{10,8},{9,1... | collective-permute-start | bytes 1376264 | tf_op jit(solution)/shard_map/ppermute | solution.py:947
  144.8 30.1 %collective-permute-start.23 = (bf16[4,32,32,128]{3,2,1,0:T(8,128)(2,1)S(1)}, bf16[4,32,32,128]{3,2,1,0:T(8,128)(2,1)S(1)}, u32[]{:S(2)}, u32[]{:S(2)}) collective-permute-start(bf16[4,32,32,128]{3,2,1,0:T(8,128)(2,1)S(1)} %get-tuple-element.123), channel_id=1, source_target_pairs={{0,4},{4,8},{8,12},{12,0},{1,5},{5,9},{9,13},{13,1},{2,6},{6,10},{... | collective-permute-start | bytes 3145736 | tf_op jit(solution)/shard_map/ppermute | solution.py:968
  160.8 10.0 %collective-permute-start.20 = (bf16[4,14,32,128]{3,2,1,0:T(8,128)(2,1)S(1)}, bf16[4,14,32,128]{3,2,1,0:T(8,128)(2,1)S(1)}, u32[]{:S(2)}, u32[]{:S(2)}) collective-permute-start(bf16[4,14,32,128]{3,2,1,0:T(8,128)(2,1)S(1)} %get-tuple-element.117.rest_5_), channel_id=1, source_target_pairs={{1,3},{2,0},{0,1},{3,2},{5,7},{6,4},{4,5},{7,6},{9,11},{10,8},{8,9... | collective-permute-start | bytes 1376264 | tf_op jit(solution)/shard_map/ppermute | solution.py:946
  161.3 16.9 %collective-permute-start.22 = (bf16[4,14,32,128]{3,2,1,0:T(8,128)(2,1)S(1)}, bf16[4,14,32,128]{3,2,1,0:T(8,128)(2,1)S(1)}, u32[]{:S(2)}, u32[]{:S(2)}) collective-permute-start(bf16[4,14,32,128]{3,2,1,0:T(8,128)(2,1)S(1)} %get-tuple-element.120.rest_8_), channel_id=1, source_target_pairs={{0,2},{2,0},{1,3},{3,1},{4,6},{6,4},{5,7},{7,5},{8,10},{10,8},{9,1... | collective-permute-start | bytes 1376264 | tf_op jit(solution)/shard_map/ppermute | solution.py:947
  174.9 24.9 %collective-permute-start.24 = (bf16[4,32,32,128]{3,2,1,0:T(8,128)(2,1)S(1)}, bf16[4,32,32,128]{3,2,1,0:T(8,128)(2,1)S(1)}, u32[]{:S(2)}, u32[]{:S(2)}) collective-permute-start(bf16[4,32,32,128]{3,2,1,0:T(8,128)(2,1)S(1)} %get-tuple-element.124), channel_id=1, source_target_pairs={{0,4},{4,8},{8,12},{12,0},{1,5},{5,9},{9,13},{13,1},{2,6},{6,10},{... | collective-permute-start | bytes 3145736 | tf_op jit(solution)/shard_map/ppermute | solution.py:968
  178.2 34.2 %collective-permute-start.27 = (bf16[8,18,32,128]{3,2,1,0:T(8,128)(2,1)S(1)}, bf16[8,18,32,128]{3,2,1,0:T(8,128)(2,1)S(1)}, u32[]{:S(2)}, u32[]{:S(2)}) collective-permute-start(bf16[8,18,32,128]{3,2,1,0:T(8,128)(2,1)S(1)} %get-tuple-element.132.rest_0_), channel_id=1, source_target_pairs={{1,3},{2,0},{0,1},{3,2},{5,7},{6,4},{4,5},{7,6},{9,11},{10,8},{8,9... | collective-permute-start | bytes 3538952 | tf_op jit(solution)/shard_map/ppermute | solution.py:946
  199.9 12.6 %collective-permute-start.26 = (bf16[4,14,32,128]{3,2,1,0:T(8,128)(2,1)S(1)}, bf16[4,14,32,128]{3,2,1,0:T(8,128)(2,1)S(1)}, u32[]{:S(2)}, u32[]{:S(2)}) collective-permute-start(bf16[4,14,32,128]{3,2,1,0:T(8,128)(2,1)S(1)} %get-tuple-element.127), channel_id=1, source_target_pairs={{0,12},{4,0},{8,4},{12,8},{1,13},{5,1},{9,5},{13,9},{2,14},{6,2},{... | collective-permute-start | bytes 1376264 | tf_op jit(solution)/shard_map/ppermute | solution.py:968
  202.2 45.2 %collective-permute-start.29 = (bf16[8,18,32,128]{3,2,1,0:T(8,128)(2,1)S(1)}, bf16[8,18,32,128]{3,2,1,0:T(8,128)(2,1)S(1)}, u32[]{:S(2)}, u32[]{:S(2)}) collective-permute-start(bf16[8,18,32,128]{3,2,1,0:T(8,128)(2,1)S(1)} %get-tuple-element.134.rest_3_), channel_id=1, source_target_pairs={{0,2},{2,0},{1,3},{3,1},{4,6},{6,4},{5,7},{7,5},{8,10},{10,8},{9,1... | collective-permute-start | bytes 3538952 | tf_op jit(solution)/shard_map/ppermute | solution.py:947
  212.4 34.9 %collective-permute-start.28 = (bf16[8,18,32,128]{3,2,1,0:T(8,128)(2,1)S(1)}, bf16[8,18,32,128]{3,2,1,0:T(8,128)(2,1)S(1)}, u32[]{:S(2)}, u32[]{:S(2)}) collective-permute-start(bf16[8,18,32,128]{3,2,1,0:T(8,128)(2,1)S(1)} %collective-permute-done.27.rest_1_), channel_id=1, source_target_pairs={{0,1},{3,2},{4,5},{7,6},{8,9},{11,10},{12,13},{15,14},{16,17},{19,... | collective-permute-start | bytes 3538952 | tf_op jit(solution)/shard_map/ppermute | solution.py:948
  225.0 27.1 %collective-permute-start.32 = (bf16[4,32,32,128]{3,2,1,0:T(8,128)(2,1)S(1)}, bf16[4,32,32,128]{3,2,1,0:T(8,128)(2,1)S(1)}, u32[]{:S(2)}, u32[]{:S(2)}) collective-permute-start(bf16[4,32,32,128]{3,2,1,0:T(8,128)(2,1)S(1)} %get-tuple-element.142.rest_0_), channel_id=1, source_target_pairs={{1,3},{2,0},{0,1},{3,2},{5,7},{6,4},{4,5},{7,6},{9,11},{10,8},{8,9... | collective-permute-start | bytes 3145736 | tf_op jit(solution)/shard_map/ppermute | solution.py:946
  225.0 22.4 %collective-permute-start.25 = (bf16[4,14,32,128]{3,2,1,0:T(8,128)(2,1)S(1)}, bf16[4,14,32,128]{3,2,1,0:T(8,128)(2,1)S(1)}, u32[]{:S(2)}, u32[]{:S(2)}) collective-permute-start(bf16[4,14,32,128]{3,2,1,0:T(8,128)(2,1)S(1)} %get-tuple-element.125), channel_id=1, source_target_pairs={{0,8},{4,12},{8,0},{12,4},{1,9},{5,13},{9,1},{13,5},{2,10},{6,14},... | collective-permute-start | bytes 1376264 | tf_op jit(solution)/shard_map/ppermute | solution.py:968
  229.3 34.6 %collective-permute-start.34 = (bf16[4,32,32,128]{3,2,1,0:T(8,128)(2,1)S(1)}, bf16[4,32,32,128]{3,2,1,0:T(8,128)(2,1)S(1)}, u32[]{:S(2)}, u32[]{:S(2)}) collective-permute-start(bf16[4,32,32,128]{3,2,1,0:T(8,128)(2,1)S(1)} %get-tuple-element.144.rest_3_), channel_id=1, source_target_pairs={{0,2},{2,0},{1,3},{3,1},{4,6},{6,4},{5,7},{7,5},{8,10},{10,8},{9,1... | collective-permute-start | bytes 3145736 | tf_op jit(solution)/shard_map/ppermute | solution.py:947
  252.1 11.8 %collective-permute-start.33 = (bf16[4,32,32,128]{3,2,1,0:T(8,128)(2,1)S(1)}, bf16[4,32,32,128]{3,2,1,0:T(8,128)(2,1)S(1)}, u32[]{:S(2)}, u32[]{:S(2)}) collective-permute-start(bf16[4,32,32,128]{3,2,1,0:T(8,128)(2,1)S(1)} %collective-permute-done.32.rest_1_), channel_id=1, source_target_pairs={{0,1},{3,2},{4,5},{7,6},{8,9},{11,10},{12,13},{15,14},{16,17},{19,... | collective-permute-start | bytes 3145736 | tf_op jit(solution)/shard_map/ppermute | solution.py:948
  254.4 16.7 %collective-permute-start.31 = (bf16[4,18,32,128]{3,2,1,0:T(8,128)(2,1)S(1)}, bf16[4,18,32,128]{3,2,1,0:T(8,128)(2,1)S(1)}, u32[]{:S(2)}, u32[]{:S(2)}) collective-permute-start(bf16[4,18,32,128]{3,2,1,0:T(8,128)(2,1)S(1)} %get-tuple-element.138), channel_id=1, source_target_pairs={{0,12},{4,0},{8,4},{12,8},{1,13},{5,1},{9,5},{13,9},{2,14},{6,2},{... | collective-permute-start | bytes 1769480 | tf_op jit(solution)/shard_map/ppermute | solution.py:968
  256.8 39.1 %collective-permute-start.30 = (bf16[4,18,32,128]{3,2,1,0:T(8,128)(2,1)S(1)}, bf16[4,18,32,128]{3,2,1,0:T(8,128)(2,1)S(1)}, u32[]{:S(2)}, u32[]{:S(2)}) collective-permute-start(bf16[4,18,32,128]{3,2,1,0:T(8,128)(2,1)S(1)} %get-tuple-element.136), channel_id=1, source_target_pairs={{0,8},{4,12},{8,0},{12,4},{1,9},{5,13},{9,1},{13,5},{2,10},{6,14},... | collective-permute-start | bytes 1769480 | tf_op jit(solution)/shard_map/ppermute | solution.py:968
  (29 other events, 494.3 us)

commit v13 on v12

--- a/solution.py
+++ b/solution.py
@@ -945,7 +945,7 @@
     both = ("chan", "sub")
     one = lax.ppermute(left, both, [(1, 3), (2, 0), (0, 1), (3, 2)])
     other = lax.ppermute(right, "chan", [(0, 1), (1, 0)])
-    two = lax.ppermute(one if over is None else after(one, over), both, [(0, 1), (3, 2)])
+    two = lax.ppermute(after(one, other if over is None else over), both, [(0, 1), (3, 2)])
     return [(left, one), (one, two)], [(right, right), (other, other)]
 
 
@@ -958,7 +958,7 @@
     near = [s for n, s in enumerate(near) if s not in near[:n]] + [0]
     layers = w_in.shape[0]
     current = pair
-    bands = [[12, 20], [14, 18]]
+    bands = [[16, 16], [20, 12]]
     chosen, place, mine = make_plan(ids, owners, slot_of, n_blk, far, slots, terms, capacity)
     in_order = jnp.repeat(jnp.arange(capacity, dtype=jnp.int32), 2)
     half = slots // 2
@@ -1005,7 +1005,7 @@
                 else:
                     ((other, _), _), ((one, _), (_, two)) = exchanged[-1]
                     left = after(left, other)
-                    right = after(right, one, two, chosen)
+                    right = after(right, one, two, made[-1])
                 exchanged = [exchange(left, right, list(by_shift.values())[-1] if by_shift else made[-1])]
                 ids = after(ids, *by_shift.values())
             made = banded_products(near, ids, chosen, exchanged, capacity, cols)
@@ -1020,7 +1020,9 @@
                 far_left, far_right = far_operands(
                     layer, ids, blocks, mine, sources, chains, wide, far, capacity, slots, hidden
                 )
-        far_exchanged = [exchange(far_left, far_right, made[-1])]
+        if layer % 2:
+            far_left, far_right = lax.optimization_barrier((far_left, far_right, made[-1]))[:2]
+        far_exchanged = [exchange(far_left, far_right, list(by_shift.values())[-1] if by_shift else made[-1])]
         (part,) = banded_products([0], ids, in_order, far_exchanged, capacity, cols)
         arrived.append((part, far, 0))
         last = layer == layers - 1

time: 306 us -> 301 us (0.984)
  starting transfers between devices: 58.1 us -> 81.5 us
  waiting for transfers between devices: 136 us -> 113 us
  local copies, waits for them, and re-layouts: 10.6 us -> 5.01 us
    ppermute x11, waiting for transfers between devices: 104 us -> 59.6 us  [over_blk(): lax.ppermute(value, 'blk', [(p, (p + shift) % n_blk) for p in range(n_blk)])]
    ppermute x4, starting transfers between devices: 11 us -> 36.4 us  [exchange_bands_incoming(): lax.ppermute(after(one, other if over is None else over), both, [(0, 1),...]
    ppermute x4, waiting for transfers between devices: 8.55 us -> 22.1 us  [exchange_bands_incoming(): one = lax.ppermute(left, both, [(1, 3), (2, 0), (0, 1), (3, 2)])]
    ppermute x4, waiting for transfers between devices: 8.26 us -> 17.2 us  [exchange_bands_incoming(): other = lax.ppermute(right, 'chan', [(0, 1), (1, 0)])]
    ppermute x11, starting transfers between devices: 18.8 us -> 14 us  [over_blk(): lax.ppermute(value, 'blk', [(p, (p + shift) % n_blk) for p in range(n_blk)])]
    unnamed x52 -> x38, local copies, waits for them, and re-layouts: 9.37 us -> 4.92 us
    pallas_call x6, Pallas kernels: 25.5 us -> 22.3 us  [banded_products(): pl.pallas_call(functools.partial(banded_kernel, shifts, capacity, tuple(p...]
    ppermute x4, starting transfers between devices: 8.37 us -> 11.5 us  [exchange_bands_outgoing(): other = lax.ppermute(left, 'sub', [(0, 1), (1, 0)])]
  transfers between devices with their start and end apart: 35 -> 35, of which waited for: 14 -> 18; matrix products, arithmetic and copies ran while one was open for 0% -> 0% of each run, Pallas kernels for 25% -> 24%
where the time goes in v13:
time: 301 us; the launch traced here: 297 us
  waiting for transfers between devices  113 us (38%)
  Pallas kernels  97.5 us (32%)
  starting transfers between devices  81.5 us (27%)
  local copies, waits for them, and re-layouts  5.01 us (2%)
    ppermute x11, waiting for transfers between devices, over_blk(): lax.ppermute(value, 'blk', [(p, (p + shift) % n_blk) for p in range(n_blk)])  59.6 us
    ppermute x4, starting transfers between devices, exchange_bands_incoming(): lax.ppermute(after(one, other if over is None else over), both, [(0, 1),...  36.4 us
    pallas_call x3, Pallas kernels, close_layer(): pl.pallas_call(functools.partial(close_kernel, *(layer, last, spots, 0 if...  35.3 us
    pallas_call x6, Pallas kernels, banded_products(): pl.pallas_call(functools.partial(banded_kernel, shifts, capacity, tuple(p...  22.3 us
    ppermute x4, waiting for transfers between devices, exchange_bands_incoming(): one = lax.ppermute(left, both, [(1, 3), (2, 0), (0, 1), (3, 2)])  22.1 us
    pallas_call x2, Pallas kernels, far_operands(): pl.pallas_call(functools.partial(far_kernel, layer, n_blk, far, lax.axis_...  20.6 us
    ppermute x4, waiting for transfers between devices, exchange_bands_incoming(): other = lax.ppermute(right, 'chan', [(0, 1), (1, 0)])  17.2 us
    pallas_call x2, Pallas kernels, open_operands(): pl.pallas_call(functools.partial(open_kernel, hidden, len(bands), lax.axi...  16.6 us
  transfers between devices with their start and end apart: 35, of which 18 were waited for; matrix products, arithmetic and copies ran while one was open for 0% of the time, Pallas kernels for 24%

profile of v13, /device:TPU:11, one launch (start us, length us, event | category | flops | bytes accessed | tf_op | source)
XLA Modules:
  0.0 297.4 jit_solution(13301514411049054717)
XLA Ops:
  3.3 8.3 %open_operands.2 = (f32[8,32,32,128]{3,2,1,0:T(8,128)S(1)}, bf16[4,16,32,128]{3,2,1,0:T(8,128)(2,1)S(1)}, bf16[8,16,32,128]{3,2,1,0:T(8,128)(2,1)S(1)}, bf16[4,1...) custom-call(s32[4]{0:T(128)S(1)} %pad_add_fusion.ids, s32[2,32]{1,0:T(2,128)S(1)} %bitcast.16, ...), custom_call_target="tpu_custom_call" | custom-call | flops 8589934592 | bytes 1048576 | tf_op jit(solution)/shard_map/open_operands/pallas_call | solution.py:567
  12.3 3.5 %collective-permute-start.1 = (bf16[4,16,32,128]{3,2,1,0:T(8,128)(2,1)S(1)}, bf16[4,16,32,128]{3,2,1,0:T(8,128)(2,1)S(1)}, u32[]{:S(2)}, u32[]{:S(2)}) collective-permute-start(bf16[4,16,32,128]{3,2,1,0:T(8,128)(2,1)S(1)} %get-tuple-element.80.rest_3_), channel_id=1, source_target_pairs={{0,2},{3,1},{1,0},{2,3},{4,6},{7,5},{5,4},{6,7},{8,10},{11,9},{9,8... | collective-permute-start | bytes 1572872 | tf_op jit(solution)/shard_map/ppermute | solution.py:939
  15.8 8.3 %open_operands.3 = (f32[8,32,32,128]{3,2,1,0:T(8,128)S(1)}, bf16[4,16,32,128]{3,2,1,0:T(8,128)(2,1)S(1)}, bf16[8,16,32,128]{3,2,1,0:T(8,128)(2,1)S(1)}, bf16[4,1...) custom-call(s32[4]{0:T(128)S(1)} %pad_add_fusion.ids, ...), custom_call_target="tpu_custom_call", output_to_operand_aliasing={{0}: (6, {}), {2}: (7, {}), {4}: (8, {})} | custom-call | flops 8589934592 | bytes 1048576 | tf_op jit(solution)/shard_map/open_operands/pallas_call | solution.py:567
  33.6 9.2 %collective-permute-done.4.rest_7_ = bf16[4,16,32,128]{3,2,1,0:T(8,128)(2,1)S(1)} collective-permute-done((bf16[4,16,32,128]{3,2,1,0:T(8,128)(2,1)S(1)}, bf16[4,16,32,128]{3,2,1,0:T(8,128)(2,1)S(1)}, u32[]{:S(2)}, u32[]{:S(2)}) %collective-permute-start.4) | collective-permute-done | bytes 524320 | tf_op jit(solution)/shard_map/ppermute | solution.py:939
  42.9 3.6 %banded_products.6 = (bf16[4,16,32,128]{3,2,1,0:T(8,128)(2,1)S(1)}, bf16[4,16,32,128]{3,2,1,0:T(8,128)(2,1)S(1)}, bf16[4,16,32,128]{3,2,1,0:T(8,128)(2,1)S(1)}) custom-call(s32[4]{0:T(128)S(1)} %pad_add_fusion.ids, s32[40]{0:T(128)S(1)} %get-tuple-element.78.chosen, bf16[4,16,32,128]{3,2,1,0:T(8,128)(2,1)S(1)} %collective-permute-done.rest_0_, ...), custom_call_target="tpu_custom_call" | custom-call | flops 402653184 | bytes 1 | tf_op jit(solution)/shard_map/banded_products/pallas_call | solution.py:771
  48.0 4.4 %collective-permute-start.10 = (bf16[8,16,32,128]{3,2,1,0:T(8,128)(2,1)S(1)}, bf16[8,16,32,128]{3,2,1,0:T(8,128)(2,1)S(1)}, u32[]{:S(2)}, u32[]{:S(2)}) collective-permute-start(bf16[8,16,32,128]{3,2,1,0:T(8,128)(2,1)S(1)} %get-tuple-element.98.rest_3_), channel_id=1, source_target_pairs={{0,2},{3,1},{1,0},{2,3},{4,6},{7,5},{5,4},{6,7},{8,10},{11,9},{9,8... | collective-permute-start | bytes 3145736 | tf_op jit(solution)/shard_map/ppermute | solution.py:939
  54.9 10.9 %far_operands.2 = (bf16[4,32,32,128]{3,2,1,0:T(8,128)(2,1)S(1)}, bf16[4,32,32,128]{3,2,1,0:T(8,128)(2,1)S(1)}) custom-call(s32[4]{0:T(128)S(1)} %pad_add_fusion.ids, s32[2,32]{1,0:T(2,128)S(1)} %bitcast.18, s32[10]{0:T(128)S(1)} %get-tuple-element.104.mine, bf16[8,32,32,128]{3,2,1,0:T(8,128)(2,1)} %collective-permute-done.6.rest_0_.rest_1_, ...), custom_call_target="tpu_custom_call" | custom-call | flops 8589934592 | bytes 1048576 | tf_op jit(solution)/shard_map/far_operands/pallas_call | solution.py:633
  65.9 9.2 %collective-permute-start.14 = (bf16[4,32,32,128]{3,2,1,0:T(8,128)(2,1)S(1)}, bf16[4,32,32,128]{3,2,1,0:T(8,128)(2,1)S(1)}, u32[]{:S(2)}, u32[]{:S(2)}) collective-permute-start(bf16[4,32,32,128]{3,2,1,0:T(8,128)(2,1)S(1)} %get-tuple-element.106.rest_1_), channel_id=1, source_target_pairs={{0,1},{1,0},{2,3},{3,2},{4,5},{5,4},{6,7},{7,6},{8,9},{9,8},{10,11... | collective-permute-start | bytes 3145736 | tf_op jit(solution)/shard_map/ppermute | solution.py:938
  76.8 11.9 %collective-permute-done.7.rest_0_ = bf16[4,16,32,128]{3,2,1,0:T(8,128)(2,1)S(1)} collective-permute-done((bf16[4,16,32,128]{3,2,1,0:T(8,128)(2,1)S(1)}, bf16[4,16,32,128]{3,2,1,0:T(8,128)(2,1)S(1)}, u32[]{:S(2)}, u32[]{:S(2)}) %collective-permute-start.7) | collective-permute-done | bytes 524320 | tf_op jit(solution)/shard_map/ppermute | solution.py:968
  89.9 3.5 %banded_products.7 = (bf16[4,16,32,128]{3,2,1,0:T(8,128)(2,1)}, bf16[4,16,32,128]{3,2,1,0:T(8,128)(2,1)}, bf16[4,16,32,128]{3,2,1,0:T(8,128)(2,1)S(1)}) custom-call(s32[4]{0:T(128)S(1)} %pad_add_fusion.ids, s32[40]{0:T(128)S(1)} %get-tuple-element.78.chosen, bf16[8,16,32,128]{3,2,1,0:T(8,128)(2,1)S(1)} %collective-permute-done.9.rest_0_, ...), custom_call_target="tpu_custom_call" | custom-call | flops 402653184 | bytes 1 | tf_op jit(solution)/shard_map/banded_products/pallas_call | solution.py:771
  98.0 4.4 %collective-permute-done.15.rest_2_ = bf16[4,32,32,128]{3,2,1,0:T(8,128)(2,1)} collective-permute-done((bf16[4,32,32,128]{3,2,1,0:T(8,128)(2,1)S(1)}, bf16[4,32,32,128]{3,2,1,0:T(8,128)(2,1)}, u32[]{:S(2)}, u32[]{:S(2)}) %collective-permute-start.15) | collective-permute-done | bytes 1048608 | tf_op jit(solution)/shard_map/ppermute | solution.py:939
  102.4 3.4 %banded_products.8.rest_6_ = bf16[4,32,32,128]{3,2,1,0:T(8,128)(2,1)S(1)} custom-call(s32[4]{0:T(128)S(1)} %pad_add_fusion.ids, s32[8]{0:T(128)S(1)} %reshape.9.chosen, bf16[4,32,32,128]{3,2,1,0:T(8,128)(2,1)S(1)} %collective-permute-done.14.rest_0_, bf16[4,32,32,128]{3,2,1,0:T(8,128)(2,1)S(1)} %get-tuple-element.106.rest_1_, ...), custom_call_target="tpu_custom_call" | custom-call | flops 268435456 | bytes 1 | tf_op jit(solution)/shard_map/banded_products/pallas_call | solution.py:771
  108.1 23.4 %collective-permute-done.12.rest_3_ = bf16[4,16,32,128]{3,2,1,0:T(8,128)(2,1)} collective-permute-done((bf16[4,16,32,128]{3,2,1,0:T(8,128)(2,1)}, bf16[4,16,32,128]{3,2,1,0:T(8,128)(2,1)}, u32[]{:S(2)}, u32[]{:S(2)}) %collective-permute-start.12) | collective-permute-done | bytes 524320 | tf_op jit(solution)/shard_map/ppermute | solution.py:968
  131.6 13.2 %close_layer.3 = (bf16[8,32,32,128]{3,2,1,0:T(8,128)(2,1)S(1)}, f32[8,32,32,128]{3,2,1,0:T(8,128)S(1)}, bf16[4,32,32,128]{3,2,1,0:T(8,128)(2,1)S(1)}, bf16[4,20,...) custom-call(s32[4]{0:T(128)S(1)} %pad_add_fusion.ids, ...), custom_call_target="tpu_custom_call" | custom-call | flops 8589934592 | bytes 1048576 | tf_op jit(solution)/shard_map/close_layer/pallas_call | solution.py:911
  146.3 13.2 %close_layer.4 = (bf16[8,32,32,128]{3,2,1,0:T(8,128)(2,1)S(1)}, f32[8,32,32,128]{3,2,1,0:T(8,128)S(1)}, bf16[4,32,32,128]{3,2,1,0:T(8,128)(2,1)S(1)}, bf16[4,20,...) custom-call(s32[4]{0:T(128)S(1)} %pad_add_fusion.ids, ...), custom_call_target="tpu_custom_call", output_to_operand_aliasing={{0}: (16, {}), {1}: (17, {}), {4}: (18, {}), {6}: (19, {})} | custom-call | flops 8589934592 | bytes 1048576 | tf_op jit(solution)/shard_map/close_layer/pallas_call | solution.py:911
  159.7 3.5 %collective-permute-start.18 = (bf16[4,20,32,128]{3,2,1,0:T(8,128)(2,1)S(1)}, bf16[4,20,32,128]{3,2,1,0:T(8,128)(2,1)S(1)}, u32[]{:S(2)}, u32[]{:S(2)}) collective-permute-start(bf16[4,20,32,128]{3,2,1,0:T(8,128)(2,1)S(1)} %collective-permute-done.17.rest_1_), channel_id=1, source_target_pairs={{0,1},{3,2},{4,5},{7,6},{8,9},{11,10},{12,13},{15,14},{16,17},{19,... | collective-permute-start | bytes 1966088 | tf_op jit(solution)/shard_map/ppermute | solution.py:948
  163.2 5.4 %collective-permute-done.19.rest_4_ = bf16[4,20,32,128]{3,2,1,0:T(8,128)(2,1)S(1)} collective-permute-done((bf16[4,20,32,128]{3,2,1,0:T(8,128)(2,1)S(1)}, bf16[4,20,32,128]{3,2,1,0:T(8,128)(2,1)S(1)}, u32[]{:S(2)}, u32[]{:S(2)}) %collective-permute-start.19) | collective-permute-done | bytes 655392 | tf_op jit(solution)/shard_map/ppermute | solution.py:947
  171.7 8.7 %collective-permute-done.20.rest_6_ = bf16[4,20,32,128]{3,2,1,0:T(8,128)(2,1)S(1)} collective-permute-done((bf16[4,20,32,128]{3,2,1,0:T(8,128)(2,1)S(1)}, bf16[4,20,32,128]{3,2,1,0:T(8,128)(2,1)S(1)}, u32[]{:S(2)}, u32[]{:S(2)}) %collective-permute-start.20) | collective-permute-done | bytes 655392 | tf_op jit(solution)/shard_map/ppermute | solution.py:946
  180.4 6.7 %collective-permute-start.21 = (bf16[4,20,32,128]{3,2,1,0:T(8,128)(2,1)S(1)}, bf16[4,20,32,128]{3,2,1,0:T(8,128)(2,1)S(1)}, u32[]{:S(2)}, u32[]{:S(2)}) collective-permute-start(bf16[4,20,32,128]{3,2,1,0:T(8,128)(2,1)S(1)} %collective-permute-done.20.rest_6_), channel_id=1, source_target_pairs={{0,1},{3,2},{4,5},{7,6},{8,9},{11,10},{12,13},{15,14},{16,17},{19,... | collective-permute-start | bytes 1966088 | tf_op jit(solution)/shard_map/ppermute | solution.py:948
  187.1 5.3 %collective-permute-done.22.rest_9_ = bf16[4,20,32,128]{3,2,1,0:T(8,128)(2,1)S(1)} collective-permute-done((bf16[4,20,32,128]{3,2,1,0:T(8,128)(2,1)S(1)}, bf16[4,20,32,128]{3,2,1,0:T(8,128)(2,1)S(1)}, u32[]{:S(2)}, u32[]{:S(2)}) %collective-permute-start.22) | collective-permute-done | bytes 655392 | tf_op jit(solution)/shard_map/ppermute | solution.py:947
  192.9 5.9 %banded_products.9 = (bf16[4,20,32,128]{3,2,1,0:T(8,128)(2,1)S(1)}, bf16[4,20,32,128]{3,2,1,0:T(8,128)(2,1)S(1)}, bf16[4,20,32,128]{3,2,1,0:T(8,128)(2,1)S(1)}) custom-call(s32[4]{0:T(128)S(1)} %pad_add_fusion.ids, s32[40]{0:T(128)S(1)} %get-tuple-element.78.chosen, bf16[4,20,32,128]{3,2,1,0:T(8,128)(2,1)S(1)} %get-tuple-element.110.rest_0_, ...), custom_call_target="tpu_custom_call" | custom-call | flops 503316480 | bytes 1 | tf_op jit(solution)/shard_map/banded_products/pallas_call | solution.py:771
  199.9 2.8 collective-permute-start.25
  203.2 9.4 %collective-permute-done.26.rest_1_ = bf16[4,20,32,128]{3,2,1,0:T(8,128)(2,1)S(1)} collective-permute-done((bf16[4,20,32,128]{3,2,1,0:T(8,128)(2,1)S(1)}, bf16[4,20,32,128]{3,2,1,0:T(8,128)(2,1)S(1)}, u32[]{:S(2)}, u32[]{:S(2)}) %collective-permute-start.26) | collective-permute-done | bytes 655392 | tf_op jit(solution)/shard_map/ppermute | solution.py:968
  212.6 22.4 %collective-permute-start.28 = (bf16[8,12,32,128]{3,2,1,0:T(8,128)(2,1)S(1)}, bf16[8,12,32,128]{3,2,1,0:T(8,128)(2,1)S(1)}, u32[]{:S(2)}, u32[]{:S(2)}) collective-permute-start(bf16[8,12,32,128]{3,2,1,0:T(8,128)(2,1)S(1)} %collective-permute-done.27.rest_1_), channel_id=1, source_target_pairs={{0,1},{3,2},{4,5},{7,6},{8,9},{11,10},{12,13},{15,14},{16,17},{19,... | collective-permute-start | bytes 2359304 | tf_op jit(solution)/shard_map/ppermute | solution.py:948
  235.0 9.6 %far_operands.3 = (bf16[4,32,32,128]{3,2,1,0:T(8,128)(2,1)S(1)}, bf16[4,32,32,128]{3,2,1,0:T(8,128)(2,1)S(1)}) custom-call(s32[4]{0:T(128)S(1)} %pad_add_fusion.ids, s32[2,32]{1,0:T(2,128)S(1)} %bitcast.21, s32[10]{0:T(128)S(1)} %get-tuple-element.104.mine, bf16[4,32,32,128]{3,2,1,0:T(8,128)(2,1)S(1)} %collective-permute-done.23.rest_0_.rest_2_, ...), custom_call_target="tpu_custom_call" | custom-call | flops 8589934592 | bytes 1048576 | tf_op jit(solution)/shard_map/far_operands/pallas_call | solution.py:633
  245.1 3.5 %banded_products.10 = (bf16[4,12,32,128]{3,2,1,0:T(8,128)(2,1)S(1)}, bf16[4,12,32,128]{3,2,1,0:T(8,128)(2,1)S(1)}, bf16[4,12,32,128]{3,2,1,0:T(8,128)(2,1)S(1)}) custom-call(s32[4]{0:T(128)S(1)} %pad_add_fusion.ids, s32[40]{0:T(128)S(1)} %get-tuple-element.78.chosen, bf16[8,12,32,128]{3,2,1,0:T(8,128)(2,1)S(1)} %get-tuple-element.134.rest_0_, ...), custom_call_target="tpu_custom_call" | custom-call | flops 301989888 | bytes 1 | tf_op jit(solution)/shard_map/banded_products/pallas_call | solution.py:771
  250.1 8.7 %collective-permute-done.31.rest_4_ = bf16[4,12,32,128]{3,2,1,0:T(8,128)(2,1)S(1)} collective-permute-done((bf16[4,12,32,128]{3,2,1,0:T(8,128)(2,1)S(1)}, bf16[4,12,32,128]{3,2,1,0:T(8,128)(2,1)S(1)}, u32[]{:S(2)}, u32[]{:S(2)}) %collective-permute-start.31) | collective-permute-done | bytes 393248 | tf_op jit(solution)/shard_map/ppermute | solution.py:968
  258.9 12.8 %collective-permute-done.32.rest_1_ = bf16[4,32,32,128]{3,2,1,0:T(8,128)(2,1)S(1)} collective-permute-done((bf16[4,32,32,128]{3,2,1,0:T(8,128)(2,1)S(1)}, bf16[4,32,32,128]{3,2,1,0:T(8,128)(2,1)S(1)}, u32[]{:S(2)}, u32[]{:S(2)}) %collective-permute-start.32) | collective-permute-done | bytes 1048608 | tf_op jit(solution)/shard_map/ppermute | solution.py:946
  271.7 3.8 %collective-permute-start.33 = (bf16[4,32,32,128]{3,2,1,0:T(8,128)(2,1)S(1)}, bf16[4,32,32,128]{3,2,1,0:T(8,128)(2,1)S(1)}, u32[]{:S(2)}, u32[]{:S(2)}) collective-permute-start(bf16[4,32,32,128]{3,2,1,0:T(8,128)(2,1)S(1)} %collective-permute-done.32.rest_1_), channel_id=1, source_target_pairs={{0,1},{3,2},{4,5},{7,6},{8,9},{11,10},{12,13},{15,14},{16,17},{19,... | collective-permute-start | bytes 3145736 | tf_op jit(solution)/shard_map/ppermute | solution.py:948
  275.5 3.2 %collective-permute-start.30 = (bf16[4,12,32,128]{3,2,1,0:T(8,128)(2,1)S(1)}, bf16[4,12,32,128]{3,2,1,0:T(8,128)(2,1)S(1)}, u32[]{:S(2)}, u32[]{:S(2)}) collective-permute-start(bf16[4,12,32,128]{3,2,1,0:T(8,128)(2,1)S(1)} %get-tuple-element.138), channel_id=1, source_target_pairs={{0,8},{4,12},{8,0},{12,4},{1,9},{5,13},{9,1},{13,5},{2,10},{6,14},... | collective-permute-start | bytes 1179656 | tf_op jit(solution)/shard_map/ppermute | solution.py:968
  278.6 6.4 %collective-permute-done.34.rest_4_ = bf16[4,32,32,128]{3,2,1,0:T(8,128)(2,1)S(1)} collective-permute-done((bf16[4,32,32,128]{3,2,1,0:T(8,128)(2,1)S(1)}, bf16[4,32,32,128]{3,2,1,0:T(8,128)(2,1)S(1)}, u32[]{:S(2)}, u32[]{:S(2)}) %collective-permute-start.34) | collective-permute-done | bytes 1048608 | tf_op jit(solution)/shard_map/ppermute | solution.py:947
  288.4 8.8 %close_layer.5 = bf16[8,32,32,128]{3,2,1,0:T(8,128)(2,1)} custom-call(s32[4]{0:T(128)S(1)} %pad_add_fusion.ids, s32[2,32]{1,0:T(2,128)S(1)} %bitcast.22, s32[16]{0:T(128)S(1)} %get-tuple-element.93.place, bf16[4,20,32,128]{3,2,1,0:T(8,128)(2,1)S(1)} %collective-permute-done.25.rest_0_, bf16[4,20,32,128]{3,2,1,0:T(8,128)(2,1)S(1)} %collective-permute-done.26.rest_1_, ...), custom_call_target="tpu_custom_call" | custom-call | flops 8589934592 | bytes 1048576 | tf_op jit(solution)/shard_map/close_layer/pallas_call | solution.py:911
  (95 shorter events, 39.3 us)
Async XLA Ops:
  0.0 52.5 %collective-permute-start.6 = (bf16[8,32,32,128]{3,2,1,0:T(8,128)(2,1)}, bf16[8,32,32,128]{3,2,1,0:T(8,128)(2,1)}, u32[]{:S(2)}, u32[]{:S(2)}) collective-permute-start(bf16[8,32,32,128]{3,2,1,0:T(8,128)(2,1)} %rest_7_.3), channel_id=1, source_target_pairs={{0,4},{4,8},{8,12},{12,0},{1,5},{5,9},{9,13},{13,1},{2,6},{6,10},{... | collective-permute-start | bytes 6291464 | tf_op jit(solution)/shard_map/ppermute | solution.py:968
  11.6 14.6 %collective-permute-start.2 = (bf16[4,16,32,128]{3,2,1,0:T(8,128)(2,1)S(1)}, bf16[4,16,32,128]{3,2,1,0:T(8,128)(2,1)S(1)}, u32[]{:S(2)}, u32[]{:S(2)}) collective-permute-start(bf16[4,16,32,128]{3,2,1,0:T(8,128)(2,1)S(1)} %get-tuple-element.80.rest_3_), channel_id=1, source_target_pairs={{1,2},{2,1},{5,6},{6,5},{9,10},{10,9},{13,14},{14,13},{17,18},{18,... | collective-permute-start | bytes 1572872 | tf_op jit(solution)/shard_map/ppermute | solution.py:940
  12.3 14.1 %collective-permute-start.1 = (bf16[4,16,32,128]{3,2,1,0:T(8,128)(2,1)S(1)}, bf16[4,16,32,128]{3,2,1,0:T(8,128)(2,1)S(1)}, u32[]{:S(2)}, u32[]{:S(2)}) collective-permute-start(bf16[4,16,32,128]{3,2,1,0:T(8,128)(2,1)S(1)} %get-tuple-element.80.rest_3_), channel_id=1, source_target_pairs={{0,2},{3,1},{1,0},{2,3},{4,6},{7,5},{5,4},{6,7},{8,10},{11,9},{9,8... | collective-permute-start | bytes 1572872 | tf_op jit(solution)/shard_map/ppermute | solution.py:939
  15.8 10.3 %collective-permute-start = (bf16[4,16,32,128]{3,2,1,0:T(8,128)(2,1)S(1)}, bf16[4,16,32,128]{3,2,1,0:T(8,128)(2,1)S(1)}, u32[]{:S(2)}, u32[]{:S(2)}) collective-permute-start(bf16[4,16,32,128]{3,2,1,0:T(8,128)(2,1)S(1)} %get-tuple-element.79.rest_1_), channel_id=1, source_target_pairs={{0,1},{1,0},{2,3},{3,2},{4,5},{5,4},{6,7},{7,6},{8,9},{9,8},{10,11... | collective-permute-start | bytes 1572872 | tf_op jit(solution)/shard_map/ppermute | solution.py:938
  29.3 13.5 %collective-permute-start.4 = (bf16[4,16,32,128]{3,2,1,0:T(8,128)(2,1)S(1)}, bf16[4,16,32,128]{3,2,1,0:T(8,128)(2,1)S(1)}, u32[]{:S(2)}, u32[]{:S(2)}) collective-permute-start(bf16[4,16,32,128]{3,2,1,0:T(8,128)(2,1)S(1)} %get-tuple-element.87.rest_8_), channel_id=1, source_target_pairs={{0,2},{3,1},{1,0},{2,3},{4,6},{7,5},{5,4},{6,7},{8,10},{11,9},{9,8... | collective-permute-start | bytes 1572872 | tf_op jit(solution)/shard_map/ppermute | solution.py:939
  47.3 18.6 %collective-permute-start.11 = (bf16[8,16,32,128]{3,2,1,0:T(8,128)(2,1)S(1)}, bf16[8,16,32,128]{3,2,1,0:T(8,128)(2,1)S(1)}, u32[]{:S(2)}, u32[]{:S(2)}) collective-permute-start(bf16[8,16,32,128]{3,2,1,0:T(8,128)(2,1)S(1)} %get-tuple-element.98.rest_3_), channel_id=1, source_target_pairs={{1,2},{2,1},{5,6},{6,5},{9,10},{10,9},{13,14},{14,13},{17,18},{18,... | collective-permute-start | bytes 3145736 | tf_op jit(solution)/shard_map/ppermute | solution.py:940
  48.0 41.9 %collective-permute-start.10 = (bf16[8,16,32,128]{3,2,1,0:T(8,128)(2,1)S(1)}, bf16[8,16,32,128]{3,2,1,0:T(8,128)(2,1)S(1)}, u32[]{:S(2)}, u32[]{:S(2)}) collective-permute-start(bf16[8,16,32,128]{3,2,1,0:T(8,128)(2,1)S(1)} %get-tuple-element.98.rest_3_), channel_id=1, source_target_pairs={{0,2},{3,1},{1,0},{2,3},{4,6},{7,5},{5,4},{6,7},{8,10},{11,9},{9,8... | collective-permute-start | bytes 3145736 | tf_op jit(solution)/shard_map/ppermute | solution.py:939
  52.5 37.4 %collective-permute-start.9 = (bf16[8,16,32,128]{3,2,1,0:T(8,128)(2,1)S(1)}, bf16[8,16,32,128]{3,2,1,0:T(8,128)(2,1)S(1)}, u32[]{:S(2)}, u32[]{:S(2)}) collective-permute-start(bf16[8,16,32,128]{3,2,1,0:T(8,128)(2,1)S(1)} %get-tuple-element.96.rest_1_), channel_id=1, source_target_pairs={{0,1},{1,0},{2,3},{3,2},{4,5},{5,4},{6,7},{7,6},{8,9},{9,8},{10,11... | collective-permute-start | bytes 3145736 | tf_op jit(solution)/shard_map/ppermute | solution.py:938
  52.5 22.7 %collective-permute-start.8 = (bf16[4,16,32,128]{3,2,1,0:T(8,128)(2,1)S(1)}, bf16[4,16,32,128]{3,2,1,0:T(8,128)(2,1)S(1)}, u32[]{:S(2)}, u32[]{:S(2)}) collective-permute-start(bf16[4,16,32,128]{3,2,1,0:T(8,128)(2,1)S(1)} %get-tuple-element.91), channel_id=1, source_target_pairs={{0,12},{4,0},{8,4},{12,8},{1,13},{5,1},{9,5},{13,9},{2,14},{6,2},{... | collective-permute-start | bytes 1572872 | tf_op jit(solution)/shard_map/ppermute | solution.py:968
  52.6 36.0 %collective-permute-start.7 = (bf16[4,16,32,128]{3,2,1,0:T(8,128)(2,1)S(1)}, bf16[4,16,32,128]{3,2,1,0:T(8,128)(2,1)S(1)}, u32[]{:S(2)}, u32[]{:S(2)}) collective-permute-start(bf16[4,16,32,128]{3,2,1,0:T(8,128)(2,1)S(1)} %get-tuple-element.89), channel_id=1, source_target_pairs={{0,8},{4,12},{8,0},{12,4},{1,9},{5,13},{9,1},{13,5},{2,10},{6,14},... | collective-permute-start | bytes 1572872 | tf_op jit(solution)/shard_map/ppermute | solution.py:968
  65.9 32.1 %collective-permute-start.14 = (bf16[4,32,32,128]{3,2,1,0:T(8,128)(2,1)S(1)}, bf16[4,32,32,128]{3,2,1,0:T(8,128)(2,1)S(1)}, u32[]{:S(2)}, u32[]{:S(2)}) collective-permute-start(bf16[4,32,32,128]{3,2,1,0:T(8,128)(2,1)S(1)} %get-tuple-element.106.rest_1_), channel_id=1, source_target_pairs={{0,1},{1,0},{2,3},{3,2},{4,5},{5,4},{6,7},{7,6},{8,9},{9,8},{10,11... | collective-permute-start | bytes 3145736 | tf_op jit(solution)/shard_map/ppermute | solution.py:938
  75.1 22.9 %collective-permute-start.16 = (bf16[4,32,32,128]{3,2,1,0:T(8,128)(2,1)S(1)}, bf16[4,32,32,128]{3,2,1,0:T(8,128)(2,1)}, u32[]{:S(2)}, u32[]{:S(2)}) collective-permute-start(bf16[4,32,32,128]{3,2,1,0:T(8,128)(2,1)S(1)} %get-tuple-element.107.rest_3_), channel_id=1, source_target_pairs={{1,2},{2,1},{5,6},{6,5},{9,10},{10,9},{13,14},{14,13},{17,18},{18,... | collective-permute-start | bytes 3145736 | tf_op jit(solution)/shard_map/ppermute | solution.py:940
  88.6 13.7 %collective-permute-start.15 = (bf16[4,32,32,128]{3,2,1,0:T(8,128)(2,1)S(1)}, bf16[4,32,32,128]{3,2,1,0:T(8,128)(2,1)}, u32[]{:S(2)}, u32[]{:S(2)}) collective-permute-start(bf16[4,32,32,128]{3,2,1,0:T(8,128)(2,1)S(1)} %get-tuple-element.107.rest_3_), channel_id=1, source_target_pairs={{0,2},{3,1},{1,0},{2,3},{4,6},{7,5},{5,4},{6,7},{8,10},{11,9},{9,8... | collective-permute-start | bytes 3145736 | tf_op jit(solution)/shard_map/ppermute | solution.py:939
  94.2 14.0 %collective-permute-start.13 = (bf16[4,16,32,128]{3,2,1,0:T(8,128)(2,1)}, bf16[4,16,32,128]{3,2,1,0:T(8,128)(2,1)}, u32[]{:S(2)}, u32[]{:S(2)}) collective-permute-start(bf16[4,16,32,128]{3,2,1,0:T(8,128)(2,1)} %get-tuple-element.102), channel_id=1, source_target_pairs={{0,12},{4,0},{8,4},{12,8},{1,13},{5,1},{9,5},{13,9},{2,14},{6,2},{... | collective-permute-start | bytes 1572872 | tf_op jit(solution)/shard_map/ppermute | solution.py:968
  95.2 36.4 %collective-permute-start.12 = (bf16[4,16,32,128]{3,2,1,0:T(8,128)(2,1)}, bf16[4,16,32,128]{3,2,1,0:T(8,128)(2,1)}, u32[]{:S(2)}, u32[]{:S(2)}) collective-permute-start(bf16[4,16,32,128]{3,2,1,0:T(8,128)(2,1)} %get-tuple-element.100), channel_id=1, source_target_pairs={{0,8},{4,12},{8,0},{12,4},{1,9},{5,13},{9,1},{13,5},{2,10},{6,14},... | collective-permute-start | bytes 1572872 | tf_op jit(solution)/shard_map/ppermute | solution.py:968
  144.8 14.8 %collective-permute-start.17 = (bf16[4,20,32,128]{3,2,1,0:T(8,128)(2,1)S(1)}, bf16[4,20,32,128]{3,2,1,0:T(8,128)(2,1)S(1)}, u32[]{:S(2)}, u32[]{:S(2)}) collective-permute-start(bf16[4,20,32,128]{3,2,1,0:T(8,128)(2,1)S(1)} %get-tuple-element.110.rest_0_), channel_id=1, source_target_pairs={{1,3},{2,0},{0,1},{3,2},{5,7},{6,4},{4,5},{7,6},{9,11},{10,8},{8,9... | collective-permute-start | bytes 1966088 | tf_op jit(solution)/shard_map/ppermute | solution.py:946
  145.0 23.6 %collective-permute-start.19 = (bf16[4,20,32,128]{3,2,1,0:T(8,128)(2,1)S(1)}, bf16[4,20,32,128]{3,2,1,0:T(8,128)(2,1)S(1)}, u32[]{:S(2)}, u32[]{:S(2)}) collective-permute-start(bf16[4,20,32,128]{3,2,1,0:T(8,128)(2,1)S(1)} %get-tuple-element.117.rest_3_), channel_id=1, source_target_pairs={{0,2},{2,0},{1,3},{3,1},{4,6},{6,4},{5,7},{7,5},{8,10},{10,8},{9,1... | collective-permute-start | bytes 1966088 | tf_op jit(solution)/shard_map/ppermute | solution.py:947
  146.3 24.8 %collective-permute-start.23 = (bf16[4,32,32,128]{3,2,1,0:T(8,128)(2,1)S(1)}, bf16[4,32,32,128]{3,2,1,0:T(8,128)(2,1)S(1)}, u32[]{:S(2)}, u32[]{:S(2)}) collective-permute-start(bf16[4,32,32,128]{3,2,1,0:T(8,128)(2,1)S(1)} %get-tuple-element.125), channel_id=1, source_target_pairs={{0,4},{4,8},{8,12},{12,0},{1,5},{5,9},{9,13},{13,1},{2,6},{6,10},{... | collective-permute-start | bytes 3145736 | tf_op jit(solution)/shard_map/ppermute | solution.py:968
  159.7 12.0 %collective-permute-start.18 = (bf16[4,20,32,128]{3,2,1,0:T(8,128)(2,1)S(1)}, bf16[4,20,32,128]{3,2,1,0:T(8,128)(2,1)S(1)}, u32[]{:S(2)}, u32[]{:S(2)}) collective-permute-start(bf16[4,20,32,128]{3,2,1,0:T(8,128)(2,1)S(1)} %collective-permute-done.17.rest_1_), channel_id=1, source_target_pairs={{0,1},{3,2},{4,5},{7,6},{8,9},{11,10},{12,13},{15,14},{16,17},{19,... | collective-permute-start | bytes 1966088 | tf_op jit(solution)/shard_map/ppermute | solution.py:948
  168.6 11.8 %collective-permute-start.20 = (bf16[4,20,32,128]{3,2,1,0:T(8,128)(2,1)S(1)}, bf16[4,20,32,128]{3,2,1,0:T(8,128)(2,1)S(1)}, u32[]{:S(2)}, u32[]{:S(2)}) collective-permute-start(bf16[4,20,32,128]{3,2,1,0:T(8,128)(2,1)S(1)} %get-tuple-element.119.rest_5_), channel_id=1, source_target_pairs={{1,3},{2,0},{0,1},{3,2},{5,7},{6,4},{4,5},{7,6},{9,11},{10,8},{8,9... | collective-permute-start | bytes 1966088 | tf_op jit(solution)/shard_map/ppermute | solution.py:946
  171.1 27.7 %collective-permute-start.24 = (bf16[4,32,32,128]{3,2,1,0:T(8,128)(2,1)S(1)}, bf16[4,32,32,128]{3,2,1,0:T(8,128)(2,1)S(1)}, u32[]{:S(2)}, u32[]{:S(2)}) collective-permute-start(bf16[4,32,32,128]{3,2,1,0:T(8,128)(2,1)S(1)} %get-tuple-element.126), channel_id=1, source_target_pairs={{0,4},{4,8},{8,12},{12,0},{1,5},{5,9},{9,13},{13,1},{2,6},{6,10},{... | collective-permute-start | bytes 3145736 | tf_op jit(solution)/shard_map/ppermute | solution.py:968
  171.7 20.7 %collective-permute-start.22 = (bf16[4,20,32,128]{3,2,1,0:T(8,128)(2,1)S(1)}, bf16[4,20,32,128]{3,2,1,0:T(8,128)(2,1)S(1)}, u32[]{:S(2)}, u32[]{:S(2)}) collective-permute-start(bf16[4,20,32,128]{3,2,1,0:T(8,128)(2,1)S(1)} %get-tuple-element.122.rest_8_), channel_id=1, source_target_pairs={{0,2},{2,0},{1,3},{3,1},{4,6},{6,4},{5,7},{7,5},{8,10},{10,8},{9,1... | collective-permute-start | bytes 1966088 | tf_op jit(solution)/shard_map/ppermute | solution.py:947
  180.4 12.0 %collective-permute-start.21 = (bf16[4,20,32,128]{3,2,1,0:T(8,128)(2,1)S(1)}, bf16[4,20,32,128]{3,2,1,0:T(8,128)(2,1)S(1)}, u32[]{:S(2)}, u32[]{:S(2)}) collective-permute-start(bf16[4,20,32,128]{3,2,1,0:T(8,128)(2,1)S(1)} %collective-permute-done.20.rest_6_), channel_id=1, source_target_pairs={{0,1},{3,2},{4,5},{7,6},{8,9},{11,10},{12,13},{15,14},{16,17},{19,... | collective-permute-start | bytes 1966088 | tf_op jit(solution)/shard_map/ppermute | solution.py:948
  192.4 10.8 %collective-permute-start.27 = (bf16[8,12,32,128]{3,2,1,0:T(8,128)(2,1)S(1)}, bf16[8,12,32,128]{3,2,1,0:T(8,128)(2,1)S(1)}, u32[]{:S(2)}, u32[]{:S(2)}) collective-permute-start(bf16[8,12,32,128]{3,2,1,0:T(8,128)(2,1)S(1)} %get-tuple-element.134.rest_0_), channel_id=1, source_target_pairs={{1,3},{2,0},{0,1},{3,2},{5,7},{6,4},{4,5},{7,6},{9,11},{10,8},{8,9... | collective-permute-start | bytes 2359304 | tf_op jit(solution)/shard_map/ppermute | solution.py:946
  198.8 13.8 %collective-permute-start.26 = (bf16[4,20,32,128]{3,2,1,0:T(8,128)(2,1)S(1)}, bf16[4,20,32,128]{3,2,1,0:T(8,128)(2,1)S(1)}, u32[]{:S(2)}, u32[]{:S(2)}) collective-permute-start(bf16[4,20,32,128]{3,2,1,0:T(8,128)(2,1)S(1)} %get-tuple-element.129), channel_id=1, source_target_pairs={{0,12},{4,0},{8,4},{12,8},{1,13},{5,1},{9,5},{13,9},{2,14},{6,2},{... | collective-permute-start | bytes 1966088 | tf_op jit(solution)/shard_map/ppermute | solution.py:968
  199.3 45.8 %collective-permute-start.29 = (bf16[8,12,32,128]{3,2,1,0:T(8,128)(2,1)S(1)}, bf16[8,12,32,128]{3,2,1,0:T(8,128)(2,1)S(1)}, u32[]{:S(2)}, u32[]{:S(2)}) collective-permute-start(bf16[8,12,32,128]{3,2,1,0:T(8,128)(2,1)S(1)} %get-tuple-element.136.rest_3_), channel_id=1, source_target_pairs={{0,2},{2,0},{1,3},{3,1},{4,6},{6,4},{5,7},{7,5},{8,10},{10,8},{9,1... | collective-permute-start | bytes 2359304 | tf_op jit(solution)/shard_map/ppermute | solution.py:947
  199.9 45.2 %collective-permute-start.25 = (bf16[4,20,32,128]{3,2,1,0:T(8,128)(2,1)S(1)}, bf16[4,20,32,128]{3,2,1,0:T(8,128)(2,1)S(1)}, u32[]{:S(2)}, u32[]{:S(2)}) collective-permute-start(bf16[4,20,32,128]{3,2,1,0:T(8,128)(2,1)S(1)} %get-tuple-element.127), channel_id=1, source_target_pairs={{0,8},{4,12},{8,0},{12,4},{1,9},{5,13},{9,1},{13,5},{2,10},{6,14},... | collective-permute-start | bytes 1966088 | tf_op jit(solution)/shard_map/ppermute | solution.py:968
  212.6 32.5 %collective-permute-start.28 = (bf16[8,12,32,128]{3,2,1,0:T(8,128)(2,1)S(1)}, bf16[8,12,32,128]{3,2,1,0:T(8,128)(2,1)S(1)}, u32[]{:S(2)}, u32[]{:S(2)}) collective-permute-start(bf16[8,12,32,128]{3,2,1,0:T(8,128)(2,1)S(1)} %collective-permute-done.27.rest_1_), channel_id=1, source_target_pairs={{0,1},{3,2},{4,5},{7,6},{8,9},{11,10},{12,13},{15,14},{16,17},{19,... | collective-permute-start | bytes 2359304 | tf_op jit(solution)/shard_map/ppermute | solution.py:948
  248.7 23.0 %collective-permute-start.32 = (bf16[4,32,32,128]{3,2,1,0:T(8,128)(2,1)S(1)}, bf16[4,32,32,128]{3,2,1,0:T(8,128)(2,1)S(1)}, u32[]{:S(2)}, u32[]{:S(2)}) collective-permute-start(bf16[4,32,32,128]{3,2,1,0:T(8,128)(2,1)S(1)} %get-tuple-element.146.rest_0_), channel_id=1, source_target_pairs={{1,3},{2,0},{0,1},{3,2},{5,7},{6,4},{4,5},{7,6},{9,11},{10,8},{8,9... | collective-permute-start | bytes 3145736 | tf_op jit(solution)/shard_map/ppermute | solution.py:946
  249.2 35.9 %collective-permute-start.34 = (bf16[4,32,32,128]{3,2,1,0:T(8,128)(2,1)S(1)}, bf16[4,32,32,128]{3,2,1,0:T(8,128)(2,1)S(1)}, u32[]{:S(2)}, u32[]{:S(2)}) collective-permute-start(bf16[4,32,32,128]{3,2,1,0:T(8,128)(2,1)S(1)} %get-tuple-element.148.rest_3_), channel_id=1, source_target_pairs={{0,2},{2,0},{1,3},{3,1},{4,6},{6,4},{5,7},{7,5},{8,10},{10,8},{9,1... | collective-permute-start | bytes 3145736 | tf_op jit(solution)/shard_map/ppermute | solution.py:947
  271.7 13.4 %collective-permute-start.33 = (bf16[4,32,32,128]{3,2,1,0:T(8,128)(2,1)S(1)}, bf16[4,32,32,128]{3,2,1,0:T(8,128)(2,1)S(1)}, u32[]{:S(2)}, u32[]{:S(2)}) collective-permute-start(bf16[4,32,32,128]{3,2,1,0:T(8,128)(2,1)S(1)} %collective-permute-done.32.rest_1_), channel_id=1, source_target_pairs={{0,1},{3,2},{4,5},{7,6},{8,9},{11,10},{12,13},{15,14},{16,17},{19,... | collective-permute-start | bytes 3145736 | tf_op jit(solution)/shard_map/ppermute | solution.py:948
  275.5 12.9 %collective-permute-start.30 = (bf16[4,12,32,128]{3,2,1,0:T(8,128)(2,1)S(1)}, bf16[4,12,32,128]{3,2,1,0:T(8,128)(2,1)S(1)}, u32[]{:S(2)}, u32[]{:S(2)}) collective-permute-start(bf16[4,12,32,128]{3,2,1,0:T(8,128)(2,1)S(1)} %get-tuple-element.138), channel_id=1, source_target_pairs={{0,8},{4,12},{8,0},{12,4},{1,9},{5,13},{9,1},{13,5},{2,10},{6,14},... | collective-permute-start | bytes 1179656 | tf_op jit(solution)/shard_map/ppermute | solution.py:968
  (22 other events, 323.4 us)

commit v14 on v13

--- a/solution.py
+++ b/solution.py
@@ -1006,7 +1006,7 @@
                     ((other, _), _), ((one, _), (_, two)) = exchanged[-1]
                     left = after(left, other)
                     right = after(right, one, two, made[-1])
-                exchanged = [exchange(left, right, list(by_shift.values())[-1] if by_shift else made[-1])]
+                exchanged = [exchange(left, right, made[-1])]
                 ids = after(ids, *by_shift.values())
             made = banded_products(near, ids, chosen, exchanged, capacity, cols)
             start = sum(bands[layer][:chunk])
@@ -1020,8 +1020,6 @@
                 far_left, far_right = far_operands(
                     layer, ids, blocks, mine, sources, chains, wide, far, capacity, slots, hidden
                 )
-        if layer % 2:
-            far_left, far_right = lax.optimization_barrier((far_left, far_right, made[-1]))[:2]
         far_exchanged = [exchange(far_left, far_right, list(by_shift.values())[-1] if by_shift else made[-1])]
         (part,) = banded_products([0], ids, in_order, far_exchanged, capacity, cols)
         arrived.append((part, far, 0))

time: 301 us -> 305 us (1.013)
  waiting for transfers between devices: 113 us -> 141 us
  starting transfers between devices: 81.5 us -> 58 us
    ppermute x11, waiting for transfers between devices: 59.6 us -> 96.3 us  [over_blk(): lax.ppermute(value, 'blk', [(p, (p + shift) % n_blk) for p in range(n_blk)])]
    ppermute x4, starting transfers between devices: 36.4 us -> 13.5 us  [exchange_bands_incoming(): lax.ppermute(after(one, other if over is None else over), both, [(0, 1),...]
    ppermute x4, waiting for transfers between devices: 22.1 us -> 12.8 us  [exchange_bands_incoming(): one = lax.ppermute(left, both, [(1, 3), (2, 0), (0, 1), (3, 2)])]
  transfers between devices with their start and end apart: 35 -> 35, of which waited for: 18 -> 16; matrix products, arithmetic and copies ran while one was open for 0% -> 0% of each run, Pallas kernels for 24% -> 25%
where the time goes in v14:
time: 305 us; the launch traced here: 303 us
  waiting for transfers between devices  141 us (46%)
  Pallas kernels  97.5 us (32%)
  starting transfers between devices  58 us (19%)
  local copies, waits for them, and re-layouts  5.01 us (2%)
    ppermute x11, waiting for transfers between devices, over_blk(): lax.ppermute(value, 'blk', [(p, (p + shift) % n_blk) for p in range(n_blk)])  96.3 us
    pallas_call x3, Pallas kernels, close_layer(): pl.pallas_call(functools.partial(close_kernel, *(layer, last, spots, 0 if...  35.3 us
    pallas_call x6, Pallas kernels, banded_products(): pl.pallas_call(functools.partial(banded_kernel, shifts, capacity, tuple(p...  22.3 us
    pallas_call x2, Pallas kernels, far_operands(): pl.pallas_call(functools.partial(far_kernel, layer, n_blk, far, lax.axis_...  20.6 us
    ppermute x4, waiting for transfers between devices, exchange_bands_incoming(): other = lax.ppermute(right, 'chan', [(0, 1), (1, 0)])  18.4 us
    pallas_call x2, Pallas kernels, open_operands(): pl.pallas_call(functools.partial(open_kernel, hidden, len(bands), lax.axi...  16.6 us
    ppermute x4, waiting for transfers between devices, exchange_bands_outgoing(): one = lax.ppermute(right, both, [(0, 2), (3, 1), (1, 0), (2, 3)])  13.8 us
    ppermute x4, starting transfers between devices, exchange_bands_incoming(): lax.ppermute(after(one, other if over is None else over), both, [(0, 1),...  13.5 us
  transfers between devices with their start and end apart: 35, of which 16 were waited for; matrix products, arithmetic and copies ran while one was open for 0% of the time, Pallas kernels for 25%

profile of v14, /device:TPU:11, one launch (start us, length us, event | category | flops | bytes accessed | tf_op | source)
XLA Modules:
  0.0 302.5 jit_solution(14421931405032967126)
XLA Ops:
  3.3 8.3 %open_operands.2 = (f32[8,32,32,128]{3,2,1,0:T(8,128)S(1)}, bf16[4,16,32,128]{3,2,1,0:T(8,128)(2,1)S(1)}, bf16[8,16,32,128]{3,2,1,0:T(8,128)(2,1)S(1)}, bf16[4,1...) custom-call(s32[4]{0:T(128)S(1)} %pad_add_fusion.ids, s32[2,32]{1,0:T(2,128)S(1)} %bitcast.16, ...), custom_call_target="tpu_custom_call" | custom-call | flops 8589934592 | bytes 1048576 | tf_op jit(solution)/shard_map/open_operands/pallas_call | solution.py:567
  12.3 3.5 %collective-permute-start.1 = (bf16[4,16,32,128]{3,2,1,0:T(8,128)(2,1)S(1)}, bf16[4,16,32,128]{3,2,1,0:T(8,128)(2,1)S(1)}, u32[]{:S(2)}, u32[]{:S(2)}) collective-permute-start(bf16[4,16,32,128]{3,2,1,0:T(8,128)(2,1)S(1)} %get-tuple-element.78.rest_3_), channel_id=1, source_target_pairs={{0,2},{3,1},{1,0},{2,3},{4,6},{7,5},{5,4},{6,7},{8,10},{11,9},{9,8... | collective-permute-start | bytes 1572872 | tf_op jit(solution)/shard_map/ppermute | solution.py:939
  15.8 8.3 %open_operands.3 = (f32[8,32,32,128]{3,2,1,0:T(8,128)S(1)}, bf16[4,16,32,128]{3,2,1,0:T(8,128)(2,1)S(1)}, bf16[8,16,32,128]{3,2,1,0:T(8,128)(2,1)S(1)}, bf16[4,1...) custom-call(s32[4]{0:T(128)S(1)} %pad_add_fusion.ids, ...), custom_call_target="tpu_custom_call", output_to_operand_aliasing={{0}: (6, {}), {2}: (7, {}), {4}: (8, {})} | custom-call | flops 8589934592 | bytes 1048576 | tf_op jit(solution)/shard_map/open_operands/pallas_call | solution.py:567
  33.6 9.2 %collective-permute-done.4.rest_7_ = bf16[4,16,32,128]{3,2,1,0:T(8,128)(2,1)S(1)} collective-permute-done((bf16[4,16,32,128]{3,2,1,0:T(8,128)(2,1)S(1)}, bf16[4,16,32,128]{3,2,1,0:T(8,128)(2,1)S(1)}, u32[]{:S(2)}, u32[]{:S(2)}) %collective-permute-start.4) | collective-permute-done | bytes 524320 | tf_op jit(solution)/shard_map/ppermute | solution.py:939
  42.9 3.6 %banded_products.6 = (bf16[4,16,32,128]{3,2,1,0:T(8,128)(2,1)S(1)}, bf16[4,16,32,128]{3,2,1,0:T(8,128)(2,1)S(1)}, bf16[4,16,32,128]{3,2,1,0:T(8,128)(2,1)S(1)}) custom-call(s32[4]{0:T(128)S(1)} %pad_add_fusion.ids, s32[40]{0:T(128)S(1)} %get-tuple-element.76.chosen, bf16[4,16,32,128]{3,2,1,0:T(8,128)(2,1)S(1)} %collective-permute-done.rest_0_, ...), custom_call_target="tpu_custom_call" | custom-call | flops 402653184 | bytes 1 | tf_op jit(solution)/shard_map/banded_products/pallas_call | solution.py:771
  48.0 4.4 %collective-permute-start.10 = (bf16[8,16,32,128]{3,2,1,0:T(8,128)(2,1)S(1)}, bf16[8,16,32,128]{3,2,1,0:T(8,128)(2,1)S(1)}, u32[]{:S(2)}, u32[]{:S(2)}) collective-permute-start(bf16[8,16,32,128]{3,2,1,0:T(8,128)(2,1)S(1)} %get-tuple-element.96.rest_3_), channel_id=1, source_target_pairs={{0,2},{3,1},{1,0},{2,3},{4,6},{7,5},{5,4},{6,7},{8,10},{11,9},{9,8... | collective-permute-start | bytes 3145736 | tf_op jit(solution)/shard_map/ppermute | solution.py:939
  54.9 10.9 %far_operands.2 = (bf16[4,32,32,128]{3,2,1,0:T(8,128)(2,1)S(1)}, bf16[4,32,32,128]{3,2,1,0:T(8,128)(2,1)S(1)}) custom-call(s32[4]{0:T(128)S(1)} %pad_add_fusion.ids, s32[2,32]{1,0:T(2,128)S(1)} %bitcast.18, s32[10]{0:T(128)S(1)} %get-tuple-element.102.mine, bf16[8,32,32,128]{3,2,1,0:T(8,128)(2,1)} %collective-permute-done.6.rest_0_.rest_1_, ...), custom_call_target="tpu_custom_call" | custom-call | flops 8589934592 | bytes 1048576 | tf_op jit(solution)/shard_map/far_operands/pallas_call | solution.py:633
  65.9 9.2 %collective-permute-start.14 = (bf16[4,32,32,128]{3,2,1,0:T(8,128)(2,1)S(1)}, bf16[4,32,32,128]{3,2,1,0:T(8,128)(2,1)S(1)}, u32[]{:S(2)}, u32[]{:S(2)}) collective-permute-start(bf16[4,32,32,128]{3,2,1,0:T(8,128)(2,1)S(1)} %get-tuple-element.104.rest_1_), channel_id=1, source_target_pairs={{0,1},{1,0},{2,3},{3,2},{4,5},{5,4},{6,7},{7,6},{8,9},{9,8},{10,11... | collective-permute-start | bytes 3145736 | tf_op jit(solution)/shard_map/ppermute | solution.py:938
  76.8 11.9 %collective-permute-done.7.rest_0_ = bf16[4,16,32,128]{3,2,1,0:T(8,128)(2,1)S(1)} collective-permute-done((bf16[4,16,32,128]{3,2,1,0:T(8,128)(2,1)S(1)}, bf16[4,16,32,128]{3,2,1,0:T(8,128)(2,1)S(1)}, u32[]{:S(2)}, u32[]{:S(2)}) %collective-permute-start.7) | collective-permute-done | bytes 524320 | tf_op jit(solution)/shard_map/ppermute | solution.py:968
  89.9 3.5 %banded_products.7 = (bf16[4,16,32,128]{3,2,1,0:T(8,128)(2,1)}, bf16[4,16,32,128]{3,2,1,0:T(8,128)(2,1)}, bf16[4,16,32,128]{3,2,1,0:T(8,128)(2,1)S(1)}) custom-call(s32[4]{0:T(128)S(1)} %pad_add_fusion.ids, s32[40]{0:T(128)S(1)} %get-tuple-element.76.chosen, bf16[8,16,32,128]{3,2,1,0:T(8,128)(2,1)S(1)} %collective-permute-done.9.rest_0_, ...), custom_call_target="tpu_custom_call" | custom-call | flops 402653184 | bytes 1 | tf_op jit(solution)/shard_map/banded_products/pallas_call | solution.py:771
  98.0 4.4 %collective-permute-done.15.rest_2_ = bf16[4,32,32,128]{3,2,1,0:T(8,128)(2,1)} collective-permute-done((bf16[4,32,32,128]{3,2,1,0:T(8,128)(2,1)S(1)}, bf16[4,32,32,128]{3,2,1,0:T(8,128)(2,1)}, u32[]{:S(2)}, u32[]{:S(2)}) %collective-permute-start.15) | collective-permute-done | bytes 1048608 | tf_op jit(solution)/shard_map/ppermute | solution.py:939
  102.4 3.4 %banded_products.8.rest_6_ = bf16[4,32,32,128]{3,2,1,0:T(8,128)(2,1)S(1)} custom-call(s32[4]{0:T(128)S(1)} %pad_add_fusion.ids, s32[8]{0:T(128)S(1)} %reshape.9.chosen, bf16[4,32,32,128]{3,2,1,0:T(8,128)(2,1)S(1)} %collective-permute-done.14.rest_0_, bf16[4,32,32,128]{3,2,1,0:T(8,128)(2,1)S(1)} %get-tuple-element.104.rest_1_, ...), custom_call_target="tpu_custom_call" | custom-call | flops 268435456 | bytes 1 | tf_op jit(solution)/shard_map/banded_products/pallas_call | solution.py:771
  108.1 23.4 %collective-permute-done.12.rest_3_ = bf16[4,16,32,128]{3,2,1,0:T(8,128)(2,1)} collective-permute-done((bf16[4,16,32,128]{3,2,1,0:T(8,128)(2,1)}, bf16[4,16,32,128]{3,2,1,0:T(8,128)(2,1)}, u32[]{:S(2)}, u32[]{:S(2)}) %collective-permute-start.12) | collective-permute-done | bytes 524320 | tf_op jit(solution)/shard_map/ppermute | solution.py:968
  131.6 13.2 %close_layer.3 = (bf16[8,32,32,128]{3,2,1,0:T(8,128)(2,1)S(1)}, f32[8,32,32,128]{3,2,1,0:T(8,128)S(1)}, bf16[4,32,32,128]{3,2,1,0:T(8,128)(2,1)S(1)}, bf16[4,20,...) custom-call(s32[4]{0:T(128)S(1)} %pad_add_fusion.ids, ...), custom_call_target="tpu_custom_call" | custom-call | flops 8589934592 | bytes 1048576 | tf_op jit(solution)/shard_map/close_layer/pallas_call | solution.py:911
  146.3 13.2 %close_layer.4 = (bf16[8,32,32,128]{3,2,1,0:T(8,128)(2,1)S(1)}, f32[8,32,32,128]{3,2,1,0:T(8,128)S(1)}, bf16[4,32,32,128]{3,2,1,0:T(8,128)(2,1)S(1)}, bf16[4,20,...) custom-call(s32[4]{0:T(128)S(1)} %pad_add_fusion.ids, ...), custom_call_target="tpu_custom_call", output_to_operand_aliasing={{0}: (16, {}), {1}: (17, {}), {4}: (18, {}), {6}: (19, {})} | custom-call | flops 8589934592 | bytes 1048576 | tf_op jit(solution)/shard_map/close_layer/pallas_call | solution.py:911
  159.7 3.5 %collective-permute-start.18 = (bf16[4,20,32,128]{3,2,1,0:T(8,128)(2,1)S(1)}, bf16[4,20,32,128]{3,2,1,0:T(8,128)(2,1)S(1)}, u32[]{:S(2)}, u32[]{:S(2)}) collective-permute-start(bf16[4,20,32,128]{3,2,1,0:T(8,128)(2,1)S(1)} %collective-permute-done.17.rest_1_), channel_id=1, source_target_pairs={{0,1},{3,2},{4,5},{7,6},{8,9},{11,10},{12,13},{15,14},{16,17},{19,... | collective-permute-start | bytes 1966088 | tf_op jit(solution)/shard_map/ppermute | solution.py:948
  163.2 5.4 %collective-permute-done.19.rest_4_ = bf16[4,20,32,128]{3,2,1,0:T(8,128)(2,1)S(1)} collective-permute-done((bf16[4,20,32,128]{3,2,1,0:T(8,128)(2,1)S(1)}, bf16[4,20,32,128]{3,2,1,0:T(8,128)(2,1)S(1)}, u32[]{:S(2)}, u32[]{:S(2)}) %collective-permute-start.19) | collective-permute-done | bytes 655392 | tf_op jit(solution)/shard_map/ppermute | solution.py:947
  170.1 12.6 %collective-permute-done.20.rest_6_ = bf16[4,20,32,128]{3,2,1,0:T(8,128)(2,1)S(1)} collective-permute-done((bf16[4,20,32,128]{3,2,1,0:T(8,128)(2,1)S(1)}, bf16[4,20,32,128]{3,2,1,0:T(8,128)(2,1)S(1)}, u32[]{:S(2)}, u32[]{:S(2)}) %collective-permute-start.20) | collective-permute-done | bytes 655392 | tf_op jit(solution)/shard_map/ppermute | solution.py:946
  182.7 4.3 %collective-permute-start.21 = (bf16[4,20,32,128]{3,2,1,0:T(8,128)(2,1)S(1)}, bf16[4,20,32,128]{3,2,1,0:T(8,128)(2,1)S(1)}, u32[]{:S(2)}, u32[]{:S(2)}) collective-permute-start(bf16[4,20,32,128]{3,2,1,0:T(8,128)(2,1)S(1)} %collective-permute-done.20.rest_6_), channel_id=1, source_target_pairs={{0,1},{3,2},{4,5},{7,6},{8,9},{11,10},{12,13},{15,14},{16,17},{19,... | collective-permute-start | bytes 1966088 | tf_op jit(solution)/shard_map/ppermute | solution.py:948
  187.1 5.3 %collective-permute-done.22.rest_9_ = bf16[4,20,32,128]{3,2,1,0:T(8,128)(2,1)S(1)} collective-permute-done((bf16[4,20,32,128]{3,2,1,0:T(8,128)(2,1)S(1)}, bf16[4,20,32,128]{3,2,1,0:T(8,128)(2,1)S(1)}, u32[]{:S(2)}, u32[]{:S(2)}) %collective-permute-start.22) | collective-permute-done | bytes 655392 | tf_op jit(solution)/shard_map/ppermute | solution.py:947
  193.9 5.9 %banded_products.9 = (bf16[4,20,32,128]{3,2,1,0:T(8,128)(2,1)S(1)}, bf16[4,20,32,128]{3,2,1,0:T(8,128)(2,1)S(1)}, bf16[4,20,32,128]{3,2,1,0:T(8,128)(2,1)S(1)}) custom-call(s32[4]{0:T(128)S(1)} %pad_add_fusion.ids, s32[40]{0:T(128)S(1)} %get-tuple-element.76.chosen, bf16[4,20,32,128]{3,2,1,0:T(8,128)(2,1)S(1)} %get-tuple-element.108.rest_0_, ...), custom_call_target="tpu_custom_call" | custom-call | flops 503316480 | bytes 1 | tf_op jit(solution)/shard_map/banded_products/pallas_call | solution.py:771
  199.8 12.3 %collective-permute-done.24.rest_1_.rest_3_ = bf16[4,32,32,128]{3,2,1,0:T(8,128)(2,1)S(1)} collective-permute-done((bf16[4,32,32,128]{3,2,1,0:T(8,128)(2,1)S(1)}, bf16[4,32,32,128]{3,2,1,0:T(8,128)(2,1)S(1)}, u32[]{:S(2)}, u32[]{:S(2)}) %collective-permute-start.24) | collective-permute-done | bytes 1048608 | tf_op jit(solution)/shard_map/ppermute | solution.py:968
  212.0 2.8 collective-permute-start.25
  217.3 9.6 %far_operands.3 = (bf16[4,32,32,128]{3,2,1,0:T(8,128)(2,1)S(1)}, bf16[4,32,32,128]{3,2,1,0:T(8,128)(2,1)S(1)}) custom-call(s32[4]{0:T(128)S(1)} %pad_add_fusion.ids, s32[2,32]{1,0:T(2,128)S(1)} %bitcast.21, s32[10]{0:T(128)S(1)} %get-tuple-element.102.mine, bf16[4,32,32,128]{3,2,1,0:T(8,128)(2,1)S(1)} %collective-permute-done.23.rest_0_.rest_2_, ...), custom_call_target="tpu_custom_call" | custom-call | flops 8589934592 | bytes 1048576 | tf_op jit(solution)/shard_map/far_operands/pallas_call | solution.py:633
  227.0 29.5 %collective-permute-done.25.rest_0_ = bf16[4,20,32,128]{3,2,1,0:T(8,128)(2,1)S(1)} collective-permute-done((bf16[4,20,32,128]{3,2,1,0:T(8,128)(2,1)S(1)}, bf16[4,20,32,128]{3,2,1,0:T(8,128)(2,1)S(1)}, u32[]{:S(2)}, u32[]{:S(2)}) %collective-permute-start.25) | collective-permute-done | bytes 655392 | tf_op jit(solution)/shard_map/ppermute | solution.py:968
  258.2 3.5 %banded_products.10 = (bf16[4,12,32,128]{3,2,1,0:T(8,128)(2,1)S(1)}, bf16[4,12,32,128]{3,2,1,0:T(8,128)(2,1)S(1)}, bf16[4,12,32,128]{3,2,1,0:T(8,128)(2,1)S(1)}) custom-call(s32[4]{0:T(128)S(1)} %pad_add_fusion.ids, s32[40]{0:T(128)S(1)} %get-tuple-element.76.chosen, bf16[8,12,32,128]{3,2,1,0:T(8,128)(2,1)S(1)} %get-tuple-element.132.rest_0_, ...), custom_call_target="tpu_custom_call" | custom-call | flops 301989888 | bytes 1 | tf_op jit(solution)/shard_map/banded_products/pallas_call | solution.py:771
  261.9 10.1 %collective-permute-done.31.rest_4_ = bf16[4,12,32,128]{3,2,1,0:T(8,128)(2,1)S(1)} collective-permute-done((bf16[4,12,32,128]{3,2,1,0:T(8,128)(2,1)S(1)}, bf16[4,12,32,128]{3,2,1,0:T(8,128)(2,1)S(1)}, u32[]{:S(2)}, u32[]{:S(2)}) %collective-permute-start.31) | collective-permute-done | bytes 393248 | tf_op jit(solution)/shard_map/ppermute | solution.py:968
  272.0 3.3 %collective-permute-start.33 = (bf16[4,32,32,128]{3,2,1,0:T(8,128)(2,1)S(1)}, bf16[4,32,32,128]{3,2,1,0:T(8,128)(2,1)S(1)}, u32[]{:S(2)}, u32[]{:S(2)}) collective-permute-start(bf16[4,32,32,128]{3,2,1,0:T(8,128)(2,1)S(1)} %collective-permute-done.32.rest_1_), channel_id=1, source_target_pairs={{0,1},{3,2},{4,5},{7,6},{8,9},{11,10},{12,13},{15,14},{16,17},{19,... | collective-permute-start | bytes 3145736 | tf_op jit(solution)/shard_map/ppermute | solution.py:948
  275.3 3.2 %collective-permute-start.30 = (bf16[4,12,32,128]{3,2,1,0:T(8,128)(2,1)S(1)}, bf16[4,12,32,128]{3,2,1,0:T(8,128)(2,1)S(1)}, u32[]{:S(2)}, u32[]{:S(2)}) collective-permute-start(bf16[4,12,32,128]{3,2,1,0:T(8,128)(2,1)S(1)} %get-tuple-element.136), channel_id=1, source_target_pairs={{0,8},{4,12},{8,0},{12,4},{1,9},{5,13},{9,1},{13,5},{2,10},{6,14},... | collective-permute-start | bytes 1179656 | tf_op jit(solution)/shard_map/ppermute | solution.py:968
  278.5 7.7 %collective-permute-done.34.rest_4_ = bf16[4,32,32,128]{3,2,1,0:T(8,128)(2,1)S(1)} collective-permute-done((bf16[4,32,32,128]{3,2,1,0:T(8,128)(2,1)S(1)}, bf16[4,32,32,128]{3,2,1,0:T(8,128)(2,1)S(1)}, u32[]{:S(2)}, u32[]{:S(2)}) %collective-permute-start.34) | collective-permute-done | bytes 1048608 | tf_op jit(solution)/shard_map/ppermute | solution.py:947
  288.5 5.0 %collective-permute-done.30.rest_3_ = bf16[4,12,32,128]{3,2,1,0:T(8,128)(2,1)S(1)} collective-permute-done((bf16[4,12,32,128]{3,2,1,0:T(8,128)(2,1)S(1)}, bf16[4,12,32,128]{3,2,1,0:T(8,128)(2,1)S(1)}, u32[]{:S(2)}, u32[]{:S(2)}) %collective-permute-start.30) | collective-permute-done | bytes 393248 | tf_op jit(solution)/shard_map/ppermute | solution.py:968
  293.5 8.8 %close_layer.5 = bf16[8,32,32,128]{3,2,1,0:T(8,128)(2,1)} custom-call(s32[4]{0:T(128)S(1)} %pad_add_fusion.ids, s32[2,32]{1,0:T(2,128)S(1)} %bitcast.22, s32[16]{0:T(128)S(1)} %get-tuple-element.91.place, bf16[4,20,32,128]{3,2,1,0:T(8,128)(2,1)S(1)} %collective-permute-done.25.rest_0_, bf16[4,20,32,128]{3,2,1,0:T(8,128)(2,1)S(1)} %collective-permute-done.26.rest_1_, ...), custom_call_target="tpu_custom_call" | custom-call | flops 8589934592 | bytes 1048576 | tf_op jit(solution)/shard_map/close_layer/pallas_call | solution.py:911
  (95 shorter events, 38.5 us)
Async XLA Ops:
  0.0 52.5 %collective-permute-start.6 = (bf16[8,32,32,128]{3,2,1,0:T(8,128)(2,1)}, bf16[8,32,32,128]{3,2,1,0:T(8,128)(2,1)}, u32[]{:S(2)}, u32[]{:S(2)}) collective-permute-start(bf16[8,32,32,128]{3,2,1,0:T(8,128)(2,1)} %rest_7_.3), channel_id=1, source_target_pairs={{0,4},{4,8},{8,12},{12,0},{1,5},{5,9},{9,13},{13,1},{2,6},{6,10},{... | collective-permute-start | bytes 6291464 | tf_op jit(solution)/shard_map/ppermute | solution.py:968
  11.6 14.6 %collective-permute-start.2 = (bf16[4,16,32,128]{3,2,1,0:T(8,128)(2,1)S(1)}, bf16[4,16,32,128]{3,2,1,0:T(8,128)(2,1)S(1)}, u32[]{:S(2)}, u32[]{:S(2)}) collective-permute-start(bf16[4,16,32,128]{3,2,1,0:T(8,128)(2,1)S(1)} %get-tuple-element.78.rest_3_), channel_id=1, source_target_pairs={{1,2},{2,1},{5,6},{6,5},{9,10},{10,9},{13,14},{14,13},{17,18},{18,... | collective-permute-start | bytes 1572872 | tf_op jit(solution)/shard_map/ppermute | solution.py:940
  12.3 14.1 %collective-permute-start.1 = (bf16[4,16,32,128]{3,2,1,0:T(8,128)(2,1)S(1)}, bf16[4,16,32,128]{3,2,1,0:T(8,128)(2,1)S(1)}, u32[]{:S(2)}, u32[]{:S(2)}) collective-permute-start(bf16[4,16,32,128]{3,2,1,0:T(8,128)(2,1)S(1)} %get-tuple-element.78.rest_3_), channel_id=1, source_target_pairs={{0,2},{3,1},{1,0},{2,3},{4,6},{7,5},{5,4},{6,7},{8,10},{11,9},{9,8... | collective-permute-start | bytes 1572872 | tf_op jit(solution)/shard_map/ppermute | solution.py:939
  15.8 10.3 %collective-permute-start = (bf16[4,16,32,128]{3,2,1,0:T(8,128)(2,1)S(1)}, bf16[4,16,32,128]{3,2,1,0:T(8,128)(2,1)S(1)}, u32[]{:S(2)}, u32[]{:S(2)}) collective-permute-start(bf16[4,16,32,128]{3,2,1,0:T(8,128)(2,1)S(1)} %get-tuple-element.77.rest_1_), channel_id=1, source_target_pairs={{0,1},{1,0},{2,3},{3,2},{4,5},{5,4},{6,7},{7,6},{8,9},{9,8},{10,11... | collective-permute-start | bytes 1572872 | tf_op jit(solution)/shard_map/ppermute | solution.py:938
  29.3 13.5 %collective-permute-start.4 = (bf16[4,16,32,128]{3,2,1,0:T(8,128)(2,1)S(1)}, bf16[4,16,32,128]{3,2,1,0:T(8,128)(2,1)S(1)}, u32[]{:S(2)}, u32[]{:S(2)}) collective-permute-start(bf16[4,16,32,128]{3,2,1,0:T(8,128)(2,1)S(1)} %get-tuple-element.85.rest_8_), channel_id=1, source_target_pairs={{0,2},{3,1},{1,0},{2,3},{4,6},{7,5},{5,4},{6,7},{8,10},{11,9},{9,8... | collective-permute-start | bytes 1572872 | tf_op jit(solution)/shard_map/ppermute | solution.py:939
  47.3 18.6 %collective-permute-start.11 = (bf16[8,16,32,128]{3,2,1,0:T(8,128)(2,1)S(1)}, bf16[8,16,32,128]{3,2,1,0:T(8,128)(2,1)S(1)}, u32[]{:S(2)}, u32[]{:S(2)}) collective-permute-start(bf16[8,16,32,128]{3,2,1,0:T(8,128)(2,1)S(1)} %get-tuple-element.96.rest_3_), channel_id=1, source_target_pairs={{1,2},{2,1},{5,6},{6,5},{9,10},{10,9},{13,14},{14,13},{17,18},{18,... | collective-permute-start | bytes 3145736 | tf_op jit(solution)/shard_map/ppermute | solution.py:940
  48.0 41.9 %collective-permute-start.10 = (bf16[8,16,32,128]{3,2,1,0:T(8,128)(2,1)S(1)}, bf16[8,16,32,128]{3,2,1,0:T(8,128)(2,1)S(1)}, u32[]{:S(2)}, u32[]{:S(2)}) collective-permute-start(bf16[8,16,32,128]{3,2,1,0:T(8,128)(2,1)S(1)} %get-tuple-element.96.rest_3_), channel_id=1, source_target_pairs={{0,2},{3,1},{1,0},{2,3},{4,6},{7,5},{5,4},{6,7},{8,10},{11,9},{9,8... | collective-permute-start | bytes 3145736 | tf_op jit(solution)/shard_map/ppermute | solution.py:939
  52.5 37.4 %collective-permute-start.9 = (bf16[8,16,32,128]{3,2,1,0:T(8,128)(2,1)S(1)}, bf16[8,16,32,128]{3,2,1,0:T(8,128)(2,1)S(1)}, u32[]{:S(2)}, u32[]{:S(2)}) collective-permute-start(bf16[8,16,32,128]{3,2,1,0:T(8,128)(2,1)S(1)} %get-tuple-element.94.rest_1_), channel_id=1, source_target_pairs={{0,1},{1,0},{2,3},{3,2},{4,5},{5,4},{6,7},{7,6},{8,9},{9,8},{10,11... | collective-permute-start | bytes 3145736 | tf_op jit(solution)/shard_map/ppermute | solution.py:938
  52.5 22.7 %collective-permute-start.8 = (bf16[4,16,32,128]{3,2,1,0:T(8,128)(2,1)S(1)}, bf16[4,16,32,128]{3,2,1,0:T(8,128)(2,1)S(1)}, u32[]{:S(2)}, u32[]{:S(2)}) collective-permute-start(bf16[4,16,32,128]{3,2,1,0:T(8,128)(2,1)S(1)} %get-tuple-element.89), channel_id=1, source_target_pairs={{0,12},{4,0},{8,4},{12,8},{1,13},{5,1},{9,5},{13,9},{2,14},{6,2},{... | collective-permute-start | bytes 1572872 | tf_op jit(solution)/shard_map/ppermute | solution.py:968
  52.6 36.0 %collective-permute-start.7 = (bf16[4,16,32,128]{3,2,1,0:T(8,128)(2,1)S(1)}, bf16[4,16,32,128]{3,2,1,0:T(8,128)(2,1)S(1)}, u32[]{:S(2)}, u32[]{:S(2)}) collective-permute-start(bf16[4,16,32,128]{3,2,1,0:T(8,128)(2,1)S(1)} %get-tuple-element.87), channel_id=1, source_target_pairs={{0,8},{4,12},{8,0},{12,4},{1,9},{5,13},{9,1},{13,5},{2,10},{6,14},... | collective-permute-start | bytes 1572872 | tf_op jit(solution)/shard_map/ppermute | solution.py:968
  65.9 32.1 %collective-permute-start.14 = (bf16[4,32,32,128]{3,2,1,0:T(8,128)(2,1)S(1)}, bf16[4,32,32,128]{3,2,1,0:T(8,128)(2,1)S(1)}, u32[]{:S(2)}, u32[]{:S(2)}) collective-permute-start(bf16[4,32,32,128]{3,2,1,0:T(8,128)(2,1)S(1)} %get-tuple-element.104.rest_1_), channel_id=1, source_target_pairs={{0,1},{1,0},{2,3},{3,2},{4,5},{5,4},{6,7},{7,6},{8,9},{9,8},{10,11... | collective-permute-start | bytes 3145736 | tf_op jit(solution)/shard_map/ppermute | solution.py:938
  75.1 22.9 %collective-permute-start.16 = (bf16[4,32,32,128]{3,2,1,0:T(8,128)(2,1)S(1)}, bf16[4,32,32,128]{3,2,1,0:T(8,128)(2,1)}, u32[]{:S(2)}, u32[]{:S(2)}) collective-permute-start(bf16[4,32,32,128]{3,2,1,0:T(8,128)(2,1)S(1)} %get-tuple-element.105.rest_3_), channel_id=1, source_target_pairs={{1,2},{2,1},{5,6},{6,5},{9,10},{10,9},{13,14},{14,13},{17,18},{18,... | collective-permute-start | bytes 3145736 | tf_op jit(solution)/shard_map/ppermute | solution.py:940
  88.6 13.7 %collective-permute-start.15 = (bf16[4,32,32,128]{3,2,1,0:T(8,128)(2,1)S(1)}, bf16[4,32,32,128]{3,2,1,0:T(8,128)(2,1)}, u32[]{:S(2)}, u32[]{:S(2)}) collective-permute-start(bf16[4,32,32,128]{3,2,1,0:T(8,128)(2,1)S(1)} %get-tuple-element.105.rest_3_), channel_id=1, source_target_pairs={{0,2},{3,1},{1,0},{2,3},{4,6},{7,5},{5,4},{6,7},{8,10},{11,9},{9,8... | collective-permute-start | bytes 3145736 | tf_op jit(solution)/shard_map/ppermute | solution.py:939
  94.2 14.0 %collective-permute-start.13 = (bf16[4,16,32,128]{3,2,1,0:T(8,128)(2,1)}, bf16[4,16,32,128]{3,2,1,0:T(8,128)(2,1)}, u32[]{:S(2)}, u32[]{:S(2)}) collective-permute-start(bf16[4,16,32,128]{3,2,1,0:T(8,128)(2,1)} %get-tuple-element.100), channel_id=1, source_target_pairs={{0,12},{4,0},{8,4},{12,8},{1,13},{5,1},{9,5},{13,9},{2,14},{6,2},{... | collective-permute-start | bytes 1572872 | tf_op jit(solution)/shard_map/ppermute | solution.py:968
  95.2 36.4 %collective-permute-start.12 = (bf16[4,16,32,128]{3,2,1,0:T(8,128)(2,1)}, bf16[4,16,32,128]{3,2,1,0:T(8,128)(2,1)}, u32[]{:S(2)}, u32[]{:S(2)}) collective-permute-start(bf16[4,16,32,128]{3,2,1,0:T(8,128)(2,1)} %get-tuple-element.98), channel_id=1, source_target_pairs={{0,8},{4,12},{8,0},{12,4},{1,9},{5,13},{9,1},{13,5},{2,10},{6,14},... | collective-permute-start | bytes 1572872 | tf_op jit(solution)/shard_map/ppermute | solution.py:968
  144.8 14.8 %collective-permute-start.17 = (bf16[4,20,32,128]{3,2,1,0:T(8,128)(2,1)S(1)}, bf16[4,20,32,128]{3,2,1,0:T(8,128)(2,1)S(1)}, u32[]{:S(2)}, u32[]{:S(2)}) collective-permute-start(bf16[4,20,32,128]{3,2,1,0:T(8,128)(2,1)S(1)} %get-tuple-element.108.rest_0_), channel_id=1, source_target_pairs={{1,3},{2,0},{0,1},{3,2},{5,7},{6,4},{4,5},{7,6},{9,11},{10,8},{8,9... | collective-permute-start | bytes 1966088 | tf_op jit(solution)/shard_map/ppermute | solution.py:946
  145.0 23.6 %collective-permute-start.19 = (bf16[4,20,32,128]{3,2,1,0:T(8,128)(2,1)S(1)}, bf16[4,20,32,128]{3,2,1,0:T(8,128)(2,1)S(1)}, u32[]{:S(2)}, u32[]{:S(2)}) collective-permute-start(bf16[4,20,32,128]{3,2,1,0:T(8,128)(2,1)S(1)} %get-tuple-element.115.rest_3_), channel_id=1, source_target_pairs={{0,2},{2,0},{1,3},{3,1},{4,6},{6,4},{5,7},{7,5},{8,10},{10,8},{9,1... | collective-permute-start | bytes 1966088 | tf_op jit(solution)/shard_map/ppermute | solution.py:947
  146.3 40.7 %collective-permute-start.23 = (bf16[4,32,32,128]{3,2,1,0:T(8,128)(2,1)S(1)}, bf16[4,32,32,128]{3,2,1,0:T(8,128)(2,1)S(1)}, u32[]{:S(2)}, u32[]{:S(2)}) collective-permute-start(bf16[4,32,32,128]{3,2,1,0:T(8,128)(2,1)S(1)} %get-tuple-element.123), channel_id=1, source_target_pairs={{0,4},{4,8},{8,12},{12,0},{1,5},{5,9},{9,13},{13,1},{2,6},{6,10},{... | collective-permute-start | bytes 3145736 | tf_op jit(solution)/shard_map/ppermute | solution.py:968
  168.6 14.1 %collective-permute-start.20 = (bf16[4,20,32,128]{3,2,1,0:T(8,128)(2,1)S(1)}, bf16[4,20,32,128]{3,2,1,0:T(8,128)(2,1)S(1)}, u32[]{:S(2)}, u32[]{:S(2)}) collective-permute-start(bf16[4,20,32,128]{3,2,1,0:T(8,128)(2,1)S(1)} %get-tuple-element.117.rest_5_), channel_id=1, source_target_pairs={{1,3},{2,0},{0,1},{3,2},{5,7},{6,4},{4,5},{7,6},{9,11},{10,8},{8,9... | collective-permute-start | bytes 1966088 | tf_op jit(solution)/shard_map/ppermute | solution.py:946
  168.6 23.8 %collective-permute-start.22 = (bf16[4,20,32,128]{3,2,1,0:T(8,128)(2,1)S(1)}, bf16[4,20,32,128]{3,2,1,0:T(8,128)(2,1)S(1)}, u32[]{:S(2)}, u32[]{:S(2)}) collective-permute-start(bf16[4,20,32,128]{3,2,1,0:T(8,128)(2,1)S(1)} %get-tuple-element.120.rest_8_), channel_id=1, source_target_pairs={{0,2},{2,0},{1,3},{3,1},{4,6},{6,4},{5,7},{7,5},{8,10},{10,8},{9,1... | collective-permute-start | bytes 1966088 | tf_op jit(solution)/shard_map/ppermute | solution.py:947
  182.7 9.7 %collective-permute-start.21 = (bf16[4,20,32,128]{3,2,1,0:T(8,128)(2,1)S(1)}, bf16[4,20,32,128]{3,2,1,0:T(8,128)(2,1)S(1)}, u32[]{:S(2)}, u32[]{:S(2)}) collective-permute-start(bf16[4,20,32,128]{3,2,1,0:T(8,128)(2,1)S(1)} %collective-permute-done.20.rest_6_), channel_id=1, source_target_pairs={{0,1},{3,2},{4,5},{7,6},{8,9},{11,10},{12,13},{15,14},{16,17},{19,... | collective-permute-start | bytes 1966088 | tf_op jit(solution)/shard_map/ppermute | solution.py:948
  187.0 25.0 %collective-permute-start.24 = (bf16[4,32,32,128]{3,2,1,0:T(8,128)(2,1)S(1)}, bf16[4,32,32,128]{3,2,1,0:T(8,128)(2,1)S(1)}, u32[]{:S(2)}, u32[]{:S(2)}) collective-permute-start(bf16[4,32,32,128]{3,2,1,0:T(8,128)(2,1)S(1)} %get-tuple-element.124), channel_id=1, source_target_pairs={{0,4},{4,8},{8,12},{12,0},{1,5},{5,9},{9,13},{13,1},{2,6},{6,10},{... | collective-permute-start | bytes 3145736 | tf_op jit(solution)/shard_map/ppermute | solution.py:968
  192.4 22.5 %collective-permute-start.27 = (bf16[8,12,32,128]{3,2,1,0:T(8,128)(2,1)S(1)}, bf16[8,12,32,128]{3,2,1,0:T(8,128)(2,1)S(1)}, u32[]{:S(2)}, u32[]{:S(2)}) collective-permute-start(bf16[8,12,32,128]{3,2,1,0:T(8,128)(2,1)S(1)} %get-tuple-element.132.rest_0_), channel_id=1, source_target_pairs={{1,3},{2,0},{0,1},{3,2},{5,7},{6,4},{4,5},{7,6},{9,11},{10,8},{8,9... | collective-permute-start | bytes 2359304 | tf_op jit(solution)/shard_map/ppermute | solution.py:946
  192.4 65.8 %collective-permute-start.29 = (bf16[8,12,32,128]{3,2,1,0:T(8,128)(2,1)S(1)}, bf16[8,12,32,128]{3,2,1,0:T(8,128)(2,1)S(1)}, u32[]{:S(2)}, u32[]{:S(2)}) collective-permute-start(bf16[8,12,32,128]{3,2,1,0:T(8,128)(2,1)S(1)} %get-tuple-element.134.rest_3_), channel_id=1, source_target_pairs={{0,2},{2,0},{1,3},{3,1},{4,6},{6,4},{5,7},{7,5},{8,10},{10,8},{9,1... | collective-permute-start | bytes 2359304 | tf_op jit(solution)/shard_map/ppermute | solution.py:947
  212.0 44.4 %collective-permute-start.25 = (bf16[4,20,32,128]{3,2,1,0:T(8,128)(2,1)S(1)}, bf16[4,20,32,128]{3,2,1,0:T(8,128)(2,1)S(1)}, u32[]{:S(2)}, u32[]{:S(2)}) collective-permute-start(bf16[4,20,32,128]{3,2,1,0:T(8,128)(2,1)S(1)} %get-tuple-element.125), channel_id=1, source_target_pairs={{0,8},{4,12},{8,0},{12,4},{1,9},{5,13},{9,1},{13,5},{2,10},{6,14},... | collective-permute-start | bytes 1966088 | tf_op jit(solution)/shard_map/ppermute | solution.py:968
  214.9 43.4 %collective-permute-start.26 = (bf16[4,20,32,128]{3,2,1,0:T(8,128)(2,1)S(1)}, bf16[4,20,32,128]{3,2,1,0:T(8,128)(2,1)S(1)}, u32[]{:S(2)}, u32[]{:S(2)}) collective-permute-start(bf16[4,20,32,128]{3,2,1,0:T(8,128)(2,1)S(1)} %get-tuple-element.127), channel_id=1, source_target_pairs={{0,12},{4,0},{8,4},{12,8},{1,13},{5,1},{9,5},{13,9},{2,14},{6,2},{... | collective-permute-start | bytes 1966088 | tf_op jit(solution)/shard_map/ppermute | solution.py:968
  214.9 43.4 %collective-permute-start.28 = (bf16[8,12,32,128]{3,2,1,0:T(8,128)(2,1)S(1)}, bf16[8,12,32,128]{3,2,1,0:T(8,128)(2,1)S(1)}, u32[]{:S(2)}, u32[]{:S(2)}) collective-permute-start(bf16[8,12,32,128]{3,2,1,0:T(8,128)(2,1)S(1)} %collective-permute-done.27.rest_1_), channel_id=1, source_target_pairs={{0,1},{3,2},{4,5},{7,6},{8,9},{11,10},{12,13},{15,14},{16,17},{19,... | collective-permute-start | bytes 2359304 | tf_op jit(solution)/shard_map/ppermute | solution.py:948
  226.9 35.0 %collective-permute-start.32 = (bf16[4,32,32,128]{3,2,1,0:T(8,128)(2,1)S(1)}, bf16[4,32,32,128]{3,2,1,0:T(8,128)(2,1)S(1)}, u32[]{:S(2)}, u32[]{:S(2)}) collective-permute-start(bf16[4,32,32,128]{3,2,1,0:T(8,128)(2,1)S(1)} %get-tuple-element.142.rest_0_), channel_id=1, source_target_pairs={{1,3},{2,0},{0,1},{3,2},{5,7},{6,4},{4,5},{7,6},{9,11},{10,8},{8,9... | collective-permute-start | bytes 3145736 | tf_op jit(solution)/shard_map/ppermute | solution.py:946
  261.7 10.3 %collective-permute-start.31 = (bf16[4,12,32,128]{3,2,1,0:T(8,128)(2,1)S(1)}, bf16[4,12,32,128]{3,2,1,0:T(8,128)(2,1)S(1)}, u32[]{:S(2)}, u32[]{:S(2)}) collective-permute-start(bf16[4,12,32,128]{3,2,1,0:T(8,128)(2,1)S(1)} %get-tuple-element.138), channel_id=1, source_target_pairs={{0,12},{4,0},{8,4},{12,8},{1,13},{5,1},{9,5},{13,9},{2,14},{6,2},{... | collective-permute-start | bytes 1179656 | tf_op jit(solution)/shard_map/ppermute | solution.py:968
  261.8 24.3 %collective-permute-start.34 = (bf16[4,32,32,128]{3,2,1,0:T(8,128)(2,1)S(1)}, bf16[4,32,32,128]{3,2,1,0:T(8,128)(2,1)S(1)}, u32[]{:S(2)}, u32[]{:S(2)}) collective-permute-start(bf16[4,32,32,128]{3,2,1,0:T(8,128)(2,1)S(1)} %get-tuple-element.144.rest_3_), channel_id=1, source_target_pairs={{0,2},{2,0},{1,3},{3,1},{4,6},{6,4},{5,7},{7,5},{8,10},{10,8},{9,1... | collective-permute-start | bytes 3145736 | tf_op jit(solution)/shard_map/ppermute | solution.py:947
  272.0 14.1 %collective-permute-start.33 = (bf16[4,32,32,128]{3,2,1,0:T(8,128)(2,1)S(1)}, bf16[4,32,32,128]{3,2,1,0:T(8,128)(2,1)S(1)}, u32[]{:S(2)}, u32[]{:S(2)}) collective-permute-start(bf16[4,32,32,128]{3,2,1,0:T(8,128)(2,1)S(1)} %collective-permute-done.32.rest_1_), channel_id=1, source_target_pairs={{0,1},{3,2},{4,5},{7,6},{8,9},{11,10},{12,13},{15,14},{16,17},{19,... | collective-permute-start | bytes 3145736 | tf_op jit(solution)/shard_map/ppermute | solution.py:948
  275.3 18.3 %collective-permute-start.30 = (bf16[4,12,32,128]{3,2,1,0:T(8,128)(2,1)S(1)}, bf16[4,12,32,128]{3,2,1,0:T(8,128)(2,1)S(1)}, u32[]{:S(2)}, u32[]{:S(2)}) collective-permute-start(bf16[4,12,32,128]{3,2,1,0:T(8,128)(2,1)S(1)} %get-tuple-element.136), channel_id=1, source_target_pairs={{0,8},{4,12},{8,0},{12,4},{1,9},{5,13},{9,1},{13,5},{2,10},{6,14},... | collective-permute-start | bytes 1179656 | tf_op jit(solution)/shard_map/ppermute | solution.py:968
  (22 other events, 322.6 us)

commit v15 on v14

--- a/solution.py
+++ b/solution.py
@@ -1006,7 +1006,7 @@
                     ((other, _), _), ((one, _), (_, two)) = exchanged[-1]
                     left = after(left, other)
                     right = after(right, one, two, made[-1])
-                exchanged = [exchange(left, right, made[-1])]
+                exchanged = [exchange(left, right, list(by_shift.values())[-1] if by_shift else made[-1])]
                 ids = after(ids, *by_shift.values())
             made = banded_products(near, ids, chosen, exchanged, capacity, cols)
             start = sum(bands[layer][:chunk])

time: 305 us -> 294 us (0.964)
  waiting for transfers between devices: 141 us -> 112 us
  starting transfers between devices: 58 us -> 76.7 us
    ppermute x11, waiting for transfers between devices: 96.3 us -> 49.9 us  [over_blk(): lax.ppermute(value, 'blk', [(p, (p + shift) % n_blk) for p in range(n_blk)])]
    ppermute x4, starting transfers between devices: 13.5 us -> 34 us  [exchange_bands_incoming(): lax.ppermute(after(one, other if over is None else over), both, [(0, 1),...]
    ppermute x4, waiting for transfers between devices: 12.8 us -> 24.2 us  [exchange_bands_incoming(): one = lax.ppermute(left, both, [(1, 3), (2, 0), (0, 1), (3, 2)])]
    ppermute x4, waiting for transfers between devices: 18.4 us -> 24.3 us  [exchange_bands_incoming(): other = lax.ppermute(right, 'chan', [(0, 1), (1, 0)])]
  transfers between devices with their start and end apart: 35 -> 35, of which waited for: 16 -> 16; matrix products, arithmetic and copies ran while one was open for 0% -> 0% of each run, Pallas kernels for 25% -> 26%
where the time goes in v15:
time: 294 us; the launch traced here: 292 us
  waiting for transfers between devices  112 us (38%)
  Pallas kernels  97.6 us (33%)
  starting transfers between devices  76.7 us (26%)
  local copies, waits for them, and re-layouts  5.01 us (2%)
    ppermute x11, waiting for transfers between devices, over_blk(): lax.ppermute(value, 'blk', [(p, (p + shift) % n_blk) for p in range(n_blk)])  49.9 us
    pallas_call x3, Pallas kernels, close_layer(): pl.pallas_call(functools.partial(close_kernel, *(layer, last, spots, 0 if...  35.3 us
    ppermute x4, starting transfers between devices, exchange_bands_incoming(): lax.ppermute(after(one, other if over is None else over), both, [(0, 1),...  34 us
    ppermute x4, waiting for transfers between devices, exchange_bands_incoming(): other = lax.ppermute(right, 'chan', [(0, 1), (1, 0)])  24.3 us
    ppermute x4, waiting for transfers between devices, exchange_bands_incoming(): one = lax.ppermute(left, both, [(1, 3), (2, 0), (0, 1), (3, 2)])  24.2 us
    pallas_call x6, Pallas kernels, banded_products(): pl.pallas_call(functools.partial(banded_kernel, shifts, capacity, tuple(p...  22.3 us
    pallas_call x2, Pallas kernels, far_operands(): pl.pallas_call(functools.partial(far_kernel, layer, n_blk, far, lax.axis_...  20.6 us
    pallas_call x2, Pallas kernels, open_operands(): pl.pallas_call(functools.partial(open_kernel, hidden, len(bands), lax.axi...  16.6 us
  transfers between devices with their start and end apart: 35, of which 16 were waited for; matrix products, arithmetic and copies ran while one was open for 0% of the time, Pallas kernels for 26%

profile of v15, /device:TPU:11, one launch (start us, length us, event | category | flops | bytes accessed | tf_op | source)
XLA Modules:
  0.0 292.2 jit_solution(3466687015290925126)
XLA Ops:
  3.3 8.3 %open_operands.2 = (f32[8,32,32,128]{3,2,1,0:T(8,128)S(1)}, bf16[4,16,32,128]{3,2,1,0:T(8,128)(2,1)S(1)}, bf16[8,16,32,128]{3,2,1,0:T(8,128)(2,1)S(1)}, bf16[4,1...) custom-call(s32[4]{0:T(128)S(1)} %pad_add_fusion.ids, s32[2,32]{1,0:T(2,128)S(1)} %bitcast.16, ...), custom_call_target="tpu_custom_call" | custom-call | flops 8589934592 | bytes 1048576 | tf_op jit(solution)/shard_map/open_operands/pallas_call | solution.py:567
  12.3 3.5 %collective-permute-start.1 = (bf16[4,16,32,128]{3,2,1,0:T(8,128)(2,1)S(1)}, bf16[4,16,32,128]{3,2,1,0:T(8,128)(2,1)S(1)}, u32[]{:S(2)}, u32[]{:S(2)}) collective-permute-start(bf16[4,16,32,128]{3,2,1,0:T(8,128)(2,1)S(1)} %get-tuple-element.78.rest_3_), channel_id=1, source_target_pairs={{0,2},{3,1},{1,0},{2,3},{4,6},{7,5},{5,4},{6,7},{8,10},{11,9},{9,8... | collective-permute-start | bytes 1572872 | tf_op jit(solution)/shard_map/ppermute | solution.py:939
  15.8 8.3 %open_operands.3 = (f32[8,32,32,128]{3,2,1,0:T(8,128)S(1)}, bf16[4,16,32,128]{3,2,1,0:T(8,128)(2,1)S(1)}, bf16[8,16,32,128]{3,2,1,0:T(8,128)(2,1)S(1)}, bf16[4,1...) custom-call(s32[4]{0:T(128)S(1)} %pad_add_fusion.ids, ...), custom_call_target="tpu_custom_call", output_to_operand_aliasing={{0}: (6, {}), {2}: (7, {}), {4}: (8, {})} | custom-call | flops 8589934592 | bytes 1048576 | tf_op jit(solution)/shard_map/open_operands/pallas_call | solution.py:567
  29.3 2.6 collective-permute-start.4
  33.6 9.2 %collective-permute-done.4.rest_7_ = bf16[4,16,32,128]{3,2,1,0:T(8,128)(2,1)S(1)} collective-permute-done((bf16[4,16,32,128]{3,2,1,0:T(8,128)(2,1)S(1)}, bf16[4,16,32,128]{3,2,1,0:T(8,128)(2,1)S(1)}, u32[]{:S(2)}, u32[]{:S(2)}) %collective-permute-start.4) | collective-permute-done | bytes 524320 | tf_op jit(solution)/shard_map/ppermute | solution.py:939
  42.9 3.6 %banded_products.6 = (bf16[4,16,32,128]{3,2,1,0:T(8,128)(2,1)S(1)}, bf16[4,16,32,128]{3,2,1,0:T(8,128)(2,1)S(1)}, bf16[4,16,32,128]{3,2,1,0:T(8,128)(2,1)S(1)}) custom-call(s32[4]{0:T(128)S(1)} %pad_add_fusion.ids, s32[40]{0:T(128)S(1)} %get-tuple-element.76.chosen, bf16[4,16,32,128]{3,2,1,0:T(8,128)(2,1)S(1)} %collective-permute-done.rest_0_, ...), custom_call_target="tpu_custom_call" | custom-call | flops 402653184 | bytes 1 | tf_op jit(solution)/shard_map/banded_products/pallas_call | solution.py:771
  48.0 4.4 %collective-permute-start.10 = (bf16[8,16,32,128]{3,2,1,0:T(8,128)(2,1)S(1)}, bf16[8,16,32,128]{3,2,1,0:T(8,128)(2,1)S(1)}, u32[]{:S(2)}, u32[]{:S(2)}) collective-permute-start(bf16[8,16,32,128]{3,2,1,0:T(8,128)(2,1)S(1)} %get-tuple-element.96.rest_3_), channel_id=1, source_target_pairs={{0,2},{3,1},{1,0},{2,3},{4,6},{7,5},{5,4},{6,7},{8,10},{11,9},{9,8... | collective-permute-start | bytes 3145736 | tf_op jit(solution)/shard_map/ppermute | solution.py:939
  54.9 10.9 %far_operands.2 = (bf16[4,32,32,128]{3,2,1,0:T(8,128)(2,1)S(1)}, bf16[4,32,32,128]{3,2,1,0:T(8,128)(2,1)S(1)}) custom-call(s32[4]{0:T(128)S(1)} %pad_add_fusion.ids, s32[2,32]{1,0:T(2,128)S(1)} %bitcast.18, s32[10]{0:T(128)S(1)} %get-tuple-element.102.mine, bf16[8,32,32,128]{3,2,1,0:T(8,128)(2,1)} %collective-permute-done.6.rest_0_.rest_1_, ...), custom_call_target="tpu_custom_call" | custom-call | flops 8589934592 | bytes 1048576 | tf_op jit(solution)/shard_map/far_operands/pallas_call | solution.py:633
  65.9 9.2 %collective-permute-start.14 = (bf16[4,32,32,128]{3,2,1,0:T(8,128)(2,1)S(1)}, bf16[4,32,32,128]{3,2,1,0:T(8,128)(2,1)S(1)}, u32[]{:S(2)}, u32[]{:S(2)}) collective-permute-start(bf16[4,32,32,128]{3,2,1,0:T(8,128)(2,1)S(1)} %get-tuple-element.104.rest_1_), channel_id=1, source_target_pairs={{0,1},{1,0},{2,3},{3,2},{4,5},{5,4},{6,7},{7,6},{8,9},{9,8},{10,11... | collective-permute-start | bytes 3145736 | tf_op jit(solution)/shard_map/ppermute | solution.py:938
  76.8 11.9 %collective-permute-done.7.rest_0_ = bf16[4,16,32,128]{3,2,1,0:T(8,128)(2,1)S(1)} collective-permute-done((bf16[4,16,32,128]{3,2,1,0:T(8,128)(2,1)S(1)}, bf16[4,16,32,128]{3,2,1,0:T(8,128)(2,1)S(1)}, u32[]{:S(2)}, u32[]{:S(2)}) %collective-permute-start.7) | collective-permute-done | bytes 524320 | tf_op jit(solution)/shard_map/ppermute | solution.py:968
  89.9 3.5 %banded_products.7 = (bf16[4,16,32,128]{3,2,1,0:T(8,128)(2,1)}, bf16[4,16,32,128]{3,2,1,0:T(8,128)(2,1)}, bf16[4,16,32,128]{3,2,1,0:T(8,128)(2,1)S(1)}) custom-call(s32[4]{0:T(128)S(1)} %pad_add_fusion.ids, s32[40]{0:T(128)S(1)} %get-tuple-element.76.chosen, bf16[8,16,32,128]{3,2,1,0:T(8,128)(2,1)S(1)} %collective-permute-done.9.rest_0_, ...), custom_call_target="tpu_custom_call" | custom-call | flops 402653184 | bytes 1 | tf_op jit(solution)/shard_map/banded_products/pallas_call | solution.py:771
  98.0 4.4 %collective-permute-done.15.rest_2_ = bf16[4,32,32,128]{3,2,1,0:T(8,128)(2,1)} collective-permute-done((bf16[4,32,32,128]{3,2,1,0:T(8,128)(2,1)S(1)}, bf16[4,32,32,128]{3,2,1,0:T(8,128)(2,1)}, u32[]{:S(2)}, u32[]{:S(2)}) %collective-permute-start.15) | collective-permute-done | bytes 1048608 | tf_op jit(solution)/shard_map/ppermute | solution.py:939
  102.4 3.4 %banded_products.8.rest_6_ = bf16[4,32,32,128]{3,2,1,0:T(8,128)(2,1)S(1)} custom-call(s32[4]{0:T(128)S(1)} %pad_add_fusion.ids, s32[8]{0:T(128)S(1)} %reshape.9.chosen, bf16[4,32,32,128]{3,2,1,0:T(8,128)(2,1)S(1)} %collective-permute-done.14.rest_0_, bf16[4,32,32,128]{3,2,1,0:T(8,128)(2,1)S(1)} %get-tuple-element.104.rest_1_, ...), custom_call_target="tpu_custom_call" | custom-call | flops 268435456 | bytes 1 | tf_op jit(solution)/shard_map/banded_products/pallas_call | solution.py:771
  108.1 23.4 %collective-permute-done.12.rest_3_ = bf16[4,16,32,128]{3,2,1,0:T(8,128)(2,1)} collective-permute-done((bf16[4,16,32,128]{3,2,1,0:T(8,128)(2,1)}, bf16[4,16,32,128]{3,2,1,0:T(8,128)(2,1)}, u32[]{:S(2)}, u32[]{:S(2)}) %collective-permute-start.12) | collective-permute-done | bytes 524320 | tf_op jit(solution)/shard_map/ppermute | solution.py:968
  131.6 13.2 %close_layer.3 = (bf16[8,32,32,128]{3,2,1,0:T(8,128)(2,1)S(1)}, f32[8,32,32,128]{3,2,1,0:T(8,128)S(1)}, bf16[4,32,32,128]{3,2,1,0:T(8,128)(2,1)S(1)}, bf16[4,20,...) custom-call(s32[4]{0:T(128)S(1)} %pad_add_fusion.ids, ...), custom_call_target="tpu_custom_call" | custom-call | flops 8589934592 | bytes 1048576 | tf_op jit(solution)/shard_map/close_layer/pallas_call | solution.py:911
  146.3 13.2 %close_layer.4 = (bf16[8,32,32,128]{3,2,1,0:T(8,128)(2,1)S(1)}, f32[8,32,32,128]{3,2,1,0:T(8,128)S(1)}, bf16[4,32,32,128]{3,2,1,0:T(8,128)(2,1)S(1)}, bf16[4,20,...) custom-call(s32[4]{0:T(128)S(1)} %pad_add_fusion.ids, ...), custom_call_target="tpu_custom_call", output_to_operand_aliasing={{0}: (16, {}), {1}: (17, {}), {4}: (18, {}), {6}: (19, {})} | custom-call | flops 8589934592 | bytes 1048576 | tf_op jit(solution)/shard_map/close_layer/pallas_call | solution.py:911
  159.7 3.5 %collective-permute-start.18 = (bf16[4,20,32,128]{3,2,1,0:T(8,128)(2,1)S(1)}, bf16[4,20,32,128]{3,2,1,0:T(8,128)(2,1)S(1)}, u32[]{:S(2)}, u32[]{:S(2)}) collective-permute-start(bf16[4,20,32,128]{3,2,1,0:T(8,128)(2,1)S(1)} %collective-permute-done.17.rest_1_), channel_id=1, source_target_pairs={{0,1},{3,2},{4,5},{7,6},{8,9},{11,10},{12,13},{15,14},{16,17},{19,... | collective-permute-start | bytes 1966088 | tf_op jit(solution)/shard_map/ppermute | solution.py:948
  163.2 5.4 %collective-permute-done.19.rest_4_ = bf16[4,20,32,128]{3,2,1,0:T(8,128)(2,1)S(1)} collective-permute-done((bf16[4,20,32,128]{3,2,1,0:T(8,128)(2,1)S(1)}, bf16[4,20,32,128]{3,2,1,0:T(8,128)(2,1)S(1)}, u32[]{:S(2)}, u32[]{:S(2)}) %collective-permute-start.19) | collective-permute-done | bytes 655392 | tf_op jit(solution)/shard_map/ppermute | solution.py:947
  168.6 2.5 collective-permute-done.23.rest_0_.rest_2_
  171.7 8.7 %collective-permute-done.20.rest_6_ = bf16[4,20,32,128]{3,2,1,0:T(8,128)(2,1)S(1)} collective-permute-done((bf16[4,20,32,128]{3,2,1,0:T(8,128)(2,1)S(1)}, bf16[4,20,32,128]{3,2,1,0:T(8,128)(2,1)S(1)}, u32[]{:S(2)}, u32[]{:S(2)}) %collective-permute-start.20) | collective-permute-done | bytes 655392 | tf_op jit(solution)/shard_map/ppermute | solution.py:946
  180.4 6.7 %collective-permute-start.21 = (bf16[4,20,32,128]{3,2,1,0:T(8,128)(2,1)S(1)}, bf16[4,20,32,128]{3,2,1,0:T(8,128)(2,1)S(1)}, u32[]{:S(2)}, u32[]{:S(2)}) collective-permute-start(bf16[4,20,32,128]{3,2,1,0:T(8,128)(2,1)S(1)} %collective-permute-done.20.rest_6_), channel_id=1, source_target_pairs={{0,1},{3,2},{4,5},{7,6},{8,9},{11,10},{12,13},{15,14},{16,17},{19,... | collective-permute-start | bytes 1966088 | tf_op jit(solution)/shard_map/ppermute | solution.py:948
  187.1 5.3 %collective-permute-done.22.rest_9_ = bf16[4,20,32,128]{3,2,1,0:T(8,128)(2,1)S(1)} collective-permute-done((bf16[4,20,32,128]{3,2,1,0:T(8,128)(2,1)S(1)}, bf16[4,20,32,128]{3,2,1,0:T(8,128)(2,1)S(1)}, u32[]{:S(2)}, u32[]{:S(2)}) %collective-permute-start.22) | collective-permute-done | bytes 655392 | tf_op jit(solution)/shard_map/ppermute | solution.py:947
  192.9 5.9 %banded_products.9 = (bf16[4,20,32,128]{3,2,1,0:T(8,128)(2,1)S(1)}, bf16[4,20,32,128]{3,2,1,0:T(8,128)(2,1)S(1)}, bf16[4,20,32,128]{3,2,1,0:T(8,128)(2,1)S(1)}) custom-call(s32[4]{0:T(128)S(1)} %pad_add_fusion.ids, s32[40]{0:T(128)S(1)} %get-tuple-element.76.chosen, bf16[4,20,32,128]{3,2,1,0:T(8,128)(2,1)S(1)} %get-tuple-element.108.rest_0_, ...), custom_call_target="tpu_custom_call" | custom-call | flops 503316480 | bytes 1 | tf_op jit(solution)/shard_map/banded_products/pallas_call | solution.py:771
  199.9 2.8 collective-permute-start.25
  203.2 9.4 %collective-permute-done.26.rest_1_ = bf16[4,20,32,128]{3,2,1,0:T(8,128)(2,1)S(1)} collective-permute-done((bf16[4,20,32,128]{3,2,1,0:T(8,128)(2,1)S(1)}, bf16[4,20,32,128]{3,2,1,0:T(8,128)(2,1)S(1)}, u32[]{:S(2)}, u32[]{:S(2)}) %collective-permute-start.26) | collective-permute-done | bytes 655392 | tf_op jit(solution)/shard_map/ppermute | solution.py:968
  212.6 22.4 %collective-permute-start.28 = (bf16[8,12,32,128]{3,2,1,0:T(8,128)(2,1)S(1)}, bf16[8,12,32,128]{3,2,1,0:T(8,128)(2,1)S(1)}, u32[]{:S(2)}, u32[]{:S(2)}) collective-permute-start(bf16[8,12,32,128]{3,2,1,0:T(8,128)(2,1)S(1)} %collective-permute-done.27.rest_1_), channel_id=1, source_target_pairs={{0,1},{3,2},{4,5},{7,6},{8,9},{11,10},{12,13},{15,14},{16,17},{19,... | collective-permute-start | bytes 2359304 | tf_op jit(solution)/shard_map/ppermute | solution.py:948
  235.0 9.6 %far_operands.3 = (bf16[4,32,32,128]{3,2,1,0:T(8,128)(2,1)S(1)}, bf16[4,32,32,128]{3,2,1,0:T(8,128)(2,1)S(1)}) custom-call(s32[4]{0:T(128)S(1)} %pad_add_fusion.ids, s32[2,32]{1,0:T(2,128)S(1)} %bitcast.21, s32[10]{0:T(128)S(1)} %get-tuple-element.102.mine, bf16[4,32,32,128]{3,2,1,0:T(8,128)(2,1)S(1)} %collective-permute-done.23.rest_0_.rest_2_, ...), custom_call_target="tpu_custom_call" | custom-call | flops 8589934592 | bytes 1048576 | tf_op jit(solution)/shard_map/far_operands/pallas_call | solution.py:633
  245.1 3.5 %banded_products.10 = (bf16[4,12,32,128]{3,2,1,0:T(8,128)(2,1)S(1)}, bf16[4,12,32,128]{3,2,1,0:T(8,128)(2,1)S(1)}, bf16[4,12,32,128]{3,2,1,0:T(8,128)(2,1)S(1)}) custom-call(s32[4]{0:T(128)S(1)} %pad_add_fusion.ids, s32[40]{0:T(128)S(1)} %get-tuple-element.76.chosen, bf16[8,12,32,128]{3,2,1,0:T(8,128)(2,1)S(1)} %get-tuple-element.132.rest_0_, ...), custom_call_target="tpu_custom_call" | custom-call | flops 301989888 | bytes 1 | tf_op jit(solution)/shard_map/banded_products/pallas_call | solution.py:771
  249.8 14.9 %collective-permute-done.32.rest_1_ = bf16[4,32,32,128]{3,2,1,0:T(8,128)(2,1)S(1)} collective-permute-done((bf16[4,32,32,128]{3,2,1,0:T(8,128)(2,1)S(1)}, bf16[4,32,32,128]{3,2,1,0:T(8,128)(2,1)S(1)}, u32[]{:S(2)}, u32[]{:S(2)}) %collective-permute-start.32) | collective-permute-done | bytes 1048608 | tf_op jit(solution)/shard_map/ppermute | solution.py:946
  267.2 13.6 %collective-permute-done.34.rest_4_ = bf16[4,32,32,128]{3,2,1,0:T(8,128)(2,1)S(1)} collective-permute-done((bf16[4,32,32,128]{3,2,1,0:T(8,128)(2,1)S(1)}, bf16[4,32,32,128]{3,2,1,0:T(8,128)(2,1)S(1)}, u32[]{:S(2)}, u32[]{:S(2)}) %collective-permute-start.34) | collective-permute-done | bytes 1048608 | tf_op jit(solution)/shard_map/ppermute | solution.py:947
  280.8 2.4 banded_products.11.rest_6_
  283.2 8.8 %close_layer.5 = bf16[8,32,32,128]{3,2,1,0:T(8,128)(2,1)} custom-call(s32[4]{0:T(128)S(1)} %pad_add_fusion.ids, s32[2,32]{1,0:T(2,128)S(1)} %bitcast.22, s32[16]{0:T(128)S(1)} %get-tuple-element.91.place, bf16[4,20,32,128]{3,2,1,0:T(8,128)(2,1)S(1)} %collective-permute-done.25.rest_0_, bf16[4,20,32,128]{3,2,1,0:T(8,128)(2,1)S(1)} %collective-permute-done.26.rest_1_, ...), custom_call_target="tpu_custom_call" | custom-call | flops 8589934592 | bytes 1048576 | tf_op jit(solution)/shard_map/close_layer/pallas_call | solution.py:911
  (95 shorter events, 33.0 us)
Async XLA Ops:
  0.0 52.5 %collective-permute-start.6 = (bf16[8,32,32,128]{3,2,1,0:T(8,128)(2,1)}, bf16[8,32,32,128]{3,2,1,0:T(8,128)(2,1)}, u32[]{:S(2)}, u32[]{:S(2)}) collective-permute-start(bf16[8,32,32,128]{3,2,1,0:T(8,128)(2,1)} %rest_7_.3), channel_id=1, source_target_pairs={{0,4},{4,8},{8,12},{12,0},{1,5},{5,9},{9,13},{13,1},{2,6},{6,10},{... | collective-permute-start | bytes 6291464 | tf_op jit(solution)/shard_map/ppermute | solution.py:968
  11.6 14.6 %collective-permute-start.2 = (bf16[4,16,32,128]{3,2,1,0:T(8,128)(2,1)S(1)}, bf16[4,16,32,128]{3,2,1,0:T(8,128)(2,1)S(1)}, u32[]{:S(2)}, u32[]{:S(2)}) collective-permute-start(bf16[4,16,32,128]{3,2,1,0:T(8,128)(2,1)S(1)} %get-tuple-element.78.rest_3_), channel_id=1, source_target_pairs={{1,2},{2,1},{5,6},{6,5},{9,10},{10,9},{13,14},{14,13},{17,18},{18,... | collective-permute-start | bytes 1572872 | tf_op jit(solution)/shard_map/ppermute | solution.py:940
  12.3 14.1 %collective-permute-start.1 = (bf16[4,16,32,128]{3,2,1,0:T(8,128)(2,1)S(1)}, bf16[4,16,32,128]{3,2,1,0:T(8,128)(2,1)S(1)}, u32[]{:S(2)}, u32[]{:S(2)}) collective-permute-start(bf16[4,16,32,128]{3,2,1,0:T(8,128)(2,1)S(1)} %get-tuple-element.78.rest_3_), channel_id=1, source_target_pairs={{0,2},{3,1},{1,0},{2,3},{4,6},{7,5},{5,4},{6,7},{8,10},{11,9},{9,8... | collective-permute-start | bytes 1572872 | tf_op jit(solution)/shard_map/ppermute | solution.py:939
  29.3 13.5 %collective-permute-start.4 = (bf16[4,16,32,128]{3,2,1,0:T(8,128)(2,1)S(1)}, bf16[4,16,32,128]{3,2,1,0:T(8,128)(2,1)S(1)}, u32[]{:S(2)}, u32[]{:S(2)}) collective-permute-start(bf16[4,16,32,128]{3,2,1,0:T(8,128)(2,1)S(1)} %get-tuple-element.85.rest_8_), channel_id=1, source_target_pairs={{0,2},{3,1},{1,0},{2,3},{4,6},{7,5},{5,4},{6,7},{8,10},{11,9},{9,8... | collective-permute-start | bytes 1572872 | tf_op jit(solution)/shard_map/ppermute | solution.py:939
  47.3 18.6 %collective-permute-start.11 = (bf16[8,16,32,128]{3,2,1,0:T(8,128)(2,1)S(1)}, bf16[8,16,32,128]{3,2,1,0:T(8,128)(2,1)S(1)}, u32[]{:S(2)}, u32[]{:S(2)}) collective-permute-start(bf16[8,16,32,128]{3,2,1,0:T(8,128)(2,1)S(1)} %get-tuple-element.96.rest_3_), channel_id=1, source_target_pairs={{1,2},{2,1},{5,6},{6,5},{9,10},{10,9},{13,14},{14,13},{17,18},{18,... | collective-permute-start | bytes 3145736 | tf_op jit(solution)/shard_map/ppermute | solution.py:940
  48.0 41.9 %collective-permute-start.10 = (bf16[8,16,32,128]{3,2,1,0:T(8,128)(2,1)S(1)}, bf16[8,16,32,128]{3,2,1,0:T(8,128)(2,1)S(1)}, u32[]{:S(2)}, u32[]{:S(2)}) collective-permute-start(bf16[8,16,32,128]{3,2,1,0:T(8,128)(2,1)S(1)} %get-tuple-element.96.rest_3_), channel_id=1, source_target_pairs={{0,2},{3,1},{1,0},{2,3},{4,6},{7,5},{5,4},{6,7},{8,10},{11,9},{9,8... | collective-permute-start | bytes 3145736 | tf_op jit(solution)/shard_map/ppermute | solution.py:939
  52.5 37.4 %collective-permute-start.9 = (bf16[8,16,32,128]{3,2,1,0:T(8,128)(2,1)S(1)}, bf16[8,16,32,128]{3,2,1,0:T(8,128)(2,1)S(1)}, u32[]{:S(2)}, u32[]{:S(2)}) collective-permute-start(bf16[8,16,32,128]{3,2,1,0:T(8,128)(2,1)S(1)} %get-tuple-element.94.rest_1_), channel_id=1, source_target_pairs={{0,1},{1,0},{2,3},{3,2},{4,5},{5,4},{6,7},{7,6},{8,9},{9,8},{10,11... | collective-permute-start | bytes 3145736 | tf_op jit(solution)/shard_map/ppermute | solution.py:938
  52.5 22.7 %collective-permute-start.8 = (bf16[4,16,32,128]{3,2,1,0:T(8,128)(2,1)S(1)}, bf16[4,16,32,128]{3,2,1,0:T(8,128)(2,1)S(1)}, u32[]{:S(2)}, u32[]{:S(2)}) collective-permute-start(bf16[4,16,32,128]{3,2,1,0:T(8,128)(2,1)S(1)} %get-tuple-element.89), channel_id=1, source_target_pairs={{0,12},{4,0},{8,4},{12,8},{1,13},{5,1},{9,5},{13,9},{2,14},{6,2},{... | collective-permute-start | bytes 1572872 | tf_op jit(solution)/shard_map/ppermute | solution.py:968
  52.6 36.0 %collective-permute-start.7 = (bf16[4,16,32,128]{3,2,1,0:T(8,128)(2,1)S(1)}, bf16[4,16,32,128]{3,2,1,0:T(8,128)(2,1)S(1)}, u32[]{:S(2)}, u32[]{:S(2)}) collective-permute-start(bf16[4,16,32,128]{3,2,1,0:T(8,128)(2,1)S(1)} %get-tuple-element.87), channel_id=1, source_target_pairs={{0,8},{4,12},{8,0},{12,4},{1,9},{5,13},{9,1},{13,5},{2,10},{6,14},... | collective-permute-start | bytes 1572872 | tf_op jit(solution)/shard_map/ppermute | solution.py:968
  65.9 32.1 %collective-permute-start.14 = (bf16[4,32,32,128]{3,2,1,0:T(8,128)(2,1)S(1)}, bf16[4,32,32,128]{3,2,1,0:T(8,128)(2,1)S(1)}, u32[]{:S(2)}, u32[]{:S(2)}) collective-permute-start(bf16[4,32,32,128]{3,2,1,0:T(8,128)(2,1)S(1)} %get-tuple-element.104.rest_1_), channel_id=1, source_target_pairs={{0,1},{1,0},{2,3},{3,2},{4,5},{5,4},{6,7},{7,6},{8,9},{9,8},{10,11... | collective-permute-start | bytes 3145736 | tf_op jit(solution)/shard_map/ppermute | solution.py:938
  75.1 22.9 %collective-permute-start.16 = (bf16[4,32,32,128]{3,2,1,0:T(8,128)(2,1)S(1)}, bf16[4,32,32,128]{3,2,1,0:T(8,128)(2,1)}, u32[]{:S(2)}, u32[]{:S(2)}) collective-permute-start(bf16[4,32,32,128]{3,2,1,0:T(8,128)(2,1)S(1)} %get-tuple-element.105.rest_3_), channel_id=1, source_target_pairs={{1,2},{2,1},{5,6},{6,5},{9,10},{10,9},{13,14},{14,13},{17,18},{18,... | collective-permute-start | bytes 3145736 | tf_op jit(solution)/shard_map/ppermute | solution.py:940
  88.6 13.7 %collective-permute-start.15 = (bf16[4,32,32,128]{3,2,1,0:T(8,128)(2,1)S(1)}, bf16[4,32,32,128]{3,2,1,0:T(8,128)(2,1)}, u32[]{:S(2)}, u32[]{:S(2)}) collective-permute-start(bf16[4,32,32,128]{3,2,1,0:T(8,128)(2,1)S(1)} %get-tuple-element.105.rest_3_), channel_id=1, source_target_pairs={{0,2},{3,1},{1,0},{2,3},{4,6},{7,5},{5,4},{6,7},{8,10},{11,9},{9,8... | collective-permute-start | bytes 3145736 | tf_op jit(solution)/shard_map/ppermute | solution.py:939
  94.2 14.0 %collective-permute-start.13 = (bf16[4,16,32,128]{3,2,1,0:T(8,128)(2,1)}, bf16[4,16,32,128]{3,2,1,0:T(8,128)(2,1)}, u32[]{:S(2)}, u32[]{:S(2)}) collective-permute-start(bf16[4,16,32,128]{3,2,1,0:T(8,128)(2,1)} %get-tuple-element.100), channel_id=1, source_target_pairs={{0,12},{4,0},{8,4},{12,8},{1,13},{5,1},{9,5},{13,9},{2,14},{6,2},{... | collective-permute-start | bytes 1572872 | tf_op jit(solution)/shard_map/ppermute | solution.py:968
  95.2 36.4 %collective-permute-start.12 = (bf16[4,16,32,128]{3,2,1,0:T(8,128)(2,1)}, bf16[4,16,32,128]{3,2,1,0:T(8,128)(2,1)}, u32[]{:S(2)}, u32[]{:S(2)}) collective-permute-start(bf16[4,16,32,128]{3,2,1,0:T(8,128)(2,1)} %get-tuple-element.98), channel_id=1, source_target_pairs={{0,8},{4,12},{8,0},{12,4},{1,9},{5,13},{9,1},{13,5},{2,10},{6,14},... | collective-permute-start | bytes 1572872 | tf_op jit(solution)/shard_map/ppermute | solution.py:968
  144.8 14.8 %collective-permute-start.17 = (bf16[4,20,32,128]{3,2,1,0:T(8,128)(2,1)S(1)}, bf16[4,20,32,128]{3,2,1,0:T(8,128)(2,1)S(1)}, u32[]{:S(2)}, u32[]{:S(2)}) collective-permute-start(bf16[4,20,32,128]{3,2,1,0:T(8,128)(2,1)S(1)} %get-tuple-element.108.rest_0_), channel_id=1, source_target_pairs={{1,3},{2,0},{0,1},{3,2},{5,7},{6,4},{4,5},{7,6},{9,11},{10,8},{8,9... | collective-permute-start | bytes 1966088 | tf_op jit(solution)/shard_map/ppermute | solution.py:946
  145.0 23.6 %collective-permute-start.19 = (bf16[4,20,32,128]{3,2,1,0:T(8,128)(2,1)S(1)}, bf16[4,20,32,128]{3,2,1,0:T(8,128)(2,1)S(1)}, u32[]{:S(2)}, u32[]{:S(2)}) collective-permute-start(bf16[4,20,32,128]{3,2,1,0:T(8,128)(2,1)S(1)} %get-tuple-element.115.rest_3_), channel_id=1, source_target_pairs={{0,2},{2,0},{1,3},{3,1},{4,6},{6,4},{5,7},{7,5},{8,10},{10,8},{9,1... | collective-permute-start | bytes 1966088 | tf_op jit(solution)/shard_map/ppermute | solution.py:947
  146.3 24.8 %collective-permute-start.23 = (bf16[4,32,32,128]{3,2,1,0:T(8,128)(2,1)S(1)}, bf16[4,32,32,128]{3,2,1,0:T(8,128)(2,1)S(1)}, u32[]{:S(2)}, u32[]{:S(2)}) collective-permute-start(bf16[4,32,32,128]{3,2,1,0:T(8,128)(2,1)S(1)} %get-tuple-element.123), channel_id=1, source_target_pairs={{0,4},{4,8},{8,12},{12,0},{1,5},{5,9},{9,13},{13,1},{2,6},{6,10},{... | collective-permute-start | bytes 3145736 | tf_op jit(solution)/shard_map/ppermute | solution.py:968
  159.7 12.0 %collective-permute-start.18 = (bf16[4,20,32,128]{3,2,1,0:T(8,128)(2,1)S(1)}, bf16[4,20,32,128]{3,2,1,0:T(8,128)(2,1)S(1)}, u32[]{:S(2)}, u32[]{:S(2)}) collective-permute-start(bf16[4,20,32,128]{3,2,1,0:T(8,128)(2,1)S(1)} %collective-permute-done.17.rest_1_), channel_id=1, source_target_pairs={{0,1},{3,2},{4,5},{7,6},{8,9},{11,10},{12,13},{15,14},{16,17},{19,... | collective-permute-start | bytes 1966088 | tf_op jit(solution)/shard_map/ppermute | solution.py:948
  168.6 11.8 %collective-permute-start.20 = (bf16[4,20,32,128]{3,2,1,0:T(8,128)(2,1)S(1)}, bf16[4,20,32,128]{3,2,1,0:T(8,128)(2,1)S(1)}, u32[]{:S(2)}, u32[]{:S(2)}) collective-permute-start(bf16[4,20,32,128]{3,2,1,0:T(8,128)(2,1)S(1)} %get-tuple-element.117.rest_5_), channel_id=1, source_target_pairs={{1,3},{2,0},{0,1},{3,2},{5,7},{6,4},{4,5},{7,6},{9,11},{10,8},{8,9... | collective-permute-start | bytes 1966088 | tf_op jit(solution)/shard_map/ppermute | solution.py:946
  171.1 27.7 %collective-permute-start.24 = (bf16[4,32,32,128]{3,2,1,0:T(8,128)(2,1)S(1)}, bf16[4,32,32,128]{3,2,1,0:T(8,128)(2,1)S(1)}, u32[]{:S(2)}, u32[]{:S(2)}) collective-permute-start(bf16[4,32,32,128]{3,2,1,0:T(8,128)(2,1)S(1)} %get-tuple-element.124), channel_id=1, source_target_pairs={{0,4},{4,8},{8,12},{12,0},{1,5},{5,9},{9,13},{13,1},{2,6},{6,10},{... | collective-permute-start | bytes 3145736 | tf_op jit(solution)/shard_map/ppermute | solution.py:968
  171.7 20.7 %collective-permute-start.22 = (bf16[4,20,32,128]{3,2,1,0:T(8,128)(2,1)S(1)}, bf16[4,20,32,128]{3,2,1,0:T(8,128)(2,1)S(1)}, u32[]{:S(2)}, u32[]{:S(2)}) collective-permute-start(bf16[4,20,32,128]{3,2,1,0:T(8,128)(2,1)S(1)} %get-tuple-element.120.rest_8_), channel_id=1, source_target_pairs={{0,2},{2,0},{1,3},{3,1},{4,6},{6,4},{5,7},{7,5},{8,10},{10,8},{9,1... | collective-permute-start | bytes 1966088 | tf_op jit(solution)/shard_map/ppermute | solution.py:947
  180.4 12.0 %collective-permute-start.21 = (bf16[4,20,32,128]{3,2,1,0:T(8,128)(2,1)S(1)}, bf16[4,20,32,128]{3,2,1,0:T(8,128)(2,1)S(1)}, u32[]{:S(2)}, u32[]{:S(2)}) collective-permute-start(bf16[4,20,32,128]{3,2,1,0:T(8,128)(2,1)S(1)} %collective-permute-done.20.rest_6_), channel_id=1, source_target_pairs={{0,1},{3,2},{4,5},{7,6},{8,9},{11,10},{12,13},{15,14},{16,17},{19,... | collective-permute-start | bytes 1966088 | tf_op jit(solution)/shard_map/ppermute | solution.py:948
  192.4 10.8 %collective-permute-start.27 = (bf16[8,12,32,128]{3,2,1,0:T(8,128)(2,1)S(1)}, bf16[8,12,32,128]{3,2,1,0:T(8,128)(2,1)S(1)}, u32[]{:S(2)}, u32[]{:S(2)}) collective-permute-start(bf16[8,12,32,128]{3,2,1,0:T(8,128)(2,1)S(1)} %get-tuple-element.132.rest_0_), channel_id=1, source_target_pairs={{1,3},{2,0},{0,1},{3,2},{5,7},{6,4},{4,5},{7,6},{9,11},{10,8},{8,9... | collective-permute-start | bytes 2359304 | tf_op jit(solution)/shard_map/ppermute | solution.py:946
  198.8 13.8 %collective-permute-start.26 = (bf16[4,20,32,128]{3,2,1,0:T(8,128)(2,1)S(1)}, bf16[4,20,32,128]{3,2,1,0:T(8,128)(2,1)S(1)}, u32[]{:S(2)}, u32[]{:S(2)}) collective-permute-start(bf16[4,20,32,128]{3,2,1,0:T(8,128)(2,1)S(1)} %get-tuple-element.127), channel_id=1, source_target_pairs={{0,12},{4,0},{8,4},{12,8},{1,13},{5,1},{9,5},{13,9},{2,14},{6,2},{... | collective-permute-start | bytes 1966088 | tf_op jit(solution)/shard_map/ppermute | solution.py:968
  199.3 45.8 %collective-permute-start.29 = (bf16[8,12,32,128]{3,2,1,0:T(8,128)(2,1)S(1)}, bf16[8,12,32,128]{3,2,1,0:T(8,128)(2,1)S(1)}, u32[]{:S(2)}, u32[]{:S(2)}) collective-permute-start(bf16[8,12,32,128]{3,2,1,0:T(8,128)(2,1)S(1)} %get-tuple-element.134.rest_3_), channel_id=1, source_target_pairs={{0,2},{2,0},{1,3},{3,1},{4,6},{6,4},{5,7},{7,5},{8,10},{10,8},{9,1... | collective-permute-start | bytes 2359304 | tf_op jit(solution)/shard_map/ppermute | solution.py:947
  199.9 45.2 %collective-permute-start.25 = (bf16[4,20,32,128]{3,2,1,0:T(8,128)(2,1)S(1)}, bf16[4,20,32,128]{3,2,1,0:T(8,128)(2,1)S(1)}, u32[]{:S(2)}, u32[]{:S(2)}) collective-permute-start(bf16[4,20,32,128]{3,2,1,0:T(8,128)(2,1)S(1)} %get-tuple-element.125), channel_id=1, source_target_pairs={{0,8},{4,12},{8,0},{12,4},{1,9},{5,13},{9,1},{13,5},{2,10},{6,14},... | collective-permute-start | bytes 1966088 | tf_op jit(solution)/shard_map/ppermute | solution.py:968
  212.6 32.5 %collective-permute-start.28 = (bf16[8,12,32,128]{3,2,1,0:T(8,128)(2,1)S(1)}, bf16[8,12,32,128]{3,2,1,0:T(8,128)(2,1)S(1)}, u32[]{:S(2)}, u32[]{:S(2)}) collective-permute-start(bf16[8,12,32,128]{3,2,1,0:T(8,128)(2,1)S(1)} %collective-permute-done.27.rest_1_), channel_id=1, source_target_pairs={{0,1},{3,2},{4,5},{7,6},{8,9},{11,10},{12,13},{15,14},{16,17},{19,... | collective-permute-start | bytes 2359304 | tf_op jit(solution)/shard_map/ppermute | solution.py:948
  244.6 20.0 %collective-permute-start.32 = (bf16[4,32,32,128]{3,2,1,0:T(8,128)(2,1)S(1)}, bf16[4,32,32,128]{3,2,1,0:T(8,128)(2,1)S(1)}, u32[]{:S(2)}, u32[]{:S(2)}) collective-permute-start(bf16[4,32,32,128]{3,2,1,0:T(8,128)(2,1)S(1)} %get-tuple-element.142.rest_0_), channel_id=1, source_target_pairs={{1,3},{2,0},{0,1},{3,2},{5,7},{6,4},{4,5},{7,6},{9,11},{10,8},{8,9... | collective-permute-start | bytes 3145736 | tf_op jit(solution)/shard_map/ppermute | solution.py:946
  248.7 16.0 %collective-permute-start.31 = (bf16[4,12,32,128]{3,2,1,0:T(8,128)(2,1)S(1)}, bf16[4,12,32,128]{3,2,1,0:T(8,128)(2,1)S(1)}, u32[]{:S(2)}, u32[]{:S(2)}) collective-permute-start(bf16[4,12,32,128]{3,2,1,0:T(8,128)(2,1)S(1)} %get-tuple-element.138), channel_id=1, source_target_pairs={{0,12},{4,0},{8,4},{12,8},{1,13},{5,1},{9,5},{13,9},{2,14},{6,2},{... | collective-permute-start | bytes 1179656 | tf_op jit(solution)/shard_map/ppermute | solution.py:968
  248.7 32.1 %collective-permute-start.34 = (bf16[4,32,32,128]{3,2,1,0:T(8,128)(2,1)S(1)}, bf16[4,32,32,128]{3,2,1,0:T(8,128)(2,1)S(1)}, u32[]{:S(2)}, u32[]{:S(2)}) collective-permute-start(bf16[4,32,32,128]{3,2,1,0:T(8,128)(2,1)S(1)} %get-tuple-element.144.rest_3_), channel_id=1, source_target_pairs={{0,2},{2,0},{1,3},{3,1},{4,6},{6,4},{5,7},{7,5},{8,10},{10,8},{9,1... | collective-permute-start | bytes 3145736 | tf_op jit(solution)/shard_map/ppermute | solution.py:947
  264.7 16.1 %collective-permute-start.33 = (bf16[4,32,32,128]{3,2,1,0:T(8,128)(2,1)S(1)}, bf16[4,32,32,128]{3,2,1,0:T(8,128)(2,1)S(1)}, u32[]{:S(2)}, u32[]{:S(2)}) collective-permute-start(bf16[4,32,32,128]{3,2,1,0:T(8,128)(2,1)S(1)} %collective-permute-done.32.rest_1_), channel_id=1, source_target_pairs={{0,1},{3,2},{4,5},{7,6},{8,9},{11,10},{12,13},{15,14},{16,17},{19,... | collective-permute-start | bytes 3145736 | tf_op jit(solution)/shard_map/ppermute | solution.py:948
  266.0 17.1 %collective-permute-start.30 = (bf16[4,12,32,128]{3,2,1,0:T(8,128)(2,1)S(1)}, bf16[4,12,32,128]{3,2,1,0:T(8,128)(2,1)S(1)}, u32[]{:S(2)}, u32[]{:S(2)}) collective-permute-start(bf16[4,12,32,128]{3,2,1,0:T(8,128)(2,1)S(1)} %get-tuple-element.136), channel_id=1, source_target_pairs={{0,8},{4,12},{8,0},{12,4},{1,9},{5,13},{9,1},{13,5},{2,10},{6,14},... | collective-permute-start | bytes 1179656 | tf_op jit(solution)/shard_map/ppermute | solution.py:968
  (22 other events, 324.0 us)

commit v16 on v15

--- a/solution.py
+++ b/solution.py
@@ -838,10 +838,10 @@
     for row in range(0, rows, half):
         for band in range(0, bands, half):
             taken = pl.ds(band, half), pl.ds(row, half)
-            total = held[(place[(base + step) * terms], *taken)].astype(jnp.float32)
-            for t in range(1, terms):
-                total = total + held[(place[(base + step) * terms + t], *taken)].astype(jnp.float32)
-            moved = swapped(total.astype(jnp.bfloat16), swap)
+            each = [held[(place[(base + step) * terms + t], *taken)] for t in range(terms)]
+            each = jnp.concatenate([x.reshape(half * half, hidden) for x in each])
+            total = dot(jnp.concatenate([swap[...]] * terms, axis=1), each)
+            moved = total.astype(jnp.bfloat16).reshape(half, half, hidden)
             for r in range(half):
                 by_row[row + r].append(moved[r])
     groups = rows // parts
@@ -958,7 +958,7 @@
     near = [s for n, s in enumerate(near) if s not in near[:n]] + [0]
     layers = w_in.shape[0]
     current = pair
-    bands = [[16, 16], [20, 12]]
+    bands = [[16, 16], [18, 14]]
     chosen, place, mine = make_plan(ids, owners, slot_of, n_blk, far, slots, terms, capacity)
     in_order = jnp.repeat(jnp.arange(capacity, dtype=jnp.int32), 2)
     half = slots // 2
@@ -1020,7 +1020,7 @@
                 far_left, far_right = far_operands(
                     layer, ids, blocks, mine, sources, chains, wide, far, capacity, slots, hidden
                 )
-        far_exchanged = [exchange(far_left, far_right, list(by_shift.values())[-1] if by_shift else made[-1])]
+        far_exchanged = [exchange(far_left, far_right, made[-1])]
         (part,) = banded_products([0], ids, in_order, far_exchanged, capacity, cols)
         arrived.append((part, far, 0))
         last = layer == layers - 1

time: 294 us -> 303 us (1.031)
  waiting for transfers between devices: 112 us -> 132 us
  starting transfers between devices: 76.7 us -> 63.4 us
    ppermute x11, waiting for transfers between devices: 49.9 us -> 90.7 us  [over_blk(): lax.ppermute(value, 'blk', [(p, (p + shift) % n_blk) for p in range(n_blk)])]
    ppermute x4, waiting for transfers between devices: 24.2 us -> 4.76 us  [exchange_bands_incoming(): one = lax.ppermute(left, both, [(1, 3), (2, 0), (0, 1), (3, 2)])]
    ppermute x4, starting transfers between devices: 34 us -> 16.9 us  [exchange_bands_incoming(): lax.ppermute(after(one, other if over is None else over), both, [(0, 1),...]
  transfers between devices with their start and end apart: 35 -> 35, of which waited for: 16 -> 16; matrix products, arithmetic and copies ran while one was open for 0% -> 0% of each run, Pallas kernels for 26% -> 25%
where the time goes in v16:
time: 303 us; the launch traced here: 301 us
  waiting for transfers between devices  132 us (44%)
  Pallas kernels  99.9 us (33%)
  starting transfers between devices  63.4 us (21%)
  local copies, waits for them, and re-layouts  5.01 us (2%)
    ppermute x11, waiting for transfers between devices, over_blk(): lax.ppermute(value, 'blk', [(p, (p + shift) % n_blk) for p in range(n_blk)])  90.7 us
    pallas_call x3, Pallas kernels, close_layer(): pl.pallas_call(functools.partial(close_kernel, *(layer, last, spots, 0 if...  37.6 us
    ppermute x4, waiting for transfers between devices, exchange_bands_incoming(): other = lax.ppermute(right, 'chan', [(0, 1), (1, 0)])  22.4 us
    pallas_call x6, Pallas kernels, banded_products(): pl.pallas_call(functools.partial(banded_kernel, shifts, capacity, tuple(p...  22.3 us
    pallas_call x2, Pallas kernels, far_operands(): pl.pallas_call(functools.partial(far_kernel, layer, n_blk, far, lax.axis_...  20.6 us
    ppermute x4, starting transfers between devices, exchange_bands_incoming(): lax.ppermute(after(one, other if over is None else over), both, [(0, 1),...  16.9 us
    pallas_call x2, Pallas kernels, open_operands(): pl.pallas_call(functools.partial(open_kernel, hidden, len(bands), lax.axi...  16.6 us
    ppermute x11, starting transfers between devices, over_blk(): lax.ppermute(value, 'blk', [(p, (p + shift) % n_blk) for p in range(n_blk)])  14.4 us
  transfers between devices with their start and end apart: 35, of which 16 were waited for; matrix products, arithmetic and copies ran while one was open for 0% of the time, Pallas kernels for 25%

profile of v16, /device:TPU:11, one launch (start us, length us, event | category | flops | bytes accessed | tf_op | source)
XLA Modules:
  0.0 300.6 jit_solution(9733015610872529489)
XLA Ops:
  3.3 8.3 %open_operands.2 = (f32[8,32,32,128]{3,2,1,0:T(8,128)S(1)}, bf16[4,16,32,128]{3,2,1,0:T(8,128)(2,1)S(1)}, bf16[8,16,32,128]{3,2,1,0:T(8,128)(2,1)S(1)}, bf16[4,1...) custom-call(s32[4]{0:T(128)S(1)} %pad_add_fusion.ids, s32[2,32]{1,0:T(2,128)S(1)} %bitcast.16, ...), custom_call_target="tpu_custom_call" | custom-call | flops 8589934592 | bytes 1048576 | tf_op jit(solution)/shard_map/open_operands/pallas_call | solution.py:567
  12.3 3.5 %collective-permute-start.1 = (bf16[4,16,32,128]{3,2,1,0:T(8,128)(2,1)S(1)}, bf16[4,16,32,128]{3,2,1,0:T(8,128)(2,1)S(1)}, u32[]{:S(2)}, u32[]{:S(2)}) collective-permute-start(bf16[4,16,32,128]{3,2,1,0:T(8,128)(2,1)S(1)} %get-tuple-element.78.rest_3_), channel_id=1, source_target_pairs={{0,2},{3,1},{1,0},{2,3},{4,6},{7,5},{5,4},{6,7},{8,10},{11,9},{9,8... | collective-permute-start | bytes 1572872 | tf_op jit(solution)/shard_map/ppermute | solution.py:939
  15.8 8.3 %open_operands.3 = (f32[8,32,32,128]{3,2,1,0:T(8,128)S(1)}, bf16[4,16,32,128]{3,2,1,0:T(8,128)(2,1)S(1)}, bf16[8,16,32,128]{3,2,1,0:T(8,128)(2,1)S(1)}, bf16[4,1...) custom-call(s32[4]{0:T(128)S(1)} %pad_add_fusion.ids, ...), custom_call_target="tpu_custom_call", output_to_operand_aliasing={{0}: (6, {}), {2}: (7, {}), {4}: (8, {})} | custom-call | flops 8589934592 | bytes 1048576 | tf_op jit(solution)/shard_map/open_operands/pallas_call | solution.py:567
  33.6 9.2 %collective-permute-done.4.rest_7_ = bf16[4,16,32,128]{3,2,1,0:T(8,128)(2,1)S(1)} collective-permute-done((bf16[4,16,32,128]{3,2,1,0:T(8,128)(2,1)S(1)}, bf16[4,16,32,128]{3,2,1,0:T(8,128)(2,1)S(1)}, u32[]{:S(2)}, u32[]{:S(2)}) %collective-permute-start.4) | collective-permute-done | bytes 524320 | tf_op jit(solution)/shard_map/ppermute | solution.py:939
  42.9 3.6 %banded_products.6 = (bf16[4,16,32,128]{3,2,1,0:T(8,128)(2,1)S(1)}, bf16[4,16,32,128]{3,2,1,0:T(8,128)(2,1)S(1)}, bf16[4,16,32,128]{3,2,1,0:T(8,128)(2,1)S(1)}) custom-call(s32[4]{0:T(128)S(1)} %pad_add_fusion.ids, s32[40]{0:T(128)S(1)} %get-tuple-element.76.chosen, bf16[4,16,32,128]{3,2,1,0:T(8,128)(2,1)S(1)} %collective-permute-done.rest_0_, ...), custom_call_target="tpu_custom_call" | custom-call | flops 402653184 | bytes 1 | tf_op jit(solution)/shard_map/banded_products/pallas_call | solution.py:771
  48.0 4.4 %collective-permute-start.10 = (bf16[8,16,32,128]{3,2,1,0:T(8,128)(2,1)S(1)}, bf16[8,16,32,128]{3,2,1,0:T(8,128)(2,1)S(1)}, u32[]{:S(2)}, u32[]{:S(2)}) collective-permute-start(bf16[8,16,32,128]{3,2,1,0:T(8,128)(2,1)S(1)} %get-tuple-element.96.rest_3_), channel_id=1, source_target_pairs={{0,2},{3,1},{1,0},{2,3},{4,6},{7,5},{5,4},{6,7},{8,10},{11,9},{9,8... | collective-permute-start | bytes 3145736 | tf_op jit(solution)/shard_map/ppermute | solution.py:939
  54.9 10.9 %far_operands.2 = (bf16[4,32,32,128]{3,2,1,0:T(8,128)(2,1)S(1)}, bf16[4,32,32,128]{3,2,1,0:T(8,128)(2,1)S(1)}) custom-call(s32[4]{0:T(128)S(1)} %pad_add_fusion.ids, s32[2,32]{1,0:T(2,128)S(1)} %bitcast.18, s32[10]{0:T(128)S(1)} %get-tuple-element.102.mine, bf16[8,32,32,128]{3,2,1,0:T(8,128)(2,1)} %collective-permute-done.6.rest_0_.rest_1_, ...), custom_call_target="tpu_custom_call" | custom-call | flops 8589934592 | bytes 1048576 | tf_op jit(solution)/shard_map/far_operands/pallas_call | solution.py:633
  65.9 9.2 %collective-permute-start.14 = (bf16[4,32,32,128]{3,2,1,0:T(8,128)(2,1)S(1)}, bf16[4,32,32,128]{3,2,1,0:T(8,128)(2,1)S(1)}, u32[]{:S(2)}, u32[]{:S(2)}) collective-permute-start(bf16[4,32,32,128]{3,2,1,0:T(8,128)(2,1)S(1)} %get-tuple-element.104.rest_1_), channel_id=1, source_target_pairs={{0,1},{1,0},{2,3},{3,2},{4,5},{5,4},{6,7},{7,6},{8,9},{9,8},{10,11... | collective-permute-start | bytes 3145736 | tf_op jit(solution)/shard_map/ppermute | solution.py:938
  76.8 11.9 %collective-permute-done.7.rest_0_ = bf16[4,16,32,128]{3,2,1,0:T(8,128)(2,1)S(1)} collective-permute-done((bf16[4,16,32,128]{3,2,1,0:T(8,128)(2,1)S(1)}, bf16[4,16,32,128]{3,2,1,0:T(8,128)(2,1)S(1)}, u32[]{:S(2)}, u32[]{:S(2)}) %collective-permute-start.7) | collective-permute-done | bytes 524320 | tf_op jit(solution)/shard_map/ppermute | solution.py:968
  89.9 3.5 %banded_products.7 = (bf16[4,16,32,128]{3,2,1,0:T(8,128)(2,1)}, bf16[4,16,32,128]{3,2,1,0:T(8,128)(2,1)}, bf16[4,16,32,128]{3,2,1,0:T(8,128)(2,1)S(1)}) custom-call(s32[4]{0:T(128)S(1)} %pad_add_fusion.ids, s32[40]{0:T(128)S(1)} %get-tuple-element.76.chosen, bf16[8,16,32,128]{3,2,1,0:T(8,128)(2,1)S(1)} %collective-permute-done.9.rest_0_, ...), custom_call_target="tpu_custom_call" | custom-call | flops 402653184 | bytes 1 | tf_op jit(solution)/shard_map/banded_products/pallas_call | solution.py:771
  98.0 4.4 %collective-permute-done.15.rest_2_ = bf16[4,32,32,128]{3,2,1,0:T(8,128)(2,1)} collective-permute-done((bf16[4,32,32,128]{3,2,1,0:T(8,128)(2,1)S(1)}, bf16[4,32,32,128]{3,2,1,0:T(8,128)(2,1)}, u32[]{:S(2)}, u32[]{:S(2)}) %collective-permute-start.15) | collective-permute-done | bytes 1048608 | tf_op jit(solution)/shard_map/ppermute | solution.py:939
  102.4 3.4 %banded_products.8.rest_6_ = bf16[4,32,32,128]{3,2,1,0:T(8,128)(2,1)S(1)} custom-call(s32[4]{0:T(128)S(1)} %pad_add_fusion.ids, s32[8]{0:T(128)S(1)} %reshape.9.chosen, bf16[4,32,32,128]{3,2,1,0:T(8,128)(2,1)S(1)} %collective-permute-done.14.rest_0_, bf16[4,32,32,128]{3,2,1,0:T(8,128)(2,1)S(1)} %get-tuple-element.104.rest_1_, ...), custom_call_target="tpu_custom_call" | custom-call | flops 268435456 | bytes 1 | tf_op jit(solution)/shard_map/banded_products/pallas_call | solution.py:771
  108.1 23.4 %collective-permute-done.12.rest_3_ = bf16[4,16,32,128]{3,2,1,0:T(8,128)(2,1)} collective-permute-done((bf16[4,16,32,128]{3,2,1,0:T(8,128)(2,1)}, bf16[4,16,32,128]{3,2,1,0:T(8,128)(2,1)}, u32[]{:S(2)}, u32[]{:S(2)}) %collective-permute-start.12) | collective-permute-done | bytes 524320 | tf_op jit(solution)/shard_map/ppermute | solution.py:968
  131.6 13.9 %close_layer.3 = (bf16[8,32,32,128]{3,2,1,0:T(8,128)(2,1)S(1)}, f32[8,32,32,128]{3,2,1,0:T(8,128)S(1)}, bf16[4,32,32,128]{3,2,1,0:T(8,128)(2,1)S(1)}, bf16[4,18,...) custom-call(s32[4]{0:T(128)S(1)} %pad_add_fusion.ids, ...), custom_call_target="tpu_custom_call" | custom-call | flops 8589934592 | bytes 1048576 | tf_op jit(solution)/shard_map/close_layer/pallas_call | solution.py:911
  147.0 13.8 %close_layer.4 = (bf16[8,32,32,128]{3,2,1,0:T(8,128)(2,1)S(1)}, f32[8,32,32,128]{3,2,1,0:T(8,128)S(1)}, bf16[4,32,32,128]{3,2,1,0:T(8,128)(2,1)S(1)}, bf16[4,18,...) custom-call(s32[4]{0:T(128)S(1)} %pad_add_fusion.ids, ...), custom_call_target="tpu_custom_call", output_to_operand_aliasing={{0}: (16, {}), {1}: (17, {}), {4}: (18, {}), {6}: (19, {})} | custom-call | flops 8589934592 | bytes 1048576 | tf_op jit(solution)/shard_map/close_layer/pallas_call | solution.py:911
  162.8 4.4 %collective-permute-done.19.rest_4_ = bf16[4,18,32,128]{3,2,1,0:T(8,128)(2,1)S(1)} collective-permute-done((bf16[4,18,32,128]{3,2,1,0:T(8,128)(2,1)S(1)}, bf16[4,18,32,128]{3,2,1,0:T(8,128)(2,1)S(1)}, u32[]{:S(2)}, u32[]{:S(2)}) %collective-permute-start.19) | collective-permute-done | bytes 589856 | tf_op jit(solution)/shard_map/ppermute | solution.py:947
  167.2 2.9 collective-permute-done.23.rest_0_.rest_2_
  171.8 4.8 %collective-permute-done.20.rest_6_ = bf16[4,18,32,128]{3,2,1,0:T(8,128)(2,1)S(1)} collective-permute-done((bf16[4,18,32,128]{3,2,1,0:T(8,128)(2,1)S(1)}, bf16[4,18,32,128]{3,2,1,0:T(8,128)(2,1)S(1)}, u32[]{:S(2)}, u32[]{:S(2)}) %collective-permute-start.20) | collective-permute-done | bytes 589856 | tf_op jit(solution)/shard_map/ppermute | solution.py:946
  176.5 6.2 %collective-permute-start.21 = (bf16[4,18,32,128]{3,2,1,0:T(8,128)(2,1)S(1)}, bf16[4,18,32,128]{3,2,1,0:T(8,128)(2,1)S(1)}, u32[]{:S(2)}, u32[]{:S(2)}) collective-permute-start(bf16[4,18,32,128]{3,2,1,0:T(8,128)(2,1)S(1)} %collective-permute-done.20.rest_6_), channel_id=1, source_target_pairs={{0,1},{3,2},{4,5},{7,6},{8,9},{11,10},{12,13},{15,14},{16,17},{19,... | collective-permute-start | bytes 1769480 | tf_op jit(solution)/shard_map/ppermute | solution.py:948
  182.7 6.2 %collective-permute-done.22.rest_9_ = bf16[4,18,32,128]{3,2,1,0:T(8,128)(2,1)S(1)} collective-permute-done((bf16[4,18,32,128]{3,2,1,0:T(8,128)(2,1)S(1)}, bf16[4,18,32,128]{3,2,1,0:T(8,128)(2,1)S(1)}, u32[]{:S(2)}, u32[]{:S(2)}) %collective-permute-start.22) | collective-permute-done | bytes 589856 | tf_op jit(solution)/shard_map/ppermute | solution.py:947
  189.4 4.7 %banded_products.9 = (bf16[4,18,32,128]{3,2,1,0:T(8,128)(2,1)S(1)}, bf16[4,18,32,128]{3,2,1,0:T(8,128)(2,1)S(1)}, bf16[4,18,32,128]{3,2,1,0:T(8,128)(2,1)S(1)}) custom-call(s32[4]{0:T(128)S(1)} %pad_add_fusion.ids, s32[40]{0:T(128)S(1)} %get-tuple-element.76.chosen, bf16[4,18,32,128]{3,2,1,0:T(8,128)(2,1)S(1)} %get-tuple-element.108.rest_0_, ...), custom_call_target="tpu_custom_call" | custom-call | flops 452984832 | bytes 1 | tf_op jit(solution)/shard_map/banded_products/pallas_call | solution.py:771
  195.3 2.9 collective-permute-start.26
  198.3 9.6 %far_operands.3 = (bf16[4,32,32,128]{3,2,1,0:T(8,128)(2,1)S(1)}, bf16[4,32,32,128]{3,2,1,0:T(8,128)(2,1)S(1)}) custom-call(s32[4]{0:T(128)S(1)} %pad_add_fusion.ids, s32[2,32]{1,0:T(2,128)S(1)} %bitcast.21, s32[10]{0:T(128)S(1)} %get-tuple-element.102.mine, bf16[4,32,32,128]{3,2,1,0:T(8,128)(2,1)S(1)} %collective-permute-done.23.rest_0_.rest_2_, ...), custom_call_target="tpu_custom_call" | custom-call | flops 8589934592 | bytes 1048576 | tf_op jit(solution)/shard_map/far_operands/pallas_call | solution.py:633
  210.1 3.7 %collective-permute-start.28 = (bf16[8,14,32,128]{3,2,1,0:T(8,128)(2,1)S(1)}, bf16[8,14,32,128]{3,2,1,0:T(8,128)(2,1)S(1)}, u32[]{:S(2)}, u32[]{:S(2)}) collective-permute-start(bf16[8,14,32,128]{3,2,1,0:T(8,128)(2,1)S(1)} %collective-permute-done.27.rest_1_), channel_id=1, source_target_pairs={{0,1},{3,2},{4,5},{7,6},{8,9},{11,10},{12,13},{15,14},{16,17},{19,... | collective-permute-start | bytes 2752520 | tf_op jit(solution)/shard_map/ppermute | solution.py:948
  216.7 24.9 %collective-permute-done.25.rest_0_ = bf16[4,18,32,128]{3,2,1,0:T(8,128)(2,1)S(1)} collective-permute-done((bf16[4,18,32,128]{3,2,1,0:T(8,128)(2,1)S(1)}, bf16[4,18,32,128]{3,2,1,0:T(8,128)(2,1)S(1)}, u32[]{:S(2)}, u32[]{:S(2)}) %collective-permute-start.25) | collective-permute-done | bytes 589856 | tf_op jit(solution)/shard_map/ppermute | solution.py:968
  241.6 8.5 %collective-permute-done.29.rest_4_ = bf16[8,14,32,128]{3,2,1,0:T(8,128)(2,1)S(1)} collective-permute-done((bf16[8,14,32,128]{3,2,1,0:T(8,128)(2,1)S(1)}, bf16[8,14,32,128]{3,2,1,0:T(8,128)(2,1)S(1)}, u32[]{:S(2)}, u32[]{:S(2)}) %collective-permute-start.29) | collective-permute-done | bytes 917536 | tf_op jit(solution)/shard_map/ppermute | solution.py:947
  250.0 4.6 %banded_products.10 = (bf16[4,14,32,128]{3,2,1,0:T(8,128)(2,1)S(1)}, bf16[4,14,32,128]{3,2,1,0:T(8,128)(2,1)S(1)}, bf16[4,14,32,128]{3,2,1,0:T(8,128)(2,1)S(1)}) custom-call(s32[4]{0:T(128)S(1)} %pad_add_fusion.ids, s32[40]{0:T(128)S(1)} %get-tuple-element.76.chosen, bf16[8,14,32,128]{3,2,1,0:T(8,128)(2,1)S(1)} %get-tuple-element.132.rest_0_, ...), custom_call_target="tpu_custom_call" | custom-call | flops 352321536 | bytes 1 | tf_op jit(solution)/shard_map/banded_products/pallas_call | solution.py:771
  254.7 5.0 %collective-permute-start.33 = (bf16[4,32,32,128]{3,2,1,0:T(8,128)(2,1)S(1)}, bf16[4,32,32,128]{3,2,1,0:T(8,128)(2,1)S(1)}, u32[]{:S(2)}, u32[]{:S(2)}) collective-permute-start(bf16[4,32,32,128]{3,2,1,0:T(8,128)(2,1)S(1)} %collective-permute-done.32.rest_1_), channel_id=1, source_target_pairs={{0,1},{3,2},{4,5},{7,6},{8,9},{11,10},{12,13},{15,14},{16,17},{19,... | collective-permute-start | bytes 3145736 | tf_op jit(solution)/shard_map/ppermute | solution.py:948
  260.7 3.3 %collective-permute-done.34.rest_4_ = bf16[4,32,32,128]{3,2,1,0:T(8,128)(2,1)S(1)} collective-permute-done((bf16[4,32,32,128]{3,2,1,0:T(8,128)(2,1)S(1)}, bf16[4,32,32,128]{3,2,1,0:T(8,128)(2,1)S(1)}, u32[]{:S(2)}, u32[]{:S(2)}) %collective-permute-start.34) | collective-permute-done | bytes 1048608 | tf_op jit(solution)/shard_map/ppermute | solution.py:947
  266.4 15.5 %collective-permute-done.31.rest_4_ = bf16[4,14,32,128]{3,2,1,0:T(8,128)(2,1)S(1)} collective-permute-done((bf16[4,14,32,128]{3,2,1,0:T(8,128)(2,1)S(1)}, bf16[4,14,32,128]{3,2,1,0:T(8,128)(2,1)S(1)}, u32[]{:S(2)}, u32[]{:S(2)}) %collective-permute-start.31) | collective-permute-done | bytes 458784 | tf_op jit(solution)/shard_map/ppermute | solution.py:968
  281.9 8.6 %collective-permute-done.30.rest_3_ = bf16[4,14,32,128]{3,2,1,0:T(8,128)(2,1)S(1)} collective-permute-done((bf16[4,14,32,128]{3,2,1,0:T(8,128)(2,1)S(1)}, bf16[4,14,32,128]{3,2,1,0:T(8,128)(2,1)S(1)}, u32[]{:S(2)}, u32[]{:S(2)}) %collective-permute-start.30) | collective-permute-done | bytes 458784 | tf_op jit(solution)/shard_map/ppermute | solution.py:968
  290.5 10.0 %close_layer.5 = bf16[8,32,32,128]{3,2,1,0:T(8,128)(2,1)} custom-call(s32[4]{0:T(128)S(1)} %pad_add_fusion.ids, s32[2,32]{1,0:T(2,128)S(1)} %bitcast.22, s32[16]{0:T(128)S(1)} %get-tuple-element.91.place, bf16[4,18,32,128]{3,2,1,0:T(8,128)(2,1)S(1)} %collective-permute-done.25.rest_0_, bf16[4,18,32,128]{3,2,1,0:T(8,128)(2,1)S(1)} %collective-permute-done.26.rest_1_, ...), custom_call_target="tpu_custom_call" | custom-call | flops 8589934592 | bytes 1048576 | tf_op jit(solution)/shard_map/close_layer/pallas_call | solution.py:911
  (95 shorter events, 42.4 us)
Async XLA Ops:
  0.0 52.5 %collective-permute-start.6 = (bf16[8,32,32,128]{3,2,1,0:T(8,128)(2,1)}, bf16[8,32,32,128]{3,2,1,0:T(8,128)(2,1)}, u32[]{:S(2)}, u32[]{:S(2)}) collective-permute-start(bf16[8,32,32,128]{3,2,1,0:T(8,128)(2,1)} %rest_7_.3), channel_id=1, source_target_pairs={{0,4},{4,8},{8,12},{12,0},{1,5},{5,9},{9,13},{13,1},{2,6},{6,10},{... | collective-permute-start | bytes 6291464 | tf_op jit(solution)/shard_map/ppermute | solution.py:968
  11.6 14.6 %collective-permute-start.2 = (bf16[4,16,32,128]{3,2,1,0:T(8,128)(2,1)S(1)}, bf16[4,16,32,128]{3,2,1,0:T(8,128)(2,1)S(1)}, u32[]{:S(2)}, u32[]{:S(2)}) collective-permute-start(bf16[4,16,32,128]{3,2,1,0:T(8,128)(2,1)S(1)} %get-tuple-element.78.rest_3_), channel_id=1, source_target_pairs={{1,2},{2,1},{5,6},{6,5},{9,10},{10,9},{13,14},{14,13},{17,18},{18,... | collective-permute-start | bytes 1572872 | tf_op jit(solution)/shard_map/ppermute | solution.py:940
  12.3 14.1 %collective-permute-start.1 = (bf16[4,16,32,128]{3,2,1,0:T(8,128)(2,1)S(1)}, bf16[4,16,32,128]{3,2,1,0:T(8,128)(2,1)S(1)}, u32[]{:S(2)}, u32[]{:S(2)}) collective-permute-start(bf16[4,16,32,128]{3,2,1,0:T(8,128)(2,1)S(1)} %get-tuple-element.78.rest_3_), channel_id=1, source_target_pairs={{0,2},{3,1},{1,0},{2,3},{4,6},{7,5},{5,4},{6,7},{8,10},{11,9},{9,8... | collective-permute-start | bytes 1572872 | tf_op jit(solution)/shard_map/ppermute | solution.py:939
  15.8 10.3 %collective-permute-start = (bf16[4,16,32,128]{3,2,1,0:T(8,128)(2,1)S(1)}, bf16[4,16,32,128]{3,2,1,0:T(8,128)(2,1)S(1)}, u32[]{:S(2)}, u32[]{:S(2)}) collective-permute-start(bf16[4,16,32,128]{3,2,1,0:T(8,128)(2,1)S(1)} %get-tuple-element.77.rest_1_), channel_id=1, source_target_pairs={{0,1},{1,0},{2,3},{3,2},{4,5},{5,4},{6,7},{7,6},{8,9},{9,8},{10,11... | collective-permute-start | bytes 1572872 | tf_op jit(solution)/shard_map/ppermute | solution.py:938
  29.3 13.5 %collective-permute-start.4 = (bf16[4,16,32,128]{3,2,1,0:T(8,128)(2,1)S(1)}, bf16[4,16,32,128]{3,2,1,0:T(8,128)(2,1)S(1)}, u32[]{:S(2)}, u32[]{:S(2)}) collective-permute-start(bf16[4,16,32,128]{3,2,1,0:T(8,128)(2,1)S(1)} %get-tuple-element.85.rest_8_), channel_id=1, source_target_pairs={{0,2},{3,1},{1,0},{2,3},{4,6},{7,5},{5,4},{6,7},{8,10},{11,9},{9,8... | collective-permute-start | bytes 1572872 | tf_op jit(solution)/shard_map/ppermute | solution.py:939
  47.3 18.6 %collective-permute-start.11 = (bf16[8,16,32,128]{3,2,1,0:T(8,128)(2,1)S(1)}, bf16[8,16,32,128]{3,2,1,0:T(8,128)(2,1)S(1)}, u32[]{:S(2)}, u32[]{:S(2)}) collective-permute-start(bf16[8,16,32,128]{3,2,1,0:T(8,128)(2,1)S(1)} %get-tuple-element.96.rest_3_), channel_id=1, source_target_pairs={{1,2},{2,1},{5,6},{6,5},{9,10},{10,9},{13,14},{14,13},{17,18},{18,... | collective-permute-start | bytes 3145736 | tf_op jit(solution)/shard_map/ppermute | solution.py:940
  48.0 41.9 %collective-permute-start.10 = (bf16[8,16,32,128]{3,2,1,0:T(8,128)(2,1)S(1)}, bf16[8,16,32,128]{3,2,1,0:T(8,128)(2,1)S(1)}, u32[]{:S(2)}, u32[]{:S(2)}) collective-permute-start(bf16[8,16,32,128]{3,2,1,0:T(8,128)(2,1)S(1)} %get-tuple-element.96.rest_3_), channel_id=1, source_target_pairs={{0,2},{3,1},{1,0},{2,3},{4,6},{7,5},{5,4},{6,7},{8,10},{11,9},{9,8... | collective-permute-start | bytes 3145736 | tf_op jit(solution)/shard_map/ppermute | solution.py:939
  52.5 37.4 %collective-permute-start.9 = (bf16[8,16,32,128]{3,2,1,0:T(8,128)(2,1)S(1)}, bf16[8,16,32,128]{3,2,1,0:T(8,128)(2,1)S(1)}, u32[]{:S(2)}, u32[]{:S(2)}) collective-permute-start(bf16[8,16,32,128]{3,2,1,0:T(8,128)(2,1)S(1)} %get-tuple-element.94.rest_1_), channel_id=1, source_target_pairs={{0,1},{1,0},{2,3},{3,2},{4,5},{5,4},{6,7},{7,6},{8,9},{9,8},{10,11... | collective-permute-start | bytes 3145736 | tf_op jit(solution)/shard_map/ppermute | solution.py:938
  52.5 22.7 %collective-permute-start.8 = (bf16[4,16,32,128]{3,2,1,0:T(8,128)(2,1)S(1)}, bf16[4,16,32,128]{3,2,1,0:T(8,128)(2,1)S(1)}, u32[]{:S(2)}, u32[]{:S(2)}) collective-permute-start(bf16[4,16,32,128]{3,2,1,0:T(8,128)(2,1)S(1)} %get-tuple-element.89), channel_id=1, source_target_pairs={{0,12},{4,0},{8,4},{12,8},{1,13},{5,1},{9,5},{13,9},{2,14},{6,2},{... | collective-permute-start | bytes 1572872 | tf_op jit(solution)/shard_map/ppermute | solution.py:968
  52.6 36.0 %collective-permute-start.7 = (bf16[4,16,32,128]{3,2,1,0:T(8,128)(2,1)S(1)}, bf16[4,16,32,128]{3,2,1,0:T(8,128)(2,1)S(1)}, u32[]{:S(2)}, u32[]{:S(2)}) collective-permute-start(bf16[4,16,32,128]{3,2,1,0:T(8,128)(2,1)S(1)} %get-tuple-element.87), channel_id=1, source_target_pairs={{0,8},{4,12},{8,0},{12,4},{1,9},{5,13},{9,1},{13,5},{2,10},{6,14},... | collective-permute-start | bytes 1572872 | tf_op jit(solution)/shard_map/ppermute | solution.py:968
  65.9 32.1 %collective-permute-start.14 = (bf16[4,32,32,128]{3,2,1,0:T(8,128)(2,1)S(1)}, bf16[4,32,32,128]{3,2,1,0:T(8,128)(2,1)S(1)}, u32[]{:S(2)}, u32[]{:S(2)}) collective-permute-start(bf16[4,32,32,128]{3,2,1,0:T(8,128)(2,1)S(1)} %get-tuple-element.104.rest_1_), channel_id=1, source_target_pairs={{0,1},{1,0},{2,3},{3,2},{4,5},{5,4},{6,7},{7,6},{8,9},{9,8},{10,11... | collective-permute-start | bytes 3145736 | tf_op jit(solution)/shard_map/ppermute | solution.py:938
  75.1 22.9 %collective-permute-start.16 = (bf16[4,32,32,128]{3,2,1,0:T(8,128)(2,1)S(1)}, bf16[4,32,32,128]{3,2,1,0:T(8,128)(2,1)}, u32[]{:S(2)}, u32[]{:S(2)}) collective-permute-start(bf16[4,32,32,128]{3,2,1,0:T(8,128)(2,1)S(1)} %get-tuple-element.105.rest_3_), channel_id=1, source_target_pairs={{1,2},{2,1},{5,6},{6,5},{9,10},{10,9},{13,14},{14,13},{17,18},{18,... | collective-permute-start | bytes 3145736 | tf_op jit(solution)/shard_map/ppermute | solution.py:940
  88.6 13.7 %collective-permute-start.15 = (bf16[4,32,32,128]{3,2,1,0:T(8,128)(2,1)S(1)}, bf16[4,32,32,128]{3,2,1,0:T(8,128)(2,1)}, u32[]{:S(2)}, u32[]{:S(2)}) collective-permute-start(bf16[4,32,32,128]{3,2,1,0:T(8,128)(2,1)S(1)} %get-tuple-element.105.rest_3_), channel_id=1, source_target_pairs={{0,2},{3,1},{1,0},{2,3},{4,6},{7,5},{5,4},{6,7},{8,10},{11,9},{9,8... | collective-permute-start | bytes 3145736 | tf_op jit(solution)/shard_map/ppermute | solution.py:939
  94.2 14.0 %collective-permute-start.13 = (bf16[4,16,32,128]{3,2,1,0:T(8,128)(2,1)}, bf16[4,16,32,128]{3,2,1,0:T(8,128)(2,1)}, u32[]{:S(2)}, u32[]{:S(2)}) collective-permute-start(bf16[4,16,32,128]{3,2,1,0:T(8,128)(2,1)} %get-tuple-element.100), channel_id=1, source_target_pairs={{0,12},{4,0},{8,4},{12,8},{1,13},{5,1},{9,5},{13,9},{2,14},{6,2},{... | collective-permute-start | bytes 1572872 | tf_op jit(solution)/shard_map/ppermute | solution.py:968
  95.2 36.4 %collective-permute-start.12 = (bf16[4,16,32,128]{3,2,1,0:T(8,128)(2,1)}, bf16[4,16,32,128]{3,2,1,0:T(8,128)(2,1)}, u32[]{:S(2)}, u32[]{:S(2)}) collective-permute-start(bf16[4,16,32,128]{3,2,1,0:T(8,128)(2,1)} %get-tuple-element.98), channel_id=1, source_target_pairs={{0,8},{4,12},{8,0},{12,4},{1,9},{5,13},{9,1},{13,5},{2,10},{6,14},... | collective-permute-start | bytes 1572872 | tf_op jit(solution)/shard_map/ppermute | solution.py:968
  145.5 24.7 %collective-permute-start.23 = (bf16[4,32,32,128]{3,2,1,0:T(8,128)(2,1)S(1)}, bf16[4,32,32,128]{3,2,1,0:T(8,128)(2,1)S(1)}, u32[]{:S(2)}, u32[]{:S(2)}) collective-permute-start(bf16[4,32,32,128]{3,2,1,0:T(8,128)(2,1)S(1)} %get-tuple-element.123), channel_id=1, source_target_pairs={{0,4},{4,8},{8,12},{12,0},{1,5},{5,9},{9,13},{13,1},{2,6},{6,10},{... | collective-permute-start | bytes 3145736 | tf_op jit(solution)/shard_map/ppermute | solution.py:968
  145.5 15.3 %collective-permute-start.17 = (bf16[4,18,32,128]{3,2,1,0:T(8,128)(2,1)S(1)}, bf16[4,18,32,128]{3,2,1,0:T(8,128)(2,1)S(1)}, u32[]{:S(2)}, u32[]{:S(2)}) collective-permute-start(bf16[4,18,32,128]{3,2,1,0:T(8,128)(2,1)S(1)} %get-tuple-element.108.rest_0_), channel_id=1, source_target_pairs={{1,3},{2,0},{0,1},{3,2},{5,7},{6,4},{4,5},{7,6},{9,11},{10,8},{8,9... | collective-permute-start | bytes 1769480 | tf_op jit(solution)/shard_map/ppermute | solution.py:946
  145.7 21.6 %collective-permute-start.19 = (bf16[4,18,32,128]{3,2,1,0:T(8,128)(2,1)S(1)}, bf16[4,18,32,128]{3,2,1,0:T(8,128)(2,1)S(1)}, u32[]{:S(2)}, u32[]{:S(2)}) collective-permute-start(bf16[4,18,32,128]{3,2,1,0:T(8,128)(2,1)S(1)} %get-tuple-element.115.rest_3_), channel_id=1, source_target_pairs={{0,2},{2,0},{1,3},{3,1},{4,6},{6,4},{5,7},{7,5},{8,10},{10,8},{9,1... | collective-permute-start | bytes 1769480 | tf_op jit(solution)/shard_map/ppermute | solution.py:947
  160.8 10.0 %collective-permute-start.18 = (bf16[4,18,32,128]{3,2,1,0:T(8,128)(2,1)S(1)}, bf16[4,18,32,128]{3,2,1,0:T(8,128)(2,1)S(1)}, u32[]{:S(2)}, u32[]{:S(2)}) collective-permute-start(bf16[4,18,32,128]{3,2,1,0:T(8,128)(2,1)S(1)} %collective-permute-done.17.rest_1_), channel_id=1, source_target_pairs={{0,1},{3,2},{4,5},{7,6},{8,9},{11,10},{12,13},{15,14},{16,17},{19,... | collective-permute-start | bytes 1769480 | tf_op jit(solution)/shard_map/ppermute | solution.py:948
  170.1 25.2 %collective-permute-start.24 = (bf16[4,32,32,128]{3,2,1,0:T(8,128)(2,1)S(1)}, bf16[4,32,32,128]{3,2,1,0:T(8,128)(2,1)S(1)}, u32[]{:S(2)}, u32[]{:S(2)}) collective-permute-start(bf16[4,32,32,128]{3,2,1,0:T(8,128)(2,1)S(1)} %get-tuple-element.124), channel_id=1, source_target_pairs={{0,4},{4,8},{8,12},{12,0},{1,5},{5,9},{9,13},{13,1},{2,6},{6,10},{... | collective-permute-start | bytes 3145736 | tf_op jit(solution)/shard_map/ppermute | solution.py:968
  170.8 18.1 %collective-permute-start.22 = (bf16[4,18,32,128]{3,2,1,0:T(8,128)(2,1)S(1)}, bf16[4,18,32,128]{3,2,1,0:T(8,128)(2,1)S(1)}, u32[]{:S(2)}, u32[]{:S(2)}) collective-permute-start(bf16[4,18,32,128]{3,2,1,0:T(8,128)(2,1)S(1)} %get-tuple-element.120.rest_8_), channel_id=1, source_target_pairs={{0,2},{2,0},{1,3},{3,1},{4,6},{6,4},{5,7},{7,5},{8,10},{10,8},{9,1... | collective-permute-start | bytes 1769480 | tf_op jit(solution)/shard_map/ppermute | solution.py:947
  176.5 12.4 %collective-permute-start.21 = (bf16[4,18,32,128]{3,2,1,0:T(8,128)(2,1)S(1)}, bf16[4,18,32,128]{3,2,1,0:T(8,128)(2,1)S(1)}, u32[]{:S(2)}, u32[]{:S(2)}) collective-permute-start(bf16[4,18,32,128]{3,2,1,0:T(8,128)(2,1)S(1)} %collective-permute-done.20.rest_6_), channel_id=1, source_target_pairs={{0,1},{3,2},{4,5},{7,6},{8,9},{11,10},{12,13},{15,14},{16,17},{19,... | collective-permute-start | bytes 1769480 | tf_op jit(solution)/shard_map/ppermute | solution.py:948
  188.9 21.2 %collective-permute-start.27 = (bf16[8,14,32,128]{3,2,1,0:T(8,128)(2,1)S(1)}, bf16[8,14,32,128]{3,2,1,0:T(8,128)(2,1)S(1)}, u32[]{:S(2)}, u32[]{:S(2)}) collective-permute-start(bf16[8,14,32,128]{3,2,1,0:T(8,128)(2,1)S(1)} %get-tuple-element.132.rest_0_), channel_id=1, source_target_pairs={{1,3},{2,0},{0,1},{3,2},{5,7},{6,4},{4,5},{7,6},{9,11},{10,8},{8,9... | collective-permute-start | bytes 2752520 | tf_op jit(solution)/shard_map/ppermute | solution.py:946
  195.3 14.7 %collective-permute-start.26 = (bf16[4,18,32,128]{3,2,1,0:T(8,128)(2,1)S(1)}, bf16[4,18,32,128]{3,2,1,0:T(8,128)(2,1)S(1)}, u32[]{:S(2)}, u32[]{:S(2)}) collective-permute-start(bf16[4,18,32,128]{3,2,1,0:T(8,128)(2,1)S(1)} %get-tuple-element.127), channel_id=1, source_target_pairs={{0,12},{4,0},{8,4},{12,8},{1,13},{5,1},{9,5},{13,9},{2,14},{6,2},{... | collective-permute-start | bytes 1769480 | tf_op jit(solution)/shard_map/ppermute | solution.py:968
  207.9 46.8 %collective-permute-start.32 = (bf16[4,32,32,128]{3,2,1,0:T(8,128)(2,1)S(1)}, bf16[4,32,32,128]{3,2,1,0:T(8,128)(2,1)S(1)}, u32[]{:S(2)}, u32[]{:S(2)}) collective-permute-start(bf16[4,32,32,128]{3,2,1,0:T(8,128)(2,1)S(1)} %get-tuple-element.142.rest_0_), channel_id=1, source_target_pairs={{1,3},{2,0},{0,1},{3,2},{5,7},{6,4},{4,5},{7,6},{9,11},{10,8},{8,9... | collective-permute-start | bytes 3145736 | tf_op jit(solution)/shard_map/ppermute | solution.py:946
  210.1 40.0 %collective-permute-start.29 = (bf16[8,14,32,128]{3,2,1,0:T(8,128)(2,1)S(1)}, bf16[8,14,32,128]{3,2,1,0:T(8,128)(2,1)S(1)}, u32[]{:S(2)}, u32[]{:S(2)}) collective-permute-start(bf16[8,14,32,128]{3,2,1,0:T(8,128)(2,1)S(1)} %get-tuple-element.134.rest_3_), channel_id=1, source_target_pairs={{0,2},{2,0},{1,3},{3,1},{4,6},{6,4},{5,7},{7,5},{8,10},{10,8},{9,1... | collective-permute-start | bytes 2752520 | tf_op jit(solution)/shard_map/ppermute | solution.py:947
  210.1 40.0 %collective-permute-start.28 = (bf16[8,14,32,128]{3,2,1,0:T(8,128)(2,1)S(1)}, bf16[8,14,32,128]{3,2,1,0:T(8,128)(2,1)S(1)}, u32[]{:S(2)}, u32[]{:S(2)}) collective-permute-start(bf16[8,14,32,128]{3,2,1,0:T(8,128)(2,1)S(1)} %collective-permute-done.27.rest_1_), channel_id=1, source_target_pairs={{0,1},{3,2},{4,5},{7,6},{8,9},{11,10},{12,13},{15,14},{16,17},{19,... | collective-permute-start | bytes 2752520 | tf_op jit(solution)/shard_map/ppermute | solution.py:948
  213.8 27.8 %collective-permute-start.25 = (bf16[4,18,32,128]{3,2,1,0:T(8,128)(2,1)S(1)}, bf16[4,18,32,128]{3,2,1,0:T(8,128)(2,1)S(1)}, u32[]{:S(2)}, u32[]{:S(2)}) collective-permute-start(bf16[4,18,32,128]{3,2,1,0:T(8,128)(2,1)S(1)} %get-tuple-element.125), channel_id=1, source_target_pairs={{0,8},{4,12},{8,0},{12,4},{1,9},{5,13},{9,1},{13,5},{2,10},{6,14},... | collective-permute-start | bytes 1769480 | tf_op jit(solution)/shard_map/ppermute | solution.py:968
  216.7 47.3 %collective-permute-start.34 = (bf16[4,32,32,128]{3,2,1,0:T(8,128)(2,1)S(1)}, bf16[4,32,32,128]{3,2,1,0:T(8,128)(2,1)S(1)}, u32[]{:S(2)}, u32[]{:S(2)}) collective-permute-start(bf16[4,32,32,128]{3,2,1,0:T(8,128)(2,1)S(1)} %get-tuple-element.144.rest_3_), channel_id=1, source_target_pairs={{0,2},{2,0},{1,3},{3,1},{4,6},{6,4},{5,7},{7,5},{8,10},{10,8},{9,1... | collective-permute-start | bytes 3145736 | tf_op jit(solution)/shard_map/ppermute | solution.py:947
  254.7 9.3 %collective-permute-start.33 = (bf16[4,32,32,128]{3,2,1,0:T(8,128)(2,1)S(1)}, bf16[4,32,32,128]{3,2,1,0:T(8,128)(2,1)S(1)}, u32[]{:S(2)}, u32[]{:S(2)}) collective-permute-start(bf16[4,32,32,128]{3,2,1,0:T(8,128)(2,1)S(1)} %collective-permute-done.32.rest_1_), channel_id=1, source_target_pairs={{0,1},{3,2},{4,5},{7,6},{8,9},{11,10},{12,13},{15,14},{16,17},{19,... | collective-permute-start | bytes 3145736 | tf_op jit(solution)/shard_map/ppermute | solution.py:948
  259.7 22.1 %collective-permute-start.31 = (bf16[4,14,32,128]{3,2,1,0:T(8,128)(2,1)S(1)}, bf16[4,14,32,128]{3,2,1,0:T(8,128)(2,1)S(1)}, u32[]{:S(2)}, u32[]{:S(2)}) collective-permute-start(bf16[4,14,32,128]{3,2,1,0:T(8,128)(2,1)S(1)} %get-tuple-element.138), channel_id=1, source_target_pairs={{0,12},{4,0},{8,4},{12,8},{1,13},{5,1},{9,5},{13,9},{2,14},{6,2},{... | collective-permute-start | bytes 1376264 | tf_op jit(solution)/shard_map/ppermute | solution.py:968
  260.4 30.1 %collective-permute-start.30 = (bf16[4,14,32,128]{3,2,1,0:T(8,128)(2,1)S(1)}, bf16[4,14,32,128]{3,2,1,0:T(8,128)(2,1)S(1)}, u32[]{:S(2)}, u32[]{:S(2)}) collective-permute-start(bf16[4,14,32,128]{3,2,1,0:T(8,128)(2,1)S(1)} %get-tuple-element.136), channel_id=1, source_target_pairs={{0,8},{4,12},{8,0},{12,4},{1,9},{5,13},{9,1},{13,5},{2,10},{6,14},... | collective-permute-start | bytes 1376264 | tf_op jit(solution)/shard_map/ppermute | solution.py:968
  (22 other events, 323.0 us)

commit v17 on v15

--- a/solution.py
+++ b/solution.py
@@ -441,7 +441,7 @@
         in_specs=[pl.BlockSpec((1,) + w_in.shape[1:], lambda s: (layer, 0, 0))],
         out_specs=pl.BlockSpec(shape, lambda s: (0, 0)),
         out_shape=jax.ShapeDtypeStruct(shape, jnp.bfloat16),
-        compiler_params=pltpu.CompilerParams(vmem_limit_bytes=16 * mebi),
+        compiler_params=pltpu.CompilerParams(vmem_limit_bytes=10 * mebi),
         cost_estimate=pl.CostEstimate(flops=1 << 30, bytes_accessed=1 << 20, transcendentals=0),
         name="spread_weights",
     )(w_in)
@@ -784,7 +784,7 @@
             ],
         ),
         out_shape=[jax.ShapeDtypeStruct((capacity, bands, rows, hidden), jnp.bfloat16)] * len(shifts),
-        compiler_params=pltpu.CompilerParams(vmem_limit_bytes=14 * mebi),
+        compiler_params=pltpu.CompilerParams(vmem_limit_bytes=10 * mebi),
         cost_estimate=pl.CostEstimate(
             flops=2 * count * bands * rows * hidden * hidden * halves, bytes_accessed=1, transcendentals=0
         ),
@@ -958,7 +958,7 @@
     near = [s for n, s in enumerate(near) if s not in near[:n]] + [0]
     layers = w_in.shape[0]
     current = pair
-    bands = [[16, 16], [20, 12]]
+    bands = [[14, 18], [20, 12]]
     chosen, place, mine = make_plan(ids, owners, slot_of, n_blk, far, slots, terms, capacity)
     in_order = jnp.repeat(jnp.arange(capacity, dtype=jnp.int32), 2)
     half = slots // 2

time: 294 us -> 295 us (level)
  waiting for transfers between devices: 112 us -> 107 us
  Pallas kernels: 97.6 us -> 101 us
    ppermute x11, waiting for transfers between devices: 49.9 us -> 40.7 us  [over_blk(): lax.ppermute(value, 'blk', [(p, (p + shift) % n_blk) for p in range(n_blk)])]
    ppermute x4, waiting for transfers between devices: 13.8 us -> 17.9 us  [exchange_bands_outgoing(): one = lax.ppermute(right, both, [(0, 2), (3, 1), (1, 0), (2, 3)])]
    pallas_call x6, Pallas kernels: 22.3 us -> 25.6 us  [banded_products(): pl.pallas_call(functools.partial(banded_kernel, shifts, capacity, tuple(p...]
  transfers between devices with their start and end apart: 35 -> 35, of which waited for: 16 -> 13; matrix products, arithmetic and copies ran while one was open for 0% -> 0% of each run, Pallas kernels for 26% -> 27%
where the time goes in v17:
time: 295 us; the launch traced here: 294 us
  waiting for transfers between devices  107 us (36%)
  Pallas kernels  101 us (34%)
  starting transfers between devices  78.2 us (27%)
  local copies, waits for them, and re-layouts  6.61 us (2%)
    ppermute x11, waiting for transfers between devices, over_blk(): lax.ppermute(value, 'blk', [(p, (p + shift) % n_blk) for p in range(n_blk)])  40.7 us
    pallas_call x3, Pallas kernels, close_layer(): pl.pallas_call(functools.partial(close_kernel, *(layer, last, spots, 0 if...  35.7 us
    ppermute x4, starting transfers between devices, exchange_bands_incoming(): lax.ppermute(after(one, other if over is None else over), both, [(0, 1),...  33.9 us
    pallas_call x6, Pallas kernels, banded_products(): pl.pallas_call(functools.partial(banded_kernel, shifts, capacity, tuple(p...  25.6 us
    ppermute x4, waiting for transfers between devices, exchange_bands_incoming(): other = lax.ppermute(right, 'chan', [(0, 1), (1, 0)])  24.3 us
    ppermute x4, waiting for transfers between devices, exchange_bands_incoming(): one = lax.ppermute(left, both, [(1, 3), (2, 0), (0, 1), (3, 2)])  24 us
    pallas_call x2, Pallas kernels, far_operands(): pl.pallas_call(functools.partial(far_kernel, layer, n_blk, far, lax.axis_...  20.6 us
    ppermute x4, waiting for transfers between devices, exchange_bands_outgoing(): one = lax.ppermute(right, both, [(0, 2), (3, 1), (1, 0), (2, 3)])  17.9 us
  transfers between devices with their start and end apart: 35, of which 13 were waited for; matrix products, arithmetic and copies ran while one was open for 0% of the time, Pallas kernels for 27%

profile of v17, /device:TPU:11, one launch (start us, length us, event | category | flops | bytes accessed | tf_op | source)
XLA Modules:
  0.0 293.7 jit_solution(14119705295614279543)
XLA Ops:
  3.3 8.3 %open_operands.2 = (f32[8,32,32,128]{3,2,1,0:T(8,128)S(1)}, bf16[4,14,32,128]{3,2,1,0:T(8,128)(2,1)S(1)}, bf16[8,18,32,128]{3,2,1,0:T(8,128)(2,1)S(1)}, bf16[4,1...) custom-call(s32[4]{0:T(128)S(1)} %pad_add_fusion.ids, s32[2,32]{1,0:T(2,128)S(1)} %bitcast.16, ...), custom_call_target="tpu_custom_call" | custom-call | flops 8589934592 | bytes 1048576 | tf_op jit(solution)/shard_map/open_operands/pallas_call | solution.py:567
  12.3 3.5 %collective-permute-start.1 = (bf16[4,14,32,128]{3,2,1,0:T(8,128)(2,1)S(1)}, bf16[4,14,32,128]{3,2,1,0:T(8,128)(2,1)S(1)}, u32[]{:S(2)}, u32[]{:S(2)}) collective-permute-start(bf16[4,14,32,128]{3,2,1,0:T(8,128)(2,1)S(1)} %get-tuple-element.78.rest_3_), channel_id=1, source_target_pairs={{0,2},{3,1},{1,0},{2,3},{4,6},{7,5},{5,4},{6,7},{8,10},{11,9},{9,8... | collective-permute-start | bytes 1376264 | tf_op jit(solution)/shard_map/ppermute | solution.py:939
  15.8 8.3 %open_operands.3 = (f32[8,32,32,128]{3,2,1,0:T(8,128)S(1)}, bf16[4,14,32,128]{3,2,1,0:T(8,128)(2,1)S(1)}, bf16[8,18,32,128]{3,2,1,0:T(8,128)(2,1)S(1)}, bf16[4,1...) custom-call(s32[4]{0:T(128)S(1)} %pad_add_fusion.ids, ...), custom_call_target="tpu_custom_call", output_to_operand_aliasing={{0}: (6, {}), {2}: (7, {}), {4}: (8, {})} | custom-call | flops 8589934592 | bytes 1048576 | tf_op jit(solution)/shard_map/open_operands/pallas_call | solution.py:567
  27.9 2.6 collective-permute-start.4
  32.3 7.8 %collective-permute-done.4.rest_7_ = bf16[4,14,32,128]{3,2,1,0:T(8,128)(2,1)S(1)} collective-permute-done((bf16[4,14,32,128]{3,2,1,0:T(8,128)(2,1)S(1)}, bf16[4,14,32,128]{3,2,1,0:T(8,128)(2,1)S(1)}, u32[]{:S(2)}, u32[]{:S(2)}) %collective-permute-start.4) | collective-permute-done | bytes 458784 | tf_op jit(solution)/shard_map/ppermute | solution.py:939
  40.1 6.0 %banded_products.6 = (bf16[4,14,32,128]{3,2,1,0:T(8,128)(2,1)S(1)}, bf16[4,14,32,128]{3,2,1,0:T(8,128)(2,1)S(1)}, bf16[4,14,32,128]{3,2,1,0:T(8,128)(2,1)S(1)}) custom-call(s32[4]{0:T(128)S(1)} %pad_add_fusion.ids, s32[40]{0:T(128)S(1)} %get-tuple-element.76.chosen, bf16[4,14,32,128]{3,2,1,0:T(8,128)(2,1)S(1)} %collective-permute-done.rest_0_, ...), custom_call_target="tpu_custom_call" | custom-call | flops 352321536 | bytes 1 | tf_op jit(solution)/shard_map/banded_products/pallas_call | solution.py:771
  47.6 4.4 %collective-permute-start.10 = (bf16[8,18,32,128]{3,2,1,0:T(8,128)(2,1)S(1)}, bf16[8,18,32,128]{3,2,1,0:T(8,128)(2,1)S(1)}, u32[]{:S(2)}, u32[]{:S(2)}) collective-permute-start(bf16[8,18,32,128]{3,2,1,0:T(8,128)(2,1)S(1)} %get-tuple-element.96.rest_3_), channel_id=1, source_target_pairs={{0,2},{3,1},{1,0},{2,3},{4,6},{7,5},{5,4},{6,7},{8,10},{11,9},{9,8... | collective-permute-start | bytes 3538952 | tf_op jit(solution)/shard_map/ppermute | solution.py:939
  54.5 11.0 %far_operands.2 = (bf16[4,32,32,128]{3,2,1,0:T(8,128)(2,1)S(1)}, bf16[4,32,32,128]{3,2,1,0:T(8,128)(2,1)S(1)}) custom-call(s32[4]{0:T(128)S(1)} %pad_add_fusion.ids, s32[2,32]{1,0:T(2,128)S(1)} %bitcast.18, s32[10]{0:T(128)S(1)} %get-tuple-element.102.mine, bf16[8,32,32,128]{3,2,1,0:T(8,128)(2,1)} %collective-permute-done.6.rest_0_.rest_1_, ...), custom_call_target="tpu_custom_call" | custom-call | flops 8589934592 | bytes 1048576 | tf_op jit(solution)/shard_map/far_operands/pallas_call | solution.py:633
  65.5 12.0 %collective-permute-start.14 = (bf16[4,32,32,128]{3,2,1,0:T(8,128)(2,1)S(1)}, bf16[4,32,32,128]{3,2,1,0:T(8,128)(2,1)S(1)}, u32[]{:S(2)}, u32[]{:S(2)}) collective-permute-start(bf16[4,32,32,128]{3,2,1,0:T(8,128)(2,1)S(1)} %get-tuple-element.104.rest_1_), channel_id=1, source_target_pairs={{0,1},{1,0},{2,3},{3,2},{4,5},{5,4},{6,7},{7,6},{8,9},{9,8},{10,11... | collective-permute-start | bytes 3145736 | tf_op jit(solution)/shard_map/ppermute | solution.py:938
  80.0 4.1 %collective-permute-done.7.rest_0_ = bf16[4,14,32,128]{3,2,1,0:T(8,128)(2,1)S(1)} collective-permute-done((bf16[4,14,32,128]{3,2,1,0:T(8,128)(2,1)S(1)}, bf16[4,14,32,128]{3,2,1,0:T(8,128)(2,1)S(1)}, u32[]{:S(2)}, u32[]{:S(2)}) %collective-permute-start.7) | collective-permute-done | bytes 458784 | tf_op jit(solution)/shard_map/ppermute | solution.py:968
  86.0 4.4 %banded_products.7 = (bf16[4,18,32,128]{3,2,1,0:T(8,128)(2,1)}, bf16[4,18,32,128]{3,2,1,0:T(8,128)(2,1)}, bf16[4,18,32,128]{3,2,1,0:T(8,128)(2,1)S(1)}) custom-call(s32[4]{0:T(128)S(1)} %pad_add_fusion.ids, s32[40]{0:T(128)S(1)} %get-tuple-element.76.chosen, bf16[8,18,32,128]{3,2,1,0:T(8,128)(2,1)S(1)} %collective-permute-done.9.rest_0_, ...), custom_call_target="tpu_custom_call" | custom-call | flops 452984832 | bytes 1 | tf_op jit(solution)/shard_map/banded_products/pallas_call | solution.py:771
  95.2 10.1 %collective-permute-done.15.rest_2_ = bf16[4,32,32,128]{3,2,1,0:T(8,128)(2,1)} collective-permute-done((bf16[4,32,32,128]{3,2,1,0:T(8,128)(2,1)S(1)}, bf16[4,32,32,128]{3,2,1,0:T(8,128)(2,1)}, u32[]{:S(2)}, u32[]{:S(2)}) %collective-permute-start.15) | collective-permute-done | bytes 1048608 | tf_op jit(solution)/shard_map/ppermute | solution.py:939
  105.2 3.4 %banded_products.8.rest_6_ = bf16[4,32,32,128]{3,2,1,0:T(8,128)(2,1)S(1)} custom-call(s32[4]{0:T(128)S(1)} %pad_add_fusion.ids, s32[8]{0:T(128)S(1)} %reshape.9.chosen, bf16[4,32,32,128]{3,2,1,0:T(8,128)(2,1)S(1)} %collective-permute-done.14.rest_0_, bf16[4,32,32,128]{3,2,1,0:T(8,128)(2,1)S(1)} %get-tuple-element.104.rest_1_, ...), custom_call_target="tpu_custom_call" | custom-call | flops 268435456 | bytes 1 | tf_op jit(solution)/shard_map/banded_products/pallas_call | solution.py:771
  108.7 24.2 %collective-permute-done.12.rest_3_ = bf16[4,18,32,128]{3,2,1,0:T(8,128)(2,1)} collective-permute-done((bf16[4,18,32,128]{3,2,1,0:T(8,128)(2,1)}, bf16[4,18,32,128]{3,2,1,0:T(8,128)(2,1)}, u32[]{:S(2)}, u32[]{:S(2)}) %collective-permute-start.12) | collective-permute-done | bytes 589856 | tf_op jit(solution)/shard_map/ppermute | solution.py:968
  133.0 13.4 %close_layer.3 = (bf16[8,32,32,128]{3,2,1,0:T(8,128)(2,1)S(1)}, f32[8,32,32,128]{3,2,1,0:T(8,128)S(1)}, bf16[4,32,32,128]{3,2,1,0:T(8,128)(2,1)S(1)}, bf16[4,20,...) custom-call(s32[4]{0:T(128)S(1)} %pad_add_fusion.ids, ...), custom_call_target="tpu_custom_call" | custom-call | flops 8589934592 | bytes 1048576 | tf_op jit(solution)/shard_map/close_layer/pallas_call | solution.py:911
  147.9 13.4 %close_layer.4 = (bf16[8,32,32,128]{3,2,1,0:T(8,128)(2,1)S(1)}, f32[8,32,32,128]{3,2,1,0:T(8,128)S(1)}, bf16[4,32,32,128]{3,2,1,0:T(8,128)(2,1)S(1)}, bf16[4,20,...) custom-call(s32[4]{0:T(128)S(1)} %pad_add_fusion.ids, ...), custom_call_target="tpu_custom_call", output_to_operand_aliasing={{0}: (16, {}), {1}: (17, {}), {4}: (18, {}), {6}: (19, {})} | custom-call | flops 8589934592 | bytes 1048576 | tf_op jit(solution)/shard_map/close_layer/pallas_call | solution.py:911
  161.3 3.4 %collective-permute-start.18 = (bf16[4,20,32,128]{3,2,1,0:T(8,128)(2,1)S(1)}, bf16[4,20,32,128]{3,2,1,0:T(8,128)(2,1)S(1)}, u32[]{:S(2)}, u32[]{:S(2)}) collective-permute-start(bf16[4,20,32,128]{3,2,1,0:T(8,128)(2,1)S(1)} %collective-permute-done.17.rest_1_), channel_id=1, source_target_pairs={{0,1},{3,2},{4,5},{7,6},{8,9},{11,10},{12,13},{15,14},{16,17},{19,... | collective-permute-start | bytes 1966088 | tf_op jit(solution)/shard_map/ppermute | solution.py:948
  164.8 5.4 %collective-permute-done.19.rest_4_ = bf16[4,20,32,128]{3,2,1,0:T(8,128)(2,1)S(1)} collective-permute-done((bf16[4,20,32,128]{3,2,1,0:T(8,128)(2,1)S(1)}, bf16[4,20,32,128]{3,2,1,0:T(8,128)(2,1)S(1)}, u32[]{:S(2)}, u32[]{:S(2)}) %collective-permute-start.19) | collective-permute-done | bytes 655392 | tf_op jit(solution)/shard_map/ppermute | solution.py:947
  170.2 2.5 collective-permute-done.23.rest_0_.rest_2_
  173.3 8.6 %collective-permute-done.20.rest_6_ = bf16[4,20,32,128]{3,2,1,0:T(8,128)(2,1)S(1)} collective-permute-done((bf16[4,20,32,128]{3,2,1,0:T(8,128)(2,1)S(1)}, bf16[4,20,32,128]{3,2,1,0:T(8,128)(2,1)S(1)}, u32[]{:S(2)}, u32[]{:S(2)}) %collective-permute-start.20) | collective-permute-done | bytes 655392 | tf_op jit(solution)/shard_map/ppermute | solution.py:946
  182.0 6.7 %collective-permute-start.21 = (bf16[4,20,32,128]{3,2,1,0:T(8,128)(2,1)S(1)}, bf16[4,20,32,128]{3,2,1,0:T(8,128)(2,1)S(1)}, u32[]{:S(2)}, u32[]{:S(2)}) collective-permute-start(bf16[4,20,32,128]{3,2,1,0:T(8,128)(2,1)S(1)} %collective-permute-done.20.rest_6_), channel_id=1, source_target_pairs={{0,1},{3,2},{4,5},{7,6},{8,9},{11,10},{12,13},{15,14},{16,17},{19,... | collective-permute-start | bytes 1966088 | tf_op jit(solution)/shard_map/ppermute | solution.py:948
  188.6 5.3 %collective-permute-done.22.rest_9_ = bf16[4,20,32,128]{3,2,1,0:T(8,128)(2,1)S(1)} collective-permute-done((bf16[4,20,32,128]{3,2,1,0:T(8,128)(2,1)S(1)}, bf16[4,20,32,128]{3,2,1,0:T(8,128)(2,1)S(1)}, u32[]{:S(2)}, u32[]{:S(2)}) %collective-permute-start.22) | collective-permute-done | bytes 655392 | tf_op jit(solution)/shard_map/ppermute | solution.py:947
  194.5 5.9 %banded_products.9 = (bf16[4,20,32,128]{3,2,1,0:T(8,128)(2,1)S(1)}, bf16[4,20,32,128]{3,2,1,0:T(8,128)(2,1)S(1)}, bf16[4,20,32,128]{3,2,1,0:T(8,128)(2,1)S(1)}) custom-call(s32[4]{0:T(128)S(1)} %pad_add_fusion.ids, s32[40]{0:T(128)S(1)} %get-tuple-element.76.chosen, bf16[4,20,32,128]{3,2,1,0:T(8,128)(2,1)S(1)} %get-tuple-element.108.rest_0_, ...), custom_call_target="tpu_custom_call" | custom-call | flops 503316480 | bytes 1 | tf_op jit(solution)/shard_map/banded_products/pallas_call | solution.py:771
  201.5 2.8 collective-permute-start.25
  204.8 9.4 %collective-permute-done.26.rest_1_ = bf16[4,20,32,128]{3,2,1,0:T(8,128)(2,1)S(1)} collective-permute-done((bf16[4,20,32,128]{3,2,1,0:T(8,128)(2,1)S(1)}, bf16[4,20,32,128]{3,2,1,0:T(8,128)(2,1)S(1)}, u32[]{:S(2)}, u32[]{:S(2)}) %collective-permute-start.26) | collective-permute-done | bytes 655392 | tf_op jit(solution)/shard_map/ppermute | solution.py:968
  214.2 22.4 %collective-permute-start.28 = (bf16[8,12,32,128]{3,2,1,0:T(8,128)(2,1)S(1)}, bf16[8,12,32,128]{3,2,1,0:T(8,128)(2,1)S(1)}, u32[]{:S(2)}, u32[]{:S(2)}) collective-permute-start(bf16[8,12,32,128]{3,2,1,0:T(8,128)(2,1)S(1)} %collective-permute-done.27.rest_1_), channel_id=1, source_target_pairs={{0,1},{3,2},{4,5},{7,6},{8,9},{11,10},{12,13},{15,14},{16,17},{19,... | collective-permute-start | bytes 2359304 | tf_op jit(solution)/shard_map/ppermute | solution.py:948
  236.6 9.6 %far_operands.3 = (bf16[4,32,32,128]{3,2,1,0:T(8,128)(2,1)S(1)}, bf16[4,32,32,128]{3,2,1,0:T(8,128)(2,1)S(1)}) custom-call(s32[4]{0:T(128)S(1)} %pad_add_fusion.ids, s32[2,32]{1,0:T(2,128)S(1)} %bitcast.21, s32[10]{0:T(128)S(1)} %get-tuple-element.102.mine, bf16[4,32,32,128]{3,2,1,0:T(8,128)(2,1)S(1)} %collective-permute-done.23.rest_0_.rest_2_, ...), custom_call_target="tpu_custom_call" | custom-call | flops 8589934592 | bytes 1048576 | tf_op jit(solution)/shard_map/far_operands/pallas_call | solution.py:633
  246.7 3.5 %banded_products.10 = (bf16[4,12,32,128]{3,2,1,0:T(8,128)(2,1)S(1)}, bf16[4,12,32,128]{3,2,1,0:T(8,128)(2,1)S(1)}, bf16[4,12,32,128]{3,2,1,0:T(8,128)(2,1)S(1)}) custom-call(s32[4]{0:T(128)S(1)} %pad_add_fusion.ids, s32[40]{0:T(128)S(1)} %get-tuple-element.76.chosen, bf16[8,12,32,128]{3,2,1,0:T(8,128)(2,1)S(1)} %get-tuple-element.132.rest_0_, ...), custom_call_target="tpu_custom_call" | custom-call | flops 301989888 | bytes 1 | tf_op jit(solution)/shard_map/banded_products/pallas_call | solution.py:771
  251.3 14.9 %collective-permute-done.32.rest_1_ = bf16[4,32,32,128]{3,2,1,0:T(8,128)(2,1)S(1)} collective-permute-done((bf16[4,32,32,128]{3,2,1,0:T(8,128)(2,1)S(1)}, bf16[4,32,32,128]{3,2,1,0:T(8,128)(2,1)S(1)}, u32[]{:S(2)}, u32[]{:S(2)}) %collective-permute-start.32) | collective-permute-done | bytes 1048608 | tf_op jit(solution)/shard_map/ppermute | solution.py:946
  268.8 13.6 %collective-permute-done.34.rest_4_ = bf16[4,32,32,128]{3,2,1,0:T(8,128)(2,1)S(1)} collective-permute-done((bf16[4,32,32,128]{3,2,1,0:T(8,128)(2,1)S(1)}, bf16[4,32,32,128]{3,2,1,0:T(8,128)(2,1)S(1)}, u32[]{:S(2)}, u32[]{:S(2)}) %collective-permute-start.34) | collective-permute-done | bytes 1048608 | tf_op jit(solution)/shard_map/ppermute | solution.py:947
  282.3 2.4 banded_products.11.rest_6_
  284.7 8.8 %close_layer.5 = bf16[8,32,32,128]{3,2,1,0:T(8,128)(2,1)} custom-call(s32[4]{0:T(128)S(1)} %pad_add_fusion.ids, s32[2,32]{1,0:T(2,128)S(1)} %bitcast.22, s32[16]{0:T(128)S(1)} %get-tuple-element.91.place, bf16[4,20,32,128]{3,2,1,0:T(8,128)(2,1)S(1)} %collective-permute-done.25.rest_0_, bf16[4,20,32,128]{3,2,1,0:T(8,128)(2,1)S(1)} %collective-permute-done.26.rest_1_, ...), custom_call_target="tpu_custom_call" | custom-call | flops 8589934592 | bytes 1048576 | tf_op jit(solution)/shard_map/close_layer/pallas_call | solution.py:911
  (95 shorter events, 30.8 us)
Async XLA Ops:
  0.0 52.0 %collective-permute-start.6 = (bf16[8,32,32,128]{3,2,1,0:T(8,128)(2,1)}, bf16[8,32,32,128]{3,2,1,0:T(8,128)(2,1)}, u32[]{:S(2)}, u32[]{:S(2)}) collective-permute-start(bf16[8,32,32,128]{3,2,1,0:T(8,128)(2,1)} %rest_7_.3), channel_id=1, source_target_pairs={{0,4},{4,8},{8,12},{12,0},{1,5},{5,9},{9,13},{13,1},{2,6},{6,10},{... | collective-permute-start | bytes 6291464 | tf_op jit(solution)/shard_map/ppermute | solution.py:968
  11.6 14.6 %collective-permute-start.2 = (bf16[4,14,32,128]{3,2,1,0:T(8,128)(2,1)S(1)}, bf16[4,14,32,128]{3,2,1,0:T(8,128)(2,1)S(1)}, u32[]{:S(2)}, u32[]{:S(2)}) collective-permute-start(bf16[4,14,32,128]{3,2,1,0:T(8,128)(2,1)S(1)} %get-tuple-element.78.rest_3_), channel_id=1, source_target_pairs={{1,2},{2,1},{5,6},{6,5},{9,10},{10,9},{13,14},{14,13},{17,18},{18,... | collective-permute-start | bytes 1376264 | tf_op jit(solution)/shard_map/ppermute | solution.py:940
  12.3 13.9 %collective-permute-start.1 = (bf16[4,14,32,128]{3,2,1,0:T(8,128)(2,1)S(1)}, bf16[4,14,32,128]{3,2,1,0:T(8,128)(2,1)S(1)}, u32[]{:S(2)}, u32[]{:S(2)}) collective-permute-start(bf16[4,14,32,128]{3,2,1,0:T(8,128)(2,1)S(1)} %get-tuple-element.78.rest_3_), channel_id=1, source_target_pairs={{0,2},{3,1},{1,0},{2,3},{4,6},{7,5},{5,4},{6,7},{8,10},{11,9},{9,8... | collective-permute-start | bytes 1376264 | tf_op jit(solution)/shard_map/ppermute | solution.py:939
  27.9 12.1 %collective-permute-start.4 = (bf16[4,14,32,128]{3,2,1,0:T(8,128)(2,1)S(1)}, bf16[4,14,32,128]{3,2,1,0:T(8,128)(2,1)S(1)}, u32[]{:S(2)}, u32[]{:S(2)}) collective-permute-start(bf16[4,14,32,128]{3,2,1,0:T(8,128)(2,1)S(1)} %get-tuple-element.85.rest_8_), channel_id=1, source_target_pairs={{0,2},{3,1},{1,0},{2,3},{4,6},{7,5},{5,4},{6,7},{8,10},{11,9},{9,8... | collective-permute-start | bytes 1376264 | tf_op jit(solution)/shard_map/ppermute | solution.py:939
  46.9 18.6 %collective-permute-start.11 = (bf16[8,18,32,128]{3,2,1,0:T(8,128)(2,1)S(1)}, bf16[8,18,32,128]{3,2,1,0:T(8,128)(2,1)S(1)}, u32[]{:S(2)}, u32[]{:S(2)}) collective-permute-start(bf16[8,18,32,128]{3,2,1,0:T(8,128)(2,1)S(1)} %get-tuple-element.96.rest_3_), channel_id=1, source_target_pairs={{1,2},{2,1},{5,6},{6,5},{9,10},{10,9},{13,14},{14,13},{17,18},{18,... | collective-permute-start | bytes 3538952 | tf_op jit(solution)/shard_map/ppermute | solution.py:940
  47.6 38.4 %collective-permute-start.10 = (bf16[8,18,32,128]{3,2,1,0:T(8,128)(2,1)S(1)}, bf16[8,18,32,128]{3,2,1,0:T(8,128)(2,1)S(1)}, u32[]{:S(2)}, u32[]{:S(2)}) collective-permute-start(bf16[8,18,32,128]{3,2,1,0:T(8,128)(2,1)S(1)} %get-tuple-element.96.rest_3_), channel_id=1, source_target_pairs={{0,2},{3,1},{1,0},{2,3},{4,6},{7,5},{5,4},{6,7},{8,10},{11,9},{9,8... | collective-permute-start | bytes 3538952 | tf_op jit(solution)/shard_map/ppermute | solution.py:939
  52.0 34.0 %collective-permute-start.9 = (bf16[8,18,32,128]{3,2,1,0:T(8,128)(2,1)S(1)}, bf16[8,18,32,128]{3,2,1,0:T(8,128)(2,1)S(1)}, u32[]{:S(2)}, u32[]{:S(2)}) collective-permute-start(bf16[8,18,32,128]{3,2,1,0:T(8,128)(2,1)S(1)} %get-tuple-element.94.rest_1_), channel_id=1, source_target_pairs={{0,1},{1,0},{2,3},{3,2},{4,5},{5,4},{6,7},{7,6},{8,9},{9,8},{10,11... | collective-permute-start | bytes 3538952 | tf_op jit(solution)/shard_map/ppermute | solution.py:938
  52.0 25.5 %collective-permute-start.8 = (bf16[4,14,32,128]{3,2,1,0:T(8,128)(2,1)S(1)}, bf16[4,14,32,128]{3,2,1,0:T(8,128)(2,1)S(1)}, u32[]{:S(2)}, u32[]{:S(2)}) collective-permute-start(bf16[4,14,32,128]{3,2,1,0:T(8,128)(2,1)S(1)} %get-tuple-element.89), channel_id=1, source_target_pairs={{0,12},{4,0},{8,4},{12,8},{1,13},{5,1},{9,5},{13,9},{2,14},{6,2},{... | collective-permute-start | bytes 1376264 | tf_op jit(solution)/shard_map/ppermute | solution.py:968
  52.2 31.8 %collective-permute-start.7 = (bf16[4,14,32,128]{3,2,1,0:T(8,128)(2,1)S(1)}, bf16[4,14,32,128]{3,2,1,0:T(8,128)(2,1)S(1)}, u32[]{:S(2)}, u32[]{:S(2)}) collective-permute-start(bf16[4,14,32,128]{3,2,1,0:T(8,128)(2,1)S(1)} %get-tuple-element.87), channel_id=1, source_target_pairs={{0,8},{4,12},{8,0},{12,4},{1,9},{5,13},{9,1},{13,5},{2,10},{6,14},... | collective-permute-start | bytes 1376264 | tf_op jit(solution)/shard_map/ppermute | solution.py:968
  65.5 29.6 %collective-permute-start.14 = (bf16[4,32,32,128]{3,2,1,0:T(8,128)(2,1)S(1)}, bf16[4,32,32,128]{3,2,1,0:T(8,128)(2,1)S(1)}, u32[]{:S(2)}, u32[]{:S(2)}) collective-permute-start(bf16[4,32,32,128]{3,2,1,0:T(8,128)(2,1)S(1)} %get-tuple-element.104.rest_1_), channel_id=1, source_target_pairs={{0,1},{1,0},{2,3},{3,2},{4,5},{5,4},{6,7},{7,6},{8,9},{9,8},{10,11... | collective-permute-start | bytes 3145736 | tf_op jit(solution)/shard_map/ppermute | solution.py:938
  78.3 16.9 %collective-permute-start.16 = (bf16[4,32,32,128]{3,2,1,0:T(8,128)(2,1)S(1)}, bf16[4,32,32,128]{3,2,1,0:T(8,128)(2,1)}, u32[]{:S(2)}, u32[]{:S(2)}) collective-permute-start(bf16[4,32,32,128]{3,2,1,0:T(8,128)(2,1)S(1)} %get-tuple-element.105.rest_3_), channel_id=1, source_target_pairs={{1,2},{2,1},{5,6},{6,5},{9,10},{10,9},{13,14},{14,13},{17,18},{18,... | collective-permute-start | bytes 3145736 | tf_op jit(solution)/shard_map/ppermute | solution.py:940
  84.8 20.4 %collective-permute-start.15 = (bf16[4,32,32,128]{3,2,1,0:T(8,128)(2,1)S(1)}, bf16[4,32,32,128]{3,2,1,0:T(8,128)(2,1)}, u32[]{:S(2)}, u32[]{:S(2)}) collective-permute-start(bf16[4,32,32,128]{3,2,1,0:T(8,128)(2,1)S(1)} %get-tuple-element.105.rest_3_), channel_id=1, source_target_pairs={{0,2},{3,1},{1,0},{2,3},{4,6},{7,5},{5,4},{6,7},{8,10},{11,9},{9,8... | collective-permute-start | bytes 3145736 | tf_op jit(solution)/shard_map/ppermute | solution.py:939
  91.3 17.4 %collective-permute-start.13 = (bf16[4,18,32,128]{3,2,1,0:T(8,128)(2,1)}, bf16[4,18,32,128]{3,2,1,0:T(8,128)(2,1)}, u32[]{:S(2)}, u32[]{:S(2)}) collective-permute-start(bf16[4,18,32,128]{3,2,1,0:T(8,128)(2,1)} %get-tuple-element.100), channel_id=1, source_target_pairs={{0,12},{4,0},{8,4},{12,8},{1,13},{5,1},{9,5},{13,9},{2,14},{6,2},{... | collective-permute-start | bytes 1769480 | tf_op jit(solution)/shard_map/ppermute | solution.py:968
  92.3 40.6 %collective-permute-start.12 = (bf16[4,18,32,128]{3,2,1,0:T(8,128)(2,1)}, bf16[4,18,32,128]{3,2,1,0:T(8,128)(2,1)}, u32[]{:S(2)}, u32[]{:S(2)}) collective-permute-start(bf16[4,18,32,128]{3,2,1,0:T(8,128)(2,1)} %get-tuple-element.98), channel_id=1, source_target_pairs={{0,8},{4,12},{8,0},{12,4},{1,9},{5,13},{9,1},{13,5},{2,10},{6,14},... | collective-permute-start | bytes 1769480 | tf_op jit(solution)/shard_map/ppermute | solution.py:968
  146.4 14.9 %collective-permute-start.17 = (bf16[4,20,32,128]{3,2,1,0:T(8,128)(2,1)S(1)}, bf16[4,20,32,128]{3,2,1,0:T(8,128)(2,1)S(1)}, u32[]{:S(2)}, u32[]{:S(2)}) collective-permute-start(bf16[4,20,32,128]{3,2,1,0:T(8,128)(2,1)S(1)} %get-tuple-element.108.rest_0_), channel_id=1, source_target_pairs={{1,3},{2,0},{0,1},{3,2},{5,7},{6,4},{4,5},{7,6},{9,11},{10,8},{8,9... | collective-permute-start | bytes 1966088 | tf_op jit(solution)/shard_map/ppermute | solution.py:946
  146.6 23.6 %collective-permute-start.19 = (bf16[4,20,32,128]{3,2,1,0:T(8,128)(2,1)S(1)}, bf16[4,20,32,128]{3,2,1,0:T(8,128)(2,1)S(1)}, u32[]{:S(2)}, u32[]{:S(2)}) collective-permute-start(bf16[4,20,32,128]{3,2,1,0:T(8,128)(2,1)S(1)} %get-tuple-element.115.rest_3_), channel_id=1, source_target_pairs={{0,2},{2,0},{1,3},{3,1},{4,6},{6,4},{5,7},{7,5},{8,10},{10,8},{9,1... | collective-permute-start | bytes 1966088 | tf_op jit(solution)/shard_map/ppermute | solution.py:947
  147.9 24.8 %collective-permute-start.23 = (bf16[4,32,32,128]{3,2,1,0:T(8,128)(2,1)S(1)}, bf16[4,32,32,128]{3,2,1,0:T(8,128)(2,1)S(1)}, u32[]{:S(2)}, u32[]{:S(2)}) collective-permute-start(bf16[4,32,32,128]{3,2,1,0:T(8,128)(2,1)S(1)} %get-tuple-element.123), channel_id=1, source_target_pairs={{0,4},{4,8},{8,12},{12,0},{1,5},{5,9},{9,13},{13,1},{2,6},{6,10},{... | collective-permute-start | bytes 3145736 | tf_op jit(solution)/shard_map/ppermute | solution.py:968
  161.3 12.0 %collective-permute-start.18 = (bf16[4,20,32,128]{3,2,1,0:T(8,128)(2,1)S(1)}, bf16[4,20,32,128]{3,2,1,0:T(8,128)(2,1)S(1)}, u32[]{:S(2)}, u32[]{:S(2)}) collective-permute-start(bf16[4,20,32,128]{3,2,1,0:T(8,128)(2,1)S(1)} %collective-permute-done.17.rest_1_), channel_id=1, source_target_pairs={{0,1},{3,2},{4,5},{7,6},{8,9},{11,10},{12,13},{15,14},{16,17},{19,... | collective-permute-start | bytes 1966088 | tf_op jit(solution)/shard_map/ppermute | solution.py:948
  170.2 11.7 %collective-permute-start.20 = (bf16[4,20,32,128]{3,2,1,0:T(8,128)(2,1)S(1)}, bf16[4,20,32,128]{3,2,1,0:T(8,128)(2,1)S(1)}, u32[]{:S(2)}, u32[]{:S(2)}) collective-permute-start(bf16[4,20,32,128]{3,2,1,0:T(8,128)(2,1)S(1)} %get-tuple-element.117.rest_5_), channel_id=1, source_target_pairs={{1,3},{2,0},{0,1},{3,2},{5,7},{6,4},{4,5},{7,6},{9,11},{10,8},{8,9... | collective-permute-start | bytes 1966088 | tf_op jit(solution)/shard_map/ppermute | solution.py:946
  172.7 27.7 %collective-permute-start.24 = (bf16[4,32,32,128]{3,2,1,0:T(8,128)(2,1)S(1)}, bf16[4,32,32,128]{3,2,1,0:T(8,128)(2,1)S(1)}, u32[]{:S(2)}, u32[]{:S(2)}) collective-permute-start(bf16[4,32,32,128]{3,2,1,0:T(8,128)(2,1)S(1)} %get-tuple-element.124), channel_id=1, source_target_pairs={{0,4},{4,8},{8,12},{12,0},{1,5},{5,9},{9,13},{13,1},{2,6},{6,10},{... | collective-permute-start | bytes 3145736 | tf_op jit(solution)/shard_map/ppermute | solution.py:968
  173.3 20.7 %collective-permute-start.22 = (bf16[4,20,32,128]{3,2,1,0:T(8,128)(2,1)S(1)}, bf16[4,20,32,128]{3,2,1,0:T(8,128)(2,1)S(1)}, u32[]{:S(2)}, u32[]{:S(2)}) collective-permute-start(bf16[4,20,32,128]{3,2,1,0:T(8,128)(2,1)S(1)} %get-tuple-element.120.rest_8_), channel_id=1, source_target_pairs={{0,2},{2,0},{1,3},{3,1},{4,6},{6,4},{5,7},{7,5},{8,10},{10,8},{9,1... | collective-permute-start | bytes 1966088 | tf_op jit(solution)/shard_map/ppermute | solution.py:947
  182.0 12.0 %collective-permute-start.21 = (bf16[4,20,32,128]{3,2,1,0:T(8,128)(2,1)S(1)}, bf16[4,20,32,128]{3,2,1,0:T(8,128)(2,1)S(1)}, u32[]{:S(2)}, u32[]{:S(2)}) collective-permute-start(bf16[4,20,32,128]{3,2,1,0:T(8,128)(2,1)S(1)} %collective-permute-done.20.rest_6_), channel_id=1, source_target_pairs={{0,1},{3,2},{4,5},{7,6},{8,9},{11,10},{12,13},{15,14},{16,17},{19,... | collective-permute-start | bytes 1966088 | tf_op jit(solution)/shard_map/ppermute | solution.py:948
  194.0 10.8 %collective-permute-start.27 = (bf16[8,12,32,128]{3,2,1,0:T(8,128)(2,1)S(1)}, bf16[8,12,32,128]{3,2,1,0:T(8,128)(2,1)S(1)}, u32[]{:S(2)}, u32[]{:S(2)}) collective-permute-start(bf16[8,12,32,128]{3,2,1,0:T(8,128)(2,1)S(1)} %get-tuple-element.132.rest_0_), channel_id=1, source_target_pairs={{1,3},{2,0},{0,1},{3,2},{5,7},{6,4},{4,5},{7,6},{9,11},{10,8},{8,9... | collective-permute-start | bytes 2359304 | tf_op jit(solution)/shard_map/ppermute | solution.py:946
  200.4 13.8 %collective-permute-start.26 = (bf16[4,20,32,128]{3,2,1,0:T(8,128)(2,1)S(1)}, bf16[4,20,32,128]{3,2,1,0:T(8,128)(2,1)S(1)}, u32[]{:S(2)}, u32[]{:S(2)}) collective-permute-start(bf16[4,20,32,128]{3,2,1,0:T(8,128)(2,1)S(1)} %get-tuple-element.127), channel_id=1, source_target_pairs={{0,12},{4,0},{8,4},{12,8},{1,13},{5,1},{9,5},{13,9},{2,14},{6,2},{... | collective-permute-start | bytes 1966088 | tf_op jit(solution)/shard_map/ppermute | solution.py:968
  201.0 45.7 %collective-permute-start.29 = (bf16[8,12,32,128]{3,2,1,0:T(8,128)(2,1)S(1)}, bf16[8,12,32,128]{3,2,1,0:T(8,128)(2,1)S(1)}, u32[]{:S(2)}, u32[]{:S(2)}) collective-permute-start(bf16[8,12,32,128]{3,2,1,0:T(8,128)(2,1)S(1)} %get-tuple-element.134.rest_3_), channel_id=1, source_target_pairs={{0,2},{2,0},{1,3},{3,1},{4,6},{6,4},{5,7},{7,5},{8,10},{10,8},{9,1... | collective-permute-start | bytes 2359304 | tf_op jit(solution)/shard_map/ppermute | solution.py:947
  201.5 45.3 %collective-permute-start.25 = (bf16[4,20,32,128]{3,2,1,0:T(8,128)(2,1)S(1)}, bf16[4,20,32,128]{3,2,1,0:T(8,128)(2,1)S(1)}, u32[]{:S(2)}, u32[]{:S(2)}) collective-permute-start(bf16[4,20,32,128]{3,2,1,0:T(8,128)(2,1)S(1)} %get-tuple-element.125), channel_id=1, source_target_pairs={{0,8},{4,12},{8,0},{12,4},{1,9},{5,13},{9,1},{13,5},{2,10},{6,14},... | collective-permute-start | bytes 1966088 | tf_op jit(solution)/shard_map/ppermute | solution.py:968
  214.2 32.5 %collective-permute-start.28 = (bf16[8,12,32,128]{3,2,1,0:T(8,128)(2,1)S(1)}, bf16[8,12,32,128]{3,2,1,0:T(8,128)(2,1)S(1)}, u32[]{:S(2)}, u32[]{:S(2)}) collective-permute-start(bf16[8,12,32,128]{3,2,1,0:T(8,128)(2,1)S(1)} %collective-permute-done.27.rest_1_), channel_id=1, source_target_pairs={{0,1},{3,2},{4,5},{7,6},{8,9},{11,10},{12,13},{15,14},{16,17},{19,... | collective-permute-start | bytes 2359304 | tf_op jit(solution)/shard_map/ppermute | solution.py:948
  246.2 20.0 %collective-permute-start.32 = (bf16[4,32,32,128]{3,2,1,0:T(8,128)(2,1)S(1)}, bf16[4,32,32,128]{3,2,1,0:T(8,128)(2,1)S(1)}, u32[]{:S(2)}, u32[]{:S(2)}) collective-permute-start(bf16[4,32,32,128]{3,2,1,0:T(8,128)(2,1)S(1)} %get-tuple-element.142.rest_0_), channel_id=1, source_target_pairs={{1,3},{2,0},{0,1},{3,2},{5,7},{6,4},{4,5},{7,6},{9,11},{10,8},{8,9... | collective-permute-start | bytes 3145736 | tf_op jit(solution)/shard_map/ppermute | solution.py:946
  250.2 16.0 %collective-permute-start.31 = (bf16[4,12,32,128]{3,2,1,0:T(8,128)(2,1)S(1)}, bf16[4,12,32,128]{3,2,1,0:T(8,128)(2,1)S(1)}, u32[]{:S(2)}, u32[]{:S(2)}) collective-permute-start(bf16[4,12,32,128]{3,2,1,0:T(8,128)(2,1)S(1)} %get-tuple-element.138), channel_id=1, source_target_pairs={{0,12},{4,0},{8,4},{12,8},{1,13},{5,1},{9,5},{13,9},{2,14},{6,2},{... | collective-permute-start | bytes 1179656 | tf_op jit(solution)/shard_map/ppermute | solution.py:968
  250.3 32.0 %collective-permute-start.34 = (bf16[4,32,32,128]{3,2,1,0:T(8,128)(2,1)S(1)}, bf16[4,32,32,128]{3,2,1,0:T(8,128)(2,1)S(1)}, u32[]{:S(2)}, u32[]{:S(2)}) collective-permute-start(bf16[4,32,32,128]{3,2,1,0:T(8,128)(2,1)S(1)} %get-tuple-element.144.rest_3_), channel_id=1, source_target_pairs={{0,2},{2,0},{1,3},{3,1},{4,6},{6,4},{5,7},{7,5},{8,10},{10,8},{9,1... | collective-permute-start | bytes 3145736 | tf_op jit(solution)/shard_map/ppermute | solution.py:947
  266.2 16.1 %collective-permute-start.33 = (bf16[4,32,32,128]{3,2,1,0:T(8,128)(2,1)S(1)}, bf16[4,32,32,128]{3,2,1,0:T(8,128)(2,1)S(1)}, u32[]{:S(2)}, u32[]{:S(2)}) collective-permute-start(bf16[4,32,32,128]{3,2,1,0:T(8,128)(2,1)S(1)} %collective-permute-done.32.rest_1_), channel_id=1, source_target_pairs={{0,1},{3,2},{4,5},{7,6},{8,9},{11,10},{12,13},{15,14},{16,17},{19,... | collective-permute-start | bytes 3145736 | tf_op jit(solution)/shard_map/ppermute | solution.py:948
  267.6 17.1 %collective-permute-start.30 = (bf16[4,12,32,128]{3,2,1,0:T(8,128)(2,1)S(1)}, bf16[4,12,32,128]{3,2,1,0:T(8,128)(2,1)S(1)}, u32[]{:S(2)}, u32[]{:S(2)}) collective-permute-start(bf16[4,12,32,128]{3,2,1,0:T(8,128)(2,1)S(1)} %get-tuple-element.136), channel_id=1, source_target_pairs={{0,8},{4,12},{8,0},{12,4},{1,9},{5,13},{9,1},{13,5},{2,10},{6,14},... | collective-permute-start | bytes 1179656 | tf_op jit(solution)/shard_map/ppermute | solution.py:968
  (22 other events, 328.2 us)

commit v18 on v15

--- a/solution.py
+++ b/solution.py
@@ -506,7 +506,7 @@
     normed = layer_norm(values)
     if gate_ref is not None:
         gate = sigmoid(dot(normed.astype(jnp.bfloat16), w_ref[0, :, -channels:]))
-        gate_ref[0, pl.ds(at, rows)] = gate.reshape(rows, cols, channels)
+        gate_ref[0, pl.ds(at, rows)] = gate.reshape(rows, cols, channels).astype(gate_ref.dtype)
     mask = row_alive[at : at + rows, None, :] * col_alive[None, :, :]
     norm_ref[pl.ds(at, rows)] = (normed.reshape(rows, cols, channels) * mask).astype(jnp.bfloat16)
 
@@ -562,7 +562,7 @@
 
 def open_operands(ids, blocks, pair, chains, w_in, wide, hidden, bands, base, count, earlier):
     slots, rows, cols, channels = pair.shape
-    out_shape = [jax.ShapeDtypeStruct(pair.shape, jnp.float32)] + operand_outputs(slots, count, rows, hidden, bands)
+    out_shape = [jax.ShapeDtypeStruct(pair.shape, jnp.bfloat16)] + operand_outputs(slots, count, rows, hidden, bands)
     more, more_specs, aliases = fill(out_shape, earlier, slots, 6)
     return pl.pallas_call(
         functools.partial(open_kernel, hidden, len(bands), lax.axis_size("chan"), lax.axis_size("sub"), base, slots),
@@ -866,7 +866,7 @@
         change = jnp.concatenate(
             [update[g * cols : (g + 1) * cols, a * channels : (a + 1) * channels] for a in range(parts)]
         )
-        gate = gate_ref[0, taken].reshape(parts * cols, channels)
+        gate = gate_ref[0, taken].astype(jnp.float32).reshape(parts * cols, channels)
         current = cur_ref[0, taken].astype(jnp.float32).reshape(parts * cols, channels)
         result = (current + gate * change).astype(jnp.bfloat16)
         out_ref[0, taken] = result.reshape(parts, cols, channels)
@@ -901,7 +901,7 @@
         operands += [chains, w_in, wide]
         in_specs += [pl.BlockSpec(chains.shape, lambda s, *_: (0, 0)), layer_spec(w_in, layer + 1)]
         in_specs += [pl.BlockSpec(wide.shape, lambda s, *_: (0, 0))]
-        out_shape += [jax.ShapeDtypeStruct(current.shape, jnp.float32)]
+        out_shape += [jax.ShapeDtypeStruct(current.shape, jnp.bfloat16)]
         out_shape += [jax.ShapeDtypeStruct((count,) + current.shape[1:], jnp.bfloat16)]
         out_shape += operand_outputs(slots, count, cols, hidden, bands[layer + 1])
         scratch += [pltpu.VMEM((rows, cols, channels), jnp.bfloat16)] + operand_scratch(cols, rows, hidden)

time: 294 us -> 294 us (level)
  no operation moved by 1% of the time
where the time goes in v18:
time: 294 us; the launch traced here: 292 us
  waiting for transfers between devices  113 us (38%)
  Pallas kernels  97.7 us (33%)
  starting transfers between devices  76.7 us (26%)
  local copies, waits for them, and re-layouts  4.35 us (1%)
    ppermute x11, waiting for transfers between devices, over_blk(): lax.ppermute(value, 'blk', [(p, (p + shift) % n_blk) for p in range(n_blk)])  49.9 us
    pallas_call x3, Pallas kernels, close_layer(): pl.pallas_call(functools.partial(close_kernel, *(layer, last, spots, 0 if...  35.4 us
    ppermute x4, starting transfers between devices, exchange_bands_incoming(): lax.ppermute(after(one, other if over is None else over), both, [(0, 1),...  34 us
    ppermute x4, waiting for transfers between devices, exchange_bands_incoming(): other = lax.ppermute(right, 'chan', [(0, 1), (1, 0)])  24.3 us
    ppermute x4, waiting for transfers between devices, exchange_bands_incoming(): one = lax.ppermute(left, both, [(1, 3), (2, 0), (0, 1), (3, 2)])  24.2 us
    pallas_call x6, Pallas kernels, banded_products(): pl.pallas_call(functools.partial(banded_kernel, shifts, capacity, tuple(p...  22.3 us
    pallas_call x2, Pallas kernels, far_operands(): pl.pallas_call(functools.partial(far_kernel, layer, n_blk, far, lax.axis_...  20.6 us
    pallas_call x2, Pallas kernels, open_operands(): pl.pallas_call(functools.partial(open_kernel, hidden, len(bands), lax.axi...  16.6 us
  transfers between devices with their start and end apart: 35, of which 16 were waited for; matrix products, arithmetic and copies ran while one was open for 0% of the time, Pallas kernels for 26%

profile of v18, /device:TPU:11, one launch (start us, length us, event | category | flops | bytes accessed | tf_op | source)
XLA Modules:
  0.0 292.3 jit_solution(17834551933645212393)
XLA Ops:
  3.3 8.3 %open_operands.2 = (bf16[8,32,32,128]{3,2,1,0:T(8,128)(2,1)S(1)}, bf16[4,16,32,128]{3,2,1,0:T(8,128)(2,1)S(1)}, bf16[8,16,32,128]{3,2,1,0:T(8,128)(2,1)S(1)}, bf...) custom-call(s32[4]{0:T(128)S(1)} %pad_add_fusion.ids, s32[2,32]{1,0:T(2,128)S(1)} %bitcast.16, ...), custom_call_target="tpu_custom_call" | custom-call | flops 8589934592 | bytes 1048576 | tf_op jit(solution)/shard_map/open_operands/pallas_call | solution.py:567
  12.3 3.5 %collective-permute-start.1 = (bf16[4,16,32,128]{3,2,1,0:T(8,128)(2,1)S(1)}, bf16[4,16,32,128]{3,2,1,0:T(8,128)(2,1)S(1)}, u32[]{:S(2)}, u32[]{:S(2)}) collective-permute-start(bf16[4,16,32,128]{3,2,1,0:T(8,128)(2,1)S(1)} %get-tuple-element.78.rest_3_), channel_id=1, source_target_pairs={{0,2},{3,1},{1,0},{2,3},{4,6},{7,5},{5,4},{6,7},{8,10},{11,9},{9,8... | collective-permute-start | bytes 1572872 | tf_op jit(solution)/shard_map/ppermute | solution.py:939
  15.8 8.3 %open_operands.3 = (bf16[8,32,32,128]{3,2,1,0:T(8,128)(2,1)S(1)}, bf16[4,16,32,128]{3,2,1,0:T(8,128)(2,1)S(1)}, bf16[8,16,32,128]{3,2,1,0:T(8,128)(2,1)S(1)}, bf...) custom-call(s32[4]{0:T(128)S(1)} %pad_add_fusion.ids, ...), custom_call_target="tpu_custom_call", output_to_operand_aliasing={{0}: (6, {}), {2}: (7, {}), {4}: (8, {})} | custom-call | flops 8589934592 | bytes 1048576 | tf_op jit(solution)/shard_map/open_operands/pallas_call | solution.py:567
  29.3 2.6 collective-permute-start.4
  33.6 9.2 %collective-permute-done.4.rest_7_ = bf16[4,16,32,128]{3,2,1,0:T(8,128)(2,1)S(1)} collective-permute-done((bf16[4,16,32,128]{3,2,1,0:T(8,128)(2,1)S(1)}, bf16[4,16,32,128]{3,2,1,0:T(8,128)(2,1)S(1)}, u32[]{:S(2)}, u32[]{:S(2)}) %collective-permute-start.4) | collective-permute-done | bytes 524320 | tf_op jit(solution)/shard_map/ppermute | solution.py:939
  42.9 3.6 %banded_products.6 = (bf16[4,16,32,128]{3,2,1,0:T(8,128)(2,1)S(1)}, bf16[4,16,32,128]{3,2,1,0:T(8,128)(2,1)S(1)}, bf16[4,16,32,128]{3,2,1,0:T(8,128)(2,1)S(1)}) custom-call(s32[4]{0:T(128)S(1)} %pad_add_fusion.ids, s32[40]{0:T(128)S(1)} %get-tuple-element.76.chosen, bf16[4,16,32,128]{3,2,1,0:T(8,128)(2,1)S(1)} %collective-permute-done.rest_0_, ...), custom_call_target="tpu_custom_call" | custom-call | flops 402653184 | bytes 1 | tf_op jit(solution)/shard_map/banded_products/pallas_call | solution.py:771
  48.0 4.4 %collective-permute-start.10 = (bf16[8,16,32,128]{3,2,1,0:T(8,128)(2,1)S(1)}, bf16[8,16,32,128]{3,2,1,0:T(8,128)(2,1)S(1)}, u32[]{:S(2)}, u32[]{:S(2)}) collective-permute-start(bf16[8,16,32,128]{3,2,1,0:T(8,128)(2,1)S(1)} %get-tuple-element.96.rest_3_), channel_id=1, source_target_pairs={{0,2},{3,1},{1,0},{2,3},{4,6},{7,5},{5,4},{6,7},{8,10},{11,9},{9,8... | collective-permute-start | bytes 3145736 | tf_op jit(solution)/shard_map/ppermute | solution.py:939
  54.9 10.9 %far_operands.2 = (bf16[4,32,32,128]{3,2,1,0:T(8,128)(2,1)S(1)}, bf16[4,32,32,128]{3,2,1,0:T(8,128)(2,1)S(1)}) custom-call(s32[4]{0:T(128)S(1)} %pad_add_fusion.ids, s32[2,32]{1,0:T(2,128)S(1)} %bitcast.18, s32[10]{0:T(128)S(1)} %get-tuple-element.102.mine, bf16[8,32,32,128]{3,2,1,0:T(8,128)(2,1)} %collective-permute-done.6.rest_0_.rest_1_, ...), custom_call_target="tpu_custom_call" | custom-call | flops 8589934592 | bytes 1048576 | tf_op jit(solution)/shard_map/far_operands/pallas_call | solution.py:633
  65.9 9.2 %collective-permute-start.14 = (bf16[4,32,32,128]{3,2,1,0:T(8,128)(2,1)S(1)}, bf16[4,32,32,128]{3,2,1,0:T(8,128)(2,1)S(1)}, u32[]{:S(2)}, u32[]{:S(2)}) collective-permute-start(bf16[4,32,32,128]{3,2,1,0:T(8,128)(2,1)S(1)} %get-tuple-element.104.rest_1_), channel_id=1, source_target_pairs={{0,1},{1,0},{2,3},{3,2},{4,5},{5,4},{6,7},{7,6},{8,9},{9,8},{10,11... | collective-permute-start | bytes 3145736 | tf_op jit(solution)/shard_map/ppermute | solution.py:938
  76.8 11.8 %collective-permute-done.7.rest_0_ = bf16[4,16,32,128]{3,2,1,0:T(8,128)(2,1)S(1)} collective-permute-done((bf16[4,16,32,128]{3,2,1,0:T(8,128)(2,1)S(1)}, bf16[4,16,32,128]{3,2,1,0:T(8,128)(2,1)S(1)}, u32[]{:S(2)}, u32[]{:S(2)}) %collective-permute-start.7) | collective-permute-done | bytes 524320 | tf_op jit(solution)/shard_map/ppermute | solution.py:968
  89.9 3.5 %banded_products.7 = (bf16[4,16,32,128]{3,2,1,0:T(8,128)(2,1)}, bf16[4,16,32,128]{3,2,1,0:T(8,128)(2,1)}, bf16[4,16,32,128]{3,2,1,0:T(8,128)(2,1)S(1)}) custom-call(s32[4]{0:T(128)S(1)} %pad_add_fusion.ids, s32[40]{0:T(128)S(1)} %get-tuple-element.76.chosen, bf16[8,16,32,128]{3,2,1,0:T(8,128)(2,1)S(1)} %collective-permute-done.9.rest_0_, ...), custom_call_target="tpu_custom_call" | custom-call | flops 402653184 | bytes 1 | tf_op jit(solution)/shard_map/banded_products/pallas_call | solution.py:771
  98.0 4.3 %collective-permute-done.15.rest_2_ = bf16[4,32,32,128]{3,2,1,0:T(8,128)(2,1)} collective-permute-done((bf16[4,32,32,128]{3,2,1,0:T(8,128)(2,1)S(1)}, bf16[4,32,32,128]{3,2,1,0:T(8,128)(2,1)}, u32[]{:S(2)}, u32[]{:S(2)}) %collective-permute-start.15) | collective-permute-done | bytes 1048608 | tf_op jit(solution)/shard_map/ppermute | solution.py:939
  102.4 3.4 %banded_products.8.rest_6_ = bf16[4,32,32,128]{3,2,1,0:T(8,128)(2,1)S(1)} custom-call(s32[4]{0:T(128)S(1)} %pad_add_fusion.ids, s32[8]{0:T(128)S(1)} %reshape.9.chosen, bf16[4,32,32,128]{3,2,1,0:T(8,128)(2,1)S(1)} %collective-permute-done.14.rest_0_, bf16[4,32,32,128]{3,2,1,0:T(8,128)(2,1)S(1)} %get-tuple-element.104.rest_1_, ...), custom_call_target="tpu_custom_call" | custom-call | flops 268435456 | bytes 1 | tf_op jit(solution)/shard_map/banded_products/pallas_call | solution.py:771
  108.2 23.4 %collective-permute-done.12.rest_3_ = bf16[4,16,32,128]{3,2,1,0:T(8,128)(2,1)} collective-permute-done((bf16[4,16,32,128]{3,2,1,0:T(8,128)(2,1)}, bf16[4,16,32,128]{3,2,1,0:T(8,128)(2,1)}, u32[]{:S(2)}, u32[]{:S(2)}) %collective-permute-start.12) | collective-permute-done | bytes 524320 | tf_op jit(solution)/shard_map/ppermute | solution.py:968
  131.6 13.3 %close_layer.3 = (bf16[8,32,32,128]{3,2,1,0:T(8,128)(2,1)S(1)}, bf16[8,32,32,128]{3,2,1,0:T(8,128)(2,1)S(1)}, bf16[4,32,32,128]{3,2,1,0:T(8,128)(2,1)S(1)}, bf16...) custom-call(s32[4]{0:T(128)S(1)} %pad_add_fusion.ids, ...), custom_call_target="tpu_custom_call" | custom-call | flops 8589934592 | bytes 1048576 | tf_op jit(solution)/shard_map/close_layer/pallas_call | solution.py:911
  146.4 13.2 %close_layer.4 = (bf16[8,32,32,128]{3,2,1,0:T(8,128)(2,1)S(1)}, bf16[8,32,32,128]{3,2,1,0:T(8,128)(2,1)S(1)}, bf16[4,32,32,128]{3,2,1,0:T(8,128)(2,1)S(1)}, bf16...) custom-call(s32[4]{0:T(128)S(1)} %pad_add_fusion.ids, ...), custom_call_target="tpu_custom_call", output_to_operand_aliasing={{0}: (16, {}), {1}: (17, {}), {4}: (18, {}), {6}: (19, {})} | custom-call | flops 8589934592 | bytes 1048576 | tf_op jit(solution)/shard_map/close_layer/pallas_call | solution.py:911
  159.7 3.5 %collective-permute-start.18 = (bf16[4,20,32,128]{3,2,1,0:T(8,128)(2,1)S(1)}, bf16[4,20,32,128]{3,2,1,0:T(8,128)(2,1)S(1)}, u32[]{:S(2)}, u32[]{:S(2)}) collective-permute-start(bf16[4,20,32,128]{3,2,1,0:T(8,128)(2,1)S(1)} %collective-permute-done.17.rest_1_), channel_id=1, source_target_pairs={{0,1},{3,2},{4,5},{7,6},{8,9},{11,10},{12,13},{15,14},{16,17},{19,... | collective-permute-start | bytes 1966088 | tf_op jit(solution)/shard_map/ppermute | solution.py:948
  163.2 5.4 %collective-permute-done.19.rest_4_ = bf16[4,20,32,128]{3,2,1,0:T(8,128)(2,1)S(1)} collective-permute-done((bf16[4,20,32,128]{3,2,1,0:T(8,128)(2,1)S(1)}, bf16[4,20,32,128]{3,2,1,0:T(8,128)(2,1)S(1)}, u32[]{:S(2)}, u32[]{:S(2)}) %collective-permute-start.19) | collective-permute-done | bytes 655392 | tf_op jit(solution)/shard_map/ppermute | solution.py:947
  168.7 2.5 collective-permute-done.23.rest_0_.rest_2_
  171.8 8.6 %collective-permute-done.20.rest_6_ = bf16[4,20,32,128]{3,2,1,0:T(8,128)(2,1)S(1)} collective-permute-done((bf16[4,20,32,128]{3,2,1,0:T(8,128)(2,1)S(1)}, bf16[4,20,32,128]{3,2,1,0:T(8,128)(2,1)S(1)}, u32[]{:S(2)}, u32[]{:S(2)}) %collective-permute-start.20) | collective-permute-done | bytes 655392 | tf_op jit(solution)/shard_map/ppermute | solution.py:946
  180.4 6.7 %collective-permute-start.21 = (bf16[4,20,32,128]{3,2,1,0:T(8,128)(2,1)S(1)}, bf16[4,20,32,128]{3,2,1,0:T(8,128)(2,1)S(1)}, u32[]{:S(2)}, u32[]{:S(2)}) collective-permute-start(bf16[4,20,32,128]{3,2,1,0:T(8,128)(2,1)S(1)} %collective-permute-done.20.rest_6_), channel_id=1, source_target_pairs={{0,1},{3,2},{4,5},{7,6},{8,9},{11,10},{12,13},{15,14},{16,17},{19,... | collective-permute-start | bytes 1966088 | tf_op jit(solution)/shard_map/ppermute | solution.py:948
  187.1 5.3 %collective-permute-done.22.rest_9_ = bf16[4,20,32,128]{3,2,1,0:T(8,128)(2,1)S(1)} collective-permute-done((bf16[4,20,32,128]{3,2,1,0:T(8,128)(2,1)S(1)}, bf16[4,20,32,128]{3,2,1,0:T(8,128)(2,1)S(1)}, u32[]{:S(2)}, u32[]{:S(2)}) %collective-permute-start.22) | collective-permute-done | bytes 655392 | tf_op jit(solution)/shard_map/ppermute | solution.py:947
  193.0 5.9 %banded_products.9 = (bf16[4,20,32,128]{3,2,1,0:T(8,128)(2,1)S(1)}, bf16[4,20,32,128]{3,2,1,0:T(8,128)(2,1)S(1)}, bf16[4,20,32,128]{3,2,1,0:T(8,128)(2,1)S(1)}) custom-call(s32[4]{0:T(128)S(1)} %pad_add_fusion.ids, s32[40]{0:T(128)S(1)} %get-tuple-element.76.chosen, bf16[4,20,32,128]{3,2,1,0:T(8,128)(2,1)S(1)} %get-tuple-element.108.rest_0_, ...), custom_call_target="tpu_custom_call" | custom-call | flops 503316480 | bytes 1 | tf_op jit(solution)/shard_map/banded_products/pallas_call | solution.py:771
  199.9 2.8 collective-permute-start.25
  203.3 9.4 %collective-permute-done.26.rest_1_ = bf16[4,20,32,128]{3,2,1,0:T(8,128)(2,1)S(1)} collective-permute-done((bf16[4,20,32,128]{3,2,1,0:T(8,128)(2,1)S(1)}, bf16[4,20,32,128]{3,2,1,0:T(8,128)(2,1)S(1)}, u32[]{:S(2)}, u32[]{:S(2)}) %collective-permute-start.26) | collective-permute-done | bytes 655392 | tf_op jit(solution)/shard_map/ppermute | solution.py:968
  212.6 22.4 %collective-permute-start.28 = (bf16[8,12,32,128]{3,2,1,0:T(8,128)(2,1)S(1)}, bf16[8,12,32,128]{3,2,1,0:T(8,128)(2,1)S(1)}, u32[]{:S(2)}, u32[]{:S(2)}) collective-permute-start(bf16[8,12,32,128]{3,2,1,0:T(8,128)(2,1)S(1)} %collective-permute-done.27.rest_1_), channel_id=1, source_target_pairs={{0,1},{3,2},{4,5},{7,6},{8,9},{11,10},{12,13},{15,14},{16,17},{19,... | collective-permute-start | bytes 2359304 | tf_op jit(solution)/shard_map/ppermute | solution.py:948
  235.1 9.6 %far_operands.3 = (bf16[4,32,32,128]{3,2,1,0:T(8,128)(2,1)S(1)}, bf16[4,32,32,128]{3,2,1,0:T(8,128)(2,1)S(1)}) custom-call(s32[4]{0:T(128)S(1)} %pad_add_fusion.ids, s32[2,32]{1,0:T(2,128)S(1)} %bitcast.21, s32[10]{0:T(128)S(1)} %get-tuple-element.102.mine, bf16[4,32,32,128]{3,2,1,0:T(8,128)(2,1)S(1)} %collective-permute-done.23.rest_0_.rest_2_, ...), custom_call_target="tpu_custom_call" | custom-call | flops 8589934592 | bytes 1048576 | tf_op jit(solution)/shard_map/far_operands/pallas_call | solution.py:633
  245.2 3.5 %banded_products.10 = (bf16[4,12,32,128]{3,2,1,0:T(8,128)(2,1)S(1)}, bf16[4,12,32,128]{3,2,1,0:T(8,128)(2,1)S(1)}, bf16[4,12,32,128]{3,2,1,0:T(8,128)(2,1)S(1)}) custom-call(s32[4]{0:T(128)S(1)} %pad_add_fusion.ids, s32[40]{0:T(128)S(1)} %get-tuple-element.76.chosen, bf16[8,12,32,128]{3,2,1,0:T(8,128)(2,1)S(1)} %get-tuple-element.132.rest_0_, ...), custom_call_target="tpu_custom_call" | custom-call | flops 301989888 | bytes 1 | tf_op jit(solution)/shard_map/banded_products/pallas_call | solution.py:771
  249.8 14.9 %collective-permute-done.32.rest_1_ = bf16[4,32,32,128]{3,2,1,0:T(8,128)(2,1)S(1)} collective-permute-done((bf16[4,32,32,128]{3,2,1,0:T(8,128)(2,1)S(1)}, bf16[4,32,32,128]{3,2,1,0:T(8,128)(2,1)S(1)}, u32[]{:S(2)}, u32[]{:S(2)}) %collective-permute-start.32) | collective-permute-done | bytes 1048608 | tf_op jit(solution)/shard_map/ppermute | solution.py:946
  267.2 13.6 %collective-permute-done.34.rest_4_ = bf16[4,32,32,128]{3,2,1,0:T(8,128)(2,1)S(1)} collective-permute-done((bf16[4,32,32,128]{3,2,1,0:T(8,128)(2,1)S(1)}, bf16[4,32,32,128]{3,2,1,0:T(8,128)(2,1)S(1)}, u32[]{:S(2)}, u32[]{:S(2)}) %collective-permute-start.34) | collective-permute-done | bytes 1048608 | tf_op jit(solution)/shard_map/ppermute | solution.py:947
  280.8 2.4 banded_products.11.rest_6_
  283.2 8.9 %close_layer.5 = bf16[8,32,32,128]{3,2,1,0:T(8,128)(2,1)} custom-call(s32[4]{0:T(128)S(1)} %pad_add_fusion.ids, s32[2,32]{1,0:T(2,128)S(1)} %bitcast.22, s32[16]{0:T(128)S(1)} %get-tuple-element.91.place, bf16[4,20,32,128]{3,2,1,0:T(8,128)(2,1)S(1)} %collective-permute-done.25.rest_0_, bf16[4,20,32,128]{3,2,1,0:T(8,128)(2,1)S(1)} %collective-permute-done.26.rest_1_, ...), custom_call_target="tpu_custom_call" | custom-call | flops 8589934592 | bytes 1048576 | tf_op jit(solution)/shard_map/close_layer/pallas_call | solution.py:911
  (95 shorter events, 33.1 us)
Async XLA Ops:
  0.0 52.4 %collective-permute-start.6 = (bf16[8,32,32,128]{3,2,1,0:T(8,128)(2,1)}, bf16[8,32,32,128]{3,2,1,0:T(8,128)(2,1)}, u32[]{:S(2)}, u32[]{:S(2)}) collective-permute-start(bf16[8,32,32,128]{3,2,1,0:T(8,128)(2,1)} %rest_7_.3), channel_id=1, source_target_pairs={{0,4},{4,8},{8,12},{12,0},{1,5},{5,9},{9,13},{13,1},{2,6},{6,10},{... | collective-permute-start | bytes 6291464 | tf_op jit(solution)/shard_map/ppermute | solution.py:968
  11.6 13.9 %collective-permute-start.2 = (bf16[4,16,32,128]{3,2,1,0:T(8,128)(2,1)S(1)}, bf16[4,16,32,128]{3,2,1,0:T(8,128)(2,1)S(1)}, u32[]{:S(2)}, u32[]{:S(2)}) collective-permute-start(bf16[4,16,32,128]{3,2,1,0:T(8,128)(2,1)S(1)} %get-tuple-element.78.rest_3_), channel_id=1, source_target_pairs={{1,2},{2,1},{5,6},{6,5},{9,10},{10,9},{13,14},{14,13},{17,18},{18,... | collective-permute-start | bytes 1572872 | tf_op jit(solution)/shard_map/ppermute | solution.py:940
  12.3 14.1 %collective-permute-start.1 = (bf16[4,16,32,128]{3,2,1,0:T(8,128)(2,1)S(1)}, bf16[4,16,32,128]{3,2,1,0:T(8,128)(2,1)S(1)}, u32[]{:S(2)}, u32[]{:S(2)}) collective-permute-start(bf16[4,16,32,128]{3,2,1,0:T(8,128)(2,1)S(1)} %get-tuple-element.78.rest_3_), channel_id=1, source_target_pairs={{0,2},{3,1},{1,0},{2,3},{4,6},{7,5},{5,4},{6,7},{8,10},{11,9},{9,8... | collective-permute-start | bytes 1572872 | tf_op jit(solution)/shard_map/ppermute | solution.py:939
  29.3 13.5 %collective-permute-start.4 = (bf16[4,16,32,128]{3,2,1,0:T(8,128)(2,1)S(1)}, bf16[4,16,32,128]{3,2,1,0:T(8,128)(2,1)S(1)}, u32[]{:S(2)}, u32[]{:S(2)}) collective-permute-start(bf16[4,16,32,128]{3,2,1,0:T(8,128)(2,1)S(1)} %get-tuple-element.85.rest_8_), channel_id=1, source_target_pairs={{0,2},{3,1},{1,0},{2,3},{4,6},{7,5},{5,4},{6,7},{8,10},{11,9},{9,8... | collective-permute-start | bytes 1572872 | tf_op jit(solution)/shard_map/ppermute | solution.py:939
  47.3 18.6 %collective-permute-start.11 = (bf16[8,16,32,128]{3,2,1,0:T(8,128)(2,1)S(1)}, bf16[8,16,32,128]{3,2,1,0:T(8,128)(2,1)S(1)}, u32[]{:S(2)}, u32[]{:S(2)}) collective-permute-start(bf16[8,16,32,128]{3,2,1,0:T(8,128)(2,1)S(1)} %get-tuple-element.96.rest_3_), channel_id=1, source_target_pairs={{1,2},{2,1},{5,6},{6,5},{9,10},{10,9},{13,14},{14,13},{17,18},{18,... | collective-permute-start | bytes 3145736 | tf_op jit(solution)/shard_map/ppermute | solution.py:940
  48.0 41.9 %collective-permute-start.10 = (bf16[8,16,32,128]{3,2,1,0:T(8,128)(2,1)S(1)}, bf16[8,16,32,128]{3,2,1,0:T(8,128)(2,1)S(1)}, u32[]{:S(2)}, u32[]{:S(2)}) collective-permute-start(bf16[8,16,32,128]{3,2,1,0:T(8,128)(2,1)S(1)} %get-tuple-element.96.rest_3_), channel_id=1, source_target_pairs={{0,2},{3,1},{1,0},{2,3},{4,6},{7,5},{5,4},{6,7},{8,10},{11,9},{9,8... | collective-permute-start | bytes 3145736 | tf_op jit(solution)/shard_map/ppermute | solution.py:939
  52.4 37.4 %collective-permute-start.9 = (bf16[8,16,32,128]{3,2,1,0:T(8,128)(2,1)S(1)}, bf16[8,16,32,128]{3,2,1,0:T(8,128)(2,1)S(1)}, u32[]{:S(2)}, u32[]{:S(2)}) collective-permute-start(bf16[8,16,32,128]{3,2,1,0:T(8,128)(2,1)S(1)} %get-tuple-element.94.rest_1_), channel_id=1, source_target_pairs={{0,1},{1,0},{2,3},{3,2},{4,5},{5,4},{6,7},{7,6},{8,9},{9,8},{10,11... | collective-permute-start | bytes 3145736 | tf_op jit(solution)/shard_map/ppermute | solution.py:938
  52.5 22.7 %collective-permute-start.8 = (bf16[4,16,32,128]{3,2,1,0:T(8,128)(2,1)S(1)}, bf16[4,16,32,128]{3,2,1,0:T(8,128)(2,1)S(1)}, u32[]{:S(2)}, u32[]{:S(2)}) collective-permute-start(bf16[4,16,32,128]{3,2,1,0:T(8,128)(2,1)S(1)} %get-tuple-element.89), channel_id=1, source_target_pairs={{0,12},{4,0},{8,4},{12,8},{1,13},{5,1},{9,5},{13,9},{2,14},{6,2},{... | collective-permute-start | bytes 1572872 | tf_op jit(solution)/shard_map/ppermute | solution.py:968
  52.6 36.0 %collective-permute-start.7 = (bf16[4,16,32,128]{3,2,1,0:T(8,128)(2,1)S(1)}, bf16[4,16,32,128]{3,2,1,0:T(8,128)(2,1)S(1)}, u32[]{:S(2)}, u32[]{:S(2)}) collective-permute-start(bf16[4,16,32,128]{3,2,1,0:T(8,128)(2,1)S(1)} %get-tuple-element.87), channel_id=1, source_target_pairs={{0,8},{4,12},{8,0},{12,4},{1,9},{5,13},{9,1},{13,5},{2,10},{6,14},... | collective-permute-start | bytes 1572872 | tf_op jit(solution)/shard_map/ppermute | solution.py:968
  65.9 32.1 %collective-permute-start.14 = (bf16[4,32,32,128]{3,2,1,0:T(8,128)(2,1)S(1)}, bf16[4,32,32,128]{3,2,1,0:T(8,128)(2,1)S(1)}, u32[]{:S(2)}, u32[]{:S(2)}) collective-permute-start(bf16[4,32,32,128]{3,2,1,0:T(8,128)(2,1)S(1)} %get-tuple-element.104.rest_1_), channel_id=1, source_target_pairs={{0,1},{1,0},{2,3},{3,2},{4,5},{5,4},{6,7},{7,6},{8,9},{9,8},{10,11... | collective-permute-start | bytes 3145736 | tf_op jit(solution)/shard_map/ppermute | solution.py:938
  75.1 22.9 %collective-permute-start.16 = (bf16[4,32,32,128]{3,2,1,0:T(8,128)(2,1)S(1)}, bf16[4,32,32,128]{3,2,1,0:T(8,128)(2,1)}, u32[]{:S(2)}, u32[]{:S(2)}) collective-permute-start(bf16[4,32,32,128]{3,2,1,0:T(8,128)(2,1)S(1)} %get-tuple-element.105.rest_3_), channel_id=1, source_target_pairs={{1,2},{2,1},{5,6},{6,5},{9,10},{10,9},{13,14},{14,13},{17,18},{18,... | collective-permute-start | bytes 3145736 | tf_op jit(solution)/shard_map/ppermute | solution.py:940
  88.7 13.7 %collective-permute-start.15 = (bf16[4,32,32,128]{3,2,1,0:T(8,128)(2,1)S(1)}, bf16[4,32,32,128]{3,2,1,0:T(8,128)(2,1)}, u32[]{:S(2)}, u32[]{:S(2)}) collective-permute-start(bf16[4,32,32,128]{3,2,1,0:T(8,128)(2,1)S(1)} %get-tuple-element.105.rest_3_), channel_id=1, source_target_pairs={{0,2},{3,1},{1,0},{2,3},{4,6},{7,5},{5,4},{6,7},{8,10},{11,9},{9,8... | collective-permute-start | bytes 3145736 | tf_op jit(solution)/shard_map/ppermute | solution.py:939
  94.2 14.0 %collective-permute-start.13 = (bf16[4,16,32,128]{3,2,1,0:T(8,128)(2,1)}, bf16[4,16,32,128]{3,2,1,0:T(8,128)(2,1)}, u32[]{:S(2)}, u32[]{:S(2)}) collective-permute-start(bf16[4,16,32,128]{3,2,1,0:T(8,128)(2,1)} %get-tuple-element.100), channel_id=1, source_target_pairs={{0,12},{4,0},{8,4},{12,8},{1,13},{5,1},{9,5},{13,9},{2,14},{6,2},{... | collective-permute-start | bytes 1572872 | tf_op jit(solution)/shard_map/ppermute | solution.py:968
  95.2 36.4 %collective-permute-start.12 = (bf16[4,16,32,128]{3,2,1,0:T(8,128)(2,1)}, bf16[4,16,32,128]{3,2,1,0:T(8,128)(2,1)}, u32[]{:S(2)}, u32[]{:S(2)}) collective-permute-start(bf16[4,16,32,128]{3,2,1,0:T(8,128)(2,1)} %get-tuple-element.98), channel_id=1, source_target_pairs={{0,8},{4,12},{8,0},{12,4},{1,9},{5,13},{9,1},{13,5},{2,10},{6,14},... | collective-permute-start | bytes 1572872 | tf_op jit(solution)/shard_map/ppermute | solution.py:968
  144.9 14.8 %collective-permute-start.17 = (bf16[4,20,32,128]{3,2,1,0:T(8,128)(2,1)S(1)}, bf16[4,20,32,128]{3,2,1,0:T(8,128)(2,1)S(1)}, u32[]{:S(2)}, u32[]{:S(2)}) collective-permute-start(bf16[4,20,32,128]{3,2,1,0:T(8,128)(2,1)S(1)} %get-tuple-element.108.rest_0_), channel_id=1, source_target_pairs={{1,3},{2,0},{0,1},{3,2},{5,7},{6,4},{4,5},{7,6},{9,11},{10,8},{8,9... | collective-permute-start | bytes 1966088 | tf_op jit(solution)/shard_map/ppermute | solution.py:946
  145.0 23.6 %collective-permute-start.19 = (bf16[4,20,32,128]{3,2,1,0:T(8,128)(2,1)S(1)}, bf16[4,20,32,128]{3,2,1,0:T(8,128)(2,1)S(1)}, u32[]{:S(2)}, u32[]{:S(2)}) collective-permute-start(bf16[4,20,32,128]{3,2,1,0:T(8,128)(2,1)S(1)} %get-tuple-element.115.rest_3_), channel_id=1, source_target_pairs={{0,2},{2,0},{1,3},{3,1},{4,6},{6,4},{5,7},{7,5},{8,10},{10,8},{9,1... | collective-permute-start | bytes 1966088 | tf_op jit(solution)/shard_map/ppermute | solution.py:947
  146.4 24.8 %collective-permute-start.23 = (bf16[4,32,32,128]{3,2,1,0:T(8,128)(2,1)S(1)}, bf16[4,32,32,128]{3,2,1,0:T(8,128)(2,1)S(1)}, u32[]{:S(2)}, u32[]{:S(2)}) collective-permute-start(bf16[4,32,32,128]{3,2,1,0:T(8,128)(2,1)S(1)} %get-tuple-element.123), channel_id=1, source_target_pairs={{0,4},{4,8},{8,12},{12,0},{1,5},{5,9},{9,13},{13,1},{2,6},{6,10},{... | collective-permute-start | bytes 3145736 | tf_op jit(solution)/shard_map/ppermute | solution.py:968
  159.7 12.0 %collective-permute-start.18 = (bf16[4,20,32,128]{3,2,1,0:T(8,128)(2,1)S(1)}, bf16[4,20,32,128]{3,2,1,0:T(8,128)(2,1)S(1)}, u32[]{:S(2)}, u32[]{:S(2)}) collective-permute-start(bf16[4,20,32,128]{3,2,1,0:T(8,128)(2,1)S(1)} %collective-permute-done.17.rest_1_), channel_id=1, source_target_pairs={{0,1},{3,2},{4,5},{7,6},{8,9},{11,10},{12,13},{15,14},{16,17},{19,... | collective-permute-start | bytes 1966088 | tf_op jit(solution)/shard_map/ppermute | solution.py:948
  168.7 11.7 %collective-permute-start.20 = (bf16[4,20,32,128]{3,2,1,0:T(8,128)(2,1)S(1)}, bf16[4,20,32,128]{3,2,1,0:T(8,128)(2,1)S(1)}, u32[]{:S(2)}, u32[]{:S(2)}) collective-permute-start(bf16[4,20,32,128]{3,2,1,0:T(8,128)(2,1)S(1)} %get-tuple-element.117.rest_5_), channel_id=1, source_target_pairs={{1,3},{2,0},{0,1},{3,2},{5,7},{6,4},{4,5},{7,6},{9,11},{10,8},{8,9... | collective-permute-start | bytes 1966088 | tf_op jit(solution)/shard_map/ppermute | solution.py:946
  171.1 27.7 %collective-permute-start.24 = (bf16[4,32,32,128]{3,2,1,0:T(8,128)(2,1)S(1)}, bf16[4,32,32,128]{3,2,1,0:T(8,128)(2,1)S(1)}, u32[]{:S(2)}, u32[]{:S(2)}) collective-permute-start(bf16[4,32,32,128]{3,2,1,0:T(8,128)(2,1)S(1)} %get-tuple-element.124), channel_id=1, source_target_pairs={{0,4},{4,8},{8,12},{12,0},{1,5},{5,9},{9,13},{13,1},{2,6},{6,10},{... | collective-permute-start | bytes 3145736 | tf_op jit(solution)/shard_map/ppermute | solution.py:968
  171.8 20.7 %collective-permute-start.22 = (bf16[4,20,32,128]{3,2,1,0:T(8,128)(2,1)S(1)}, bf16[4,20,32,128]{3,2,1,0:T(8,128)(2,1)S(1)}, u32[]{:S(2)}, u32[]{:S(2)}) collective-permute-start(bf16[4,20,32,128]{3,2,1,0:T(8,128)(2,1)S(1)} %get-tuple-element.120.rest_8_), channel_id=1, source_target_pairs={{0,2},{2,0},{1,3},{3,1},{4,6},{6,4},{5,7},{7,5},{8,10},{10,8},{9,1... | collective-permute-start | bytes 1966088 | tf_op jit(solution)/shard_map/ppermute | solution.py:947
  180.4 12.0 %collective-permute-start.21 = (bf16[4,20,32,128]{3,2,1,0:T(8,128)(2,1)S(1)}, bf16[4,20,32,128]{3,2,1,0:T(8,128)(2,1)S(1)}, u32[]{:S(2)}, u32[]{:S(2)}) collective-permute-start(bf16[4,20,32,128]{3,2,1,0:T(8,128)(2,1)S(1)} %collective-permute-done.20.rest_6_), channel_id=1, source_target_pairs={{0,1},{3,2},{4,5},{7,6},{8,9},{11,10},{12,13},{15,14},{16,17},{19,... | collective-permute-start | bytes 1966088 | tf_op jit(solution)/shard_map/ppermute | solution.py:948
  192.4 10.8 %collective-permute-start.27 = (bf16[8,12,32,128]{3,2,1,0:T(8,128)(2,1)S(1)}, bf16[8,12,32,128]{3,2,1,0:T(8,128)(2,1)S(1)}, u32[]{:S(2)}, u32[]{:S(2)}) collective-permute-start(bf16[8,12,32,128]{3,2,1,0:T(8,128)(2,1)S(1)} %get-tuple-element.132.rest_0_), channel_id=1, source_target_pairs={{1,3},{2,0},{0,1},{3,2},{5,7},{6,4},{4,5},{7,6},{9,11},{10,8},{8,9... | collective-permute-start | bytes 2359304 | tf_op jit(solution)/shard_map/ppermute | solution.py:946
  198.9 13.8 %collective-permute-start.26 = (bf16[4,20,32,128]{3,2,1,0:T(8,128)(2,1)S(1)}, bf16[4,20,32,128]{3,2,1,0:T(8,128)(2,1)S(1)}, u32[]{:S(2)}, u32[]{:S(2)}) collective-permute-start(bf16[4,20,32,128]{3,2,1,0:T(8,128)(2,1)S(1)} %get-tuple-element.127), channel_id=1, source_target_pairs={{0,12},{4,0},{8,4},{12,8},{1,13},{5,1},{9,5},{13,9},{2,14},{6,2},{... | collective-permute-start | bytes 1966088 | tf_op jit(solution)/shard_map/ppermute | solution.py:968
  199.4 45.8 %collective-permute-start.29 = (bf16[8,12,32,128]{3,2,1,0:T(8,128)(2,1)S(1)}, bf16[8,12,32,128]{3,2,1,0:T(8,128)(2,1)S(1)}, u32[]{:S(2)}, u32[]{:S(2)}) collective-permute-start(bf16[8,12,32,128]{3,2,1,0:T(8,128)(2,1)S(1)} %get-tuple-element.134.rest_3_), channel_id=1, source_target_pairs={{0,2},{2,0},{1,3},{3,1},{4,6},{6,4},{5,7},{7,5},{8,10},{10,8},{9,1... | collective-permute-start | bytes 2359304 | tf_op jit(solution)/shard_map/ppermute | solution.py:947
  199.9 45.2 %collective-permute-start.25 = (bf16[4,20,32,128]{3,2,1,0:T(8,128)(2,1)S(1)}, bf16[4,20,32,128]{3,2,1,0:T(8,128)(2,1)S(1)}, u32[]{:S(2)}, u32[]{:S(2)}) collective-permute-start(bf16[4,20,32,128]{3,2,1,0:T(8,128)(2,1)S(1)} %get-tuple-element.125), channel_id=1, source_target_pairs={{0,8},{4,12},{8,0},{12,4},{1,9},{5,13},{9,1},{13,5},{2,10},{6,14},... | collective-permute-start | bytes 1966088 | tf_op jit(solution)/shard_map/ppermute | solution.py:968
  212.6 32.5 %collective-permute-start.28 = (bf16[8,12,32,128]{3,2,1,0:T(8,128)(2,1)S(1)}, bf16[8,12,32,128]{3,2,1,0:T(8,128)(2,1)S(1)}, u32[]{:S(2)}, u32[]{:S(2)}) collective-permute-start(bf16[8,12,32,128]{3,2,1,0:T(8,128)(2,1)S(1)} %collective-permute-done.27.rest_1_), channel_id=1, source_target_pairs={{0,1},{3,2},{4,5},{7,6},{8,9},{11,10},{12,13},{15,14},{16,17},{19,... | collective-permute-start | bytes 2359304 | tf_op jit(solution)/shard_map/ppermute | solution.py:948
  244.7 20.0 %collective-permute-start.32 = (bf16[4,32,32,128]{3,2,1,0:T(8,128)(2,1)S(1)}, bf16[4,32,32,128]{3,2,1,0:T(8,128)(2,1)S(1)}, u32[]{:S(2)}, u32[]{:S(2)}) collective-permute-start(bf16[4,32,32,128]{3,2,1,0:T(8,128)(2,1)S(1)} %get-tuple-element.142.rest_0_), channel_id=1, source_target_pairs={{1,3},{2,0},{0,1},{3,2},{5,7},{6,4},{4,5},{7,6},{9,11},{10,8},{8,9... | collective-permute-start | bytes 3145736 | tf_op jit(solution)/shard_map/ppermute | solution.py:946
  248.7 16.0 %collective-permute-start.31 = (bf16[4,12,32,128]{3,2,1,0:T(8,128)(2,1)S(1)}, bf16[4,12,32,128]{3,2,1,0:T(8,128)(2,1)S(1)}, u32[]{:S(2)}, u32[]{:S(2)}) collective-permute-start(bf16[4,12,32,128]{3,2,1,0:T(8,128)(2,1)S(1)} %get-tuple-element.138), channel_id=1, source_target_pairs={{0,12},{4,0},{8,4},{12,8},{1,13},{5,1},{9,5},{13,9},{2,14},{6,2},{... | collective-permute-start | bytes 1179656 | tf_op jit(solution)/shard_map/ppermute | solution.py:968
  248.8 32.0 %collective-permute-start.34 = (bf16[4,32,32,128]{3,2,1,0:T(8,128)(2,1)S(1)}, bf16[4,32,32,128]{3,2,1,0:T(8,128)(2,1)S(1)}, u32[]{:S(2)}, u32[]{:S(2)}) collective-permute-start(bf16[4,32,32,128]{3,2,1,0:T(8,128)(2,1)S(1)} %get-tuple-element.144.rest_3_), channel_id=1, source_target_pairs={{0,2},{2,0},{1,3},{3,1},{4,6},{6,4},{5,7},{7,5},{8,10},{10,8},{9,1... | collective-permute-start | bytes 3145736 | tf_op jit(solution)/shard_map/ppermute | solution.py:947
  264.7 16.1 %collective-permute-start.33 = (bf16[4,32,32,128]{3,2,1,0:T(8,128)(2,1)S(1)}, bf16[4,32,32,128]{3,2,1,0:T(8,128)(2,1)S(1)}, u32[]{:S(2)}, u32[]{:S(2)}) collective-permute-start(bf16[4,32,32,128]{3,2,1,0:T(8,128)(2,1)S(1)} %collective-permute-done.32.rest_1_), channel_id=1, source_target_pairs={{0,1},{3,2},{4,5},{7,6},{8,9},{11,10},{12,13},{15,14},{16,17},{19,... | collective-permute-start | bytes 3145736 | tf_op jit(solution)/shard_map/ppermute | solution.py:948
  266.1 17.1 %collective-permute-start.30 = (bf16[4,12,32,128]{3,2,1,0:T(8,128)(2,1)S(1)}, bf16[4,12,32,128]{3,2,1,0:T(8,128)(2,1)S(1)}, u32[]{:S(2)}, u32[]{:S(2)}) collective-permute-start(bf16[4,12,32,128]{3,2,1,0:T(8,128)(2,1)S(1)} %get-tuple-element.136), channel_id=1, source_target_pairs={{0,8},{4,12},{8,0},{12,4},{1,9},{5,13},{9,1},{13,5},{2,10},{6,14},... | collective-permute-start | bytes 1179656 | tf_op jit(solution)/shard_map/ppermute | solution.py:968
  (22 other events, 322.7 us)
